TPU v7x, 32 devices: a whole 2x2x4 slice. The times are simulated.
32 devices in a mesh: frame: 8 (over z, x), patch: 4 (over y, core).
Axes of the slice: x: 2, y: 2, z: 4, core: 2. Of those that a mesh axis runs over, the one named last changes fastest.
Arguments:
- tokens: bfloat16 [8, 512, 1152], P('frame', 'patch'), may hold values from -5 to 5
- modulation: float32 [6, 1152], replicated, may hold values from -4 to 4
- spatial_qkv: bfloat16 [3456, 1152], P('patch'), may hold values from -4 to 4
- spatial_out: bfloat16 [1152, 1152], P('patch'), may hold values from -0.1875 to 0.1875
- temporal_qkv: bfloat16 [3456, 1152], P('patch'), may hold values from -4 to 4
- temporal_out: bfloat16 [1152, 1152], P('patch'), may hold values from -0.1875 to 0.1875
Outputs:
- result: bfloat16 [8, 512, 1152], P('frame', 'patch')
All inputs are finite; a program needn't handle non-finite values.
Results may differ from a plain program's by a relative error of at most 0.022.
The roundings to bfloat16 on the way count: a program that leaves them out, or rounds other values in their place, can miss the bound.
Values may be sent and summed in bfloat16 or wider, within the bound.
No kernel may reach another device: no remote copies, remote signals or barrier semaphores. Data moves between devices by JAX's collectives and lax.ppermute only.
A program may use at most 64 MiB of HBM per device.

v0:
```python
import math

import jax
import jax.numpy as jnp
from jax import lax
from jax.sharding import PartitionSpec as P

HD = 72


def modulate(rows, shift, scale):
    values = rows.astype(jnp.float32)
    average = jnp.mean(values, axis=-1, keepdims=True)
    centred = values - average
    variance = jnp.mean(centred * centred, axis=-1, keepdims=True)
    normed = centred * lax.rsqrt(variance + 1e-06)
    return (normed * (1.0 + shift * 0.0 + scale) + shift).astype(jnp.bfloat16)


def project_rows(flat_rows, weight_rows):
    return lax.dot_general(
        flat_rows, weight_rows, (((1,), (1,)), ((), ())), preferred_element_type=jnp.float32
    )


def weigh_block(query_part, key_part, value_part):
    scores = jnp.einsum("nqhd,nkhd->nhqk", query_part, key_part, preferred_element_type=jnp.float32)
    scores = scores * query_part.shape[-1] ** (-0.5)
    probs = jax.nn.softmax(scores, axis=-1).astype(jnp.bfloat16)
    mixed = jnp.einsum("nhqk,nkhd->nqhd", probs, value_part, preferred_element_type=jnp.float32)
    return mixed.astype(jnp.bfloat16)


def spatial_attend(projected):
    frame_count, row_count, head_count, three, head_size = projected.shape
    query_part = projected[:, :, :, 0]
    key_part = projected[:, :, :, 1]
    value_part = projected[:, :, :, 2]
    block_rows = row_count if row_count <= 512 else math.gcd(row_count, 512)
    segments = query_part.reshape(
        frame_count, row_count // block_rows, block_rows, head_count, head_size
    )
    segments = segments.transpose(1, 0, 2, 3, 4)

    def attend_segment(segment):
        return weigh_block(segment, key_part, value_part)

    mixed = lax.map(attend_segment, segments)
    mixed = mixed.transpose(1, 0, 2, 3, 4)
    return mixed.reshape(frame_count, row_count, head_count * head_size)


def temporal_attend(projected):
    frame_count, group_count, head_count, three, head_size = projected.shape
    query_part = projected[:, :, :, 0]
    key_part = projected[:, :, :, 1]
    value_part = projected[:, :, :, 2]
    scores = jnp.einsum("qmhd,kmhd->mhqk", query_part, key_part, preferred_element_type=jnp.float32)
    scores = scores * head_size ** (-0.5)
    probs = jax.nn.softmax(scores, axis=-1).astype(jnp.bfloat16)
    mixed = jnp.einsum("mhqk,kmhd->qmhd", probs, value_part, preferred_element_type=jnp.float32)
    return mixed.astype(jnp.bfloat16).reshape(frame_count, group_count, head_count * head_size)


def per_device(tokens, modulation, spatial_qkv, spatial_out, temporal_qkv, temporal_out):
    frames_here, patches_here, model_width = tokens.shape
    heads_here = spatial_qkv.shape[0] // (3 * HD)
    spatial_in = modulate(tokens, modulation[0], modulation[1])
    gathered, spatial_full, temporal_full = (
        lax.all_gather(spatial_in, "patch", axis=1, tiled=True),
        lax.all_gather(spatial_out, "patch", axis=0, tiled=True),
        lax.all_gather(temporal_out, "patch", axis=0, tiled=True),
    )
    row_count = gathered.shape[1]
    spatial_proj = project_rows(gathered.reshape(-1, model_width), spatial_qkv)
    spatial_proj = spatial_proj.astype(jnp.bfloat16).reshape(
        frames_here, row_count, heads_here, 3, HD
    )
    spatial_heads = spatial_attend(spatial_proj)
    returned = lax.all_to_all(spatial_heads, "patch", split_axis=1, concat_axis=2, tiled=True)
    spatial_update = jnp.dot(
        returned.reshape(-1, model_width), spatial_full, preferred_element_type=jnp.float32
    )
    middle = (
        tokens.reshape(-1, model_width).astype(jnp.float32) + modulation[2] * spatial_update
    ).astype(jnp.bfloat16)
    temporal_in = modulate(middle, modulation[3], modulation[4]).reshape(
        frames_here, patches_here, model_width
    )
    regrouped = lax.all_to_all(temporal_in, "frame", split_axis=1, concat_axis=0, tiled=True)
    segment = lax.all_gather(regrouped, "patch", axis=1, tiled=True)
    flat_rows = project_rows(segment.reshape(-1, model_width), temporal_qkv)
    temporal_proj = flat_rows.astype(jnp.bfloat16).reshape(segment.shape[0], segment.shape[1], -1)
    seq_frames, group_count = (temporal_proj.shape[0], temporal_proj.shape[1])
    temporal_heads = temporal_attend(
        temporal_proj.reshape(seq_frames, group_count, heads_here, 3, HD)
    )
    returned_heads = lax.all_to_all(
        lax.all_to_all(temporal_heads, "patch", split_axis=1, concat_axis=2, tiled=True),
        "frame",
        split_axis=0,
        concat_axis=1,
        tiled=True,
    )
    temporal_update = jnp.dot(
        returned_heads.reshape(-1, model_width), temporal_full, preferred_element_type=jnp.float32
    )
    result = (middle.astype(jnp.float32) + modulation[5] * temporal_update).astype(jnp.bfloat16)
    return result.reshape(frames_here, patches_here, model_width)


def solution(mesh):
    in_specs = (
        P("frame", "patch", None),
        P(),
        P("patch", None),
        P("patch", None),
        P("patch", None),
        P("patch", None),
    )
    out_specs = P("frame", "patch", None)
    return jax.shard_map(
        per_device, mesh=mesh, in_specs=in_specs, out_specs=out_specs, check_vma=False
    )
```

profile of v0, /device:TPU:0, one launch (start us, length us, event | category | flops | bytes accessed | tf_op | source)
XLA Modules:
  0.0 157.1 jit_solution(14037374664378682633)
XLA Ops:
  6.5 1.2 slice_reduce_fusion
  7.7 1.1 convert_reduce_fusion
  8.8 1.2 fusion.20
  10.0 1.9 %fusion.23 = bf16[1,128,1152]{2,1,0:T(8,128)(2,1)} fusion(bf16[1,128,1152]{2,1,0:T(8,128)(2,1)} %param.6, f32[1152]{0:T(1024)S(1)} %get-tuple-element.20, f32[1152]{0:T(1024)S(1)} %add_add_fusion, f32[128]{0:T(128)S(1)} %add_rsqrt_fusion.1, f32[128]{0:T(128)S(1)} %broadcast_multiply_fusion.1), kind=kLoop, calls=%fused_computation.34 | loop fusion | flops 884736 | bytes 600064 | tf_op jit(solution)/shard_map/convert_element_type | solution.py:17
  12.0 0.7 all-gather.7.cloned.1.call-update
  12.7 19.5 %all-gather.5.cloned.1.call-done = bf16[1,512,1152]{2,1,0:T(8,128)(2,1)} async-done(((bf16[1,128,1152]{2,1,0:T(8,128)(2,1)}), bf16[1,512,1152]{2,1,0:T(8,128)(2,1)}) %all-gather.5.cloned.1.call-update) | async-done | bytes 1179664 | tf_op jit(solution)/shard_map/all_gather | solution.py:70
  32.3 2.6 %convolution_convert_fusion.1 = bf16[512,864]{0,1:T(8,128)(2,1)S(1)} fusion(bf16[864,1152]{1,0:T(8,128)(2,1)S(1)} %copy-done, bf16[1,512,1152]{2,1,0:T(8,128)(2,1)} %all-gather.5.cloned.1.call-done), kind=kOutput, calls=%fused_computation.18 | convolution fusion | flops 1019658240 | bytes 4055040 | tf_op jit(solution)/shard_map/dot_general | solution.py:21
  34.9 3.4 %fusion.44 = (f32[4,512]{1,0:T(4,128)S(1)}, f32[4,512,512]{1,2,0:T(8,128)}) fusion(bf16[1,512,4,3,72]{1,4,3,2,0:T(8,128)(2,1)S(1)} %bitcast.111), kind=kOutput, calls=%fused_computation.63 | convolution fusion | flops 154141184 | bytes 4792320 | tf_op jit(solution)/shard_map/while/body/eval_jaxpr/sub | solution.py:29
  38.3 3.0 %fusion.16 = bf16[4,72,512]{2,1,0:T(8,128)(2,1)S(1)} fusion(f32[4,512,512]{1,2,0:T(8,128)} %get-tuple-element.30, f32[4,512]{1,0:T(4,128)S(1)} %get-tuple-element.29, bf16[1,512,4,3,72]{1,4,3,2,0:T(8,128)(2,1)} %bitcast.112), kind=kOutput, calls=%fused_computation.23 | convolution fusion | flops 153239552 | bytes 4792320 | tf_op jit(solution)/shard_map/while/body/eval_jaxpr/nhqk,nkhd->nqhd/dot_general | solution.py:30
  41.3 1.2 copy.55
  43.0 3.3 %reduce.18 = bf16[512,288]{1,0:T(8,128)(2,1)S(1)} reduce(bf16[512,1,288]{2,1,0:T(2,128)(2,1)S(1)} %bitcast.99, bf16[]{:T(256)} %broadcast.104), dimensions={1}, to_apply=%bitcast.73.reduce_sub_computation | reduce | bytes 589826
  46.9 12.4 %all_to_all.54 = bf16[4,2,18432]{2,1,0:T(2,128)(2,1)S(1)} all-to-all(bf16[4,2,18432]{2,1,0:T(2,128)(2,1)S(1)} %reshape.140), channel_id=1, replica_groups=mesh['frame'=8,'patch'=4] {'patch'}, dimensions={0} | all-to-all | bytes 589824 | tf_op jit(solution)/shard_map/all_to_all | solution.py:80
  59.3 1.9 %reshape.141 = bf16[512,1,288]{2,1,0:T(2,128)(2,1)} reshape(bf16[4,2,18432]{2,1,0:T(2,128)(2,1)S(1)} %all_to_all.54) | data formatting | bytes 589824
  61.2 2.2 %copy.56 = bf16[1,512,288]{1,2,0:T(8,128)(2,1)S(1)} copy(bf16[1,512,288]{2,0,1:T(2,128)(2,1)} %bitcast.100) | data formatting | bytes 589824 | tf_op jit(solution)/shard_map/all_to_all | solution.py:80
  63.6 2.5 %fusion.45 = (f32[128]{0:T(128)S(1)}, f32[128,1152]{1,0:T(8,128)S(1)}) fusion(bf16[128,1152]{0,1:T(8,128)(2,1)S(1)} %bitcast.105, bf16[1152,1152]{1,0:T(8,128)(2,1)} %all-gather.7.cloned.1.call-done, f32[1152]{0:T(1024)S(1)} %get-tuple-element.22, bf16[1,128,1152]{2,1,0:T(8,128)(2,1)S(1)} %copy-done.1), kind=kOutput, calls=%fused_computation.64 | convolution fusion | flops 340623232 | bytes 3838976 | tf_op jit(solution)/shard_map/dot_general | solution.py:81
  66.9 2.5 %reduce.19 = bf16[128,1152]{1,0:T(8,128)(2,1)S(1)} reduce(bf16[128,1,1152]{2,1,0:T(2,128)(2,1)S(1)} %bitcast.101, bf16[]{:T(256)} %broadcast.104), dimensions={1}, to_apply=%bitcast.98.reduce_sub_computation | reduce | bytes 589826
  69.5 15.7 %all_to_all.55 = bf16[8,2,9216]{2,1,0:T(2,128)(2,1)S(1)} all-to-all(bf16[8,2,9216]{2,1,0:T(2,128)(2,1)S(1)} %reshape.142), channel_id=1, replica_groups=mesh['frame'=8,'patch'=4] {'frame'}, dimensions={0} | all-to-all | bytes 589824 | tf_op jit(solution)/shard_map/all_to_all | solution.py:90
  85.4 0.8 copy.70
  86.8 14.4 %all-gather.9.cloned.1.call-done = bf16[8,64,1152]{2,1,0:T(8,128)(2,1)} async-done(((bf16[8,16,1152]{2,1,0:T(8,128)(2,1)}), bf16[8,64,1152]{2,1,0:T(8,128)(2,1)}) %all-gather.9.cloned.1.call-update) | async-done | bytes 1179664 | tf_op jit(solution)/shard_map/all_gather | solution.py:91
  101.2 3.3 %convolution_convert_fusion = bf16[512,864]{0,1:T(8,128)(2,1)S(1)} fusion(bf16[512,1152]{1,0:T(8,128)(2,1)} %bitcast.110, bf16[864,1152]{1,0:T(8,128)(2,1)} %param.10), kind=kOutput, calls=%fused_computation.17 | convolution fusion | flops 1019658240 | bytes 4055040 | tf_op jit(solution)/shard_map/dot_general | solution.py:21
  104.4 1.8 %reshape_reshape.3 = bf16[8,64,4,3,72]{1,0,4,3,2:T(8,128)(2,1)} reshape(bf16[512,864]{0,1:T(8,128)(2,1)S(1)} %convolution_convert_fusion) | data formatting | bytes 1769472 | tf_op jit(solution)/shard_map/reshape;reshape | solution.py:96
  106.3 2.6 %fusion.43 = (bf16[8,64,4,1,72]{1,0,4,3,2:T(8,128)(2,1)S(1)}, bf16[8,64,4,1,72]{1,0,4,3,2:T(8,128)(2,1)}, bf16[8,64,4,1,72]{1,0,4,3,2:T(8,128)(2,1)}) fusion(bf16[8,64,4,3,72]{1,0,4,3,2:T(8,128)(2,1)} %reshape_reshape.3), kind=kLoop, calls=%fused_computation.62 | loop fusion | bytes 1769472 | tf_op jit(solution)/shard_map/slice | solution.py:57
  108.8 2.8 %copy.75 = bf16[8,64,4,1,72]{4,0,2,1,3:T(8,128)(2,1)} copy(bf16[8,64,4,1,72]{1,0,4,3,2:T(8,128)(2,1)} %get-tuple-element.27) | data formatting | bytes 589824
  111.6 2.8 %copy.76 = bf16[8,64,4,1,72]{4,0,2,1,3:T(8,128)(2,1)} copy(bf16[8,64,4,1,72]{1,0,4,3,2:T(8,128)(2,1)} %get-tuple-element.28) | data formatting | bytes 589824
  114.4 1.8 %copy.74 = bf16[8,64,4,1,72]{4,0,2,1,3:T(8,128)(2,1)} copy(bf16[8,64,4,1,72]{1,0,4,3,2:T(8,128)(2,1)S(1)} %get-tuple-element.26) | data formatting | bytes 589824
  116.2 3.1 %fusion.46 = (f32[64,4,8]{2,1,0:T(4,128)S(1)}, f32[64,4,8,8]{2,3,1,0:T(8,128)}) fusion(bf16[8,64,4,1,72]{4,0,2,1,3:T(8,128)(2,1)} %copy.76, bf16[8,64,4,1,72]{4,0,2,1,3:T(8,128)(2,1)} %copy.75), kind=kOutput, calls=%fused_computation.65 | convolution fusion | flops 2408455 | bytes 663552 | tf_op jit(solution)/shard_map/sub | solution.py:60
  119.3 1.8 %fusion.15 = bf16[8,64,4,72]{3,0,2,1:T(8,128)(2,1)S(1)} fusion(f32[64,4,8,8]{2,3,1,0:T(8,128)} %get-tuple-element.34, bf16[8,64,4,1,72]{4,0,2,1,3:T(8,128)(2,1)S(1)} %copy-done.2, f32[64,4,8]{2,1,0:T(4,128)S(1)} %get-tuple-element.33), kind=kOutput, calls=%fused_computation.22 | convolution fusion | flops 2539520 | bytes 663552 | tf_op jit(solution)/shard_map/mhqk,kmhd->qmhd/dot_general | solution.py:61
  121.7 9.8 %all_to_all.56 = bf16[8,64,288]{2,0,1:T(8,128)(2,1)S(1)} all-to-all(bf16[8,64,288]{2,0,1:T(8,128)(2,1)S(1)} %reshape.133), channel_id=1, replica_groups=mesh['frame'=8,'patch'=4] {'patch'}, dimensions={1} | all-to-all | bytes 589824 | tf_op jit(solution)/shard_map/all_to_all | solution.py:99
  131.8 1.0 all_to_all.48
  132.8 5.5 %all-to-all-start.3 = ((bf16[8,16,1152]{2,1,0:T(8,128)(2,1)}), bf16[8,16,1152]{2,1,0:T(8,128)(2,1)S(1)}, u32[]{:S(2)}, u32[]{:S(2)}) async-start(bf16[8,16,1152]{2,1,0:T(8,128)(2,1)} %all_to_all.48), calls=%async_computation.3 | async-start | bytes 589824 | tf_op jit(solution)/shard_map/all_to_all | solution.py:98
  138.3 9.2 %all-to-all-done.3 = bf16[8,16,1152]{2,1,0:T(8,128)(2,1)S(1)} async-done(((bf16[8,16,1152]{2,1,0:T(8,128)(2,1)}), bf16[8,16,1152]{2,1,0:T(8,128)(2,1)S(1)}, u32[]{:S(2)}, u32[]{:S(2)}) %all-to-all-start.3) | async-done | bytes 294944 | tf_op jit(solution)/shard_map/all_to_all | solution.py:98
  147.5 3.1 %fusion.10 = bf16[1,128,1152]{2,1,0:T(8,128)(2,1)} fusion(f32[128,1152]{1,0:T(8,128)S(1)} %get-tuple-element.32, bf16[128,1152]{1,0:T(8,128)(2,1)S(1)} %bitcast.108, bf16[1152,1152]{1,0:T(8,128)(2,1)} %all-gather.11.cloned.1.call-done, f32[1152]{0:T(1024)S(1)} %get-tuple-element.13), kind=kOutput, calls=%fused_computation.13 | convolution fusion | flops 340180992 | bytes 3838464 | tf_op jit(solution)/shard_map/dot_general | solution.py:105
  (34 shorter events, 4.0 us)
Async XLA Ops:
  6.5 25.7 %copy-start = (bf16[864,1152]{1,0:T(8,128)(2,1)S(1)}, bf16[864,1152]{1,0:T(8,128)(2,1)}, u32[]{:S(2)}) copy-start(bf16[864,1152]{1,0:T(8,128)(2,1)} %param.8) | copy-start | bytes 5971972
  6.5 25.7 %all-gather.5.cloned.1.call-start = ((), (), s32[]{:S(2)}) async-start(), calls=%async_computation.4 | async-start | bytes 1474560 | tf_op jit(solution)/shard_map/all_gather | solution.py:70
  11.9 51.6 %all-gather.7.cloned.1.call-start = ((), (), s32[]{:S(2)}) async-start(), calls=%async_computation.5 | async-start | bytes 3317760 | tf_op jit(solution)/shard_map/all_gather | solution.py:71
  12.7 88.5 %all-gather.9.cloned.1.call-start = ((), (), s32[]{:S(2)}) async-start(), calls=%async_computation.6 | async-start | bytes 1474560 | tf_op jit(solution)/shard_map/all_gather | solution.py:91
  34.9 3.4 %copy-start.3 = (bf16[512,864]{0,1:T(8,128)(2,1)}, bf16[512,864]{0,1:T(8,128)(2,1)S(1)}, u32[]{:S(2)}) copy-start(bf16[512,864]{0,1:T(8,128)(2,1)S(1)} %convolution_convert_fusion.1) | copy-start | bytes 2654212
  46.9 16.7 %copy-start.1 = (bf16[1,128,1152]{2,1,0:T(8,128)(2,1)S(1)}, bf16[1,128,1152]{2,1,0:T(8,128)(2,1)}, u32[]{:S(2)}) copy-start(bf16[1,128,1152]{2,1,0:T(8,128)(2,1)} %param.6) | copy-start | bytes 884740
  86.2 52.1 %all-gather.11.cloned.1.call-start = ((), (), s32[]{:S(2)}) async-start(), calls=%async_computation.7 | async-start | bytes 3317760 | tf_op jit(solution)/shard_map/all_gather | solution.py:72
  116.2 3.1 %copy-start.2 = (bf16[8,64,4,1,72]{4,0,2,1,3:T(8,128)(2,1)S(1)}, bf16[8,64,4,1,72]{4,0,2,1,3:T(8,128)(2,1)}, u32[]{:S(2)}) copy-start(bf16[8,64,4,1,72]{4,0,2,1,3:T(8,128)(2,1)} %copy.74) | copy-start | bytes 884740
  132.8 14.7 %all-to-all-start.3 = ((bf16[8,16,1152]{2,1,0:T(8,128)(2,1)}), bf16[8,16,1152]{2,1,0:T(8,128)(2,1)S(1)}, u32[]{:S(2)}, u32[]{:S(2)}) async-start(bf16[8,16,1152]{2,1,0:T(8,128)(2,1)} %all_to_all.48), calls=%async_computation.3 | async-start | bytes 589824 | tf_op jit(solution)/shard_map/all_to_all | solution.py:98
Sparse Core Ops, SparseCore 0:
  12.1 20.1 all-gather.4
  33.8 28.8 all-gather.6
  86.3 14.8 all-gather.8
  102.6 25.7 all-gather.10
where the time goes:
time: 158 us; the launch traced here: 157 us
  waiting for transfers between devices  44.2 us (28%)
  blocking collectives  37.9 us (24%)
  matrix products  22.7 us (14%)
  local copies, waits for them, and re-layouts  21.7 us (14%)
  between operations  13.3 us (8%)
  other arithmetic  11.5 us (7%)
  starting transfers between devices  5.81 us (4%)
    all_gather x1, waiting for transfers between devices, per_device(): lax.all_gather(spatial_in, 'patch', axis=1, tiled=True)  19.5 us
    all_to_all x1, blocking collectives, per_device(): lax.all_to_all(temporal_in, 'frame', split_axis=1, concat_axis=0, tiled=T...  15.7 us
    all_gather x1, waiting for transfers between devices, per_device(): segment = lax.all_gather(regrouped, 'patch', axis=1, tiled=True)  14.4 us
    all_to_all x1, blocking collectives, per_device(): lax.all_to_all(spatial_heads, 'patch', split_axis=1, concat_axis=2, tiled...  12.4 us
    unnamed x17, local copies, waits for them, and re-layouts  11.5 us
    all_to_all x1, blocking collectives, per_device(): lax.all_to_all(temporal_heads, 'patch', split_axis=1, concat_axis=2, tile...  9.84 us
    all_to_all x1, waiting for transfers between devices, per_device(): lax.all_to_all(lax.all_to_all(temporal_heads, 'patch', split_axis=1, conc...  9.18 us
    dot_general x2, matrix products, project_rows(): lax.dot_general(flat_rows, weight_rows, (((1,), (1,)), ((), ())), preferr...  5.86 us
  transfers between devices with their start and end apart: 5, of which 3 were waited for; matrix products, arithmetic and copies ran while one was open for 25% of the time, Pallas kernels for 0%

commit v1 on v0

v1 whole, which is shorter than its diff:
```python
import functools

import jax
import jax.numpy as jnp
from jax import lax
from jax.experimental import pallas as pl
from jax.experimental.pallas import tpu as pltpu
from jax.sharding import PartitionSpec as P

HD = 72
MIB = 1 << 20
LOG2E = 1.4426950408889634
F32 = jnp.float32
BF16 = jnp.bfloat16


def norm_rows(values, shift, scale):
    average = jnp.mean(values, axis=-1, keepdims=True)
    centred = values - average
    variance = jnp.mean(centred * centred, axis=-1, keepdims=True)
    normed = centred * lax.rsqrt(variance + 1e-06)
    return (normed * (1.0 + scale) + shift).astype(BF16)


def dot(left, right, left_dim=1, right_dim=0):
    return lax.dot_general(
        left, right, (((left_dim,), (right_dim,)), ((), ())), preferred_element_type=F32
    )


def softmax_over_rows(scores, mask=None):
    if mask is not None:
        scores = jnp.where(mask, scores, -1e30)
    top = jnp.max(scores, axis=0, keepdims=True)
    grown = jnp.exp2((scores - top) * (HD**-0.5 * LOG2E))
    total = jnp.sum(grown, axis=0, keepdims=True)
    return (grown * (1.0 / total)).astype(BF16)


def spatial_kernel(count, mod_ref, weight_ref, *refs):
    token_refs, out_refs = refs[:count], refs[count : 2 * count]
    proj_ref, heads_ref = refs[2 * count :]
    shift, scale = mod_ref[0:1, :], mod_ref[1:2, :]
    block = token_refs[0].shape[1]
    heads = weight_ref.shape[0] // (3 * HD)
    step = 2 if count % 2 == 0 else 1
    for at in range(0, count, step):
        rows = [
            norm_rows(token_refs[at + i][0].astype(F32), shift, scale) for i in range(step)
        ]
        rows = jnp.concatenate(rows, axis=0)
        proj_ref[:, at * block : (at + step) * block] = dot(weight_ref[...], rows, 1, 1)
    for head in range(heads):
        base = head * 3 * HD
        keys = proj_ref[base + HD : base + 2 * HD, :].astype(BF16).T
        values = proj_ref[base + 2 * HD : base + 3 * HD, :].astype(BF16)
        for at in range(0, count, step):
            cols = slice(at * block, (at + step) * block)
            query = proj_ref[base : base + HD, cols].astype(BF16)
            probs = softmax_over_rows(dot(keys, query))
            heads_ref[head * HD : (head + 1) * HD, cols] = dot(values, probs)
    for at in range(count):
        out_refs[at][...] = heads_ref[:, at * block : (at + 1) * block].astype(BF16)


def middle_kernel(count, pieces, mod_ref, token_ref, *refs):
    head_refs, weight_refs = refs[:count], refs[count : 2 * count]
    middle_ref, piece_refs, scratch = refs[2 * count], refs[2 * count + 1 : -1], refs[-1]
    heads = jnp.concatenate([ref[...] for ref in head_refs], axis=0)
    weights = jnp.concatenate([ref[...] for ref in weight_refs], axis=0)
    update = dot(heads.T, weights)
    middle = (token_ref[0].astype(F32) + mod_ref[2:3, :] * update).astype(BF16)
    middle_ref[...] = middle
    normed = norm_rows(middle.astype(F32), mod_ref[3:4, :], mod_ref[4:5, :])
    if pieces == 1:
        piece_refs[0][...] = normed
        return
    scratch[...] = normed
    here = lax.axis_index("frame")
    size = normed.shape[0] // pieces
    for at in range(pieces):
        start = pl.multiple_of((here ^ at) * size, size)
        piece_refs[at][...] = scratch[pl.ds(start, size), :]


def temporal_kernel(groups, pieces, cores, period, *refs):
    weight_refs = refs[:cores]
    piece_refs = refs[cores : cores + groups * pieces]
    out_refs = refs[cores + groups * pieces : -2]
    proj_ref, heads_ref = refs[-2:]
    rows = jnp.concatenate([ref[...] for ref in piece_refs], axis=0)
    block = rows.shape[0] // groups
    depth = weight_refs[0].shape[0]
    for core in range(cores):
        proj_ref[core * depth : (core + 1) * depth, :] = dot(weight_refs[core][...], rows, 1, 1)
    heads = cores * depth // (3 * HD)
    key_patch = lax.broadcasted_iota(jnp.int32, (block, block), 0) % period
    query_patch = lax.broadcasted_iota(jnp.int32, (block, block), 1) % period
    mask = key_patch == query_patch
    for head in range(heads):
        base = head * 3 * HD
        for group in range(groups):
            cols = slice(group * block, (group + 1) * block)
            query = proj_ref[base : base + HD, cols].astype(BF16)
            keys = proj_ref[base + HD : base + 2 * HD, cols].astype(BF16)
            values = proj_ref[base + 2 * HD : base + 3 * HD, cols].astype(BF16)
            probs = softmax_over_rows(dot(keys.T, query), mask)
            heads_ref[head * HD : (head + 1) * HD, cols] = dot(values, probs)
    for group in range(groups):
        out_refs[group][...] = heads_ref[:, group * block : (group + 1) * block].astype(BF16)


def update_kernel(groups, pieces, *refs):
    count = len(refs) - groups - pieces
    head_refs, weight_refs, piece_refs = refs[:groups], refs[groups:-pieces], refs[-pieces:]
    heads = jnp.concatenate([ref[...] for ref in head_refs], axis=0)
    weights = jnp.concatenate([ref[...] for ref in weight_refs], axis=0)
    update = dot(heads.T, weights).astype(BF16)
    size = update.shape[0] // pieces
    for at in range(pieces):
        piece_refs[at][...] = update[at * size : (at + 1) * size]


def result_kernel(pieces, mod_ref, middle_ref, *refs):
    piece_refs, out_ref = refs[:-1], refs[-1]
    gate = mod_ref[5:6, :]
    here = lax.axis_index("frame")
    size = middle_ref.shape[0] // pieces
    for at in range(pieces):
        start = pl.multiple_of((here ^ at) * size, size) if pieces > 1 else 0
        rows = pl.ds(start, size)
        update = piece_refs[at][...].astype(F32)
        out_ref[0, rows, :] = (middle_ref[rows, :].astype(F32) + gate * update).astype(BF16)


def call(body, operands, outs, scratch=(), flops=0, limit=24):
    moved = sum(x.size * x.dtype.itemsize for x in (*operands, *outs))
    return pl.pallas_call(
        body,
        out_shape=outs,
        in_specs=[pl.BlockSpec(memory_space=pltpu.VMEM)] * len(operands),
        out_specs=[pl.BlockSpec(memory_space=pltpu.VMEM)] * len(outs),
        scratch_shapes=list(scratch),
        compiler_params=pltpu.CompilerParams(vmem_limit_bytes=limit * MIB),
        cost_estimate=pl.CostEstimate(flops=flops, bytes_accessed=moved, transcendentals=0),
    )(*operands)


def swap(value, axis, offset):
    size = lax.axis_size(axis)
    return lax.ppermute(value, axis, [(at, at ^ offset) for at in range(size)])


def gather_patch(value):
    size = lax.axis_size("patch")
    blocks = [value] + [None] * (size - 1)
    for offset in range(2, size, 2):
        blocks[offset] = swap(value, "patch", offset)
    for offset in range(0, size, 2):
        blocks[offset + 1] = swap(blocks[offset], "patch", 1)
    return blocks


def per_device(tokens, modulation, spatial_qkv, spatial_out, temporal_qkv, temporal_out):
    _, rows, width = tokens.shape
    shard = spatial_out.shape[0]
    count, frames = lax.axis_size("patch"), lax.axis_size("frame")
    period = rows // frames
    pieces = frames if period % 16 == 0 else 1
    groups = count // 2
    shape = jax.ShapeDtypeStruct

    blocks = gather_patch(tokens)
    spatial_weights = gather_patch(spatial_out)
    temporal_pair = [temporal_qkv, swap(temporal_qkv, "patch", 1)]
    temporal_weights = gather_patch(temporal_out)

    mixed = call(
        functools.partial(spatial_kernel, count),
        (modulation, spatial_qkv, *blocks),
        [shape((shard, rows), BF16)] * count,
        [pltpu.VMEM((3 * shard, count * rows), F32), pltpu.VMEM((shard, count * rows), F32)],
        flops=2 * count * rows * 3 * shard * width,
    )
    returned = [swap(mixed[at], "patch", at) if at else mixed[0] for at in range(count)]
    middle, *parts = call(
        functools.partial(middle_kernel, count, pieces),
        (modulation, tokens, *returned, *spatial_weights),
        [shape((rows, width), BF16)] + [shape((rows // pieces, width), BF16)] * pieces,
        [pltpu.VMEM((rows, width), BF16)],
        flops=2 * rows * width * width,
    )

    def exchange_frames(parts):
        if pieces > 1:
            return [swap(parts[at], "frame", at) if at else parts[0] for at in range(pieces)]
        return [lax.all_to_all(parts[0], "frame", split_axis=0, concat_axis=0, tiled=True)]

    parts = exchange_frames(parts)
    segments = list(parts)
    for group in range(1, groups):
        segments += [swap(part, "patch", 2 * group) for part in parts]
    mixed = call(
        functools.partial(temporal_kernel, groups, pieces, 2, period),
        (*temporal_pair, *segments),
        [shape((2 * shard, rows), BF16)] * groups,
        [pltpu.VMEM((6 * shard, groups * rows), F32), pltpu.VMEM((2 * shard, groups * rows), F32)],
        flops=2 * groups * rows * 6 * shard * width,
    )
    returned = [swap(mixed[at], "patch", 2 * at) if at else mixed[0] for at in range(groups)]
    parts = call(
        functools.partial(update_kernel, groups, pieces),
        (*returned, *temporal_weights),
        [shape((rows // pieces, width), BF16)] * pieces,
        flops=2 * rows * width * width,
    )
    parts = exchange_frames(parts)
    (result,) = call(
        functools.partial(result_kernel, pieces),
        (modulation, middle, *parts),
        [shape((1, rows, width), BF16)],
    )
    return result


def solution(mesh):
    in_specs = (
        P("frame", "patch", None),
        P(),
        P("patch", None),
        P("patch", None),
        P("patch", None),
        P("patch", None),
    )
    out_specs = P("frame", "patch", None)
    return jax.shard_map(
        per_device, mesh=mesh, in_specs=in_specs, out_specs=out_specs, check_vma=False
    )
```

time: 158 us -> 111 us (0.70)
  starting transfers between devices: 5.81 us -> 51.2 us
  blocking collectives: 37.9 us -> 0 us
  matrix products: 22.7 us -> 0 us
  local copies, waits for them, and re-layouts: 21.7 us -> 3.3 us
  between operations: 13.3 us -> 0.08 us
  other arithmetic: 11.5 us -> 0 us
  Pallas kernels: 0 us -> 11 us
    ppermute x0 -> x36, starting transfers between devices: none -> 51.2 us  [swap(): return lax.ppermute(value, axis, [(at, at ^ offset) for at in range(size)])]
    ppermute x0 -> x36, waiting for transfers between devices: none -> 45.6 us  [swap(): return lax.ppermute(value, axis, [(at, at ^ offset) for at in range(size)])]
    all_to_all x3 -> x0, blocking collectives: 37.9 us -> none  [the longest x1 15.7 us: per_device(): lax.all_to_all(temporal_in, 'frame', split_axis=1, concat_axis=0, tiled=T...]
    all_gather x4 -> x0, waiting for transfers between devices: 33.9 us -> none  [the longest x1 19.5 us: per_device(): lax.all_gather(spatial_in, 'patch', axis=1, tiled=True)]
    dot_general x6 -> x0, matrix products: 16.2 us -> none  [the longest x2 5.86 us: project_rows(): lax.dot_general(flat_rows, weight_rows, (((1,), (1,)), ((), ())), preferr...]
    pallas_call x0 -> x5, Pallas kernels: none -> 11 us  [call(): pl.pallas_call(body, out_shape=outs, in_specs=[pl.BlockSpec(memory_space=...]
    all_to_all x1 -> x0, waiting for transfers between devices: 9.18 us -> none  [per_device(): lax.all_to_all(lax.all_to_all(temporal_heads, 'patch', split_axis=1, conc...]
    unnamed x17 -> x14, local copies, waits for them, and re-layouts: 11.5 us -> 3.3 us
  transfers between devices with their start and end apart: 5 -> 36, of which waited for: 3 -> 21; matrix products, arithmetic and copies ran while one was open for 25% -> 0% of each run, Pallas kernels for 0% -> 9%
where the time goes in v1:
time: 111 us
  starting transfers between devices  51.2 us (46%)
  waiting for transfers between devices  45.6 us (41%)
  Pallas kernels  11 us (10%)
  local copies, waits for them, and re-layouts  3.3 us (3%)
    ppermute x36, starting transfers between devices, swap(): return lax.ppermute(value, axis, [(at, at ^ offset) for at in range(size)])  51.2 us
    ppermute x36, waiting for transfers between devices, swap(): return lax.ppermute(value, axis, [(at, at ^ offset) for at in range(size)])  45.6 us
    pallas_call x5, Pallas kernels, call(): pl.pallas_call(body, out_shape=outs, in_specs=[pl.BlockSpec(memory_space=...  11 us
    unnamed x14, local copies, waits for them, and re-layouts  3.3 us
  transfers between devices with their start and end apart: 36, of which 21 were waited for; matrix products, arithmetic and copies ran while one was open for 0% of the time, Pallas kernels for 9%

profile of v1, /device:TPU:0, one launch (start us, length us, event | category | flops | bytes accessed | tf_op | source)
XLA Modules:
  0.0 111.2 jit_solution(8012773797482223178)
XLA Ops:
  0.5 2.6 %collective-permute-start.7 = (bf16[288,1152]{1,0:T(8,128)(2,1)}, bf16[288,1152]{1,0:T(8,128)(2,1)S(1)}, u32[]{:S(2)}, u32[]{:S(2)}) collective-permute-start(bf16[288,1152]{1,0:T(8,128)(2,1)} %refs_4_.1), channel_id=1, source_target_pairs={{0,2},{1,3},{2,0},{3,1},{4,6},{5,7},{6,4},{7,5},{8,10},{9,11},{10,... | collective-permute-start | bytes 1990664 | tf_op jit(solution)/shard_map/ppermute | solution.py:151
  3.6 1.3 %collective-permute-done.refs_1_ = bf16[1,128,1152]{2,1,0:T(8,128)(2,1)S(1)} collective-permute-done((bf16[1,128,1152]{2,1,0:T(8,128)(2,1)}, bf16[1,128,1152]{2,1,0:T(8,128)(2,1)S(1)}, u32[]{:S(2)}, u32[]{:S(2)}) %collective-permute-start) | collective-permute-done | bytes 294944 | tf_op jit(solution)/shard_map/ppermute | solution.py:151
  4.8 2.8 %collective-permute-start.27 = (bf16[288,1152]{1,0:T(8,128)(2,1)}, bf16[288,1152]{1,0:T(8,128)(2,1)S(1)}, u32[]{:S(2)}, u32[]{:S(2)}) collective-permute-start(bf16[288,1152]{1,0:T(8,128)(2,1)} %refs_2_.1), channel_id=1, source_target_pairs={{0,2},{1,3},{2,0},{3,1},{4,6},{5,7},{6,4},{7,5},{8,10},{9,11},{10,... | collective-permute-start | bytes 1990664 | tf_op jit(solution)/shard_map/ppermute | solution.py:151
  7.6 11.4 %collective-permute-done.7.refs_6_ = bf16[288,1152]{1,0:T(8,128)(2,1)S(1)} collective-permute-done((bf16[288,1152]{1,0:T(8,128)(2,1)}, bf16[288,1152]{1,0:T(8,128)(2,1)S(1)}, u32[]{:S(2)}, u32[]{:S(2)}) %collective-permute-start.7) | collective-permute-done | bytes 663584 | tf_op jit(solution)/shard_map/ppermute | solution.py:151
  19.0 6.3 %collective-permute-done.1.refs_2_ = bf16[1,128,1152]{2,1,0:T(8,128)(2,1)S(1)} collective-permute-done((bf16[1,128,1152]{2,1,0:T(8,128)(2,1)}, bf16[1,128,1152]{2,1,0:T(8,128)(2,1)S(1)}, u32[]{:S(2)}, u32[]{:S(2)}) %collective-permute-start.1) | collective-permute-done | bytes 294944 | tf_op jit(solution)/shard_map/ppermute | solution.py:151
  25.3 1.6 %collective-permute-done.2.refs_3_ = bf16[1,128,1152]{2,1,0:T(8,128)(2,1)S(1)} collective-permute-done((bf16[1,128,1152]{2,1,0:T(8,128)(2,1)S(1)}, bf16[1,128,1152]{2,1,0:T(8,128)(2,1)S(1)}, u32[]{:S(2)}, u32[]{:S(2)}) %collective-permute-start.2) | collective-permute-done | bytes 294944 | tf_op jit(solution)/shard_map/ppermute | solution.py:151
  28.7 1.6 %copy-done.6 = bf16[864,1152]{1,0:T(8,128)(2,1)S(1)} copy-done((bf16[864,1152]{1,0:T(8,128)(2,1)S(1)}, bf16[864,1152]{1,0:T(8,128)(2,1)}, u32[]{:S(2)}) %copy-start.6) | copy-done | bytes 1990680
  30.2 5.7 %shard_map.64 = (bf16[288,128]{1,0:T(8,128)(2,1)S(1)}, bf16[288,128]{1,0:T(8,128)(2,1)S(1)}, bf16[288,128]{1,0:T(8,128)(2,1)S(1)}, bf16[288,128]{1,0:T(8,128)(2,1)S(1)}) custom-call(f32[6,1152]{1,0:T(8,128)S(1)} %copy-done.4, bf16[864,1152]{1,0:T(8,128)(2,1)S(1)} %copy-done.6, bf16[1,128,1152]{2,1,0:T(8,128)(2,1)S(1)} %copy-done.3, ...), custom_call_target="tpu_custom_call" | custom-call | flops 1019215872 | bytes 3492864 | tf_op jit(solution)/shard_map/pallas_call | solution.py:138
  36.1 2.0 %collective-permute-start.4 = (bf16[288,128]{1,0:T(8,128)(2,1)S(1)}, bf16[288,128]{1,0:T(8,128)(2,1)S(1)}, u32[]{:S(2)}, u32[]{:S(2)}) collective-permute-start(bf16[288,128]{1,0:T(8,128)(2,1)S(1)} %get-tuple-element.30), channel_id=1, source_target_pairs={{0,2},{1,3},{2,0},{3,1},{4,6},{5,7},{6,4},{7,5},{8,10},{9,11},{10,... | collective-permute-start | bytes 221192 | tf_op jit(solution)/shard_map/ppermute | solution.py:151
  38.1 1.2 %collective-permute-done.27.refs_4_ = bf16[288,1152]{1,0:T(8,128)(2,1)S(1)} collective-permute-done((bf16[288,1152]{1,0:T(8,128)(2,1)}, bf16[288,1152]{1,0:T(8,128)(2,1)S(1)}, u32[]{:S(2)}, u32[]{:S(2)}) %collective-permute-start.27) | collective-permute-done | bytes 663584 | tf_op jit(solution)/shard_map/ppermute | solution.py:151
  41.8 3.3 %collective-permute-done.5.refs_3_ = bf16[288,128]{1,0:T(8,128)(2,1)S(1)} collective-permute-done((bf16[288,128]{1,0:T(8,128)(2,1)S(1)}, bf16[288,128]{1,0:T(8,128)(2,1)S(1)}, u32[]{:S(2)}, u32[]{:S(2)}) %collective-permute-start.5) | collective-permute-done | bytes 73760 | tf_op jit(solution)/shard_map/ppermute | solution.py:151
  46.1 2.0 %collective-permute-start.10 = (bf16[16,1152]{1,0:T(8,128)(2,1)S(1)}, bf16[16,1152]{1,0:T(8,128)(2,1)S(1)}, u32[]{:S(2)}, u32[]{:S(2)}) collective-permute-start(bf16[16,1152]{1,0:T(8,128)(2,1)S(1)} %get-tuple-element.34), channel_id=1, source_target_pairs={{0,4},{4,0},{8,12},{12,8},{16,20},{20,16},{24,28},{28,24},{1,5},{5... | collective-permute-start | bytes 110600 | tf_op jit(solution)/shard_map/ppermute | solution.py:151
  48.1 1.6 %collective-permute-start.11 = (bf16[16,1152]{1,0:T(8,128)(2,1)S(1)}, bf16[16,1152]{1,0:T(8,128)(2,1)S(1)}, u32[]{:S(2)}, u32[]{:S(2)}) collective-permute-start(bf16[16,1152]{1,0:T(8,128)(2,1)S(1)} %get-tuple-element.35), channel_id=1, source_target_pairs={{0,8},{4,12},{8,0},{12,4},{16,24},{20,28},{24,16},{28,20},{1,9},{5... | collective-permute-start | bytes 110600 | tf_op jit(solution)/shard_map/ppermute | solution.py:151
  50.1 3.0 %collective-permute-start.12 = (bf16[16,1152]{1,0:T(8,128)(2,1)S(1)}, bf16[16,1152]{1,0:T(8,128)(2,1)S(1)}, u32[]{:S(2)}, u32[]{:S(2)}) collective-permute-start(bf16[16,1152]{1,0:T(8,128)(2,1)S(1)} %get-tuple-element.36), channel_id=1, source_target_pairs={{0,12},{4,8},{8,4},{12,0},{16,28},{20,24},{24,20},{28,16},{1,13},{... | collective-permute-start | bytes 110600 | tf_op jit(solution)/shard_map/ppermute | solution.py:151
  53.1 2.6 %collective-permute-start.13 = (bf16[16,1152]{1,0:T(8,128)(2,1)S(1)}, bf16[16,1152]{1,0:T(8,128)(2,1)S(1)}, u32[]{:S(2)}, u32[]{:S(2)}) collective-permute-start(bf16[16,1152]{1,0:T(8,128)(2,1)S(1)} %get-tuple-element.37), channel_id=1, source_target_pairs={{0,16},{4,20},{8,24},{12,28},{16,0},{20,4},{24,8},{28,12},{1,17},{... | collective-permute-start | bytes 110600 | tf_op jit(solution)/shard_map/ppermute | solution.py:151
  55.7 3.3 %collective-permute-start.14 = (bf16[16,1152]{1,0:T(8,128)(2,1)S(1)}, bf16[16,1152]{1,0:T(8,128)(2,1)S(1)}, u32[]{:S(2)}, u32[]{:S(2)}) collective-permute-start(bf16[16,1152]{1,0:T(8,128)(2,1)S(1)} %get-tuple-element.38), channel_id=1, source_target_pairs={{0,20},{4,16},{8,28},{12,24},{16,4},{20,0},{24,12},{28,8},{1,21},{... | collective-permute-start | bytes 110600 | tf_op jit(solution)/shard_map/ppermute | solution.py:151
  59.0 1.6 %collective-permute-start.15 = (bf16[16,1152]{1,0:T(8,128)(2,1)S(1)}, bf16[16,1152]{1,0:T(8,128)(2,1)S(1)}, u32[]{:S(2)}, u32[]{:S(2)}) collective-permute-start(bf16[16,1152]{1,0:T(8,128)(2,1)S(1)} %get-tuple-element.39), channel_id=1, source_target_pairs={{0,24},{4,28},{8,16},{12,20},{16,8},{20,12},{24,0},{28,4},{1,25},{... | collective-permute-start | bytes 110600 | tf_op jit(solution)/shard_map/ppermute | solution.py:151
  61.6 4.4 %collective-permute-start.16 = (bf16[16,1152]{1,0:T(8,128)(2,1)S(1)}, bf16[16,1152]{1,0:T(8,128)(2,1)S(1)}, u32[]{:S(2)}, u32[]{:S(2)}) collective-permute-start(bf16[16,1152]{1,0:T(8,128)(2,1)S(1)} %get-tuple-element.40), channel_id=1, source_target_pairs={{0,28},{4,24},{8,20},{12,16},{16,12},{20,8},{24,4},{28,0},{1,29},{... | collective-permute-start | bytes 110600 | tf_op jit(solution)/shard_map/ppermute | solution.py:151
  66.0 1.5 %collective-permute-start.17 = (bf16[16,1152]{1,0:T(8,128)(2,1)S(1)}, bf16[16,1152]{1,0:T(8,128)(2,1)S(1)}, u32[]{:S(2)}, u32[]{:S(2)}) collective-permute-start(bf16[16,1152]{1,0:T(8,128)(2,1)S(1)} %get-tuple-element.33.refs_2_), channel_id=1, source_target_pairs={{0,2},{1,3},{2,0},{3,1},{4,6},{5,7},{6,4},{7,5},{8,10},{9,11},{10,... | collective-permute-start | bytes 110600 | tf_op jit(solution)/shard_map/ppermute | solution.py:151
  70.0 1.5 %collective-permute-start.19 = (bf16[16,1152]{1,0:T(8,128)(2,1)S(1)}, bf16[16,1152]{1,0:T(8,128)(2,1)S(1)}, u32[]{:S(2)}, u32[]{:S(2)}) collective-permute-start(bf16[16,1152]{1,0:T(8,128)(2,1)S(1)} %collective-permute-done.11.refs_4_), channel_id=1, source_target_pairs={{0,2},{1,3},{2,0},{3,1},{4,6},{5,7},{6,4},{7,5},{8,10},{9,11},{10,... | collective-permute-start | bytes 110600 | tf_op jit(solution)/shard_map/ppermute | solution.py:151
  74.2 1.5 %collective-permute-start.21 = (bf16[16,1152]{1,0:T(8,128)(2,1)S(1)}, bf16[16,1152]{1,0:T(8,128)(2,1)S(1)}, u32[]{:S(2)}, u32[]{:S(2)}) collective-permute-start(bf16[16,1152]{1,0:T(8,128)(2,1)S(1)} %collective-permute-done.13.refs_6_), channel_id=1, source_target_pairs={{0,2},{1,3},{2,0},{3,1},{4,6},{5,7},{6,4},{7,5},{8,10},{9,11},{10,... | collective-permute-start | bytes 110600 | tf_op jit(solution)/shard_map/ppermute | solution.py:151
  78.2 1.5 %collective-permute-start.23 = (bf16[16,1152]{1,0:T(8,128)(2,1)S(1)}, bf16[16,1152]{1,0:T(8,128)(2,1)S(1)}, u32[]{:S(2)}, u32[]{:S(2)}) collective-permute-start(bf16[16,1152]{1,0:T(8,128)(2,1)S(1)} %collective-permute-done.15.refs_8_), channel_id=1, source_target_pairs={{0,2},{1,3},{2,0},{3,1},{4,6},{5,7},{6,4},{7,5},{8,10},{9,11},{10,... | collective-permute-start | bytes 110600 | tf_op jit(solution)/shard_map/ppermute | solution.py:151
  82.1 2.4 %collective-permute-done.24.refs_17_ = bf16[16,1152]{1,0:T(8,128)(2,1)S(1)} collective-permute-done((bf16[16,1152]{1,0:T(8,128)(2,1)S(1)}, bf16[16,1152]{1,0:T(8,128)(2,1)S(1)}, u32[]{:S(2)}, u32[]{:S(2)}) %collective-permute-start.24) | collective-permute-done | bytes 36896 | tf_op jit(solution)/shard_map/ppermute | solution.py:151
  84.5 2.9 %shard_map.66 = (bf16[576,128]{1,0:T(8,128)(2,1)S(1)}, bf16[576,128]{1,0:T(8,128)(2,1)S(1)}) custom-call(bf16[864,1152]{1,0:T(8,128)(2,1)S(1)} %copy-done, bf16[864,1152]{1,0:T(8,128)(2,1)S(1)} %collective-permute-done.9.refs_1_, bf16[16,1152]{1,0:T(8,128)(2,1)S(1)} %get-tuple-element.33.refs_2_, bf16[16,1152]{1,0:T(8,128)(2,1)S(1)} %collective-permute-done.10.refs_3_, ...), custom_call_target="tpu_custom_call" | custom-call | flops 1019215872 | bytes 4866048 | tf_op jit(solution)/shard_map/pallas_call | solution.py:138
  88.5 4.1 %collective-permute-done.25.refs_1_ = bf16[576,128]{1,0:T(8,128)(2,1)S(1)} collective-permute-done((bf16[576,128]{1,0:T(8,128)(2,1)S(1)}, bf16[576,128]{1,0:T(8,128)(2,1)S(1)}, u32[]{:S(2)}, u32[]{:S(2)}) %collective-permute-start.25) | collective-permute-done | bytes 147488 | tf_op jit(solution)/shard_map/ppermute | solution.py:151
  93.3 1.5 %collective-permute-start.29 = (bf16[16,1152]{1,0:T(8,128)(2,1)S(1)}, bf16[16,1152]{1,0:T(8,128)(2,1)S(1)}, u32[]{:S(2)}, u32[]{:S(2)}) collective-permute-start(bf16[16,1152]{1,0:T(8,128)(2,1)S(1)} %get-tuple-element.44), channel_id=1, source_target_pairs={{0,4},{4,0},{8,12},{12,8},{16,20},{20,16},{24,28},{28,24},{1,5},{5... | collective-permute-start | bytes 110600 | tf_op jit(solution)/shard_map/ppermute | solution.py:151
  94.8 2.0 %collective-permute-start.31 = (bf16[16,1152]{1,0:T(8,128)(2,1)S(1)}, bf16[16,1152]{1,0:T(8,128)(2,1)S(1)}, u32[]{:S(2)}, u32[]{:S(2)}) collective-permute-start(bf16[16,1152]{1,0:T(8,128)(2,1)S(1)} %get-tuple-element.46), channel_id=1, source_target_pairs={{0,12},{4,8},{8,4},{12,0},{16,28},{20,24},{24,20},{28,16},{1,13},{... | collective-permute-start | bytes 110600 | tf_op jit(solution)/shard_map/ppermute | solution.py:151
  96.9 1.8 %collective-permute-start.32 = (bf16[16,1152]{1,0:T(8,128)(2,1)S(1)}, bf16[16,1152]{1,0:T(8,128)(2,1)S(1)}, u32[]{:S(2)}, u32[]{:S(2)}) collective-permute-start(bf16[16,1152]{1,0:T(8,128)(2,1)S(1)} %get-tuple-element.47), channel_id=1, source_target_pairs={{0,16},{4,20},{8,24},{12,28},{16,0},{20,4},{24,8},{28,12},{1,17},{... | collective-permute-start | bytes 110600 | tf_op jit(solution)/shard_map/ppermute | solution.py:151
  98.6 2.0 %collective-permute-start.33 = (bf16[16,1152]{1,0:T(8,128)(2,1)S(1)}, bf16[16,1152]{1,0:T(8,128)(2,1)S(1)}, u32[]{:S(2)}, u32[]{:S(2)}) collective-permute-start(bf16[16,1152]{1,0:T(8,128)(2,1)S(1)} %get-tuple-element.48), channel_id=1, source_target_pairs={{0,20},{4,16},{8,28},{12,24},{16,4},{20,0},{24,12},{28,8},{1,21},{... | collective-permute-start | bytes 110600 | tf_op jit(solution)/shard_map/ppermute | solution.py:151
  100.7 3.0 %collective-permute-start.34 = (bf16[16,1152]{1,0:T(8,128)(2,1)S(1)}, bf16[16,1152]{1,0:T(8,128)(2,1)S(1)}, u32[]{:S(2)}, u32[]{:S(2)}) collective-permute-start(bf16[16,1152]{1,0:T(8,128)(2,1)S(1)} %get-tuple-element.49), channel_id=1, source_target_pairs={{0,24},{4,28},{8,16},{12,20},{16,8},{20,12},{24,0},{28,4},{1,25},{... | collective-permute-start | bytes 110600 | tf_op jit(solution)/shard_map/ppermute | solution.py:151
  104.5 2.0 %collective-permute-done.34.refs_6_ = bf16[16,1152]{1,0:T(8,128)(2,1)S(1)} collective-permute-done((bf16[16,1152]{1,0:T(8,128)(2,1)S(1)}, bf16[16,1152]{1,0:T(8,128)(2,1)S(1)}, u32[]{:S(2)}, u32[]{:S(2)}) %collective-permute-start.34) | collective-permute-done | bytes 36896 | tf_op jit(solution)/shard_map/ppermute | solution.py:151
  106.5 3.8 %collective-permute-done.35.refs_7_ = bf16[16,1152]{1,0:T(8,128)(2,1)S(1)} collective-permute-done((bf16[16,1152]{1,0:T(8,128)(2,1)S(1)}, bf16[16,1152]{1,0:T(8,128)(2,1)S(1)}, u32[]{:S(2)}, u32[]{:S(2)}) %collective-permute-start.35) | collective-permute-done | bytes 36896 | tf_op jit(solution)/shard_map/ppermute | solution.py:151
  (59 shorter events, 21.3 us)
Async XLA Ops:
  0.0 84.5 %collective-permute-start.9 = (bf16[864,1152]{1,0:T(8,128)(2,1)}, bf16[864,1152]{1,0:T(8,128)(2,1)S(1)}, u32[]{:S(2)}, u32[]{:S(2)}) collective-permute-start(bf16[864,1152]{1,0:T(8,128)(2,1)} %refs_0_.3), channel_id=1, source_target_pairs={{0,1},{1,0},{2,3},{3,2},{4,5},{5,4},{6,7},{7,6},{8,9},{9,8},{10,11... | collective-permute-start | bytes 5971976 | tf_op jit(solution)/shard_map/ppermute | solution.py:151
  0.5 18.6 %collective-permute-start.7 = (bf16[288,1152]{1,0:T(8,128)(2,1)}, bf16[288,1152]{1,0:T(8,128)(2,1)S(1)}, u32[]{:S(2)}, u32[]{:S(2)}) collective-permute-start(bf16[288,1152]{1,0:T(8,128)(2,1)} %refs_4_.1), channel_id=1, source_target_pairs={{0,2},{1,3},{2,0},{3,1},{4,6},{5,7},{6,4},{7,5},{8,10},{9,11},{10,... | collective-permute-start | bytes 1990664 | tf_op jit(solution)/shard_map/ppermute | solution.py:151
  3.2 22.1 %collective-permute-start.1 = (bf16[1,128,1152]{2,1,0:T(8,128)(2,1)}, bf16[1,128,1152]{2,1,0:T(8,128)(2,1)S(1)}, u32[]{:S(2)}, u32[]{:S(2)}) collective-permute-start(bf16[1,128,1152]{2,1,0:T(8,128)(2,1)} %token_ref.1), channel_id=1, source_target_pairs={{0,2},{1,3},{2,0},{3,1},{4,6},{5,7},{6,4},{7,5},{8,10},{9,11},{10,... | collective-permute-start | bytes 884744 | tf_op jit(solution)/shard_map/ppermute | solution.py:151
  3.5 32.6 %collective-permute-start.6 = (bf16[288,1152]{1,0:T(8,128)(2,1)}, bf16[288,1152]{1,0:T(8,128)(2,1)S(1)}, u32[]{:S(2)}, u32[]{:S(2)}) collective-permute-start(bf16[288,1152]{1,0:T(8,128)(2,1)} %refs_4_.1), channel_id=1, source_target_pairs={{0,1},{1,0},{2,3},{3,2},{4,5},{5,4},{6,7},{7,6},{8,9},{9,8},{10,11... | collective-permute-start | bytes 1990664 | tf_op jit(solution)/shard_map/ppermute | solution.py:151
  4.8 34.5 %collective-permute-start.27 = (bf16[288,1152]{1,0:T(8,128)(2,1)}, bf16[288,1152]{1,0:T(8,128)(2,1)S(1)}, u32[]{:S(2)}, u32[]{:S(2)}) collective-permute-start(bf16[288,1152]{1,0:T(8,128)(2,1)} %refs_2_.1), channel_id=1, source_target_pairs={{0,2},{1,3},{2,0},{3,1},{4,6},{5,7},{6,4},{7,5},{8,10},{9,11},{10,... | collective-permute-start | bytes 1990664 | tf_op jit(solution)/shard_map/ppermute | solution.py:151
  19.0 26.1 %collective-permute-start.8 = (bf16[288,1152]{1,0:T(8,128)(2,1)S(1)}, bf16[288,1152]{1,0:T(8,128)(2,1)S(1)}, u32[]{:S(2)}, u32[]{:S(2)}) collective-permute-start(bf16[288,1152]{1,0:T(8,128)(2,1)S(1)} %collective-permute-done.7.refs_6_), channel_id=1, source_target_pairs={{0,1},{1,0},{2,3},{3,2},{4,5},{5,4},{6,7},{7,6},{8,9},{9,8},{10,11... | collective-permute-start | bytes 1990664 | tf_op jit(solution)/shard_map/ppermute | solution.py:151
  36.1 4.8 %collective-permute-start.4 = (bf16[288,128]{1,0:T(8,128)(2,1)S(1)}, bf16[288,128]{1,0:T(8,128)(2,1)S(1)}, u32[]{:S(2)}, u32[]{:S(2)}) collective-permute-start(bf16[288,128]{1,0:T(8,128)(2,1)S(1)} %get-tuple-element.30), channel_id=1, source_target_pairs={{0,2},{1,3},{2,0},{3,1},{4,6},{5,7},{6,4},{7,5},{8,10},{9,11},{10,... | collective-permute-start | bytes 221192 | tf_op jit(solution)/shard_map/ppermute | solution.py:151
  39.3 49.2 %collective-permute-start.26 = (bf16[288,1152]{1,0:T(8,128)(2,1)S(1)}, bf16[288,1152]{1,0:T(8,128)(2,1)S(1)}, u32[]{:S(2)}, u32[]{:S(2)}) collective-permute-start(bf16[288,1152]{1,0:T(8,128)(2,1)S(1)} %copy-done.2), channel_id=1, source_target_pairs={{0,1},{1,0},{2,3},{3,2},{4,5},{5,4},{6,7},{7,6},{8,9},{9,8},{10,11... | collective-permute-start | bytes 1990664 | tf_op jit(solution)/shard_map/ppermute | solution.py:151
  39.3 49.2 %collective-permute-start.28 = (bf16[288,1152]{1,0:T(8,128)(2,1)S(1)}, bf16[288,1152]{1,0:T(8,128)(2,1)S(1)}, u32[]{:S(2)}, u32[]{:S(2)}) collective-permute-start(bf16[288,1152]{1,0:T(8,128)(2,1)S(1)} %collective-permute-done.27.refs_4_), channel_id=1, source_target_pairs={{0,1},{1,0},{2,3},{3,2},{4,5},{5,4},{6,7},{7,6},{8,9},{9,8},{10,11... | collective-permute-start | bytes 1990664 | tf_op jit(solution)/shard_map/ppermute | solution.py:151
  40.9 4.3 %collective-permute-start.5 = (bf16[288,128]{1,0:T(8,128)(2,1)S(1)}, bf16[288,128]{1,0:T(8,128)(2,1)S(1)}, u32[]{:S(2)}, u32[]{:S(2)}) collective-permute-start(bf16[288,128]{1,0:T(8,128)(2,1)S(1)} %get-tuple-element.31), channel_id=1, source_target_pairs={{0,3},{1,2},{2,1},{3,0},{4,7},{5,6},{6,5},{7,4},{8,11},{9,10},{10,... | collective-permute-start | bytes 221192 | tf_op jit(solution)/shard_map/ppermute | solution.py:151
  46.1 4.0 %collective-permute-start.10 = (bf16[16,1152]{1,0:T(8,128)(2,1)S(1)}, bf16[16,1152]{1,0:T(8,128)(2,1)S(1)}, u32[]{:S(2)}, u32[]{:S(2)}) collective-permute-start(bf16[16,1152]{1,0:T(8,128)(2,1)S(1)} %get-tuple-element.34), channel_id=1, source_target_pairs={{0,4},{4,0},{8,12},{12,8},{16,20},{20,16},{24,28},{28,24},{1,5},{5... | collective-permute-start | bytes 110600 | tf_op jit(solution)/shard_map/ppermute | solution.py:151
  48.1 5.0 %collective-permute-start.11 = (bf16[16,1152]{1,0:T(8,128)(2,1)S(1)}, bf16[16,1152]{1,0:T(8,128)(2,1)S(1)}, u32[]{:S(2)}, u32[]{:S(2)}) collective-permute-start(bf16[16,1152]{1,0:T(8,128)(2,1)S(1)} %get-tuple-element.35), channel_id=1, source_target_pairs={{0,8},{4,12},{8,0},{12,4},{16,24},{20,28},{24,16},{28,20},{1,9},{5... | collective-permute-start | bytes 110600 | tf_op jit(solution)/shard_map/ppermute | solution.py:151
  50.1 5.6 %collective-permute-start.12 = (bf16[16,1152]{1,0:T(8,128)(2,1)S(1)}, bf16[16,1152]{1,0:T(8,128)(2,1)S(1)}, u32[]{:S(2)}, u32[]{:S(2)}) collective-permute-start(bf16[16,1152]{1,0:T(8,128)(2,1)S(1)} %get-tuple-element.36), channel_id=1, source_target_pairs={{0,12},{4,8},{8,4},{12,0},{16,28},{20,24},{24,20},{28,16},{1,13},{... | collective-permute-start | bytes 110600 | tf_op jit(solution)/shard_map/ppermute | solution.py:151
  53.1 5.9 %collective-permute-start.13 = (bf16[16,1152]{1,0:T(8,128)(2,1)S(1)}, bf16[16,1152]{1,0:T(8,128)(2,1)S(1)}, u32[]{:S(2)}, u32[]{:S(2)}) collective-permute-start(bf16[16,1152]{1,0:T(8,128)(2,1)S(1)} %get-tuple-element.37), channel_id=1, source_target_pairs={{0,16},{4,20},{8,24},{12,28},{16,0},{20,4},{24,8},{28,12},{1,17},{... | collective-permute-start | bytes 110600 | tf_op jit(solution)/shard_map/ppermute | solution.py:151
  55.7 6.0 %collective-permute-start.14 = (bf16[16,1152]{1,0:T(8,128)(2,1)S(1)}, bf16[16,1152]{1,0:T(8,128)(2,1)S(1)}, u32[]{:S(2)}, u32[]{:S(2)}) collective-permute-start(bf16[16,1152]{1,0:T(8,128)(2,1)S(1)} %get-tuple-element.38), channel_id=1, source_target_pairs={{0,20},{4,16},{8,28},{12,24},{16,4},{20,0},{24,12},{28,8},{1,21},{... | collective-permute-start | bytes 110600 | tf_op jit(solution)/shard_map/ppermute | solution.py:151
  59.0 7.0 %collective-permute-start.15 = (bf16[16,1152]{1,0:T(8,128)(2,1)S(1)}, bf16[16,1152]{1,0:T(8,128)(2,1)S(1)}, u32[]{:S(2)}, u32[]{:S(2)}) collective-permute-start(bf16[16,1152]{1,0:T(8,128)(2,1)S(1)} %get-tuple-element.39), channel_id=1, source_target_pairs={{0,24},{4,28},{8,16},{12,20},{16,8},{20,12},{24,0},{28,4},{1,25},{... | collective-permute-start | bytes 110600 | tf_op jit(solution)/shard_map/ppermute | solution.py:151
  61.6 6.7 %collective-permute-start.16 = (bf16[16,1152]{1,0:T(8,128)(2,1)S(1)}, bf16[16,1152]{1,0:T(8,128)(2,1)S(1)}, u32[]{:S(2)}, u32[]{:S(2)}) collective-permute-start(bf16[16,1152]{1,0:T(8,128)(2,1)S(1)} %get-tuple-element.40), channel_id=1, source_target_pairs={{0,28},{4,24},{8,20},{12,16},{16,12},{20,8},{24,4},{28,0},{1,29},{... | collective-permute-start | bytes 110600 | tf_op jit(solution)/shard_map/ppermute | solution.py:151
  66.0 4.0 %collective-permute-start.17 = (bf16[16,1152]{1,0:T(8,128)(2,1)S(1)}, bf16[16,1152]{1,0:T(8,128)(2,1)S(1)}, u32[]{:S(2)}, u32[]{:S(2)}) collective-permute-start(bf16[16,1152]{1,0:T(8,128)(2,1)S(1)} %get-tuple-element.33.refs_2_), channel_id=1, source_target_pairs={{0,2},{1,3},{2,0},{3,1},{4,6},{5,7},{6,4},{7,5},{8,10},{9,11},{10,... | collective-permute-start | bytes 110600 | tf_op jit(solution)/shard_map/ppermute | solution.py:151
  68.3 4.0 %collective-permute-start.18 = (bf16[16,1152]{1,0:T(8,128)(2,1)S(1)}, bf16[16,1152]{1,0:T(8,128)(2,1)S(1)}, u32[]{:S(2)}, u32[]{:S(2)}) collective-permute-start(bf16[16,1152]{1,0:T(8,128)(2,1)S(1)} %collective-permute-done.10.refs_3_), channel_id=1, source_target_pairs={{0,2},{1,3},{2,0},{3,1},{4,6},{5,7},{6,4},{7,5},{8,10},{9,11},{10,... | collective-permute-start | bytes 110600 | tf_op jit(solution)/shard_map/ppermute | solution.py:151
  70.0 4.2 %collective-permute-start.19 = (bf16[16,1152]{1,0:T(8,128)(2,1)S(1)}, bf16[16,1152]{1,0:T(8,128)(2,1)S(1)}, u32[]{:S(2)}, u32[]{:S(2)}) collective-permute-start(bf16[16,1152]{1,0:T(8,128)(2,1)S(1)} %collective-permute-done.11.refs_4_), channel_id=1, source_target_pairs={{0,2},{1,3},{2,0},{3,1},{4,6},{5,7},{6,4},{7,5},{8,10},{9,11},{10,... | collective-permute-start | bytes 110600 | tf_op jit(solution)/shard_map/ppermute | solution.py:151
  72.3 4.0 %collective-permute-start.20 = (bf16[16,1152]{1,0:T(8,128)(2,1)S(1)}, bf16[16,1152]{1,0:T(8,128)(2,1)S(1)}, u32[]{:S(2)}, u32[]{:S(2)}) collective-permute-start(bf16[16,1152]{1,0:T(8,128)(2,1)S(1)} %collective-permute-done.12.refs_5_), channel_id=1, source_target_pairs={{0,2},{1,3},{2,0},{3,1},{4,6},{5,7},{6,4},{7,5},{8,10},{9,11},{10,... | collective-permute-start | bytes 110600 | tf_op jit(solution)/shard_map/ppermute | solution.py:151
  74.2 4.0 %collective-permute-start.21 = (bf16[16,1152]{1,0:T(8,128)(2,1)S(1)}, bf16[16,1152]{1,0:T(8,128)(2,1)S(1)}, u32[]{:S(2)}, u32[]{:S(2)}) collective-permute-start(bf16[16,1152]{1,0:T(8,128)(2,1)S(1)} %collective-permute-done.13.refs_6_), channel_id=1, source_target_pairs={{0,2},{1,3},{2,0},{3,1},{4,6},{5,7},{6,4},{7,5},{8,10},{9,11},{10,... | collective-permute-start | bytes 110600 | tf_op jit(solution)/shard_map/ppermute | solution.py:151
  76.3 4.0 %collective-permute-start.22 = (bf16[16,1152]{1,0:T(8,128)(2,1)S(1)}, bf16[16,1152]{1,0:T(8,128)(2,1)S(1)}, u32[]{:S(2)}, u32[]{:S(2)}) collective-permute-start(bf16[16,1152]{1,0:T(8,128)(2,1)S(1)} %collective-permute-done.14.refs_7_), channel_id=1, source_target_pairs={{0,2},{1,3},{2,0},{3,1},{4,6},{5,7},{6,4},{7,5},{8,10},{9,11},{10,... | collective-permute-start | bytes 110600 | tf_op jit(solution)/shard_map/ppermute | solution.py:151
  80.2 4.3 %collective-permute-start.24 = (bf16[16,1152]{1,0:T(8,128)(2,1)S(1)}, bf16[16,1152]{1,0:T(8,128)(2,1)S(1)}, u32[]{:S(2)}, u32[]{:S(2)}) collective-permute-start(bf16[16,1152]{1,0:T(8,128)(2,1)S(1)} %collective-permute-done.16.refs_9_), channel_id=1, source_target_pairs={{0,2},{1,3},{2,0},{3,1},{4,6},{5,7},{6,4},{7,5},{8,10},{9,11},{10,... | collective-permute-start | bytes 110600 | tf_op jit(solution)/shard_map/ppermute | solution.py:151
  87.5 5.2 %collective-permute-start.25 = (bf16[576,128]{1,0:T(8,128)(2,1)S(1)}, bf16[576,128]{1,0:T(8,128)(2,1)S(1)}, u32[]{:S(2)}, u32[]{:S(2)}) collective-permute-start(bf16[576,128]{1,0:T(8,128)(2,1)S(1)} %get-tuple-element.42), channel_id=1, source_target_pairs={{0,2},{1,3},{2,0},{3,1},{4,6},{5,7},{6,4},{7,5},{8,10},{9,11},{10,... | collective-permute-start | bytes 442376 | tf_op jit(solution)/shard_map/ppermute | solution.py:151
  93.3 7.4 %collective-permute-start.29 = (bf16[16,1152]{1,0:T(8,128)(2,1)S(1)}, bf16[16,1152]{1,0:T(8,128)(2,1)S(1)}, u32[]{:S(2)}, u32[]{:S(2)}) collective-permute-start(bf16[16,1152]{1,0:T(8,128)(2,1)S(1)} %get-tuple-element.44), channel_id=1, source_target_pairs={{0,4},{4,0},{8,12},{12,8},{16,20},{20,16},{24,28},{28,24},{1,5},{5... | collective-permute-start | bytes 110600 | tf_op jit(solution)/shard_map/ppermute | solution.py:151
  94.8 8.9 %collective-permute-start.30 = (bf16[16,1152]{1,0:T(8,128)(2,1)S(1)}, bf16[16,1152]{1,0:T(8,128)(2,1)S(1)}, u32[]{:S(2)}, u32[]{:S(2)}) collective-permute-start(bf16[16,1152]{1,0:T(8,128)(2,1)S(1)} %get-tuple-element.45), channel_id=1, source_target_pairs={{0,8},{4,12},{8,0},{12,4},{16,24},{20,28},{24,16},{28,20},{1,9},{5... | collective-permute-start | bytes 110600 | tf_op jit(solution)/shard_map/ppermute | solution.py:151
  94.8 9.7 %collective-permute-start.31 = (bf16[16,1152]{1,0:T(8,128)(2,1)S(1)}, bf16[16,1152]{1,0:T(8,128)(2,1)S(1)}, u32[]{:S(2)}, u32[]{:S(2)}) collective-permute-start(bf16[16,1152]{1,0:T(8,128)(2,1)S(1)} %get-tuple-element.46), channel_id=1, source_target_pairs={{0,12},{4,8},{8,4},{12,0},{16,28},{20,24},{24,20},{28,16},{1,13},{... | collective-permute-start | bytes 110600 | tf_op jit(solution)/shard_map/ppermute | solution.py:151
  96.9 7.7 %collective-permute-start.32 = (bf16[16,1152]{1,0:T(8,128)(2,1)S(1)}, bf16[16,1152]{1,0:T(8,128)(2,1)S(1)}, u32[]{:S(2)}, u32[]{:S(2)}) collective-permute-start(bf16[16,1152]{1,0:T(8,128)(2,1)S(1)} %get-tuple-element.47), channel_id=1, source_target_pairs={{0,16},{4,20},{8,24},{12,28},{16,0},{20,4},{24,8},{28,12},{1,17},{... | collective-permute-start | bytes 110600 | tf_op jit(solution)/shard_map/ppermute | solution.py:151
  98.6 5.9 %collective-permute-start.33 = (bf16[16,1152]{1,0:T(8,128)(2,1)S(1)}, bf16[16,1152]{1,0:T(8,128)(2,1)S(1)}, u32[]{:S(2)}, u32[]{:S(2)}) collective-permute-start(bf16[16,1152]{1,0:T(8,128)(2,1)S(1)} %get-tuple-element.48), channel_id=1, source_target_pairs={{0,20},{4,16},{8,28},{12,24},{16,4},{20,0},{24,12},{28,8},{1,21},{... | collective-permute-start | bytes 110600 | tf_op jit(solution)/shard_map/ppermute | solution.py:151
  100.7 5.9 %collective-permute-start.34 = (bf16[16,1152]{1,0:T(8,128)(2,1)S(1)}, bf16[16,1152]{1,0:T(8,128)(2,1)S(1)}, u32[]{:S(2)}, u32[]{:S(2)}) collective-permute-start(bf16[16,1152]{1,0:T(8,128)(2,1)S(1)} %get-tuple-element.49), channel_id=1, source_target_pairs={{0,24},{4,28},{8,16},{12,20},{16,8},{20,12},{24,0},{28,4},{1,25},{... | collective-permute-start | bytes 110600 | tf_op jit(solution)/shard_map/ppermute | solution.py:151
  103.7 6.7 %collective-permute-start.35 = (bf16[16,1152]{1,0:T(8,128)(2,1)S(1)}, bf16[16,1152]{1,0:T(8,128)(2,1)S(1)}, u32[]{:S(2)}, u32[]{:S(2)}) collective-permute-start(bf16[16,1152]{1,0:T(8,128)(2,1)S(1)} %get-tuple-element.50), channel_id=1, source_target_pairs={{0,28},{4,24},{8,20},{12,16},{16,12},{20,8},{24,4},{28,0},{1,29},{... | collective-permute-start | bytes 110600 | tf_op jit(solution)/shard_map/ppermute | solution.py:151
  (11 other events, 170.0 us)

commit v2 on v1

--- a/solution.py
+++ b/solution.py
@@ -63,24 +63,15 @@
         out_refs[at][...] = heads_ref[:, at * block : (at + 1) * block].astype(BF16)
 
 
-def middle_kernel(count, pieces, mod_ref, token_ref, *refs):
+def middle_kernel(count, mod_ref, token_ref, *refs):
     head_refs, weight_refs = refs[:count], refs[count : 2 * count]
-    middle_ref, piece_refs, scratch = refs[2 * count], refs[2 * count + 1 : -1], refs[-1]
+    middle_ref, normed_ref = refs[2 * count :]
     heads = jnp.concatenate([ref[...] for ref in head_refs], axis=0)
     weights = jnp.concatenate([ref[...] for ref in weight_refs], axis=0)
     update = dot(heads.T, weights)
     middle = (token_ref[0].astype(F32) + mod_ref[2:3, :] * update).astype(BF16)
     middle_ref[...] = middle
-    normed = norm_rows(middle.astype(F32), mod_ref[3:4, :], mod_ref[4:5, :])
-    if pieces == 1:
-        piece_refs[0][...] = normed
-        return
-    scratch[...] = normed
-    here = lax.axis_index("frame")
-    size = normed.shape[0] // pieces
-    for at in range(pieces):
-        start = pl.multiple_of((here ^ at) * size, size)
-        piece_refs[at][...] = scratch[pl.ds(start, size), :]
+    normed_ref[...] = norm_rows(middle.astype(F32), mod_ref[3:4, :], mod_ref[4:5, :])
 
 
 def temporal_kernel(groups, pieces, cores, period, *refs):
@@ -110,27 +101,15 @@
         out_refs[group][...] = heads_ref[:, group * block : (group + 1) * block].astype(BF16)
 
 
-def update_kernel(groups, pieces, *refs):
-    count = len(refs) - groups - pieces
-    head_refs, weight_refs, piece_refs = refs[:groups], refs[groups:-pieces], refs[-pieces:]
-    heads = jnp.concatenate([ref[...] for ref in head_refs], axis=0)
-    weights = jnp.concatenate([ref[...] for ref in weight_refs], axis=0)
-    update = dot(heads.T, weights).astype(BF16)
-    size = update.shape[0] // pieces
-    for at in range(pieces):
-        piece_refs[at][...] = update[at * size : (at + 1) * size]
-
-
-def result_kernel(pieces, mod_ref, middle_ref, *refs):
-    piece_refs, out_ref = refs[:-1], refs[-1]
-    gate = mod_ref[5:6, :]
-    here = lax.axis_index("frame")
-    size = middle_ref.shape[0] // pieces
-    for at in range(pieces):
-        start = pl.multiple_of((here ^ at) * size, size) if pieces > 1 else 0
-        rows = pl.ds(start, size)
-        update = piece_refs[at][...].astype(F32)
-        out_ref[0, rows, :] = (middle_ref[rows, :].astype(F32) + gate * update).astype(BF16)
+def update_kernel(groups, *refs):
+    heads = jnp.concatenate([ref[...] for ref in refs[:groups]], axis=0)
+    weights = jnp.concatenate([ref[...] for ref in refs[groups:-1]], axis=0)
+    refs[-1][...] = dot(heads.T, weights).astype(BF16)
+
+
+def result_kernel(mod_ref, middle_ref, update_ref, out_ref):
+    update = update_ref[...].astype(F32)
+    out_ref[0] = (middle_ref[...].astype(F32) + mod_ref[5:6, :] * update).astype(BF16)
 
 
 def call(body, operands, outs, scratch=(), flops=0, limit=24):
@@ -151,14 +130,17 @@
     return lax.ppermute(value, axis, [(at, at ^ offset) for at in range(size)])
 
 
-def gather_patch(value):
+def after(value, *others):
+    return lax.optimization_barrier((value, *others))[0]
+
+
+def across(value):
     size = lax.axis_size("patch")
-    blocks = [value] + [None] * (size - 1)
-    for offset in range(2, size, 2):
-        blocks[offset] = swap(value, "patch", offset)
-    for offset in range(0, size, 2):
-        blocks[offset + 1] = swap(blocks[offset], "patch", 1)
-    return blocks
+    return [swap(value, "patch", at) if at else value for at in range(0, size, 2)]
+
+
+def both_cores(blocks):
+    return [part for block in blocks for part in (block, swap(block, "patch", 1))]
 
 
 def per_device(tokens, modulation, spatial_qkv, spatial_out, temporal_qkv, temporal_out):
@@ -166,14 +148,20 @@
     shard = spatial_out.shape[0]
     count, frames = lax.axis_size("patch"), lax.axis_size("frame")
     period = rows // frames
-    pieces = frames if period % 16 == 0 else 1
     groups = count // 2
     shape = jax.ShapeDtypeStruct
 
-    blocks = gather_patch(tokens)
-    spatial_weights = gather_patch(spatial_out)
-    temporal_pair = [temporal_qkv, swap(temporal_qkv, "patch", 1)]
-    temporal_weights = gather_patch(temporal_out)
+    def exchange_frames(value):
+        blocks = value.reshape(frames, period, width)
+        blocks = lax.all_to_all(blocks, "frame", split_axis=0, concat_axis=0, tiled=True)
+        return blocks.reshape(rows, width)
+
+    sister = swap(tokens, "patch", 1)
+    far = across(tokens)[1:]
+    early_out = after(spatial_out, sister)
+    near_weights = [spatial_out, swap(early_out, "patch", 1)]
+    far_weights = across(early_out)[1:]
+    blocks = [tokens, sister] + both_cores([after(block, near_weights[1]) for block in far])
 
     mixed = call(
         functools.partial(spatial_kernel, count),
@@ -182,42 +170,39 @@
         [pltpu.VMEM((3 * shard, count * rows), F32), pltpu.VMEM((shard, count * rows), F32)],
         flops=2 * count * rows * 3 * shard * width,
     )
-    returned = [swap(mixed[at], "patch", at) if at else mixed[0] for at in range(count)]
-    middle, *parts = call(
-        functools.partial(middle_kernel, count, pieces),
-        (modulation, tokens, *returned, *spatial_weights),
-        [shape((rows, width), BF16)] + [shape((rows // pieces, width), BF16)] * pieces,
-        [pltpu.VMEM((rows, width), BF16)],
+    returned = list(mixed)
+    for at in reversed(range(1, count)):
+        returned[at] = swap(mixed[at], "patch", at)
+    far_weights = both_cores([after(block, *returned) for block in far_weights])
+    temporal_pair = [temporal_qkv, swap(after(temporal_qkv, returned[1]), "patch", 1)]
+    temporal_weights = across(after(temporal_out, returned[1]))
+    middle, part = call(
+        functools.partial(middle_kernel, count),
+        (modulation, tokens, *returned, *near_weights, *far_weights),
+        [shape((rows, width), BF16)] * 2,
         flops=2 * rows * width * width,
     )
-
-    def exchange_frames(parts):
-        if pieces > 1:
-            return [swap(parts[at], "frame", at) if at else parts[0] for at in range(pieces)]
-        return [lax.all_to_all(parts[0], "frame", split_axis=0, concat_axis=0, tiled=True)]
-
-    parts = exchange_frames(parts)
-    segments = list(parts)
-    for group in range(1, groups):
-        segments += [swap(part, "patch", 2 * group) for part in parts]
+    part = exchange_frames(part)
+    segments = across(part)
+    temporal_weights = both_cores([after(block, *segments) for block in temporal_weights])
     mixed = call(
-        functools.partial(temporal_kernel, groups, pieces, 2, period),
+        functools.partial(temporal_kernel, groups, 1, 2, period),
         (*temporal_pair, *segments),
         [shape((2 * shard, rows), BF16)] * groups,
         [pltpu.VMEM((6 * shard, groups * rows), F32), pltpu.VMEM((2 * shard, groups * rows), F32)],
         flops=2 * groups * rows * 6 * shard * width,
     )
     returned = [swap(mixed[at], "patch", 2 * at) if at else mixed[0] for at in range(groups)]
-    parts = call(
-        functools.partial(update_kernel, groups, pieces),
+    (update,) = call(
+        functools.partial(update_kernel, groups),
         (*returned, *temporal_weights),
-        [shape((rows // pieces, width), BF16)] * pieces,
+        [shape((rows, width), BF16)],
         flops=2 * rows * width * width,
     )
-    parts = exchange_frames(parts)
+    update = exchange_frames(update)
     (result,) = call(
-        functools.partial(result_kernel, pieces),
-        (modulation, middle, *parts),
+        result_kernel,
+        (modulation, middle, update),
         [shape((1, rows, width), BF16)],
     )
     return result

time: 111 us -> 91.6 us (0.83)
  starting transfers between devices: 51.2 us -> 16.6 us
  blocking collectives: 0 us -> 15.1 us
  waiting for transfers between devices: 45.6 us -> 41.9 us
  Pallas kernels: 11 us -> 14.3 us
    ppermute x36 -> x15, starting transfers between devices: 51.2 us -> 10.7 us  [swap(): return lax.ppermute(value, axis, [(at, at ^ offset) for at in range(size)])]
    all_to_all x0 -> x1, blocking collectives: none -> 15.1 us  [exchange_frames(): lax.all_to_all(blocks, 'frame', split_axis=0, concat_axis=0, tiled=True)]
    ppermute x36 -> x15, waiting for transfers between devices: 45.6 us -> 33.3 us  [swap(): return lax.ppermute(value, axis, [(at, at ^ offset) for at in range(size)])]
    all_to_all x0 -> x1, waiting for transfers between devices: none -> 8.59 us  [exchange_frames(): lax.all_to_all(blocks, 'frame', split_axis=0, concat_axis=0, tiled=True)]
    all_to_all x0 -> x1, starting transfers between devices: none -> 5.8 us  [exchange_frames(): lax.all_to_all(blocks, 'frame', split_axis=0, concat_axis=0, tiled=True)]
    pallas_call x5, Pallas kernels: 11 us -> 14.3 us  [call(): pl.pallas_call(body, out_shape=outs, in_specs=[pl.BlockSpec(memory_space=...]
  transfers between devices with their start and end apart: 36 -> 16, of which waited for: 21 -> 10; matrix products, arithmetic and copies ran while one was open for 0% -> 0% of each run, Pallas kernels for 9% -> 13%
where the time goes in v2:
time: 91.6 us; the launch traced here: 91.2 us
  waiting for transfers between devices  41.9 us (46%)
  starting transfers between devices  16.6 us (18%)
  blocking collectives  15.1 us (16%)
  Pallas kernels  14.3 us (16%)
  local copies, waits for them, and re-layouts  3.3 us (4%)
    ppermute x15, waiting for transfers between devices, swap(): return lax.ppermute(value, axis, [(at, at ^ offset) for at in range(size)])  33.3 us
    all_to_all x1, blocking collectives, exchange_frames(): lax.all_to_all(blocks, 'frame', split_axis=0, concat_axis=0, tiled=True)  15.1 us
    pallas_call x5, Pallas kernels, call(): pl.pallas_call(body, out_shape=outs, in_specs=[pl.BlockSpec(memory_space=...  14.3 us
    ppermute x15, starting transfers between devices, swap(): return lax.ppermute(value, axis, [(at, at ^ offset) for at in range(size)])  10.7 us
    all_to_all x1, waiting for transfers between devices, exchange_frames(): lax.all_to_all(blocks, 'frame', split_axis=0, concat_axis=0, tiled=True)  8.59 us
    all_to_all x1, starting transfers between devices, exchange_frames(): lax.all_to_all(blocks, 'frame', split_axis=0, concat_axis=0, tiled=True)  5.8 us
    unnamed x14, local copies, waits for them, and re-layouts  3.3 us
  transfers between devices with their start and end apart: 16, of which 10 were waited for; matrix products, arithmetic and copies ran while one was open for 0% of the time, Pallas kernels for 13%

profile of v2, /device:TPU:0, one launch (start us, length us, event | category | flops | bytes accessed | tf_op | source)
XLA Modules:
  0.0 91.2 jit_solution(460948291703059921)
XLA Ops:
  0.0 0.5 collective-permute-start
  0.5 1.4 %collective-permute-done.refs_1_ = bf16[1,128,1152]{2,1,0:T(8,128)(2,1)S(1)} collective-permute-done((bf16[1,128,1152]{2,1,0:T(8,128)(2,1)}, bf16[1,128,1152]{2,1,0:T(8,128)(2,1)S(1)}, u32[]{:S(2)}, u32[]{:S(2)}) %collective-permute-start) | collective-permute-done | bytes 294944 | tf_op jit(solution)/shard_map/ppermute | solution.py:130
  1.9 0.4 collective-permute-start.2
  2.3 2.7 %collective-permute-start.1 = (bf16[1,128,1152]{2,1,0:T(8,128)(2,1)}, bf16[1,128,1152]{2,1,0:T(8,128)(2,1)S(1)}, u32[]{:S(2)}, u32[]{:S(2)}) collective-permute-start(bf16[1,128,1152]{2,1,0:T(8,128)(2,1)} %token_ref.1), channel_id=1, source_target_pairs={{0,2},{1,3},{2,0},{3,1},{4,6},{5,7},{6,4},{7,5},{8,10},{9,11},{10,... | collective-permute-start | bytes 884744 | tf_op jit(solution)/shard_map/ppermute | solution.py:130
  4.9 0.0 collective-permute-start.7
  5.0 8.0 %collective-permute-done.1.refs_2_ = bf16[1,128,1152]{2,1,0:T(8,128)(2,1)S(1)} collective-permute-done((bf16[1,128,1152]{2,1,0:T(8,128)(2,1)}, bf16[1,128,1152]{2,1,0:T(8,128)(2,1)S(1)}, u32[]{:S(2)}, u32[]{:S(2)}) %collective-permute-start.1) | collective-permute-done | bytes 294944 | tf_op jit(solution)/shard_map/ppermute | solution.py:130
  13.0 1.6 %collective-permute-done.3.refs_3_ = bf16[1,128,1152]{2,1,0:T(8,128)(2,1)S(1)} collective-permute-done((bf16[1,128,1152]{2,1,0:T(8,128)(2,1)S(1)}, bf16[1,128,1152]{2,1,0:T(8,128)(2,1)S(1)}, u32[]{:S(2)}, u32[]{:S(2)}) %collective-permute-start.3) | collective-permute-done | bytes 294944 | tf_op jit(solution)/shard_map/ppermute | solution.py:130
  14.6 1.0 %copy-done.3 = bf16[1,128,1152]{2,1,0:T(8,128)(2,1)S(1)} copy-done((bf16[1,128,1152]{2,1,0:T(8,128)(2,1)S(1)}, bf16[1,128,1152]{2,1,0:T(8,128)(2,1)}, u32[]{:S(2)}) %copy-start.3) | copy-done | bytes 294936
  15.5 0.8 copy-done.4
  16.3 1.6 %copy-done.6 = bf16[864,1152]{1,0:T(8,128)(2,1)S(1)} copy-done((bf16[864,1152]{1,0:T(8,128)(2,1)S(1)}, bf16[864,1152]{1,0:T(8,128)(2,1)}, u32[]{:S(2)}) %copy-start.6) | copy-done | bytes 1990680
  17.8 5.7 %shard_map.64 = (bf16[288,128]{1,0:T(8,128)(2,1)S(1)}, bf16[288,128]{1,0:T(8,128)(2,1)S(1)}, bf16[288,128]{1,0:T(8,128)(2,1)S(1)}, bf16[288,128]{1,0:T(8,128)(2,1)S(1)}) custom-call(f32[6,1152]{1,0:T(8,128)S(1)} %copy-done.4, bf16[864,1152]{1,0:T(8,128)(2,1)S(1)} %copy-done.6, bf16[1,128,1152]{2,1,0:T(8,128)(2,1)S(1)} %copy-done.3, ...), custom_call_target="tpu_custom_call" | custom-call | flops 1019215872 | bytes 3492864 | tf_op jit(solution)/shard_map/pallas_call | solution.py:117
  23.6 0.2 collective-permute-start.4
  23.8 2.0 %collective-permute-start.5 = (bf16[288,128]{1,0:T(8,128)(2,1)S(1)}, bf16[288,128]{1,0:T(8,128)(2,1)S(1)}, u32[]{:S(2)}, u32[]{:S(2)}) collective-permute-start(bf16[288,128]{1,0:T(8,128)(2,1)S(1)} %get-tuple-element.24), channel_id=1, source_target_pairs={{0,2},{1,3},{2,0},{3,1},{4,6},{5,7},{6,4},{7,5},{8,10},{9,11},{10,... | collective-permute-start | bytes 221192 | tf_op jit(solution)/shard_map/ppermute | solution.py:130
  25.8 0.1 collective-permute-start.9
  25.9 0.9 %collective-permute-done.7.refs_6_ = bf16[288,1152]{1,0:T(8,128)(2,1)S(1)} collective-permute-done((bf16[288,1152]{1,0:T(8,128)(2,1)}, bf16[288,1152]{1,0:T(8,128)(2,1)S(1)}, u32[]{:S(2)}, u32[]{:S(2)}) %collective-permute-start.7) | collective-permute-done | bytes 663584 | tf_op jit(solution)/shard_map/ppermute | solution.py:130
  26.9 1.7 %collective-permute-done.5.refs_2_ = bf16[288,128]{1,0:T(8,128)(2,1)S(1)} collective-permute-done((bf16[288,128]{1,0:T(8,128)(2,1)S(1)}, bf16[288,128]{1,0:T(8,128)(2,1)S(1)}, u32[]{:S(2)}, u32[]{:S(2)}) %collective-permute-start.5) | collective-permute-done | bytes 73760 | tf_op jit(solution)/shard_map/ppermute | solution.py:130
  28.6 1.5 %collective-permute-done.6.refs_3_ = bf16[288,128]{1,0:T(8,128)(2,1)S(1)} collective-permute-done((bf16[288,128]{1,0:T(8,128)(2,1)S(1)}, bf16[288,128]{1,0:T(8,128)(2,1)S(1)}, u32[]{:S(2)}, u32[]{:S(2)}) %collective-permute-start.6) | collective-permute-done | bytes 73760 | tf_op jit(solution)/shard_map/ppermute | solution.py:130
  30.1 0.1 collective-permute-start.8
  30.2 2.0 %collective-permute-done.8.refs_7_ = bf16[288,1152]{1,0:T(8,128)(2,1)S(1)} collective-permute-done((bf16[288,1152]{1,0:T(8,128)(2,1)S(1)}, bf16[288,1152]{1,0:T(8,128)(2,1)S(1)}, u32[]{:S(2)}, u32[]{:S(2)}) %collective-permute-start.8) | collective-permute-done | bytes 663584 | tf_op jit(solution)/shard_map/ppermute | solution.py:130
  32.2 1.6 %shard_map.65 = (bf16[128,1152]{1,0:T(8,128)(2,1)S(1)}, bf16[128,1152]{1,0:T(8,128)(2,1)}) custom-call(f32[6,1152]{1,0:T(8,128)S(1)} %copy-done.4, bf16[1,128,1152]{2,1,0:T(8,128)(2,1)S(1)} %copy-done.3, bf16[288,128]{1,0:T(8,128)(2,1)S(1)} %get-tuple-element.22.refs_0_, bf16[288,128]{1,0:T(8,128)(2,1)S(1)} %collective-permute-done.4.refs_1_, ...), custom_call_target="tpu_custom_call" | custom-call | flops 339738624 | bytes 3861504 | tf_op jit(solution)/shard_map/pallas_call | solution.py:117
  33.8 5.8 %all-to-all-start = ((bf16[8,16,1152]{2,1,0:T(8,128)(2,1)}), bf16[8,16,1152]{2,1,0:T(8,128)(2,1)S(1)}, u32[]{:S(2)}, u32[]{:S(2)}) async-start(bf16[8,16,1152]{2,1,0:T(8,128)(2,1)} %bitcast), calls=%async_computation | async-start | bytes 589824 | tf_op jit(solution)/shard_map/all_to_all | solution.py:156
  39.7 1.3 %collective-permute-start.13 = (bf16[288,1152]{1,0:T(8,128)(2,1)S(1)}, bf16[288,1152]{1,0:T(8,128)(2,1)}, u32[]{:S(2)}, u32[]{:S(2)}) collective-permute-start(bf16[288,1152]{1,0:T(8,128)(2,1)S(1)} %copy-done.2), channel_id=1, source_target_pairs={{0,2},{1,3},{2,0},{3,1},{4,6},{5,7},{6,4},{7,5},{8,10},{9,11},{10,... | collective-permute-start | bytes 1990664 | tf_op jit(solution)/shard_map/ppermute | solution.py:130
  40.9 8.6 %all-to-all-done = bf16[8,16,1152]{2,1,0:T(8,128)(2,1)S(1)} async-done(((bf16[8,16,1152]{2,1,0:T(8,128)(2,1)}), bf16[8,16,1152]{2,1,0:T(8,128)(2,1)S(1)}, u32[]{:S(2)}, u32[]{:S(2)}) %all-to-all-start) | async-done | bytes 294944 | tf_op jit(solution)/shard_map/all_to_all | solution.py:156
  49.5 1.4 %collective-permute-start.10 = (bf16[128,1152]{1,0:T(8,128)(2,1)S(1)}, bf16[128,1152]{1,0:T(8,128)(2,1)S(1)}, u32[]{:S(2)}, u32[]{:S(2)}) collective-permute-start(bf16[128,1152]{1,0:T(8,128)(2,1)S(1)} %bitcast.4), channel_id=1, source_target_pairs={{0,2},{1,3},{2,0},{3,1},{4,6},{5,7},{6,4},{7,5},{8,10},{9,11},{10,... | collective-permute-start | bytes 884744 | tf_op jit(solution)/shard_map/ppermute | solution.py:130
  51.0 11.8 %collective-permute-done.10.refs_3_ = bf16[128,1152]{1,0:T(8,128)(2,1)S(1)} collective-permute-done((bf16[128,1152]{1,0:T(8,128)(2,1)S(1)}, bf16[128,1152]{1,0:T(8,128)(2,1)S(1)}, u32[]{:S(2)}, u32[]{:S(2)}) %collective-permute-start.10) | collective-permute-done | bytes 294944 | tf_op jit(solution)/shard_map/ppermute | solution.py:130
  62.7 0.5 collective-permute-start.14
  63.2 4.5 %shard_map.66 = (bf16[576,128]{1,0:T(8,128)(2,1)S(1)}, bf16[576,128]{1,0:T(8,128)(2,1)S(1)}) custom-call(bf16[864,1152]{1,0:T(8,128)(2,1)S(1)} %copy-done, bf16[864,1152]{1,0:T(8,128)(2,1)} %collective-permute-done.9.refs_1_, bf16[128,1152]{1,0:T(8,128)(2,1)S(1)} %bitcast.5, bf16[128,1152]{1,0:T(8,128)(2,1)S(1)} %collective-permute-done.10.refs_3_), custom_call_target="tpu_custom_call" | custom-call | flops 1019215872 | bytes 4866048 | tf_op jit(solution)/shard_map/pallas_call | solution.py:117
  67.7 1.5 %collective-permute-start.11 = (bf16[576,128]{1,0:T(8,128)(2,1)S(1)}, bf16[576,128]{1,0:T(8,128)(2,1)S(1)}, u32[]{:S(2)}, u32[]{:S(2)}) collective-permute-start(bf16[576,128]{1,0:T(8,128)(2,1)S(1)} %get-tuple-element.31), channel_id=1, source_target_pairs={{0,2},{1,3},{2,0},{3,1},{4,6},{5,7},{6,4},{7,5},{8,10},{9,11},{10,... | collective-permute-start | bytes 442376 | tf_op jit(solution)/shard_map/ppermute | solution.py:130
  69.2 4.3 %collective-permute-done.11.refs_1_ = bf16[576,128]{1,0:T(8,128)(2,1)S(1)} collective-permute-done((bf16[576,128]{1,0:T(8,128)(2,1)S(1)}, bf16[576,128]{1,0:T(8,128)(2,1)S(1)}, u32[]{:S(2)}, u32[]{:S(2)}) %collective-permute-start.11) | collective-permute-done | bytes 147488 | tf_op jit(solution)/shard_map/ppermute | solution.py:130
  73.5 1.7 %shard_map.67 = bf16[128,1152]{1,0:T(8,128)(2,1)S(1)} custom-call(bf16[576,128]{1,0:T(8,128)(2,1)S(1)} %get-tuple-element.30.refs_0_, bf16[576,128]{1,0:T(8,128)(2,1)S(1)} %collective-permute-done.11.refs_1_, bf16[288,1152]{1,0:T(8,128)(2,1)S(1)} %copy-done.2, bf16[288,1152]{1,0:T(8,128)(2,1)S(1)} %collective-permute-done.12.refs_3_, ...), custom_call_target="tpu_custom_call" | custom-call | flops 339738624 | bytes 3244032 | tf_op jit(solution)/shard_map/pallas_call | solution.py:117
  75.3 15.1 %all_to_all.10 = bf16[8,16,1152]{2,1,0:T(8,128)(2,1)S(1)} all-to-all(bf16[8,16,1152]{2,1,0:T(8,128)(2,1)S(1)} %bitcast.6), channel_id=1, replica_groups=mesh['frame'=8,'patch'=4] {'frame'}, dimensions={0} | all-to-all | bytes 589824 | tf_op jit(solution)/shard_map/all_to_all | solution.py:156
  90.4 0.8 shard_map.68
  (20 shorter events, 0.0 us)
Async XLA Ops:
  0.0 32.2 %copy-start.1 = (bf16[288,1152]{1,0:T(8,128)(2,1)S(1)}, bf16[288,1152]{1,0:T(8,128)(2,1)}, u32[]{:S(2)}) copy-start(bf16[288,1152]{1,0:T(8,128)(2,1)} %refs_4_.1) | copy-start | bytes 1990660
  0.0 25.8 %copy-start = (bf16[864,1152]{1,0:T(8,128)(2,1)S(1)}, bf16[864,1152]{1,0:T(8,128)(2,1)}, u32[]{:S(2)}) copy-start(bf16[864,1152]{1,0:T(8,128)(2,1)} %refs_0_.3) | copy-start | bytes 5971972
  0.0 1.9 %collective-permute-start = (bf16[1,128,1152]{2,1,0:T(8,128)(2,1)}, bf16[1,128,1152]{2,1,0:T(8,128)(2,1)S(1)}, u32[]{:S(2)}, u32[]{:S(2)}) collective-permute-start(bf16[1,128,1152]{2,1,0:T(8,128)(2,1)} %token_ref.1), channel_id=1, source_target_pairs={{0,1},{1,0},{2,3},{3,2},{4,5},{5,4},{6,7},{7,6},{8,9},{9,8},{10,11... | collective-permute-start | bytes 884744 | tf_op jit(solution)/shard_map/ppermute | solution.py:130
  1.9 11.1 %collective-permute-start.2 = (bf16[288,1152]{1,0:T(8,128)(2,1)}, bf16[288,1152]{1,0:T(8,128)(2,1)S(1)}, u32[]{:S(2)}, u32[]{:S(2)}) collective-permute-start(bf16[288,1152]{1,0:T(8,128)(2,1)} %refs_4_.1), channel_id=1, source_target_pairs={{0,1},{1,0},{2,3},{3,2},{4,5},{5,4},{6,7},{7,6},{8,9},{9,8},{10,11... | collective-permute-start | bytes 1990664 | tf_op jit(solution)/shard_map/ppermute | solution.py:130
  2.3 10.7 %collective-permute-start.1 = (bf16[1,128,1152]{2,1,0:T(8,128)(2,1)}, bf16[1,128,1152]{2,1,0:T(8,128)(2,1)S(1)}, u32[]{:S(2)}, u32[]{:S(2)}) collective-permute-start(bf16[1,128,1152]{2,1,0:T(8,128)(2,1)} %token_ref.1), channel_id=1, source_target_pairs={{0,2},{1,3},{2,0},{3,1},{4,6},{5,7},{6,4},{7,5},{8,10},{9,11},{10,... | collective-permute-start | bytes 884744 | tf_op jit(solution)/shard_map/ppermute | solution.py:130
  4.9 21.9 %collective-permute-start.7 = (bf16[288,1152]{1,0:T(8,128)(2,1)}, bf16[288,1152]{1,0:T(8,128)(2,1)S(1)}, u32[]{:S(2)}, u32[]{:S(2)}) collective-permute-start(bf16[288,1152]{1,0:T(8,128)(2,1)} %refs_4_.1), channel_id=1, source_target_pairs={{0,2},{1,3},{2,0},{3,1},{4,6},{5,7},{6,4},{7,5},{8,10},{9,11},{10,... | collective-permute-start | bytes 1990664 | tf_op jit(solution)/shard_map/ppermute | solution.py:130
  13.0 1.6 %collective-permute-start.3 = (bf16[1,128,1152]{2,1,0:T(8,128)(2,1)S(1)}, bf16[1,128,1152]{2,1,0:T(8,128)(2,1)S(1)}, u32[]{:S(2)}, u32[]{:S(2)}) collective-permute-start(bf16[1,128,1152]{2,1,0:T(8,128)(2,1)S(1)} %collective-permute-done.1.refs_2_), channel_id=1, source_target_pairs={{0,1},{1,0},{2,3},{3,2},{4,5},{5,4},{6,7},{7,6},{8,9},{9,8},{10,11... | collective-permute-start | bytes 884744 | tf_op jit(solution)/shard_map/ppermute | solution.py:130
  14.6 1.0 %copy-start.3 = (bf16[1,128,1152]{2,1,0:T(8,128)(2,1)S(1)}, bf16[1,128,1152]{2,1,0:T(8,128)(2,1)}, u32[]{:S(2)}) copy-start(bf16[1,128,1152]{2,1,0:T(8,128)(2,1)} %token_ref.1) | copy-start | bytes 884740
  15.5 0.8 copy-start.4
  16.3 1.6 %copy-start.6 = (bf16[864,1152]{1,0:T(8,128)(2,1)S(1)}, bf16[864,1152]{1,0:T(8,128)(2,1)}, u32[]{:S(2)}) copy-start(bf16[864,1152]{1,0:T(8,128)(2,1)} %weight_ref.1) | copy-start | bytes 5971972
  23.5 16.1 %copy-start.2 = (bf16[288,1152]{1,0:T(8,128)(2,1)S(1)}, bf16[288,1152]{1,0:T(8,128)(2,1)}, u32[]{:S(2)}) copy-start(bf16[288,1152]{1,0:T(8,128)(2,1)} %refs_2_) | copy-start | bytes 1990660
  23.6 2.2 %collective-permute-start.4 = (bf16[288,128]{1,0:T(8,128)(2,1)S(1)}, bf16[288,128]{1,0:T(8,128)(2,1)S(1)}, u32[]{:S(2)}, u32[]{:S(2)}) collective-permute-start(bf16[288,128]{1,0:T(8,128)(2,1)S(1)} %get-tuple-element.23), channel_id=1, source_target_pairs={{0,1},{1,0},{2,3},{3,2},{4,5},{5,4},{6,7},{7,6},{8,9},{9,8},{10,11... | collective-permute-start | bytes 221192 | tf_op jit(solution)/shard_map/ppermute | solution.py:130
  23.8 4.8 %collective-permute-start.5 = (bf16[288,128]{1,0:T(8,128)(2,1)S(1)}, bf16[288,128]{1,0:T(8,128)(2,1)S(1)}, u32[]{:S(2)}, u32[]{:S(2)}) collective-permute-start(bf16[288,128]{1,0:T(8,128)(2,1)S(1)} %get-tuple-element.24), channel_id=1, source_target_pairs={{0,2},{1,3},{2,0},{3,1},{4,6},{5,7},{6,4},{7,5},{8,10},{9,11},{10,... | collective-permute-start | bytes 221192 | tf_op jit(solution)/shard_map/ppermute | solution.py:130
  25.8 4.3 %collective-permute-start.6 = (bf16[288,128]{1,0:T(8,128)(2,1)S(1)}, bf16[288,128]{1,0:T(8,128)(2,1)S(1)}, u32[]{:S(2)}, u32[]{:S(2)}) collective-permute-start(bf16[288,128]{1,0:T(8,128)(2,1)S(1)} %get-tuple-element.25), channel_id=1, source_target_pairs={{0,3},{1,2},{2,1},{3,0},{4,7},{5,6},{6,5},{7,4},{8,11},{9,10},{10,... | collective-permute-start | bytes 221192 | tf_op jit(solution)/shard_map/ppermute | solution.py:130
  25.8 37.4 %collective-permute-start.9 = (bf16[864,1152]{1,0:T(8,128)(2,1)S(1)}, bf16[864,1152]{1,0:T(8,128)(2,1)}, u32[]{:S(2)}, u32[]{:S(2)}) collective-permute-start(bf16[864,1152]{1,0:T(8,128)(2,1)S(1)} %copy-done), channel_id=1, source_target_pairs={{0,1},{1,0},{2,3},{3,2},{4,5},{5,4},{6,7},{7,6},{8,9},{9,8},{10,11... | collective-permute-start | bytes 5971976 | tf_op jit(solution)/shard_map/ppermute | solution.py:130
  30.1 2.1 %collective-permute-start.8 = (bf16[288,1152]{1,0:T(8,128)(2,1)S(1)}, bf16[288,1152]{1,0:T(8,128)(2,1)S(1)}, u32[]{:S(2)}, u32[]{:S(2)}) collective-permute-start(bf16[288,1152]{1,0:T(8,128)(2,1)S(1)} %collective-permute-done.7.refs_6_), channel_id=1, source_target_pairs={{0,1},{1,0},{2,3},{3,2},{4,5},{5,4},{6,7},{7,6},{8,9},{9,8},{10,11... | collective-permute-start | bytes 1990664 | tf_op jit(solution)/shard_map/ppermute | solution.py:130
  33.8 15.7 %all-to-all-start = ((bf16[8,16,1152]{2,1,0:T(8,128)(2,1)}), bf16[8,16,1152]{2,1,0:T(8,128)(2,1)S(1)}, u32[]{:S(2)}, u32[]{:S(2)}) async-start(bf16[8,16,1152]{2,1,0:T(8,128)(2,1)} %bitcast), calls=%async_computation | async-start | bytes 589824 | tf_op jit(solution)/shard_map/all_to_all | solution.py:156
  39.7 23.1 %collective-permute-start.13 = (bf16[288,1152]{1,0:T(8,128)(2,1)S(1)}, bf16[288,1152]{1,0:T(8,128)(2,1)}, u32[]{:S(2)}, u32[]{:S(2)}) collective-permute-start(bf16[288,1152]{1,0:T(8,128)(2,1)S(1)} %copy-done.2), channel_id=1, source_target_pairs={{0,2},{1,3},{2,0},{3,1},{4,6},{5,7},{6,4},{7,5},{8,10},{9,11},{10,... | collective-permute-start | bytes 1990664 | tf_op jit(solution)/shard_map/ppermute | solution.py:130
  49.5 13.2 %collective-permute-start.10 = (bf16[128,1152]{1,0:T(8,128)(2,1)S(1)}, bf16[128,1152]{1,0:T(8,128)(2,1)S(1)}, u32[]{:S(2)}, u32[]{:S(2)}) collective-permute-start(bf16[128,1152]{1,0:T(8,128)(2,1)S(1)} %bitcast.4), channel_id=1, source_target_pairs={{0,2},{1,3},{2,0},{3,1},{4,6},{5,7},{6,4},{7,5},{8,10},{9,11},{10,... | collective-permute-start | bytes 884744 | tf_op jit(solution)/shard_map/ppermute | solution.py:130
  62.7 10.8 %collective-permute-start.12 = (bf16[288,1152]{1,0:T(8,128)(2,1)S(1)}, bf16[288,1152]{1,0:T(8,128)(2,1)S(1)}, u32[]{:S(2)}, u32[]{:S(2)}) collective-permute-start(bf16[288,1152]{1,0:T(8,128)(2,1)S(1)} %copy-done.2), channel_id=1, source_target_pairs={{0,1},{1,0},{2,3},{3,2},{4,5},{5,4},{6,7},{7,6},{8,9},{9,8},{10,11... | collective-permute-start | bytes 1990664 | tf_op jit(solution)/shard_map/ppermute | solution.py:130
  62.7 10.8 %collective-permute-start.14 = (bf16[288,1152]{1,0:T(8,128)(2,1)}, bf16[288,1152]{1,0:T(8,128)(2,1)S(1)}, u32[]{:S(2)}, u32[]{:S(2)}) collective-permute-start(bf16[288,1152]{1,0:T(8,128)(2,1)} %collective-permute-done.13.refs_4_), channel_id=1, source_target_pairs={{0,1},{1,0},{2,3},{3,2},{4,5},{5,4},{6,7},{7,6},{8,9},{9,8},{10,11... | collective-permute-start | bytes 1990664 | tf_op jit(solution)/shard_map/ppermute | solution.py:130
  67.7 22.7 %copy-start.5 = (f32[6,1152]{1,0:T(8,128)S(1)}, f32[6,1152]{1,0:T(8,128)}, u32[]{:S(2)}) copy-start(f32[6,1152]{1,0:T(8,128)} %mod_ref.5) | copy-start | bytes 82948
  67.7 5.8 %collective-permute-start.11 = (bf16[576,128]{1,0:T(8,128)(2,1)S(1)}, bf16[576,128]{1,0:T(8,128)(2,1)S(1)}, u32[]{:S(2)}, u32[]{:S(2)}) collective-permute-start(bf16[576,128]{1,0:T(8,128)(2,1)S(1)} %get-tuple-element.31), channel_id=1, source_target_pairs={{0,2},{1,3},{2,0},{3,1},{4,6},{5,7},{6,4},{7,5},{8,10},{9,11},{10,... | collective-permute-start | bytes 442376 | tf_op jit(solution)/shard_map/ppermute | solution.py:130

commit v3 on v2

v3 whole, which is shorter than its diff:
```python
import functools

import jax
import jax.numpy as jnp
from jax import lax
from jax.experimental import pallas as pl
from jax.experimental.pallas import tpu as pltpu
from jax.sharding import PartitionSpec as P

HD = 72
MIB = 1 << 20
LOG2E = 1.4426950408889634
F32 = jnp.float32
BF16 = jnp.bfloat16


def norm_rows(values, shift, scale):
    average = jnp.mean(values, axis=-1, keepdims=True)
    centred = values - average
    variance = jnp.mean(centred * centred, axis=-1, keepdims=True)
    normed = centred * lax.rsqrt(variance + 1e-06)
    return (normed * (1.0 + scale) + shift).astype(BF16)


def dot(left, right, left_dim=1, right_dim=0):
    return lax.dot_general(
        left, right, (((left_dim,), (right_dim,)), ((), ())), preferred_element_type=F32
    )


def softmax_over_rows(scores, mask=None):
    if mask is not None:
        scores = jnp.where(mask, scores, -1e30)
    top = jnp.max(scores, axis=0, keepdims=True)
    grown = jnp.exp2((scores - top) * (HD**-0.5 * LOG2E))
    total = jnp.sum(grown, axis=0, keepdims=True)
    return (grown * (1.0 / total)).astype(BF16)


def project(mod_ref, weight_ref, token_refs, proj_ref):
    shift, scale = mod_ref[0:1, :], mod_ref[1:2, :]
    block = token_refs[0].shape[1]
    for at in range(0, len(token_refs), 2):
        rows = [norm_rows(ref[0].astype(F32), shift, scale) for ref in token_refs[at : at + 2]]
        rows = jnp.concatenate(rows, axis=0)
        proj_ref[:, at * block : (at + 2) * block] = dot(weight_ref[...], rows, 1, 1)


def near_kernel(mod_ref, weight_ref, own_ref, sister_ref, proj_ref):
    project(mod_ref, weight_ref, (own_ref, sister_ref), proj_ref)


def spatial_kernel(count, mod_ref, weight_ref, near_ref, *refs):
    token_refs, out_refs = refs[: count - 2], refs[count - 2 : -2]
    far_ref, heads_ref = refs[-2:]
    block = token_refs[0].shape[1]
    heads = weight_ref.shape[0] // (3 * HD)
    project(mod_ref, weight_ref, token_refs, far_ref)

    def whole(start):
        parts = [ref[start : start + HD, :].astype(BF16) for ref in (near_ref, far_ref)]
        return jnp.concatenate(parts, axis=1)

    for head in range(heads):
        base = head * 3 * HD
        queries, keys, values = (whole(base + part * HD) for part in range(3))
        keys = keys.T
        for at in range(0, count, 2):
            cols = slice(at * block, (at + 2) * block)
            probs = softmax_over_rows(dot(keys, queries[:, cols]))
            heads_ref[head * HD : (head + 1) * HD, cols] = dot(values, probs)
    for at in range(count):
        out_refs[at][...] = heads_ref[:, at * block : (at + 1) * block].astype(BF16)


def ordered(*weight_refs):
    here = lax.axis_index("patch") // 2
    parts = [ref[here ^ at] for at in range(weight_refs[0].shape[0]) for ref in weight_refs]
    return jnp.concatenate(parts, axis=0)


def middle_kernel(count, pieces, mod_ref, token_ref, own_ref, sister_ref, *refs):
    head_refs, middle_ref = refs[:count], refs[count]
    piece_refs, scratch = refs[count + 1 : -1], refs[-1]
    heads = jnp.concatenate([ref[...] for ref in head_refs], axis=0)
    weights = ordered(own_ref, sister_ref)
    update = dot(heads.T, weights)
    middle = (token_ref[0].astype(F32) + mod_ref[2:3, :] * update).astype(BF16)
    middle_ref[...] = middle
    normed = norm_rows(middle.astype(F32), mod_ref[3:4, :], mod_ref[4:5, :])
    if pieces == 1:
        piece_refs[0][...] = normed
        return
    scratch[...] = normed
    here = lax.axis_index("frame")
    size = normed.shape[0] // pieces
    for at in range(pieces):
        start = pl.multiple_of((here ^ at) * size, size)
        piece_refs[at][...] = scratch[pl.ds(start, size), :]


def join_kernel(*refs):
    size = refs[0].shape[0]
    for at, ref in enumerate(refs[:-1]):
        refs[-1][at * size : (at + 1) * size, :] = ref[...]


def temporal_kernel(groups, cores, period, *refs):
    weight_refs = refs[:cores]
    row_refs = refs[cores : cores + groups]
    out_refs = refs[cores + groups : -2]
    proj_ref, heads_ref = refs[-2:]
    rows = jnp.concatenate([ref[...] for ref in row_refs], axis=0)
    block = rows.shape[0] // groups
    depth = weight_refs[0].shape[0]
    for core in range(cores):
        proj_ref[core * depth : (core + 1) * depth, :] = dot(weight_refs[core][...], rows, 1, 1)
    heads = cores * depth // (3 * HD)
    key_patch = lax.broadcasted_iota(jnp.int32, (block, block), 0) % period
    query_patch = lax.broadcasted_iota(jnp.int32, (block, block), 1) % period
    mask = key_patch == query_patch
    for head in range(heads):
        base = head * 3 * HD
        for group in range(groups):
            cols = slice(group * block, (group + 1) * block)
            query = proj_ref[base : base + HD, cols].astype(BF16)
            keys = proj_ref[base + HD : base + 2 * HD, cols].astype(BF16)
            values = proj_ref[base + 2 * HD : base + 3 * HD, cols].astype(BF16)
            probs = softmax_over_rows(dot(keys.T, query), mask)
            heads_ref[head * HD : (head + 1) * HD, cols] = dot(values, probs)
    for group in range(groups):
        out_refs[group][...] = heads_ref[:, group * block : (group + 1) * block].astype(BF16)


def turn_kernel(pieces, *refs):
    heads = jnp.concatenate([ref[...] for ref in refs[:-pieces]], axis=0).T
    size = heads.shape[0] // pieces
    for at in range(pieces):
        refs[at - pieces][...] = heads[at * size : (at + 1) * size, :]


def result_kernel(pieces, mod_ref, middle_ref, own_ref, sister_ref, *refs):
    piece_refs, out_ref = refs[:pieces], refs[-1]
    heads = jnp.concatenate([ref[...] for ref in piece_refs], axis=0)
    change = mod_ref[5:6, :] * dot(heads, ordered(own_ref, sister_ref))
    here = lax.axis_index("frame")
    size = heads.shape[0] // pieces
    for at in range(pieces):
        start = pl.multiple_of((here ^ at) * size, size) if pieces > 1 else 0
        rows = pl.ds(start, size)
        part = change[at * size : (at + 1) * size, :]
        out_ref[0, rows, :] = (middle_ref[rows, :].astype(F32) + part).astype(BF16)


def call(body, operands, outs, scratch=(), limit=24):
    return pl.pallas_call(
        body,
        out_shape=outs,
        in_specs=[pl.BlockSpec(memory_space=pltpu.VMEM)] * len(operands),
        out_specs=[pl.BlockSpec(memory_space=pltpu.VMEM)] * len(outs),
        scratch_shapes=list(scratch),
        compiler_params=pltpu.CompilerParams(vmem_limit_bytes=limit * MIB),
        cost_estimate=pl.CostEstimate(flops=1, bytes_accessed=1, transcendentals=0),
    )(*operands)


def swap(value, axis, offset):
    size = lax.axis_size(axis)
    return lax.ppermute(value, axis, [(at, at ^ offset) for at in range(size)])


def after(value, *others):
    return lax.optimization_barrier((value, *others))[0]


def across(value):
    size = lax.axis_size("patch")
    return [swap(value, "patch", at) if at else value for at in range(0, size, 2)]


def both_cores(blocks):
    return [part for block in blocks for part in (block, swap(block, "patch", 1))]


def gather_chips(weights):
    size = lax.axis_size("patch")
    groups = [list(range(core, size, 2)) for core in range(2)]
    return lax.all_gather(weights, "patch", axis_index_groups=groups)


def per_device(tokens, modulation, spatial_qkv, spatial_out, temporal_qkv, temporal_out):
    _, rows, width = tokens.shape
    shard = spatial_out.shape[0]
    count, frames = lax.axis_size("patch"), lax.axis_size("frame")
    period = rows // frames
    pieces = frames if period % 16 == 0 else 1
    shape = jax.ShapeDtypeStruct
    parts_shape = [shape((rows // pieces, width), BF16)] * pieces

    def exchange_frames(parts):
        if pieces == 1:
            blocks = parts[0].reshape(frames, period, width)
            blocks = lax.all_to_all(blocks, "frame", split_axis=0, concat_axis=0, tiled=True)
            return [blocks.reshape(rows, width)]
        parts = list(parts)
        for at in reversed(range(1, pieces)):
            parts[at] = swap(parts[at], "frame", at)
        return parts

    sister = swap(tokens, "patch", 1)
    far = across(tokens)[1:]
    (near,) = call(
        near_kernel,
        (modulation, spatial_qkv, tokens, sister),
        [shape((3 * shard, 2 * rows), F32)],
    )
    far = both_cores([after(block, near) for block in far])
    temporal_pair = [temporal_qkv, swap(after(temporal_qkv, sister), "patch", 1)]
    spatial_weights = gather_chips(after(spatial_out, sister))
    mixed = call(
        functools.partial(spatial_kernel, count),
        (modulation, spatial_qkv, near, *far),
        [shape((shard, rows), BF16)] * count,
        [pltpu.VMEM((3 * shard, (count - 2) * rows), F32), pltpu.VMEM((shard, count * rows), F32)],
    )
    returned = list(mixed)
    for at in reversed(range(1, count)):
        returned[at] = swap(mixed[at], "patch", at)
    spatial_weights = both_cores([after(spatial_weights, *returned)])
    middle, *parts = call(
        functools.partial(middle_kernel, count, pieces),
        (modulation, tokens, *spatial_weights, *returned),
        [shape((rows, width), BF16)] + parts_shape,
        [pltpu.VMEM((rows, width), BF16)],
    )
    temporal_weights = gather_chips(after(temporal_out, middle))
    (segment,) = call(join_kernel, exchange_frames(parts), [shape((rows, width), BF16)])

    def attend(weights, segments):
        columns = len(segments) * rows
        return call(
            functools.partial(temporal_kernel, len(segments), 2, period),
            (*weights, *segments),
            [shape((2 * shard, rows), BF16)] * len(segments),
            [pltpu.VMEM((6 * shard, columns), F32), pltpu.VMEM((2 * shard, columns), F32)],
        )

    others = across(segment)[1:]
    (own,) = attend(temporal_pair, [segment])
    mixed = attend([after(block, own) for block in temporal_pair], others)
    returned = [own] + [swap(part, "patch", 2 * at + 2) for at, part in enumerate(mixed)]
    temporal_weights = both_cores([after(temporal_weights, *returned)])
    parts = call(functools.partial(turn_kernel, pieces), returned, parts_shape)
    (result,) = call(
        functools.partial(result_kernel, pieces),
        (modulation, middle, *temporal_weights, *exchange_frames(parts)),
        [shape((1, rows, width), BF16)],
    )
    return result


def solution(mesh):
    in_specs = (
        P("frame", "patch", None),
        P(),
        P("patch", None),
        P("patch", None),
        P("patch", None),
        P("patch", None),
    )
    out_specs = P("frame", "patch", None)
    return jax.shard_map(
        per_device, mesh=mesh, in_specs=in_specs, out_specs=out_specs, check_vma=False
    )
```

time: 91.6 us -> 111 us (1.21)
  blocking collectives: 15.1 us -> 0 us
  between operations: 0.07 us -> 13.5 us
  starting transfers between devices: 16.6 us -> 28.8 us
  waiting for transfers between devices: 41.9 us -> 47.3 us
  local copies, waits for them, and re-layouts: 3.3 us -> 5.95 us
  Pallas kernels: 14.3 us -> 15.7 us
    ppermute x15 -> x25, starting transfers between devices: 10.7 us -> 28.7 us  [swap(): return lax.ppermute(value, axis, [(at, at ^ offset) for at in range(size)])]
    all_to_all x1 -> x0, blocking collectives: 15.1 us -> none  [exchange_frames(): lax.all_to_all(blocks, 'frame', split_axis=0, concat_axis=0, tiled=True)]
    ppermute x15 -> x25, waiting for transfers between devices: 33.3 us -> 43.1 us  [swap(): return lax.ppermute(value, axis, [(at, at ^ offset) for at in range(size)])]
    all_to_all x1 -> x0, waiting for transfers between devices: 8.59 us -> none  [exchange_frames(): lax.all_to_all(blocks, 'frame', split_axis=0, concat_axis=0, tiled=True)]
    all_to_all x1 -> x0, starting transfers between devices: 5.8 us -> none  [exchange_frames(): lax.all_to_all(blocks, 'frame', split_axis=0, concat_axis=0, tiled=True)]
    all_gather x0 -> x2, waiting for transfers between devices: none -> 4.17 us  [gather_chips(): return lax.all_gather(weights, 'patch', axis_index_groups=groups)]
    unnamed x14 -> x16, local copies, waits for them, and re-layouts: 3.3 us -> 5.95 us
    pallas_call x5 -> x8, Pallas kernels: 14.3 us -> 15.7 us  [call(): pl.pallas_call(body, out_shape=outs, in_specs=[pl.BlockSpec(memory_space=...]
  transfers between devices with their start and end apart: 16 -> 27, of which waited for: 10 -> 15; matrix products, arithmetic and copies ran while one was open for 0% -> 0% of each run, Pallas kernels for 13% -> 13%
where the time goes in v3:
time: 111 us
  waiting for transfers between devices  47.3 us (43%)
  starting transfers between devices  28.8 us (26%)
  Pallas kernels  15.7 us (14%)
  between operations  13.5 us (12%)
  local copies, waits for them, and re-layouts  5.95 us (5%)
    ppermute x25, waiting for transfers between devices, swap(): return lax.ppermute(value, axis, [(at, at ^ offset) for at in range(size)])  43.1 us
    ppermute x25, starting transfers between devices, swap(): return lax.ppermute(value, axis, [(at, at ^ offset) for at in range(size)])  28.7 us
    pallas_call x8, Pallas kernels, call(): pl.pallas_call(body, out_shape=outs, in_specs=[pl.BlockSpec(memory_space=...  15.7 us
    unnamed x16, local copies, waits for them, and re-layouts  5.95 us
    all_gather x2, waiting for transfers between devices, gather_chips(): return lax.all_gather(weights, 'patch', axis_index_groups=groups)  4.17 us
  transfers between devices with their start and end apart: 27, of which 15 were waited for; matrix products, arithmetic and copies ran while one was open for 0% of the time, Pallas kernels for 13%

profile of v3, /device:TPU:0, one launch (start us, length us, event | category | flops | bytes accessed | tf_op | source)
XLA Modules:
  0.0 111.1 jit_solution(11969665913936333194)
XLA Ops:
  7.0 1.4 %collective-permute-done.sister_ref = bf16[1,128,1152]{2,1,0:T(8,128)(2,1)S(1)} collective-permute-done((bf16[1,128,1152]{2,1,0:T(8,128)(2,1)}, bf16[1,128,1152]{2,1,0:T(8,128)(2,1)S(1)}, u32[]{:S(2)}, u32[]{:S(2)}) %collective-permute-start) | collective-permute-done | bytes 294944 | tf_op jit(solution)/shard_map/ppermute | solution.py:169
  8.5 3.0 %collective-permute-start.1 = (bf16[1,128,1152]{2,1,0:T(8,128)(2,1)}, bf16[1,128,1152]{2,1,0:T(8,128)(2,1)S(1)}, u32[]{:S(2)}, u32[]{:S(2)}) collective-permute-start(bf16[1,128,1152]{2,1,0:T(8,128)(2,1)} %token_ref.1), channel_id=1, source_target_pairs={{0,2},{1,3},{2,0},{3,1},{4,6},{5,7},{6,4},{7,5},{8,10},{9,11},{10,... | collective-permute-start | bytes 884744 | tf_op jit(solution)/shard_map/ppermute | solution.py:169
  11.4 1.6 %copy-done = bf16[864,1152]{1,0:T(8,128)(2,1)S(1)} copy-done((bf16[864,1152]{1,0:T(8,128)(2,1)S(1)}, bf16[864,1152]{1,0:T(8,128)(2,1)}, u32[]{:S(2)}) %copy-start) | copy-done | bytes 1990680
  13.0 1.0 copy-done.4
  14.7 1.1 shard_map.64.near_ref
  15.9 3.1 %collective-permute-done.1.refs_0_ = bf16[1,128,1152]{2,1,0:T(8,128)(2,1)S(1)} collective-permute-done((bf16[1,128,1152]{2,1,0:T(8,128)(2,1)}, bf16[1,128,1152]{2,1,0:T(8,128)(2,1)S(1)}, u32[]{:S(2)}, u32[]{:S(2)}) %collective-permute-start.1) | collective-permute-done | bytes 294944 | tf_op jit(solution)/shard_map/ppermute | solution.py:169
  19.0 1.6 %collective-permute-done.2.refs_1_ = bf16[1,128,1152]{2,1,0:T(8,128)(2,1)S(1)} collective-permute-done((bf16[1,128,1152]{2,1,0:T(8,128)(2,1)S(1)}, bf16[1,128,1152]{2,1,0:T(8,128)(2,1)S(1)}, u32[]{:S(2)}, u32[]{:S(2)}) %collective-permute-start.2) | collective-permute-done | bytes 294944 | tf_op jit(solution)/shard_map/ppermute | solution.py:169
  20.5 5.3 %shard_map.65 = (bf16[288,128]{1,0:T(8,128)(2,1)S(1)}, bf16[288,128]{1,0:T(8,128)(2,1)S(1)}, bf16[288,128]{1,0:T(8,128)(2,1)S(1)}, bf16[288,128]{1,0:T(8,128)(2,1)S(1)}) custom-call(f32[6,1152]{1,0:T(8,128)S(1)} %copy-done.6, bf16[864,1152]{1,0:T(8,128)(2,1)S(1)} %copy-done, f32[864,256]{1,0:T(8,128)S(1)} %shard_map.64.near_ref, ...), custom_call_target="tpu_custom_call" | custom-call | flops 1 | bytes 1 | tf_op jit(solution)/shard_map/pallas_call | solution.py:156
  26.0 1.8 %collective-permute-start.4 = (bf16[288,128]{1,0:T(8,128)(2,1)S(1)}, bf16[288,128]{1,0:T(8,128)(2,1)S(1)}, u32[]{:S(2)}, u32[]{:S(2)}) collective-permute-start(bf16[288,128]{1,0:T(8,128)(2,1)S(1)} %get-tuple-element.38), channel_id=1, source_target_pairs={{0,2},{1,3},{2,0},{3,1},{4,6},{5,7},{6,4},{7,5},{8,10},{9,11},{10,... | collective-permute-start | bytes 221192 | tf_op jit(solution)/shard_map/ppermute | solution.py:169
  27.8 4.9 %collective-permute-done.4.refs_2_ = bf16[288,128]{1,0:T(8,128)(2,1)S(1)} collective-permute-done((bf16[288,128]{1,0:T(8,128)(2,1)S(1)}, bf16[288,128]{1,0:T(8,128)(2,1)S(1)}, u32[]{:S(2)}, u32[]{:S(2)}) %collective-permute-start.4) | collective-permute-done | bytes 73760 | tf_op jit(solution)/shard_map/ppermute | solution.py:169
  32.7 2.4 %collective-permute-done.5.refs_3_ = bf16[288,128]{1,0:T(8,128)(2,1)S(1)} collective-permute-done((bf16[288,128]{1,0:T(8,128)(2,1)S(1)}, bf16[288,128]{1,0:T(8,128)(2,1)S(1)}, u32[]{:S(2)}, u32[]{:S(2)}) %collective-permute-start.5) | collective-permute-done | bytes 73760 | tf_op jit(solution)/shard_map/ppermute | solution.py:169
  35.1 4.2 %all-gather.5.cloned.1.call-done = bf16[576,1152]{1,0:T(8,128)(2,1)} async-done(((bf16[288,1152]{1,0:T(8,128)(2,1)}), bf16[576,1152]{1,0:T(8,128)(2,1)}) %all-gather.5.cloned.1.call-update) | async-done | bytes 1327120 | tf_op jit(solution)/shard_map/all_gather | solution.py:188
  39.7 4.6 %collective-permute-done.6.sister_ref = bf16[2,288,1152]{2,1,0:T(8,128)(2,1)S(1)} collective-permute-done((bf16[2,288,1152]{2,1,0:T(8,128)(2,1)}, bf16[2,288,1152]{2,1,0:T(8,128)(2,1)S(1)}, u32[]{:S(2)}, u32[]{:S(2)}) %collective-permute-start.6) | collective-permute-done | bytes 1327136 | tf_op jit(solution)/shard_map/ppermute | solution.py:169
  44.4 1.3 %copy-done.2 = bf16[576,1152]{1,0:T(8,128)(2,1)S(1)} copy-done((bf16[576,1152]{1,0:T(8,128)(2,1)S(1)}, bf16[576,1152]{1,0:T(8,128)(2,1)}, u32[]{:S(2)}) %copy-start.2) | copy-done | bytes 1327128
  46.6 2.5 %collective-permute-start.10 = (bf16[16,1152]{1,0:T(8,128)(2,1)S(1)}, bf16[16,1152]{1,0:T(8,128)(2,1)S(1)}, u32[]{:S(2)}, u32[]{:S(2)}) collective-permute-start(bf16[16,1152]{1,0:T(8,128)(2,1)S(1)} %get-tuple-element.47), channel_id=1, source_target_pairs={{0,12},{4,8},{8,4},{12,0},{16,28},{20,24},{24,20},{28,16},{1,13},{... | collective-permute-start | bytes 110600 | tf_op jit(solution)/shard_map/ppermute | solution.py:169
  49.1 2.4 %collective-permute-start.11 = (bf16[16,1152]{1,0:T(8,128)(2,1)S(1)}, bf16[16,1152]{1,0:T(8,128)(2,1)S(1)}, u32[]{:S(2)}, u32[]{:S(2)}) collective-permute-start(bf16[16,1152]{1,0:T(8,128)(2,1)S(1)} %get-tuple-element.48), channel_id=1, source_target_pairs={{0,16},{4,20},{8,24},{12,28},{16,0},{20,4},{24,8},{28,12},{1,17},{... | collective-permute-start | bytes 110600 | tf_op jit(solution)/shard_map/ppermute | solution.py:169
  52.0 2.4 %collective-permute-start.13 = (bf16[16,1152]{1,0:T(8,128)(2,1)S(1)}, bf16[16,1152]{1,0:T(8,128)(2,1)S(1)}, u32[]{:S(2)}, u32[]{:S(2)}) collective-permute-start(bf16[16,1152]{1,0:T(8,128)(2,1)S(1)} %get-tuple-element.50), channel_id=1, source_target_pairs={{0,24},{4,28},{8,16},{12,20},{16,8},{20,12},{24,0},{28,4},{1,25},{... | collective-permute-start | bytes 110600 | tf_op jit(solution)/shard_map/ppermute | solution.py:169
  54.4 2.4 %collective-permute-start.14 = (bf16[16,1152]{1,0:T(8,128)(2,1)S(1)}, bf16[16,1152]{1,0:T(8,128)(2,1)S(1)}, u32[]{:S(2)}, u32[]{:S(2)}) collective-permute-start(bf16[16,1152]{1,0:T(8,128)(2,1)S(1)} %get-tuple-element.51), channel_id=1, source_target_pairs={{0,28},{4,24},{8,20},{12,16},{16,12},{20,8},{24,4},{28,0},{1,29},{... | collective-permute-start | bytes 110600 | tf_op jit(solution)/shard_map/ppermute | solution.py:169
  58.2 2.9 %collective-permute-done.14.refs_7_ = bf16[16,1152]{1,0:T(8,128)(2,1)S(1)} collective-permute-done((bf16[16,1152]{1,0:T(8,128)(2,1)S(1)}, bf16[16,1152]{1,0:T(8,128)(2,1)S(1)}, u32[]{:S(2)}, u32[]{:S(2)}) %collective-permute-start.14) | collective-permute-done | bytes 36896 | tf_op jit(solution)/shard_map/ppermute | solution.py:169
  61.1 1.0 collective-permute-done.9.refs_2_
  62.8 3.4 %shard_map.68.refs_0_ = bf16[576,128]{1,0:T(8,128)(2,1)S(1)} custom-call(bf16[864,1152]{1,0:T(8,128)(2,1)S(1)} %copy-done.1, bf16[864,1152]{1,0:T(8,128)(2,1)} %collective-permute-done.7.refs_1_, bf16[128,1152]{1,0:T(8,128)(2,1)S(1)} %shard_map.67.refs_2_), custom_call_target="tpu_custom_call" | custom-call | flops 1 | bytes 1 | tf_op jit(solution)/shard_map/pallas_call | solution.py:156
  66.2 10.9 %collective-permute-done.15.refs_2_ = bf16[128,1152]{1,0:T(8,128)(2,1)S(1)} collective-permute-done((bf16[128,1152]{1,0:T(8,128)(2,1)S(1)}, bf16[128,1152]{1,0:T(8,128)(2,1)S(1)}, u32[]{:S(2)}, u32[]{:S(2)}) %collective-permute-start.15) | collective-permute-done | bytes 294944 | tf_op jit(solution)/shard_map/ppermute | solution.py:169
  77.2 3.4 %shard_map.69 = bf16[576,128]{1,0:T(8,128)(2,1)S(1)} custom-call(bf16[864,1152]{1,0:T(8,128)(2,1)S(1)} %copy-done.1, bf16[864,1152]{1,0:T(8,128)(2,1)} %collective-permute-done.7.refs_1_, bf16[128,1152]{1,0:T(8,128)(2,1)S(1)} %collective-permute-done.15.refs_2_), custom_call_target="tpu_custom_call" | custom-call | flops 1 | bytes 1 | tf_op jit(solution)/shard_map/pallas_call | solution.py:156
  81.1 4.7 %collective-permute-done.16.refs_1_ = bf16[576,128]{1,0:T(8,128)(2,1)S(1)} collective-permute-done((bf16[576,128]{1,0:T(8,128)(2,1)S(1)}, bf16[576,128]{1,0:T(8,128)(2,1)S(1)}, u32[]{:S(2)}, u32[]{:S(2)}) %collective-permute-start.16) | collective-permute-done | bytes 147488 | tf_op jit(solution)/shard_map/ppermute | solution.py:169
  86.8 2.7 %collective-permute-start.20 = (bf16[16,1152]{1,0:T(8,128)(2,1)S(1)}, bf16[16,1152]{1,0:T(8,128)(2,1)S(1)}, u32[]{:S(2)}, u32[]{:S(2)}) collective-permute-start(bf16[16,1152]{1,0:T(8,128)(2,1)S(1)} %get-tuple-element.58), channel_id=1, source_target_pairs={{0,12},{4,8},{8,4},{12,0},{16,28},{20,24},{24,20},{28,16},{1,13},{... | collective-permute-start | bytes 110600 | tf_op jit(solution)/shard_map/ppermute | solution.py:169
  89.9 2.7 %collective-permute-start.22 = (bf16[16,1152]{1,0:T(8,128)(2,1)S(1)}, bf16[16,1152]{1,0:T(8,128)(2,1)S(1)}, u32[]{:S(2)}, u32[]{:S(2)}) collective-permute-start(bf16[16,1152]{1,0:T(8,128)(2,1)S(1)} %get-tuple-element.60), channel_id=1, source_target_pairs={{0,20},{4,16},{8,28},{12,24},{16,4},{20,0},{24,12},{28,8},{1,21},{... | collective-permute-start | bytes 110600 | tf_op jit(solution)/shard_map/ppermute | solution.py:169
  92.6 2.4 %collective-permute-start.23 = (bf16[16,1152]{1,0:T(8,128)(2,1)S(1)}, bf16[16,1152]{1,0:T(8,128)(2,1)S(1)}, u32[]{:S(2)}, u32[]{:S(2)}) collective-permute-start(bf16[16,1152]{1,0:T(8,128)(2,1)S(1)} %get-tuple-element.61), channel_id=1, source_target_pairs={{0,24},{4,28},{8,16},{12,20},{16,8},{20,12},{24,0},{28,4},{1,25},{... | collective-permute-start | bytes 110600 | tf_op jit(solution)/shard_map/ppermute | solution.py:169
  95.0 2.2 %collective-permute-start.24 = (bf16[16,1152]{1,0:T(8,128)(2,1)S(1)}, bf16[16,1152]{1,0:T(8,128)(2,1)S(1)}, u32[]{:S(2)}, u32[]{:S(2)}) collective-permute-start(bf16[16,1152]{1,0:T(8,128)(2,1)S(1)} %get-tuple-element.62), channel_id=1, source_target_pairs={{0,28},{4,24},{8,20},{12,16},{16,12},{20,8},{24,4},{28,0},{1,29},{... | collective-permute-start | bytes 110600 | tf_op jit(solution)/shard_map/ppermute | solution.py:169
  97.1 1.4 %collective-permute-done.23.refs_6_ = bf16[16,1152]{1,0:T(8,128)(2,1)S(1)} collective-permute-done((bf16[16,1152]{1,0:T(8,128)(2,1)S(1)}, bf16[16,1152]{1,0:T(8,128)(2,1)S(1)}, u32[]{:S(2)}, u32[]{:S(2)}) %collective-permute-start.23) | collective-permute-done | bytes 36896 | tf_op jit(solution)/shard_map/ppermute | solution.py:169
  98.5 3.1 %collective-permute-done.24.refs_7_ = bf16[16,1152]{1,0:T(8,128)(2,1)S(1)} collective-permute-done((bf16[16,1152]{1,0:T(8,128)(2,1)S(1)}, bf16[16,1152]{1,0:T(8,128)(2,1)S(1)}, u32[]{:S(2)}, u32[]{:S(2)}) %collective-permute-start.24) | collective-permute-done | bytes 36896 | tf_op jit(solution)/shard_map/ppermute | solution.py:169
  101.6 1.3 %copy-done.3 = bf16[576,1152]{1,0:T(8,128)(2,1)S(1)} copy-done((bf16[576,1152]{1,0:T(8,128)(2,1)S(1)}, bf16[576,1152]{1,0:T(8,128)(2,1)}, u32[]{:S(2)}) %copy-start.3) | copy-done | bytes 1327128
  102.9 1.3 %shard_map.71 = bf16[1,128,1152]{2,1,0:T(8,128)(2,1)} custom-call(f32[6,1152]{1,0:T(8,128)S(1)} %copy-done.7, bf16[128,1152]{1,0:T(8,128)(2,1)S(1)} %get-tuple-element.41.middle_ref, bf16[2,288,1152]{2,1,0:T(8,128)(2,1)S(1)} %bitcast.5, bf16[2,288,1152]{2,1,0:T(8,128)(2,1)S(1)} %collective-permute-done.17.sister_ref, ...), custom_call_target="tpu_custom_call" | custom-call | flops 1 | bytes 1 | tf_op jit(solution)/shard_map/pallas_call | solution.py:156
  (48 shorter events, 7.6 us)
Async XLA Ops:
  6.5 32.7 %all-gather.5.cloned.1.call-start = ((), (), s32[]{:S(2)}) async-start(), calls=%async_computation | async-start | bytes 1990656 | tf_op jit(solution)/shard_map/all_gather | solution.py:188
  6.5 1.9 %collective-permute-start = (bf16[1,128,1152]{2,1,0:T(8,128)(2,1)}, bf16[1,128,1152]{2,1,0:T(8,128)(2,1)S(1)}, u32[]{:S(2)}, u32[]{:S(2)}) collective-permute-start(bf16[1,128,1152]{2,1,0:T(8,128)(2,1)} %token_ref.1), channel_id=1, source_target_pairs={{0,1},{1,0},{2,3},{3,2},{4,5},{5,4},{6,7},{7,6},{8,9},{9,8},{10,11... | collective-permute-start | bytes 884744 | tf_op jit(solution)/shard_map/ppermute | solution.py:169
  8.4 77.3 %all-gather.7.cloned.1.call-start = ((), (), s32[]{:S(2)}) async-start(), calls=%async_computation.1 | async-start | bytes 1990656 | tf_op jit(solution)/shard_map/all_gather | solution.py:188
  8.5 10.5 %collective-permute-start.1 = (bf16[1,128,1152]{2,1,0:T(8,128)(2,1)}, bf16[1,128,1152]{2,1,0:T(8,128)(2,1)S(1)}, u32[]{:S(2)}, u32[]{:S(2)}) collective-permute-start(bf16[1,128,1152]{2,1,0:T(8,128)(2,1)} %token_ref.1), channel_id=1, source_target_pairs={{0,2},{1,3},{2,0},{3,1},{4,6},{5,7},{6,4},{7,5},{8,10},{9,11},{10,... | collective-permute-start | bytes 884744 | tf_op jit(solution)/shard_map/ppermute | solution.py:169
  11.4 1.6 %copy-start = (bf16[864,1152]{1,0:T(8,128)(2,1)S(1)}, bf16[864,1152]{1,0:T(8,128)(2,1)}, u32[]{:S(2)}) copy-start(bf16[864,1152]{1,0:T(8,128)(2,1)} %weight_ref.3) | copy-start | bytes 5971972
  15.8 23.4 %copy-start.1 = (bf16[864,1152]{1,0:T(8,128)(2,1)S(1)}, bf16[864,1152]{1,0:T(8,128)(2,1)}, u32[]{:S(2)}) copy-start(bf16[864,1152]{1,0:T(8,128)(2,1)} %refs_0_.2) | copy-start | bytes 5971972
  15.8 28.5 %copy-start.5 = (bf16[1,128,1152]{2,1,0:T(8,128)(2,1)S(1)}, bf16[1,128,1152]{2,1,0:T(8,128)(2,1)}, u32[]{:S(2)}) copy-start(bf16[1,128,1152]{2,1,0:T(8,128)(2,1)} %token_ref.1) | copy-start | bytes 884740
  15.9 28.5 %copy-start.7 = (f32[6,1152]{1,0:T(8,128)S(1)}, f32[6,1152]{1,0:T(8,128)}, u32[]{:S(2)}) copy-start(f32[6,1152]{1,0:T(8,128)} %mod_ref.7) | copy-start | bytes 82948
  19.0 1.6 %collective-permute-start.2 = (bf16[1,128,1152]{2,1,0:T(8,128)(2,1)S(1)}, bf16[1,128,1152]{2,1,0:T(8,128)(2,1)S(1)}, u32[]{:S(2)}, u32[]{:S(2)}) collective-permute-start(bf16[1,128,1152]{2,1,0:T(8,128)(2,1)S(1)} %collective-permute-done.1.refs_0_), channel_id=1, source_target_pairs={{0,1},{1,0},{2,3},{3,2},{4,5},{5,4},{6,7},{7,6},{8,9},{9,8},{10,11... | collective-permute-start | bytes 884744 | tf_op jit(solution)/shard_map/ppermute | solution.py:169
  25.8 2.0 %collective-permute-start.3 = (bf16[288,128]{1,0:T(8,128)(2,1)S(1)}, bf16[288,128]{1,0:T(8,128)(2,1)S(1)}, u32[]{:S(2)}, u32[]{:S(2)}) collective-permute-start(bf16[288,128]{1,0:T(8,128)(2,1)S(1)} %get-tuple-element.37), channel_id=1, source_target_pairs={{0,1},{1,0},{2,3},{3,2},{4,5},{5,4},{6,7},{7,6},{8,9},{9,8},{10,11... | collective-permute-start | bytes 221192 | tf_op jit(solution)/shard_map/ppermute | solution.py:169
  26.0 6.7 %collective-permute-start.4 = (bf16[288,128]{1,0:T(8,128)(2,1)S(1)}, bf16[288,128]{1,0:T(8,128)(2,1)S(1)}, u32[]{:S(2)}, u32[]{:S(2)}) collective-permute-start(bf16[288,128]{1,0:T(8,128)(2,1)S(1)} %get-tuple-element.38), channel_id=1, source_target_pairs={{0,2},{1,3},{2,0},{3,1},{4,6},{5,7},{6,4},{7,5},{8,10},{9,11},{10,... | collective-permute-start | bytes 221192 | tf_op jit(solution)/shard_map/ppermute | solution.py:169
  27.8 7.3 %collective-permute-start.5 = (bf16[288,128]{1,0:T(8,128)(2,1)S(1)}, bf16[288,128]{1,0:T(8,128)(2,1)S(1)}, u32[]{:S(2)}, u32[]{:S(2)}) collective-permute-start(bf16[288,128]{1,0:T(8,128)(2,1)S(1)} %get-tuple-element.39), channel_id=1, source_target_pairs={{0,3},{1,2},{2,1},{3,0},{4,7},{5,6},{6,5},{7,4},{8,11},{9,10},{10,... | collective-permute-start | bytes 221192 | tf_op jit(solution)/shard_map/ppermute | solution.py:169
  39.2 5.1 %collective-permute-start.6 = (bf16[2,288,1152]{2,1,0:T(8,128)(2,1)}, bf16[2,288,1152]{2,1,0:T(8,128)(2,1)S(1)}, u32[]{:S(2)}, u32[]{:S(2)}) collective-permute-start(bf16[2,288,1152]{2,1,0:T(8,128)(2,1)} %bitcast.2), channel_id=1, source_target_pairs={{0,1},{1,0},{2,3},{3,2},{4,5},{5,4},{6,7},{7,6},{8,9},{9,8},{10,11... | collective-permute-start | bytes 3981320 | tf_op jit(solution)/shard_map/ppermute | solution.py:169
  39.2 23.6 %collective-permute-start.7 = (bf16[864,1152]{1,0:T(8,128)(2,1)S(1)}, bf16[864,1152]{1,0:T(8,128)(2,1)}, u32[]{:S(2)}, u32[]{:S(2)}) collective-permute-start(bf16[864,1152]{1,0:T(8,128)(2,1)S(1)} %copy-done.1), channel_id=1, source_target_pairs={{0,1},{1,0},{2,3},{3,2},{4,5},{5,4},{6,7},{7,6},{8,9},{9,8},{10,11... | collective-permute-start | bytes 5971976 | tf_op jit(solution)/shard_map/ppermute | solution.py:169
  46.6 7.8 %collective-permute-start.10 = (bf16[16,1152]{1,0:T(8,128)(2,1)S(1)}, bf16[16,1152]{1,0:T(8,128)(2,1)S(1)}, u32[]{:S(2)}, u32[]{:S(2)}) collective-permute-start(bf16[16,1152]{1,0:T(8,128)(2,1)S(1)} %get-tuple-element.47), channel_id=1, source_target_pairs={{0,12},{4,8},{8,4},{12,0},{16,28},{20,24},{24,20},{28,16},{1,13},{... | collective-permute-start | bytes 110600 | tf_op jit(solution)/shard_map/ppermute | solution.py:169
  49.1 7.7 %collective-permute-start.11 = (bf16[16,1152]{1,0:T(8,128)(2,1)S(1)}, bf16[16,1152]{1,0:T(8,128)(2,1)S(1)}, u32[]{:S(2)}, u32[]{:S(2)}) collective-permute-start(bf16[16,1152]{1,0:T(8,128)(2,1)S(1)} %get-tuple-element.48), channel_id=1, source_target_pairs={{0,16},{4,20},{8,24},{12,28},{16,0},{20,4},{24,8},{28,12},{1,17},{... | collective-permute-start | bytes 110600 | tf_op jit(solution)/shard_map/ppermute | solution.py:169
  51.5 6.7 %collective-permute-start.12 = (bf16[16,1152]{1,0:T(8,128)(2,1)S(1)}, bf16[16,1152]{1,0:T(8,128)(2,1)S(1)}, u32[]{:S(2)}, u32[]{:S(2)}) collective-permute-start(bf16[16,1152]{1,0:T(8,128)(2,1)S(1)} %get-tuple-element.49), channel_id=1, source_target_pairs={{0,20},{4,16},{8,28},{12,24},{16,4},{20,0},{24,12},{28,8},{1,21},{... | collective-permute-start | bytes 110600 | tf_op jit(solution)/shard_map/ppermute | solution.py:169
  52.0 6.2 %collective-permute-start.13 = (bf16[16,1152]{1,0:T(8,128)(2,1)S(1)}, bf16[16,1152]{1,0:T(8,128)(2,1)S(1)}, u32[]{:S(2)}, u32[]{:S(2)}) collective-permute-start(bf16[16,1152]{1,0:T(8,128)(2,1)S(1)} %get-tuple-element.50), channel_id=1, source_target_pairs={{0,24},{4,28},{8,16},{12,20},{16,8},{20,12},{24,0},{28,4},{1,25},{... | collective-permute-start | bytes 110600 | tf_op jit(solution)/shard_map/ppermute | solution.py:169
  54.4 6.7 %collective-permute-start.14 = (bf16[16,1152]{1,0:T(8,128)(2,1)S(1)}, bf16[16,1152]{1,0:T(8,128)(2,1)S(1)}, u32[]{:S(2)}, u32[]{:S(2)}) collective-permute-start(bf16[16,1152]{1,0:T(8,128)(2,1)S(1)} %get-tuple-element.51), channel_id=1, source_target_pairs={{0,28},{4,24},{8,20},{12,16},{16,12},{20,8},{24,4},{28,0},{1,29},{... | collective-permute-start | bytes 110600 | tf_op jit(solution)/shard_map/ppermute | solution.py:169
  56.7 4.4 %collective-permute-start.8 = (bf16[16,1152]{1,0:T(8,128)(2,1)S(1)}, bf16[16,1152]{1,0:T(8,128)(2,1)S(1)}, u32[]{:S(2)}, u32[]{:S(2)}) collective-permute-start(bf16[16,1152]{1,0:T(8,128)(2,1)S(1)} %get-tuple-element.45), channel_id=1, source_target_pairs={{0,4},{4,0},{8,12},{12,8},{16,20},{20,16},{24,28},{28,24},{1,5},{5... | collective-permute-start | bytes 110600 | tf_op jit(solution)/shard_map/ppermute | solution.py:169
  58.2 4.0 %collective-permute-start.9 = (bf16[16,1152]{1,0:T(8,128)(2,1)S(1)}, bf16[16,1152]{1,0:T(8,128)(2,1)S(1)}, u32[]{:S(2)}, u32[]{:S(2)}) collective-permute-start(bf16[16,1152]{1,0:T(8,128)(2,1)S(1)} %get-tuple-element.46), channel_id=1, source_target_pairs={{0,8},{4,12},{8,0},{12,4},{16,24},{20,28},{24,16},{28,20},{1,9},{5... | collective-permute-start | bytes 110600 | tf_op jit(solution)/shard_map/ppermute | solution.py:169
  62.2 15.0 %collective-permute-start.15 = (bf16[128,1152]{1,0:T(8,128)(2,1)S(1)}, bf16[128,1152]{1,0:T(8,128)(2,1)S(1)}, u32[]{:S(2)}, u32[]{:S(2)}) collective-permute-start(bf16[128,1152]{1,0:T(8,128)(2,1)S(1)} %shard_map.67.refs_2_), channel_id=1, source_target_pairs={{0,2},{1,3},{2,0},{3,1},{4,6},{5,7},{6,4},{7,5},{8,10},{9,11},{10,... | collective-permute-start | bytes 884744 | tf_op jit(solution)/shard_map/ppermute | solution.py:169
  80.6 5.2 %collective-permute-start.16 = (bf16[576,128]{1,0:T(8,128)(2,1)S(1)}, bf16[576,128]{1,0:T(8,128)(2,1)S(1)}, u32[]{:S(2)}, u32[]{:S(2)}) collective-permute-start(bf16[576,128]{1,0:T(8,128)(2,1)S(1)} %shard_map.69), channel_id=1, source_target_pairs={{0,2},{1,3},{2,0},{3,1},{4,6},{5,7},{6,4},{7,5},{8,10},{9,11},{10,... | collective-permute-start | bytes 442376 | tf_op jit(solution)/shard_map/ppermute | solution.py:169
  85.8 15.8 %collective-permute-start.17 = (bf16[2,288,1152]{2,1,0:T(8,128)(2,1)}, bf16[2,288,1152]{2,1,0:T(8,128)(2,1)S(1)}, u32[]{:S(2)}, u32[]{:S(2)}) collective-permute-start(bf16[2,288,1152]{2,1,0:T(8,128)(2,1)} %bitcast.4), channel_id=1, source_target_pairs={{0,1},{1,0},{2,3},{3,2},{4,5},{5,4},{6,7},{7,6},{8,9},{9,8},{10,11... | collective-permute-start | bytes 3981320 | tf_op jit(solution)/shard_map/ppermute | solution.py:169
  85.9 4.0 %collective-permute-start.18 = (bf16[16,1152]{1,0:T(8,128)(2,1)S(1)}, bf16[16,1152]{1,0:T(8,128)(2,1)S(1)}, u32[]{:S(2)}, u32[]{:S(2)}) collective-permute-start(bf16[16,1152]{1,0:T(8,128)(2,1)S(1)} %get-tuple-element.56), channel_id=1, source_target_pairs={{0,4},{4,0},{8,12},{12,8},{16,20},{20,16},{24,28},{28,24},{1,5},{5... | collective-permute-start | bytes 110600 | tf_op jit(solution)/shard_map/ppermute | solution.py:169
  86.7 5.9 %collective-permute-start.19 = (bf16[16,1152]{1,0:T(8,128)(2,1)S(1)}, bf16[16,1152]{1,0:T(8,128)(2,1)S(1)}, u32[]{:S(2)}, u32[]{:S(2)}) collective-permute-start(bf16[16,1152]{1,0:T(8,128)(2,1)S(1)} %get-tuple-element.57), channel_id=1, source_target_pairs={{0,8},{4,12},{8,0},{12,4},{16,24},{20,28},{24,16},{28,20},{1,9},{5... | collective-permute-start | bytes 110600 | tf_op jit(solution)/shard_map/ppermute | solution.py:169
  86.8 8.1 %collective-permute-start.20 = (bf16[16,1152]{1,0:T(8,128)(2,1)S(1)}, bf16[16,1152]{1,0:T(8,128)(2,1)S(1)}, u32[]{:S(2)}, u32[]{:S(2)}) collective-permute-start(bf16[16,1152]{1,0:T(8,128)(2,1)S(1)} %get-tuple-element.58), channel_id=1, source_target_pairs={{0,12},{4,8},{8,4},{12,0},{16,28},{20,24},{24,20},{28,16},{1,13},{... | collective-permute-start | bytes 110600 | tf_op jit(solution)/shard_map/ppermute | solution.py:169
  89.5 7.7 %collective-permute-start.21 = (bf16[16,1152]{1,0:T(8,128)(2,1)S(1)}, bf16[16,1152]{1,0:T(8,128)(2,1)S(1)}, u32[]{:S(2)}, u32[]{:S(2)}) collective-permute-start(bf16[16,1152]{1,0:T(8,128)(2,1)S(1)} %get-tuple-element.59), channel_id=1, source_target_pairs={{0,16},{4,20},{8,24},{12,28},{16,0},{20,4},{24,8},{28,12},{1,17},{... | collective-permute-start | bytes 110600 | tf_op jit(solution)/shard_map/ppermute | solution.py:169
  89.9 7.2 %collective-permute-start.22 = (bf16[16,1152]{1,0:T(8,128)(2,1)S(1)}, bf16[16,1152]{1,0:T(8,128)(2,1)S(1)}, u32[]{:S(2)}, u32[]{:S(2)}) collective-permute-start(bf16[16,1152]{1,0:T(8,128)(2,1)S(1)} %get-tuple-element.60), channel_id=1, source_target_pairs={{0,20},{4,16},{8,28},{12,24},{16,4},{20,0},{24,12},{28,8},{1,21},{... | collective-permute-start | bytes 110600 | tf_op jit(solution)/shard_map/ppermute | solution.py:169
  92.6 5.9 %collective-permute-start.23 = (bf16[16,1152]{1,0:T(8,128)(2,1)S(1)}, bf16[16,1152]{1,0:T(8,128)(2,1)S(1)}, u32[]{:S(2)}, u32[]{:S(2)}) collective-permute-start(bf16[16,1152]{1,0:T(8,128)(2,1)S(1)} %get-tuple-element.61), channel_id=1, source_target_pairs={{0,24},{4,28},{8,16},{12,20},{16,8},{20,12},{24,0},{28,4},{1,25},{... | collective-permute-start | bytes 110600 | tf_op jit(solution)/shard_map/ppermute | solution.py:169
  95.0 6.7 %collective-permute-start.24 = (bf16[16,1152]{1,0:T(8,128)(2,1)S(1)}, bf16[16,1152]{1,0:T(8,128)(2,1)S(1)}, u32[]{:S(2)}, u32[]{:S(2)}) collective-permute-start(bf16[16,1152]{1,0:T(8,128)(2,1)S(1)} %get-tuple-element.62), channel_id=1, source_target_pairs={{0,28},{4,24},{8,20},{12,16},{16,12},{20,8},{24,4},{28,0},{1,29},{... | collective-permute-start | bytes 110600 | tf_op jit(solution)/shard_map/ppermute | solution.py:169
  101.6 1.3 %copy-start.3 = (bf16[576,1152]{1,0:T(8,128)(2,1)S(1)}, bf16[576,1152]{1,0:T(8,128)(2,1)}, u32[]{:S(2)}) copy-start(bf16[576,1152]{1,0:T(8,128)(2,1)} %all-gather.7.cloned.1.call-done) | copy-start | bytes 3981316
  (3 other events, 3.1 us)
Sparse Core Ops, SparseCore 0:
  8.9 30.2 all-gather.4
  46.7 30.7 all-gather.6

commit v4 on v2

--- a/solution.py
+++ b/solution.py
@@ -37,27 +37,37 @@
     return (grown * (1.0 / total)).astype(BF16)
 
 
-def spatial_kernel(count, mod_ref, weight_ref, *refs):
-    token_refs, out_refs = refs[:count], refs[count : 2 * count]
-    proj_ref, heads_ref = refs[2 * count :]
+def project(mod_ref, weight_ref, token_refs, proj_ref):
     shift, scale = mod_ref[0:1, :], mod_ref[1:2, :]
     block = token_refs[0].shape[1]
+    for at in range(0, len(token_refs), 2):
+        rows = [norm_rows(ref[0].astype(F32), shift, scale) for ref in token_refs[at : at + 2]]
+        rows = jnp.concatenate(rows, axis=0)
+        proj_ref[:, at * block : (at + 2) * block] = dot(weight_ref[...], rows, 1, 1)
+
+
+def near_kernel(mod_ref, weight_ref, own_ref, sister_ref, proj_ref):
+    project(mod_ref, weight_ref, (own_ref, sister_ref), proj_ref)
+
+
+def spatial_kernel(count, mod_ref, weight_ref, near_ref, *refs):
+    token_refs, out_refs = refs[: count - 2], refs[count - 2 : -2]
+    far_ref, heads_ref = refs[-2:]
+    block = token_refs[0].shape[1]
     heads = weight_ref.shape[0] // (3 * HD)
-    step = 2 if count % 2 == 0 else 1
-    for at in range(0, count, step):
-        rows = [
-            norm_rows(token_refs[at + i][0].astype(F32), shift, scale) for i in range(step)
-        ]
-        rows = jnp.concatenate(rows, axis=0)
-        proj_ref[:, at * block : (at + step) * block] = dot(weight_ref[...], rows, 1, 1)
+    project(mod_ref, weight_ref, token_refs, far_ref)
+
+    def whole(start):
+        parts = [ref[start : start + HD, :].astype(BF16) for ref in (near_ref, far_ref)]
+        return jnp.concatenate(parts, axis=1)
+
     for head in range(heads):
         base = head * 3 * HD
-        keys = proj_ref[base + HD : base + 2 * HD, :].astype(BF16).T
-        values = proj_ref[base + 2 * HD : base + 3 * HD, :].astype(BF16)
-        for at in range(0, count, step):
-            cols = slice(at * block, (at + step) * block)
-            query = proj_ref[base : base + HD, cols].astype(BF16)
-            probs = softmax_over_rows(dot(keys, query))
+        queries, keys, values = (whole(base + part * HD) for part in range(3))
+        keys = keys.T
+        for at in range(0, count, 2):
+            cols = slice(at * block, (at + 2) * block)
+            probs = softmax_over_rows(dot(keys, queries[:, cols]))
             heads_ref[head * HD : (head + 1) * HD, cols] = dot(values, probs)
     for at in range(count):
         out_refs[at][...] = heads_ref[:, at * block : (at + 1) * block].astype(BF16)
@@ -74,12 +84,12 @@
     normed_ref[...] = norm_rows(middle.astype(F32), mod_ref[3:4, :], mod_ref[4:5, :])
 
 
-def temporal_kernel(groups, pieces, cores, period, *refs):
+def temporal_kernel(groups, cores, period, *refs):
     weight_refs = refs[:cores]
-    piece_refs = refs[cores : cores + groups * pieces]
-    out_refs = refs[cores + groups * pieces : -2]
+    row_refs = refs[cores : cores + groups]
+    out_refs = refs[cores + groups : -2]
     proj_ref, heads_ref = refs[-2:]
-    rows = jnp.concatenate([ref[...] for ref in piece_refs], axis=0)
+    rows = jnp.concatenate([ref[...] for ref in row_refs], axis=0)
     block = rows.shape[0] // groups
     depth = weight_refs[0].shape[0]
     for core in range(cores):
@@ -101,19 +111,17 @@
         out_refs[group][...] = heads_ref[:, group * block : (group + 1) * block].astype(BF16)
 
 
-def update_kernel(groups, *refs):
-    heads = jnp.concatenate([ref[...] for ref in refs[:groups]], axis=0)
-    weights = jnp.concatenate([ref[...] for ref in refs[groups:-1]], axis=0)
-    refs[-1][...] = dot(heads.T, weights).astype(BF16)
-
-
-def result_kernel(mod_ref, middle_ref, update_ref, out_ref):
-    update = update_ref[...].astype(F32)
-    out_ref[0] = (middle_ref[...].astype(F32) + mod_ref[5:6, :] * update).astype(BF16)
-
-
-def call(body, operands, outs, scratch=(), flops=0, limit=24):
-    moved = sum(x.size * x.dtype.itemsize for x in (*operands, *outs))
+def turn_kernel(*refs):
+    refs[-1][...] = jnp.concatenate([ref[...] for ref in refs[:-1]], axis=0).T
+
+
+def result_kernel(mod_ref, middle_ref, heads_ref, *refs):
+    weights = jnp.concatenate([ref[...] for ref in refs[:-1]], axis=0)
+    update = dot(heads_ref[...], weights)
+    refs[-1][0] = (middle_ref[...].astype(F32) + mod_ref[5:6, :] * update).astype(BF16)
+
+
+def call(body, operands, outs, scratch=(), limit=24):
     return pl.pallas_call(
         body,
         out_shape=outs,
@@ -121,7 +129,7 @@
         out_specs=[pl.BlockSpec(memory_space=pltpu.VMEM)] * len(outs),
         scratch_shapes=list(scratch),
         compiler_params=pltpu.CompilerParams(vmem_limit_bytes=limit * MIB),
-        cost_estimate=pl.CostEstimate(flops=flops, bytes_accessed=moved, transcendentals=0),
+        cost_estimate=pl.CostEstimate(flops=1, bytes_accessed=1, transcendentals=0),
     )(*operands)
 
 
@@ -161,48 +169,44 @@
     early_out = after(spatial_out, sister)
     near_weights = [spatial_out, swap(early_out, "patch", 1)]
     far_weights = across(early_out)[1:]
-    blocks = [tokens, sister] + both_cores([after(block, near_weights[1]) for block in far])
-
+    temporal_pair = [temporal_qkv, swap(after(temporal_qkv, near_weights[1]), "patch", 1)]
+    (near,) = call(
+        near_kernel,
+        (modulation, spatial_qkv, tokens, sister),
+        [shape((3 * shard, 2 * rows), F32)],
+    )
+    far = both_cores([after(block, near) for block in far])
     mixed = call(
         functools.partial(spatial_kernel, count),
-        (modulation, spatial_qkv, *blocks),
+        (modulation, spatial_qkv, near, *far),
         [shape((shard, rows), BF16)] * count,
-        [pltpu.VMEM((3 * shard, count * rows), F32), pltpu.VMEM((shard, count * rows), F32)],
-        flops=2 * count * rows * 3 * shard * width,
+        [pltpu.VMEM((3 * shard, (count - 2) * rows), F32), pltpu.VMEM((shard, count * rows), F32)],
     )
     returned = list(mixed)
     for at in reversed(range(1, count)):
         returned[at] = swap(mixed[at], "patch", at)
-    far_weights = both_cores([after(block, *returned) for block in far_weights])
-    temporal_pair = [temporal_qkv, swap(after(temporal_qkv, returned[1]), "patch", 1)]
-    temporal_weights = across(after(temporal_out, returned[1]))
+    far_weights = both_cores([after(block, *returned[2:]) for block in far_weights])
+    late_out = after(temporal_out, *returned)
+    late_near = [temporal_out, swap(late_out, "patch", 1)]
+    late_far = across(late_out)[1:]
     middle, part = call(
         functools.partial(middle_kernel, count),
         (modulation, tokens, *returned, *near_weights, *far_weights),
         [shape((rows, width), BF16)] * 2,
-        flops=2 * rows * width * width,
-    )
-    part = exchange_frames(part)
-    segments = across(part)
-    temporal_weights = both_cores([after(block, *segments) for block in temporal_weights])
+    )
+    segments = across(exchange_frames(part))
     mixed = call(
-        functools.partial(temporal_kernel, groups, 1, 2, period),
+        functools.partial(temporal_kernel, groups, 2, period),
         (*temporal_pair, *segments),
         [shape((2 * shard, rows), BF16)] * groups,
         [pltpu.VMEM((6 * shard, groups * rows), F32), pltpu.VMEM((2 * shard, groups * rows), F32)],
-        flops=2 * groups * rows * 6 * shard * width,
-    )
+    )
+    late_far = both_cores([after(block, mixed[0]) for block in late_far])
     returned = [swap(mixed[at], "patch", 2 * at) if at else mixed[0] for at in range(groups)]
-    (update,) = call(
-        functools.partial(update_kernel, groups),
-        (*returned, *temporal_weights),
-        [shape((rows, width), BF16)],
-        flops=2 * rows * width * width,
-    )
-    update = exchange_frames(update)
+    (turned,) = call(turn_kernel, returned, [shape((rows, width), BF16)])
     (result,) = call(
         result_kernel,
-        (modulation, middle, update),
+        (modulation, middle, exchange_frames(turned), *late_near, *late_far),
         [shape((1, rows, width), BF16)],
     )
     return result

time: 91.6 us -> 90.4 us (0.987)
  blocking collectives: 15.1 us -> 0 us
  waiting for transfers between devices: 41.9 us -> 48.3 us
  starting transfers between devices: 16.6 us -> 22.3 us
  Pallas kernels: 14.3 us -> 15.9 us
    all_to_all x1 -> x0, blocking collectives: 15.1 us -> none  [exchange_frames(): lax.all_to_all(blocks, 'frame', split_axis=0, concat_axis=0, tiled=True)]
    all_to_all x1 -> x2, waiting for transfers between devices: 8.59 us -> 16.9 us  [exchange_frames(): lax.all_to_all(blocks, 'frame', split_axis=0, concat_axis=0, tiled=True)]
    all_to_all x1 -> x2, starting transfers between devices: 5.8 us -> 11.4 us  [exchange_frames(): lax.all_to_all(blocks, 'frame', split_axis=0, concat_axis=0, tiled=True)]
    ppermute x15, waiting for transfers between devices: 33.3 us -> 31.3 us  [swap(): return lax.ppermute(value, axis, [(at, at ^ offset) for at in range(size)])]
    pallas_call x5 -> x6, Pallas kernels: 14.3 us -> 15.9 us  [call(): pl.pallas_call(body, out_shape=outs, in_specs=[pl.BlockSpec(memory_space=...]
    unnamed x14 -> x16, local copies, waits for them, and re-layouts: 3.3 us -> 3.31 us
  transfers between devices with their start and end apart: 16 -> 17, of which waited for: 10 -> 10; matrix products, arithmetic and copies ran while one was open for 0% -> 0% of each run, Pallas kernels for 13% -> 15%
where the time goes in v4:
time: 90.4 us; the launch traced here: 89.9 us
  waiting for transfers between devices  48.3 us (53%)
  starting transfers between devices  22.3 us (25%)
  Pallas kernels  15.9 us (18%)
  local copies, waits for them, and re-layouts  3.31 us (4%)
    ppermute x15, waiting for transfers between devices, swap(): return lax.ppermute(value, axis, [(at, at ^ offset) for at in range(size)])  31.3 us
    all_to_all x2, waiting for transfers between devices, exchange_frames(): lax.all_to_all(blocks, 'frame', split_axis=0, concat_axis=0, tiled=True)  16.9 us
    pallas_call x6, Pallas kernels, call(): pl.pallas_call(body, out_shape=outs, in_specs=[pl.BlockSpec(memory_space=...  15.9 us
    all_to_all x2, starting transfers between devices, exchange_frames(): lax.all_to_all(blocks, 'frame', split_axis=0, concat_axis=0, tiled=True)  11.4 us
    ppermute x15, starting transfers between devices, swap(): return lax.ppermute(value, axis, [(at, at ^ offset) for at in range(size)])  10.8 us
    unnamed x16, local copies, waits for them, and re-layouts  3.31 us
  transfers between devices with their start and end apart: 17, of which 10 were waited for; matrix products, arithmetic and copies ran while one was open for 0% of the time, Pallas kernels for 15%

profile of v4, /device:TPU:0, one launch (start us, length us, event | category | flops | bytes accessed | tf_op | source)
XLA Modules:
  0.0 89.9 jit_solution(13796504082022488905)
XLA Ops:
  0.0 0.5 collective-permute-start
  0.5 1.4 %collective-permute-done.sister_ref = bf16[1,128,1152]{2,1,0:T(8,128)(2,1)S(1)} collective-permute-done((bf16[1,128,1152]{2,1,0:T(8,128)(2,1)}, bf16[1,128,1152]{2,1,0:T(8,128)(2,1)S(1)}, u32[]{:S(2)}, u32[]{:S(2)}) %collective-permute-start) | collective-permute-done | bytes 294944 | tf_op jit(solution)/shard_map/ppermute | solution.py:138
  1.9 0.4 collective-permute-start.6
  2.2 2.7 %collective-permute-start.1 = (bf16[1,128,1152]{2,1,0:T(8,128)(2,1)}, bf16[1,128,1152]{2,1,0:T(8,128)(2,1)S(1)}, u32[]{:S(2)}, u32[]{:S(2)}) collective-permute-start(bf16[1,128,1152]{2,1,0:T(8,128)(2,1)} %token_ref.1), channel_id=1, source_target_pairs={{0,2},{1,3},{2,0},{3,1},{4,6},{5,7},{6,4},{7,5},{8,10},{9,11},{10,... | collective-permute-start | bytes 884744 | tf_op jit(solution)/shard_map/ppermute | solution.py:138
  4.9 0.0 collective-permute-start.7
  5.0 0.1 collective-permute-start.9
  5.0 1.6 %copy-done = bf16[864,1152]{1,0:T(8,128)(2,1)S(1)} copy-done((bf16[864,1152]{1,0:T(8,128)(2,1)S(1)}, bf16[864,1152]{1,0:T(8,128)(2,1)}, u32[]{:S(2)}) %copy-start) | copy-done | bytes 1990680
  6.6 1.0 %copy-done.2 = bf16[1,128,1152]{2,1,0:T(8,128)(2,1)S(1)} copy-done((bf16[1,128,1152]{2,1,0:T(8,128)(2,1)S(1)}, bf16[1,128,1152]{2,1,0:T(8,128)(2,1)}, u32[]{:S(2)}) %copy-start.2) | copy-done | bytes 294936
  7.5 0.8 copy-done.6
  8.3 1.1 %shard_map.64.near_ref = f32[864,256]{1,0:T(8,128)S(1)} custom-call(f32[6,1152]{1,0:T(8,128)S(1)} %copy-done.6, bf16[864,1152]{1,0:T(8,128)(2,1)S(1)} %copy-done, bf16[1,128,1152]{2,1,0:T(8,128)(2,1)S(1)} %copy-done.2, bf16[1,128,1152]{2,1,0:T(8,128)(2,1)S(1)} %collective-permute-done.sister_ref), custom_call_target="tpu_custom_call" | custom-call | flops 1 | bytes 1 | tf_op jit(solution)/shard_map/pallas_call | solution.py:125
  9.4 3.5 %collective-permute-done.1.refs_0_ = bf16[1,128,1152]{2,1,0:T(8,128)(2,1)S(1)} collective-permute-done((bf16[1,128,1152]{2,1,0:T(8,128)(2,1)}, bf16[1,128,1152]{2,1,0:T(8,128)(2,1)S(1)}, u32[]{:S(2)}, u32[]{:S(2)}) %collective-permute-start.1) | collective-permute-done | bytes 294944 | tf_op jit(solution)/shard_map/ppermute | solution.py:138
  13.0 1.6 %collective-permute-done.2.refs_1_ = bf16[1,128,1152]{2,1,0:T(8,128)(2,1)S(1)} collective-permute-done((bf16[1,128,1152]{2,1,0:T(8,128)(2,1)S(1)}, bf16[1,128,1152]{2,1,0:T(8,128)(2,1)S(1)}, u32[]{:S(2)}, u32[]{:S(2)}) %collective-permute-start.2) | collective-permute-done | bytes 294944 | tf_op jit(solution)/shard_map/ppermute | solution.py:138
  14.5 5.3 %shard_map.65 = (bf16[288,128]{1,0:T(8,128)(2,1)S(1)}, bf16[288,128]{1,0:T(8,128)(2,1)S(1)}, bf16[288,128]{1,0:T(8,128)(2,1)S(1)}, bf16[288,128]{1,0:T(8,128)(2,1)S(1)}) custom-call(f32[6,1152]{1,0:T(8,128)S(1)} %copy-done.6, bf16[864,1152]{1,0:T(8,128)(2,1)S(1)} %copy-done, f32[864,256]{1,0:T(8,128)S(1)} %shard_map.64.near_ref, ...), custom_call_target="tpu_custom_call" | custom-call | flops 1 | bytes 1 | tf_op jit(solution)/shard_map/pallas_call | solution.py:125
  19.8 2.1 %collective-permute-start.4 = (bf16[288,128]{1,0:T(8,128)(2,1)S(1)}, bf16[288,128]{1,0:T(8,128)(2,1)S(1)}, u32[]{:S(2)}, u32[]{:S(2)}) collective-permute-start(bf16[288,128]{1,0:T(8,128)(2,1)S(1)} %get-tuple-element.22), channel_id=1, source_target_pairs={{0,2},{1,3},{2,0},{3,1},{4,6},{5,7},{6,4},{7,5},{8,10},{9,11},{10,... | collective-permute-start | bytes 221192 | tf_op jit(solution)/shard_map/ppermute | solution.py:138
  21.9 6.9 %collective-permute-done.4.refs_2_ = bf16[288,128]{1,0:T(8,128)(2,1)S(1)} collective-permute-done((bf16[288,128]{1,0:T(8,128)(2,1)S(1)}, bf16[288,128]{1,0:T(8,128)(2,1)S(1)}, u32[]{:S(2)}, u32[]{:S(2)}) %collective-permute-start.4) | collective-permute-done | bytes 73760 | tf_op jit(solution)/shard_map/ppermute | solution.py:138
  28.8 0.9 %collective-permute-done.5.refs_3_ = bf16[288,128]{1,0:T(8,128)(2,1)S(1)} collective-permute-done((bf16[288,128]{1,0:T(8,128)(2,1)S(1)}, bf16[288,128]{1,0:T(8,128)(2,1)S(1)}, u32[]{:S(2)}, u32[]{:S(2)}) %collective-permute-start.5) | collective-permute-done | bytes 73760 | tf_op jit(solution)/shard_map/ppermute | solution.py:138
  29.7 0.1 collective-permute-start.8
  29.9 0.4 collective-permute-start.3
  30.2 1.7 %collective-permute-done.3.refs_1_ = bf16[288,128]{1,0:T(8,128)(2,1)S(1)} collective-permute-done((bf16[288,128]{1,0:T(8,128)(2,1)S(1)}, bf16[288,128]{1,0:T(8,128)(2,1)S(1)}, u32[]{:S(2)}, u32[]{:S(2)}) %collective-permute-start.3) | collective-permute-done | bytes 73760 | tf_op jit(solution)/shard_map/ppermute | solution.py:138
  31.9 1.6 %shard_map.66 = (bf16[128,1152]{1,0:T(8,128)(2,1)S(1)}, bf16[128,1152]{1,0:T(8,128)(2,1)}) custom-call(f32[6,1152]{1,0:T(8,128)S(1)} %copy-done.6, bf16[1,128,1152]{2,1,0:T(8,128)(2,1)S(1)} %copy-done.3, bf16[288,128]{1,0:T(8,128)(2,1)S(1)} %get-tuple-element.20.refs_0_, bf16[288,128]{1,0:T(8,128)(2,1)S(1)} %collective-permute-done.3.refs_1_, ...), custom_call_target="tpu_custom_call" | custom-call | flops 1 | bytes 1 | tf_op jit(solution)/shard_map/pallas_call | solution.py:125
  33.6 5.8 %all-to-all-start = ((bf16[8,16,1152]{2,1,0:T(8,128)(2,1)}), bf16[8,16,1152]{2,1,0:T(8,128)(2,1)S(1)}, u32[]{:S(2)}, u32[]{:S(2)}) async-start(bf16[8,16,1152]{2,1,0:T(8,128)(2,1)} %bitcast), calls=%async_computation | async-start | bytes 589824 | tf_op jit(solution)/shard_map/all_to_all | solution.py:164
  39.4 1.6 %collective-permute-start.13 = (bf16[288,1152]{1,0:T(8,128)(2,1)S(1)}, bf16[288,1152]{1,0:T(8,128)(2,1)}, u32[]{:S(2)}, u32[]{:S(2)}) collective-permute-start(bf16[288,1152]{1,0:T(8,128)(2,1)S(1)} %copy-done.5), channel_id=1, source_target_pairs={{0,2},{1,3},{2,0},{3,1},{4,6},{5,7},{6,4},{7,5},{8,10},{9,11},{10,... | collective-permute-start | bytes 1990664 | tf_op jit(solution)/shard_map/ppermute | solution.py:138
  41.0 8.5 %all-to-all-done = bf16[8,16,1152]{2,1,0:T(8,128)(2,1)S(1)} async-done(((bf16[8,16,1152]{2,1,0:T(8,128)(2,1)}), bf16[8,16,1152]{2,1,0:T(8,128)(2,1)S(1)}, u32[]{:S(2)}, u32[]{:S(2)}) %all-to-all-start) | async-done | bytes 294944 | tf_op jit(solution)/shard_map/all_to_all | solution.py:164
  49.5 1.5 %collective-permute-start.10 = (bf16[128,1152]{1,0:T(8,128)(2,1)S(1)}, bf16[128,1152]{1,0:T(8,128)(2,1)S(1)}, u32[]{:S(2)}, u32[]{:S(2)}) collective-permute-start(bf16[128,1152]{1,0:T(8,128)(2,1)S(1)} %bitcast.4), channel_id=1, source_target_pairs={{0,2},{1,3},{2,0},{3,1},{4,6},{5,7},{6,4},{7,5},{8,10},{9,11},{10,... | collective-permute-start | bytes 884744 | tf_op jit(solution)/shard_map/ppermute | solution.py:138
  51.0 11.7 %collective-permute-done.10.refs_3_ = bf16[128,1152]{1,0:T(8,128)(2,1)S(1)} collective-permute-done((bf16[128,1152]{1,0:T(8,128)(2,1)S(1)}, bf16[128,1152]{1,0:T(8,128)(2,1)S(1)}, u32[]{:S(2)}, u32[]{:S(2)}) %collective-permute-start.10) | collective-permute-done | bytes 294944 | tf_op jit(solution)/shard_map/ppermute | solution.py:138
  62.7 4.5 %shard_map.67 = (bf16[576,128]{1,0:T(8,128)(2,1)S(1)}, bf16[576,128]{1,0:T(8,128)(2,1)S(1)}) custom-call(bf16[864,1152]{1,0:T(8,128)(2,1)S(1)} %copy-done.1, bf16[864,1152]{1,0:T(8,128)(2,1)} %collective-permute-done.9.refs_1_, bf16[128,1152]{1,0:T(8,128)(2,1)S(1)} %bitcast.5, bf16[128,1152]{1,0:T(8,128)(2,1)S(1)} %collective-permute-done.10.refs_3_), custom_call_target="tpu_custom_call" | custom-call | flops 1 | bytes 1 | tf_op jit(solution)/shard_map/pallas_call | solution.py:125
  67.1 1.5 %collective-permute-start.11 = (bf16[576,128]{1,0:T(8,128)(2,1)S(1)}, bf16[576,128]{1,0:T(8,128)(2,1)S(1)}, u32[]{:S(2)}, u32[]{:S(2)}) collective-permute-start(bf16[576,128]{1,0:T(8,128)(2,1)S(1)} %get-tuple-element.30), channel_id=1, source_target_pairs={{0,2},{1,3},{2,0},{3,1},{4,6},{5,7},{6,4},{7,5},{8,10},{9,11},{10,... | collective-permute-start | bytes 442376 | tf_op jit(solution)/shard_map/ppermute | solution.py:138
  68.7 3.6 %collective-permute-done.11.refs_1_ = bf16[576,128]{1,0:T(8,128)(2,1)S(1)} collective-permute-done((bf16[576,128]{1,0:T(8,128)(2,1)S(1)}, bf16[576,128]{1,0:T(8,128)(2,1)S(1)}, u32[]{:S(2)}, u32[]{:S(2)}) %collective-permute-start.11) | collective-permute-done | bytes 147488 | tf_op jit(solution)/shard_map/ppermute | solution.py:138
  72.3 0.9 shard_map.68
  73.2 5.6 %all-to-all-start.1 = ((bf16[8,16,1152]{2,1,0:T(8,128)(2,1)}), bf16[8,16,1152]{2,1,0:T(8,128)(2,1)S(1)}, u32[]{:S(2)}, u32[]{:S(2)}) async-start(bf16[8,16,1152]{2,1,0:T(8,128)(2,1)} %bitcast.2), calls=%async_computation.1 | async-start | bytes 589824 | tf_op jit(solution)/shard_map/all_to_all | solution.py:164
  78.8 8.4 %all-to-all-done.1 = bf16[8,16,1152]{2,1,0:T(8,128)(2,1)S(1)} async-done(((bf16[8,16,1152]{2,1,0:T(8,128)(2,1)}), bf16[8,16,1152]{2,1,0:T(8,128)(2,1)S(1)}, u32[]{:S(2)}, u32[]{:S(2)}) %all-to-all-start.1) | async-done | bytes 294944 | tf_op jit(solution)/shard_map/all_to_all | solution.py:164
  87.3 2.6 %shard_map.69 = bf16[1,128,1152]{2,1,0:T(8,128)(2,1)} custom-call(f32[6,1152]{1,0:T(8,128)S(1)} %copy-done.7, bf16[128,1152]{1,0:T(8,128)(2,1)S(1)} %get-tuple-element.26.middle_ref, bf16[128,1152]{1,0:T(8,128)(2,1)S(1)} %bitcast.6, bf16[288,1152]{1,0:T(8,128)(2,1)S(1)} %copy-done.5, bf16[288,1152]{1,0:T(8,128)(2,1)} %collective-permute-done.12.refs_1_, ...), custom_call_target="tpu_custom_call" | custom-call | flops 1 | bytes 1 | tf_op jit(solution)/shard_map/pallas_call | solution.py:125
  (24 shorter events, 0.1 us)
Async XLA Ops:
  0.0 1.9 %collective-permute-start = (bf16[1,128,1152]{2,1,0:T(8,128)(2,1)}, bf16[1,128,1152]{2,1,0:T(8,128)(2,1)S(1)}, u32[]{:S(2)}, u32[]{:S(2)}) collective-permute-start(bf16[1,128,1152]{2,1,0:T(8,128)(2,1)} %token_ref.1), channel_id=1, source_target_pairs={{0,1},{1,0},{2,3},{3,2},{4,5},{5,4},{6,7},{7,6},{8,9},{9,8},{10,11... | collective-permute-start | bytes 884744 | tf_op jit(solution)/shard_map/ppermute | solution.py:138
  1.9 3.1 %collective-permute-start.6 = (bf16[288,1152]{1,0:T(8,128)(2,1)}, bf16[288,1152]{1,0:T(8,128)(2,1)S(1)}, u32[]{:S(2)}, u32[]{:S(2)}) collective-permute-start(bf16[288,1152]{1,0:T(8,128)(2,1)} %refs_4_.1), channel_id=1, source_target_pairs={{0,1},{1,0},{2,3},{3,2},{4,5},{5,4},{6,7},{7,6},{8,9},{9,8},{10,11... | collective-permute-start | bytes 1990664 | tf_op jit(solution)/shard_map/ppermute | solution.py:138
  2.2 10.7 %collective-permute-start.1 = (bf16[1,128,1152]{2,1,0:T(8,128)(2,1)}, bf16[1,128,1152]{2,1,0:T(8,128)(2,1)S(1)}, u32[]{:S(2)}, u32[]{:S(2)}) collective-permute-start(bf16[1,128,1152]{2,1,0:T(8,128)(2,1)} %token_ref.1), channel_id=1, source_target_pairs={{0,2},{1,3},{2,0},{3,1},{4,6},{5,7},{6,4},{7,5},{8,10},{9,11},{10,... | collective-permute-start | bytes 884744 | tf_op jit(solution)/shard_map/ppermute | solution.py:138
  4.9 24.8 %collective-permute-start.7 = (bf16[288,1152]{1,0:T(8,128)(2,1)}, bf16[288,1152]{1,0:T(8,128)(2,1)S(1)}, u32[]{:S(2)}, u32[]{:S(2)}) collective-permute-start(bf16[288,1152]{1,0:T(8,128)(2,1)} %refs_4_.1), channel_id=1, source_target_pairs={{0,2},{1,3},{2,0},{3,1},{4,6},{5,7},{6,4},{7,5},{8,10},{9,11},{10,... | collective-permute-start | bytes 1990664 | tf_op jit(solution)/shard_map/ppermute | solution.py:138
  5.0 57.7 %collective-permute-start.9 = (bf16[864,1152]{1,0:T(8,128)(2,1)}, bf16[864,1152]{1,0:T(8,128)(2,1)}, u32[]{:S(2)}, u32[]{:S(2)}) collective-permute-start(bf16[864,1152]{1,0:T(8,128)(2,1)} %refs_0_.2), channel_id=1, source_target_pairs={{0,1},{1,0},{2,3},{3,2},{4,5},{5,4},{6,7},{7,6},{8,9},{9,8},{10,11... | collective-permute-start | bytes 5971976 | tf_op jit(solution)/shard_map/ppermute | solution.py:138
  5.0 1.6 %copy-start = (bf16[864,1152]{1,0:T(8,128)(2,1)S(1)}, bf16[864,1152]{1,0:T(8,128)(2,1)}, u32[]{:S(2)}) copy-start(bf16[864,1152]{1,0:T(8,128)(2,1)} %weight_ref.3) | copy-start | bytes 5971972
  6.6 1.0 %copy-start.2 = (bf16[1,128,1152]{2,1,0:T(8,128)(2,1)S(1)}, bf16[1,128,1152]{2,1,0:T(8,128)(2,1)}, u32[]{:S(2)}) copy-start(bf16[1,128,1152]{2,1,0:T(8,128)(2,1)} %token_ref.1) | copy-start | bytes 884740
  7.5 0.8 copy-start.6
  9.4 22.5 %copy-start.3 = (bf16[1,128,1152]{2,1,0:T(8,128)(2,1)S(1)}, bf16[1,128,1152]{2,1,0:T(8,128)(2,1)}, u32[]{:S(2)}) copy-start(bf16[1,128,1152]{2,1,0:T(8,128)(2,1)} %token_ref.1) | copy-start | bytes 884740
  9.4 22.5 %copy-start.4 = (bf16[288,1152]{1,0:T(8,128)(2,1)S(1)}, bf16[288,1152]{1,0:T(8,128)(2,1)}, u32[]{:S(2)}) copy-start(bf16[288,1152]{1,0:T(8,128)(2,1)} %refs_4_.1) | copy-start | bytes 1990660
  13.0 1.6 %collective-permute-start.2 = (bf16[1,128,1152]{2,1,0:T(8,128)(2,1)S(1)}, bf16[1,128,1152]{2,1,0:T(8,128)(2,1)S(1)}, u32[]{:S(2)}, u32[]{:S(2)}) collective-permute-start(bf16[1,128,1152]{2,1,0:T(8,128)(2,1)S(1)} %collective-permute-done.1.refs_0_), channel_id=1, source_target_pairs={{0,1},{1,0},{2,3},{3,2},{4,5},{5,4},{6,7},{7,6},{8,9},{9,8},{10,11... | collective-permute-start | bytes 884744 | tf_op jit(solution)/shard_map/ppermute | solution.py:138
  19.8 19.6 %copy-start.5 = (bf16[288,1152]{1,0:T(8,128)(2,1)S(1)}, bf16[288,1152]{1,0:T(8,128)(2,1)}, u32[]{:S(2)}) copy-start(bf16[288,1152]{1,0:T(8,128)(2,1)} %refs_0_.3) | copy-start | bytes 1990660
  19.8 42.8 %copy-start.1 = (bf16[864,1152]{1,0:T(8,128)(2,1)S(1)}, bf16[864,1152]{1,0:T(8,128)(2,1)}, u32[]{:S(2)}) copy-start(bf16[864,1152]{1,0:T(8,128)(2,1)} %refs_0_.2) | copy-start | bytes 5971972
  19.8 8.9 %collective-permute-start.4 = (bf16[288,128]{1,0:T(8,128)(2,1)S(1)}, bf16[288,128]{1,0:T(8,128)(2,1)S(1)}, u32[]{:S(2)}, u32[]{:S(2)}) collective-permute-start(bf16[288,128]{1,0:T(8,128)(2,1)S(1)} %get-tuple-element.22), channel_id=1, source_target_pairs={{0,2},{1,3},{2,0},{3,1},{4,6},{5,7},{6,4},{7,5},{8,10},{9,11},{10,... | collective-permute-start | bytes 221192 | tf_op jit(solution)/shard_map/ppermute | solution.py:138
  21.9 7.8 %collective-permute-start.5 = (bf16[288,128]{1,0:T(8,128)(2,1)S(1)}, bf16[288,128]{1,0:T(8,128)(2,1)S(1)}, u32[]{:S(2)}, u32[]{:S(2)}) collective-permute-start(bf16[288,128]{1,0:T(8,128)(2,1)S(1)} %get-tuple-element.23), channel_id=1, source_target_pairs={{0,3},{1,2},{2,1},{3,0},{4,7},{5,6},{6,5},{7,4},{8,11},{9,10},{10,... | collective-permute-start | bytes 221192 | tf_op jit(solution)/shard_map/ppermute | solution.py:138
  29.7 2.2 %collective-permute-start.8 = (bf16[288,1152]{1,0:T(8,128)(2,1)S(1)}, bf16[288,1152]{1,0:T(8,128)(2,1)S(1)}, u32[]{:S(2)}, u32[]{:S(2)}) collective-permute-start(bf16[288,1152]{1,0:T(8,128)(2,1)S(1)} %collective-permute-done.7.refs_6_), channel_id=1, source_target_pairs={{0,1},{1,0},{2,3},{3,2},{4,5},{5,4},{6,7},{7,6},{8,9},{9,8},{10,11... | collective-permute-start | bytes 1990664 | tf_op jit(solution)/shard_map/ppermute | solution.py:138
  29.9 2.1 %collective-permute-start.3 = (bf16[288,128]{1,0:T(8,128)(2,1)S(1)}, bf16[288,128]{1,0:T(8,128)(2,1)S(1)}, u32[]{:S(2)}, u32[]{:S(2)}) collective-permute-start(bf16[288,128]{1,0:T(8,128)(2,1)S(1)} %get-tuple-element.21), channel_id=1, source_target_pairs={{0,1},{1,0},{2,3},{3,2},{4,5},{5,4},{6,7},{7,6},{8,9},{9,8},{10,11... | collective-permute-start | bytes 221192 | tf_op jit(solution)/shard_map/ppermute | solution.py:138
  33.6 15.9 %all-to-all-start = ((bf16[8,16,1152]{2,1,0:T(8,128)(2,1)}), bf16[8,16,1152]{2,1,0:T(8,128)(2,1)S(1)}, u32[]{:S(2)}, u32[]{:S(2)}) async-start(bf16[8,16,1152]{2,1,0:T(8,128)(2,1)} %bitcast), calls=%async_computation | async-start | bytes 589824 | tf_op jit(solution)/shard_map/all_to_all | solution.py:164
  39.4 29.3 %collective-permute-start.13 = (bf16[288,1152]{1,0:T(8,128)(2,1)S(1)}, bf16[288,1152]{1,0:T(8,128)(2,1)}, u32[]{:S(2)}, u32[]{:S(2)}) collective-permute-start(bf16[288,1152]{1,0:T(8,128)(2,1)S(1)} %copy-done.5), channel_id=1, source_target_pairs={{0,2},{1,3},{2,0},{3,1},{4,6},{5,7},{6,4},{7,5},{8,10},{9,11},{10,... | collective-permute-start | bytes 1990664 | tf_op jit(solution)/shard_map/ppermute | solution.py:138
  49.5 37.8 %copy-start.7 = (f32[6,1152]{1,0:T(8,128)S(1)}, f32[6,1152]{1,0:T(8,128)}, u32[]{:S(2)}) copy-start(f32[6,1152]{1,0:T(8,128)} %mod_ref.7) | copy-start | bytes 82948
  49.5 13.2 %collective-permute-start.10 = (bf16[128,1152]{1,0:T(8,128)(2,1)S(1)}, bf16[128,1152]{1,0:T(8,128)(2,1)S(1)}, u32[]{:S(2)}, u32[]{:S(2)}) collective-permute-start(bf16[128,1152]{1,0:T(8,128)(2,1)S(1)} %bitcast.4), channel_id=1, source_target_pairs={{0,2},{1,3},{2,0},{3,1},{4,6},{5,7},{6,4},{7,5},{8,10},{9,11},{10,... | collective-permute-start | bytes 884744 | tf_op jit(solution)/shard_map/ppermute | solution.py:138
  51.0 27.8 %collective-permute-start.12 = (bf16[288,1152]{1,0:T(8,128)(2,1)S(1)}, bf16[288,1152]{1,0:T(8,128)(2,1)}, u32[]{:S(2)}, u32[]{:S(2)}) collective-permute-start(bf16[288,1152]{1,0:T(8,128)(2,1)S(1)} %copy-done.5), channel_id=1, source_target_pairs={{0,1},{1,0},{2,3},{3,2},{4,5},{5,4},{6,7},{7,6},{8,9},{9,8},{10,11... | collective-permute-start | bytes 1990664 | tf_op jit(solution)/shard_map/ppermute | solution.py:138
  67.1 5.2 %collective-permute-start.11 = (bf16[576,128]{1,0:T(8,128)(2,1)S(1)}, bf16[576,128]{1,0:T(8,128)(2,1)S(1)}, u32[]{:S(2)}, u32[]{:S(2)}) collective-permute-start(bf16[576,128]{1,0:T(8,128)(2,1)S(1)} %get-tuple-element.30), channel_id=1, source_target_pairs={{0,2},{1,3},{2,0},{3,1},{4,6},{5,7},{6,4},{7,5},{8,10},{9,11},{10,... | collective-permute-start | bytes 442376 | tf_op jit(solution)/shard_map/ppermute | solution.py:138
  68.7 18.6 %collective-permute-start.14 = (bf16[288,1152]{1,0:T(8,128)(2,1)}, bf16[288,1152]{1,0:T(8,128)(2,1)S(1)}, u32[]{:S(2)}, u32[]{:S(2)}) collective-permute-start(bf16[288,1152]{1,0:T(8,128)(2,1)} %collective-permute-done.13.refs_2_), channel_id=1, source_target_pairs={{0,1},{1,0},{2,3},{3,2},{4,5},{5,4},{6,7},{7,6},{8,9},{9,8},{10,11... | collective-permute-start | bytes 1990664 | tf_op jit(solution)/shard_map/ppermute | solution.py:138
  73.2 14.1 %all-to-all-start.1 = ((bf16[8,16,1152]{2,1,0:T(8,128)(2,1)}), bf16[8,16,1152]{2,1,0:T(8,128)(2,1)S(1)}, u32[]{:S(2)}, u32[]{:S(2)}) async-start(bf16[8,16,1152]{2,1,0:T(8,128)(2,1)} %bitcast.2), calls=%async_computation.1 | async-start | bytes 589824 | tf_op jit(solution)/shard_map/all_to_all | solution.py:164

commit v5 on v4

--- a/solution.py
+++ b/solution.py
@@ -51,8 +51,7 @@
 
 
 def spatial_kernel(count, mod_ref, weight_ref, near_ref, *refs):
-    token_refs, out_refs = refs[: count - 2], refs[count - 2 : -2]
-    far_ref, heads_ref = refs[-2:]
+    token_refs, (kept_ref, sent_ref, far_ref, heads_ref) = refs[: count - 2], refs[count - 2 :]
     block = token_refs[0].shape[1]
     heads = weight_ref.shape[0] // (3 * HD)
     project(mod_ref, weight_ref, token_refs, far_ref)
@@ -70,31 +69,39 @@
             probs = softmax_over_rows(dot(keys, queries[:, cols]))
             heads_ref[head * HD : (head + 1) * HD, cols] = dot(values, probs)
     for at in range(count):
-        out_refs[at][...] = heads_ref[:, at * block : (at + 1) * block].astype(BF16)
-
-
-def middle_kernel(count, mod_ref, token_ref, *refs):
-    head_refs, weight_refs = refs[:count], refs[count : 2 * count]
-    middle_ref, normed_ref = refs[2 * count :]
-    heads = jnp.concatenate([ref[...] for ref in head_refs], axis=0)
+        out_ref = (kept_ref, sent_ref)[at % 2]
+        cols = slice(at // 2 * block, (at // 2 + 1) * block)
+        out_ref[:, cols] = heads_ref[:, at * block : (at + 1) * block].astype(BF16)
+
+
+def partial_kernel(first, *refs):
+    head_refs, weight_refs, out_refs = refs[:2], refs[2:4], refs[4:]
     weights = jnp.concatenate([ref[...] for ref in weight_refs], axis=0)
-    update = dot(heads.T, weights)
+    block = out_refs[0].shape[0]
+    for at, ref in enumerate(out_refs, first):
+        cols = slice(at * block, (at + 1) * block)
+        heads = jnp.concatenate([heads[:, cols] for heads in head_refs], axis=0)
+        ref[...] = dot(heads.T, weights).astype(ref.dtype)
+
+
+def middle_kernel(mod_ref, token_ref, *refs):
+    middle_ref, normed_ref = refs[-2:]
+    update = sum(ref[...].astype(F32) for ref in refs[:-2])
     middle = (token_ref[0].astype(F32) + mod_ref[2:3, :] * update).astype(BF16)
     middle_ref[...] = middle
     normed_ref[...] = norm_rows(middle.astype(F32), mod_ref[3:4, :], mod_ref[4:5, :])
 
 
-def temporal_kernel(groups, cores, period, *refs):
-    weight_refs = refs[:cores]
-    row_refs = refs[cores : cores + groups]
-    out_refs = refs[cores + groups : -2]
+def temporal_kernel(groups, period, *refs):
+    weight_refs, output_refs, row_refs = refs[:2], refs[2:4], refs[4 : 4 + groups]
+    update_refs = refs[4 + groups : -2]
     proj_ref, heads_ref = refs[-2:]
     rows = jnp.concatenate([ref[...] for ref in row_refs], axis=0)
     block = rows.shape[0] // groups
     depth = weight_refs[0].shape[0]
-    for core in range(cores):
+    for core in range(2):
         proj_ref[core * depth : (core + 1) * depth, :] = dot(weight_refs[core][...], rows, 1, 1)
-    heads = cores * depth // (3 * HD)
+    heads = 2 * depth // (3 * HD)
     key_patch = lax.broadcasted_iota(jnp.int32, (block, block), 0) % period
     query_patch = lax.broadcasted_iota(jnp.int32, (block, block), 1) % period
     mask = key_patch == query_patch
@@ -107,18 +114,19 @@
             values = proj_ref[base + 2 * HD : base + 3 * HD, cols].astype(BF16)
             probs = softmax_over_rows(dot(keys.T, query), mask)
             heads_ref[head * HD : (head + 1) * HD, cols] = dot(values, probs)
-    for group in range(groups):
-        out_refs[group][...] = heads_ref[:, group * block : (group + 1) * block].astype(BF16)
-
-
-def turn_kernel(*refs):
-    refs[-1][...] = jnp.concatenate([ref[...] for ref in refs[:-1]], axis=0).T
-
-
-def result_kernel(mod_ref, middle_ref, heads_ref, *refs):
-    weights = jnp.concatenate([ref[...] for ref in refs[:-1]], axis=0)
-    update = dot(heads_ref[...], weights)
-    refs[-1][0] = (middle_ref[...].astype(F32) + mod_ref[5:6, :] * update).astype(BF16)
+    weights = jnp.concatenate([ref[...] for ref in output_refs], axis=0)
+    for group, ref in enumerate(update_refs):
+        mixed = heads_ref[:, group * block : (group + 1) * block].astype(BF16)
+        ref[...] = dot(mixed.T, weights).astype(ref.dtype)
+
+
+def sum_kernel(*refs):
+    refs[-1][...] = sum(ref[...].astype(F32) for ref in refs[:-1]).astype(BF16)
+
+
+def result_kernel(mod_ref, middle_ref, update_ref, out_ref):
+    update = update_ref[...].astype(F32)
+    out_ref[0] = (middle_ref[...].astype(F32) + mod_ref[5:6, :] * update).astype(BF16)
 
 
 def call(body, operands, outs, scratch=(), limit=24):
@@ -164,49 +172,58 @@
         blocks = lax.all_to_all(blocks, "frame", split_axis=0, concat_axis=0, tiled=True)
         return blocks.reshape(rows, width)
 
+    def with_sister(weights, *others):
+        return [weights, swap(after(weights, *others), "patch", 1)]
+
+    def return_far(parts):
+        return [swap(part, "patch", 2 * at) for at, part in enumerate(parts, 1)]
+
+    own_update = [shape((rows, width), F32)]
+    far_updates = [shape((rows, width), BF16)] * (groups - 1)
+
     sister = swap(tokens, "patch", 1)
     far = across(tokens)[1:]
-    early_out = after(spatial_out, sister)
-    near_weights = [spatial_out, swap(early_out, "patch", 1)]
-    far_weights = across(early_out)[1:]
-    temporal_pair = [temporal_qkv, swap(after(temporal_qkv, near_weights[1]), "patch", 1)]
     (near,) = call(
         near_kernel,
         (modulation, spatial_qkv, tokens, sister),
         [shape((3 * shard, 2 * rows), F32)],
     )
     far = both_cores([after(block, near) for block in far])
-    mixed = call(
+    out_pair = with_sister(spatial_out, *far)
+    temporal_pair = with_sister(temporal_qkv, *far)
+    late_pair = with_sister(temporal_out, *far)
+
+    kept, sent = call(
         functools.partial(spatial_kernel, count),
         (modulation, spatial_qkv, near, *far),
-        [shape((shard, rows), BF16)] * count,
+        [shape((shard, groups * rows), BF16)] * 2,
         [pltpu.VMEM((3 * shard, (count - 2) * rows), F32), pltpu.VMEM((shard, count * rows), F32)],
     )
-    returned = list(mixed)
-    for at in reversed(range(1, count)):
-        returned[at] = swap(mixed[at], "patch", at)
-    far_weights = both_cores([after(block, *returned[2:]) for block in far_weights])
-    late_out = after(temporal_out, *returned)
-    late_near = [temporal_out, swap(late_out, "patch", 1)]
-    late_far = across(late_out)[1:]
+    heads = (kept, swap(sent, "patch", 1))
+    parts = call(functools.partial(partial_kernel, 1), (*heads, *out_pair), far_updates)
+    own = call(functools.partial(partial_kernel, 0), (*heads, *out_pair), own_update)
     middle, part = call(
-        functools.partial(middle_kernel, count),
-        (modulation, tokens, *returned, *near_weights, *far_weights),
+        middle_kernel,
+        (modulation, tokens, *own, *return_far(parts)),
         [shape((rows, width), BF16)] * 2,
     )
+
+    def attend(segments, updates):
+        columns = len(segments) * rows
+        return call(
+            functools.partial(temporal_kernel, len(segments), period),
+            (*temporal_pair, *late_pair, *segments),
+            updates,
+            [pltpu.VMEM((6 * shard, columns), F32), pltpu.VMEM((2 * shard, columns), F32)],
+        )
+
     segments = across(exchange_frames(part))
-    mixed = call(
-        functools.partial(temporal_kernel, groups, 2, period),
-        (*temporal_pair, *segments),
-        [shape((2 * shard, rows), BF16)] * groups,
-        [pltpu.VMEM((6 * shard, groups * rows), F32), pltpu.VMEM((2 * shard, groups * rows), F32)],
-    )
-    late_far = both_cores([after(block, mixed[0]) for block in late_far])
-    returned = [swap(mixed[at], "patch", 2 * at) if at else mixed[0] for at in range(groups)]
-    (turned,) = call(turn_kernel, returned, [shape((rows, width), BF16)])
+    own = attend(segments[:1], own_update)
+    parts = attend(segments[1:], far_updates)
+    (update,) = call(sum_kernel, (*own, *return_far(parts)), [shape((rows, width), BF16)])
     (result,) = call(
         result_kernel,
-        (modulation, middle, exchange_frames(turned), *late_near, *late_far),
+        (modulation, middle, exchange_frames(update)),
         [shape((1, rows, width), BF16)],
     )
     return result

time: 90.4 us -> 79.4 us (0.88)
  waiting for transfers between devices: 48.3 us -> 29 us
  blocking collectives: 0 us -> 14.3 us
  starting transfers between devices: 22.3 us -> 14.7 us
  Pallas kernels: 15.9 us -> 16.9 us
    all_to_all x0 -> x1, blocking collectives: none -> 14.3 us  [exchange_frames(): lax.all_to_all(blocks, 'frame', split_axis=0, concat_axis=0, tiled=True)]
    ppermute x15 -> x10, waiting for transfers between devices: 31.3 us -> 19.9 us  [swap(): return lax.ppermute(value, axis, [(at, at ^ offset) for at in range(size)])]
    all_to_all x2 -> x1, waiting for transfers between devices: 16.9 us -> 9.07 us  [exchange_frames(): lax.all_to_all(blocks, 'frame', split_axis=0, concat_axis=0, tiled=True)]
    all_to_all x2 -> x1, starting transfers between devices: 11.4 us -> 6.02 us  [exchange_frames(): lax.all_to_all(blocks, 'frame', split_axis=0, concat_axis=0, tiled=True)]
    ppermute x15 -> x10, starting transfers between devices: 10.8 us -> 8.67 us  [swap(): return lax.ppermute(value, axis, [(at, at ^ offset) for at in range(size)])]
    pallas_call x6 -> x9, Pallas kernels: 15.9 us -> 16.9 us  [call(): pl.pallas_call(body, out_shape=outs, in_specs=[pl.BlockSpec(memory_space=...]
    unnamed x16 -> x20, local copies, waits for them, and re-layouts: 3.31 us -> 4.02 us
  transfers between devices with their start and end apart: 17 -> 11, of which waited for: 10 -> 7; matrix products, arithmetic and copies ran while one was open for 0% -> 0% of each run, Pallas kernels for 15% -> 15%
where the time goes in v5:
time: 79.4 us; the launch traced here: 79 us
  waiting for transfers between devices  29 us (37%)
  Pallas kernels  16.9 us (21%)
  starting transfers between devices  14.7 us (19%)
  blocking collectives  14.3 us (18%)
  local copies, waits for them, and re-layouts  4.02 us (5%)
    ppermute x10, waiting for transfers between devices, swap(): return lax.ppermute(value, axis, [(at, at ^ offset) for at in range(size)])  19.9 us
    pallas_call x9, Pallas kernels, call(): pl.pallas_call(body, out_shape=outs, in_specs=[pl.BlockSpec(memory_space=...  16.9 us
    all_to_all x1, blocking collectives, exchange_frames(): lax.all_to_all(blocks, 'frame', split_axis=0, concat_axis=0, tiled=True)  14.3 us
    all_to_all x1, waiting for transfers between devices, exchange_frames(): lax.all_to_all(blocks, 'frame', split_axis=0, concat_axis=0, tiled=True)  9.07 us
    ppermute x10, starting transfers between devices, swap(): return lax.ppermute(value, axis, [(at, at ^ offset) for at in range(size)])  8.67 us
    all_to_all x1, starting transfers between devices, exchange_frames(): lax.all_to_all(blocks, 'frame', split_axis=0, concat_axis=0, tiled=True)  6.02 us
    unnamed x20, local copies, waits for them, and re-layouts  4.02 us
  transfers between devices with their start and end apart: 11, of which 7 were waited for; matrix products, arithmetic and copies ran while one was open for 0% of the time, Pallas kernels for 15%

profile of v5, /device:TPU:0, one launch (start us, length us, event | category | flops | bytes accessed | tf_op | source)
XLA Modules:
  0.0 79.0 jit_solution(8684091503896181529)
XLA Ops:
  0.0 0.5 collective-permute-start
  0.5 2.5 %collective-permute-start.1 = (bf16[1,128,1152]{2,1,0:T(8,128)(2,1)}, bf16[1,128,1152]{2,1,0:T(8,128)(2,1)S(1)}, u32[]{:S(2)}, u32[]{:S(2)}) collective-permute-start(bf16[1,128,1152]{2,1,0:T(8,128)(2,1)} %token_ref.1), channel_id=1, source_target_pairs={{0,2},{1,3},{2,0},{3,1},{4,6},{5,7},{6,4},{7,5},{8,10},{9,11},{10,... | collective-permute-start | bytes 884744 | tf_op jit(solution)/shard_map/ppermute | solution.py:146
  3.0 1.6 %copy-done = bf16[864,1152]{1,0:T(8,128)(2,1)S(1)} copy-done((bf16[864,1152]{1,0:T(8,128)(2,1)S(1)}, bf16[864,1152]{1,0:T(8,128)(2,1)}, u32[]{:S(2)}) %copy-start) | copy-done | bytes 1990680
  4.5 1.0 %copy-done.4 = bf16[1,128,1152]{2,1,0:T(8,128)(2,1)S(1)} copy-done((bf16[1,128,1152]{2,1,0:T(8,128)(2,1)S(1)}, bf16[1,128,1152]{2,1,0:T(8,128)(2,1)}, u32[]{:S(2)}) %copy-start.4) | copy-done | bytes 294936
  5.5 0.8 copy-done.6
  6.3 1.1 %shard_map.64.near_ref = f32[864,256]{1,0:T(8,128)S(1)} custom-call(f32[6,1152]{1,0:T(8,128)S(1)} %copy-done.6, bf16[864,1152]{1,0:T(8,128)(2,1)S(1)} %copy-done, bf16[1,128,1152]{2,1,0:T(8,128)(2,1)S(1)} %copy-done.4, bf16[1,128,1152]{2,1,0:T(8,128)(2,1)S(1)} %collective-permute-done.sister_ref), custom_call_target="tpu_custom_call" | custom-call | flops 1 | bytes 1 | tf_op jit(solution)/shard_map/pallas_call | solution.py:133
  7.4 3.5 %collective-permute-done.1.refs_0_ = bf16[1,128,1152]{2,1,0:T(8,128)(2,1)S(1)} collective-permute-done((bf16[1,128,1152]{2,1,0:T(8,128)(2,1)}, bf16[1,128,1152]{2,1,0:T(8,128)(2,1)S(1)}, u32[]{:S(2)}, u32[]{:S(2)}) %collective-permute-start.1) | collective-permute-done | bytes 294944 | tf_op jit(solution)/shard_map/ppermute | solution.py:146
  10.9 1.6 %collective-permute-done.2.refs_1_ = bf16[1,128,1152]{2,1,0:T(8,128)(2,1)S(1)} collective-permute-done((bf16[1,128,1152]{2,1,0:T(8,128)(2,1)S(1)}, bf16[1,128,1152]{2,1,0:T(8,128)(2,1)S(1)}, u32[]{:S(2)}, u32[]{:S(2)}) %collective-permute-start.2) | collective-permute-done | bytes 294944 | tf_op jit(solution)/shard_map/ppermute | solution.py:146
  12.4 0.1 collective-permute-start.6
  12.6 0.4 collective-permute-start.4
  13.0 5.3 %shard_map.65 = (bf16[288,256]{1,0:T(8,128)(2,1)S(1)}, bf16[288,256]{1,0:T(8,128)(2,1)S(1)}) custom-call(f32[6,1152]{1,0:T(8,128)S(1)} %copy-done.6, bf16[864,1152]{1,0:T(8,128)(2,1)S(1)} %copy-done, f32[864,256]{1,0:T(8,128)S(1)} %shard_map.64.near_ref, bf16[1,128,1152]{2,1,0:T(8,128)(2,1)S(1)} %collective-permute-done.1.refs_0_, ...), custom_call_target="tpu_custom_call" | custom-call | flops 1 | bytes 1 | tf_op jit(solution)/shard_map/pallas_call | solution.py:133
  18.2 0.2 collective-permute-start.3
  18.4 1.2 %collective-permute-done.3.refs_1_ = bf16[288,256]{1,0:T(8,128)(2,1)S(1)} collective-permute-done((bf16[288,256]{1,0:T(8,128)(2,1)S(1)}, bf16[288,256]{1,0:T(8,128)(2,1)S(1)}, u32[]{:S(2)}, u32[]{:S(2)}) %collective-permute-start.3) | collective-permute-done | bytes 147488 | tf_op jit(solution)/shard_map/ppermute | solution.py:146
  19.7 0.5 shard_map.67
  20.1 0.0 copy-start.2
  20.1 1.8 %collective-permute-start.5 = (bf16[128,1152]{1,0:T(8,128)(2,1)S(1)}, bf16[128,1152]{1,0:T(8,128)(2,1)S(1)}, u32[]{:S(2)}, u32[]{:S(2)}) collective-permute-start(bf16[128,1152]{1,0:T(8,128)(2,1)S(1)} %shard_map.67), channel_id=1, source_target_pairs={{0,2},{1,3},{2,0},{3,1},{4,6},{5,7},{6,4},{7,5},{8,10},{9,11},{10,... | collective-permute-start | bytes 884744 | tf_op jit(solution)/shard_map/ppermute | solution.py:146
  22.0 0.5 shard_map.66.refs_0_
  22.4 6.9 %collective-permute-done.5.refs_1_ = bf16[128,1152]{1,0:T(8,128)(2,1)S(1)} collective-permute-done((bf16[128,1152]{1,0:T(8,128)(2,1)S(1)}, bf16[128,1152]{1,0:T(8,128)(2,1)S(1)}, u32[]{:S(2)}, u32[]{:S(2)}) %collective-permute-start.5) | collective-permute-done | bytes 294944 | tf_op jit(solution)/shard_map/ppermute | solution.py:146
  29.3 1.1 %shard_map.68 = (bf16[128,1152]{1,0:T(8,128)(2,1)S(1)}, bf16[128,1152]{1,0:T(8,128)(2,1)}) custom-call(f32[6,1152]{1,0:T(8,128)S(1)} %copy-done.7, bf16[1,128,1152]{2,1,0:T(8,128)(2,1)S(1)} %copy-done.5, f32[128,1152]{1,0:T(8,128)S(1)} %shard_map.66.refs_0_, bf16[128,1152]{1,0:T(8,128)(2,1)S(1)} %collective-permute-done.5.refs_1_), custom_call_target="tpu_custom_call" | custom-call | flops 1 | bytes 1 | tf_op jit(solution)/shard_map/pallas_call | solution.py:133
  30.4 0.7 copy-done.8
  31.1 6.0 %all-to-all-start = ((bf16[8,16,1152]{2,1,0:T(8,128)(2,1)}), bf16[8,16,1152]{2,1,0:T(8,128)(2,1)}, u32[]{:S(2)}, u32[]{:S(2)}) async-start(bf16[8,16,1152]{2,1,0:T(8,128)(2,1)} %bitcast), calls=%async_computation | async-start | bytes 589824 | tf_op jit(solution)/shard_map/all_to_all | solution.py:172
  37.1 0.1 collective-permute-start.7
  37.2 9.1 %all-to-all-done = bf16[8,16,1152]{2,1,0:T(8,128)(2,1)} async-done(((bf16[8,16,1152]{2,1,0:T(8,128)(2,1)}), bf16[8,16,1152]{2,1,0:T(8,128)(2,1)}, u32[]{:S(2)}, u32[]{:S(2)}) %all-to-all-start) | async-done | bytes 294944 | tf_op jit(solution)/shard_map/all_to_all | solution.py:172
  46.2 1.5 %collective-permute-start.8 = (bf16[128,1152]{1,0:T(8,128)(2,1)}, bf16[128,1152]{1,0:T(8,128)(2,1)S(1)}, u32[]{:S(2)}, u32[]{:S(2)}) collective-permute-start(bf16[128,1152]{1,0:T(8,128)(2,1)} %bitcast.1.refs_4_), channel_id=1, source_target_pairs={{0,2},{1,3},{2,0},{3,1},{4,6},{5,7},{6,4},{7,5},{8,10},{9,11},{10,... | collective-permute-start | bytes 884744 | tf_op jit(solution)/shard_map/ppermute | solution.py:146
  47.8 5.4 %collective-permute-done.8.refs_4_ = bf16[128,1152]{1,0:T(8,128)(2,1)S(1)} collective-permute-done((bf16[128,1152]{1,0:T(8,128)(2,1)}, bf16[128,1152]{1,0:T(8,128)(2,1)S(1)}, u32[]{:S(2)}, u32[]{:S(2)}) %collective-permute-start.8) | collective-permute-done | bytes 294944 | tf_op jit(solution)/shard_map/ppermute | solution.py:146
  53.2 3.8 %shard_map.70 = bf16[128,1152]{1,0:T(8,128)(2,1)S(1)} custom-call(bf16[864,1152]{1,0:T(8,128)(2,1)S(1)} %copy-done.1, bf16[864,1152]{1,0:T(8,128)(2,1)} %collective-permute-done.6.refs_1_, bf16[288,1152]{1,0:T(8,128)(2,1)S(1)} %copy-done.2, bf16[288,1152]{1,0:T(8,128)(2,1)S(1)} %collective-permute-done.7.refs_3_, ...), custom_call_target="tpu_custom_call" | custom-call | flops 1 | bytes 1 | tf_op jit(solution)/shard_map/pallas_call | solution.py:133
  57.0 1.6 %collective-permute-start.9 = (bf16[128,1152]{1,0:T(8,128)(2,1)S(1)}, bf16[128,1152]{1,0:T(8,128)(2,1)S(1)}, u32[]{:S(2)}, u32[]{:S(2)}) collective-permute-start(bf16[128,1152]{1,0:T(8,128)(2,1)S(1)} %shard_map.70), channel_id=1, source_target_pairs={{0,2},{1,3},{2,0},{3,1},{4,6},{5,7},{6,4},{7,5},{8,10},{9,11},{10,... | collective-permute-start | bytes 884744 | tf_op jit(solution)/shard_map/ppermute | solution.py:146
  58.6 3.9 %shard_map.69.refs_0_ = f32[128,1152]{1,0:T(8,128)S(1)} custom-call(bf16[864,1152]{1,0:T(8,128)(2,1)S(1)} %copy-done.1, bf16[864,1152]{1,0:T(8,128)(2,1)} %collective-permute-done.6.refs_1_, bf16[288,1152]{1,0:T(8,128)(2,1)S(1)} %copy-done.2, bf16[288,1152]{1,0:T(8,128)(2,1)S(1)} %collective-permute-done.7.refs_3_, bf16[128,1152]{1,0:T(8,128)(2,1)} %bitcast.1.refs_4_), custom_call_target="tpu_custom_call" | custom-call | flops 1 | bytes 1 | tf_op jit(solution)/shard_map/pallas_call | solution.py:133
  62.5 1.3 %collective-permute-done.9.refs_1_ = bf16[128,1152]{1,0:T(8,128)(2,1)S(1)} collective-permute-done((bf16[128,1152]{1,0:T(8,128)(2,1)S(1)}, bf16[128,1152]{1,0:T(8,128)(2,1)S(1)}, u32[]{:S(2)}, u32[]{:S(2)}) %collective-permute-start.9) | collective-permute-done | bytes 294944 | tf_op jit(solution)/shard_map/ppermute | solution.py:146
  63.8 0.1 shard_map.71
  63.9 14.3 %all_to_all.10 = bf16[8,16,1152]{2,1,0:T(8,128)(2,1)S(1)} all-to-all(bf16[8,16,1152]{2,1,0:T(8,128)(2,1)S(1)} %bitcast.5), channel_id=1, replica_groups=mesh['frame'=8,'patch'=4] {'frame'}, dimensions={0} | all-to-all | bytes 589824 | tf_op jit(solution)/shard_map/all_to_all | solution.py:172
  78.2 0.8 %shard_map.72 = bf16[1,128,1152]{2,1,0:T(8,128)(2,1)} custom-call(f32[6,1152]{1,0:T(8,128)S(1)} %copy-done.7, bf16[128,1152]{1,0:T(8,128)(2,1)S(1)} %copy-done.9, bf16[128,1152]{1,0:T(8,128)(2,1)S(1)} %bitcast.4), custom_call_target="tpu_custom_call" | custom-call | flops 1 | bytes 1 | tf_op jit(solution)/shard_map/pallas_call | solution.py:133
  (20 shorter events, 0.0 us)
Async XLA Ops:
  0.0 3.0 %collective-permute-start = (bf16[1,128,1152]{2,1,0:T(8,128)(2,1)}, bf16[1,128,1152]{2,1,0:T(8,128)(2,1)S(1)}, u32[]{:S(2)}, u32[]{:S(2)}) collective-permute-start(bf16[1,128,1152]{2,1,0:T(8,128)(2,1)} %token_ref.1), channel_id=1, source_target_pairs={{0,1},{1,0},{2,3},{3,2},{4,5},{5,4},{6,7},{7,6},{8,9},{9,8},{10,11... | collective-permute-start | bytes 884744 | tf_op jit(solution)/shard_map/ppermute | solution.py:146
  0.5 10.4 %collective-permute-start.1 = (bf16[1,128,1152]{2,1,0:T(8,128)(2,1)}, bf16[1,128,1152]{2,1,0:T(8,128)(2,1)S(1)}, u32[]{:S(2)}, u32[]{:S(2)}) collective-permute-start(bf16[1,128,1152]{2,1,0:T(8,128)(2,1)} %token_ref.1), channel_id=1, source_target_pairs={{0,2},{1,3},{2,0},{3,1},{4,6},{5,7},{6,4},{7,5},{8,10},{9,11},{10,... | collective-permute-start | bytes 884744 | tf_op jit(solution)/shard_map/ppermute | solution.py:146
  3.0 1.6 %copy-start = (bf16[864,1152]{1,0:T(8,128)(2,1)S(1)}, bf16[864,1152]{1,0:T(8,128)(2,1)}, u32[]{:S(2)}) copy-start(bf16[864,1152]{1,0:T(8,128)(2,1)} %weight_ref.3) | copy-start | bytes 5971972
  4.5 1.0 %copy-start.4 = (bf16[1,128,1152]{2,1,0:T(8,128)(2,1)S(1)}, bf16[1,128,1152]{2,1,0:T(8,128)(2,1)}, u32[]{:S(2)}) copy-start(bf16[1,128,1152]{2,1,0:T(8,128)(2,1)} %token_ref.1) | copy-start | bytes 884740
  5.5 0.8 copy-start.6
  6.3 6.2 %copy-start.1 = (bf16[864,1152]{1,0:T(8,128)(2,1)S(1)}, bf16[864,1152]{1,0:T(8,128)(2,1)}, u32[]{:S(2)}) copy-start(bf16[864,1152]{1,0:T(8,128)(2,1)} %refs_0_.3) | copy-start | bytes 5971972
  6.3 6.3 %copy-start.3 = (bf16[288,1152]{1,0:T(8,128)(2,1)S(1)}, bf16[288,1152]{1,0:T(8,128)(2,1)}, u32[]{:S(2)}) copy-start(bf16[288,1152]{1,0:T(8,128)(2,1)} %refs_2_.5) | copy-start | bytes 1990660
  10.9 1.6 %collective-permute-start.2 = (bf16[1,128,1152]{2,1,0:T(8,128)(2,1)S(1)}, bf16[1,128,1152]{2,1,0:T(8,128)(2,1)S(1)}, u32[]{:S(2)}, u32[]{:S(2)}) collective-permute-start(bf16[1,128,1152]{2,1,0:T(8,128)(2,1)S(1)} %collective-permute-done.1.refs_0_), channel_id=1, source_target_pairs={{0,1},{1,0},{2,3},{3,2},{4,5},{5,4},{6,7},{7,6},{8,9},{9,8},{10,11... | collective-permute-start | bytes 884744 | tf_op jit(solution)/shard_map/ppermute | solution.py:146
  12.4 40.7 %collective-permute-start.6 = (bf16[864,1152]{1,0:T(8,128)(2,1)S(1)}, bf16[864,1152]{1,0:T(8,128)(2,1)}, u32[]{:S(2)}, u32[]{:S(2)}) collective-permute-start(bf16[864,1152]{1,0:T(8,128)(2,1)S(1)} %copy-done.1), channel_id=1, source_target_pairs={{0,1},{1,0},{2,3},{3,2},{4,5},{5,4},{6,7},{7,6},{8,9},{9,8},{10,11... | collective-permute-start | bytes 5971976 | tf_op jit(solution)/shard_map/ppermute | solution.py:146
  12.6 7.1 %collective-permute-start.4 = (bf16[288,1152]{1,0:T(8,128)(2,1)S(1)}, bf16[288,1152]{1,0:T(8,128)(2,1)S(1)}, u32[]{:S(2)}, u32[]{:S(2)}) collective-permute-start(bf16[288,1152]{1,0:T(8,128)(2,1)S(1)} %copy-done.3), channel_id=1, source_target_pairs={{0,1},{1,0},{2,3},{3,2},{4,5},{5,4},{6,7},{7,6},{8,9},{9,8},{10,11... | collective-permute-start | bytes 1990664 | tf_op jit(solution)/shard_map/ppermute | solution.py:146
  18.2 1.4 %collective-permute-start.3 = (bf16[288,256]{1,0:T(8,128)(2,1)S(1)}, bf16[288,256]{1,0:T(8,128)(2,1)S(1)}, u32[]{:S(2)}, u32[]{:S(2)}) collective-permute-start(bf16[288,256]{1,0:T(8,128)(2,1)S(1)} %get-tuple-element.15), channel_id=1, source_target_pairs={{0,1},{1,0},{2,3},{3,2},{4,5},{5,4},{6,7},{7,6},{8,9},{9,8},{10,11... | collective-permute-start | bytes 442376 | tf_op jit(solution)/shard_map/ppermute | solution.py:146
  19.7 9.6 %copy-start.5 = (bf16[1,128,1152]{2,1,0:T(8,128)(2,1)S(1)}, bf16[1,128,1152]{2,1,0:T(8,128)(2,1)}, u32[]{:S(2)}) copy-start(bf16[1,128,1152]{2,1,0:T(8,128)(2,1)} %token_ref.1) | copy-start | bytes 884740
  19.7 9.6 %copy-start.7 = (f32[6,1152]{1,0:T(8,128)S(1)}, f32[6,1152]{1,0:T(8,128)}, u32[]{:S(2)}) copy-start(f32[6,1152]{1,0:T(8,128)} %mod_ref.7) | copy-start | bytes 82948
  20.1 17.0 %copy-start.2 = (bf16[288,1152]{1,0:T(8,128)(2,1)S(1)}, bf16[288,1152]{1,0:T(8,128)(2,1)}, u32[]{:S(2)}) copy-start(bf16[288,1152]{1,0:T(8,128)(2,1)} %refs_2_.7) | copy-start | bytes 1990660
  20.1 9.1 %collective-permute-start.5 = (bf16[128,1152]{1,0:T(8,128)(2,1)S(1)}, bf16[128,1152]{1,0:T(8,128)(2,1)S(1)}, u32[]{:S(2)}, u32[]{:S(2)}) collective-permute-start(bf16[128,1152]{1,0:T(8,128)(2,1)S(1)} %shard_map.67), channel_id=1, source_target_pairs={{0,2},{1,3},{2,0},{3,1},{4,6},{5,7},{6,4},{7,5},{8,10},{9,11},{10,... | collective-permute-start | bytes 884744 | tf_op jit(solution)/shard_map/ppermute | solution.py:146
  30.4 0.7 copy-start.8
  31.1 15.2 %all-to-all-start = ((bf16[8,16,1152]{2,1,0:T(8,128)(2,1)}), bf16[8,16,1152]{2,1,0:T(8,128)(2,1)}, u32[]{:S(2)}, u32[]{:S(2)}) async-start(bf16[8,16,1152]{2,1,0:T(8,128)(2,1)} %bitcast), calls=%async_computation | async-start | bytes 589824 | tf_op jit(solution)/shard_map/all_to_all | solution.py:172
  37.1 10.7 %collective-permute-start.7 = (bf16[288,1152]{1,0:T(8,128)(2,1)S(1)}, bf16[288,1152]{1,0:T(8,128)(2,1)S(1)}, u32[]{:S(2)}, u32[]{:S(2)}) collective-permute-start(bf16[288,1152]{1,0:T(8,128)(2,1)S(1)} %copy-done.2), channel_id=1, source_target_pairs={{0,1},{1,0},{2,3},{3,2},{4,5},{5,4},{6,7},{7,6},{8,9},{9,8},{10,11... | collective-permute-start | bytes 1990664 | tf_op jit(solution)/shard_map/ppermute | solution.py:146
  46.2 6.9 %collective-permute-start.8 = (bf16[128,1152]{1,0:T(8,128)(2,1)}, bf16[128,1152]{1,0:T(8,128)(2,1)S(1)}, u32[]{:S(2)}, u32[]{:S(2)}) collective-permute-start(bf16[128,1152]{1,0:T(8,128)(2,1)} %bitcast.1.refs_4_), channel_id=1, source_target_pairs={{0,2},{1,3},{2,0},{3,1},{4,6},{5,7},{6,4},{7,5},{8,10},{9,11},{10,... | collective-permute-start | bytes 884744 | tf_op jit(solution)/shard_map/ppermute | solution.py:146
  57.0 21.1 %copy-start.9 = (bf16[128,1152]{1,0:T(8,128)(2,1)S(1)}, bf16[128,1152]{1,0:T(8,128)(2,1)}, u32[]{:S(2)}) copy-start(bf16[128,1152]{1,0:T(8,128)(2,1)} %copy-done.8) | copy-start | bytes 884740
  57.0 6.8 %collective-permute-start.9 = (bf16[128,1152]{1,0:T(8,128)(2,1)S(1)}, bf16[128,1152]{1,0:T(8,128)(2,1)S(1)}, u32[]{:S(2)}, u32[]{:S(2)}) collective-permute-start(bf16[128,1152]{1,0:T(8,128)(2,1)S(1)} %shard_map.70), channel_id=1, source_target_pairs={{0,2},{1,3},{2,0},{3,1},{4,6},{5,7},{6,4},{7,5},{8,10},{9,11},{10,... | collective-permute-start | bytes 884744 | tf_op jit(solution)/shard_map/ppermute | solution.py:146

commit v6 on v5

--- a/solution.py
+++ b/solution.py
@@ -74,22 +74,56 @@
         out_ref[:, cols] = heads_ref[:, at * block : (at + 1) * block].astype(BF16)
 
 
-def partial_kernel(first, *refs):
+def halves(value, size):
+    return [
+        jnp.concatenate(
+            [value[at : at + size] for at in range(first * size, value.shape[0], 2 * size)], axis=0
+        )
+        for first in range(2)
+    ]
+
+
+def of_this_half(value, size):
+    even, odd = halves(value, size)
+    first = lax.axis_index("frame") % 2 == 0
+    return jnp.where(first, even, odd), jnp.where(first, odd, even)
+
+
+def partial_kernel(first, period, *refs):
     head_refs, weight_refs, out_refs = refs[:2], refs[2:4], refs[4:]
     weights = jnp.concatenate([ref[...] for ref in weight_refs], axis=0)
-    block = out_refs[0].shape[0]
-    for at, ref in enumerate(out_refs, first):
-        cols = slice(at * block, (at + 1) * block)
-        heads = jnp.concatenate([heads[:, cols] for heads in head_refs], axis=0)
-        ref[...] = dot(heads.T, weights).astype(ref.dtype)
-
-
-def middle_kernel(mod_ref, token_ref, *refs):
-    middle_ref, normed_ref = refs[-2:]
-    update = sum(ref[...].astype(F32) for ref in refs[:-2])
-    middle = (token_ref[0].astype(F32) + mod_ref[2:3, :] * update).astype(BF16)
-    middle_ref[...] = middle
-    normed_ref[...] = norm_rows(middle.astype(F32), mod_ref[3:4, :], mod_ref[4:5, :])
+    block = 2 * out_refs[0].shape[0]
+    for at in range(len(out_refs) // 2):
+        cols = slice((first + at) * block, (first + at + 1) * block)
+        heads = jnp.concatenate([ref[:, cols] for ref in head_refs], axis=0)
+        for ref, part in zip(
+            out_refs[2 * at : 2 * at + 2], of_this_half(dot(heads.T, weights), period)
+        ):
+            ref[...] = part.astype(ref.dtype)
+
+
+def middle_kernel(pieces, groups, mod_ref, own_ref, paired_ref, *refs):
+    update_refs = (refs[:groups], refs[groups : 2 * groups])
+    kept_ref, sent_ref, *piece_refs, scratch = refs[2 * groups :]
+    _, period, width = kept_ref.shape
+    for at, (token_ref, middle_ref) in enumerate(((own_ref, kept_ref), (paired_ref, sent_ref))):
+        update = sum(ref[...].astype(F32) for ref in update_refs[at])
+        tokens = of_this_half(token_ref[0].astype(F32), period)[0]
+        middle = (tokens + mod_ref[2:3, :] * update).astype(BF16)
+        normed = norm_rows(middle.astype(F32), mod_ref[3:4, :], mod_ref[4:5, :])
+        for piece in range(pieces):
+            rows = slice(piece * period, (piece + 1) * period)
+            middle_ref[piece] = middle[rows]
+            scratch[piece, at * period : (at + 1) * period, :] = normed[rows]
+    here = lax.axis_index("frame") // 2
+    for at, ref in enumerate(piece_refs):
+        ref[...] = scratch[here ^ at]
+
+
+def join_kernel(*refs):
+    size = refs[0].shape[0]
+    for at, ref in enumerate(refs[:-1]):
+        refs[-1][at * size : (at + 1) * size, :] = ref[...]
 
 
 def temporal_kernel(groups, period, *refs):
@@ -115,18 +149,35 @@
             probs = softmax_over_rows(dot(keys.T, query), mask)
             heads_ref[head * HD : (head + 1) * HD, cols] = dot(values, probs)
     weights = jnp.concatenate([ref[...] for ref in output_refs], axis=0)
-    for group, ref in enumerate(update_refs):
+    for group in range(groups):
         mixed = heads_ref[:, group * block : (group + 1) * block].astype(BF16)
-        ref[...] = dot(mixed.T, weights).astype(ref.dtype)
-
-
-def sum_kernel(*refs):
-    refs[-1][...] = sum(ref[...].astype(F32) for ref in refs[:-1]).astype(BF16)
-
-
-def result_kernel(mod_ref, middle_ref, update_ref, out_ref):
-    update = update_ref[...].astype(F32)
-    out_ref[0] = (middle_ref[...].astype(F32) + mod_ref[5:6, :] * update).astype(BF16)
+        parts = halves(dot(mixed.T, weights), period)
+        for ref, part in zip(update_refs[2 * group : 2 * group + 2], parts):
+            ref[...] = part.astype(ref.dtype)
+
+
+def sum_kernel(pieces, groups, *refs):
+    update_refs, piece_refs = (refs[:groups], refs[groups : 2 * groups]), refs[2 * groups :]
+    period = piece_refs[0].shape[0] // 2
+    for at, parts in enumerate(update_refs):
+        update = sum(ref[...].astype(F32) for ref in parts).astype(BF16)
+        for piece, ref in enumerate(piece_refs):
+            rows = update[piece * period : (piece + 1) * period]
+            ref[at * period : (at + 1) * period, :] = rows
+
+
+def result_kernel(pieces, mod_ref, kept_ref, other_ref, *refs):
+    piece_refs, out_ref = refs[:-1], refs[-1]
+    period = kept_ref.shape[1]
+    here = lax.axis_index("frame")
+    for at, ref in enumerate(piece_refs):
+        there = here // 2 ^ at
+        for half, middle_ref in enumerate((kept_ref, other_ref)):
+            update = ref[half * period : (half + 1) * period, :].astype(F32)
+            middle = middle_ref[there].astype(F32)
+            out_ref[2 * there + (here % 2 ^ half)] = (middle + mod_ref[5:6, :] * update).astype(
+                BF16
+            )
 
 
 def call(body, operands, outs, scratch=(), limit=24):
@@ -159,27 +210,45 @@
     return [part for block in blocks for part in (block, swap(block, "patch", 1))]
 
 
+def swap_diagonal(value, offset):
+    frames, size = lax.axis_size("frame"), lax.axis_size("patch")
+    pairs = [
+        (frame * size + at, (frame ^ 1) * size + (at ^ offset))
+        for frame in range(frames)
+        for at in range(size)
+    ]
+    return lax.ppermute(value, ("frame", "patch"), pairs)
+
+
 def per_device(tokens, modulation, spatial_qkv, spatial_out, temporal_qkv, temporal_out):
     _, rows, width = tokens.shape
     shard = spatial_out.shape[0]
     count, frames = lax.axis_size("patch"), lax.axis_size("frame")
     period = rows // frames
-    groups = count // 2
+    pieces, groups = frames // 2, count // 2
     shape = jax.ShapeDtypeStruct
-
-    def exchange_frames(value):
-        blocks = value.reshape(frames, period, width)
-        blocks = lax.all_to_all(blocks, "frame", split_axis=0, concat_axis=0, tiled=True)
-        return blocks.reshape(rows, width)
 
     def with_sister(weights, *others):
         return [weights, swap(after(weights, *others), "patch", 1)]
 
-    def return_far(parts):
-        return [swap(part, "patch", 2 * at) for at, part in enumerate(parts, 1)]
-
-    own_update = [shape((rows, width), F32)]
-    far_updates = [shape((rows, width), BF16)] * (groups - 1)
+    def exchange_frames(parts):
+        parts = list(parts)
+        for at in reversed(range(1, pieces)):
+            parts[at] = swap(parts[at], "frame", 2 * at)
+        return parts
+
+    def return_updates(own, far):
+        kept, sent = own
+        same = [swap(part, "patch", 2 * at) for at, part in enumerate(far[::2], 1)]
+        diagonal = [swap_diagonal(part, 2 * at) for at, part in enumerate(far[1::2], 1)]
+        return [kept, *same, swap(sent, "frame", 1), *diagonal]
+
+    def halves_shape(dtype):
+        return shape((rows // 2, width), dtype)
+
+    own_shapes = [halves_shape(F32), halves_shape(BF16)]
+    far_shapes = [halves_shape(BF16)] * (2 * groups - 2)
+    piece_shapes = [shape((2 * period, width), BF16)] * pieces
 
     sister = swap(tokens, "patch", 1)
     far = across(tokens)[1:]
@@ -188,10 +257,10 @@
         (modulation, spatial_qkv, tokens, sister),
         [shape((3 * shard, 2 * rows), F32)],
     )
-    far = both_cores([after(block, near) for block in far])
+    paired = swap(after(tokens, sister), "frame", 1)
+    far = both_cores([after(block, near, paired) for block in far])
     out_pair = with_sister(spatial_out, *far)
     temporal_pair = with_sister(temporal_qkv, *far)
-    late_pair = with_sister(temporal_out, *far)
 
     kept, sent = call(
         functools.partial(spatial_kernel, count),
@@ -199,34 +268,42 @@
         [shape((shard, groups * rows), BF16)] * 2,
         [pltpu.VMEM((3 * shard, (count - 2) * rows), F32), pltpu.VMEM((shard, count * rows), F32)],
     )
-    heads = (kept, swap(sent, "patch", 1))
-    parts = call(functools.partial(partial_kernel, 1), (*heads, *out_pair), far_updates)
-    own = call(functools.partial(partial_kernel, 0), (*heads, *out_pair), own_update)
-    middle, part = call(
-        middle_kernel,
-        (modulation, tokens, *own, *return_far(parts)),
-        [shape((rows, width), BF16)] * 2,
-    )
-
-    def attend(segments, updates):
+    heads = (kept, swap(sent, "patch", 1), *out_pair)
+    far_parts = call(functools.partial(partial_kernel, 1, period), heads, far_shapes)
+    own_parts = call(functools.partial(partial_kernel, 0, period), heads, own_shapes)
+    late_pair = with_sister(temporal_out, far_parts[0])
+    middle, middle_sent, *parts = call(
+        functools.partial(middle_kernel, pieces, groups),
+        (modulation, tokens, paired, *return_updates(own_parts, far_parts)),
+        [shape((pieces, period, width), BF16)] * 2 + piece_shapes,
+        [pltpu.VMEM((pieces, 2 * period, width), BF16)],
+    )
+    (segment,) = call(join_kernel, exchange_frames(parts), [shape((rows, width), BF16)])
+
+    def attend(segments, shapes):
         columns = len(segments) * rows
         return call(
             functools.partial(temporal_kernel, len(segments), period),
             (*temporal_pair, *late_pair, *segments),
-            updates,
+            shapes,
             [pltpu.VMEM((6 * shard, columns), F32), pltpu.VMEM((2 * shard, columns), F32)],
         )
 
-    segments = across(exchange_frames(part))
-    own = attend(segments[:1], own_update)
-    parts = attend(segments[1:], far_updates)
-    (update,) = call(sum_kernel, (*own, *return_far(parts)), [shape((rows, width), BF16)])
+    segments = across(segment)
+    middle_other = swap(after(middle_sent, segment), "frame", 1)
+    own_parts = attend([segment], own_shapes)
+    far_parts = attend([after(block, own_parts[0]) for block in segments[1:]], far_shapes)
+    parts = call(
+        functools.partial(sum_kernel, pieces, groups),
+        return_updates(own_parts, far_parts),
+        piece_shapes,
+    )
     (result,) = call(
-        result_kernel,
-        (modulation, middle, exchange_frames(update)),
-        [shape((1, rows, width), BF16)],
-    )
-    return result
+        functools.partial(result_kernel, pieces),
+        (modulation, middle, middle_other, *exchange_frames(parts)),
+        [shape((frames, period, width), BF16)],
+    )
+    return result.reshape(1, rows, width)
 
 
 def solution(mesh):

time: 79.4 us -> 71.9 us (0.906)
  blocking collectives: 14.3 us -> 0 us
  starting transfers between devices: 14.7 us -> 23.7 us
  Pallas kernels: 16.9 us -> 13.2 us
  waiting for transfers between devices: 29 us -> 31.3 us
    all_to_all x1 -> x0, blocking collectives: 14.3 us -> none  [exchange_frames(): lax.all_to_all(blocks, 'frame', split_axis=0, concat_axis=0, tiled=True)]
    ppermute x10 -> x20, starting transfers between devices: 8.67 us -> 19.8 us  [swap(): return lax.ppermute(value, axis, [(at, at ^ offset) for at in range(size)])]
    all_to_all x1 -> x0, waiting for transfers between devices: 9.07 us -> none  [exchange_frames(): lax.all_to_all(blocks, 'frame', split_axis=0, concat_axis=0, tiled=True)]
    ppermute x10 -> x20, waiting for transfers between devices: 19.9 us -> 27.4 us  [swap(): return lax.ppermute(value, axis, [(at, at ^ offset) for at in range(size)])]
    all_to_all x1 -> x0, starting transfers between devices: 6.02 us -> none  [exchange_frames(): lax.all_to_all(blocks, 'frame', split_axis=0, concat_axis=0, tiled=True)]
    ppermute x0 -> x2, starting transfers between devices: none -> 3.94 us  [swap_diagonal(): return lax.ppermute(value, ('frame', 'patch'), pairs)]
    ppermute x0 -> x2, waiting for transfers between devices: none -> 3.84 us  [swap_diagonal(): return lax.ppermute(value, ('frame', 'patch'), pairs)]
    pallas_call x9 -> x10, Pallas kernels: 16.9 us -> 13.2 us  [call(): pl.pallas_call(body, out_shape=outs, in_specs=[pl.BlockSpec(memory_space=...]
  transfers between devices with their start and end apart: 11 -> 22, of which waited for: 7 -> 15; matrix products, arithmetic and copies ran while one was open for 0% -> 0% of each run, Pallas kernels for 15% -> 14%
where the time goes in v6:
time: 71.9 us; the launch traced here: 71.6 us
  waiting for transfers between devices  31.3 us (44%)
  starting transfers between devices  23.7 us (33%)
  Pallas kernels  13.2 us (18%)
  local copies, waits for them, and re-layouts  3.31 us (5%)
    ppermute x20, waiting for transfers between devices, swap(): return lax.ppermute(value, axis, [(at, at ^ offset) for at in range(size)])  27.4 us
    ppermute x20, starting transfers between devices, swap(): return lax.ppermute(value, axis, [(at, at ^ offset) for at in range(size)])  19.8 us
    pallas_call x10, Pallas kernels, call(): pl.pallas_call(body, out_shape=outs, in_specs=[pl.BlockSpec(memory_space=...  13.2 us
    ppermute x2, starting transfers between devices, swap_diagonal(): return lax.ppermute(value, ('frame', 'patch'), pairs)  3.94 us
    ppermute x2, waiting for transfers between devices, swap_diagonal(): return lax.ppermute(value, ('frame', 'patch'), pairs)  3.84 us
    unnamed x16, local copies, waits for them, and re-layouts  3.31 us
  transfers between devices with their start and end apart: 22, of which 15 were waited for; matrix products, arithmetic and copies ran while one was open for 0% of the time, Pallas kernels for 14%

profile of v6, /device:TPU:0, one launch (start us, length us, event | category | flops | bytes accessed | tf_op | source)
XLA Modules:
  0.0 71.6 jit_solution(15628405565983627813)
XLA Ops:
  0.5 2.5 %collective-permute-start.2 = (bf16[1,128,1152]{2,1,0:T(8,128)(2,1)}, bf16[1,128,1152]{2,1,0:T(8,128)(2,1)S(1)}, u32[]{:S(2)}, u32[]{:S(2)}) collective-permute-start(bf16[1,128,1152]{2,1,0:T(8,128)(2,1)} %own_ref.3), channel_id=1, source_target_pairs={{0,2},{1,3},{2,0},{3,1},{4,6},{5,7},{6,4},{7,5},{8,10},{9,11},{10,... | collective-permute-start | bytes 884744 | tf_op jit(solution)/shard_map/ppermute | solution.py:197
  3.0 1.8 %collective-permute-start.1 = (bf16[1,128,1152]{2,1,0:T(8,128)(2,1)}, bf16[1,128,1152]{2,1,0:T(8,128)(2,1)S(1)}, u32[]{:S(2)}, u32[]{:S(2)}) collective-permute-start(bf16[1,128,1152]{2,1,0:T(8,128)(2,1)} %own_ref.3), channel_id=1, source_target_pairs={{0,4},{4,0},{8,12},{12,8},{16,20},{20,16},{24,28},{28,24},{1,5},{5... | collective-permute-start | bytes 884744 | tf_op jit(solution)/shard_map/ppermute | solution.py:197
  4.7 1.6 %copy-done = bf16[864,1152]{1,0:T(8,128)(2,1)S(1)} copy-done((bf16[864,1152]{1,0:T(8,128)(2,1)S(1)}, bf16[864,1152]{1,0:T(8,128)(2,1)}, u32[]{:S(2)}) %copy-start) | copy-done | bytes 1990680
  6.3 1.0 %copy-done.4 = bf16[1,128,1152]{2,1,0:T(8,128)(2,1)S(1)} copy-done((bf16[1,128,1152]{2,1,0:T(8,128)(2,1)S(1)}, bf16[1,128,1152]{2,1,0:T(8,128)(2,1)}, u32[]{:S(2)}) %copy-start.4) | copy-done | bytes 294936
  7.3 0.8 %copy-done.6 = f32[6,1152]{1,0:T(8,128)S(1)} copy-done((f32[6,1152]{1,0:T(8,128)S(1)}, f32[6,1152]{1,0:T(8,128)}, u32[]{:S(2)}) %copy-start.6) | copy-done | bytes 27672
  8.0 1.1 %shard_map.64.near_ref = f32[864,256]{1,0:T(8,128)S(1)} custom-call(f32[6,1152]{1,0:T(8,128)S(1)} %copy-done.6, bf16[864,1152]{1,0:T(8,128)(2,1)S(1)} %copy-done, bf16[1,128,1152]{2,1,0:T(8,128)(2,1)S(1)} %copy-done.4, bf16[1,128,1152]{2,1,0:T(8,128)(2,1)S(1)} %collective-permute-done.sister_ref), custom_call_target="tpu_custom_call" | custom-call | flops 1 | bytes 1 | tf_op jit(solution)/shard_map/pallas_call | solution.py:184
  9.1 1.7 %collective-permute-done.2.refs_0_ = bf16[1,128,1152]{2,1,0:T(8,128)(2,1)S(1)} collective-permute-done((bf16[1,128,1152]{2,1,0:T(8,128)(2,1)}, bf16[1,128,1152]{2,1,0:T(8,128)(2,1)S(1)}, u32[]{:S(2)}, u32[]{:S(2)}) %collective-permute-start.2) | collective-permute-done | bytes 294944 | tf_op jit(solution)/shard_map/ppermute | solution.py:197
  10.9 1.5 %collective-permute-done.1.paired_ref = bf16[1,128,1152]{2,1,0:T(8,128)(2,1)S(1)} collective-permute-done((bf16[1,128,1152]{2,1,0:T(8,128)(2,1)}, bf16[1,128,1152]{2,1,0:T(8,128)(2,1)S(1)}, u32[]{:S(2)}, u32[]{:S(2)}) %collective-permute-start.1) | collective-permute-done | bytes 294944 | tf_op jit(solution)/shard_map/ppermute | solution.py:197
  12.3 1.6 %collective-permute-done.3.refs_1_ = bf16[1,128,1152]{2,1,0:T(8,128)(2,1)S(1)} collective-permute-done((bf16[1,128,1152]{2,1,0:T(8,128)(2,1)S(1)}, bf16[1,128,1152]{2,1,0:T(8,128)(2,1)S(1)}, u32[]{:S(2)}, u32[]{:S(2)}) %collective-permute-start.3) | collective-permute-done | bytes 294944 | tf_op jit(solution)/shard_map/ppermute | solution.py:197
  14.4 5.3 %shard_map.65 = (bf16[288,256]{1,0:T(8,128)(2,1)S(1)}, bf16[288,256]{1,0:T(8,128)(2,1)S(1)}) custom-call(f32[6,1152]{1,0:T(8,128)S(1)} %copy-done.6, bf16[864,1152]{1,0:T(8,128)(2,1)S(1)} %copy-done, f32[864,256]{1,0:T(8,128)S(1)} %shard_map.64.near_ref, bf16[1,128,1152]{2,1,0:T(8,128)(2,1)S(1)} %collective-permute-done.2.refs_0_, ...), custom_call_target="tpu_custom_call" | custom-call | flops 1 | bytes 1 | tf_op jit(solution)/shard_map/pallas_call | solution.py:184
  19.9 1.2 %collective-permute-done.4.refs_1_ = bf16[288,256]{1,0:T(8,128)(2,1)S(1)} collective-permute-done((bf16[288,256]{1,0:T(8,128)(2,1)S(1)}, bf16[288,256]{1,0:T(8,128)(2,1)S(1)}, u32[]{:S(2)}, u32[]{:S(2)}) %collective-permute-start.4) | collective-permute-done | bytes 147488 | tf_op jit(solution)/shard_map/ppermute | solution.py:197
  22.3 1.7 %collective-permute-start.7 = (bf16[64,1152]{1,0:T(8,128)(2,1)S(1)}, bf16[64,1152]{1,0:T(8,128)(2,1)S(1)}, u32[]{:S(2)}, u32[]{:S(2)}) collective-permute-start(bf16[64,1152]{1,0:T(8,128)(2,1)S(1)} %get-tuple-element.39), channel_id=1, source_target_pairs={{0,4},{4,0},{8,12},{12,8},{16,20},{20,16},{24,28},{28,24},{1,5},{5... | collective-permute-start | bytes 442376 | tf_op jit(solution)/shard_map/ppermute | solution.py:197
  24.1 1.5 %collective-permute-start.8 = (bf16[64,1152]{1,0:T(8,128)(2,1)S(1)}, bf16[64,1152]{1,0:T(8,128)(2,1)S(1)}, u32[]{:S(2)}, u32[]{:S(2)}) collective-permute-start(bf16[64,1152]{1,0:T(8,128)(2,1)S(1)} %get-tuple-element.40), channel_id=1, source_target_pairs={{0,6},{1,7},{2,4},{3,5},{4,2},{5,3},{6,0},{7,1},{8,14},{9,15},{10,... | collective-permute-start | bytes 442376 | tf_op jit(solution)/shard_map/ppermute | solution.py:220
  25.9 3.2 %collective-permute-done.7.refs_2_ = bf16[64,1152]{1,0:T(8,128)(2,1)S(1)} collective-permute-done((bf16[64,1152]{1,0:T(8,128)(2,1)S(1)}, bf16[64,1152]{1,0:T(8,128)(2,1)S(1)}, u32[]{:S(2)}, u32[]{:S(2)}) %collective-permute-start.7) | collective-permute-done | bytes 147488 | tf_op jit(solution)/shard_map/ppermute | solution.py:197
  29.1 3.8 %collective-permute-done.8.refs_3_ = bf16[64,1152]{1,0:T(8,128)(2,1)S(1)} collective-permute-done((bf16[64,1152]{1,0:T(8,128)(2,1)S(1)}, bf16[64,1152]{1,0:T(8,128)(2,1)S(1)}, u32[]{:S(2)}, u32[]{:S(2)}) %collective-permute-start.8) | collective-permute-done | bytes 147488 | tf_op jit(solution)/shard_map/ppermute | solution.py:220
  32.9 1.4 %collective-permute-done.6.refs_1_ = bf16[64,1152]{1,0:T(8,128)(2,1)S(1)} collective-permute-done((bf16[64,1152]{1,0:T(8,128)(2,1)S(1)}, bf16[64,1152]{1,0:T(8,128)(2,1)S(1)}, u32[]{:S(2)}, u32[]{:S(2)}) %collective-permute-start.6) | collective-permute-done | bytes 147488 | tf_op jit(solution)/shard_map/ppermute | solution.py:197
  34.7 1.6 %collective-permute-start.9 = (bf16[32,1152]{1,0:T(8,128)(2,1)S(1)}, bf16[32,1152]{1,0:T(8,128)(2,1)S(1)}, u32[]{:S(2)}, u32[]{:S(2)}) collective-permute-start(bf16[32,1152]{1,0:T(8,128)(2,1)S(1)} %get-tuple-element.44), channel_id=1, source_target_pairs={{0,8},{4,12},{8,0},{12,4},{16,24},{20,28},{24,16},{28,20},{1,9},{5... | collective-permute-start | bytes 221192 | tf_op jit(solution)/shard_map/ppermute | solution.py:197
  36.3 2.6 %collective-permute-start.10 = (bf16[32,1152]{1,0:T(8,128)(2,1)S(1)}, bf16[32,1152]{1,0:T(8,128)(2,1)S(1)}, u32[]{:S(2)}, u32[]{:S(2)}) collective-permute-start(bf16[32,1152]{1,0:T(8,128)(2,1)S(1)} %get-tuple-element.45), channel_id=1, source_target_pairs={{0,16},{4,20},{8,24},{12,28},{16,0},{20,4},{24,8},{28,12},{1,17},{... | collective-permute-start | bytes 221192 | tf_op jit(solution)/shard_map/ppermute | solution.py:197
  39.8 3.4 %collective-permute-done.10.refs_2_ = bf16[32,1152]{1,0:T(8,128)(2,1)S(1)} collective-permute-done((bf16[32,1152]{1,0:T(8,128)(2,1)S(1)}, bf16[32,1152]{1,0:T(8,128)(2,1)S(1)}, u32[]{:S(2)}, u32[]{:S(2)}) %collective-permute-start.10) | collective-permute-done | bytes 73760 | tf_op jit(solution)/shard_map/ppermute | solution.py:197
  43.2 1.9 %collective-permute-done.11.refs_3_ = bf16[32,1152]{1,0:T(8,128)(2,1)S(1)} collective-permute-done((bf16[32,1152]{1,0:T(8,128)(2,1)S(1)}, bf16[32,1152]{1,0:T(8,128)(2,1)S(1)}, u32[]{:S(2)}, u32[]{:S(2)}) %collective-permute-start.11) | collective-permute-done | bytes 73760 | tf_op jit(solution)/shard_map/ppermute | solution.py:197
  45.7 2.3 %shard_map.70 = (f32[64,1152]{1,0:T(8,128)S(1)}, bf16[64,1152]{1,0:T(8,128)(2,1)S(1)}) custom-call(bf16[864,1152]{1,0:T(8,128)(2,1)S(1)} %copy-done.1, bf16[864,1152]{1,0:T(8,128)(2,1)S(1)} %collective-permute-done.13.refs_1_, bf16[288,1152]{1,0:T(8,128)(2,1)S(1)} %copy-done.3, bf16[288,1152]{1,0:T(8,128)(2,1)S(1)} %collective-permute-done.14.refs_3_, ...), custom_call_target="tpu_custom_call" | custom-call | flops 1 | bytes 1 | tf_op jit(solution)/shard_map/pallas_call | solution.py:184
  48.0 3.9 %collective-permute-done.15.refs_4_ = bf16[128,1152]{1,0:T(8,128)(2,1)S(1)} collective-permute-done((bf16[128,1152]{1,0:T(8,128)(2,1)S(1)}, bf16[128,1152]{1,0:T(8,128)(2,1)S(1)}, u32[]{:S(2)}, u32[]{:S(2)}) %collective-permute-start.15) | collective-permute-done | bytes 294944 | tf_op jit(solution)/shard_map/ppermute | solution.py:197
  51.9 2.3 %shard_map.71 = (bf16[64,1152]{1,0:T(8,128)(2,1)S(1)}, bf16[64,1152]{1,0:T(8,128)(2,1)S(1)}) custom-call(bf16[864,1152]{1,0:T(8,128)(2,1)S(1)} %copy-done.1, bf16[864,1152]{1,0:T(8,128)(2,1)S(1)} %collective-permute-done.13.refs_1_, bf16[288,1152]{1,0:T(8,128)(2,1)S(1)} %copy-done.3, bf16[288,1152]{1,0:T(8,128)(2,1)S(1)} %collective-permute-done.14.refs_3_, ...), custom_call_target="tpu_custom_call" | custom-call | flops 1 | bytes 1 | tf_op jit(solution)/shard_map/pallas_call | solution.py:184
  54.8 2.5 %collective-permute-start.18 = (bf16[64,1152]{1,0:T(8,128)(2,1)S(1)}, bf16[64,1152]{1,0:T(8,128)(2,1)S(1)}, u32[]{:S(2)}, u32[]{:S(2)}) collective-permute-start(bf16[64,1152]{1,0:T(8,128)(2,1)S(1)} %get-tuple-element.54), channel_id=1, source_target_pairs={{0,6},{1,7},{2,4},{3,5},{4,2},{5,3},{6,0},{7,1},{8,14},{9,15},{10,... | collective-permute-start | bytes 442376 | tf_op jit(solution)/shard_map/ppermute | solution.py:220
  57.7 1.5 %collective-permute-start.12 = (bf16[4,16,1152]{2,1,0:T(8,128)(2,1)S(1)}, bf16[4,16,1152]{2,1,0:T(8,128)(2,1)S(1)}, u32[]{:S(2)}, u32[]{:S(2)}) collective-permute-start(bf16[4,16,1152]{2,1,0:T(8,128)(2,1)S(1)} %get-tuple-element.47), channel_id=1, source_target_pairs={{0,4},{4,0},{8,12},{12,8},{16,20},{20,16},{24,28},{28,24},{1,5},{5... | collective-permute-start | bytes 442376 | tf_op jit(solution)/shard_map/ppermute | solution.py:197
  59.2 1.7 %collective-permute-done.16.refs_1_ = bf16[64,1152]{1,0:T(8,128)(2,1)S(1)} collective-permute-done((bf16[64,1152]{1,0:T(8,128)(2,1)S(1)}, bf16[64,1152]{1,0:T(8,128)(2,1)S(1)}, u32[]{:S(2)}, u32[]{:S(2)}) %collective-permute-start.16) | collective-permute-done | bytes 147488 | tf_op jit(solution)/shard_map/ppermute | solution.py:197
  61.0 1.5 %collective-permute-done.17.refs_2_ = bf16[64,1152]{1,0:T(8,128)(2,1)S(1)} collective-permute-done((bf16[64,1152]{1,0:T(8,128)(2,1)S(1)}, bf16[64,1152]{1,0:T(8,128)(2,1)S(1)}, u32[]{:S(2)}, u32[]{:S(2)}) %collective-permute-start.17) | collective-permute-done | bytes 147488 | tf_op jit(solution)/shard_map/ppermute | solution.py:197
  62.6 2.0 %collective-permute-start.20 = (bf16[32,1152]{1,0:T(8,128)(2,1)S(1)}, bf16[32,1152]{1,0:T(8,128)(2,1)S(1)}, u32[]{:S(2)}, u32[]{:S(2)}) collective-permute-start(bf16[32,1152]{1,0:T(8,128)(2,1)S(1)} %get-tuple-element.57), channel_id=1, source_target_pairs={{0,16},{4,20},{8,24},{12,28},{16,0},{20,4},{24,8},{28,12},{1,17},{... | collective-permute-start | bytes 221192 | tf_op jit(solution)/shard_map/ppermute | solution.py:197
  64.6 2.4 %collective-permute-start.21 = (bf16[32,1152]{1,0:T(8,128)(2,1)S(1)}, bf16[32,1152]{1,0:T(8,128)(2,1)S(1)}, u32[]{:S(2)}, u32[]{:S(2)}) collective-permute-start(bf16[32,1152]{1,0:T(8,128)(2,1)S(1)} %get-tuple-element.58), channel_id=1, source_target_pairs={{0,24},{4,28},{8,16},{12,20},{16,8},{20,12},{24,0},{28,4},{1,25},{... | collective-permute-start | bytes 221192 | tf_op jit(solution)/shard_map/ppermute | solution.py:197
  67.0 0.9 %collective-permute-done.20.refs_2_ = bf16[32,1152]{1,0:T(8,128)(2,1)S(1)} collective-permute-done((bf16[32,1152]{1,0:T(8,128)(2,1)S(1)}, bf16[32,1152]{1,0:T(8,128)(2,1)S(1)}, u32[]{:S(2)}, u32[]{:S(2)}) %collective-permute-start.20) | collective-permute-done | bytes 73760 | tf_op jit(solution)/shard_map/ppermute | solution.py:197
  67.9 2.9 %collective-permute-done.21.refs_3_ = bf16[32,1152]{1,0:T(8,128)(2,1)S(1)} collective-permute-done((bf16[32,1152]{1,0:T(8,128)(2,1)S(1)}, bf16[32,1152]{1,0:T(8,128)(2,1)S(1)}, u32[]{:S(2)}, u32[]{:S(2)}) %collective-permute-start.21) | collective-permute-done | bytes 73760 | tf_op jit(solution)/shard_map/ppermute | solution.py:197
  70.8 0.8 %shard_map.73 = bf16[8,16,1152]{2,1,0:T(8,128)(2,1)} custom-call(f32[6,1152]{1,0:T(8,128)S(1)} %copy-done.7, bf16[4,16,1152]{2,1,0:T(8,128)(2,1)S(1)} %get-tuple-element.41.kept_ref, bf16[4,16,1152]{2,1,0:T(8,128)(2,1)S(1)} %collective-permute-done.12.other_ref, bf16[32,1152]{1,0:T(8,128)(2,1)S(1)} %get-tuple-element.55.refs_0_, ...), custom_call_target="tpu_custom_call" | custom-call | flops 1 | bytes 1 | tf_op jit(solution)/shard_map/pallas_call | solution.py:184
  (38 shorter events, 5.8 us)
Async XLA Ops:
  0.0 3.0 %collective-permute-start = (bf16[1,128,1152]{2,1,0:T(8,128)(2,1)}, bf16[1,128,1152]{2,1,0:T(8,128)(2,1)S(1)}, u32[]{:S(2)}, u32[]{:S(2)}) collective-permute-start(bf16[1,128,1152]{2,1,0:T(8,128)(2,1)} %own_ref.3), channel_id=1, source_target_pairs={{0,1},{1,0},{2,3},{3,2},{4,5},{5,4},{6,7},{7,6},{8,9},{9,8},{10,11... | collective-permute-start | bytes 884744 | tf_op jit(solution)/shard_map/ppermute | solution.py:197
  0.5 10.4 %collective-permute-start.2 = (bf16[1,128,1152]{2,1,0:T(8,128)(2,1)}, bf16[1,128,1152]{2,1,0:T(8,128)(2,1)S(1)}, u32[]{:S(2)}, u32[]{:S(2)}) collective-permute-start(bf16[1,128,1152]{2,1,0:T(8,128)(2,1)} %own_ref.3), channel_id=1, source_target_pairs={{0,2},{1,3},{2,0},{3,1},{4,6},{5,7},{6,4},{7,5},{8,10},{9,11},{10,... | collective-permute-start | bytes 884744 | tf_op jit(solution)/shard_map/ppermute | solution.py:197
  3.0 9.4 %collective-permute-start.1 = (bf16[1,128,1152]{2,1,0:T(8,128)(2,1)}, bf16[1,128,1152]{2,1,0:T(8,128)(2,1)S(1)}, u32[]{:S(2)}, u32[]{:S(2)}) collective-permute-start(bf16[1,128,1152]{2,1,0:T(8,128)(2,1)} %own_ref.3), channel_id=1, source_target_pairs={{0,4},{4,0},{8,12},{12,8},{16,20},{20,16},{24,28},{28,24},{1,5},{5... | collective-permute-start | bytes 884744 | tf_op jit(solution)/shard_map/ppermute | solution.py:197
  4.7 1.6 %copy-start = (bf16[864,1152]{1,0:T(8,128)(2,1)S(1)}, bf16[864,1152]{1,0:T(8,128)(2,1)}, u32[]{:S(2)}) copy-start(bf16[864,1152]{1,0:T(8,128)(2,1)} %weight_ref.3) | copy-start | bytes 5971972
  6.3 1.0 %copy-start.4 = (bf16[1,128,1152]{2,1,0:T(8,128)(2,1)S(1)}, bf16[1,128,1152]{2,1,0:T(8,128)(2,1)}, u32[]{:S(2)}) copy-start(bf16[1,128,1152]{2,1,0:T(8,128)(2,1)} %own_ref.3) | copy-start | bytes 884740
  7.2 0.8 %copy-start.6 = (f32[6,1152]{1,0:T(8,128)S(1)}, f32[6,1152]{1,0:T(8,128)}, u32[]{:S(2)}) copy-start(f32[6,1152]{1,0:T(8,128)} %mod_ref.7) | copy-start | bytes 82948
  8.0 5.9 %copy-start.1 = (bf16[864,1152]{1,0:T(8,128)(2,1)S(1)}, bf16[864,1152]{1,0:T(8,128)(2,1)}, u32[]{:S(2)}) copy-start(bf16[864,1152]{1,0:T(8,128)(2,1)} %refs_0_.3) | copy-start | bytes 5971972
  8.0 6.0 %copy-start.2 = (bf16[288,1152]{1,0:T(8,128)(2,1)S(1)}, bf16[288,1152]{1,0:T(8,128)(2,1)}, u32[]{:S(2)}) copy-start(bf16[288,1152]{1,0:T(8,128)(2,1)} %refs_2_.5) | copy-start | bytes 1990660
  9.1 12.5 %copy-start.3 = (bf16[288,1152]{1,0:T(8,128)(2,1)S(1)}, bf16[288,1152]{1,0:T(8,128)(2,1)}, u32[]{:S(2)}) copy-start(bf16[288,1152]{1,0:T(8,128)(2,1)} %refs_2_.7) | copy-start | bytes 1990660
  12.3 1.6 %collective-permute-start.3 = (bf16[1,128,1152]{2,1,0:T(8,128)(2,1)S(1)}, bf16[1,128,1152]{2,1,0:T(8,128)(2,1)S(1)}, u32[]{:S(2)}, u32[]{:S(2)}) collective-permute-start(bf16[1,128,1152]{2,1,0:T(8,128)(2,1)S(1)} %collective-permute-done.2.refs_0_), channel_id=1, source_target_pairs={{0,1},{1,0},{2,3},{3,2},{4,5},{5,4},{6,7},{7,6},{8,9},{9,8},{10,11... | collective-permute-start | bytes 884744 | tf_op jit(solution)/shard_map/ppermute | solution.py:197
  13.9 31.8 %collective-permute-start.13 = (bf16[864,1152]{1,0:T(8,128)(2,1)S(1)}, bf16[864,1152]{1,0:T(8,128)(2,1)S(1)}, u32[]{:S(2)}, u32[]{:S(2)}) collective-permute-start(bf16[864,1152]{1,0:T(8,128)(2,1)S(1)} %copy-done.1), channel_id=1, source_target_pairs={{0,1},{1,0},{2,3},{3,2},{4,5},{5,4},{6,7},{7,6},{8,9},{9,8},{10,11... | collective-permute-start | bytes 5971976 | tf_op jit(solution)/shard_map/ppermute | solution.py:197
  14.1 7.1 %collective-permute-start.5 = (bf16[288,1152]{1,0:T(8,128)(2,1)S(1)}, bf16[288,1152]{1,0:T(8,128)(2,1)S(1)}, u32[]{:S(2)}, u32[]{:S(2)}) collective-permute-start(bf16[288,1152]{1,0:T(8,128)(2,1)S(1)} %copy-done.2), channel_id=1, source_target_pairs={{0,1},{1,0},{2,3},{3,2},{4,5},{5,4},{6,7},{7,6},{8,9},{9,8},{10,11... | collective-permute-start | bytes 1990664 | tf_op jit(solution)/shard_map/ppermute | solution.py:197
  19.7 14.6 %copy-start.5 = (bf16[1,128,1152]{2,1,0:T(8,128)(2,1)S(1)}, bf16[1,128,1152]{2,1,0:T(8,128)(2,1)}, u32[]{:S(2)}) copy-start(bf16[1,128,1152]{2,1,0:T(8,128)(2,1)} %own_ref.3) | copy-start | bytes 884740
  19.7 14.5 %copy-start.7 = (f32[6,1152]{1,0:T(8,128)S(1)}, f32[6,1152]{1,0:T(8,128)}, u32[]{:S(2)}) copy-start(f32[6,1152]{1,0:T(8,128)} %mod_ref.7) | copy-start | bytes 82948
  19.7 1.4 %collective-permute-start.4 = (bf16[288,256]{1,0:T(8,128)(2,1)S(1)}, bf16[288,256]{1,0:T(8,128)(2,1)S(1)}, u32[]{:S(2)}, u32[]{:S(2)}) collective-permute-start(bf16[288,256]{1,0:T(8,128)(2,1)S(1)} %get-tuple-element.35), channel_id=1, source_target_pairs={{0,1},{1,0},{2,3},{3,2},{4,5},{5,4},{6,7},{7,6},{8,9},{9,8},{10,11... | collective-permute-start | bytes 442376 | tf_op jit(solution)/shard_map/ppermute | solution.py:197
  21.6 24.0 %collective-permute-start.14 = (bf16[288,1152]{1,0:T(8,128)(2,1)S(1)}, bf16[288,1152]{1,0:T(8,128)(2,1)S(1)}, u32[]{:S(2)}, u32[]{:S(2)}) collective-permute-start(bf16[288,1152]{1,0:T(8,128)(2,1)S(1)} %copy-done.3), channel_id=1, source_target_pairs={{0,1},{1,0},{2,3},{3,2},{4,5},{5,4},{6,7},{7,6},{8,9},{9,8},{10,11... | collective-permute-start | bytes 1990664 | tf_op jit(solution)/shard_map/ppermute | solution.py:197
  22.3 6.7 %collective-permute-start.7 = (bf16[64,1152]{1,0:T(8,128)(2,1)S(1)}, bf16[64,1152]{1,0:T(8,128)(2,1)S(1)}, u32[]{:S(2)}, u32[]{:S(2)}) collective-permute-start(bf16[64,1152]{1,0:T(8,128)(2,1)S(1)} %get-tuple-element.39), channel_id=1, source_target_pairs={{0,4},{4,0},{8,12},{12,8},{16,20},{20,16},{24,28},{28,24},{1,5},{5... | collective-permute-start | bytes 442376 | tf_op jit(solution)/shard_map/ppermute | solution.py:197
  24.1 8.8 %collective-permute-start.8 = (bf16[64,1152]{1,0:T(8,128)(2,1)S(1)}, bf16[64,1152]{1,0:T(8,128)(2,1)S(1)}, u32[]{:S(2)}, u32[]{:S(2)}) collective-permute-start(bf16[64,1152]{1,0:T(8,128)(2,1)S(1)} %get-tuple-element.40), channel_id=1, source_target_pairs={{0,6},{1,7},{2,4},{3,5},{4,2},{5,3},{6,0},{7,1},{8,14},{9,15},{10,... | collective-permute-start | bytes 442376 | tf_op jit(solution)/shard_map/ppermute | solution.py:220
  25.5 8.7 %collective-permute-start.6 = (bf16[64,1152]{1,0:T(8,128)(2,1)S(1)}, bf16[64,1152]{1,0:T(8,128)(2,1)S(1)}, u32[]{:S(2)}, u32[]{:S(2)}) collective-permute-start(bf16[64,1152]{1,0:T(8,128)(2,1)S(1)} %get-tuple-element.38), channel_id=1, source_target_pairs={{0,2},{1,3},{2,0},{3,1},{4,6},{5,7},{6,4},{7,5},{8,10},{9,11},{10,... | collective-permute-start | bytes 442376 | tf_op jit(solution)/shard_map/ppermute | solution.py:197
  34.7 5.1 %collective-permute-start.9 = (bf16[32,1152]{1,0:T(8,128)(2,1)S(1)}, bf16[32,1152]{1,0:T(8,128)(2,1)S(1)}, u32[]{:S(2)}, u32[]{:S(2)}) collective-permute-start(bf16[32,1152]{1,0:T(8,128)(2,1)S(1)} %get-tuple-element.44), channel_id=1, source_target_pairs={{0,8},{4,12},{8,0},{12,4},{16,24},{20,28},{24,16},{28,20},{1,9},{5... | collective-permute-start | bytes 221192 | tf_op jit(solution)/shard_map/ppermute | solution.py:197
  36.3 6.9 %collective-permute-start.10 = (bf16[32,1152]{1,0:T(8,128)(2,1)S(1)}, bf16[32,1152]{1,0:T(8,128)(2,1)S(1)}, u32[]{:S(2)}, u32[]{:S(2)}) collective-permute-start(bf16[32,1152]{1,0:T(8,128)(2,1)S(1)} %get-tuple-element.45), channel_id=1, source_target_pairs={{0,16},{4,20},{8,24},{12,28},{16,0},{20,4},{24,8},{28,12},{1,17},{... | collective-permute-start | bytes 221192 | tf_op jit(solution)/shard_map/ppermute | solution.py:197
  38.9 6.2 %collective-permute-start.11 = (bf16[32,1152]{1,0:T(8,128)(2,1)S(1)}, bf16[32,1152]{1,0:T(8,128)(2,1)S(1)}, u32[]{:S(2)}, u32[]{:S(2)}) collective-permute-start(bf16[32,1152]{1,0:T(8,128)(2,1)S(1)} %get-tuple-element.46), channel_id=1, source_target_pairs={{0,24},{4,28},{8,16},{12,20},{16,8},{20,12},{24,0},{28,4},{1,25},{... | collective-permute-start | bytes 221192 | tf_op jit(solution)/shard_map/ppermute | solution.py:197
  45.1 6.8 %collective-permute-start.15 = (bf16[128,1152]{1,0:T(8,128)(2,1)S(1)}, bf16[128,1152]{1,0:T(8,128)(2,1)S(1)}, u32[]{:S(2)}, u32[]{:S(2)}) collective-permute-start(bf16[128,1152]{1,0:T(8,128)(2,1)S(1)} %shard_map.69.refs_4_), channel_id=1, source_target_pairs={{0,2},{1,3},{2,0},{3,1},{4,6},{5,7},{6,4},{7,5},{8,10},{9,11},{10,... | collective-permute-start | bytes 884744 | tf_op jit(solution)/shard_map/ppermute | solution.py:197
  54.2 6.8 %collective-permute-start.16 = (bf16[64,1152]{1,0:T(8,128)(2,1)S(1)}, bf16[64,1152]{1,0:T(8,128)(2,1)S(1)}, u32[]{:S(2)}, u32[]{:S(2)}) collective-permute-start(bf16[64,1152]{1,0:T(8,128)(2,1)S(1)} %get-tuple-element.52), channel_id=1, source_target_pairs={{0,2},{1,3},{2,0},{3,1},{4,6},{5,7},{6,4},{7,5},{8,10},{9,11},{10,... | collective-permute-start | bytes 442376 | tf_op jit(solution)/shard_map/ppermute | solution.py:197
  54.8 6.2 %collective-permute-start.18 = (bf16[64,1152]{1,0:T(8,128)(2,1)S(1)}, bf16[64,1152]{1,0:T(8,128)(2,1)S(1)}, u32[]{:S(2)}, u32[]{:S(2)}) collective-permute-start(bf16[64,1152]{1,0:T(8,128)(2,1)S(1)} %get-tuple-element.54), channel_id=1, source_target_pairs={{0,6},{1,7},{2,4},{3,5},{4,2},{5,3},{6,0},{7,1},{8,14},{9,15},{10,... | collective-permute-start | bytes 442376 | tf_op jit(solution)/shard_map/ppermute | solution.py:220
  57.2 5.2 %collective-permute-start.17 = (bf16[64,1152]{1,0:T(8,128)(2,1)S(1)}, bf16[64,1152]{1,0:T(8,128)(2,1)S(1)}, u32[]{:S(2)}, u32[]{:S(2)}) collective-permute-start(bf16[64,1152]{1,0:T(8,128)(2,1)S(1)} %get-tuple-element.53), channel_id=1, source_target_pairs={{0,4},{4,0},{8,12},{12,8},{16,20},{20,16},{24,28},{28,24},{1,5},{5... | collective-permute-start | bytes 442376 | tf_op jit(solution)/shard_map/ppermute | solution.py:197
  57.7 9.2 %collective-permute-start.12 = (bf16[4,16,1152]{2,1,0:T(8,128)(2,1)S(1)}, bf16[4,16,1152]{2,1,0:T(8,128)(2,1)S(1)}, u32[]{:S(2)}, u32[]{:S(2)}) collective-permute-start(bf16[4,16,1152]{2,1,0:T(8,128)(2,1)S(1)} %get-tuple-element.47), channel_id=1, source_target_pairs={{0,4},{4,0},{8,12},{12,8},{16,20},{20,16},{24,28},{28,24},{1,5},{5... | collective-permute-start | bytes 442376 | tf_op jit(solution)/shard_map/ppermute | solution.py:197
  62.5 4.5 %collective-permute-start.19 = (bf16[32,1152]{1,0:T(8,128)(2,1)S(1)}, bf16[32,1152]{1,0:T(8,128)(2,1)S(1)}, u32[]{:S(2)}, u32[]{:S(2)}) collective-permute-start(bf16[32,1152]{1,0:T(8,128)(2,1)S(1)} %get-tuple-element.56), channel_id=1, source_target_pairs={{0,8},{4,12},{8,0},{12,4},{16,24},{20,28},{24,16},{28,20},{1,9},{5... | collective-permute-start | bytes 221192 | tf_op jit(solution)/shard_map/ppermute | solution.py:197
  62.6 5.3 %collective-permute-start.20 = (bf16[32,1152]{1,0:T(8,128)(2,1)S(1)}, bf16[32,1152]{1,0:T(8,128)(2,1)S(1)}, u32[]{:S(2)}, u32[]{:S(2)}) collective-permute-start(bf16[32,1152]{1,0:T(8,128)(2,1)S(1)} %get-tuple-element.57), channel_id=1, source_target_pairs={{0,16},{4,20},{8,24},{12,28},{16,0},{20,4},{24,8},{28,12},{1,17},{... | collective-permute-start | bytes 221192 | tf_op jit(solution)/shard_map/ppermute | solution.py:197
  64.6 6.3 %collective-permute-start.21 = (bf16[32,1152]{1,0:T(8,128)(2,1)S(1)}, bf16[32,1152]{1,0:T(8,128)(2,1)S(1)}, u32[]{:S(2)}, u32[]{:S(2)}) collective-permute-start(bf16[32,1152]{1,0:T(8,128)(2,1)S(1)} %get-tuple-element.58), channel_id=1, source_target_pairs={{0,24},{4,28},{8,16},{12,20},{16,8},{20,12},{24,0},{28,4},{1,25},{... | collective-permute-start | bytes 221192 | tf_op jit(solution)/shard_map/ppermute | solution.py:197

commit v7 on v6

--- a/solution.py
+++ b/solution.py
@@ -28,13 +28,15 @@
     )
 
 
-def softmax_over_rows(scores, mask=None):
+def attend(keys, query, values, mask=None):
+    scores = dot(keys, query)
     if mask is not None:
         scores = jnp.where(mask, scores, -1e30)
     top = jnp.max(scores, axis=0, keepdims=True)
-    grown = jnp.exp2((scores - top) * (HD**-0.5 * LOG2E))
-    total = jnp.sum(grown, axis=0, keepdims=True)
-    return (grown * (1.0 / total)).astype(BF16)
+    weights = jnp.exp2((scores - top) * (HD**-0.5 * LOG2E)).astype(BF16)
+    ones = jnp.ones((8, values.shape[1]), F32)
+    mixed = dot(jnp.concatenate([values, ones], axis=0).astype(BF16), weights)
+    return mixed[:HD] * (1.0 / mixed[HD : HD + 1])
 
 
 def project(mod_ref, weight_ref, token_refs, proj_ref):
@@ -57,17 +59,16 @@
     project(mod_ref, weight_ref, token_refs, far_ref)
 
     def whole(start):
-        parts = [ref[start : start + HD, :].astype(BF16) for ref in (near_ref, far_ref)]
-        return jnp.concatenate(parts, axis=1)
+        return jnp.concatenate([ref[start : start + HD, :] for ref in (near_ref, far_ref)], axis=1)
 
     for head in range(heads):
         base = head * 3 * HD
         queries, keys, values = (whole(base + part * HD) for part in range(3))
-        keys = keys.T
+        keys, queries = keys.astype(BF16).T, queries.astype(BF16)
         for at in range(0, count, 2):
             cols = slice(at * block, (at + 2) * block)
-            probs = softmax_over_rows(dot(keys, queries[:, cols]))
-            heads_ref[head * HD : (head + 1) * HD, cols] = dot(values, probs)
+            rows = slice(head * HD, (head + 1) * HD)
+            heads_ref[rows, cols] = attend(keys, queries[:, cols], values)
     for at in range(count):
         out_ref = (kept_ref, sent_ref)[at % 2]
         cols = slice(at // 2 * block, (at // 2 + 1) * block)
@@ -84,17 +85,21 @@
 
 
 def of_this_half(value, size):
-    even, odd = halves(value, size)
+    even, odd = (half.astype(F32) for half in halves(value, size))
     first = lax.axis_index("frame") % 2 == 0
     return jnp.where(first, even, odd), jnp.where(first, odd, even)
 
 
-def partial_kernel(first, period, *refs):
+def share_kernel(period, token_ref, sent_ref):
+    sent_ref[...] = of_this_half(token_ref[0], period)[1].astype(BF16)
+
+
+def partial_kernel(period, *refs):
     head_refs, weight_refs, out_refs = refs[:2], refs[2:4], refs[4:]
     weights = jnp.concatenate([ref[...] for ref in weight_refs], axis=0)
     block = 2 * out_refs[0].shape[0]
     for at in range(len(out_refs) // 2):
-        cols = slice((first + at) * block, (first + at + 1) * block)
+        cols = slice(at * block, (at + 1) * block)
         heads = jnp.concatenate([ref[:, cols] for ref in head_refs], axis=0)
         for ref, part in zip(
             out_refs[2 * at : 2 * at + 2], of_this_half(dot(heads.T, weights), period)
@@ -106,10 +111,10 @@
     update_refs = (refs[:groups], refs[groups : 2 * groups])
     kept_ref, sent_ref, *piece_refs, scratch = refs[2 * groups :]
     _, period, width = kept_ref.shape
-    for at, (token_ref, middle_ref) in enumerate(((own_ref, kept_ref), (paired_ref, sent_ref))):
+    inputs = (of_this_half(own_ref[0], period)[0], paired_ref[...])
+    for at, (tokens, middle_ref) in enumerate(zip(inputs, (kept_ref, sent_ref))):
         update = sum(ref[...].astype(F32) for ref in update_refs[at])
-        tokens = of_this_half(token_ref[0].astype(F32), period)[0]
-        middle = (tokens + mod_ref[2:3, :] * update).astype(BF16)
+        middle = (tokens.astype(F32) + mod_ref[2:3, :] * update).astype(BF16)
         normed = norm_rows(middle.astype(F32), mod_ref[3:4, :], mod_ref[4:5, :])
         for piece in range(pieces):
             rows = slice(piece * period, (piece + 1) * period)
@@ -117,7 +122,7 @@
             scratch[piece, at * period : (at + 1) * period, :] = normed[rows]
     here = lax.axis_index("frame") // 2
     for at, ref in enumerate(piece_refs):
-        ref[...] = scratch[here ^ at]
+        ref[...] = scratch[here ^ (pieces - 1 - at)]
 
 
 def join_kernel(*refs):
@@ -145,9 +150,8 @@
             cols = slice(group * block, (group + 1) * block)
             query = proj_ref[base : base + HD, cols].astype(BF16)
             keys = proj_ref[base + HD : base + 2 * HD, cols].astype(BF16)
-            values = proj_ref[base + 2 * HD : base + 3 * HD, cols].astype(BF16)
-            probs = softmax_over_rows(dot(keys.T, query), mask)
-            heads_ref[head * HD : (head + 1) * HD, cols] = dot(values, probs)
+            values = proj_ref[base + 2 * HD : base + 3 * HD, cols]
+            heads_ref[head * HD : (head + 1) * HD, cols] = attend(keys.T, query, values, mask)
     weights = jnp.concatenate([ref[...] for ref in output_refs], axis=0)
     for group in range(groups):
         mixed = heads_ref[:, group * block : (group + 1) * block].astype(BF16)
@@ -171,7 +175,7 @@
     period = kept_ref.shape[1]
     here = lax.axis_index("frame")
     for at, ref in enumerate(piece_refs):
-        there = here // 2 ^ at
+        there = here // 2 ^ (pieces - 1 - at)
         for half, middle_ref in enumerate((kept_ref, other_ref)):
             update = ref[half * period : (half + 1) * period, :].astype(F32)
             middle = middle_ref[there].astype(F32)
@@ -232,10 +236,8 @@
         return [weights, swap(after(weights, *others), "patch", 1)]
 
     def exchange_frames(parts):
-        parts = list(parts)
-        for at in reversed(range(1, pieces)):
-            parts[at] = swap(parts[at], "frame", 2 * at)
-        return parts
+        offsets = reversed(range(pieces))
+        return [swap(part, "frame", 2 * at) if at else part for at, part in zip(offsets, parts)]
 
     def return_updates(own, far):
         kept, sent = own
@@ -257,10 +259,14 @@
         (modulation, spatial_qkv, tokens, sister),
         [shape((3 * shard, 2 * rows), F32)],
     )
-    paired = swap(after(tokens, sister), "frame", 1)
+    (shared,) = call(
+        functools.partial(share_kernel, period), (after(tokens, sister),), [halves_shape(BF16)]
+    )
+    paired = swap(shared, "frame", 1)
+    out_pair = with_sister(spatial_out, near)
     far = both_cores([after(block, near, paired) for block in far])
-    out_pair = with_sister(spatial_out, *far)
     temporal_pair = with_sister(temporal_qkv, *far)
+    late_pair = with_sister(temporal_out, *far)
 
     kept, sent = call(
         functools.partial(spatial_kernel, count),
@@ -268,19 +274,21 @@
         [shape((shard, groups * rows), BF16)] * 2,
         [pltpu.VMEM((3 * shard, (count - 2) * rows), F32), pltpu.VMEM((shard, count * rows), F32)],
     )
-    heads = (kept, swap(sent, "patch", 1), *out_pair)
-    far_parts = call(functools.partial(partial_kernel, 1, period), heads, far_shapes)
-    own_parts = call(functools.partial(partial_kernel, 0, period), heads, own_shapes)
-    late_pair = with_sister(temporal_out, far_parts[0])
+    parts = call(
+        functools.partial(partial_kernel, period),
+        (kept, swap(sent, "patch", 1), *out_pair),
+        own_shapes + far_shapes,
+    )
+    updates = return_updates(parts[:2], parts[2:])
     middle, middle_sent, *parts = call(
         functools.partial(middle_kernel, pieces, groups),
-        (modulation, tokens, paired, *return_updates(own_parts, far_parts)),
+        (modulation, tokens, paired, *updates),
         [shape((pieces, period, width), BF16)] * 2 + piece_shapes,
         [pltpu.VMEM((pieces, 2 * period, width), BF16)],
     )
     (segment,) = call(join_kernel, exchange_frames(parts), [shape((rows, width), BF16)])
 
-    def attend(segments, shapes):
+    def attend_frames(segments, shapes):
         columns = len(segments) * rows
         return call(
             functools.partial(temporal_kernel, len(segments), period),
@@ -289,10 +297,11 @@
             [pltpu.VMEM((6 * shard, columns), F32), pltpu.VMEM((2 * shard, columns), F32)],
         )
 
-    segments = across(segment)
+    others = across(segment)[1:]
     middle_other = swap(after(middle_sent, segment), "frame", 1)
-    own_parts = attend([segment], own_shapes)
-    far_parts = attend([after(block, own_parts[0]) for block in segments[1:]], far_shapes)
+    own_parts = attend_frames([segment], own_shapes)
+    others = [after(block, own_parts[0], middle_other) for block in others]
+    far_parts = attend_frames(others, far_shapes)
     parts = call(
         functools.partial(sum_kernel, pieces, groups),
         return_updates(own_parts, far_parts),

time: 71.9 us -> 67.9 us (0.944)
  waiting for transfers between devices: 31.3 us -> 27.1 us
  starting transfers between devices: 23.7 us -> 24.9 us
  Pallas kernels: 13.2 us -> 12.2 us
    ppermute x20, starting transfers between devices: 19.8 us -> 23.3 us  [swap(): return lax.ppermute(value, axis, [(at, at ^ offset) for at in range(size)])]
    ppermute x20, waiting for transfers between devices: 27.4 us -> 24 us  [swap(): return lax.ppermute(value, axis, [(at, at ^ offset) for at in range(size)])]
    ppermute x2, starting transfers between devices: 3.94 us -> 1.69 us  [swap_diagonal(): return lax.ppermute(value, ('frame', 'patch'), pairs)]
    pallas_call x10, Pallas kernels: 13.2 us -> 12.2 us  [call(): pl.pallas_call(body, out_shape=outs, in_specs=[pl.BlockSpec(memory_space=...]
    ppermute x2, waiting for transfers between devices: 3.84 us -> 3.11 us  [swap_diagonal(): return lax.ppermute(value, ('frame', 'patch'), pairs)]
    unnamed x16 -> x18, local copies, waits for them, and re-layouts: 3.31 us -> 3.34 us
  transfers between devices with their start and end apart: 22 -> 22, of which waited for: 15 -> 15; matrix products, arithmetic and copies ran while one was open for 0% -> 0% of each run, Pallas kernels for 14% -> 13%
where the time goes in v7:
time: 67.9 us; the launch traced here: 67.7 us
  waiting for transfers between devices  27.1 us (40%)
  starting transfers between devices  24.9 us (37%)
  Pallas kernels  12.2 us (18%)
  local copies, waits for them, and re-layouts  3.34 us (5%)
    ppermute x20, waiting for transfers between devices, swap(): return lax.ppermute(value, axis, [(at, at ^ offset) for at in range(size)])  24 us
    ppermute x20, starting transfers between devices, swap(): return lax.ppermute(value, axis, [(at, at ^ offset) for at in range(size)])  23.3 us
    pallas_call x10, Pallas kernels, call(): pl.pallas_call(body, out_shape=outs, in_specs=[pl.BlockSpec(memory_space=...  12.2 us
    unnamed x18, local copies, waits for them, and re-layouts  3.34 us
    ppermute x2, waiting for transfers between devices, swap_diagonal(): return lax.ppermute(value, ('frame', 'patch'), pairs)  3.11 us
    ppermute x2, starting transfers between devices, swap_diagonal(): return lax.ppermute(value, ('frame', 'patch'), pairs)  1.69 us
  transfers between devices with their start and end apart: 22, of which 15 were waited for; matrix products, arithmetic and copies ran while one was open for 0% of the time, Pallas kernels for 13%

profile of v7, /device:TPU:0, one launch (start us, length us, event | category | flops | bytes accessed | tf_op | source)
XLA Modules:
  0.0 67.7 jit_solution(9290397560641429096)
XLA Ops:
  0.5 2.5 %collective-permute-start.2 = (bf16[1,128,1152]{2,1,0:T(8,128)(2,1)}, bf16[1,128,1152]{2,1,0:T(8,128)(2,1)S(1)}, u32[]{:S(2)}, u32[]{:S(2)}) collective-permute-start(bf16[1,128,1152]{2,1,0:T(8,128)(2,1)} %own_ref.3), channel_id=1, source_target_pairs={{0,2},{1,3},{2,0},{3,1},{4,6},{5,7},{6,4},{7,5},{8,10},{9,11},{10,... | collective-permute-start | bytes 884744 | tf_op jit(solution)/shard_map/ppermute | solution.py:201
  3.0 1.0 %copy-done.3 = bf16[1,128,1152]{2,1,0:T(8,128)(2,1)S(1)} copy-done((bf16[1,128,1152]{2,1,0:T(8,128)(2,1)S(1)}, bf16[1,128,1152]{2,1,0:T(8,128)(2,1)}, u32[]{:S(2)}) %copy-start.3) | copy-done | bytes 294936
  4.0 1.8 %collective-permute-start.1 = (bf16[64,1152]{1,0:T(8,128)(2,1)S(1)}, bf16[64,1152]{1,0:T(8,128)(2,1)S(1)}, u32[]{:S(2)}, u32[]{:S(2)}) collective-permute-start(bf16[64,1152]{1,0:T(8,128)(2,1)S(1)} %shard_map.64), channel_id=1, source_target_pairs={{0,4},{4,0},{8,12},{12,8},{16,20},{20,16},{24,28},{28,24},{1,5},{5... | collective-permute-start | bytes 442376 | tf_op jit(solution)/shard_map/ppermute | solution.py:201
  5.8 1.6 %copy-done = bf16[864,1152]{1,0:T(8,128)(2,1)S(1)} copy-done((bf16[864,1152]{1,0:T(8,128)(2,1)S(1)}, bf16[864,1152]{1,0:T(8,128)(2,1)}, u32[]{:S(2)}) %copy-start) | copy-done | bytes 1990680
  8.1 1.1 %shard_map.65.near_ref = f32[864,256]{1,0:T(8,128)S(1)} custom-call(f32[6,1152]{1,0:T(8,128)S(1)} %copy-done.7, bf16[864,1152]{1,0:T(8,128)(2,1)S(1)} %copy-done, bf16[1,128,1152]{2,1,0:T(8,128)(2,1)S(1)} %copy-done.3, bf16[1,128,1152]{2,1,0:T(8,128)(2,1)S(1)} %collective-permute-done.sister_ref), custom_call_target="tpu_custom_call" | custom-call | flops 1 | bytes 1 | tf_op jit(solution)/shard_map/pallas_call | solution.py:188
  9.3 1.6 %collective-permute-done.2.refs_0_ = bf16[1,128,1152]{2,1,0:T(8,128)(2,1)S(1)} collective-permute-done((bf16[1,128,1152]{2,1,0:T(8,128)(2,1)}, bf16[1,128,1152]{2,1,0:T(8,128)(2,1)S(1)}, u32[]{:S(2)}, u32[]{:S(2)}) %collective-permute-start.2) | collective-permute-done | bytes 294944 | tf_op jit(solution)/shard_map/ppermute | solution.py:201
  10.9 1.6 %collective-permute-done.3.refs_1_ = bf16[1,128,1152]{2,1,0:T(8,128)(2,1)S(1)} collective-permute-done((bf16[1,128,1152]{2,1,0:T(8,128)(2,1)S(1)}, bf16[1,128,1152]{2,1,0:T(8,128)(2,1)S(1)}, u32[]{:S(2)}, u32[]{:S(2)}) %collective-permute-start.3) | collective-permute-done | bytes 294944 | tf_op jit(solution)/shard_map/ppermute | solution.py:201
  13.0 4.6 %shard_map.66 = (bf16[288,256]{1,0:T(8,128)(2,1)S(1)}, bf16[288,256]{1,0:T(8,128)(2,1)S(1)}) custom-call(f32[6,1152]{1,0:T(8,128)S(1)} %copy-done.8, bf16[864,1152]{1,0:T(8,128)(2,1)S(1)} %copy-done.1, f32[864,256]{1,0:T(8,128)S(1)} %shard_map.65.near_ref, bf16[1,128,1152]{2,1,0:T(8,128)(2,1)S(1)} %collective-permute-done.2.refs_0_, ...), custom_call_target="tpu_custom_call" | custom-call | flops 1 | bytes 1 | tf_op jit(solution)/shard_map/pallas_call | solution.py:188
  18.1 0.9 %collective-permute-done.4.refs_1_ = bf16[288,256]{1,0:T(8,128)(2,1)S(1)} collective-permute-done((bf16[288,256]{1,0:T(8,128)(2,1)S(1)}, bf16[288,256]{1,0:T(8,128)(2,1)S(1)}, u32[]{:S(2)}, u32[]{:S(2)}) %collective-permute-start.4) | collective-permute-done | bytes 147488 | tf_op jit(solution)/shard_map/ppermute | solution.py:201
  19.7 1.8 %collective-permute-start.6 = (bf16[64,1152]{1,0:T(8,128)(2,1)S(1)}, bf16[64,1152]{1,0:T(8,128)(2,1)S(1)}, u32[]{:S(2)}, u32[]{:S(2)}) collective-permute-start(bf16[64,1152]{1,0:T(8,128)(2,1)S(1)} %get-tuple-element.38), channel_id=1, source_target_pairs={{0,2},{1,3},{2,0},{3,1},{4,6},{5,7},{6,4},{7,5},{8,10},{9,11},{10,... | collective-permute-start | bytes 442376 | tf_op jit(solution)/shard_map/ppermute | solution.py:201
  21.5 1.5 %collective-permute-start.7 = (bf16[64,1152]{1,0:T(8,128)(2,1)S(1)}, bf16[64,1152]{1,0:T(8,128)(2,1)S(1)}, u32[]{:S(2)}, u32[]{:S(2)}) collective-permute-start(bf16[64,1152]{1,0:T(8,128)(2,1)S(1)} %get-tuple-element.39), channel_id=1, source_target_pairs={{0,4},{4,0},{8,12},{12,8},{16,20},{20,16},{24,28},{28,24},{1,5},{5... | collective-permute-start | bytes 442376 | tf_op jit(solution)/shard_map/ppermute | solution.py:201
  23.3 2.4 %collective-permute-done.6.refs_1_ = bf16[64,1152]{1,0:T(8,128)(2,1)S(1)} collective-permute-done((bf16[64,1152]{1,0:T(8,128)(2,1)S(1)}, bf16[64,1152]{1,0:T(8,128)(2,1)S(1)}, u32[]{:S(2)}, u32[]{:S(2)}) %collective-permute-start.6) | collective-permute-done | bytes 147488 | tf_op jit(solution)/shard_map/ppermute | solution.py:201
  25.7 2.6 %collective-permute-done.7.refs_2_ = bf16[64,1152]{1,0:T(8,128)(2,1)S(1)} collective-permute-done((bf16[64,1152]{1,0:T(8,128)(2,1)S(1)}, bf16[64,1152]{1,0:T(8,128)(2,1)S(1)}, u32[]{:S(2)}, u32[]{:S(2)}) %collective-permute-start.7) | collective-permute-done | bytes 147488 | tf_op jit(solution)/shard_map/ppermute | solution.py:201
  28.2 1.8 %collective-permute-done.8.refs_3_ = bf16[64,1152]{1,0:T(8,128)(2,1)S(1)} collective-permute-done((bf16[64,1152]{1,0:T(8,128)(2,1)S(1)}, bf16[64,1152]{1,0:T(8,128)(2,1)S(1)}, u32[]{:S(2)}, u32[]{:S(2)}) %collective-permute-start.8) | collective-permute-done | bytes 147488 | tf_op jit(solution)/shard_map/ppermute | solution.py:224
  30.5 3.8 %collective-permute-start.9 = (bf16[32,1152]{1,0:T(8,128)(2,1)S(1)}, bf16[32,1152]{1,0:T(8,128)(2,1)S(1)}, u32[]{:S(2)}, u32[]{:S(2)}) collective-permute-start(bf16[32,1152]{1,0:T(8,128)(2,1)S(1)} %get-tuple-element.43), channel_id=1, source_target_pairs={{0,24},{4,28},{8,16},{12,20},{16,8},{20,12},{24,0},{28,4},{1,25},{... | collective-permute-start | bytes 221192 | tf_op jit(solution)/shard_map/ppermute | solution.py:201
  35.0 2.4 %collective-permute-done.9.refs_0_ = bf16[32,1152]{1,0:T(8,128)(2,1)S(1)} collective-permute-done((bf16[32,1152]{1,0:T(8,128)(2,1)S(1)}, bf16[32,1152]{1,0:T(8,128)(2,1)S(1)}, u32[]{:S(2)}, u32[]{:S(2)}) %collective-permute-start.9) | collective-permute-done | bytes 73760 | tf_op jit(solution)/shard_map/ppermute | solution.py:201
  37.3 2.7 %collective-permute-done.10.refs_1_ = bf16[32,1152]{1,0:T(8,128)(2,1)S(1)} collective-permute-done((bf16[32,1152]{1,0:T(8,128)(2,1)S(1)}, bf16[32,1152]{1,0:T(8,128)(2,1)S(1)}, u32[]{:S(2)}, u32[]{:S(2)}) %collective-permute-start.10) | collective-permute-done | bytes 73760 | tf_op jit(solution)/shard_map/ppermute | solution.py:201
  40.1 1.6 %collective-permute-start.15 = (bf16[128,1152]{1,0:T(8,128)(2,1)S(1)}, bf16[128,1152]{1,0:T(8,128)(2,1)S(1)}, u32[]{:S(2)}, u32[]{:S(2)}) collective-permute-start(bf16[128,1152]{1,0:T(8,128)(2,1)S(1)} %shard_map.69.refs_4_), channel_id=1, source_target_pairs={{0,2},{1,3},{2,0},{3,1},{4,6},{5,7},{6,4},{7,5},{8,10},{9,11},{10,... | collective-permute-start | bytes 884744 | tf_op jit(solution)/shard_map/ppermute | solution.py:201
  41.7 1.5 %collective-permute-start.12 = (bf16[4,16,1152]{2,1,0:T(8,128)(2,1)S(1)}, bf16[4,16,1152]{2,1,0:T(8,128)(2,1)S(1)}, u32[]{:S(2)}, u32[]{:S(2)}) collective-permute-start(bf16[4,16,1152]{2,1,0:T(8,128)(2,1)S(1)} %get-tuple-element.47), channel_id=1, source_target_pairs={{0,4},{4,0},{8,12},{12,8},{16,20},{20,16},{24,28},{28,24},{1,5},{5... | collective-permute-start | bytes 442376 | tf_op jit(solution)/shard_map/ppermute | solution.py:201
  43.2 2.2 %shard_map.70 = (f32[64,1152]{1,0:T(8,128)S(1)}, bf16[64,1152]{1,0:T(8,128)(2,1)S(1)}) custom-call(bf16[864,1152]{1,0:T(8,128)(2,1)S(1)} %copy-done.2, bf16[864,1152]{1,0:T(8,128)(2,1)S(1)} %collective-permute-done.13.refs_1_, bf16[288,1152]{1,0:T(8,128)(2,1)S(1)} %copy-done.5, bf16[288,1152]{1,0:T(8,128)(2,1)S(1)} %collective-permute-done.14.refs_3_, ...), custom_call_target="tpu_custom_call" | custom-call | flops 1 | bytes 1 | tf_op jit(solution)/shard_map/pallas_call | solution.py:188
  45.4 1.4 %collective-permute-done.12.other_ref = bf16[4,16,1152]{2,1,0:T(8,128)(2,1)S(1)} collective-permute-done((bf16[4,16,1152]{2,1,0:T(8,128)(2,1)S(1)}, bf16[4,16,1152]{2,1,0:T(8,128)(2,1)S(1)}, u32[]{:S(2)}, u32[]{:S(2)}) %collective-permute-start.12) | collective-permute-done | bytes 147488 | tf_op jit(solution)/shard_map/ppermute | solution.py:201
  46.8 1.7 %collective-permute-done.15.refs_4_ = bf16[128,1152]{1,0:T(8,128)(2,1)S(1)} collective-permute-done((bf16[128,1152]{1,0:T(8,128)(2,1)S(1)}, bf16[128,1152]{1,0:T(8,128)(2,1)S(1)}, u32[]{:S(2)}, u32[]{:S(2)}) %collective-permute-start.15) | collective-permute-done | bytes 294944 | tf_op jit(solution)/shard_map/ppermute | solution.py:201
  48.5 2.2 %shard_map.71 = (bf16[64,1152]{1,0:T(8,128)(2,1)S(1)}, bf16[64,1152]{1,0:T(8,128)(2,1)S(1)}) custom-call(bf16[864,1152]{1,0:T(8,128)(2,1)S(1)} %copy-done.2, bf16[864,1152]{1,0:T(8,128)(2,1)S(1)} %collective-permute-done.13.refs_1_, bf16[288,1152]{1,0:T(8,128)(2,1)S(1)} %copy-done.5, bf16[288,1152]{1,0:T(8,128)(2,1)S(1)} %collective-permute-done.14.refs_3_, ...), custom_call_target="tpu_custom_call" | custom-call | flops 1 | bytes 1 | tf_op jit(solution)/shard_map/pallas_call | solution.py:188
  50.7 1.5 %collective-permute-start.16 = (bf16[64,1152]{1,0:T(8,128)(2,1)S(1)}, bf16[64,1152]{1,0:T(8,128)(2,1)S(1)}, u32[]{:S(2)}, u32[]{:S(2)}) collective-permute-start(bf16[64,1152]{1,0:T(8,128)(2,1)S(1)} %get-tuple-element.52), channel_id=1, source_target_pairs={{0,2},{1,3},{2,0},{3,1},{4,6},{5,7},{6,4},{7,5},{8,10},{9,11},{10,... | collective-permute-start | bytes 442376 | tf_op jit(solution)/shard_map/ppermute | solution.py:201
  52.3 1.4 %collective-permute-start.18 = (bf16[64,1152]{1,0:T(8,128)(2,1)S(1)}, bf16[64,1152]{1,0:T(8,128)(2,1)S(1)}, u32[]{:S(2)}, u32[]{:S(2)}) collective-permute-start(bf16[64,1152]{1,0:T(8,128)(2,1)S(1)} %get-tuple-element.54), channel_id=1, source_target_pairs={{0,6},{1,7},{2,4},{3,5},{4,2},{5,3},{6,0},{7,1},{8,14},{9,15},{10,... | collective-permute-start | bytes 442376 | tf_op jit(solution)/shard_map/ppermute | solution.py:224
  54.3 3.1 %collective-permute-done.16.refs_1_ = bf16[64,1152]{1,0:T(8,128)(2,1)S(1)} collective-permute-done((bf16[64,1152]{1,0:T(8,128)(2,1)S(1)}, bf16[64,1152]{1,0:T(8,128)(2,1)S(1)}, u32[]{:S(2)}, u32[]{:S(2)}) %collective-permute-start.16) | collective-permute-done | bytes 147488 | tf_op jit(solution)/shard_map/ppermute | solution.py:201
  57.4 1.3 %collective-permute-done.18.refs_3_ = bf16[64,1152]{1,0:T(8,128)(2,1)S(1)} collective-permute-done((bf16[64,1152]{1,0:T(8,128)(2,1)S(1)}, bf16[64,1152]{1,0:T(8,128)(2,1)S(1)}, u32[]{:S(2)}, u32[]{:S(2)}) %collective-permute-start.18) | collective-permute-done | bytes 147488 | tf_op jit(solution)/shard_map/ppermute | solution.py:224
  58.7 0.8 %collective-permute-done.17.refs_2_ = bf16[64,1152]{1,0:T(8,128)(2,1)S(1)} collective-permute-done((bf16[64,1152]{1,0:T(8,128)(2,1)S(1)}, bf16[64,1152]{1,0:T(8,128)(2,1)S(1)}, u32[]{:S(2)}, u32[]{:S(2)}) %collective-permute-start.17) | collective-permute-done | bytes 147488 | tf_op jit(solution)/shard_map/ppermute | solution.py:201
  60.2 3.9 %collective-permute-start.21 = (bf16[32,1152]{1,0:T(8,128)(2,1)S(1)}, bf16[32,1152]{1,0:T(8,128)(2,1)S(1)}, u32[]{:S(2)}, u32[]{:S(2)}) collective-permute-start(bf16[32,1152]{1,0:T(8,128)(2,1)S(1)} %get-tuple-element.57), channel_id=1, source_target_pairs={{0,8},{4,12},{8,0},{12,4},{16,24},{20,28},{24,16},{28,20},{1,9},{5... | collective-permute-start | bytes 221192 | tf_op jit(solution)/shard_map/ppermute | solution.py:201
  64.1 1.9 %collective-permute-done.19.refs_0_ = bf16[32,1152]{1,0:T(8,128)(2,1)S(1)} collective-permute-done((bf16[32,1152]{1,0:T(8,128)(2,1)S(1)}, bf16[32,1152]{1,0:T(8,128)(2,1)S(1)}, u32[]{:S(2)}, u32[]{:S(2)}) %collective-permute-start.19) | collective-permute-done | bytes 73760 | tf_op jit(solution)/shard_map/ppermute | solution.py:201
  66.0 0.9 %collective-permute-done.20.refs_1_ = bf16[32,1152]{1,0:T(8,128)(2,1)S(1)} collective-permute-done((bf16[32,1152]{1,0:T(8,128)(2,1)S(1)}, bf16[32,1152]{1,0:T(8,128)(2,1)S(1)}, u32[]{:S(2)}, u32[]{:S(2)}) %collective-permute-start.20) | collective-permute-done | bytes 73760 | tf_op jit(solution)/shard_map/ppermute | solution.py:201
  66.9 0.8 %shard_map.73 = bf16[8,16,1152]{2,1,0:T(8,128)(2,1)} custom-call(f32[6,1152]{1,0:T(8,128)S(1)} %copy-done.8, bf16[4,16,1152]{2,1,0:T(8,128)(2,1)S(1)} %get-tuple-element.41.kept_ref, bf16[4,16,1152]{2,1,0:T(8,128)(2,1)S(1)} %collective-permute-done.12.other_ref, bf16[32,1152]{1,0:T(8,128)(2,1)S(1)} %collective-permute-done.19.refs_0_, ...), custom_call_target="tpu_custom_call" | custom-call | flops 1 | bytes 1 | tf_op jit(solution)/shard_map/pallas_call | solution.py:188
  (40 shorter events, 5.7 us)
Async XLA Ops:
  0.0 3.0 %collective-permute-start = (bf16[1,128,1152]{2,1,0:T(8,128)(2,1)}, bf16[1,128,1152]{2,1,0:T(8,128)(2,1)S(1)}, u32[]{:S(2)}, u32[]{:S(2)}) collective-permute-start(bf16[1,128,1152]{2,1,0:T(8,128)(2,1)} %own_ref.3), channel_id=1, source_target_pairs={{0,1},{1,0},{2,3},{3,2},{4,5},{5,4},{6,7},{7,6},{8,9},{9,8},{10,11... | collective-permute-start | bytes 884744 | tf_op jit(solution)/shard_map/ppermute | solution.py:201
  0.5 10.4 %collective-permute-start.2 = (bf16[1,128,1152]{2,1,0:T(8,128)(2,1)}, bf16[1,128,1152]{2,1,0:T(8,128)(2,1)S(1)}, u32[]{:S(2)}, u32[]{:S(2)}) collective-permute-start(bf16[1,128,1152]{2,1,0:T(8,128)(2,1)} %own_ref.3), channel_id=1, source_target_pairs={{0,2},{1,3},{2,0},{3,1},{4,6},{5,7},{6,4},{7,5},{8,10},{9,11},{10,... | collective-permute-start | bytes 884744 | tf_op jit(solution)/shard_map/ppermute | solution.py:201
  3.0 1.0 %copy-start.3 = (bf16[1,128,1152]{2,1,0:T(8,128)(2,1)S(1)}, bf16[1,128,1152]{2,1,0:T(8,128)(2,1)}, u32[]{:S(2)}) copy-start(bf16[1,128,1152]{2,1,0:T(8,128)(2,1)} %own_ref.3) | copy-start | bytes 884740
  4.0 9.0 %copy-start.8 = (f32[6,1152]{1,0:T(8,128)S(1)}, f32[6,1152]{1,0:T(8,128)}, u32[]{:S(2)}) copy-start(f32[6,1152]{1,0:T(8,128)} %mod_ref.7) | copy-start | bytes 82948
  4.0 6.8 %collective-permute-start.1 = (bf16[64,1152]{1,0:T(8,128)(2,1)S(1)}, bf16[64,1152]{1,0:T(8,128)(2,1)S(1)}, u32[]{:S(2)}, u32[]{:S(2)}) collective-permute-start(bf16[64,1152]{1,0:T(8,128)(2,1)S(1)} %shard_map.64), channel_id=1, source_target_pairs={{0,4},{4,0},{8,12},{12,8},{16,20},{20,16},{24,28},{28,24},{1,5},{5... | collective-permute-start | bytes 442376 | tf_op jit(solution)/shard_map/ppermute | solution.py:201
  5.8 1.6 %copy-start = (bf16[864,1152]{1,0:T(8,128)(2,1)S(1)}, bf16[864,1152]{1,0:T(8,128)(2,1)}, u32[]{:S(2)}) copy-start(bf16[864,1152]{1,0:T(8,128)(2,1)} %weight_ref.3) | copy-start | bytes 5971972
  7.4 0.8 %copy-start.7 = (f32[6,1152]{1,0:T(8,128)S(1)}, f32[6,1152]{1,0:T(8,128)}, u32[]{:S(2)}) copy-start(f32[6,1152]{1,0:T(8,128)} %mod_ref.7) | copy-start | bytes 82948
  8.1 4.4 %copy-start.6 = (bf16[288,1152]{1,0:T(8,128)(2,1)S(1)}, bf16[288,1152]{1,0:T(8,128)(2,1)}, u32[]{:S(2)}) copy-start(bf16[288,1152]{1,0:T(8,128)(2,1)} %refs_2_.3) | copy-start | bytes 1990660
  8.1 4.8 %copy-start.1 = (bf16[864,1152]{1,0:T(8,128)(2,1)S(1)}, bf16[864,1152]{1,0:T(8,128)(2,1)}, u32[]{:S(2)}) copy-start(bf16[864,1152]{1,0:T(8,128)(2,1)} %weight_ref.3) | copy-start | bytes 5971972
  9.2 8.5 %copy-start.5 = (bf16[288,1152]{1,0:T(8,128)(2,1)S(1)}, bf16[288,1152]{1,0:T(8,128)(2,1)}, u32[]{:S(2)}) copy-start(bf16[288,1152]{1,0:T(8,128)(2,1)} %refs_2_.5) | copy-start | bytes 1990660
  9.3 20.8 %copy-start.4 = (bf16[1,128,1152]{2,1,0:T(8,128)(2,1)S(1)}, bf16[1,128,1152]{2,1,0:T(8,128)(2,1)}, u32[]{:S(2)}) copy-start(bf16[1,128,1152]{2,1,0:T(8,128)(2,1)} %own_ref.3) | copy-start | bytes 884740
  10.9 1.6 %collective-permute-start.3 = (bf16[1,128,1152]{2,1,0:T(8,128)(2,1)S(1)}, bf16[1,128,1152]{2,1,0:T(8,128)(2,1)S(1)}, u32[]{:S(2)}, u32[]{:S(2)}) collective-permute-start(bf16[1,128,1152]{2,1,0:T(8,128)(2,1)S(1)} %collective-permute-done.2.refs_0_), channel_id=1, source_target_pairs={{0,1},{1,0},{2,3},{3,2},{4,5},{5,4},{6,7},{7,6},{8,9},{9,8},{10,11... | collective-permute-start | bytes 884744 | tf_op jit(solution)/shard_map/ppermute | solution.py:201
  12.4 30.7 %collective-permute-start.13 = (bf16[864,1152]{1,0:T(8,128)(2,1)}, bf16[864,1152]{1,0:T(8,128)(2,1)S(1)}, u32[]{:S(2)}, u32[]{:S(2)}) collective-permute-start(bf16[864,1152]{1,0:T(8,128)(2,1)} %refs_0_.3), channel_id=1, source_target_pairs={{0,1},{1,0},{2,3},{3,2},{4,5},{5,4},{6,7},{7,6},{8,9},{9,8},{10,11... | collective-permute-start | bytes 5971976 | tf_op jit(solution)/shard_map/ppermute | solution.py:201
  12.6 6.4 %collective-permute-start.5 = (bf16[288,1152]{1,0:T(8,128)(2,1)S(1)}, bf16[288,1152]{1,0:T(8,128)(2,1)S(1)}, u32[]{:S(2)}, u32[]{:S(2)}) collective-permute-start(bf16[288,1152]{1,0:T(8,128)(2,1)S(1)} %copy-done.6), channel_id=1, source_target_pairs={{0,1},{1,0},{2,3},{3,2},{4,5},{5,4},{6,7},{7,6},{8,9},{9,8},{10,11... | collective-permute-start | bytes 1990664 | tf_op jit(solution)/shard_map/ppermute | solution.py:201
  17.5 25.6 %copy-start.2 = (bf16[864,1152]{1,0:T(8,128)(2,1)S(1)}, bf16[864,1152]{1,0:T(8,128)(2,1)}, u32[]{:S(2)}) copy-start(bf16[864,1152]{1,0:T(8,128)(2,1)} %refs_0_.3) | copy-start | bytes 5971972
  17.5 1.4 %collective-permute-start.4 = (bf16[288,256]{1,0:T(8,128)(2,1)S(1)}, bf16[288,256]{1,0:T(8,128)(2,1)S(1)}, u32[]{:S(2)}, u32[]{:S(2)}) collective-permute-start(bf16[288,256]{1,0:T(8,128)(2,1)S(1)} %get-tuple-element.35), channel_id=1, source_target_pairs={{0,1},{1,0},{2,3},{3,2},{4,5},{5,4},{6,7},{7,6},{8,9},{9,8},{10,11... | collective-permute-start | bytes 442376 | tf_op jit(solution)/shard_map/ppermute | solution.py:201
  17.7 25.4 %collective-permute-start.14 = (bf16[288,1152]{1,0:T(8,128)(2,1)S(1)}, bf16[288,1152]{1,0:T(8,128)(2,1)S(1)}, u32[]{:S(2)}, u32[]{:S(2)}) collective-permute-start(bf16[288,1152]{1,0:T(8,128)(2,1)S(1)} %copy-done.5), channel_id=1, source_target_pairs={{0,1},{1,0},{2,3},{3,2},{4,5},{5,4},{6,7},{7,6},{8,9},{9,8},{10,11... | collective-permute-start | bytes 1990664 | tf_op jit(solution)/shard_map/ppermute | solution.py:201
  19.7 6.0 %collective-permute-start.6 = (bf16[64,1152]{1,0:T(8,128)(2,1)S(1)}, bf16[64,1152]{1,0:T(8,128)(2,1)S(1)}, u32[]{:S(2)}, u32[]{:S(2)}) collective-permute-start(bf16[64,1152]{1,0:T(8,128)(2,1)S(1)} %get-tuple-element.38), channel_id=1, source_target_pairs={{0,2},{1,3},{2,0},{3,1},{4,6},{5,7},{6,4},{7,5},{8,10},{9,11},{10,... | collective-permute-start | bytes 442376 | tf_op jit(solution)/shard_map/ppermute | solution.py:201
  21.5 6.7 %collective-permute-start.7 = (bf16[64,1152]{1,0:T(8,128)(2,1)S(1)}, bf16[64,1152]{1,0:T(8,128)(2,1)S(1)}, u32[]{:S(2)}, u32[]{:S(2)}) collective-permute-start(bf16[64,1152]{1,0:T(8,128)(2,1)S(1)} %get-tuple-element.39), channel_id=1, source_target_pairs={{0,4},{4,0},{8,12},{12,8},{16,20},{20,16},{24,28},{28,24},{1,5},{5... | collective-permute-start | bytes 442376 | tf_op jit(solution)/shard_map/ppermute | solution.py:201
  23.0 7.1 %collective-permute-start.8 = (bf16[64,1152]{1,0:T(8,128)(2,1)S(1)}, bf16[64,1152]{1,0:T(8,128)(2,1)S(1)}, u32[]{:S(2)}, u32[]{:S(2)}) collective-permute-start(bf16[64,1152]{1,0:T(8,128)(2,1)S(1)} %get-tuple-element.40), channel_id=1, source_target_pairs={{0,6},{1,7},{2,4},{3,5},{4,2},{5,3},{6,0},{7,1},{8,14},{9,15},{10,... | collective-permute-start | bytes 442376 | tf_op jit(solution)/shard_map/ppermute | solution.py:224
  30.5 6.8 %collective-permute-start.9 = (bf16[32,1152]{1,0:T(8,128)(2,1)S(1)}, bf16[32,1152]{1,0:T(8,128)(2,1)S(1)}, u32[]{:S(2)}, u32[]{:S(2)}) collective-permute-start(bf16[32,1152]{1,0:T(8,128)(2,1)S(1)} %get-tuple-element.43), channel_id=1, source_target_pairs={{0,24},{4,28},{8,16},{12,20},{16,8},{20,12},{24,0},{28,4},{1,25},{... | collective-permute-start | bytes 221192 | tf_op jit(solution)/shard_map/ppermute | solution.py:201
  34.3 5.7 %collective-permute-start.10 = (bf16[32,1152]{1,0:T(8,128)(2,1)S(1)}, bf16[32,1152]{1,0:T(8,128)(2,1)S(1)}, u32[]{:S(2)}, u32[]{:S(2)}) collective-permute-start(bf16[32,1152]{1,0:T(8,128)(2,1)S(1)} %get-tuple-element.44), channel_id=1, source_target_pairs={{0,16},{4,20},{8,24},{12,28},{16,0},{20,4},{24,8},{28,12},{1,17},{... | collective-permute-start | bytes 221192 | tf_op jit(solution)/shard_map/ppermute | solution.py:201
  34.3 5.7 %collective-permute-start.11 = (bf16[32,1152]{1,0:T(8,128)(2,1)S(1)}, bf16[32,1152]{1,0:T(8,128)(2,1)S(1)}, u32[]{:S(2)}, u32[]{:S(2)}) collective-permute-start(bf16[32,1152]{1,0:T(8,128)(2,1)S(1)} %get-tuple-element.45), channel_id=1, source_target_pairs={{0,8},{4,12},{8,0},{12,4},{16,24},{20,28},{24,16},{28,20},{1,9},{5... | collective-permute-start | bytes 221192 | tf_op jit(solution)/shard_map/ppermute | solution.py:201
  40.1 8.4 %collective-permute-start.15 = (bf16[128,1152]{1,0:T(8,128)(2,1)S(1)}, bf16[128,1152]{1,0:T(8,128)(2,1)S(1)}, u32[]{:S(2)}, u32[]{:S(2)}) collective-permute-start(bf16[128,1152]{1,0:T(8,128)(2,1)S(1)} %shard_map.69.refs_4_), channel_id=1, source_target_pairs={{0,2},{1,3},{2,0},{3,1},{4,6},{5,7},{6,4},{7,5},{8,10},{9,11},{10,... | collective-permute-start | bytes 884744 | tf_op jit(solution)/shard_map/ppermute | solution.py:201
  41.7 5.1 %collective-permute-start.12 = (bf16[4,16,1152]{2,1,0:T(8,128)(2,1)S(1)}, bf16[4,16,1152]{2,1,0:T(8,128)(2,1)S(1)}, u32[]{:S(2)}, u32[]{:S(2)}) collective-permute-start(bf16[4,16,1152]{2,1,0:T(8,128)(2,1)S(1)} %get-tuple-element.47), channel_id=1, source_target_pairs={{0,4},{4,0},{8,12},{12,8},{16,20},{20,16},{24,28},{28,24},{1,5},{5... | collective-permute-start | bytes 442376 | tf_op jit(solution)/shard_map/ppermute | solution.py:201
  50.7 6.7 %collective-permute-start.16 = (bf16[64,1152]{1,0:T(8,128)(2,1)S(1)}, bf16[64,1152]{1,0:T(8,128)(2,1)S(1)}, u32[]{:S(2)}, u32[]{:S(2)}) collective-permute-start(bf16[64,1152]{1,0:T(8,128)(2,1)S(1)} %get-tuple-element.52), channel_id=1, source_target_pairs={{0,2},{1,3},{2,0},{3,1},{4,6},{5,7},{6,4},{7,5},{8,10},{9,11},{10,... | collective-permute-start | bytes 442376 | tf_op jit(solution)/shard_map/ppermute | solution.py:201
  52.3 6.4 %collective-permute-start.18 = (bf16[64,1152]{1,0:T(8,128)(2,1)S(1)}, bf16[64,1152]{1,0:T(8,128)(2,1)S(1)}, u32[]{:S(2)}, u32[]{:S(2)}) collective-permute-start(bf16[64,1152]{1,0:T(8,128)(2,1)S(1)} %get-tuple-element.54), channel_id=1, source_target_pairs={{0,6},{1,7},{2,4},{3,5},{4,2},{5,3},{6,0},{7,1},{8,14},{9,15},{10,... | collective-permute-start | bytes 442376 | tf_op jit(solution)/shard_map/ppermute | solution.py:224
  53.7 5.8 %collective-permute-start.17 = (bf16[64,1152]{1,0:T(8,128)(2,1)S(1)}, bf16[64,1152]{1,0:T(8,128)(2,1)S(1)}, u32[]{:S(2)}, u32[]{:S(2)}) collective-permute-start(bf16[64,1152]{1,0:T(8,128)(2,1)S(1)} %get-tuple-element.53), channel_id=1, source_target_pairs={{0,4},{4,0},{8,12},{12,8},{16,20},{20,16},{24,28},{28,24},{1,5},{5... | collective-permute-start | bytes 442376 | tf_op jit(solution)/shard_map/ppermute | solution.py:201
  59.6 6.3 %collective-permute-start.19 = (bf16[32,1152]{1,0:T(8,128)(2,1)S(1)}, bf16[32,1152]{1,0:T(8,128)(2,1)S(1)}, u32[]{:S(2)}, u32[]{:S(2)}) collective-permute-start(bf16[32,1152]{1,0:T(8,128)(2,1)S(1)} %get-tuple-element.55), channel_id=1, source_target_pairs={{0,24},{4,28},{8,16},{12,20},{16,8},{20,12},{24,0},{28,4},{1,25},{... | collective-permute-start | bytes 221192 | tf_op jit(solution)/shard_map/ppermute | solution.py:201
  60.0 6.8 %collective-permute-start.20 = (bf16[32,1152]{1,0:T(8,128)(2,1)S(1)}, bf16[32,1152]{1,0:T(8,128)(2,1)S(1)}, u32[]{:S(2)}, u32[]{:S(2)}) collective-permute-start(bf16[32,1152]{1,0:T(8,128)(2,1)S(1)} %get-tuple-element.56), channel_id=1, source_target_pairs={{0,16},{4,20},{8,24},{12,28},{16,0},{20,4},{24,8},{28,12},{1,17},{... | collective-permute-start | bytes 221192 | tf_op jit(solution)/shard_map/ppermute | solution.py:201
  60.2 6.7 %collective-permute-start.21 = (bf16[32,1152]{1,0:T(8,128)(2,1)S(1)}, bf16[32,1152]{1,0:T(8,128)(2,1)S(1)}, u32[]{:S(2)}, u32[]{:S(2)}) collective-permute-start(bf16[32,1152]{1,0:T(8,128)(2,1)S(1)} %get-tuple-element.57), channel_id=1, source_target_pairs={{0,8},{4,12},{8,0},{12,4},{16,24},{20,28},{24,16},{28,20},{1,9},{5... | collective-permute-start | bytes 221192 | tf_op jit(solution)/shard_map/ppermute | solution.py:201

commit v8 on v7

--- a/solution.py
+++ b/solution.py
@@ -28,12 +28,12 @@
     )
 
 
-def attend(keys, query, values, mask=None):
-    scores = dot(keys, query)
-    if mask is not None:
-        scores = jnp.where(mask, scores, -1e30)
+def soften(scores):
     top = jnp.max(scores, axis=0, keepdims=True)
-    weights = jnp.exp2((scores - top) * (HD**-0.5 * LOG2E)).astype(BF16)
+    return jnp.exp2((scores - top) * (HD**-0.5 * LOG2E)).astype(BF16)
+
+
+def mix(values, weights):
     ones = jnp.ones((8, values.shape[1]), F32)
     mixed = dot(jnp.concatenate([values, ones], axis=0).astype(BF16), weights)
     return mixed[:HD] * (1.0 / mixed[HD : HD + 1])
@@ -61,14 +61,19 @@
     def whole(start):
         return jnp.concatenate([ref[start : start + HD, :] for ref in (near_ref, far_ref)], axis=1)
 
-    for head in range(heads):
+    def score(head, at):
         base = head * 3 * HD
-        queries, keys, values = (whole(base + part * HD) for part in range(3))
-        keys, queries = keys.astype(BF16).T, queries.astype(BF16)
-        for at in range(0, count, 2):
-            cols = slice(at * block, (at + 2) * block)
-            rows = slice(head * HD, (head + 1) * HD)
-            heads_ref[rows, cols] = attend(keys, queries[:, cols], values)
+        source, start = (near_ref, 0) if at == 0 else (far_ref, (at - 2) * block)
+        query = source[base : base + HD, start : start + 2 * block].astype(BF16)
+        return dot(whole(base + HD).astype(BF16).T, query)
+
+    steps = [(head, at) for head in range(heads) for at in range(0, count, 2)]
+    scores = score(*steps[0])
+    for (head, at), later in zip(steps, [*steps[1:], None]):
+        coming = score(*later) if later else None
+        rows, cols = slice(head * HD, (head + 1) * HD), slice(at * block, (at + 2) * block)
+        heads_ref[rows, cols] = mix(whole(head * 3 * HD + 2 * HD), soften(scores))
+        scores = coming
     for at in range(count):
         out_ref = (kept_ref, sent_ref)[at % 2]
         cols = slice(at // 2 * block, (at // 2 + 1) * block)
@@ -131,12 +136,11 @@
         refs[-1][at * size : (at + 1) * size, :] = ref[...]
 
 
-def temporal_kernel(groups, period, *refs):
-    weight_refs, output_refs, row_refs = refs[:2], refs[2:4], refs[4 : 4 + groups]
-    update_refs = refs[4 + groups : -2]
-    proj_ref, heads_ref = refs[-2:]
+def temporal_kernel(period, block, *refs):
+    weight_refs, output_refs, (proj_ref, heads_ref) = refs[:2], refs[2:4], refs[-2:]
+    groups = proj_ref.shape[1] // block
+    row_refs, update_refs = refs[4 : -2 - 2 * groups], refs[-2 - 2 * groups : -2]
     rows = jnp.concatenate([ref[...] for ref in row_refs], axis=0)
-    block = rows.shape[0] // groups
     depth = weight_refs[0].shape[0]
     for core in range(2):
         proj_ref[core * depth : (core + 1) * depth, :] = dot(weight_refs[core][...], rows, 1, 1)
@@ -144,20 +148,26 @@
     key_patch = lax.broadcasted_iota(jnp.int32, (block, block), 0) % period
     query_patch = lax.broadcasted_iota(jnp.int32, (block, block), 1) % period
     mask = key_patch == query_patch
-    for head in range(heads):
-        base = head * 3 * HD
-        for group in range(groups):
-            cols = slice(group * block, (group + 1) * block)
-            query = proj_ref[base : base + HD, cols].astype(BF16)
-            keys = proj_ref[base + HD : base + 2 * HD, cols].astype(BF16)
-            values = proj_ref[base + 2 * HD : base + 3 * HD, cols]
-            heads_ref[head * HD : (head + 1) * HD, cols] = attend(keys.T, query, values, mask)
     weights = jnp.concatenate([ref[...] for ref in output_refs], axis=0)
     for group in range(groups):
-        mixed = heads_ref[:, group * block : (group + 1) * block].astype(BF16)
+        cols = slice(group * block, (group + 1) * block)
+
+        def part(head, at):
+            start = (head * 3 + at) * HD
+            return proj_ref[start : start + HD, cols]
+
+        scores = []
+        for head in range(heads):
+            keys, query = part(head, 1).astype(BF16).T, part(head, 0).astype(BF16)
+            scores.append(jnp.where(mask, dot(keys, query), -1e30))
+        soft = soften(jnp.concatenate(scores, axis=1))
+        for head in range(heads):
+            mixed = mix(part(head, 2), soft[:, head * block : (head + 1) * block])
+            heads_ref[head * HD : (head + 1) * HD, cols] = mixed
+        mixed = heads_ref[:, cols].astype(BF16)
         parts = halves(dot(mixed.T, weights), period)
-        for ref, part in zip(update_refs[2 * group : 2 * group + 2], parts):
-            ref[...] = part.astype(ref.dtype)
+        for ref, half in zip(update_refs[2 * group : 2 * group + 2], parts):
+            ref[...] = half.astype(ref.dtype)
 
 
 def sum_kernel(pieces, groups, *refs):
@@ -286,22 +296,25 @@
         [shape((pieces, period, width), BF16)] * 2 + piece_shapes,
         [pltpu.VMEM((pieces, 2 * period, width), BF16)],
     )
-    (segment,) = call(join_kernel, exchange_frames(parts), [shape((rows, width), BF16)])
-
-    def attend_frames(segments, shapes):
+    arrived = exchange_frames(parts)
+    first = [[part] for part in across(parts[-1])]
+    (rest,) = call(join_kernel, arrived[:-1], [shape((rows - 2 * period, width), BF16)])
+    rest = across(after(rest, *(part for (part,) in first[1:])))
+    segments = [[late, *early] for late, early in zip(rest, first)]
+
+    def attend_frames(segments, shapes, *others):
         columns = len(segments) * rows
+        inputs = [after(part, *others) for segment in segments for part in segment]
         return call(
-            functools.partial(temporal_kernel, len(segments), period),
-            (*temporal_pair, *late_pair, *segments),
+            functools.partial(temporal_kernel, period, rows),
+            (*temporal_pair, *late_pair, *inputs),
             shapes,
             [pltpu.VMEM((6 * shard, columns), F32), pltpu.VMEM((2 * shard, columns), F32)],
         )
 
-    others = across(segment)[1:]
-    middle_other = swap(after(middle_sent, segment), "frame", 1)
-    own_parts = attend_frames([segment], own_shapes)
-    others = [after(block, own_parts[0], middle_other) for block in others]
-    far_parts = attend_frames(others, far_shapes)
+    middle_other = swap(after(middle_sent, rest[0]), "frame", 1)
+    own_parts = attend_frames(segments[:1], own_shapes)
+    far_parts = attend_frames(segments[1:], far_shapes, own_parts[0], middle_other)
     parts = call(
         functools.partial(sum_kernel, pieces, groups),
         return_updates(own_parts, far_parts),

time: 67.9 us -> 69 us (1.016)
  starting transfers between devices: 24.9 us -> 27.4 us
  Pallas kernels: 12.2 us -> 10.4 us
    pallas_call x10, Pallas kernels: 12.2 us -> 10.4 us  [call(): pl.pallas_call(body, out_shape=outs, in_specs=[pl.BlockSpec(memory_space=...]
    ppermute x20 -> x21, starting transfers between devices: 23.3 us -> 24.9 us  [swap(): return lax.ppermute(value, axis, [(at, at ^ offset) for at in range(size)])]
    ppermute x2, starting transfers between devices: 1.69 us -> 2.43 us  [swap_diagonal(): return lax.ppermute(value, ('frame', 'patch'), pairs)]
    ppermute x20 -> x21, waiting for transfers between devices: 24 us -> 24 us  [swap(): return lax.ppermute(value, axis, [(at, at ^ offset) for at in range(size)])]
  transfers between devices with their start and end apart: 22 -> 23, of which waited for: 15 -> 16; matrix products, arithmetic and copies ran while one was open for 0% -> 0% of each run, Pallas kernels for 13% -> 11%
where the time goes in v8:
time: 69 us; the launch traced here: 68.8 us
  waiting for transfers between devices  27.5 us (40%)
  starting transfers between devices  27.4 us (40%)
  Pallas kernels  10.4 us (15%)
  local copies, waits for them, and re-layouts  3.34 us (5%)
    ppermute x21, starting transfers between devices, swap(): return lax.ppermute(value, axis, [(at, at ^ offset) for at in range(size)])  24.9 us
    ppermute x21, waiting for transfers between devices, swap(): return lax.ppermute(value, axis, [(at, at ^ offset) for at in range(size)])  24 us
    pallas_call x10, Pallas kernels, call(): pl.pallas_call(body, out_shape=outs, in_specs=[pl.BlockSpec(memory_space=...  10.4 us
    ppermute x2, waiting for transfers between devices, swap_diagonal(): return lax.ppermute(value, ('frame', 'patch'), pairs)  3.55 us
    unnamed x18, local copies, waits for them, and re-layouts  3.34 us
    ppermute x2, starting transfers between devices, swap_diagonal(): return lax.ppermute(value, ('frame', 'patch'), pairs)  2.43 us
  transfers between devices with their start and end apart: 23, of which 16 were waited for; matrix products, arithmetic and copies ran while one was open for 0% of the time, Pallas kernels for 11%

profile of v8, /device:TPU:0, one launch (start us, length us, event | category | flops | bytes accessed | tf_op | source)
XLA Modules:
  0.0 68.8 jit_solution(13924315384106545524)
XLA Ops:
  0.5 2.5 %collective-permute-start.2 = (bf16[1,128,1152]{2,1,0:T(8,128)(2,1)}, bf16[1,128,1152]{2,1,0:T(8,128)(2,1)S(1)}, u32[]{:S(2)}, u32[]{:S(2)}) collective-permute-start(bf16[1,128,1152]{2,1,0:T(8,128)(2,1)} %own_ref.3), channel_id=1, source_target_pairs={{0,2},{1,3},{2,0},{3,1},{4,6},{5,7},{6,4},{7,5},{8,10},{9,11},{10,... | collective-permute-start | bytes 884744 | tf_op jit(solution)/shard_map/ppermute | solution.py:211
  3.0 1.0 %copy-done.3 = bf16[1,128,1152]{2,1,0:T(8,128)(2,1)S(1)} copy-done((bf16[1,128,1152]{2,1,0:T(8,128)(2,1)S(1)}, bf16[1,128,1152]{2,1,0:T(8,128)(2,1)}, u32[]{:S(2)}) %copy-start.3) | copy-done | bytes 294936
  4.0 1.8 %collective-permute-start.1 = (bf16[64,1152]{1,0:T(8,128)(2,1)S(1)}, bf16[64,1152]{1,0:T(8,128)(2,1)S(1)}, u32[]{:S(2)}, u32[]{:S(2)}) collective-permute-start(bf16[64,1152]{1,0:T(8,128)(2,1)S(1)} %shard_map.64), channel_id=1, source_target_pairs={{0,4},{4,0},{8,12},{12,8},{16,20},{20,16},{24,28},{28,24},{1,5},{5... | collective-permute-start | bytes 442376 | tf_op jit(solution)/shard_map/ppermute | solution.py:211
  5.8 1.6 %copy-done = bf16[864,1152]{1,0:T(8,128)(2,1)S(1)} copy-done((bf16[864,1152]{1,0:T(8,128)(2,1)S(1)}, bf16[864,1152]{1,0:T(8,128)(2,1)}, u32[]{:S(2)}) %copy-start) | copy-done | bytes 1990680
  8.1 1.1 %shard_map.65.near_ref = f32[864,256]{1,0:T(8,128)S(1)} custom-call(f32[6,1152]{1,0:T(8,128)S(1)} %copy-done.7, bf16[864,1152]{1,0:T(8,128)(2,1)S(1)} %copy-done, bf16[1,128,1152]{2,1,0:T(8,128)(2,1)S(1)} %copy-done.3, bf16[1,128,1152]{2,1,0:T(8,128)(2,1)S(1)} %collective-permute-done.sister_ref), custom_call_target="tpu_custom_call" | custom-call | flops 1 | bytes 1 | tf_op jit(solution)/shard_map/pallas_call | solution.py:198
  9.3 1.6 %collective-permute-done.2.refs_0_ = bf16[1,128,1152]{2,1,0:T(8,128)(2,1)S(1)} collective-permute-done((bf16[1,128,1152]{2,1,0:T(8,128)(2,1)}, bf16[1,128,1152]{2,1,0:T(8,128)(2,1)S(1)}, u32[]{:S(2)}, u32[]{:S(2)}) %collective-permute-start.2) | collective-permute-done | bytes 294944 | tf_op jit(solution)/shard_map/ppermute | solution.py:211
  10.9 1.6 %collective-permute-done.3.refs_1_ = bf16[1,128,1152]{2,1,0:T(8,128)(2,1)S(1)} collective-permute-done((bf16[1,128,1152]{2,1,0:T(8,128)(2,1)S(1)}, bf16[1,128,1152]{2,1,0:T(8,128)(2,1)S(1)}, u32[]{:S(2)}, u32[]{:S(2)}) %collective-permute-start.3) | collective-permute-done | bytes 294944 | tf_op jit(solution)/shard_map/ppermute | solution.py:211
  13.0 3.3 %shard_map.66 = (bf16[288,256]{1,0:T(8,128)(2,1)S(1)}, bf16[288,256]{1,0:T(8,128)(2,1)S(1)}) custom-call(f32[6,1152]{1,0:T(8,128)S(1)} %copy-done.8, bf16[864,1152]{1,0:T(8,128)(2,1)S(1)} %copy-done.1, f32[864,256]{1,0:T(8,128)S(1)} %shard_map.65.near_ref, bf16[1,128,1152]{2,1,0:T(8,128)(2,1)S(1)} %collective-permute-done.2.refs_0_, ...), custom_call_target="tpu_custom_call" | custom-call | flops 1 | bytes 1 | tf_op jit(solution)/shard_map/pallas_call | solution.py:198
  18.5 1.8 %collective-permute-start.6 = (bf16[64,1152]{1,0:T(8,128)(2,1)S(1)}, bf16[64,1152]{1,0:T(8,128)(2,1)S(1)}, u32[]{:S(2)}, u32[]{:S(2)}) collective-permute-start(bf16[64,1152]{1,0:T(8,128)(2,1)S(1)} %get-tuple-element.40), channel_id=1, source_target_pairs={{0,2},{1,3},{2,0},{3,1},{4,6},{5,7},{6,4},{7,5},{8,10},{9,11},{10,... | collective-permute-start | bytes 442376 | tf_op jit(solution)/shard_map/ppermute | solution.py:211
  20.3 1.5 %collective-permute-start.7 = (bf16[64,1152]{1,0:T(8,128)(2,1)S(1)}, bf16[64,1152]{1,0:T(8,128)(2,1)S(1)}, u32[]{:S(2)}, u32[]{:S(2)}) collective-permute-start(bf16[64,1152]{1,0:T(8,128)(2,1)S(1)} %get-tuple-element.41), channel_id=1, source_target_pairs={{0,4},{4,0},{8,12},{12,8},{16,20},{20,16},{24,28},{28,24},{1,5},{5... | collective-permute-start | bytes 442376 | tf_op jit(solution)/shard_map/ppermute | solution.py:211
  22.0 2.4 %collective-permute-done.6.refs_1_ = bf16[64,1152]{1,0:T(8,128)(2,1)S(1)} collective-permute-done((bf16[64,1152]{1,0:T(8,128)(2,1)S(1)}, bf16[64,1152]{1,0:T(8,128)(2,1)S(1)}, u32[]{:S(2)}, u32[]{:S(2)}) %collective-permute-start.6) | collective-permute-done | bytes 147488 | tf_op jit(solution)/shard_map/ppermute | solution.py:211
  24.4 2.6 %collective-permute-done.7.refs_2_ = bf16[64,1152]{1,0:T(8,128)(2,1)S(1)} collective-permute-done((bf16[64,1152]{1,0:T(8,128)(2,1)S(1)}, bf16[64,1152]{1,0:T(8,128)(2,1)S(1)}, u32[]{:S(2)}, u32[]{:S(2)}) %collective-permute-start.7) | collective-permute-done | bytes 147488 | tf_op jit(solution)/shard_map/ppermute | solution.py:211
  27.0 1.9 %collective-permute-done.8.refs_3_ = bf16[64,1152]{1,0:T(8,128)(2,1)S(1)} collective-permute-done((bf16[64,1152]{1,0:T(8,128)(2,1)S(1)}, bf16[64,1152]{1,0:T(8,128)(2,1)S(1)}, u32[]{:S(2)}, u32[]{:S(2)}) %collective-permute-start.8) | collective-permute-done | bytes 147488 | tf_op jit(solution)/shard_map/ppermute | solution.py:234
  29.3 3.8 %collective-permute-start.9 = (bf16[32,1152]{1,0:T(8,128)(2,1)S(1)}, bf16[32,1152]{1,0:T(8,128)(2,1)S(1)}, u32[]{:S(2)}, u32[]{:S(2)}) collective-permute-start(bf16[32,1152]{1,0:T(8,128)(2,1)S(1)} %get-tuple-element.45), channel_id=1, source_target_pairs={{0,24},{4,28},{8,16},{12,20},{16,8},{20,12},{24,0},{28,4},{1,25},{... | collective-permute-start | bytes 221192 | tf_op jit(solution)/shard_map/ppermute | solution.py:211
  33.7 2.4 %collective-permute-done.9.refs_0_ = bf16[32,1152]{1,0:T(8,128)(2,1)S(1)} collective-permute-done((bf16[32,1152]{1,0:T(8,128)(2,1)S(1)}, bf16[32,1152]{1,0:T(8,128)(2,1)S(1)}, u32[]{:S(2)}, u32[]{:S(2)}) %collective-permute-start.9) | collective-permute-done | bytes 73760 | tf_op jit(solution)/shard_map/ppermute | solution.py:211
  36.1 1.4 %collective-permute-start.12 = (bf16[32,1152]{1,0:T(8,128)(2,1)S(1)}, bf16[32,1152]{1,0:T(8,128)(2,1)S(1)}, u32[]{:S(2)}, u32[]{:S(2)}) collective-permute-start(bf16[32,1152]{1,0:T(8,128)(2,1)S(1)} %get-tuple-element.48.refs_5_), channel_id=1, source_target_pairs={{0,2},{1,3},{2,0},{3,1},{4,6},{5,7},{6,4},{7,5},{8,10},{9,11},{10,... | collective-permute-start | bytes 221192 | tf_op jit(solution)/shard_map/ppermute | solution.py:211
  37.5 1.3 %collective-permute-done.10.refs_1_ = bf16[32,1152]{1,0:T(8,128)(2,1)S(1)} collective-permute-done((bf16[32,1152]{1,0:T(8,128)(2,1)S(1)}, bf16[32,1152]{1,0:T(8,128)(2,1)S(1)}, u32[]{:S(2)}, u32[]{:S(2)}) %collective-permute-start.10) | collective-permute-done | bytes 73760 | tf_op jit(solution)/shard_map/ppermute | solution.py:211
  38.8 1.6 %collective-permute-done.12.refs_5_ = bf16[32,1152]{1,0:T(8,128)(2,1)S(1)} collective-permute-done((bf16[32,1152]{1,0:T(8,128)(2,1)S(1)}, bf16[32,1152]{1,0:T(8,128)(2,1)S(1)}, u32[]{:S(2)}, u32[]{:S(2)}) %collective-permute-start.12) | collective-permute-done | bytes 73760 | tf_op jit(solution)/shard_map/ppermute | solution.py:211
  40.5 1.4 %collective-permute-start.16 = (bf16[96,1152]{1,0:T(8,128)(2,1)S(1)}, bf16[96,1152]{1,0:T(8,128)(2,1)S(1)}, u32[]{:S(2)}, u32[]{:S(2)}) collective-permute-start(bf16[96,1152]{1,0:T(8,128)(2,1)S(1)} %shard_map.69.refs_4_), channel_id=1, source_target_pairs={{0,2},{1,3},{2,0},{3,1},{4,6},{5,7},{6,4},{7,5},{8,10},{9,11},{10,... | collective-permute-start | bytes 663560 | tf_op jit(solution)/shard_map/ppermute | solution.py:211
  41.9 1.5 %collective-permute-start.13 = (bf16[4,16,1152]{2,1,0:T(8,128)(2,1)S(1)}, bf16[4,16,1152]{2,1,0:T(8,128)(2,1)S(1)}, u32[]{:S(2)}, u32[]{:S(2)}) collective-permute-start(bf16[4,16,1152]{2,1,0:T(8,128)(2,1)S(1)} %get-tuple-element.50), channel_id=1, source_target_pairs={{0,4},{4,0},{8,12},{12,8},{16,20},{20,16},{24,28},{28,24},{1,5},{5... | collective-permute-start | bytes 442376 | tf_op jit(solution)/shard_map/ppermute | solution.py:211
  43.4 2.0 %shard_map.70 = (f32[64,1152]{1,0:T(8,128)S(1)}, bf16[64,1152]{1,0:T(8,128)(2,1)S(1)}) custom-call(bf16[864,1152]{1,0:T(8,128)(2,1)S(1)} %copy-done.2, bf16[864,1152]{1,0:T(8,128)(2,1)S(1)} %collective-permute-done.14.refs_1_, bf16[288,1152]{1,0:T(8,128)(2,1)S(1)} %copy-done.5, bf16[288,1152]{1,0:T(8,128)(2,1)S(1)} %collective-permute-done.15.refs_3_, ...), custom_call_target="tpu_custom_call" | custom-call | flops 1 | bytes 1 | tf_op jit(solution)/shard_map/pallas_call | solution.py:198
  45.4 1.6 %collective-permute-done.13.other_ref = bf16[4,16,1152]{2,1,0:T(8,128)(2,1)S(1)} collective-permute-done((bf16[4,16,1152]{2,1,0:T(8,128)(2,1)S(1)}, bf16[4,16,1152]{2,1,0:T(8,128)(2,1)S(1)}, u32[]{:S(2)}, u32[]{:S(2)}) %collective-permute-start.13) | collective-permute-done | bytes 147488 | tf_op jit(solution)/shard_map/ppermute | solution.py:211
  47.0 2.0 %shard_map.71 = (bf16[64,1152]{1,0:T(8,128)(2,1)S(1)}, bf16[64,1152]{1,0:T(8,128)(2,1)S(1)}) custom-call(bf16[864,1152]{1,0:T(8,128)(2,1)S(1)} %copy-done.2, bf16[864,1152]{1,0:T(8,128)(2,1)S(1)} %collective-permute-done.14.refs_1_, bf16[288,1152]{1,0:T(8,128)(2,1)S(1)} %copy-done.5, bf16[288,1152]{1,0:T(8,128)(2,1)S(1)} %collective-permute-done.15.refs_3_, ...), custom_call_target="tpu_custom_call" | custom-call | flops 1 | bytes 1 | tf_op jit(solution)/shard_map/pallas_call | solution.py:198
  49.0 0.9 %collective-permute-start.17 = (bf16[64,1152]{1,0:T(8,128)(2,1)S(1)}, bf16[64,1152]{1,0:T(8,128)(2,1)S(1)}, u32[]{:S(2)}, u32[]{:S(2)}) collective-permute-start(bf16[64,1152]{1,0:T(8,128)(2,1)S(1)} %get-tuple-element.56), channel_id=1, source_target_pairs={{0,2},{1,3},{2,0},{3,1},{4,6},{5,7},{6,4},{7,5},{8,10},{9,11},{10,... | collective-permute-start | bytes 442376 | tf_op jit(solution)/shard_map/ppermute | solution.py:211
  49.8 2.2 %collective-permute-start.19 = (bf16[64,1152]{1,0:T(8,128)(2,1)S(1)}, bf16[64,1152]{1,0:T(8,128)(2,1)S(1)}, u32[]{:S(2)}, u32[]{:S(2)}) collective-permute-start(bf16[64,1152]{1,0:T(8,128)(2,1)S(1)} %get-tuple-element.58), channel_id=1, source_target_pairs={{0,6},{1,7},{2,4},{3,5},{4,2},{5,3},{6,0},{7,1},{8,14},{9,15},{10,... | collective-permute-start | bytes 442376 | tf_op jit(solution)/shard_map/ppermute | solution.py:234
  52.5 1.7 %collective-permute-done.17.refs_1_ = bf16[64,1152]{1,0:T(8,128)(2,1)S(1)} collective-permute-done((bf16[64,1152]{1,0:T(8,128)(2,1)S(1)}, bf16[64,1152]{1,0:T(8,128)(2,1)S(1)}, u32[]{:S(2)}, u32[]{:S(2)}) %collective-permute-start.17) | collective-permute-done | bytes 147488 | tf_op jit(solution)/shard_map/ppermute | solution.py:211
  54.2 1.7 %collective-permute-done.19.refs_3_ = bf16[64,1152]{1,0:T(8,128)(2,1)S(1)} collective-permute-done((bf16[64,1152]{1,0:T(8,128)(2,1)S(1)}, bf16[64,1152]{1,0:T(8,128)(2,1)S(1)}, u32[]{:S(2)}, u32[]{:S(2)}) %collective-permute-start.19) | collective-permute-done | bytes 147488 | tf_op jit(solution)/shard_map/ppermute | solution.py:234
  55.9 1.3 %collective-permute-done.18.refs_2_ = bf16[64,1152]{1,0:T(8,128)(2,1)S(1)} collective-permute-done((bf16[64,1152]{1,0:T(8,128)(2,1)S(1)}, bf16[64,1152]{1,0:T(8,128)(2,1)S(1)}, u32[]{:S(2)}, u32[]{:S(2)}) %collective-permute-start.18) | collective-permute-done | bytes 147488 | tf_op jit(solution)/shard_map/ppermute | solution.py:211
  57.3 4.6 %collective-permute-start.20 = (bf16[32,1152]{1,0:T(8,128)(2,1)S(1)}, bf16[32,1152]{1,0:T(8,128)(2,1)S(1)}, u32[]{:S(2)}, u32[]{:S(2)}) collective-permute-start(bf16[32,1152]{1,0:T(8,128)(2,1)S(1)} %get-tuple-element.59), channel_id=1, source_target_pairs={{0,24},{4,28},{8,16},{12,20},{16,8},{20,12},{24,0},{28,4},{1,25},{... | collective-permute-start | bytes 221192 | tf_op jit(solution)/shard_map/ppermute | solution.py:211
  61.9 1.0 %collective-permute-start.21 = (bf16[32,1152]{1,0:T(8,128)(2,1)S(1)}, bf16[32,1152]{1,0:T(8,128)(2,1)S(1)}, u32[]{:S(2)}, u32[]{:S(2)}) collective-permute-start(bf16[32,1152]{1,0:T(8,128)(2,1)S(1)} %get-tuple-element.60), channel_id=1, source_target_pairs={{0,16},{4,20},{8,24},{12,28},{16,0},{20,4},{24,8},{28,12},{1,17},{... | collective-permute-start | bytes 221192 | tf_op jit(solution)/shard_map/ppermute | solution.py:211
  63.0 1.3 %collective-permute-done.20.refs_0_ = bf16[32,1152]{1,0:T(8,128)(2,1)S(1)} collective-permute-done((bf16[32,1152]{1,0:T(8,128)(2,1)S(1)}, bf16[32,1152]{1,0:T(8,128)(2,1)S(1)}, u32[]{:S(2)}, u32[]{:S(2)}) %collective-permute-start.20) | collective-permute-done | bytes 73760 | tf_op jit(solution)/shard_map/ppermute | solution.py:211
  64.2 3.0 %collective-permute-done.21.refs_1_ = bf16[32,1152]{1,0:T(8,128)(2,1)S(1)} collective-permute-done((bf16[32,1152]{1,0:T(8,128)(2,1)S(1)}, bf16[32,1152]{1,0:T(8,128)(2,1)S(1)}, u32[]{:S(2)}, u32[]{:S(2)}) %collective-permute-start.21) | collective-permute-done | bytes 73760 | tf_op jit(solution)/shard_map/ppermute | solution.py:211
  (42 shorter events, 7.4 us)
Async XLA Ops:
  0.0 3.0 %collective-permute-start = (bf16[1,128,1152]{2,1,0:T(8,128)(2,1)}, bf16[1,128,1152]{2,1,0:T(8,128)(2,1)S(1)}, u32[]{:S(2)}, u32[]{:S(2)}) collective-permute-start(bf16[1,128,1152]{2,1,0:T(8,128)(2,1)} %own_ref.3), channel_id=1, source_target_pairs={{0,1},{1,0},{2,3},{3,2},{4,5},{5,4},{6,7},{7,6},{8,9},{9,8},{10,11... | collective-permute-start | bytes 884744 | tf_op jit(solution)/shard_map/ppermute | solution.py:211
  0.5 10.4 %collective-permute-start.2 = (bf16[1,128,1152]{2,1,0:T(8,128)(2,1)}, bf16[1,128,1152]{2,1,0:T(8,128)(2,1)S(1)}, u32[]{:S(2)}, u32[]{:S(2)}) collective-permute-start(bf16[1,128,1152]{2,1,0:T(8,128)(2,1)} %own_ref.3), channel_id=1, source_target_pairs={{0,2},{1,3},{2,0},{3,1},{4,6},{5,7},{6,4},{7,5},{8,10},{9,11},{10,... | collective-permute-start | bytes 884744 | tf_op jit(solution)/shard_map/ppermute | solution.py:211
  3.0 1.0 %copy-start.3 = (bf16[1,128,1152]{2,1,0:T(8,128)(2,1)S(1)}, bf16[1,128,1152]{2,1,0:T(8,128)(2,1)}, u32[]{:S(2)}) copy-start(bf16[1,128,1152]{2,1,0:T(8,128)(2,1)} %own_ref.3) | copy-start | bytes 884740
  4.0 9.0 %copy-start.8 = (f32[6,1152]{1,0:T(8,128)S(1)}, f32[6,1152]{1,0:T(8,128)}, u32[]{:S(2)}) copy-start(f32[6,1152]{1,0:T(8,128)} %mod_ref.7) | copy-start | bytes 82948
  4.0 6.8 %collective-permute-start.1 = (bf16[64,1152]{1,0:T(8,128)(2,1)S(1)}, bf16[64,1152]{1,0:T(8,128)(2,1)S(1)}, u32[]{:S(2)}, u32[]{:S(2)}) collective-permute-start(bf16[64,1152]{1,0:T(8,128)(2,1)S(1)} %shard_map.64), channel_id=1, source_target_pairs={{0,4},{4,0},{8,12},{12,8},{16,20},{20,16},{24,28},{28,24},{1,5},{5... | collective-permute-start | bytes 442376 | tf_op jit(solution)/shard_map/ppermute | solution.py:211
  5.8 1.6 %copy-start = (bf16[864,1152]{1,0:T(8,128)(2,1)S(1)}, bf16[864,1152]{1,0:T(8,128)(2,1)}, u32[]{:S(2)}) copy-start(bf16[864,1152]{1,0:T(8,128)(2,1)} %weight_ref.3) | copy-start | bytes 5971972
  7.4 0.8 %copy-start.7 = (f32[6,1152]{1,0:T(8,128)S(1)}, f32[6,1152]{1,0:T(8,128)}, u32[]{:S(2)}) copy-start(f32[6,1152]{1,0:T(8,128)} %mod_ref.7) | copy-start | bytes 82948
  8.1 4.4 %copy-start.6 = (bf16[288,1152]{1,0:T(8,128)(2,1)S(1)}, bf16[288,1152]{1,0:T(8,128)(2,1)}, u32[]{:S(2)}) copy-start(bf16[288,1152]{1,0:T(8,128)(2,1)} %refs_2_.3) | copy-start | bytes 1990660
  8.1 4.8 %copy-start.1 = (bf16[864,1152]{1,0:T(8,128)(2,1)S(1)}, bf16[864,1152]{1,0:T(8,128)(2,1)}, u32[]{:S(2)}) copy-start(bf16[864,1152]{1,0:T(8,128)(2,1)} %weight_ref.3) | copy-start | bytes 5971972
  9.2 7.3 %copy-start.5 = (bf16[288,1152]{1,0:T(8,128)(2,1)S(1)}, bf16[288,1152]{1,0:T(8,128)(2,1)}, u32[]{:S(2)}) copy-start(bf16[288,1152]{1,0:T(8,128)(2,1)} %refs_2_.5) | copy-start | bytes 1990660
  9.3 19.6 %copy-start.4 = (bf16[1,128,1152]{2,1,0:T(8,128)(2,1)S(1)}, bf16[1,128,1152]{2,1,0:T(8,128)(2,1)}, u32[]{:S(2)}) copy-start(bf16[1,128,1152]{2,1,0:T(8,128)(2,1)} %own_ref.3) | copy-start | bytes 884740
  10.9 1.6 %collective-permute-start.3 = (bf16[1,128,1152]{2,1,0:T(8,128)(2,1)S(1)}, bf16[1,128,1152]{2,1,0:T(8,128)(2,1)S(1)}, u32[]{:S(2)}, u32[]{:S(2)}) collective-permute-start(bf16[1,128,1152]{2,1,0:T(8,128)(2,1)S(1)} %collective-permute-done.2.refs_0_), channel_id=1, source_target_pairs={{0,1},{1,0},{2,3},{3,2},{4,5},{5,4},{6,7},{7,6},{8,9},{9,8},{10,11... | collective-permute-start | bytes 884744 | tf_op jit(solution)/shard_map/ppermute | solution.py:211
  12.4 30.9 %collective-permute-start.14 = (bf16[864,1152]{1,0:T(8,128)(2,1)}, bf16[864,1152]{1,0:T(8,128)(2,1)S(1)}, u32[]{:S(2)}, u32[]{:S(2)}) collective-permute-start(bf16[864,1152]{1,0:T(8,128)(2,1)} %refs_0_.3), channel_id=1, source_target_pairs={{0,1},{1,0},{2,3},{3,2},{4,5},{5,4},{6,7},{7,6},{8,9},{9,8},{10,11... | collective-permute-start | bytes 5971976 | tf_op jit(solution)/shard_map/ppermute | solution.py:211
  12.6 5.2 %collective-permute-start.5 = (bf16[288,1152]{1,0:T(8,128)(2,1)S(1)}, bf16[288,1152]{1,0:T(8,128)(2,1)S(1)}, u32[]{:S(2)}, u32[]{:S(2)}) collective-permute-start(bf16[288,1152]{1,0:T(8,128)(2,1)S(1)} %copy-done.6), channel_id=1, source_target_pairs={{0,1},{1,0},{2,3},{3,2},{4,5},{5,4},{6,7},{7,6},{8,9},{9,8},{10,11... | collective-permute-start | bytes 1990664 | tf_op jit(solution)/shard_map/ppermute | solution.py:211
  16.3 27.1 %copy-start.2 = (bf16[864,1152]{1,0:T(8,128)(2,1)S(1)}, bf16[864,1152]{1,0:T(8,128)(2,1)}, u32[]{:S(2)}) copy-start(bf16[864,1152]{1,0:T(8,128)(2,1)} %refs_0_.3) | copy-start | bytes 5971972
  16.3 1.4 %collective-permute-start.4 = (bf16[288,256]{1,0:T(8,128)(2,1)S(1)}, bf16[288,256]{1,0:T(8,128)(2,1)S(1)}, u32[]{:S(2)}, u32[]{:S(2)}) collective-permute-start(bf16[288,256]{1,0:T(8,128)(2,1)S(1)} %get-tuple-element.37), channel_id=1, source_target_pairs={{0,1},{1,0},{2,3},{3,2},{4,5},{5,4},{6,7},{7,6},{8,9},{9,8},{10,11... | collective-permute-start | bytes 442376 | tf_op jit(solution)/shard_map/ppermute | solution.py:211
  16.5 26.9 %collective-permute-start.15 = (bf16[288,1152]{1,0:T(8,128)(2,1)S(1)}, bf16[288,1152]{1,0:T(8,128)(2,1)S(1)}, u32[]{:S(2)}, u32[]{:S(2)}) collective-permute-start(bf16[288,1152]{1,0:T(8,128)(2,1)S(1)} %copy-done.5), channel_id=1, source_target_pairs={{0,1},{1,0},{2,3},{3,2},{4,5},{5,4},{6,7},{7,6},{8,9},{9,8},{10,11... | collective-permute-start | bytes 1990664 | tf_op jit(solution)/shard_map/ppermute | solution.py:211
  18.5 6.0 %collective-permute-start.6 = (bf16[64,1152]{1,0:T(8,128)(2,1)S(1)}, bf16[64,1152]{1,0:T(8,128)(2,1)S(1)}, u32[]{:S(2)}, u32[]{:S(2)}) collective-permute-start(bf16[64,1152]{1,0:T(8,128)(2,1)S(1)} %get-tuple-element.40), channel_id=1, source_target_pairs={{0,2},{1,3},{2,0},{3,1},{4,6},{5,7},{6,4},{7,5},{8,10},{9,11},{10,... | collective-permute-start | bytes 442376 | tf_op jit(solution)/shard_map/ppermute | solution.py:211
  20.3 6.7 %collective-permute-start.7 = (bf16[64,1152]{1,0:T(8,128)(2,1)S(1)}, bf16[64,1152]{1,0:T(8,128)(2,1)S(1)}, u32[]{:S(2)}, u32[]{:S(2)}) collective-permute-start(bf16[64,1152]{1,0:T(8,128)(2,1)S(1)} %get-tuple-element.41), channel_id=1, source_target_pairs={{0,4},{4,0},{8,12},{12,8},{16,20},{20,16},{24,28},{28,24},{1,5},{5... | collective-permute-start | bytes 442376 | tf_op jit(solution)/shard_map/ppermute | solution.py:211
  21.8 7.1 %collective-permute-start.8 = (bf16[64,1152]{1,0:T(8,128)(2,1)S(1)}, bf16[64,1152]{1,0:T(8,128)(2,1)S(1)}, u32[]{:S(2)}, u32[]{:S(2)}) collective-permute-start(bf16[64,1152]{1,0:T(8,128)(2,1)S(1)} %get-tuple-element.42), channel_id=1, source_target_pairs={{0,6},{1,7},{2,4},{3,5},{4,2},{5,3},{6,0},{7,1},{8,14},{9,15},{10,... | collective-permute-start | bytes 442376 | tf_op jit(solution)/shard_map/ppermute | solution.py:234
  29.3 6.8 %collective-permute-start.9 = (bf16[32,1152]{1,0:T(8,128)(2,1)S(1)}, bf16[32,1152]{1,0:T(8,128)(2,1)S(1)}, u32[]{:S(2)}, u32[]{:S(2)}) collective-permute-start(bf16[32,1152]{1,0:T(8,128)(2,1)S(1)} %get-tuple-element.45), channel_id=1, source_target_pairs={{0,24},{4,28},{8,16},{12,20},{16,8},{20,12},{24,0},{28,4},{1,25},{... | collective-permute-start | bytes 221192 | tf_op jit(solution)/shard_map/ppermute | solution.py:211
  33.1 5.7 %collective-permute-start.10 = (bf16[32,1152]{1,0:T(8,128)(2,1)S(1)}, bf16[32,1152]{1,0:T(8,128)(2,1)S(1)}, u32[]{:S(2)}, u32[]{:S(2)}) collective-permute-start(bf16[32,1152]{1,0:T(8,128)(2,1)S(1)} %get-tuple-element.46), channel_id=1, source_target_pairs={{0,16},{4,20},{8,24},{12,28},{16,0},{20,4},{24,8},{28,12},{1,17},{... | collective-permute-start | bytes 221192 | tf_op jit(solution)/shard_map/ppermute | solution.py:211
  33.1 5.7 %collective-permute-start.11 = (bf16[32,1152]{1,0:T(8,128)(2,1)S(1)}, bf16[32,1152]{1,0:T(8,128)(2,1)S(1)}, u32[]{:S(2)}, u32[]{:S(2)}) collective-permute-start(bf16[32,1152]{1,0:T(8,128)(2,1)S(1)} %get-tuple-element.47), channel_id=1, source_target_pairs={{0,8},{4,12},{8,0},{12,4},{16,24},{20,28},{24,16},{28,20},{1,9},{5... | collective-permute-start | bytes 221192 | tf_op jit(solution)/shard_map/ppermute | solution.py:211
  36.1 4.4 %collective-permute-start.12 = (bf16[32,1152]{1,0:T(8,128)(2,1)S(1)}, bf16[32,1152]{1,0:T(8,128)(2,1)S(1)}, u32[]{:S(2)}, u32[]{:S(2)}) collective-permute-start(bf16[32,1152]{1,0:T(8,128)(2,1)S(1)} %get-tuple-element.48.refs_5_), channel_id=1, source_target_pairs={{0,2},{1,3},{2,0},{3,1},{4,6},{5,7},{6,4},{7,5},{8,10},{9,11},{10,... | collective-permute-start | bytes 221192 | tf_op jit(solution)/shard_map/ppermute | solution.py:211
  40.5 6.5 %collective-permute-start.16 = (bf16[96,1152]{1,0:T(8,128)(2,1)S(1)}, bf16[96,1152]{1,0:T(8,128)(2,1)S(1)}, u32[]{:S(2)}, u32[]{:S(2)}) collective-permute-start(bf16[96,1152]{1,0:T(8,128)(2,1)S(1)} %shard_map.69.refs_4_), channel_id=1, source_target_pairs={{0,2},{1,3},{2,0},{3,1},{4,6},{5,7},{6,4},{7,5},{8,10},{9,11},{10,... | collective-permute-start | bytes 663560 | tf_op jit(solution)/shard_map/ppermute | solution.py:211
  41.9 5.1 %collective-permute-start.13 = (bf16[4,16,1152]{2,1,0:T(8,128)(2,1)S(1)}, bf16[4,16,1152]{2,1,0:T(8,128)(2,1)S(1)}, u32[]{:S(2)}, u32[]{:S(2)}) collective-permute-start(bf16[4,16,1152]{2,1,0:T(8,128)(2,1)S(1)} %get-tuple-element.50), channel_id=1, source_target_pairs={{0,4},{4,0},{8,12},{12,8},{16,20},{20,16},{24,28},{28,24},{1,5},{5... | collective-permute-start | bytes 442376 | tf_op jit(solution)/shard_map/ppermute | solution.py:211
  49.0 5.2 %collective-permute-start.17 = (bf16[64,1152]{1,0:T(8,128)(2,1)S(1)}, bf16[64,1152]{1,0:T(8,128)(2,1)S(1)}, u32[]{:S(2)}, u32[]{:S(2)}) collective-permute-start(bf16[64,1152]{1,0:T(8,128)(2,1)S(1)} %get-tuple-element.56), channel_id=1, source_target_pairs={{0,2},{1,3},{2,0},{3,1},{4,6},{5,7},{6,4},{7,5},{8,10},{9,11},{10,... | collective-permute-start | bytes 442376 | tf_op jit(solution)/shard_map/ppermute | solution.py:211
  49.8 6.0 %collective-permute-start.19 = (bf16[64,1152]{1,0:T(8,128)(2,1)S(1)}, bf16[64,1152]{1,0:T(8,128)(2,1)S(1)}, u32[]{:S(2)}, u32[]{:S(2)}) collective-permute-start(bf16[64,1152]{1,0:T(8,128)(2,1)S(1)} %get-tuple-element.58), channel_id=1, source_target_pairs={{0,6},{1,7},{2,4},{3,5},{4,2},{5,3},{6,0},{7,1},{8,14},{9,15},{10,... | collective-permute-start | bytes 442376 | tf_op jit(solution)/shard_map/ppermute | solution.py:234
  52.0 5.2 %collective-permute-start.18 = (bf16[64,1152]{1,0:T(8,128)(2,1)S(1)}, bf16[64,1152]{1,0:T(8,128)(2,1)S(1)}, u32[]{:S(2)}, u32[]{:S(2)}) collective-permute-start(bf16[64,1152]{1,0:T(8,128)(2,1)S(1)} %get-tuple-element.57), channel_id=1, source_target_pairs={{0,4},{4,0},{8,12},{12,8},{16,20},{20,16},{24,28},{28,24},{1,5},{5... | collective-permute-start | bytes 442376 | tf_op jit(solution)/shard_map/ppermute | solution.py:211
  57.3 6.9 %collective-permute-start.20 = (bf16[32,1152]{1,0:T(8,128)(2,1)S(1)}, bf16[32,1152]{1,0:T(8,128)(2,1)S(1)}, u32[]{:S(2)}, u32[]{:S(2)}) collective-permute-start(bf16[32,1152]{1,0:T(8,128)(2,1)S(1)} %get-tuple-element.59), channel_id=1, source_target_pairs={{0,24},{4,28},{8,16},{12,20},{16,8},{20,12},{24,0},{28,4},{1,25},{... | collective-permute-start | bytes 221192 | tf_op jit(solution)/shard_map/ppermute | solution.py:211
  61.9 5.3 %collective-permute-start.21 = (bf16[32,1152]{1,0:T(8,128)(2,1)S(1)}, bf16[32,1152]{1,0:T(8,128)(2,1)S(1)}, u32[]{:S(2)}, u32[]{:S(2)}) collective-permute-start(bf16[32,1152]{1,0:T(8,128)(2,1)S(1)} %get-tuple-element.60), channel_id=1, source_target_pairs={{0,16},{4,20},{8,24},{12,28},{16,0},{20,4},{24,8},{28,12},{1,17},{... | collective-permute-start | bytes 221192 | tf_op jit(solution)/shard_map/ppermute | solution.py:211
  63.0 5.0 %collective-permute-start.22 = (bf16[32,1152]{1,0:T(8,128)(2,1)S(1)}, bf16[32,1152]{1,0:T(8,128)(2,1)S(1)}, u32[]{:S(2)}, u32[]{:S(2)}) collective-permute-start(bf16[32,1152]{1,0:T(8,128)(2,1)S(1)} %get-tuple-element.61), channel_id=1, source_target_pairs={{0,8},{4,12},{8,0},{12,4},{16,24},{20,28},{24,16},{28,20},{1,9},{5... | collective-permute-start | bytes 221192 | tf_op jit(solution)/shard_map/ppermute | solution.py:211

commit v9 on v8

--- a/solution.py
+++ b/solution.py
@@ -99,26 +99,38 @@
     sent_ref[...] = of_this_half(token_ref[0], period)[1].astype(BF16)
 
 
+def joined(refs):
+    return jnp.concatenate([ref[...] for ref in refs], axis=0)
+
+
 def partial_kernel(period, *refs):
-    head_refs, weight_refs, out_refs = refs[:2], refs[2:4], refs[4:]
-    weights = jnp.concatenate([ref[...] for ref in weight_refs], axis=0)
+    head_refs, weights, out_refs = refs[:2], joined(refs[2:4]), refs[4:]
     block = 2 * out_refs[0].shape[0]
     for at in range(len(out_refs) // 2):
         cols = slice(at * block, (at + 1) * block)
-        heads = jnp.concatenate([ref[:, cols] for ref in head_refs], axis=0)
-        for ref, part in zip(
-            out_refs[2 * at : 2 * at + 2], of_this_half(dot(heads.T, weights), period)
-        ):
+        heads = jnp.concatenate([ref[:, cols] for ref in head_refs], axis=0).T
+        if at == 0:
+            kept, sent = (half.astype(BF16) for half in of_this_half(heads, period))
+            parts = dot(kept, weights), sent
+        else:
+            parts = of_this_half(dot(heads, weights), period)
+        for ref, part in zip(out_refs[2 * at : 2 * at + 2], parts):
             ref[...] = part.astype(ref.dtype)
 
 
+def total_updates(groups, weight_refs, refs):
+    kept = sum(ref[...].astype(F32) for ref in refs[:groups])
+    paired = dot(refs[groups][...], joined(weight_refs))
+    return kept, paired + sum(ref[...].astype(F32) for ref in refs[groups + 1 : 2 * groups])
+
+
 def middle_kernel(pieces, groups, mod_ref, own_ref, paired_ref, *refs):
-    update_refs = (refs[:groups], refs[groups : 2 * groups])
-    kept_ref, sent_ref, *piece_refs, scratch = refs[2 * groups :]
+    kept_ref, sent_ref, *piece_refs, scratch = refs[2 + 2 * groups :]
+    updates = total_updates(groups, refs[:2], refs[2:])
     _, period, width = kept_ref.shape
     inputs = (of_this_half(own_ref[0], period)[0], paired_ref[...])
     for at, (tokens, middle_ref) in enumerate(zip(inputs, (kept_ref, sent_ref))):
-        update = sum(ref[...].astype(F32) for ref in update_refs[at])
+        update = updates[at]
         middle = (tokens.astype(F32) + mod_ref[2:3, :] * update).astype(BF16)
         normed = norm_rows(middle.astype(F32), mod_ref[3:4, :], mod_ref[4:5, :])
         for piece in range(pieces):
@@ -136,7 +148,7 @@
         refs[-1][at * size : (at + 1) * size, :] = ref[...]
 
 
-def temporal_kernel(period, block, *refs):
+def temporal_kernel(own, period, block, *refs):
     weight_refs, output_refs, (proj_ref, heads_ref) = refs[:2], refs[2:4], refs[-2:]
     groups = proj_ref.shape[1] // block
     row_refs, update_refs = refs[4 : -2 - 2 * groups], refs[-2 - 2 * groups : -2]
@@ -148,7 +160,7 @@
     key_patch = lax.broadcasted_iota(jnp.int32, (block, block), 0) % period
     query_patch = lax.broadcasted_iota(jnp.int32, (block, block), 1) % period
     mask = key_patch == query_patch
-    weights = jnp.concatenate([ref[...] for ref in output_refs], axis=0)
+    weights = joined(output_refs)
     for group in range(groups):
         cols = slice(group * block, (group + 1) * block)
 
@@ -164,17 +176,21 @@
         for head in range(heads):
             mixed = mix(part(head, 2), soft[:, head * block : (head + 1) * block])
             heads_ref[head * HD : (head + 1) * HD, cols] = mixed
-        mixed = heads_ref[:, cols].astype(BF16)
-        parts = halves(dot(mixed.T, weights), period)
+        mixed = heads_ref[:, cols].astype(BF16).T
+        if own:
+            kept, sent = halves(mixed, period)
+            parts = dot(kept, weights), sent
+        else:
+            parts = halves(dot(mixed, weights), period)
         for ref, half in zip(update_refs[2 * group : 2 * group + 2], parts):
             ref[...] = half.astype(ref.dtype)
 
 
-def sum_kernel(pieces, groups, *refs):
-    update_refs, piece_refs = (refs[:groups], refs[groups : 2 * groups]), refs[2 * groups :]
+def sum_kernel(groups, *refs):
+    piece_refs = refs[2 + 2 * groups :]
     period = piece_refs[0].shape[0] // 2
-    for at, parts in enumerate(update_refs):
-        update = sum(ref[...].astype(F32) for ref in parts).astype(BF16)
+    for at, update in enumerate(total_updates(groups, refs[:2], refs[2:])):
+        update = update.astype(BF16)
         for piece, ref in enumerate(piece_refs):
             rows = update[piece * period : (piece + 1) * period]
             ref[at * period : (at + 1) * period, :] = rows
@@ -250,15 +266,14 @@
         return [swap(part, "frame", 2 * at) if at else part for at, part in zip(offsets, parts)]
 
     def return_updates(own, far):
-        kept, sent = own
         same = [swap(part, "patch", 2 * at) for at, part in enumerate(far[::2], 1)]
         diagonal = [swap_diagonal(part, 2 * at) for at, part in enumerate(far[1::2], 1)]
-        return [kept, *same, swap(sent, "frame", 1), *diagonal]
+        return [own[0], *same, own[1], *diagonal]
 
     def halves_shape(dtype):
         return shape((rows // 2, width), dtype)
 
-    own_shapes = [halves_shape(F32), halves_shape(BF16)]
+    own_shapes = [halves_shape(F32), shape((rows // 2, 2 * shard), BF16)]
     far_shapes = [halves_shape(BF16)] * (2 * groups - 2)
     piece_shapes = [shape((2 * period, width), BF16)] * pieces
 
@@ -289,35 +304,35 @@
         (kept, swap(sent, "patch", 1), *out_pair),
         own_shapes + far_shapes,
     )
-    updates = return_updates(parts[:2], parts[2:])
+    updates = return_updates((parts[0], swap(parts[1], "frame", 1)), parts[2:])
     middle, middle_sent, *parts = call(
         functools.partial(middle_kernel, pieces, groups),
-        (modulation, tokens, paired, *updates),
+        (modulation, tokens, paired, *out_pair, *updates),
         [shape((pieces, period, width), BF16)] * 2 + piece_shapes,
         [pltpu.VMEM((pieces, 2 * period, width), BF16)],
     )
     arrived = exchange_frames(parts)
-    first = [[part] for part in across(parts[-1])]
-    (rest,) = call(join_kernel, arrived[:-1], [shape((rows - 2 * period, width), BF16)])
-    rest = across(after(rest, *(part for (part,) in first[1:])))
-    segments = [[late, *early] for late, early in zip(rest, first)]
-
-    def attend_frames(segments, shapes, *others):
+    (segment,) = call(join_kernel, arrived, [shape((rows, width), BF16)])
+    segments = across(segment)
+
+    def attend_frames(own, segments, shapes):
         columns = len(segments) * rows
-        inputs = [after(part, *others) for segment in segments for part in segment]
         return call(
-            functools.partial(temporal_kernel, period, rows),
-            (*temporal_pair, *late_pair, *inputs),
+            functools.partial(temporal_kernel, own, period, rows),
+            (*temporal_pair, *late_pair, *segments),
             shapes,
             [pltpu.VMEM((6 * shard, columns), F32), pltpu.VMEM((2 * shard, columns), F32)],
         )
 
-    middle_other = swap(after(middle_sent, rest[0]), "frame", 1)
-    own_parts = attend_frames(segments[:1], own_shapes)
-    far_parts = attend_frames(segments[1:], far_shapes, own_parts[0], middle_other)
+    kept, sent = attend_frames(True, [segment], own_shapes)
+    received = swap(sent, "frame", 1)
+    middle_other = swap(after(middle_sent, segment), "frame", 1)
+    others = [after(block, received, middle_other) for block in segments[1:]]
+    far_parts = attend_frames(False, others, far_shapes)
+    updates = return_updates((kept, received), far_parts)
     parts = call(
-        functools.partial(sum_kernel, pieces, groups),
-        return_updates(own_parts, far_parts),
+        functools.partial(sum_kernel, groups),
+        (*late_pair, *updates),
         piece_shapes,
     )
     (result,) = call(

time: 69 us -> 66.8 us (0.968)
  starting transfers between devices: 27.4 us -> 24.1 us
    ppermute x21 -> x20, waiting for transfers between devices: 24 us -> 27.8 us  [swap(): return lax.ppermute(value, axis, [(at, at ^ offset) for at in range(size)])]
    ppermute x21 -> x20, starting transfers between devices: 24.9 us -> 21.1 us  [swap(): return lax.ppermute(value, axis, [(at, at ^ offset) for at in range(size)])]
    ppermute x2, waiting for transfers between devices: 3.55 us -> 0.22 us  [swap_diagonal(): return lax.ppermute(value, ('frame', 'patch'), pairs)]
  transfers between devices with their start and end apart: 23 -> 22, of which waited for: 16 -> 13; matrix products, arithmetic and copies ran while one was open for 0% -> 0% of each run, Pallas kernels for 11% -> 12%
where the time goes in v9:
time: 66.8 us; the launch traced here: 66.6 us
  waiting for transfers between devices  28 us (42%)
  starting transfers between devices  24.1 us (36%)
  Pallas kernels  11 us (16%)
  local copies, waits for them, and re-layouts  3.34 us (5%)
    ppermute x20, waiting for transfers between devices, swap(): return lax.ppermute(value, axis, [(at, at ^ offset) for at in range(size)])  27.8 us
    ppermute x20, starting transfers between devices, swap(): return lax.ppermute(value, axis, [(at, at ^ offset) for at in range(size)])  21.1 us
    pallas_call x10, Pallas kernels, call(): pl.pallas_call(body, out_shape=outs, in_specs=[pl.BlockSpec(memory_space=...  11 us
    unnamed x18, local copies, waits for them, and re-layouts  3.34 us
    ppermute x2, starting transfers between devices, swap_diagonal(): return lax.ppermute(value, ('frame', 'patch'), pairs)  2.98 us
  transfers between devices with their start and end apart: 22, of which 13 were waited for; matrix products, arithmetic and copies ran while one was open for 0% of the time, Pallas kernels for 12%

profile of v9, /device:TPU:0, one launch (start us, length us, event | category | flops | bytes accessed | tf_op | source)
XLA Modules:
  0.0 66.6 jit_solution(10512667386885763062)
XLA Ops:
  0.5 2.5 %collective-permute-start.3 = (bf16[1,128,1152]{2,1,0:T(8,128)(2,1)}, bf16[1,128,1152]{2,1,0:T(8,128)(2,1)S(1)}, u32[]{:S(2)}, u32[]{:S(2)}) collective-permute-start(bf16[1,128,1152]{2,1,0:T(8,128)(2,1)} %own_ref.3), channel_id=1, source_target_pairs={{0,2},{1,3},{2,0},{3,1},{4,6},{5,7},{6,4},{7,5},{8,10},{9,11},{10,... | collective-permute-start | bytes 884744 | tf_op jit(solution)/shard_map/ppermute | solution.py:227
  3.0 1.0 %copy-done.4 = bf16[1,128,1152]{2,1,0:T(8,128)(2,1)S(1)} copy-done((bf16[1,128,1152]{2,1,0:T(8,128)(2,1)S(1)}, bf16[1,128,1152]{2,1,0:T(8,128)(2,1)}, u32[]{:S(2)}) %copy-start.4) | copy-done | bytes 294936
  4.0 1.8 %collective-permute-start.1 = (bf16[64,1152]{1,0:T(8,128)(2,1)S(1)}, bf16[64,1152]{1,0:T(8,128)(2,1)S(1)}, u32[]{:S(2)}, u32[]{:S(2)}) collective-permute-start(bf16[64,1152]{1,0:T(8,128)(2,1)S(1)} %shard_map.64), channel_id=1, source_target_pairs={{0,4},{4,0},{8,12},{12,8},{16,20},{20,16},{24,28},{28,24},{1,5},{5... | collective-permute-start | bytes 442376 | tf_op jit(solution)/shard_map/ppermute | solution.py:227
  5.8 1.6 %copy-done = bf16[864,1152]{1,0:T(8,128)(2,1)S(1)} copy-done((bf16[864,1152]{1,0:T(8,128)(2,1)S(1)}, bf16[864,1152]{1,0:T(8,128)(2,1)}, u32[]{:S(2)}) %copy-start) | copy-done | bytes 1990680
  7.4 0.8 %copy-done.7 = f32[6,1152]{1,0:T(8,128)S(1)} copy-done((f32[6,1152]{1,0:T(8,128)S(1)}, f32[6,1152]{1,0:T(8,128)}, u32[]{:S(2)}) %copy-start.7) | copy-done | bytes 27672
  8.1 1.1 %shard_map.65.near_ref = f32[864,256]{1,0:T(8,128)S(1)} custom-call(f32[6,1152]{1,0:T(8,128)S(1)} %copy-done.7, bf16[864,1152]{1,0:T(8,128)(2,1)S(1)} %copy-done, bf16[1,128,1152]{2,1,0:T(8,128)(2,1)S(1)} %copy-done.4, bf16[1,128,1152]{2,1,0:T(8,128)(2,1)S(1)} %collective-permute-done.sister_ref), custom_call_target="tpu_custom_call" | custom-call | flops 1 | bytes 1 | tf_op jit(solution)/shard_map/pallas_call | solution.py:214
  9.3 1.6 %collective-permute-done.3.refs_0_ = bf16[1,128,1152]{2,1,0:T(8,128)(2,1)S(1)} collective-permute-done((bf16[1,128,1152]{2,1,0:T(8,128)(2,1)}, bf16[1,128,1152]{2,1,0:T(8,128)(2,1)S(1)}, u32[]{:S(2)}, u32[]{:S(2)}) %collective-permute-start.3) | collective-permute-done | bytes 294944 | tf_op jit(solution)/shard_map/ppermute | solution.py:227
  10.9 1.6 %collective-permute-done.4.refs_1_ = bf16[1,128,1152]{2,1,0:T(8,128)(2,1)S(1)} collective-permute-done((bf16[1,128,1152]{2,1,0:T(8,128)(2,1)S(1)}, bf16[1,128,1152]{2,1,0:T(8,128)(2,1)S(1)}, u32[]{:S(2)}, u32[]{:S(2)}) %collective-permute-start.4) | collective-permute-done | bytes 294944 | tf_op jit(solution)/shard_map/ppermute | solution.py:227
  13.1 3.3 %shard_map.66 = (bf16[288,256]{1,0:T(8,128)(2,1)S(1)}, bf16[288,256]{1,0:T(8,128)(2,1)S(1)}) custom-call(f32[6,1152]{1,0:T(8,128)S(1)} %copy-done.7, bf16[864,1152]{1,0:T(8,128)(2,1)S(1)} %copy-done.1, f32[864,256]{1,0:T(8,128)S(1)} %shard_map.65.near_ref, bf16[1,128,1152]{2,1,0:T(8,128)(2,1)S(1)} %collective-permute-done.3.refs_0_, ...), custom_call_target="tpu_custom_call" | custom-call | flops 1 | bytes 1 | tf_op jit(solution)/shard_map/pallas_call | solution.py:214
  16.9 1.7 %collective-permute-done.5.refs_1_ = bf16[288,256]{1,0:T(8,128)(2,1)S(1)} collective-permute-done((bf16[288,256]{1,0:T(8,128)(2,1)S(1)}, bf16[288,256]{1,0:T(8,128)(2,1)S(1)}, u32[]{:S(2)}, u32[]{:S(2)}) %collective-permute-start.5) | collective-permute-done | bytes 147488 | tf_op jit(solution)/shard_map/ppermute | solution.py:227
  18.6 0.7 %shard_map.67 = (f32[64,1152]{1,0:T(8,128)S(1)}, bf16[64,576]{1,0:T(8,128)(2,1)S(1)}, bf16[64,1152]{1,0:T(8,128)(2,1)S(1)}, bf16[64,1152]{1,0:T(8,128)(2,1)S(1)}) custom-call(bf16[288,256]{1,0:T(8,128)(2,1)S(1)} %get-tuple-element.35.refs_0_, bf16[288,256]{1,0:T(8,128)(2,1)S(1)} %collective-permute-done.5.refs_1_, bf16[288,1152]{1,0:T(8,128)(2,1)S(1)} %copy-done.6, ...), custom_call_target="tpu_custom_call" | custom-call | flops 1 | bytes 1 | tf_op jit(solution)/shard_map/pallas_call | solution.py:214
  19.3 1.8 %collective-permute-start.6 = (bf16[64,1152]{1,0:T(8,128)(2,1)S(1)}, bf16[64,1152]{1,0:T(8,128)(2,1)S(1)}, u32[]{:S(2)}, u32[]{:S(2)}) collective-permute-start(bf16[64,1152]{1,0:T(8,128)(2,1)S(1)} %get-tuple-element.38), channel_id=1, source_target_pairs={{0,2},{1,3},{2,0},{3,1},{4,6},{5,7},{6,4},{7,5},{8,10},{9,11},{10,... | collective-permute-start | bytes 442376 | tf_op jit(solution)/shard_map/ppermute | solution.py:227
  21.1 1.4 %collective-permute-start.8 = (bf16[64,1152]{1,0:T(8,128)(2,1)S(1)}, bf16[64,1152]{1,0:T(8,128)(2,1)S(1)}, u32[]{:S(2)}, u32[]{:S(2)}) collective-permute-start(bf16[64,1152]{1,0:T(8,128)(2,1)S(1)} %get-tuple-element.40), channel_id=1, source_target_pairs={{0,6},{1,7},{2,4},{3,5},{4,2},{5,3},{6,0},{7,1},{8,14},{9,15},{10,... | collective-permute-start | bytes 442376 | tf_op jit(solution)/shard_map/ppermute | solution.py:250
  22.8 5.5 %collective-permute-done.7.refs_4_ = bf16[64,576]{1,0:T(8,128)(2,1)S(1)} collective-permute-done((bf16[64,576]{1,0:T(8,128)(2,1)S(1)}, bf16[64,576]{1,0:T(8,128)(2,1)S(1)}, u32[]{:S(2)}, u32[]{:S(2)}) %collective-permute-start.7) | collective-permute-done | bytes 73760 | tf_op jit(solution)/shard_map/ppermute | solution.py:227
  28.5 0.7 %shard_map.68 = (bf16[4,16,1152]{2,1,0:T(8,128)(2,1)S(1)}, bf16[4,16,1152]{2,1,0:T(8,128)(2,1)S(1)}, bf16[32,1152]{1,0:T(8,128)(2,1)S(1)}, bf16[32,1152]{1,0:T(8...) custom-call(f32[6,1152]{1,0:T(8,128)S(1)} %copy-done.7, bf16[1,128,1152]{2,1,0:T(8,128)(2,1)S(1)} %copy-done.5, ...), custom_call_target="tpu_custom_call" | custom-call | flops 1 | bytes 1 | tf_op jit(solution)/shard_map/pallas_call | solution.py:214
  29.2 3.8 %collective-permute-start.9 = (bf16[32,1152]{1,0:T(8,128)(2,1)S(1)}, bf16[32,1152]{1,0:T(8,128)(2,1)S(1)}, u32[]{:S(2)}, u32[]{:S(2)}) collective-permute-start(bf16[32,1152]{1,0:T(8,128)(2,1)S(1)} %get-tuple-element.43), channel_id=1, source_target_pairs={{0,24},{4,28},{8,16},{12,20},{16,8},{20,12},{24,0},{28,4},{1,25},{... | collective-permute-start | bytes 221192 | tf_op jit(solution)/shard_map/ppermute | solution.py:227
  33.7 2.1 %collective-permute-done.9.refs_0_ = bf16[32,1152]{1,0:T(8,128)(2,1)S(1)} collective-permute-done((bf16[32,1152]{1,0:T(8,128)(2,1)S(1)}, bf16[32,1152]{1,0:T(8,128)(2,1)S(1)}, u32[]{:S(2)}, u32[]{:S(2)}) %collective-permute-start.9) | collective-permute-done | bytes 73760 | tf_op jit(solution)/shard_map/ppermute | solution.py:227
  35.8 2.9 %collective-permute-done.10.refs_1_ = bf16[32,1152]{1,0:T(8,128)(2,1)S(1)} collective-permute-done((bf16[32,1152]{1,0:T(8,128)(2,1)S(1)}, bf16[32,1152]{1,0:T(8,128)(2,1)S(1)}, u32[]{:S(2)}, u32[]{:S(2)}) %collective-permute-start.10) | collective-permute-done | bytes 73760 | tf_op jit(solution)/shard_map/ppermute | solution.py:227
  38.7 1.7 %collective-permute-start.15 = (bf16[128,1152]{1,0:T(8,128)(2,1)S(1)}, bf16[128,1152]{1,0:T(8,128)(2,1)S(1)}, u32[]{:S(2)}, u32[]{:S(2)}) collective-permute-start(bf16[128,1152]{1,0:T(8,128)(2,1)S(1)} %shard_map.69.refs_4_), channel_id=1, source_target_pairs={{0,2},{1,3},{2,0},{3,1},{4,6},{5,7},{6,4},{7,5},{8,10},{9,11},{10,... | collective-permute-start | bytes 884744 | tf_op jit(solution)/shard_map/ppermute | solution.py:227
  40.4 1.5 %collective-permute-start.12 = (bf16[4,16,1152]{2,1,0:T(8,128)(2,1)S(1)}, bf16[4,16,1152]{2,1,0:T(8,128)(2,1)S(1)}, u32[]{:S(2)}, u32[]{:S(2)}) collective-permute-start(bf16[4,16,1152]{2,1,0:T(8,128)(2,1)S(1)} %get-tuple-element.47), channel_id=1, source_target_pairs={{0,4},{4,0},{8,12},{12,8},{16,20},{20,16},{24,28},{28,24},{1,5},{5... | collective-permute-start | bytes 442376 | tf_op jit(solution)/shard_map/ppermute | solution.py:227
  41.9 1.9 %shard_map.70 = (f32[64,1152]{1,0:T(8,128)S(1)}, bf16[64,576]{1,0:T(8,128)(2,1)S(1)}) custom-call(bf16[864,1152]{1,0:T(8,128)(2,1)S(1)} %copy-done.2, bf16[864,1152]{1,0:T(8,128)(2,1)S(1)} %collective-permute-done.14.refs_1_, bf16[288,1152]{1,0:T(8,128)(2,1)S(1)} %copy-done.3, bf16[288,1152]{1,0:T(8,128)(2,1)S(1)} %collective-permute-done.13.refs_3_.refs_1_, ...), custom_call_target="tpu_custom_call" | custom-call | flops 1 | bytes 1 | tf_op jit(solution)/shard_map/pallas_call | solution.py:214
  44.5 1.2 %collective-permute-done.12.other_ref = bf16[4,16,1152]{2,1,0:T(8,128)(2,1)S(1)} collective-permute-done((bf16[4,16,1152]{2,1,0:T(8,128)(2,1)S(1)}, bf16[4,16,1152]{2,1,0:T(8,128)(2,1)S(1)}, u32[]{:S(2)}, u32[]{:S(2)}) %collective-permute-start.12) | collective-permute-done | bytes 147488 | tf_op jit(solution)/shard_map/ppermute | solution.py:227
  45.7 1.5 %collective-permute-done.15.refs_4_ = bf16[128,1152]{1,0:T(8,128)(2,1)S(1)} collective-permute-done((bf16[128,1152]{1,0:T(8,128)(2,1)S(1)}, bf16[128,1152]{1,0:T(8,128)(2,1)S(1)}, u32[]{:S(2)}, u32[]{:S(2)}) %collective-permute-start.15) | collective-permute-done | bytes 294944 | tf_op jit(solution)/shard_map/ppermute | solution.py:227
  47.2 1.2 %collective-permute-done.16.refs_4_ = bf16[64,576]{1,0:T(8,128)(2,1)S(1)} collective-permute-done((bf16[64,576]{1,0:T(8,128)(2,1)S(1)}, bf16[64,576]{1,0:T(8,128)(2,1)S(1)}, u32[]{:S(2)}, u32[]{:S(2)}) %collective-permute-start.16) | collective-permute-done | bytes 73760 | tf_op jit(solution)/shard_map/ppermute | solution.py:227
  48.4 2.0 %shard_map.71 = (bf16[64,1152]{1,0:T(8,128)(2,1)S(1)}, bf16[64,1152]{1,0:T(8,128)(2,1)S(1)}) custom-call(bf16[864,1152]{1,0:T(8,128)(2,1)S(1)} %copy-done.2, bf16[864,1152]{1,0:T(8,128)(2,1)S(1)} %collective-permute-done.14.refs_1_, bf16[288,1152]{1,0:T(8,128)(2,1)S(1)} %copy-done.3, bf16[288,1152]{1,0:T(8,128)(2,1)S(1)} %collective-permute-done.13.refs_3_.refs_1_, ...), custom_call_target="tpu_custom_call" | custom-call | flops 1 | bytes 1 | tf_op jit(solution)/shard_map/pallas_call | solution.py:214
  50.9 1.6 %collective-permute-start.18 = (bf16[64,1152]{1,0:T(8,128)(2,1)S(1)}, bf16[64,1152]{1,0:T(8,128)(2,1)S(1)}, u32[]{:S(2)}, u32[]{:S(2)}) collective-permute-start(bf16[64,1152]{1,0:T(8,128)(2,1)S(1)} %get-tuple-element.54), channel_id=1, source_target_pairs={{0,6},{1,7},{2,4},{3,5},{4,2},{5,3},{6,0},{7,1},{8,14},{9,15},{10,... | collective-permute-start | bytes 442376 | tf_op jit(solution)/shard_map/ppermute | solution.py:250
  52.4 5.1 %collective-permute-done.17.refs_3_ = bf16[64,1152]{1,0:T(8,128)(2,1)S(1)} collective-permute-done((bf16[64,1152]{1,0:T(8,128)(2,1)S(1)}, bf16[64,1152]{1,0:T(8,128)(2,1)S(1)}, u32[]{:S(2)}, u32[]{:S(2)}) %collective-permute-start.17) | collective-permute-done | bytes 147488 | tf_op jit(solution)/shard_map/ppermute | solution.py:227
  57.9 2.2 %collective-permute-start.19 = (bf16[32,1152]{1,0:T(8,128)(2,1)S(1)}, bf16[32,1152]{1,0:T(8,128)(2,1)S(1)}, u32[]{:S(2)}, u32[]{:S(2)}) collective-permute-start(bf16[32,1152]{1,0:T(8,128)(2,1)S(1)} %get-tuple-element.55), channel_id=1, source_target_pairs={{0,24},{4,28},{8,16},{12,20},{16,8},{20,12},{24,0},{28,4},{1,25},{... | collective-permute-start | bytes 221192 | tf_op jit(solution)/shard_map/ppermute | solution.py:227
  60.2 2.2 %collective-permute-start.21 = (bf16[32,1152]{1,0:T(8,128)(2,1)S(1)}, bf16[32,1152]{1,0:T(8,128)(2,1)S(1)}, u32[]{:S(2)}, u32[]{:S(2)}) collective-permute-start(bf16[32,1152]{1,0:T(8,128)(2,1)S(1)} %get-tuple-element.57), channel_id=1, source_target_pairs={{0,8},{4,12},{8,0},{12,4},{16,24},{20,28},{24,16},{28,20},{1,9},{5... | collective-permute-start | bytes 221192 | tf_op jit(solution)/shard_map/ppermute | solution.py:227
  62.4 1.8 %collective-permute-done.19.refs_0_ = bf16[32,1152]{1,0:T(8,128)(2,1)S(1)} collective-permute-done((bf16[32,1152]{1,0:T(8,128)(2,1)S(1)}, bf16[32,1152]{1,0:T(8,128)(2,1)S(1)}, u32[]{:S(2)}, u32[]{:S(2)}) %collective-permute-start.19) | collective-permute-done | bytes 73760 | tf_op jit(solution)/shard_map/ppermute | solution.py:227
  64.2 1.6 %collective-permute-done.20.refs_1_ = bf16[32,1152]{1,0:T(8,128)(2,1)S(1)} collective-permute-done((bf16[32,1152]{1,0:T(8,128)(2,1)S(1)}, bf16[32,1152]{1,0:T(8,128)(2,1)S(1)}, u32[]{:S(2)}, u32[]{:S(2)}) %collective-permute-start.20) | collective-permute-done | bytes 73760 | tf_op jit(solution)/shard_map/ppermute | solution.py:227
  65.7 0.8 %shard_map.73 = bf16[8,16,1152]{2,1,0:T(8,128)(2,1)} custom-call(f32[6,1152]{1,0:T(8,128)S(1)} %copy-done.8, bf16[4,16,1152]{2,1,0:T(8,128)(2,1)S(1)} %get-tuple-element.41.kept_ref, bf16[4,16,1152]{2,1,0:T(8,128)(2,1)S(1)} %collective-permute-done.12.other_ref, bf16[32,1152]{1,0:T(8,128)(2,1)S(1)} %collective-permute-done.19.refs_0_, ...), custom_call_target="tpu_custom_call" | custom-call | flops 1 | bytes 1 | tf_op jit(solution)/shard_map/pallas_call | solution.py:214
  (40 shorter events, 4.4 us)
Async XLA Ops:
  0.0 3.0 %collective-permute-start = (bf16[1,128,1152]{2,1,0:T(8,128)(2,1)}, bf16[1,128,1152]{2,1,0:T(8,128)(2,1)S(1)}, u32[]{:S(2)}, u32[]{:S(2)}) collective-permute-start(bf16[1,128,1152]{2,1,0:T(8,128)(2,1)} %own_ref.3), channel_id=1, source_target_pairs={{0,1},{1,0},{2,3},{3,2},{4,5},{5,4},{6,7},{7,6},{8,9},{9,8},{10,11... | collective-permute-start | bytes 884744 | tf_op jit(solution)/shard_map/ppermute | solution.py:227
  0.5 10.4 %collective-permute-start.3 = (bf16[1,128,1152]{2,1,0:T(8,128)(2,1)}, bf16[1,128,1152]{2,1,0:T(8,128)(2,1)S(1)}, u32[]{:S(2)}, u32[]{:S(2)}) collective-permute-start(bf16[1,128,1152]{2,1,0:T(8,128)(2,1)} %own_ref.3), channel_id=1, source_target_pairs={{0,2},{1,3},{2,0},{3,1},{4,6},{5,7},{6,4},{7,5},{8,10},{9,11},{10,... | collective-permute-start | bytes 884744 | tf_op jit(solution)/shard_map/ppermute | solution.py:227
  3.0 1.0 %copy-start.4 = (bf16[1,128,1152]{2,1,0:T(8,128)(2,1)S(1)}, bf16[1,128,1152]{2,1,0:T(8,128)(2,1)}, u32[]{:S(2)}) copy-start(bf16[1,128,1152]{2,1,0:T(8,128)(2,1)} %own_ref.3) | copy-start | bytes 884740
  4.0 6.8 %collective-permute-start.1 = (bf16[64,1152]{1,0:T(8,128)(2,1)S(1)}, bf16[64,1152]{1,0:T(8,128)(2,1)S(1)}, u32[]{:S(2)}, u32[]{:S(2)}) collective-permute-start(bf16[64,1152]{1,0:T(8,128)(2,1)S(1)} %shard_map.64), channel_id=1, source_target_pairs={{0,4},{4,0},{8,12},{12,8},{16,20},{20,16},{24,28},{28,24},{1,5},{5... | collective-permute-start | bytes 442376 | tf_op jit(solution)/shard_map/ppermute | solution.py:227
  5.8 1.6 %copy-start = (bf16[864,1152]{1,0:T(8,128)(2,1)S(1)}, bf16[864,1152]{1,0:T(8,128)(2,1)}, u32[]{:S(2)}) copy-start(bf16[864,1152]{1,0:T(8,128)(2,1)} %weight_ref.3) | copy-start | bytes 5971972
  7.4 0.8 %copy-start.7 = (f32[6,1152]{1,0:T(8,128)S(1)}, f32[6,1152]{1,0:T(8,128)}, u32[]{:S(2)}) copy-start(f32[6,1152]{1,0:T(8,128)} %mod_ref.7) | copy-start | bytes 82948
  8.1 4.4 %copy-start.6 = (bf16[288,1152]{1,0:T(8,128)(2,1)S(1)}, bf16[288,1152]{1,0:T(8,128)(2,1)}, u32[]{:S(2)}) copy-start(bf16[288,1152]{1,0:T(8,128)(2,1)} %refs_0_.4) | copy-start | bytes 1990660
  8.1 4.8 %copy-start.3 = (bf16[288,1152]{1,0:T(8,128)(2,1)S(1)}, bf16[288,1152]{1,0:T(8,128)(2,1)}, u32[]{:S(2)}) copy-start(bf16[288,1152]{1,0:T(8,128)(2,1)} %refs_0_.7) | copy-start | bytes 1990660
  8.1 5.0 %copy-start.1 = (bf16[864,1152]{1,0:T(8,128)(2,1)S(1)}, bf16[864,1152]{1,0:T(8,128)(2,1)}, u32[]{:S(2)}) copy-start(bf16[864,1152]{1,0:T(8,128)(2,1)} %weight_ref.3) | copy-start | bytes 5971972
  9.2 19.3 %copy-start.5 = (bf16[1,128,1152]{2,1,0:T(8,128)(2,1)S(1)}, bf16[1,128,1152]{2,1,0:T(8,128)(2,1)}, u32[]{:S(2)}) copy-start(bf16[1,128,1152]{2,1,0:T(8,128)(2,1)} %own_ref.3) | copy-start | bytes 884740
  10.9 1.6 %collective-permute-start.4 = (bf16[1,128,1152]{2,1,0:T(8,128)(2,1)S(1)}, bf16[1,128,1152]{2,1,0:T(8,128)(2,1)S(1)}, u32[]{:S(2)}, u32[]{:S(2)}) collective-permute-start(bf16[1,128,1152]{2,1,0:T(8,128)(2,1)S(1)} %collective-permute-done.3.refs_0_), channel_id=1, source_target_pairs={{0,1},{1,0},{2,3},{3,2},{4,5},{5,4},{6,7},{7,6},{8,9},{9,8},{10,11... | collective-permute-start | bytes 884744 | tf_op jit(solution)/shard_map/ppermute | solution.py:227
  12.4 29.5 %collective-permute-start.14 = (bf16[864,1152]{1,0:T(8,128)(2,1)}, bf16[864,1152]{1,0:T(8,128)(2,1)S(1)}, u32[]{:S(2)}, u32[]{:S(2)}) collective-permute-start(bf16[864,1152]{1,0:T(8,128)(2,1)} %refs_0_.6), channel_id=1, source_target_pairs={{0,1},{1,0},{2,3},{3,2},{4,5},{5,4},{6,7},{7,6},{8,9},{9,8},{10,11... | collective-permute-start | bytes 5971976 | tf_op jit(solution)/shard_map/ppermute | solution.py:227
  12.6 6.0 %collective-permute-start.2 = (bf16[288,1152]{1,0:T(8,128)(2,1)S(1)}, bf16[288,1152]{1,0:T(8,128)(2,1)S(1)}, u32[]{:S(2)}, u32[]{:S(2)}) collective-permute-start(bf16[288,1152]{1,0:T(8,128)(2,1)S(1)} %copy-done.6), channel_id=1, source_target_pairs={{0,1},{1,0},{2,3},{3,2},{4,5},{5,4},{6,7},{7,6},{8,9},{9,8},{10,11... | collective-permute-start | bytes 1990664 | tf_op jit(solution)/shard_map/ppermute | solution.py:227
  13.0 29.0 %collective-permute-start.13 = (bf16[288,1152]{1,0:T(8,128)(2,1)S(1)}, bf16[288,1152]{1,0:T(8,128)(2,1)S(1)}, u32[]{:S(2)}, u32[]{:S(2)}) collective-permute-start(bf16[288,1152]{1,0:T(8,128)(2,1)S(1)} %copy-done.3), channel_id=1, source_target_pairs={{0,1},{1,0},{2,3},{3,2},{4,5},{5,4},{6,7},{7,6},{8,9},{9,8},{10,11... | collective-permute-start | bytes 1990664 | tf_op jit(solution)/shard_map/ppermute | solution.py:227
  16.4 2.1 %collective-permute-start.5 = (bf16[288,256]{1,0:T(8,128)(2,1)S(1)}, bf16[288,256]{1,0:T(8,128)(2,1)S(1)}, u32[]{:S(2)}, u32[]{:S(2)}) collective-permute-start(bf16[288,256]{1,0:T(8,128)(2,1)S(1)} %get-tuple-element.36), channel_id=1, source_target_pairs={{0,1},{1,0},{2,3},{3,2},{4,5},{5,4},{6,7},{7,6},{8,9},{9,8},{10,11... | collective-permute-start | bytes 442376 | tf_op jit(solution)/shard_map/ppermute | solution.py:227
  18.6 23.4 %copy-start.2 = (bf16[864,1152]{1,0:T(8,128)(2,1)S(1)}, bf16[864,1152]{1,0:T(8,128)(2,1)}, u32[]{:S(2)}) copy-start(bf16[864,1152]{1,0:T(8,128)(2,1)} %refs_0_.6) | copy-start | bytes 5971972
  19.3 9.0 %collective-permute-start.6 = (bf16[64,1152]{1,0:T(8,128)(2,1)S(1)}, bf16[64,1152]{1,0:T(8,128)(2,1)S(1)}, u32[]{:S(2)}, u32[]{:S(2)}) collective-permute-start(bf16[64,1152]{1,0:T(8,128)(2,1)S(1)} %get-tuple-element.38), channel_id=1, source_target_pairs={{0,2},{1,3},{2,0},{3,1},{4,6},{5,7},{6,4},{7,5},{8,10},{9,11},{10,... | collective-permute-start | bytes 442376 | tf_op jit(solution)/shard_map/ppermute | solution.py:227
  21.1 7.4 %collective-permute-start.8 = (bf16[64,1152]{1,0:T(8,128)(2,1)S(1)}, bf16[64,1152]{1,0:T(8,128)(2,1)S(1)}, u32[]{:S(2)}, u32[]{:S(2)}) collective-permute-start(bf16[64,1152]{1,0:T(8,128)(2,1)S(1)} %get-tuple-element.40), channel_id=1, source_target_pairs={{0,6},{1,7},{2,4},{3,5},{4,2},{5,3},{6,0},{7,1},{8,14},{9,15},{10,... | collective-permute-start | bytes 442376 | tf_op jit(solution)/shard_map/ppermute | solution.py:250
  22.5 5.8 %collective-permute-start.7 = (bf16[64,576]{1,0:T(8,128)(2,1)S(1)}, bf16[64,576]{1,0:T(8,128)(2,1)S(1)}, u32[]{:S(2)}, u32[]{:S(2)}) collective-permute-start(bf16[64,576]{1,0:T(8,128)(2,1)S(1)} %get-tuple-element.39), channel_id=1, source_target_pairs={{0,4},{4,0},{8,12},{12,8},{16,20},{20,16},{24,28},{28,24},{1,5},{5... | collective-permute-start | bytes 221192 | tf_op jit(solution)/shard_map/ppermute | solution.py:227
  29.2 6.5 %collective-permute-start.9 = (bf16[32,1152]{1,0:T(8,128)(2,1)S(1)}, bf16[32,1152]{1,0:T(8,128)(2,1)S(1)}, u32[]{:S(2)}, u32[]{:S(2)}) collective-permute-start(bf16[32,1152]{1,0:T(8,128)(2,1)S(1)} %get-tuple-element.43), channel_id=1, source_target_pairs={{0,24},{4,28},{8,16},{12,20},{16,8},{20,12},{24,0},{28,4},{1,25},{... | collective-permute-start | bytes 221192 | tf_op jit(solution)/shard_map/ppermute | solution.py:227
  33.0 5.7 %collective-permute-start.10 = (bf16[32,1152]{1,0:T(8,128)(2,1)S(1)}, bf16[32,1152]{1,0:T(8,128)(2,1)S(1)}, u32[]{:S(2)}, u32[]{:S(2)}) collective-permute-start(bf16[32,1152]{1,0:T(8,128)(2,1)S(1)} %get-tuple-element.44), channel_id=1, source_target_pairs={{0,16},{4,20},{8,24},{12,28},{16,0},{20,4},{24,8},{28,12},{1,17},{... | collective-permute-start | bytes 221192 | tf_op jit(solution)/shard_map/ppermute | solution.py:227
  33.0 5.7 %collective-permute-start.11 = (bf16[32,1152]{1,0:T(8,128)(2,1)S(1)}, bf16[32,1152]{1,0:T(8,128)(2,1)S(1)}, u32[]{:S(2)}, u32[]{:S(2)}) collective-permute-start(bf16[32,1152]{1,0:T(8,128)(2,1)S(1)} %get-tuple-element.45), channel_id=1, source_target_pairs={{0,8},{4,12},{8,0},{12,4},{16,24},{20,28},{24,16},{28,20},{1,9},{5... | collective-permute-start | bytes 221192 | tf_op jit(solution)/shard_map/ppermute | solution.py:227
  38.7 8.4 %collective-permute-start.15 = (bf16[128,1152]{1,0:T(8,128)(2,1)S(1)}, bf16[128,1152]{1,0:T(8,128)(2,1)S(1)}, u32[]{:S(2)}, u32[]{:S(2)}) collective-permute-start(bf16[128,1152]{1,0:T(8,128)(2,1)S(1)} %shard_map.69.refs_4_), channel_id=1, source_target_pairs={{0,2},{1,3},{2,0},{3,1},{4,6},{5,7},{6,4},{7,5},{8,10},{9,11},{10,... | collective-permute-start | bytes 884744 | tf_op jit(solution)/shard_map/ppermute | solution.py:227
  40.4 5.2 %collective-permute-start.12 = (bf16[4,16,1152]{2,1,0:T(8,128)(2,1)S(1)}, bf16[4,16,1152]{2,1,0:T(8,128)(2,1)S(1)}, u32[]{:S(2)}, u32[]{:S(2)}) collective-permute-start(bf16[4,16,1152]{2,1,0:T(8,128)(2,1)S(1)} %get-tuple-element.47), channel_id=1, source_target_pairs={{0,4},{4,0},{8,12},{12,8},{16,20},{20,16},{24,28},{28,24},{1,5},{5... | collective-permute-start | bytes 442376 | tf_op jit(solution)/shard_map/ppermute | solution.py:227
  43.9 4.5 %collective-permute-start.16 = (bf16[64,576]{1,0:T(8,128)(2,1)S(1)}, bf16[64,576]{1,0:T(8,128)(2,1)S(1)}, u32[]{:S(2)}, u32[]{:S(2)}) collective-permute-start(bf16[64,576]{1,0:T(8,128)(2,1)S(1)} %get-tuple-element.51), channel_id=1, source_target_pairs={{0,4},{4,0},{8,12},{12,8},{16,20},{20,16},{24,28},{28,24},{1,5},{5... | collective-permute-start | bytes 221192 | tf_op jit(solution)/shard_map/ppermute | solution.py:227
  50.4 15.4 %copy-start.8 = (f32[6,1152]{1,0:T(8,128)S(1)}, f32[6,1152]{1,0:T(8,128)}, u32[]{:S(2)}) copy-start(f32[6,1152]{1,0:T(8,128)} %mod_ref.7) | copy-start | bytes 82948
  50.4 7.2 %collective-permute-start.17 = (bf16[64,1152]{1,0:T(8,128)(2,1)S(1)}, bf16[64,1152]{1,0:T(8,128)(2,1)S(1)}, u32[]{:S(2)}, u32[]{:S(2)}) collective-permute-start(bf16[64,1152]{1,0:T(8,128)(2,1)S(1)} %get-tuple-element.53), channel_id=1, source_target_pairs={{0,2},{1,3},{2,0},{3,1},{4,6},{5,7},{6,4},{7,5},{8,10},{9,11},{10,... | collective-permute-start | bytes 442376 | tf_op jit(solution)/shard_map/ppermute | solution.py:227
  50.9 6.7 %collective-permute-start.18 = (bf16[64,1152]{1,0:T(8,128)(2,1)S(1)}, bf16[64,1152]{1,0:T(8,128)(2,1)S(1)}, u32[]{:S(2)}, u32[]{:S(2)}) collective-permute-start(bf16[64,1152]{1,0:T(8,128)(2,1)S(1)} %get-tuple-element.54), channel_id=1, source_target_pairs={{0,6},{1,7},{2,4},{3,5},{4,2},{5,3},{6,0},{7,1},{8,14},{9,15},{10,... | collective-permute-start | bytes 442376 | tf_op jit(solution)/shard_map/ppermute | solution.py:250
  57.9 6.2 %collective-permute-start.19 = (bf16[32,1152]{1,0:T(8,128)(2,1)S(1)}, bf16[32,1152]{1,0:T(8,128)(2,1)S(1)}, u32[]{:S(2)}, u32[]{:S(2)}) collective-permute-start(bf16[32,1152]{1,0:T(8,128)(2,1)S(1)} %get-tuple-element.55), channel_id=1, source_target_pairs={{0,24},{4,28},{8,16},{12,20},{16,8},{20,12},{24,0},{28,4},{1,25},{... | collective-permute-start | bytes 221192 | tf_op jit(solution)/shard_map/ppermute | solution.py:227
  60.2 5.6 %collective-permute-start.20 = (bf16[32,1152]{1,0:T(8,128)(2,1)S(1)}, bf16[32,1152]{1,0:T(8,128)(2,1)S(1)}, u32[]{:S(2)}, u32[]{:S(2)}) collective-permute-start(bf16[32,1152]{1,0:T(8,128)(2,1)S(1)} %get-tuple-element.56), channel_id=1, source_target_pairs={{0,16},{4,20},{8,24},{12,28},{16,0},{20,4},{24,8},{28,12},{1,17},{... | collective-permute-start | bytes 221192 | tf_op jit(solution)/shard_map/ppermute | solution.py:227
  60.2 5.6 %collective-permute-start.21 = (bf16[32,1152]{1,0:T(8,128)(2,1)S(1)}, bf16[32,1152]{1,0:T(8,128)(2,1)S(1)}, u32[]{:S(2)}, u32[]{:S(2)}) collective-permute-start(bf16[32,1152]{1,0:T(8,128)(2,1)S(1)} %get-tuple-element.57), channel_id=1, source_target_pairs={{0,8},{4,12},{8,0},{12,4},{16,24},{20,28},{24,16},{28,20},{1,9},{5... | collective-permute-start | bytes 221192 | tf_op jit(solution)/shard_map/ppermute | solution.py:227

commit v10 on v9

--- a/solution.py
+++ b/solution.py
@@ -124,7 +124,7 @@
     return kept, paired + sum(ref[...].astype(F32) for ref in refs[groups + 1 : 2 * groups])
 
 
-def middle_kernel(pieces, groups, mod_ref, own_ref, paired_ref, *refs):
+def middle_kernel(offsets, groups, mod_ref, own_ref, paired_ref, *refs):
     kept_ref, sent_ref, *piece_refs, scratch = refs[2 + 2 * groups :]
     updates = total_updates(groups, refs[:2], refs[2:])
     _, period, width = kept_ref.shape
@@ -133,13 +133,13 @@
         update = updates[at]
         middle = (tokens.astype(F32) + mod_ref[2:3, :] * update).astype(BF16)
         normed = norm_rows(middle.astype(F32), mod_ref[3:4, :], mod_ref[4:5, :])
-        for piece in range(pieces):
+        for piece in range(len(offsets)):
             rows = slice(piece * period, (piece + 1) * period)
             middle_ref[piece] = middle[rows]
             scratch[piece, at * period : (at + 1) * period, :] = normed[rows]
     here = lax.axis_index("frame") // 2
-    for at, ref in enumerate(piece_refs):
-        ref[...] = scratch[here ^ (pieces - 1 - at)]
+    for offset, ref in zip(offsets, piece_refs):
+        ref[...] = scratch[here ^ offset]
 
 
 def join_kernel(*refs):
@@ -196,12 +196,12 @@
             ref[at * period : (at + 1) * period, :] = rows
 
 
-def result_kernel(pieces, mod_ref, kept_ref, other_ref, *refs):
+def result_kernel(offsets, mod_ref, kept_ref, other_ref, *refs):
     piece_refs, out_ref = refs[:-1], refs[-1]
     period = kept_ref.shape[1]
     here = lax.axis_index("frame")
-    for at, ref in enumerate(piece_refs):
-        there = here // 2 ^ (pieces - 1 - at)
+    for offset, ref in zip(offsets, piece_refs):
+        there = here // 2 ^ offset
         for half, middle_ref in enumerate((kept_ref, other_ref)):
             update = ref[half * period : (half + 1) * period, :].astype(F32)
             middle = middle_ref[there].astype(F32)
@@ -258,11 +258,13 @@
     pieces, groups = frames // 2, count // 2
     shape = jax.ShapeDtypeStruct
 
+    first = pieces // 2
+    offsets = (*reversed(range(first + 1, pieces)), 0, *reversed(range(1, first + 1)))
+
     def with_sister(weights, *others):
         return [weights, swap(after(weights, *others), "patch", 1)]
 
     def exchange_frames(parts):
-        offsets = reversed(range(pieces))
         return [swap(part, "frame", 2 * at) if at else part for at, part in zip(offsets, parts)]
 
     def return_updates(own, far):
@@ -299,24 +301,26 @@
         [shape((shard, groups * rows), BF16)] * 2,
         [pltpu.VMEM((3 * shard, (count - 2) * rows), F32), pltpu.VMEM((shard, count * rows), F32)],
     )
+    received = swap(sent, "patch", 1)
     parts = call(
         functools.partial(partial_kernel, period),
-        (kept, swap(sent, "patch", 1), *out_pair),
+        (kept, received, *out_pair),
         own_shapes + far_shapes,
     )
     updates = return_updates((parts[0], swap(parts[1], "frame", 1)), parts[2:])
     middle, middle_sent, *parts = call(
-        functools.partial(middle_kernel, pieces, groups),
+        functools.partial(middle_kernel, offsets, groups),
         (modulation, tokens, paired, *out_pair, *updates),
         [shape((pieces, period, width), BF16)] * 2 + piece_shapes,
         [pltpu.VMEM((pieces, 2 * period, width), BF16)],
     )
     arrived = exchange_frames(parts)
-    (segment,) = call(join_kernel, arrived, [shape((rows, width), BF16)])
-    segments = across(segment)
+    half_shape = [halves_shape(BF16)]
+    early = across(call(join_kernel, arrived[:first], half_shape)[0])
+    late = across(call(join_kernel, arrived[first:], half_shape)[0])
 
     def attend_frames(own, segments, shapes):
-        columns = len(segments) * rows
+        columns = len(segments) // 2 * rows
         return call(
             functools.partial(temporal_kernel, own, period, rows),
             (*temporal_pair, *late_pair, *segments),
@@ -324,19 +328,21 @@
             [pltpu.VMEM((6 * shard, columns), F32), pltpu.VMEM((2 * shard, columns), F32)],
         )
 
-    kept, sent = attend_frames(True, [segment], own_shapes)
+    own_early = after(early[0], *early[1:])
+    middle_other = swap(after(middle_sent, *late[1:]), "frame", 1)
+    kept, sent = attend_frames(True, [own_early, late[0]], own_shapes)
     received = swap(sent, "frame", 1)
-    middle_other = swap(after(middle_sent, segment), "frame", 1)
-    others = [after(block, received, middle_other) for block in segments[1:]]
+    others = [part for pair in zip(early[1:], late[1:]) for part in pair]
+    others = [after(part, received) for part in others]
     far_parts = attend_frames(False, others, far_shapes)
-    updates = return_updates((kept, received), far_parts)
+    updates = return_updates((after(kept, middle_other), received), far_parts)
     parts = call(
         functools.partial(sum_kernel, groups),
         (*late_pair, *updates),
         piece_shapes,
     )
     (result,) = call(
-        functools.partial(result_kernel, pieces),
+        functools.partial(result_kernel, offsets),
         (modulation, middle, middle_other, *exchange_frames(parts)),
         [shape((frames, period, width), BF16)],
     )

time: 66.8 us -> 68.5 us (1.025)
  starting transfers between devices: 24.1 us -> 27.9 us
  waiting for transfers between devices: 28 us -> 25.9 us
    ppermute x20 -> x21, starting transfers between devices: 21.1 us -> 25.5 us  [swap(): return lax.ppermute(value, axis, [(at, at ^ offset) for at in range(size)])]
    ppermute x20 -> x21, waiting for transfers between devices: 27.8 us -> 23.9 us  [swap(): return lax.ppermute(value, axis, [(at, at ^ offset) for at in range(size)])]
    ppermute x2, waiting for transfers between devices: 0.22 us -> 1.99 us  [swap_diagonal(): return lax.ppermute(value, ('frame', 'patch'), pairs)]
    pallas_call x10 -> x11, Pallas kernels: 11 us -> 11 us  [call(): pl.pallas_call(body, out_shape=outs, in_specs=[pl.BlockSpec(memory_space=...]
  transfers between devices with their start and end apart: 22 -> 23, of which waited for: 13 -> 13; matrix products, arithmetic and copies ran while one was open for 0% -> 0% of each run, Pallas kernels for 12% -> 14%
where the time goes in v10:
time: 68.5 us; the launch traced here: 68.3 us
  starting transfers between devices  27.9 us (41%)
  waiting for transfers between devices  25.9 us (38%)
  Pallas kernels  11 us (16%)
  local copies, waits for them, and re-layouts  3.34 us (5%)
    ppermute x21, starting transfers between devices, swap(): return lax.ppermute(value, axis, [(at, at ^ offset) for at in range(size)])  25.5 us
    ppermute x21, waiting for transfers between devices, swap(): return lax.ppermute(value, axis, [(at, at ^ offset) for at in range(size)])  23.9 us
    pallas_call x11, Pallas kernels, call(): pl.pallas_call(body, out_shape=outs, in_specs=[pl.BlockSpec(memory_space=...  11 us
    unnamed x18, local copies, waits for them, and re-layouts  3.34 us
    ppermute x2, starting transfers between devices, swap_diagonal(): return lax.ppermute(value, ('frame', 'patch'), pairs)  2.39 us
    ppermute x2, waiting for transfers between devices, swap_diagonal(): return lax.ppermute(value, ('frame', 'patch'), pairs)  1.99 us
  transfers between devices with their start and end apart: 23, of which 13 were waited for; matrix products, arithmetic and copies ran while one was open for 0% of the time, Pallas kernels for 14%

profile of v10, /device:TPU:0, one launch (start us, length us, event | category | flops | bytes accessed | tf_op | source)
XLA Modules:
  0.0 68.3 jit_solution(131294292071882754)
XLA Ops:
  0.5 2.5 %collective-permute-start.3 = (bf16[1,128,1152]{2,1,0:T(8,128)(2,1)}, bf16[1,128,1152]{2,1,0:T(8,128)(2,1)S(1)}, u32[]{:S(2)}, u32[]{:S(2)}) collective-permute-start(bf16[1,128,1152]{2,1,0:T(8,128)(2,1)} %own_ref.3), channel_id=1, source_target_pairs={{0,2},{1,3},{2,0},{3,1},{4,6},{5,7},{6,4},{7,5},{8,10},{9,11},{10,... | collective-permute-start | bytes 884744 | tf_op jit(solution)/shard_map/ppermute | solution.py:227
  3.0 1.0 %copy-done.4 = bf16[1,128,1152]{2,1,0:T(8,128)(2,1)S(1)} copy-done((bf16[1,128,1152]{2,1,0:T(8,128)(2,1)S(1)}, bf16[1,128,1152]{2,1,0:T(8,128)(2,1)}, u32[]{:S(2)}) %copy-start.4) | copy-done | bytes 294936
  4.0 1.8 %collective-permute-start.1 = (bf16[64,1152]{1,0:T(8,128)(2,1)S(1)}, bf16[64,1152]{1,0:T(8,128)(2,1)S(1)}, u32[]{:S(2)}, u32[]{:S(2)}) collective-permute-start(bf16[64,1152]{1,0:T(8,128)(2,1)S(1)} %shard_map.64), channel_id=1, source_target_pairs={{0,4},{4,0},{8,12},{12,8},{16,20},{20,16},{24,28},{28,24},{1,5},{5... | collective-permute-start | bytes 442376 | tf_op jit(solution)/shard_map/ppermute | solution.py:227
  5.8 1.6 %copy-done = bf16[864,1152]{1,0:T(8,128)(2,1)S(1)} copy-done((bf16[864,1152]{1,0:T(8,128)(2,1)S(1)}, bf16[864,1152]{1,0:T(8,128)(2,1)}, u32[]{:S(2)}) %copy-start) | copy-done | bytes 1990680
  7.4 0.8 %copy-done.7 = f32[6,1152]{1,0:T(8,128)S(1)} copy-done((f32[6,1152]{1,0:T(8,128)S(1)}, f32[6,1152]{1,0:T(8,128)}, u32[]{:S(2)}) %copy-start.7) | copy-done | bytes 27672
  8.1 1.1 %shard_map.65.near_ref = f32[864,256]{1,0:T(8,128)S(1)} custom-call(f32[6,1152]{1,0:T(8,128)S(1)} %copy-done.7, bf16[864,1152]{1,0:T(8,128)(2,1)S(1)} %copy-done, bf16[1,128,1152]{2,1,0:T(8,128)(2,1)S(1)} %copy-done.4, bf16[1,128,1152]{2,1,0:T(8,128)(2,1)S(1)} %collective-permute-done.sister_ref), custom_call_target="tpu_custom_call" | custom-call | flops 1 | bytes 1 | tf_op jit(solution)/shard_map/pallas_call | solution.py:214
  9.3 1.6 %collective-permute-done.3.refs_0_ = bf16[1,128,1152]{2,1,0:T(8,128)(2,1)S(1)} collective-permute-done((bf16[1,128,1152]{2,1,0:T(8,128)(2,1)}, bf16[1,128,1152]{2,1,0:T(8,128)(2,1)S(1)}, u32[]{:S(2)}, u32[]{:S(2)}) %collective-permute-start.3) | collective-permute-done | bytes 294944 | tf_op jit(solution)/shard_map/ppermute | solution.py:227
  10.9 1.6 %collective-permute-done.4.refs_1_ = bf16[1,128,1152]{2,1,0:T(8,128)(2,1)S(1)} collective-permute-done((bf16[1,128,1152]{2,1,0:T(8,128)(2,1)S(1)}, bf16[1,128,1152]{2,1,0:T(8,128)(2,1)S(1)}, u32[]{:S(2)}, u32[]{:S(2)}) %collective-permute-start.4) | collective-permute-done | bytes 294944 | tf_op jit(solution)/shard_map/ppermute | solution.py:227
  13.1 3.3 %shard_map.66 = (bf16[288,256]{1,0:T(8,128)(2,1)S(1)}, bf16[288,256]{1,0:T(8,128)(2,1)S(1)}) custom-call(f32[6,1152]{1,0:T(8,128)S(1)} %copy-done.7, bf16[864,1152]{1,0:T(8,128)(2,1)S(1)} %copy-done.1, f32[864,256]{1,0:T(8,128)S(1)} %shard_map.65.near_ref, bf16[1,128,1152]{2,1,0:T(8,128)(2,1)S(1)} %collective-permute-done.3.refs_0_, ...), custom_call_target="tpu_custom_call" | custom-call | flops 1 | bytes 1 | tf_op jit(solution)/shard_map/pallas_call | solution.py:214
  16.9 1.7 %collective-permute-done.5.refs_1_ = bf16[288,256]{1,0:T(8,128)(2,1)S(1)} collective-permute-done((bf16[288,256]{1,0:T(8,128)(2,1)S(1)}, bf16[288,256]{1,0:T(8,128)(2,1)S(1)}, u32[]{:S(2)}, u32[]{:S(2)}) %collective-permute-start.5) | collective-permute-done | bytes 147488 | tf_op jit(solution)/shard_map/ppermute | solution.py:227
  19.3 1.8 %collective-permute-start.6 = (bf16[64,1152]{1,0:T(8,128)(2,1)S(1)}, bf16[64,1152]{1,0:T(8,128)(2,1)S(1)}, u32[]{:S(2)}, u32[]{:S(2)}) collective-permute-start(bf16[64,1152]{1,0:T(8,128)(2,1)S(1)} %get-tuple-element.41), channel_id=1, source_target_pairs={{0,2},{1,3},{2,0},{3,1},{4,6},{5,7},{6,4},{7,5},{8,10},{9,11},{10,... | collective-permute-start | bytes 442376 | tf_op jit(solution)/shard_map/ppermute | solution.py:227
  21.1 1.4 %collective-permute-start.8 = (bf16[64,1152]{1,0:T(8,128)(2,1)S(1)}, bf16[64,1152]{1,0:T(8,128)(2,1)S(1)}, u32[]{:S(2)}, u32[]{:S(2)}) collective-permute-start(bf16[64,1152]{1,0:T(8,128)(2,1)S(1)} %get-tuple-element.43), channel_id=1, source_target_pairs={{0,6},{1,7},{2,4},{3,5},{4,2},{5,3},{6,0},{7,1},{8,14},{9,15},{10,... | collective-permute-start | bytes 442376 | tf_op jit(solution)/shard_map/ppermute | solution.py:250
  22.8 5.5 %collective-permute-done.7.refs_4_ = bf16[64,576]{1,0:T(8,128)(2,1)S(1)} collective-permute-done((bf16[64,576]{1,0:T(8,128)(2,1)S(1)}, bf16[64,576]{1,0:T(8,128)(2,1)S(1)}, u32[]{:S(2)}, u32[]{:S(2)}) %collective-permute-start.7) | collective-permute-done | bytes 73760 | tf_op jit(solution)/shard_map/ppermute | solution.py:227
  29.2 3.8 %collective-permute-start.15 = (bf16[32,1152]{1,0:T(8,128)(2,1)S(1)}, bf16[32,1152]{1,0:T(8,128)(2,1)S(1)}, u32[]{:S(2)}, u32[]{:S(2)}) collective-permute-start(bf16[32,1152]{1,0:T(8,128)(2,1)S(1)} %get-tuple-element.51), channel_id=1, source_target_pairs={{0,24},{4,28},{8,16},{12,20},{16,8},{20,12},{24,0},{28,4},{1,25},{... | collective-permute-start | bytes 221192 | tf_op jit(solution)/shard_map/ppermute | solution.py:227
  33.7 2.1 %collective-permute-done.15.refs_0_ = bf16[32,1152]{1,0:T(8,128)(2,1)S(1)} collective-permute-done((bf16[32,1152]{1,0:T(8,128)(2,1)S(1)}, bf16[32,1152]{1,0:T(8,128)(2,1)S(1)}, u32[]{:S(2)}, u32[]{:S(2)}) %collective-permute-start.15) | collective-permute-done | bytes 73760 | tf_op jit(solution)/shard_map/ppermute | solution.py:227
  35.8 2.0 %collective-permute-start.16 = (bf16[64,1152]{1,0:T(8,128)(2,1)S(1)}, bf16[64,1152]{1,0:T(8,128)(2,1)S(1)}, u32[]{:S(2)}, u32[]{:S(2)}) collective-permute-start(bf16[64,1152]{1,0:T(8,128)(2,1)S(1)} %shard_map.70.refs_4_), channel_id=1, source_target_pairs={{0,2},{1,3},{2,0},{3,1},{4,6},{5,7},{6,4},{7,5},{8,10},{9,11},{10,... | collective-permute-start | bytes 442376 | tf_op jit(solution)/shard_map/ppermute | solution.py:227
  37.8 0.9 %collective-permute-done.9.refs_0_ = bf16[32,1152]{1,0:T(8,128)(2,1)S(1)} collective-permute-done((bf16[32,1152]{1,0:T(8,128)(2,1)S(1)}, bf16[32,1152]{1,0:T(8,128)(2,1)S(1)}, u32[]{:S(2)}, u32[]{:S(2)}) %collective-permute-start.9) | collective-permute-done | bytes 73760 | tf_op jit(solution)/shard_map/ppermute | solution.py:227
  38.7 1.7 %collective-permute-start.11 = (bf16[64,1152]{1,0:T(8,128)(2,1)S(1)}, bf16[64,1152]{1,0:T(8,128)(2,1)S(1)}, u32[]{:S(2)}, u32[]{:S(2)}) collective-permute-start(bf16[64,1152]{1,0:T(8,128)(2,1)S(1)} %shard_map.69.refs_5_), channel_id=1, source_target_pairs={{0,2},{1,3},{2,0},{3,1},{4,6},{5,7},{6,4},{7,5},{8,10},{9,11},{10,... | collective-permute-start | bytes 442376 | tf_op jit(solution)/shard_map/ppermute | solution.py:227
  41.1 1.9 %shard_map.71 = (f32[64,1152]{1,0:T(8,128)S(1)}, bf16[64,576]{1,0:T(8,128)(2,1)S(1)}) custom-call(bf16[864,1152]{1,0:T(8,128)(2,1)S(1)} %copy-done.2, bf16[864,1152]{1,0:T(8,128)(2,1)S(1)} %collective-permute-done.14.refs_1_, bf16[288,1152]{1,0:T(8,128)(2,1)S(1)} %copy-done.3, bf16[288,1152]{1,0:T(8,128)(2,1)S(1)} %collective-permute-done.13.refs_3_.refs_1_, ...), custom_call_target="tpu_custom_call" | custom-call | flops 1 | bytes 1 | tf_op jit(solution)/shard_map/pallas_call | solution.py:214
  43.0 1.6 %collective-permute-start.17 = (bf16[64,576]{1,0:T(8,128)(2,1)S(1)}, bf16[64,576]{1,0:T(8,128)(2,1)S(1)}, u32[]{:S(2)}, u32[]{:S(2)}) collective-permute-start(bf16[64,576]{1,0:T(8,128)(2,1)S(1)} %get-tuple-element.56), channel_id=1, source_target_pairs={{0,4},{4,0},{8,12},{12,8},{16,20},{20,16},{24,28},{28,24},{1,5},{5... | collective-permute-start | bytes 221192 | tf_op jit(solution)/shard_map/ppermute | solution.py:227
  44.6 1.0 %collective-permute-start.12 = (bf16[4,16,1152]{2,1,0:T(8,128)(2,1)S(1)}, bf16[4,16,1152]{2,1,0:T(8,128)(2,1)S(1)}, u32[]{:S(2)}, u32[]{:S(2)}) collective-permute-start(bf16[4,16,1152]{2,1,0:T(8,128)(2,1)S(1)} %get-tuple-element.48), channel_id=1, source_target_pairs={{0,4},{4,0},{8,12},{12,8},{16,20},{20,16},{24,28},{28,24},{1,5},{5... | collective-permute-start | bytes 442376 | tf_op jit(solution)/shard_map/ppermute | solution.py:227
  45.7 2.2 %collective-permute-done.17.refs_4_ = bf16[64,576]{1,0:T(8,128)(2,1)S(1)} collective-permute-done((bf16[64,576]{1,0:T(8,128)(2,1)S(1)}, bf16[64,576]{1,0:T(8,128)(2,1)S(1)}, u32[]{:S(2)}, u32[]{:S(2)}) %collective-permute-start.17) | collective-permute-done | bytes 73760 | tf_op jit(solution)/shard_map/ppermute | solution.py:227
  47.9 2.0 %shard_map.72 = (bf16[64,1152]{1,0:T(8,128)(2,1)S(1)}, bf16[64,1152]{1,0:T(8,128)(2,1)S(1)}) custom-call(bf16[864,1152]{1,0:T(8,128)(2,1)S(1)} %copy-done.2, bf16[864,1152]{1,0:T(8,128)(2,1)S(1)} %collective-permute-done.14.refs_1_, bf16[288,1152]{1,0:T(8,128)(2,1)S(1)} %copy-done.3, bf16[288,1152]{1,0:T(8,128)(2,1)S(1)} %collective-permute-done.13.refs_3_.refs_1_, ...), custom_call_target="tpu_custom_call" | custom-call | flops 1 | bytes 1 | tf_op jit(solution)/shard_map/pallas_call | solution.py:214
  49.9 2.3 %collective-permute-start.18 = (bf16[64,1152]{1,0:T(8,128)(2,1)S(1)}, bf16[64,1152]{1,0:T(8,128)(2,1)S(1)}, u32[]{:S(2)}, u32[]{:S(2)}) collective-permute-start(bf16[64,1152]{1,0:T(8,128)(2,1)S(1)} %get-tuple-element.59), channel_id=1, source_target_pairs={{0,2},{1,3},{2,0},{3,1},{4,6},{5,7},{6,4},{7,5},{8,10},{9,11},{10,... | collective-permute-start | bytes 442376 | tf_op jit(solution)/shard_map/ppermute | solution.py:227
  52.2 1.0 %collective-permute-start.19 = (bf16[64,1152]{1,0:T(8,128)(2,1)S(1)}, bf16[64,1152]{1,0:T(8,128)(2,1)S(1)}, u32[]{:S(2)}, u32[]{:S(2)}) collective-permute-start(bf16[64,1152]{1,0:T(8,128)(2,1)S(1)} %get-tuple-element.60), channel_id=1, source_target_pairs={{0,6},{1,7},{2,4},{3,5},{4,2},{5,3},{6,0},{7,1},{8,14},{9,15},{10,... | collective-permute-start | bytes 442376 | tf_op jit(solution)/shard_map/ppermute | solution.py:250
  53.2 3.3 %collective-permute-done.18.refs_3_ = bf16[64,1152]{1,0:T(8,128)(2,1)S(1)} collective-permute-done((bf16[64,1152]{1,0:T(8,128)(2,1)S(1)}, bf16[64,1152]{1,0:T(8,128)(2,1)S(1)}, u32[]{:S(2)}, u32[]{:S(2)}) %collective-permute-start.18) | collective-permute-done | bytes 147488 | tf_op jit(solution)/shard_map/ppermute | solution.py:227
  56.5 1.8 %collective-permute-done.19.refs_5_ = bf16[64,1152]{1,0:T(8,128)(2,1)S(1)} collective-permute-done((bf16[64,1152]{1,0:T(8,128)(2,1)S(1)}, bf16[64,1152]{1,0:T(8,128)(2,1)S(1)}, u32[]{:S(2)}, u32[]{:S(2)}) %collective-permute-start.19) | collective-permute-done | bytes 147488 | tf_op jit(solution)/shard_map/ppermute | solution.py:250
  58.7 3.1 %collective-permute-start.20 = (bf16[32,1152]{1,0:T(8,128)(2,1)S(1)}, bf16[32,1152]{1,0:T(8,128)(2,1)S(1)}, u32[]{:S(2)}, u32[]{:S(2)}) collective-permute-start(bf16[32,1152]{1,0:T(8,128)(2,1)S(1)} %get-tuple-element.61), channel_id=1, source_target_pairs={{0,24},{4,28},{8,16},{12,20},{16,8},{20,12},{24,0},{28,4},{1,25},{... | collective-permute-start | bytes 221192 | tf_op jit(solution)/shard_map/ppermute | solution.py:227
  61.8 1.4 %collective-permute-start.22 = (bf16[32,1152]{1,0:T(8,128)(2,1)S(1)}, bf16[32,1152]{1,0:T(8,128)(2,1)S(1)}, u32[]{:S(2)}, u32[]{:S(2)}) collective-permute-start(bf16[32,1152]{1,0:T(8,128)(2,1)S(1)} %get-tuple-element.64), channel_id=1, source_target_pairs={{0,8},{4,12},{8,0},{12,4},{16,24},{20,28},{24,16},{28,20},{1,9},{5... | collective-permute-start | bytes 221192 | tf_op jit(solution)/shard_map/ppermute | solution.py:227
  63.1 1.8 %collective-permute-done.20.refs_0_ = bf16[32,1152]{1,0:T(8,128)(2,1)S(1)} collective-permute-done((bf16[32,1152]{1,0:T(8,128)(2,1)S(1)}, bf16[32,1152]{1,0:T(8,128)(2,1)S(1)}, u32[]{:S(2)}, u32[]{:S(2)}) %collective-permute-start.20) | collective-permute-done | bytes 73760 | tf_op jit(solution)/shard_map/ppermute | solution.py:227
  64.9 2.5 %collective-permute-done.21.refs_2_ = bf16[32,1152]{1,0:T(8,128)(2,1)S(1)} collective-permute-done((bf16[32,1152]{1,0:T(8,128)(2,1)S(1)}, bf16[32,1152]{1,0:T(8,128)(2,1)S(1)}, u32[]{:S(2)}, u32[]{:S(2)}) %collective-permute-start.21) | collective-permute-done | bytes 73760 | tf_op jit(solution)/shard_map/ppermute | solution.py:227
  67.4 0.8 %shard_map.74 = bf16[8,16,1152]{2,1,0:T(8,128)(2,1)} custom-call(f32[6,1152]{1,0:T(8,128)S(1)} %copy-done.8, bf16[4,16,1152]{2,1,0:T(8,128)(2,1)S(1)} %get-tuple-element.44.kept_ref, bf16[4,16,1152]{2,1,0:T(8,128)(2,1)S(1)} %collective-permute-done.12.other_ref, bf16[32,1152]{1,0:T(8,128)(2,1)S(1)} %collective-permute-done.20.refs_0_, ...), custom_call_target="tpu_custom_call" | custom-call | flops 1 | bytes 1 | tf_op jit(solution)/shard_map/pallas_call | solution.py:214
  (43 shorter events, 5.4 us)
Async XLA Ops:
  0.0 3.0 %collective-permute-start = (bf16[1,128,1152]{2,1,0:T(8,128)(2,1)}, bf16[1,128,1152]{2,1,0:T(8,128)(2,1)S(1)}, u32[]{:S(2)}, u32[]{:S(2)}) collective-permute-start(bf16[1,128,1152]{2,1,0:T(8,128)(2,1)} %own_ref.3), channel_id=1, source_target_pairs={{0,1},{1,0},{2,3},{3,2},{4,5},{5,4},{6,7},{7,6},{8,9},{9,8},{10,11... | collective-permute-start | bytes 884744 | tf_op jit(solution)/shard_map/ppermute | solution.py:227
  0.5 10.4 %collective-permute-start.3 = (bf16[1,128,1152]{2,1,0:T(8,128)(2,1)}, bf16[1,128,1152]{2,1,0:T(8,128)(2,1)S(1)}, u32[]{:S(2)}, u32[]{:S(2)}) collective-permute-start(bf16[1,128,1152]{2,1,0:T(8,128)(2,1)} %own_ref.3), channel_id=1, source_target_pairs={{0,2},{1,3},{2,0},{3,1},{4,6},{5,7},{6,4},{7,5},{8,10},{9,11},{10,... | collective-permute-start | bytes 884744 | tf_op jit(solution)/shard_map/ppermute | solution.py:227
  3.0 1.0 %copy-start.4 = (bf16[1,128,1152]{2,1,0:T(8,128)(2,1)S(1)}, bf16[1,128,1152]{2,1,0:T(8,128)(2,1)}, u32[]{:S(2)}) copy-start(bf16[1,128,1152]{2,1,0:T(8,128)(2,1)} %own_ref.3) | copy-start | bytes 884740
  4.0 6.8 %collective-permute-start.1 = (bf16[64,1152]{1,0:T(8,128)(2,1)S(1)}, bf16[64,1152]{1,0:T(8,128)(2,1)S(1)}, u32[]{:S(2)}, u32[]{:S(2)}) collective-permute-start(bf16[64,1152]{1,0:T(8,128)(2,1)S(1)} %shard_map.64), channel_id=1, source_target_pairs={{0,4},{4,0},{8,12},{12,8},{16,20},{20,16},{24,28},{28,24},{1,5},{5... | collective-permute-start | bytes 442376 | tf_op jit(solution)/shard_map/ppermute | solution.py:227
  5.8 1.6 %copy-start = (bf16[864,1152]{1,0:T(8,128)(2,1)S(1)}, bf16[864,1152]{1,0:T(8,128)(2,1)}, u32[]{:S(2)}) copy-start(bf16[864,1152]{1,0:T(8,128)(2,1)} %weight_ref.3) | copy-start | bytes 5971972
  7.4 0.8 %copy-start.7 = (f32[6,1152]{1,0:T(8,128)S(1)}, f32[6,1152]{1,0:T(8,128)}, u32[]{:S(2)}) copy-start(f32[6,1152]{1,0:T(8,128)} %mod_ref.7) | copy-start | bytes 82948
  8.1 4.4 %copy-start.6 = (bf16[288,1152]{1,0:T(8,128)(2,1)S(1)}, bf16[288,1152]{1,0:T(8,128)(2,1)}, u32[]{:S(2)}) copy-start(bf16[288,1152]{1,0:T(8,128)(2,1)} %refs_0_.4) | copy-start | bytes 1990660
  8.1 4.8 %copy-start.3 = (bf16[288,1152]{1,0:T(8,128)(2,1)S(1)}, bf16[288,1152]{1,0:T(8,128)(2,1)}, u32[]{:S(2)}) copy-start(bf16[288,1152]{1,0:T(8,128)(2,1)} %refs_0_.7) | copy-start | bytes 1990660
  8.1 5.0 %copy-start.1 = (bf16[864,1152]{1,0:T(8,128)(2,1)S(1)}, bf16[864,1152]{1,0:T(8,128)(2,1)}, u32[]{:S(2)}) copy-start(bf16[864,1152]{1,0:T(8,128)(2,1)} %weight_ref.3) | copy-start | bytes 5971972
  9.2 19.3 %copy-start.5 = (bf16[1,128,1152]{2,1,0:T(8,128)(2,1)S(1)}, bf16[1,128,1152]{2,1,0:T(8,128)(2,1)}, u32[]{:S(2)}) copy-start(bf16[1,128,1152]{2,1,0:T(8,128)(2,1)} %own_ref.3) | copy-start | bytes 884740
  10.9 1.6 %collective-permute-start.4 = (bf16[1,128,1152]{2,1,0:T(8,128)(2,1)S(1)}, bf16[1,128,1152]{2,1,0:T(8,128)(2,1)S(1)}, u32[]{:S(2)}, u32[]{:S(2)}) collective-permute-start(bf16[1,128,1152]{2,1,0:T(8,128)(2,1)S(1)} %collective-permute-done.3.refs_0_), channel_id=1, source_target_pairs={{0,1},{1,0},{2,3},{3,2},{4,5},{5,4},{6,7},{7,6},{8,9},{9,8},{10,11... | collective-permute-start | bytes 884744 | tf_op jit(solution)/shard_map/ppermute | solution.py:227
  12.4 28.7 %collective-permute-start.14 = (bf16[864,1152]{1,0:T(8,128)(2,1)}, bf16[864,1152]{1,0:T(8,128)(2,1)S(1)}, u32[]{:S(2)}, u32[]{:S(2)}) collective-permute-start(bf16[864,1152]{1,0:T(8,128)(2,1)} %refs_0_.6), channel_id=1, source_target_pairs={{0,1},{1,0},{2,3},{3,2},{4,5},{5,4},{6,7},{7,6},{8,9},{9,8},{10,11... | collective-permute-start | bytes 5971976 | tf_op jit(solution)/shard_map/ppermute | solution.py:227
  12.6 6.0 %collective-permute-start.2 = (bf16[288,1152]{1,0:T(8,128)(2,1)S(1)}, bf16[288,1152]{1,0:T(8,128)(2,1)S(1)}, u32[]{:S(2)}, u32[]{:S(2)}) collective-permute-start(bf16[288,1152]{1,0:T(8,128)(2,1)S(1)} %copy-done.6), channel_id=1, source_target_pairs={{0,1},{1,0},{2,3},{3,2},{4,5},{5,4},{6,7},{7,6},{8,9},{9,8},{10,11... | collective-permute-start | bytes 1990664 | tf_op jit(solution)/shard_map/ppermute | solution.py:227
  13.0 28.1 %collective-permute-start.13 = (bf16[288,1152]{1,0:T(8,128)(2,1)S(1)}, bf16[288,1152]{1,0:T(8,128)(2,1)S(1)}, u32[]{:S(2)}, u32[]{:S(2)}) collective-permute-start(bf16[288,1152]{1,0:T(8,128)(2,1)S(1)} %copy-done.3), channel_id=1, source_target_pairs={{0,1},{1,0},{2,3},{3,2},{4,5},{5,4},{6,7},{7,6},{8,9},{9,8},{10,11... | collective-permute-start | bytes 1990664 | tf_op jit(solution)/shard_map/ppermute | solution.py:227
  16.4 2.1 %collective-permute-start.5 = (bf16[288,256]{1,0:T(8,128)(2,1)S(1)}, bf16[288,256]{1,0:T(8,128)(2,1)S(1)}, u32[]{:S(2)}, u32[]{:S(2)}) collective-permute-start(bf16[288,256]{1,0:T(8,128)(2,1)S(1)} %get-tuple-element.39), channel_id=1, source_target_pairs={{0,1},{1,0},{2,3},{3,2},{4,5},{5,4},{6,7},{7,6},{8,9},{9,8},{10,11... | collective-permute-start | bytes 442376 | tf_op jit(solution)/shard_map/ppermute | solution.py:227
  18.6 22.5 %copy-start.2 = (bf16[864,1152]{1,0:T(8,128)(2,1)S(1)}, bf16[864,1152]{1,0:T(8,128)(2,1)}, u32[]{:S(2)}) copy-start(bf16[864,1152]{1,0:T(8,128)(2,1)} %refs_0_.6) | copy-start | bytes 5971972
  19.3 9.0 %collective-permute-start.6 = (bf16[64,1152]{1,0:T(8,128)(2,1)S(1)}, bf16[64,1152]{1,0:T(8,128)(2,1)S(1)}, u32[]{:S(2)}, u32[]{:S(2)}) collective-permute-start(bf16[64,1152]{1,0:T(8,128)(2,1)S(1)} %get-tuple-element.41), channel_id=1, source_target_pairs={{0,2},{1,3},{2,0},{3,1},{4,6},{5,7},{6,4},{7,5},{8,10},{9,11},{10,... | collective-permute-start | bytes 442376 | tf_op jit(solution)/shard_map/ppermute | solution.py:227
  21.1 7.4 %collective-permute-start.8 = (bf16[64,1152]{1,0:T(8,128)(2,1)S(1)}, bf16[64,1152]{1,0:T(8,128)(2,1)S(1)}, u32[]{:S(2)}, u32[]{:S(2)}) collective-permute-start(bf16[64,1152]{1,0:T(8,128)(2,1)S(1)} %get-tuple-element.43), channel_id=1, source_target_pairs={{0,6},{1,7},{2,4},{3,5},{4,2},{5,3},{6,0},{7,1},{8,14},{9,15},{10,... | collective-permute-start | bytes 442376 | tf_op jit(solution)/shard_map/ppermute | solution.py:250
  22.5 5.8 %collective-permute-start.7 = (bf16[64,576]{1,0:T(8,128)(2,1)S(1)}, bf16[64,576]{1,0:T(8,128)(2,1)S(1)}, u32[]{:S(2)}, u32[]{:S(2)}) collective-permute-start(bf16[64,576]{1,0:T(8,128)(2,1)S(1)} %get-tuple-element.42), channel_id=1, source_target_pairs={{0,4},{4,0},{8,12},{12,8},{16,20},{20,16},{24,28},{28,24},{1,5},{5... | collective-permute-start | bytes 221192 | tf_op jit(solution)/shard_map/ppermute | solution.py:227
  29.2 6.5 %collective-permute-start.15 = (bf16[32,1152]{1,0:T(8,128)(2,1)S(1)}, bf16[32,1152]{1,0:T(8,128)(2,1)S(1)}, u32[]{:S(2)}, u32[]{:S(2)}) collective-permute-start(bf16[32,1152]{1,0:T(8,128)(2,1)S(1)} %get-tuple-element.51), channel_id=1, source_target_pairs={{0,24},{4,28},{8,16},{12,20},{16,8},{20,12},{24,0},{28,4},{1,25},{... | collective-permute-start | bytes 221192 | tf_op jit(solution)/shard_map/ppermute | solution.py:227
  33.0 5.7 %collective-permute-start.9 = (bf16[32,1152]{1,0:T(8,128)(2,1)S(1)}, bf16[32,1152]{1,0:T(8,128)(2,1)S(1)}, u32[]{:S(2)}, u32[]{:S(2)}) collective-permute-start(bf16[32,1152]{1,0:T(8,128)(2,1)S(1)} %get-tuple-element.46), channel_id=1, source_target_pairs={{0,16},{4,20},{8,24},{12,28},{16,0},{20,4},{24,8},{28,12},{1,17},{... | collective-permute-start | bytes 221192 | tf_op jit(solution)/shard_map/ppermute | solution.py:227
  33.0 5.7 %collective-permute-start.10 = (bf16[32,1152]{1,0:T(8,128)(2,1)S(1)}, bf16[32,1152]{1,0:T(8,128)(2,1)S(1)}, u32[]{:S(2)}, u32[]{:S(2)}) collective-permute-start(bf16[32,1152]{1,0:T(8,128)(2,1)S(1)} %get-tuple-element.47), channel_id=1, source_target_pairs={{0,8},{4,12},{8,0},{12,4},{16,24},{20,28},{24,16},{28,20},{1,9},{5... | collective-permute-start | bytes 221192 | tf_op jit(solution)/shard_map/ppermute | solution.py:227
  35.8 5.3 %collective-permute-start.16 = (bf16[64,1152]{1,0:T(8,128)(2,1)S(1)}, bf16[64,1152]{1,0:T(8,128)(2,1)S(1)}, u32[]{:S(2)}, u32[]{:S(2)}) collective-permute-start(bf16[64,1152]{1,0:T(8,128)(2,1)S(1)} %shard_map.70.refs_4_), channel_id=1, source_target_pairs={{0,2},{1,3},{2,0},{3,1},{4,6},{5,7},{6,4},{7,5},{8,10},{9,11},{10,... | collective-permute-start | bytes 442376 | tf_op jit(solution)/shard_map/ppermute | solution.py:227
  38.7 5.9 %collective-permute-start.11 = (bf16[64,1152]{1,0:T(8,128)(2,1)S(1)}, bf16[64,1152]{1,0:T(8,128)(2,1)S(1)}, u32[]{:S(2)}, u32[]{:S(2)}) collective-permute-start(bf16[64,1152]{1,0:T(8,128)(2,1)S(1)} %shard_map.69.refs_5_), channel_id=1, source_target_pairs={{0,2},{1,3},{2,0},{3,1},{4,6},{5,7},{6,4},{7,5},{8,10},{9,11},{10,... | collective-permute-start | bytes 442376 | tf_op jit(solution)/shard_map/ppermute | solution.py:227
  43.0 4.8 %collective-permute-start.17 = (bf16[64,576]{1,0:T(8,128)(2,1)S(1)}, bf16[64,576]{1,0:T(8,128)(2,1)S(1)}, u32[]{:S(2)}, u32[]{:S(2)}) collective-permute-start(bf16[64,576]{1,0:T(8,128)(2,1)S(1)} %get-tuple-element.56), channel_id=1, source_target_pairs={{0,4},{4,0},{8,12},{12,8},{16,20},{20,16},{24,28},{28,24},{1,5},{5... | collective-permute-start | bytes 221192 | tf_op jit(solution)/shard_map/ppermute | solution.py:227
  44.6 8.6 %collective-permute-start.12 = (bf16[4,16,1152]{2,1,0:T(8,128)(2,1)S(1)}, bf16[4,16,1152]{2,1,0:T(8,128)(2,1)S(1)}, u32[]{:S(2)}, u32[]{:S(2)}) collective-permute-start(bf16[4,16,1152]{2,1,0:T(8,128)(2,1)S(1)} %get-tuple-element.48), channel_id=1, source_target_pairs={{0,4},{4,0},{8,12},{12,8},{16,20},{20,16},{24,28},{28,24},{1,5},{5... | collective-permute-start | bytes 442376 | tf_op jit(solution)/shard_map/ppermute | solution.py:227
  49.9 17.6 %copy-start.8 = (f32[6,1152]{1,0:T(8,128)S(1)}, f32[6,1152]{1,0:T(8,128)}, u32[]{:S(2)}) copy-start(f32[6,1152]{1,0:T(8,128)} %mod_ref.7) | copy-start | bytes 82948
  49.9 6.6 %collective-permute-start.18 = (bf16[64,1152]{1,0:T(8,128)(2,1)S(1)}, bf16[64,1152]{1,0:T(8,128)(2,1)S(1)}, u32[]{:S(2)}, u32[]{:S(2)}) collective-permute-start(bf16[64,1152]{1,0:T(8,128)(2,1)S(1)} %get-tuple-element.59), channel_id=1, source_target_pairs={{0,2},{1,3},{2,0},{3,1},{4,6},{5,7},{6,4},{7,5},{8,10},{9,11},{10,... | collective-permute-start | bytes 442376 | tf_op jit(solution)/shard_map/ppermute | solution.py:227
  52.2 6.0 %collective-permute-start.19 = (bf16[64,1152]{1,0:T(8,128)(2,1)S(1)}, bf16[64,1152]{1,0:T(8,128)(2,1)S(1)}, u32[]{:S(2)}, u32[]{:S(2)}) collective-permute-start(bf16[64,1152]{1,0:T(8,128)(2,1)S(1)} %get-tuple-element.60), channel_id=1, source_target_pairs={{0,6},{1,7},{2,4},{3,5},{4,2},{5,3},{6,0},{7,1},{8,14},{9,15},{10,... | collective-permute-start | bytes 442376 | tf_op jit(solution)/shard_map/ppermute | solution.py:250
  58.7 6.2 %collective-permute-start.20 = (bf16[32,1152]{1,0:T(8,128)(2,1)S(1)}, bf16[32,1152]{1,0:T(8,128)(2,1)S(1)}, u32[]{:S(2)}, u32[]{:S(2)}) collective-permute-start(bf16[32,1152]{1,0:T(8,128)(2,1)S(1)} %get-tuple-element.61), channel_id=1, source_target_pairs={{0,24},{4,28},{8,16},{12,20},{16,8},{20,12},{24,0},{28,4},{1,25},{... | collective-permute-start | bytes 221192 | tf_op jit(solution)/shard_map/ppermute | solution.py:227
  61.8 5.7 %collective-permute-start.21 = (bf16[32,1152]{1,0:T(8,128)(2,1)S(1)}, bf16[32,1152]{1,0:T(8,128)(2,1)S(1)}, u32[]{:S(2)}, u32[]{:S(2)}) collective-permute-start(bf16[32,1152]{1,0:T(8,128)(2,1)S(1)} %get-tuple-element.63), channel_id=1, source_target_pairs={{0,16},{4,20},{8,24},{12,28},{16,0},{20,4},{24,8},{28,12},{1,17},{... | collective-permute-start | bytes 221192 | tf_op jit(solution)/shard_map/ppermute | solution.py:227
  61.8 5.7 %collective-permute-start.22 = (bf16[32,1152]{1,0:T(8,128)(2,1)S(1)}, bf16[32,1152]{1,0:T(8,128)(2,1)S(1)}, u32[]{:S(2)}, u32[]{:S(2)}) collective-permute-start(bf16[32,1152]{1,0:T(8,128)(2,1)S(1)} %get-tuple-element.64), channel_id=1, source_target_pairs={{0,8},{4,12},{8,0},{12,4},{16,24},{20,28},{24,16},{28,20},{1,9},{5... | collective-permute-start | bytes 221192 | tf_op jit(solution)/shard_map/ppermute | solution.py:227

commit v11 on v9

--- a/solution.py
+++ b/solution.py
@@ -125,7 +125,7 @@
 
 
 def middle_kernel(pieces, groups, mod_ref, own_ref, paired_ref, *refs):
-    kept_ref, sent_ref, *piece_refs, scratch = refs[2 + 2 * groups :]
+    kept_ref, sent_ref, normed_ref = refs[2 + 2 * groups :]
     updates = total_updates(groups, refs[:2], refs[2:])
     _, period, width = kept_ref.shape
     inputs = (of_this_half(own_ref[0], period)[0], paired_ref[...])
@@ -136,16 +136,7 @@
         for piece in range(pieces):
             rows = slice(piece * period, (piece + 1) * period)
             middle_ref[piece] = middle[rows]
-            scratch[piece, at * period : (at + 1) * period, :] = normed[rows]
-    here = lax.axis_index("frame") // 2
-    for at, ref in enumerate(piece_refs):
-        ref[...] = scratch[here ^ (pieces - 1 - at)]
-
-
-def join_kernel(*refs):
-    size = refs[0].shape[0]
-    for at, ref in enumerate(refs[:-1]):
-        refs[-1][at * size : (at + 1) * size, :] = ref[...]
+            normed_ref[piece, at * period : (at + 1) * period, :] = normed[rows]
 
 
 def temporal_kernel(own, period, block, *refs):
@@ -187,27 +178,23 @@
 
 
 def sum_kernel(groups, *refs):
-    piece_refs = refs[2 + 2 * groups :]
-    period = piece_refs[0].shape[0] // 2
+    out_ref = refs[-1]
+    pieces, period = out_ref.shape[0], out_ref.shape[1] // 2
     for at, update in enumerate(total_updates(groups, refs[:2], refs[2:])):
         update = update.astype(BF16)
-        for piece, ref in enumerate(piece_refs):
+        for piece in range(pieces):
             rows = update[piece * period : (piece + 1) * period]
-            ref[at * period : (at + 1) * period, :] = rows
-
-
-def result_kernel(pieces, mod_ref, kept_ref, other_ref, *refs):
-    piece_refs, out_ref = refs[:-1], refs[-1]
-    period = kept_ref.shape[1]
-    here = lax.axis_index("frame")
-    for at, ref in enumerate(piece_refs):
-        there = here // 2 ^ (pieces - 1 - at)
+            out_ref[piece, at * period : (at + 1) * period, :] = rows
+
+
+def result_kernel(mod_ref, kept_ref, other_ref, update_ref, out_ref):
+    pieces, period, _ = kept_ref.shape
+    here = lax.axis_index("frame") % 2
+    for piece in range(pieces):
         for half, middle_ref in enumerate((kept_ref, other_ref)):
-            update = ref[half * period : (half + 1) * period, :].astype(F32)
-            middle = middle_ref[there].astype(F32)
-            out_ref[2 * there + (here % 2 ^ half)] = (middle + mod_ref[5:6, :] * update).astype(
-                BF16
-            )
+            update = update_ref[piece, half * period : (half + 1) * period, :].astype(F32)
+            middle = middle_ref[piece].astype(F32) + mod_ref[5:6, :] * update
+            out_ref[2 * piece + (here ^ half)] = middle.astype(BF16)
 
 
 def call(body, operands, outs, scratch=(), limit=24):
@@ -261,9 +248,11 @@
     def with_sister(weights, *others):
         return [weights, swap(after(weights, *others), "patch", 1)]
 
-    def exchange_frames(parts):
-        offsets = reversed(range(pieces))
-        return [swap(part, "frame", 2 * at) if at else part for at, part in zip(offsets, parts)]
+    def exchange_frames(blocks):
+        lines = [list(range(first, frames, 2)) for first in range(2)]
+        return lax.all_to_all(
+            blocks, "frame", split_axis=0, concat_axis=0, tiled=True, axis_index_groups=lines
+        )
 
     def return_updates(own, far):
         same = [swap(part, "patch", 2 * at) for at, part in enumerate(far[::2], 1)]
@@ -275,7 +264,7 @@
 
     own_shapes = [halves_shape(F32), shape((rows // 2, 2 * shard), BF16)]
     far_shapes = [halves_shape(BF16)] * (2 * groups - 2)
-    piece_shapes = [shape((2 * period, width), BF16)] * pieces
+    blocks_shape = shape((pieces, 2 * period, width), BF16)
 
     sister = swap(tokens, "patch", 1)
     far = across(tokens)[1:]
@@ -305,14 +294,12 @@
         own_shapes + far_shapes,
     )
     updates = return_updates((parts[0], swap(parts[1], "frame", 1)), parts[2:])
-    middle, middle_sent, *parts = call(
+    middle, middle_sent, normed = call(
         functools.partial(middle_kernel, pieces, groups),
         (modulation, tokens, paired, *out_pair, *updates),
-        [shape((pieces, period, width), BF16)] * 2 + piece_shapes,
-        [pltpu.VMEM((pieces, 2 * period, width), BF16)],
-    )
-    arrived = exchange_frames(parts)
-    (segment,) = call(join_kernel, arrived, [shape((rows, width), BF16)])
+        [shape((pieces, period, width), BF16)] * 2 + [blocks_shape],
+    )
+    segment = exchange_frames(normed).reshape(rows, width)
     segments = across(segment)
 
     def attend_frames(own, segments, shapes):
@@ -330,14 +317,14 @@
     others = [after(block, received, middle_other) for block in segments[1:]]
     far_parts = attend_frames(False, others, far_shapes)
     updates = return_updates((kept, received), far_parts)
-    parts = call(
+    (update,) = call(
         functools.partial(sum_kernel, groups),
         (*late_pair, *updates),
-        piece_shapes,
+        [blocks_shape],
     )
     (result,) = call(
-        functools.partial(result_kernel, pieces),
-        (modulation, middle, middle_other, *exchange_frames(parts)),
+        result_kernel,
+        (modulation, middle, middle_other, exchange_frames(update)),
         [shape((frames, period, width), BF16)],
     )
     return result.reshape(1, rows, width)

time: 66.8 us -> 72.6 us (1.087)
  blocking collectives: 0 us -> 24.1 us
  waiting for transfers between devices: 28 us -> 18.7 us
  starting transfers between devices: 24.1 us -> 15.2 us
    all_to_all x0 -> x2, blocking collectives: none -> 24.1 us  [exchange_frames(): lax.all_to_all(blocks, 'frame', split_axis=0, concat_axis=0, tiled=True,...]
    ppermute x20 -> x14, starting transfers between devices: 21.1 us -> 11.8 us  [swap(): return lax.ppermute(value, axis, [(at, at ^ offset) for at in range(size)])]
    ppermute x20 -> x14, waiting for transfers between devices: 27.8 us -> 18.5 us  [swap(): return lax.ppermute(value, axis, [(at, at ^ offset) for at in range(size)])]
    pallas_call x10 -> x9, Pallas kernels: 11 us -> 10.9 us  [call(): pl.pallas_call(body, out_shape=outs, in_specs=[pl.BlockSpec(memory_space=...]
  transfers between devices with their start and end apart: 22 -> 16, of which waited for: 13 -> 8; matrix products, arithmetic and copies ran while one was open for 0% -> 0% of each run, Pallas kernels for 12% -> 11%
where the time goes in v11:
time: 72.6 us; the launch traced here: 72.3 us
  blocking collectives  24.1 us (33%)
  waiting for transfers between devices  18.7 us (26%)
  starting transfers between devices  15.2 us (21%)
  Pallas kernels  10.9 us (15%)
  local copies, waits for them, and re-layouts  3.34 us (5%)
    all_to_all x2, blocking collectives, exchange_frames(): lax.all_to_all(blocks, 'frame', split_axis=0, concat_axis=0, tiled=True,...  24.1 us
    ppermute x14, waiting for transfers between devices, swap(): return lax.ppermute(value, axis, [(at, at ^ offset) for at in range(size)])  18.5 us
    ppermute x14, starting transfers between devices, swap(): return lax.ppermute(value, axis, [(at, at ^ offset) for at in range(size)])  11.8 us
    pallas_call x9, Pallas kernels, call(): pl.pallas_call(body, out_shape=outs, in_specs=[pl.BlockSpec(memory_space=...  10.9 us
    ppermute x2, starting transfers between devices, swap_diagonal(): return lax.ppermute(value, ('frame', 'patch'), pairs)  3.36 us
    unnamed x18, local copies, waits for them, and re-layouts  3.34 us
  transfers between devices with their start and end apart: 16, of which 8 were waited for; matrix products, arithmetic and copies ran while one was open for 0% of the time, Pallas kernels for 11%

profile of v11, /device:TPU:0, one launch (start us, length us, event | category | flops | bytes accessed | tf_op | source)
XLA Modules:
  0.0 72.3 jit_solution(4235211711125135822)
XLA Ops:
  0.0 0.5 collective-permute-start
  0.5 2.5 %collective-permute-start.3 = (bf16[1,128,1152]{2,1,0:T(8,128)(2,1)}, bf16[1,128,1152]{2,1,0:T(8,128)(2,1)S(1)}, u32[]{:S(2)}, u32[]{:S(2)}) collective-permute-start(bf16[1,128,1152]{2,1,0:T(8,128)(2,1)} %own_ref.3), channel_id=1, source_target_pairs={{0,2},{1,3},{2,0},{3,1},{4,6},{5,7},{6,4},{7,5},{8,10},{9,11},{10,... | collective-permute-start | bytes 884744 | tf_op jit(solution)/shard_map/ppermute | solution.py:214
  3.0 1.0 %copy-done.4 = bf16[1,128,1152]{2,1,0:T(8,128)(2,1)S(1)} copy-done((bf16[1,128,1152]{2,1,0:T(8,128)(2,1)S(1)}, bf16[1,128,1152]{2,1,0:T(8,128)(2,1)}, u32[]{:S(2)}) %copy-start.4) | copy-done | bytes 294936
  4.0 1.8 %collective-permute-start.1 = (bf16[64,1152]{1,0:T(8,128)(2,1)S(1)}, bf16[64,1152]{1,0:T(8,128)(2,1)S(1)}, u32[]{:S(2)}, u32[]{:S(2)}) collective-permute-start(bf16[64,1152]{1,0:T(8,128)(2,1)S(1)} %shard_map.64), channel_id=1, source_target_pairs={{0,4},{4,0},{8,12},{12,8},{16,20},{20,16},{24,28},{28,24},{1,5},{5... | collective-permute-start | bytes 442376 | tf_op jit(solution)/shard_map/ppermute | solution.py:214
  5.8 1.6 %copy-done = bf16[864,1152]{1,0:T(8,128)(2,1)S(1)} copy-done((bf16[864,1152]{1,0:T(8,128)(2,1)S(1)}, bf16[864,1152]{1,0:T(8,128)(2,1)}, u32[]{:S(2)}) %copy-start) | copy-done | bytes 1990680
  7.4 0.8 %copy-done.7 = f32[6,1152]{1,0:T(8,128)S(1)} copy-done((f32[6,1152]{1,0:T(8,128)S(1)}, f32[6,1152]{1,0:T(8,128)}, u32[]{:S(2)}) %copy-start.7) | copy-done | bytes 27672
  8.1 1.1 %shard_map.65.near_ref = f32[864,256]{1,0:T(8,128)S(1)} custom-call(f32[6,1152]{1,0:T(8,128)S(1)} %copy-done.7, bf16[864,1152]{1,0:T(8,128)(2,1)S(1)} %copy-done, bf16[1,128,1152]{2,1,0:T(8,128)(2,1)S(1)} %copy-done.4, bf16[1,128,1152]{2,1,0:T(8,128)(2,1)S(1)} %collective-permute-done.sister_ref), custom_call_target="tpu_custom_call" | custom-call | flops 1 | bytes 1 | tf_op jit(solution)/shard_map/pallas_call | solution.py:201
  9.3 1.6 %collective-permute-done.3.refs_0_ = bf16[1,128,1152]{2,1,0:T(8,128)(2,1)S(1)} collective-permute-done((bf16[1,128,1152]{2,1,0:T(8,128)(2,1)}, bf16[1,128,1152]{2,1,0:T(8,128)(2,1)S(1)}, u32[]{:S(2)}, u32[]{:S(2)}) %collective-permute-start.3) | collective-permute-done | bytes 294944 | tf_op jit(solution)/shard_map/ppermute | solution.py:214
  10.9 1.6 %collective-permute-done.4.refs_1_ = bf16[1,128,1152]{2,1,0:T(8,128)(2,1)S(1)} collective-permute-done((bf16[1,128,1152]{2,1,0:T(8,128)(2,1)S(1)}, bf16[1,128,1152]{2,1,0:T(8,128)(2,1)S(1)}, u32[]{:S(2)}, u32[]{:S(2)}) %collective-permute-start.4) | collective-permute-done | bytes 294944 | tf_op jit(solution)/shard_map/ppermute | solution.py:214
  12.6 0.4 collective-permute-start.2
  13.0 3.3 %shard_map.66 = (bf16[288,256]{1,0:T(8,128)(2,1)S(1)}, bf16[288,256]{1,0:T(8,128)(2,1)S(1)}) custom-call(f32[6,1152]{1,0:T(8,128)S(1)} %copy-done.7, bf16[864,1152]{1,0:T(8,128)(2,1)S(1)} %copy-done.1, f32[864,256]{1,0:T(8,128)S(1)} %shard_map.65.near_ref, bf16[1,128,1152]{2,1,0:T(8,128)(2,1)S(1)} %collective-permute-done.3.refs_0_, ...), custom_call_target="tpu_custom_call" | custom-call | flops 1 | bytes 1 | tf_op jit(solution)/shard_map/pallas_call | solution.py:201
  16.5 1.2 %collective-permute-done.5.refs_1_ = bf16[288,256]{1,0:T(8,128)(2,1)S(1)} collective-permute-done((bf16[288,256]{1,0:T(8,128)(2,1)S(1)}, bf16[288,256]{1,0:T(8,128)(2,1)S(1)}, u32[]{:S(2)}, u32[]{:S(2)}) %collective-permute-start.5) | collective-permute-done | bytes 147488 | tf_op jit(solution)/shard_map/ppermute | solution.py:214
  17.7 0.7 shard_map.67
  18.4 1.8 %collective-permute-start.6 = (bf16[64,1152]{1,0:T(8,128)(2,1)S(1)}, bf16[64,1152]{1,0:T(8,128)(2,1)S(1)}, u32[]{:S(2)}, u32[]{:S(2)}) collective-permute-start(bf16[64,1152]{1,0:T(8,128)(2,1)S(1)} %get-tuple-element.31), channel_id=1, source_target_pairs={{0,2},{1,3},{2,0},{3,1},{4,6},{5,7},{6,4},{7,5},{8,10},{9,11},{10,... | collective-permute-start | bytes 442376 | tf_op jit(solution)/shard_map/ppermute | solution.py:214
  20.3 1.4 %collective-permute-start.8 = (bf16[64,1152]{1,0:T(8,128)(2,1)S(1)}, bf16[64,1152]{1,0:T(8,128)(2,1)S(1)}, u32[]{:S(2)}, u32[]{:S(2)}) collective-permute-start(bf16[64,1152]{1,0:T(8,128)(2,1)S(1)} %get-tuple-element.33), channel_id=1, source_target_pairs={{0,6},{1,7},{2,4},{3,5},{4,2},{5,3},{6,0},{7,1},{8,14},{9,15},{10,... | collective-permute-start | bytes 442376 | tf_op jit(solution)/shard_map/ppermute | solution.py:237
  21.7 0.3 collective-permute-start.7
  22.0 5.5 %collective-permute-done.7.refs_4_ = bf16[64,576]{1,0:T(8,128)(2,1)S(1)} collective-permute-done((bf16[64,576]{1,0:T(8,128)(2,1)S(1)}, bf16[64,576]{1,0:T(8,128)(2,1)S(1)}, u32[]{:S(2)}, u32[]{:S(2)}) %collective-permute-start.7) | collective-permute-done | bytes 73760 | tf_op jit(solution)/shard_map/ppermute | solution.py:214
  27.5 0.2 collective-permute-done.8.refs_5_
  27.7 0.7 shard_map.68
  28.4 13.4 %all_to_all.10 = bf16[4,32,1152]{2,1,0:T(8,128)(2,1)S(1)} all-to-all(bf16[4,32,1152]{2,1,0:T(8,128)(2,1)S(1)} %get-tuple-element.36), channel_id=1, replica_groups={{0,8,16,24},{4,12,20,28},{1,9,17,25},{5,13,21,29},{2,10,18,26},{6,14,22..., dimensions={0} | all-to-all | bytes 589824 | tf_op jit(solution)/shard_map/all_to_all | solution.py:253
  41.8 2.0 %collective-permute-start.12 = (bf16[128,1152]{1,0:T(8,128)(2,1)S(1)}, bf16[128,1152]{1,0:T(8,128)(2,1)S(1)}, u32[]{:S(2)}, u32[]{:S(2)}) collective-permute-start(bf16[128,1152]{1,0:T(8,128)(2,1)S(1)} %bitcast.2), channel_id=1, source_target_pairs={{0,2},{1,3},{2,0},{3,1},{4,6},{5,7},{6,4},{7,5},{8,10},{9,11},{10,... | collective-permute-start | bytes 884744 | tf_op jit(solution)/shard_map/ppermute | solution.py:214
  43.7 1.5 %collective-permute-start.9 = (bf16[4,16,1152]{2,1,0:T(8,128)(2,1)S(1)}, bf16[4,16,1152]{2,1,0:T(8,128)(2,1)S(1)}, u32[]{:S(2)}, u32[]{:S(2)}) collective-permute-start(bf16[4,16,1152]{2,1,0:T(8,128)(2,1)S(1)} %get-tuple-element.37), channel_id=1, source_target_pairs={{0,4},{4,0},{8,12},{12,8},{16,20},{20,16},{24,28},{28,24},{1,5},{5... | collective-permute-start | bytes 442376 | tf_op jit(solution)/shard_map/ppermute | solution.py:214
  45.2 1.9 %shard_map.69 = (f32[64,1152]{1,0:T(8,128)S(1)}, bf16[64,576]{1,0:T(8,128)(2,1)S(1)}) custom-call(bf16[864,1152]{1,0:T(8,128)(2,1)S(1)} %copy-done.2, bf16[864,1152]{1,0:T(8,128)(2,1)S(1)} %collective-permute-done.11.refs_1_, bf16[288,1152]{1,0:T(8,128)(2,1)S(1)} %copy-done.3, bf16[288,1152]{1,0:T(8,128)(2,1)S(1)} %collective-permute-done.10.refs_3_.refs_1_, ...), custom_call_target="tpu_custom_call" | custom-call | flops 1 | bytes 1 | tf_op jit(solution)/shard_map/pallas_call | solution.py:201
  47.1 0.6 collective-permute-start.13
  47.7 1.3 %collective-permute-done.9.other_ref = bf16[4,16,1152]{2,1,0:T(8,128)(2,1)S(1)} collective-permute-done((bf16[4,16,1152]{2,1,0:T(8,128)(2,1)S(1)}, bf16[4,16,1152]{2,1,0:T(8,128)(2,1)S(1)}, u32[]{:S(2)}, u32[]{:S(2)}) %collective-permute-start.9) | collective-permute-done | bytes 147488 | tf_op jit(solution)/shard_map/ppermute | solution.py:214
  49.1 2.6 %collective-permute-done.13.refs_4_ = bf16[64,576]{1,0:T(8,128)(2,1)S(1)} collective-permute-done((bf16[64,576]{1,0:T(8,128)(2,1)S(1)}, bf16[64,576]{1,0:T(8,128)(2,1)S(1)}, u32[]{:S(2)}, u32[]{:S(2)}) %collective-permute-start.13) | collective-permute-done | bytes 73760 | tf_op jit(solution)/shard_map/ppermute | solution.py:214
  51.7 2.0 %shard_map.70 = (bf16[64,1152]{1,0:T(8,128)(2,1)S(1)}, bf16[64,1152]{1,0:T(8,128)(2,1)S(1)}) custom-call(bf16[864,1152]{1,0:T(8,128)(2,1)S(1)} %copy-done.2, bf16[864,1152]{1,0:T(8,128)(2,1)S(1)} %collective-permute-done.11.refs_1_, bf16[288,1152]{1,0:T(8,128)(2,1)S(1)} %copy-done.3, bf16[288,1152]{1,0:T(8,128)(2,1)S(1)} %collective-permute-done.10.refs_3_.refs_1_, ...), custom_call_target="tpu_custom_call" | custom-call | flops 1 | bytes 1 | tf_op jit(solution)/shard_map/pallas_call | solution.py:201
  53.8 1.9 %collective-permute-start.15 = (bf16[64,1152]{1,0:T(8,128)(2,1)S(1)}, bf16[64,1152]{1,0:T(8,128)(2,1)S(1)}, u32[]{:S(2)}, u32[]{:S(2)}) collective-permute-start(bf16[64,1152]{1,0:T(8,128)(2,1)S(1)} %get-tuple-element.44), channel_id=1, source_target_pairs={{0,6},{1,7},{2,4},{3,5},{4,2},{5,3},{6,0},{7,1},{8,14},{9,15},{10,... | collective-permute-start | bytes 442376 | tf_op jit(solution)/shard_map/ppermute | solution.py:237
  55.7 4.7 %collective-permute-done.14.refs_3_ = bf16[64,1152]{1,0:T(8,128)(2,1)S(1)} collective-permute-done((bf16[64,1152]{1,0:T(8,128)(2,1)S(1)}, bf16[64,1152]{1,0:T(8,128)(2,1)S(1)}, u32[]{:S(2)}, u32[]{:S(2)}) %collective-permute-start.14) | collective-permute-done | bytes 147488 | tf_op jit(solution)/shard_map/ppermute | solution.py:214
  60.4 0.4 shard_map.71
  60.8 10.7 %all_to_all.11.update_ref = bf16[4,32,1152]{2,1,0:T(8,128)(2,1)S(1)} all-to-all(bf16[4,32,1152]{2,1,0:T(8,128)(2,1)S(1)} %shard_map.71), channel_id=1, replica_groups={{0,8,16,24},{4,12,20,28},{1,9,17,25},{5,13,21,29},{2,10,18,26},{6,14,22..., dimensions={0} | all-to-all | bytes 589824 | tf_op jit(solution)/shard_map/all_to_all | solution.py:253
  71.5 0.8 %shard_map.72 = bf16[8,16,1152]{2,1,0:T(8,128)(2,1)} custom-call(f32[6,1152]{1,0:T(8,128)S(1)} %copy-done.8, bf16[4,16,1152]{2,1,0:T(8,128)(2,1)S(1)} %get-tuple-element.34.kept_ref, bf16[4,16,1152]{2,1,0:T(8,128)(2,1)S(1)} %collective-permute-done.9.other_ref, bf16[4,32,1152]{2,1,0:T(8,128)(2,1)S(1)} %all_to_all.11.update_ref), custom_call_target="tpu_custom_call" | custom-call | flops 1 | bytes 1 | tf_op jit(solution)/shard_map/pallas_call | solution.py:201
  (29 shorter events, 0.6 us)
Async XLA Ops:
  0.0 3.0 %collective-permute-start = (bf16[1,128,1152]{2,1,0:T(8,128)(2,1)}, bf16[1,128,1152]{2,1,0:T(8,128)(2,1)S(1)}, u32[]{:S(2)}, u32[]{:S(2)}) collective-permute-start(bf16[1,128,1152]{2,1,0:T(8,128)(2,1)} %own_ref.3), channel_id=1, source_target_pairs={{0,1},{1,0},{2,3},{3,2},{4,5},{5,4},{6,7},{7,6},{8,9},{9,8},{10,11... | collective-permute-start | bytes 884744 | tf_op jit(solution)/shard_map/ppermute | solution.py:214
  0.5 10.4 %collective-permute-start.3 = (bf16[1,128,1152]{2,1,0:T(8,128)(2,1)}, bf16[1,128,1152]{2,1,0:T(8,128)(2,1)S(1)}, u32[]{:S(2)}, u32[]{:S(2)}) collective-permute-start(bf16[1,128,1152]{2,1,0:T(8,128)(2,1)} %own_ref.3), channel_id=1, source_target_pairs={{0,2},{1,3},{2,0},{3,1},{4,6},{5,7},{6,4},{7,5},{8,10},{9,11},{10,... | collective-permute-start | bytes 884744 | tf_op jit(solution)/shard_map/ppermute | solution.py:214
  3.0 1.0 %copy-start.4 = (bf16[1,128,1152]{2,1,0:T(8,128)(2,1)S(1)}, bf16[1,128,1152]{2,1,0:T(8,128)(2,1)}, u32[]{:S(2)}) copy-start(bf16[1,128,1152]{2,1,0:T(8,128)(2,1)} %own_ref.3) | copy-start | bytes 884740
  4.0 6.8 %collective-permute-start.1 = (bf16[64,1152]{1,0:T(8,128)(2,1)S(1)}, bf16[64,1152]{1,0:T(8,128)(2,1)S(1)}, u32[]{:S(2)}, u32[]{:S(2)}) collective-permute-start(bf16[64,1152]{1,0:T(8,128)(2,1)S(1)} %shard_map.64), channel_id=1, source_target_pairs={{0,4},{4,0},{8,12},{12,8},{16,20},{20,16},{24,28},{28,24},{1,5},{5... | collective-permute-start | bytes 442376 | tf_op jit(solution)/shard_map/ppermute | solution.py:214
  5.8 1.6 %copy-start = (bf16[864,1152]{1,0:T(8,128)(2,1)S(1)}, bf16[864,1152]{1,0:T(8,128)(2,1)}, u32[]{:S(2)}) copy-start(bf16[864,1152]{1,0:T(8,128)(2,1)} %weight_ref.3) | copy-start | bytes 5971972
  7.4 0.8 %copy-start.7 = (f32[6,1152]{1,0:T(8,128)S(1)}, f32[6,1152]{1,0:T(8,128)}, u32[]{:S(2)}) copy-start(f32[6,1152]{1,0:T(8,128)} %mod_ref.7) | copy-start | bytes 82948
  8.1 4.4 %copy-start.6 = (bf16[288,1152]{1,0:T(8,128)(2,1)S(1)}, bf16[288,1152]{1,0:T(8,128)(2,1)}, u32[]{:S(2)}) copy-start(bf16[288,1152]{1,0:T(8,128)(2,1)} %refs_0_.4) | copy-start | bytes 1990660
  8.1 4.8 %copy-start.1 = (bf16[864,1152]{1,0:T(8,128)(2,1)S(1)}, bf16[864,1152]{1,0:T(8,128)(2,1)}, u32[]{:S(2)}) copy-start(bf16[864,1152]{1,0:T(8,128)(2,1)} %weight_ref.3) | copy-start | bytes 5971972
  9.2 12.8 %copy-start.3 = (bf16[288,1152]{1,0:T(8,128)(2,1)S(1)}, bf16[288,1152]{1,0:T(8,128)(2,1)}, u32[]{:S(2)}) copy-start(bf16[288,1152]{1,0:T(8,128)(2,1)} %refs_0_.7) | copy-start | bytes 1990660
  9.3 18.4 %copy-start.5 = (bf16[1,128,1152]{2,1,0:T(8,128)(2,1)S(1)}, bf16[1,128,1152]{2,1,0:T(8,128)(2,1)}, u32[]{:S(2)}) copy-start(bf16[1,128,1152]{2,1,0:T(8,128)(2,1)} %own_ref.3) | copy-start | bytes 884740
  10.9 1.6 %collective-permute-start.4 = (bf16[1,128,1152]{2,1,0:T(8,128)(2,1)S(1)}, bf16[1,128,1152]{2,1,0:T(8,128)(2,1)S(1)}, u32[]{:S(2)}, u32[]{:S(2)}) collective-permute-start(bf16[1,128,1152]{2,1,0:T(8,128)(2,1)S(1)} %collective-permute-done.3.refs_0_), channel_id=1, source_target_pairs={{0,1},{1,0},{2,3},{3,2},{4,5},{5,4},{6,7},{7,6},{8,9},{9,8},{10,11... | collective-permute-start | bytes 884744 | tf_op jit(solution)/shard_map/ppermute | solution.py:214
  12.4 32.8 %collective-permute-start.11 = (bf16[864,1152]{1,0:T(8,128)(2,1)}, bf16[864,1152]{1,0:T(8,128)(2,1)S(1)}, u32[]{:S(2)}, u32[]{:S(2)}) collective-permute-start(bf16[864,1152]{1,0:T(8,128)(2,1)} %refs_0_.6), channel_id=1, source_target_pairs={{0,1},{1,0},{2,3},{3,2},{4,5},{5,4},{6,7},{7,6},{8,9},{9,8},{10,11... | collective-permute-start | bytes 5971976 | tf_op jit(solution)/shard_map/ppermute | solution.py:214
  12.6 5.1 %collective-permute-start.2 = (bf16[288,1152]{1,0:T(8,128)(2,1)S(1)}, bf16[288,1152]{1,0:T(8,128)(2,1)S(1)}, u32[]{:S(2)}, u32[]{:S(2)}) collective-permute-start(bf16[288,1152]{1,0:T(8,128)(2,1)S(1)} %copy-done.6), channel_id=1, source_target_pairs={{0,1},{1,0},{2,3},{3,2},{4,5},{5,4},{6,7},{7,6},{8,9},{9,8},{10,11... | collective-permute-start | bytes 1990664 | tf_op jit(solution)/shard_map/ppermute | solution.py:214
  16.3 1.4 %collective-permute-start.5 = (bf16[288,256]{1,0:T(8,128)(2,1)S(1)}, bf16[288,256]{1,0:T(8,128)(2,1)S(1)}, u32[]{:S(2)}, u32[]{:S(2)}) collective-permute-start(bf16[288,256]{1,0:T(8,128)(2,1)S(1)} %get-tuple-element.29), channel_id=1, source_target_pairs={{0,1},{1,0},{2,3},{3,2},{4,5},{5,4},{6,7},{7,6},{8,9},{9,8},{10,11... | collective-permute-start | bytes 442376 | tf_op jit(solution)/shard_map/ppermute | solution.py:214
  17.7 27.5 %copy-start.2 = (bf16[864,1152]{1,0:T(8,128)(2,1)S(1)}, bf16[864,1152]{1,0:T(8,128)(2,1)}, u32[]{:S(2)}) copy-start(bf16[864,1152]{1,0:T(8,128)(2,1)} %refs_0_.6) | copy-start | bytes 5971972
  18.4 9.0 %collective-permute-start.6 = (bf16[64,1152]{1,0:T(8,128)(2,1)S(1)}, bf16[64,1152]{1,0:T(8,128)(2,1)S(1)}, u32[]{:S(2)}, u32[]{:S(2)}) collective-permute-start(bf16[64,1152]{1,0:T(8,128)(2,1)S(1)} %get-tuple-element.31), channel_id=1, source_target_pairs={{0,2},{1,3},{2,0},{3,1},{4,6},{5,7},{6,4},{7,5},{8,10},{9,11},{10,... | collective-permute-start | bytes 442376 | tf_op jit(solution)/shard_map/ppermute | solution.py:214
  20.3 7.5 %collective-permute-start.8 = (bf16[64,1152]{1,0:T(8,128)(2,1)S(1)}, bf16[64,1152]{1,0:T(8,128)(2,1)S(1)}, u32[]{:S(2)}, u32[]{:S(2)}) collective-permute-start(bf16[64,1152]{1,0:T(8,128)(2,1)S(1)} %get-tuple-element.33), channel_id=1, source_target_pairs={{0,6},{1,7},{2,4},{3,5},{4,2},{5,3},{6,0},{7,1},{8,14},{9,15},{10,... | collective-permute-start | bytes 442376 | tf_op jit(solution)/shard_map/ppermute | solution.py:237
  21.7 5.8 %collective-permute-start.7 = (bf16[64,576]{1,0:T(8,128)(2,1)S(1)}, bf16[64,576]{1,0:T(8,128)(2,1)S(1)}, u32[]{:S(2)}, u32[]{:S(2)}) collective-permute-start(bf16[64,576]{1,0:T(8,128)(2,1)S(1)} %get-tuple-element.32), channel_id=1, source_target_pairs={{0,4},{4,0},{8,12},{12,8},{16,20},{20,16},{24,28},{28,24},{1,5},{5... | collective-permute-start | bytes 221192 | tf_op jit(solution)/shard_map/ppermute | solution.py:214
  22.0 23.2 %collective-permute-start.10 = (bf16[288,1152]{1,0:T(8,128)(2,1)S(1)}, bf16[288,1152]{1,0:T(8,128)(2,1)S(1)}, u32[]{:S(2)}, u32[]{:S(2)}) collective-permute-start(bf16[288,1152]{1,0:T(8,128)(2,1)S(1)} %copy-done.3), channel_id=1, source_target_pairs={{0,1},{1,0},{2,3},{3,2},{4,5},{5,4},{6,7},{7,6},{8,9},{9,8},{10,11... | collective-permute-start | bytes 1990664 | tf_op jit(solution)/shard_map/ppermute | solution.py:214
  41.8 7.3 %collective-permute-start.12 = (bf16[128,1152]{1,0:T(8,128)(2,1)S(1)}, bf16[128,1152]{1,0:T(8,128)(2,1)S(1)}, u32[]{:S(2)}, u32[]{:S(2)}) collective-permute-start(bf16[128,1152]{1,0:T(8,128)(2,1)S(1)} %bitcast.2), channel_id=1, source_target_pairs={{0,2},{1,3},{2,0},{3,1},{4,6},{5,7},{6,4},{7,5},{8,10},{9,11},{10,... | collective-permute-start | bytes 884744 | tf_op jit(solution)/shard_map/ppermute | solution.py:214
  43.7 5.4 %collective-permute-start.9 = (bf16[4,16,1152]{2,1,0:T(8,128)(2,1)S(1)}, bf16[4,16,1152]{2,1,0:T(8,128)(2,1)S(1)}, u32[]{:S(2)}, u32[]{:S(2)}) collective-permute-start(bf16[4,16,1152]{2,1,0:T(8,128)(2,1)S(1)} %get-tuple-element.37), channel_id=1, source_target_pairs={{0,4},{4,0},{8,12},{12,8},{16,20},{20,16},{24,28},{28,24},{1,5},{5... | collective-permute-start | bytes 442376 | tf_op jit(solution)/shard_map/ppermute | solution.py:214
  47.1 4.5 %collective-permute-start.13 = (bf16[64,576]{1,0:T(8,128)(2,1)S(1)}, bf16[64,576]{1,0:T(8,128)(2,1)S(1)}, u32[]{:S(2)}, u32[]{:S(2)}) collective-permute-start(bf16[64,576]{1,0:T(8,128)(2,1)S(1)} %get-tuple-element.41), channel_id=1, source_target_pairs={{0,4},{4,0},{8,12},{12,8},{16,20},{20,16},{24,28},{28,24},{1,5},{5... | collective-permute-start | bytes 221192 | tf_op jit(solution)/shard_map/ppermute | solution.py:214
  53.6 17.9 %copy-start.8 = (f32[6,1152]{1,0:T(8,128)S(1)}, f32[6,1152]{1,0:T(8,128)}, u32[]{:S(2)}) copy-start(f32[6,1152]{1,0:T(8,128)} %mod_ref.7) | copy-start | bytes 82948
  53.6 6.8 %collective-permute-start.14 = (bf16[64,1152]{1,0:T(8,128)(2,1)S(1)}, bf16[64,1152]{1,0:T(8,128)(2,1)S(1)}, u32[]{:S(2)}, u32[]{:S(2)}) collective-permute-start(bf16[64,1152]{1,0:T(8,128)(2,1)S(1)} %get-tuple-element.43), channel_id=1, source_target_pairs={{0,2},{1,3},{2,0},{3,1},{4,6},{5,7},{6,4},{7,5},{8,10},{9,11},{10,... | collective-permute-start | bytes 442376 | tf_op jit(solution)/shard_map/ppermute | solution.py:214
  53.8 6.7 %collective-permute-start.15 = (bf16[64,1152]{1,0:T(8,128)(2,1)S(1)}, bf16[64,1152]{1,0:T(8,128)(2,1)S(1)}, u32[]{:S(2)}, u32[]{:S(2)}) collective-permute-start(bf16[64,1152]{1,0:T(8,128)(2,1)S(1)} %get-tuple-element.44), channel_id=1, source_target_pairs={{0,6},{1,7},{2,4},{3,5},{4,2},{5,3},{6,0},{7,1},{8,14},{9,15},{10,... | collective-permute-start | bytes 442376 | tf_op jit(solution)/shard_map/ppermute | solution.py:237

commit v12 on v9

--- a/solution.py
+++ b/solution.py
@@ -291,7 +291,6 @@
     out_pair = with_sister(spatial_out, near)
     far = both_cores([after(block, near, paired) for block in far])
     temporal_pair = with_sister(temporal_qkv, *far)
-    late_pair = with_sister(temporal_out, *far)
 
     kept, sent = call(
         functools.partial(spatial_kernel, count),
@@ -304,6 +303,7 @@
         (kept, swap(sent, "patch", 1), *out_pair),
         own_shapes + far_shapes,
     )
+    late_pair = with_sister(temporal_out, parts[0])
     updates = return_updates((parts[0], swap(parts[1], "frame", 1)), parts[2:])
     middle, middle_sent, *parts = call(
         functools.partial(middle_kernel, pieces, groups),
@@ -327,7 +327,7 @@
     kept, sent = attend_frames(True, [segment], own_shapes)
     received = swap(sent, "frame", 1)
     middle_other = swap(after(middle_sent, segment), "frame", 1)
-    others = [after(block, received, middle_other) for block in segments[1:]]
+    others = [after(block, received) for block in segments[1:]]
     far_parts = attend_frames(False, others, far_shapes)
     updates = return_updates((kept, received), far_parts)
     parts = call(

time: 66.8 us -> 66.6 us (level)
  waiting for transfers between devices: 28 us -> 26.8 us
  starting transfers between devices: 24.1 us -> 25 us
    ppermute x20, waiting for transfers between devices: 27.8 us -> 25 us  [swap(): return lax.ppermute(value, axis, [(at, at ^ offset) for at in range(size)])]
    ppermute x2, waiting for transfers between devices: 0.22 us -> 1.8 us  [swap_diagonal(): return lax.ppermute(value, ('frame', 'patch'), pairs)]
    ppermute x20, starting transfers between devices: 21.1 us -> 22.4 us  [swap(): return lax.ppermute(value, axis, [(at, at ^ offset) for at in range(size)])]
  transfers between devices with their start and end apart: 22 -> 22, of which waited for: 13 -> 12; matrix products, arithmetic and copies ran while one was open for 0% -> 0% of each run, Pallas kernels for 12% -> 12%
where the time goes in v12:
time: 66.6 us; the launch traced here: 66.3 us
  waiting for transfers between devices  26.8 us (40%)
  starting transfers between devices  25 us (38%)
  Pallas kernels  11 us (17%)
  local copies, waits for them, and re-layouts  3.34 us (5%)
    ppermute x20, waiting for transfers between devices, swap(): return lax.ppermute(value, axis, [(at, at ^ offset) for at in range(size)])  25 us
    ppermute x20, starting transfers between devices, swap(): return lax.ppermute(value, axis, [(at, at ^ offset) for at in range(size)])  22.4 us
    pallas_call x10, Pallas kernels, call(): pl.pallas_call(body, out_shape=outs, in_specs=[pl.BlockSpec(memory_space=...  11 us
    unnamed x18, local copies, waits for them, and re-layouts  3.34 us
    ppermute x2, starting transfers between devices, swap_diagonal(): return lax.ppermute(value, ('frame', 'patch'), pairs)  2.62 us
    ppermute x2, waiting for transfers between devices, swap_diagonal(): return lax.ppermute(value, ('frame', 'patch'), pairs)  1.8 us
  transfers between devices with their start and end apart: 22, of which 12 were waited for; matrix products, arithmetic and copies ran while one was open for 0% of the time, Pallas kernels for 12%

profile of v12, /device:TPU:0, one launch (start us, length us, event | category | flops | bytes accessed | tf_op | source)
XLA Modules:
  0.0 66.3 jit_solution(3693510349751658359)
XLA Ops:
  0.5 2.5 %collective-permute-start.3 = (bf16[1,128,1152]{2,1,0:T(8,128)(2,1)}, bf16[1,128,1152]{2,1,0:T(8,128)(2,1)S(1)}, u32[]{:S(2)}, u32[]{:S(2)}) collective-permute-start(bf16[1,128,1152]{2,1,0:T(8,128)(2,1)} %own_ref.3), channel_id=1, source_target_pairs={{0,2},{1,3},{2,0},{3,1},{4,6},{5,7},{6,4},{7,5},{8,10},{9,11},{10,... | collective-permute-start | bytes 884744 | tf_op jit(solution)/shard_map/ppermute | solution.py:227
  3.0 1.0 %copy-done.4 = bf16[1,128,1152]{2,1,0:T(8,128)(2,1)S(1)} copy-done((bf16[1,128,1152]{2,1,0:T(8,128)(2,1)S(1)}, bf16[1,128,1152]{2,1,0:T(8,128)(2,1)}, u32[]{:S(2)}) %copy-start.4) | copy-done | bytes 294936
  4.0 1.8 %collective-permute-start.1 = (bf16[64,1152]{1,0:T(8,128)(2,1)S(1)}, bf16[64,1152]{1,0:T(8,128)(2,1)S(1)}, u32[]{:S(2)}, u32[]{:S(2)}) collective-permute-start(bf16[64,1152]{1,0:T(8,128)(2,1)S(1)} %shard_map.64), channel_id=1, source_target_pairs={{0,4},{4,0},{8,12},{12,8},{16,20},{20,16},{24,28},{28,24},{1,5},{5... | collective-permute-start | bytes 442376 | tf_op jit(solution)/shard_map/ppermute | solution.py:227
  5.8 1.6 %copy-done = bf16[864,1152]{1,0:T(8,128)(2,1)S(1)} copy-done((bf16[864,1152]{1,0:T(8,128)(2,1)S(1)}, bf16[864,1152]{1,0:T(8,128)(2,1)}, u32[]{:S(2)}) %copy-start) | copy-done | bytes 1990680
  7.4 0.8 %copy-done.7 = f32[6,1152]{1,0:T(8,128)S(1)} copy-done((f32[6,1152]{1,0:T(8,128)S(1)}, f32[6,1152]{1,0:T(8,128)}, u32[]{:S(2)}) %copy-start.7) | copy-done | bytes 27672
  8.1 1.1 %shard_map.65.near_ref = f32[864,256]{1,0:T(8,128)S(1)} custom-call(f32[6,1152]{1,0:T(8,128)S(1)} %copy-done.7, bf16[864,1152]{1,0:T(8,128)(2,1)S(1)} %copy-done, bf16[1,128,1152]{2,1,0:T(8,128)(2,1)S(1)} %copy-done.4, bf16[1,128,1152]{2,1,0:T(8,128)(2,1)S(1)} %collective-permute-done.sister_ref), custom_call_target="tpu_custom_call" | custom-call | flops 1 | bytes 1 | tf_op jit(solution)/shard_map/pallas_call | solution.py:214
  9.3 1.6 %collective-permute-done.3.refs_0_ = bf16[1,128,1152]{2,1,0:T(8,128)(2,1)S(1)} collective-permute-done((bf16[1,128,1152]{2,1,0:T(8,128)(2,1)}, bf16[1,128,1152]{2,1,0:T(8,128)(2,1)S(1)}, u32[]{:S(2)}, u32[]{:S(2)}) %collective-permute-start.3) | collective-permute-done | bytes 294944 | tf_op jit(solution)/shard_map/ppermute | solution.py:227
  10.9 1.6 %collective-permute-done.4.refs_1_ = bf16[1,128,1152]{2,1,0:T(8,128)(2,1)S(1)} collective-permute-done((bf16[1,128,1152]{2,1,0:T(8,128)(2,1)S(1)}, bf16[1,128,1152]{2,1,0:T(8,128)(2,1)S(1)}, u32[]{:S(2)}, u32[]{:S(2)}) %collective-permute-start.4) | collective-permute-done | bytes 294944 | tf_op jit(solution)/shard_map/ppermute | solution.py:227
  13.0 3.3 %shard_map.66 = (bf16[288,256]{1,0:T(8,128)(2,1)S(1)}, bf16[288,256]{1,0:T(8,128)(2,1)S(1)}) custom-call(f32[6,1152]{1,0:T(8,128)S(1)} %copy-done.7, bf16[864,1152]{1,0:T(8,128)(2,1)S(1)} %copy-done.1, f32[864,256]{1,0:T(8,128)S(1)} %shard_map.65.near_ref, bf16[1,128,1152]{2,1,0:T(8,128)(2,1)S(1)} %collective-permute-done.3.refs_0_, ...), custom_call_target="tpu_custom_call" | custom-call | flops 1 | bytes 1 | tf_op jit(solution)/shard_map/pallas_call | solution.py:214
  16.5 1.2 %collective-permute-done.5.refs_1_ = bf16[288,256]{1,0:T(8,128)(2,1)S(1)} collective-permute-done((bf16[288,256]{1,0:T(8,128)(2,1)S(1)}, bf16[288,256]{1,0:T(8,128)(2,1)S(1)}, u32[]{:S(2)}, u32[]{:S(2)}) %collective-permute-start.5) | collective-permute-done | bytes 147488 | tf_op jit(solution)/shard_map/ppermute | solution.py:227
  17.7 0.7 %shard_map.67 = (f32[64,1152]{1,0:T(8,128)S(1)}, bf16[64,576]{1,0:T(8,128)(2,1)S(1)}, bf16[64,1152]{1,0:T(8,128)(2,1)S(1)}, bf16[64,1152]{1,0:T(8,128)(2,1)S(1)}) custom-call(bf16[288,256]{1,0:T(8,128)(2,1)S(1)} %get-tuple-element.35.refs_0_, bf16[288,256]{1,0:T(8,128)(2,1)S(1)} %collective-permute-done.5.refs_1_, bf16[288,1152]{1,0:T(8,128)(2,1)S(1)} %copy-done.6, ...), custom_call_target="tpu_custom_call" | custom-call | flops 1 | bytes 1 | tf_op jit(solution)/shard_map/pallas_call | solution.py:214
  18.7 1.8 %collective-permute-start.6 = (bf16[64,1152]{1,0:T(8,128)(2,1)S(1)}, bf16[64,1152]{1,0:T(8,128)(2,1)S(1)}, u32[]{:S(2)}, u32[]{:S(2)}) collective-permute-start(bf16[64,1152]{1,0:T(8,128)(2,1)S(1)} %get-tuple-element.38), channel_id=1, source_target_pairs={{0,2},{1,3},{2,0},{3,1},{4,6},{5,7},{6,4},{7,5},{8,10},{9,11},{10,... | collective-permute-start | bytes 442376 | tf_op jit(solution)/shard_map/ppermute | solution.py:227
  20.4 1.4 %collective-permute-start.8 = (bf16[64,1152]{1,0:T(8,128)(2,1)S(1)}, bf16[64,1152]{1,0:T(8,128)(2,1)S(1)}, u32[]{:S(2)}, u32[]{:S(2)}) collective-permute-start(bf16[64,1152]{1,0:T(8,128)(2,1)S(1)} %get-tuple-element.40), channel_id=1, source_target_pairs={{0,6},{1,7},{2,4},{3,5},{4,2},{5,3},{6,0},{7,1},{8,14},{9,15},{10,... | collective-permute-start | bytes 442376 | tf_op jit(solution)/shard_map/ppermute | solution.py:250
  22.2 5.6 %collective-permute-done.7.refs_4_ = bf16[64,576]{1,0:T(8,128)(2,1)S(1)} collective-permute-done((bf16[64,576]{1,0:T(8,128)(2,1)S(1)}, bf16[64,576]{1,0:T(8,128)(2,1)S(1)}, u32[]{:S(2)}, u32[]{:S(2)}) %collective-permute-start.7) | collective-permute-done | bytes 73760 | tf_op jit(solution)/shard_map/ppermute | solution.py:227
  28.1 0.7 %shard_map.68 = (bf16[4,16,1152]{2,1,0:T(8,128)(2,1)S(1)}, bf16[4,16,1152]{2,1,0:T(8,128)(2,1)S(1)}, bf16[32,1152]{1,0:T(8,128)(2,1)S(1)}, bf16[32,1152]{1,0:T(8...) custom-call(f32[6,1152]{1,0:T(8,128)S(1)} %copy-done.7, bf16[1,128,1152]{2,1,0:T(8,128)(2,1)S(1)} %copy-done.5, ...), custom_call_target="tpu_custom_call" | custom-call | flops 1 | bytes 1 | tf_op jit(solution)/shard_map/pallas_call | solution.py:214
  28.8 3.8 %collective-permute-start.9 = (bf16[32,1152]{1,0:T(8,128)(2,1)S(1)}, bf16[32,1152]{1,0:T(8,128)(2,1)S(1)}, u32[]{:S(2)}, u32[]{:S(2)}) collective-permute-start(bf16[32,1152]{1,0:T(8,128)(2,1)S(1)} %get-tuple-element.43), channel_id=1, source_target_pairs={{0,24},{4,28},{8,16},{12,20},{16,8},{20,12},{24,0},{28,4},{1,25},{... | collective-permute-start | bytes 221192 | tf_op jit(solution)/shard_map/ppermute | solution.py:227
  32.5 0.7 %collective-permute-start.11 = (bf16[32,1152]{1,0:T(8,128)(2,1)S(1)}, bf16[32,1152]{1,0:T(8,128)(2,1)S(1)}, u32[]{:S(2)}, u32[]{:S(2)}) collective-permute-start(bf16[32,1152]{1,0:T(8,128)(2,1)S(1)} %get-tuple-element.45), channel_id=1, source_target_pairs={{0,8},{4,12},{8,0},{12,4},{16,24},{20,28},{24,16},{28,20},{1,9},{5... | collective-permute-start | bytes 221192 | tf_op jit(solution)/shard_map/ppermute | solution.py:227
  33.2 2.3 %collective-permute-done.9.refs_0_ = bf16[32,1152]{1,0:T(8,128)(2,1)S(1)} collective-permute-done((bf16[32,1152]{1,0:T(8,128)(2,1)S(1)}, bf16[32,1152]{1,0:T(8,128)(2,1)S(1)}, u32[]{:S(2)}, u32[]{:S(2)}) %collective-permute-start.9) | collective-permute-done | bytes 73760 | tf_op jit(solution)/shard_map/ppermute | solution.py:227
  35.5 2.7 %collective-permute-done.10.refs_1_ = bf16[32,1152]{1,0:T(8,128)(2,1)S(1)} collective-permute-done((bf16[32,1152]{1,0:T(8,128)(2,1)S(1)}, bf16[32,1152]{1,0:T(8,128)(2,1)S(1)}, u32[]{:S(2)}, u32[]{:S(2)}) %collective-permute-start.10) | collective-permute-done | bytes 73760 | tf_op jit(solution)/shard_map/ppermute | solution.py:227
  38.3 1.8 %collective-permute-start.15 = (bf16[128,1152]{1,0:T(8,128)(2,1)S(1)}, bf16[128,1152]{1,0:T(8,128)(2,1)S(1)}, u32[]{:S(2)}, u32[]{:S(2)}) collective-permute-start(bf16[128,1152]{1,0:T(8,128)(2,1)S(1)} %shard_map.69.refs_4_), channel_id=1, source_target_pairs={{0,2},{1,3},{2,0},{3,1},{4,6},{5,7},{6,4},{7,5},{8,10},{9,11},{10,... | collective-permute-start | bytes 884744 | tf_op jit(solution)/shard_map/ppermute | solution.py:227
  40.1 1.9 %shard_map.70 = (f32[64,1152]{1,0:T(8,128)S(1)}, bf16[64,576]{1,0:T(8,128)(2,1)S(1)}) custom-call(bf16[864,1152]{1,0:T(8,128)(2,1)S(1)} %copy-done.2, bf16[864,1152]{1,0:T(8,128)(2,1)S(1)} %collective-permute-done.14.refs_1_, bf16[288,1152]{1,0:T(8,128)(2,1)S(1)} %copy-done.3, bf16[288,1152]{1,0:T(8,128)(2,1)S(1)} %collective-permute-done.13.refs_3_.refs_1_, ...), custom_call_target="tpu_custom_call" | custom-call | flops 1 | bytes 1 | tf_op jit(solution)/shard_map/pallas_call | solution.py:214
  42.0 1.6 %collective-permute-start.16 = (bf16[64,576]{1,0:T(8,128)(2,1)S(1)}, bf16[64,576]{1,0:T(8,128)(2,1)S(1)}, u32[]{:S(2)}, u32[]{:S(2)}) collective-permute-start(bf16[64,576]{1,0:T(8,128)(2,1)S(1)} %get-tuple-element.51), channel_id=1, source_target_pairs={{0,4},{4,0},{8,12},{12,8},{16,20},{20,16},{24,28},{28,24},{1,5},{5... | collective-permute-start | bytes 221192 | tf_op jit(solution)/shard_map/ppermute | solution.py:227
  43.6 3.6 %collective-permute-done.15.refs_4_ = bf16[128,1152]{1,0:T(8,128)(2,1)S(1)} collective-permute-done((bf16[128,1152]{1,0:T(8,128)(2,1)S(1)}, bf16[128,1152]{1,0:T(8,128)(2,1)S(1)}, u32[]{:S(2)}, u32[]{:S(2)}) %collective-permute-start.15) | collective-permute-done | bytes 294944 | tf_op jit(solution)/shard_map/ppermute | solution.py:227
  47.2 2.0 %shard_map.71 = (bf16[64,1152]{1,0:T(8,128)(2,1)S(1)}, bf16[64,1152]{1,0:T(8,128)(2,1)S(1)}) custom-call(bf16[864,1152]{1,0:T(8,128)(2,1)S(1)} %copy-done.2, bf16[864,1152]{1,0:T(8,128)(2,1)S(1)} %collective-permute-done.14.refs_1_, bf16[288,1152]{1,0:T(8,128)(2,1)S(1)} %copy-done.3, bf16[288,1152]{1,0:T(8,128)(2,1)S(1)} %collective-permute-done.13.refs_3_.refs_1_, ...), custom_call_target="tpu_custom_call" | custom-call | flops 1 | bytes 1 | tf_op jit(solution)/shard_map/pallas_call | solution.py:214
  49.2 1.8 %collective-permute-start.17 = (bf16[64,1152]{1,0:T(8,128)(2,1)S(1)}, bf16[64,1152]{1,0:T(8,128)(2,1)S(1)}, u32[]{:S(2)}, u32[]{:S(2)}) collective-permute-start(bf16[64,1152]{1,0:T(8,128)(2,1)S(1)} %get-tuple-element.53), channel_id=1, source_target_pairs={{0,2},{1,3},{2,0},{3,1},{4,6},{5,7},{6,4},{7,5},{8,10},{9,11},{10,... | collective-permute-start | bytes 442376 | tf_op jit(solution)/shard_map/ppermute | solution.py:227
  51.0 1.2 %collective-permute-start.18 = (bf16[64,1152]{1,0:T(8,128)(2,1)S(1)}, bf16[64,1152]{1,0:T(8,128)(2,1)S(1)}, u32[]{:S(2)}, u32[]{:S(2)}) collective-permute-start(bf16[64,1152]{1,0:T(8,128)(2,1)S(1)} %get-tuple-element.54), channel_id=1, source_target_pairs={{0,6},{1,7},{2,4},{3,5},{4,2},{5,3},{6,0},{7,1},{8,14},{9,15},{10,... | collective-permute-start | bytes 442376 | tf_op jit(solution)/shard_map/ppermute | solution.py:250
  52.8 3.8 %collective-permute-done.17.refs_3_ = bf16[64,1152]{1,0:T(8,128)(2,1)S(1)} collective-permute-done((bf16[64,1152]{1,0:T(8,128)(2,1)S(1)}, bf16[64,1152]{1,0:T(8,128)(2,1)S(1)}, u32[]{:S(2)}, u32[]{:S(2)}) %collective-permute-start.17) | collective-permute-done | bytes 147488 | tf_op jit(solution)/shard_map/ppermute | solution.py:227
  56.6 1.5 %collective-permute-done.18.refs_5_ = bf16[64,1152]{1,0:T(8,128)(2,1)S(1)} collective-permute-done((bf16[64,1152]{1,0:T(8,128)(2,1)S(1)}, bf16[64,1152]{1,0:T(8,128)(2,1)S(1)}, u32[]{:S(2)}, u32[]{:S(2)}) %collective-permute-start.18) | collective-permute-done | bytes 147488 | tf_op jit(solution)/shard_map/ppermute | solution.py:250
  58.6 4.3 %collective-permute-start.21 = (bf16[32,1152]{1,0:T(8,128)(2,1)S(1)}, bf16[32,1152]{1,0:T(8,128)(2,1)S(1)}, u32[]{:S(2)}, u32[]{:S(2)}) collective-permute-start(bf16[32,1152]{1,0:T(8,128)(2,1)S(1)} %get-tuple-element.57), channel_id=1, source_target_pairs={{0,8},{4,12},{8,0},{12,4},{16,24},{20,28},{24,16},{28,20},{1,9},{5... | collective-permute-start | bytes 221192 | tf_op jit(solution)/shard_map/ppermute | solution.py:227
  62.9 1.8 %collective-permute-done.19.refs_0_ = bf16[32,1152]{1,0:T(8,128)(2,1)S(1)} collective-permute-done((bf16[32,1152]{1,0:T(8,128)(2,1)S(1)}, bf16[32,1152]{1,0:T(8,128)(2,1)S(1)}, u32[]{:S(2)}, u32[]{:S(2)}) %collective-permute-start.19) | collective-permute-done | bytes 73760 | tf_op jit(solution)/shard_map/ppermute | solution.py:227
  64.7 0.8 %collective-permute-done.21.refs_2_ = bf16[32,1152]{1,0:T(8,128)(2,1)S(1)} collective-permute-done((bf16[32,1152]{1,0:T(8,128)(2,1)S(1)}, bf16[32,1152]{1,0:T(8,128)(2,1)S(1)}, u32[]{:S(2)}, u32[]{:S(2)}) %collective-permute-start.21) | collective-permute-done | bytes 73760 | tf_op jit(solution)/shard_map/ppermute | solution.py:227
  65.5 0.8 %shard_map.73 = bf16[8,16,1152]{2,1,0:T(8,128)(2,1)} custom-call(f32[6,1152]{1,0:T(8,128)S(1)} %copy-done.8, bf16[4,16,1152]{2,1,0:T(8,128)(2,1)S(1)} %get-tuple-element.41.kept_ref, bf16[4,16,1152]{2,1,0:T(8,128)(2,1)S(1)} %collective-permute-done.12.other_ref, bf16[32,1152]{1,0:T(8,128)(2,1)S(1)} %collective-permute-done.19.refs_0_, ...), custom_call_target="tpu_custom_call" | custom-call | flops 1 | bytes 1 | tf_op jit(solution)/shard_map/pallas_call | solution.py:214
  (40 shorter events, 3.2 us)
Async XLA Ops:
  0.0 3.0 %collective-permute-start = (bf16[1,128,1152]{2,1,0:T(8,128)(2,1)}, bf16[1,128,1152]{2,1,0:T(8,128)(2,1)S(1)}, u32[]{:S(2)}, u32[]{:S(2)}) collective-permute-start(bf16[1,128,1152]{2,1,0:T(8,128)(2,1)} %own_ref.3), channel_id=1, source_target_pairs={{0,1},{1,0},{2,3},{3,2},{4,5},{5,4},{6,7},{7,6},{8,9},{9,8},{10,11... | collective-permute-start | bytes 884744 | tf_op jit(solution)/shard_map/ppermute | solution.py:227
  0.5 10.4 %collective-permute-start.3 = (bf16[1,128,1152]{2,1,0:T(8,128)(2,1)}, bf16[1,128,1152]{2,1,0:T(8,128)(2,1)S(1)}, u32[]{:S(2)}, u32[]{:S(2)}) collective-permute-start(bf16[1,128,1152]{2,1,0:T(8,128)(2,1)} %own_ref.3), channel_id=1, source_target_pairs={{0,2},{1,3},{2,0},{3,1},{4,6},{5,7},{6,4},{7,5},{8,10},{9,11},{10,... | collective-permute-start | bytes 884744 | tf_op jit(solution)/shard_map/ppermute | solution.py:227
  3.0 1.0 %copy-start.4 = (bf16[1,128,1152]{2,1,0:T(8,128)(2,1)S(1)}, bf16[1,128,1152]{2,1,0:T(8,128)(2,1)}, u32[]{:S(2)}) copy-start(bf16[1,128,1152]{2,1,0:T(8,128)(2,1)} %own_ref.3) | copy-start | bytes 884740
  4.0 6.8 %collective-permute-start.1 = (bf16[64,1152]{1,0:T(8,128)(2,1)S(1)}, bf16[64,1152]{1,0:T(8,128)(2,1)S(1)}, u32[]{:S(2)}, u32[]{:S(2)}) collective-permute-start(bf16[64,1152]{1,0:T(8,128)(2,1)S(1)} %shard_map.64), channel_id=1, source_target_pairs={{0,4},{4,0},{8,12},{12,8},{16,20},{20,16},{24,28},{28,24},{1,5},{5... | collective-permute-start | bytes 442376 | tf_op jit(solution)/shard_map/ppermute | solution.py:227
  5.8 1.6 %copy-start = (bf16[864,1152]{1,0:T(8,128)(2,1)S(1)}, bf16[864,1152]{1,0:T(8,128)(2,1)}, u32[]{:S(2)}) copy-start(bf16[864,1152]{1,0:T(8,128)(2,1)} %weight_ref.3) | copy-start | bytes 5971972
  7.4 0.8 %copy-start.7 = (f32[6,1152]{1,0:T(8,128)S(1)}, f32[6,1152]{1,0:T(8,128)}, u32[]{:S(2)}) copy-start(f32[6,1152]{1,0:T(8,128)} %mod_ref.7) | copy-start | bytes 82948
  8.1 4.4 %copy-start.6 = (bf16[288,1152]{1,0:T(8,128)(2,1)S(1)}, bf16[288,1152]{1,0:T(8,128)(2,1)}, u32[]{:S(2)}) copy-start(bf16[288,1152]{1,0:T(8,128)(2,1)} %refs_0_.4) | copy-start | bytes 1990660
  8.1 4.8 %copy-start.1 = (bf16[864,1152]{1,0:T(8,128)(2,1)S(1)}, bf16[864,1152]{1,0:T(8,128)(2,1)}, u32[]{:S(2)}) copy-start(bf16[864,1152]{1,0:T(8,128)(2,1)} %weight_ref.3) | copy-start | bytes 5971972
  9.2 9.2 %copy-start.3 = (bf16[288,1152]{1,0:T(8,128)(2,1)S(1)}, bf16[288,1152]{1,0:T(8,128)(2,1)}, u32[]{:S(2)}) copy-start(bf16[288,1152]{1,0:T(8,128)(2,1)} %refs_0_.7) | copy-start | bytes 1990660
  9.3 18.8 %copy-start.5 = (bf16[1,128,1152]{2,1,0:T(8,128)(2,1)S(1)}, bf16[1,128,1152]{2,1,0:T(8,128)(2,1)}, u32[]{:S(2)}) copy-start(bf16[1,128,1152]{2,1,0:T(8,128)(2,1)} %own_ref.3) | copy-start | bytes 884740
  10.9 1.6 %collective-permute-start.4 = (bf16[1,128,1152]{2,1,0:T(8,128)(2,1)S(1)}, bf16[1,128,1152]{2,1,0:T(8,128)(2,1)S(1)}, u32[]{:S(2)}, u32[]{:S(2)}) collective-permute-start(bf16[1,128,1152]{2,1,0:T(8,128)(2,1)S(1)} %collective-permute-done.3.refs_0_), channel_id=1, source_target_pairs={{0,1},{1,0},{2,3},{3,2},{4,5},{5,4},{6,7},{7,6},{8,9},{9,8},{10,11... | collective-permute-start | bytes 884744 | tf_op jit(solution)/shard_map/ppermute | solution.py:227
  12.4 27.7 %collective-permute-start.14 = (bf16[864,1152]{1,0:T(8,128)(2,1)}, bf16[864,1152]{1,0:T(8,128)(2,1)S(1)}, u32[]{:S(2)}, u32[]{:S(2)}) collective-permute-start(bf16[864,1152]{1,0:T(8,128)(2,1)} %refs_0_.6), channel_id=1, source_target_pairs={{0,1},{1,0},{2,3},{3,2},{4,5},{5,4},{6,7},{7,6},{8,9},{9,8},{10,11... | collective-permute-start | bytes 5971976 | tf_op jit(solution)/shard_map/ppermute | solution.py:227
  12.6 5.1 %collective-permute-start.2 = (bf16[288,1152]{1,0:T(8,128)(2,1)S(1)}, bf16[288,1152]{1,0:T(8,128)(2,1)S(1)}, u32[]{:S(2)}, u32[]{:S(2)}) collective-permute-start(bf16[288,1152]{1,0:T(8,128)(2,1)S(1)} %copy-done.6), channel_id=1, source_target_pairs={{0,1},{1,0},{2,3},{3,2},{4,5},{5,4},{6,7},{7,6},{8,9},{9,8},{10,11... | collective-permute-start | bytes 1990664 | tf_op jit(solution)/shard_map/ppermute | solution.py:227
  16.3 1.4 %collective-permute-start.5 = (bf16[288,256]{1,0:T(8,128)(2,1)S(1)}, bf16[288,256]{1,0:T(8,128)(2,1)S(1)}, u32[]{:S(2)}, u32[]{:S(2)}) collective-permute-start(bf16[288,256]{1,0:T(8,128)(2,1)S(1)} %get-tuple-element.36), channel_id=1, source_target_pairs={{0,1},{1,0},{2,3},{3,2},{4,5},{5,4},{6,7},{7,6},{8,9},{9,8},{10,11... | collective-permute-start | bytes 442376 | tf_op jit(solution)/shard_map/ppermute | solution.py:227
  17.7 22.4 %copy-start.2 = (bf16[864,1152]{1,0:T(8,128)(2,1)S(1)}, bf16[864,1152]{1,0:T(8,128)(2,1)}, u32[]{:S(2)}) copy-start(bf16[864,1152]{1,0:T(8,128)(2,1)} %refs_0_.6) | copy-start | bytes 5971972
  18.5 21.6 %collective-permute-start.13 = (bf16[288,1152]{1,0:T(8,128)(2,1)S(1)}, bf16[288,1152]{1,0:T(8,128)(2,1)S(1)}, u32[]{:S(2)}, u32[]{:S(2)}) collective-permute-start(bf16[288,1152]{1,0:T(8,128)(2,1)S(1)} %copy-done.3), channel_id=1, source_target_pairs={{0,1},{1,0},{2,3},{3,2},{4,5},{5,4},{6,7},{7,6},{8,9},{9,8},{10,11... | collective-permute-start | bytes 1990664 | tf_op jit(solution)/shard_map/ppermute | solution.py:227
  18.7 9.1 %collective-permute-start.6 = (bf16[64,1152]{1,0:T(8,128)(2,1)S(1)}, bf16[64,1152]{1,0:T(8,128)(2,1)S(1)}, u32[]{:S(2)}, u32[]{:S(2)}) collective-permute-start(bf16[64,1152]{1,0:T(8,128)(2,1)S(1)} %get-tuple-element.38), channel_id=1, source_target_pairs={{0,2},{1,3},{2,0},{3,1},{4,6},{5,7},{6,4},{7,5},{8,10},{9,11},{10,... | collective-permute-start | bytes 442376 | tf_op jit(solution)/shard_map/ppermute | solution.py:227
  20.4 7.6 %collective-permute-start.8 = (bf16[64,1152]{1,0:T(8,128)(2,1)S(1)}, bf16[64,1152]{1,0:T(8,128)(2,1)S(1)}, u32[]{:S(2)}, u32[]{:S(2)}) collective-permute-start(bf16[64,1152]{1,0:T(8,128)(2,1)S(1)} %get-tuple-element.40), channel_id=1, source_target_pairs={{0,6},{1,7},{2,4},{3,5},{4,2},{5,3},{6,0},{7,1},{8,14},{9,15},{10,... | collective-permute-start | bytes 442376 | tf_op jit(solution)/shard_map/ppermute | solution.py:250
  21.9 5.9 %collective-permute-start.7 = (bf16[64,576]{1,0:T(8,128)(2,1)S(1)}, bf16[64,576]{1,0:T(8,128)(2,1)S(1)}, u32[]{:S(2)}, u32[]{:S(2)}) collective-permute-start(bf16[64,576]{1,0:T(8,128)(2,1)S(1)} %get-tuple-element.39), channel_id=1, source_target_pairs={{0,4},{4,0},{8,12},{12,8},{16,20},{20,16},{24,28},{28,24},{1,5},{5... | collective-permute-start | bytes 221192 | tf_op jit(solution)/shard_map/ppermute | solution.py:227
  28.8 6.7 %collective-permute-start.9 = (bf16[32,1152]{1,0:T(8,128)(2,1)S(1)}, bf16[32,1152]{1,0:T(8,128)(2,1)S(1)}, u32[]{:S(2)}, u32[]{:S(2)}) collective-permute-start(bf16[32,1152]{1,0:T(8,128)(2,1)S(1)} %get-tuple-element.43), channel_id=1, source_target_pairs={{0,24},{4,28},{8,16},{12,20},{16,8},{20,12},{24,0},{28,4},{1,25},{... | collective-permute-start | bytes 221192 | tf_op jit(solution)/shard_map/ppermute | solution.py:227
  32.5 5.7 %collective-permute-start.10 = (bf16[32,1152]{1,0:T(8,128)(2,1)S(1)}, bf16[32,1152]{1,0:T(8,128)(2,1)S(1)}, u32[]{:S(2)}, u32[]{:S(2)}) collective-permute-start(bf16[32,1152]{1,0:T(8,128)(2,1)S(1)} %get-tuple-element.44), channel_id=1, source_target_pairs={{0,16},{4,20},{8,24},{12,28},{16,0},{20,4},{24,8},{28,12},{1,17},{... | collective-permute-start | bytes 221192 | tf_op jit(solution)/shard_map/ppermute | solution.py:227
  32.5 5.7 %collective-permute-start.11 = (bf16[32,1152]{1,0:T(8,128)(2,1)S(1)}, bf16[32,1152]{1,0:T(8,128)(2,1)S(1)}, u32[]{:S(2)}, u32[]{:S(2)}) collective-permute-start(bf16[32,1152]{1,0:T(8,128)(2,1)S(1)} %get-tuple-element.45), channel_id=1, source_target_pairs={{0,8},{4,12},{8,0},{12,4},{16,24},{20,28},{24,16},{28,20},{1,9},{5... | collective-permute-start | bytes 221192 | tf_op jit(solution)/shard_map/ppermute | solution.py:227
  38.3 8.9 %collective-permute-start.15 = (bf16[128,1152]{1,0:T(8,128)(2,1)S(1)}, bf16[128,1152]{1,0:T(8,128)(2,1)S(1)}, u32[]{:S(2)}, u32[]{:S(2)}) collective-permute-start(bf16[128,1152]{1,0:T(8,128)(2,1)S(1)} %shard_map.69.refs_4_), channel_id=1, source_target_pairs={{0,2},{1,3},{2,0},{3,1},{4,6},{5,7},{6,4},{7,5},{8,10},{9,11},{10,... | collective-permute-start | bytes 884744 | tf_op jit(solution)/shard_map/ppermute | solution.py:227
  42.0 5.2 %collective-permute-start.16 = (bf16[64,576]{1,0:T(8,128)(2,1)S(1)}, bf16[64,576]{1,0:T(8,128)(2,1)S(1)}, u32[]{:S(2)}, u32[]{:S(2)}) collective-permute-start(bf16[64,576]{1,0:T(8,128)(2,1)S(1)} %get-tuple-element.51), channel_id=1, source_target_pairs={{0,4},{4,0},{8,12},{12,8},{16,20},{20,16},{24,28},{28,24},{1,5},{5... | collective-permute-start | bytes 221192 | tf_op jit(solution)/shard_map/ppermute | solution.py:227
  49.2 16.3 %copy-start.8 = (f32[6,1152]{1,0:T(8,128)S(1)}, f32[6,1152]{1,0:T(8,128)}, u32[]{:S(2)}) copy-start(f32[6,1152]{1,0:T(8,128)} %mod_ref.7) | copy-start | bytes 82948
  49.2 7.3 %collective-permute-start.17 = (bf16[64,1152]{1,0:T(8,128)(2,1)S(1)}, bf16[64,1152]{1,0:T(8,128)(2,1)S(1)}, u32[]{:S(2)}, u32[]{:S(2)}) collective-permute-start(bf16[64,1152]{1,0:T(8,128)(2,1)S(1)} %get-tuple-element.53), channel_id=1, source_target_pairs={{0,2},{1,3},{2,0},{3,1},{4,6},{5,7},{6,4},{7,5},{8,10},{9,11},{10,... | collective-permute-start | bytes 442376 | tf_op jit(solution)/shard_map/ppermute | solution.py:227
  51.0 7.1 %collective-permute-start.18 = (bf16[64,1152]{1,0:T(8,128)(2,1)S(1)}, bf16[64,1152]{1,0:T(8,128)(2,1)S(1)}, u32[]{:S(2)}, u32[]{:S(2)}) collective-permute-start(bf16[64,1152]{1,0:T(8,128)(2,1)S(1)} %get-tuple-element.54), channel_id=1, source_target_pairs={{0,6},{1,7},{2,4},{3,5},{4,2},{5,3},{6,0},{7,1},{8,14},{9,15},{10,... | collective-permute-start | bytes 442376 | tf_op jit(solution)/shard_map/ppermute | solution.py:250
  52.2 10.7 %collective-permute-start.12 = (bf16[4,16,1152]{2,1,0:T(8,128)(2,1)S(1)}, bf16[4,16,1152]{2,1,0:T(8,128)(2,1)S(1)}, u32[]{:S(2)}, u32[]{:S(2)}) collective-permute-start(bf16[4,16,1152]{2,1,0:T(8,128)(2,1)S(1)} %get-tuple-element.47), channel_id=1, source_target_pairs={{0,4},{4,0},{8,12},{12,8},{16,20},{20,16},{24,28},{28,24},{1,5},{5... | collective-permute-start | bytes 442376 | tf_op jit(solution)/shard_map/ppermute | solution.py:227
  58.5 6.2 %collective-permute-start.19 = (bf16[32,1152]{1,0:T(8,128)(2,1)S(1)}, bf16[32,1152]{1,0:T(8,128)(2,1)S(1)}, u32[]{:S(2)}, u32[]{:S(2)}) collective-permute-start(bf16[32,1152]{1,0:T(8,128)(2,1)S(1)} %get-tuple-element.55), channel_id=1, source_target_pairs={{0,24},{4,28},{8,16},{12,20},{16,8},{20,12},{24,0},{28,4},{1,25},{... | collective-permute-start | bytes 221192 | tf_op jit(solution)/shard_map/ppermute | solution.py:227
  58.6 6.2 %collective-permute-start.20 = (bf16[32,1152]{1,0:T(8,128)(2,1)S(1)}, bf16[32,1152]{1,0:T(8,128)(2,1)S(1)}, u32[]{:S(2)}, u32[]{:S(2)}) collective-permute-start(bf16[32,1152]{1,0:T(8,128)(2,1)S(1)} %get-tuple-element.56), channel_id=1, source_target_pairs={{0,16},{4,20},{8,24},{12,28},{16,0},{20,4},{24,8},{28,12},{1,17},{... | collective-permute-start | bytes 221192 | tf_op jit(solution)/shard_map/ppermute | solution.py:227
  58.6 6.8 %collective-permute-start.21 = (bf16[32,1152]{1,0:T(8,128)(2,1)S(1)}, bf16[32,1152]{1,0:T(8,128)(2,1)S(1)}, u32[]{:S(2)}, u32[]{:S(2)}) collective-permute-start(bf16[32,1152]{1,0:T(8,128)(2,1)S(1)} %get-tuple-element.57), channel_id=1, source_target_pairs={{0,8},{4,12},{8,0},{12,4},{16,24},{20,28},{24,16},{28,20},{1,9},{5... | collective-permute-start | bytes 221192 | tf_op jit(solution)/shard_map/ppermute | solution.py:227

commit v13 on v12

--- a/solution.py
+++ b/solution.py
@@ -118,15 +118,15 @@
             ref[...] = part.astype(ref.dtype)
 
 
-def total_updates(groups, weight_refs, refs):
-    kept = sum(ref[...].astype(F32) for ref in refs[:groups])
-    paired = dot(refs[groups][...], joined(weight_refs))
-    return kept, paired + sum(ref[...].astype(F32) for ref in refs[groups + 1 : 2 * groups])
-
-
-def middle_kernel(pieces, groups, mod_ref, own_ref, paired_ref, *refs):
-    kept_ref, sent_ref, *piece_refs, scratch = refs[2 + 2 * groups :]
-    updates = total_updates(groups, refs[:2], refs[2:])
+def total_updates(count, weight_refs, refs):
+    kept = sum(ref[...].astype(F32) for ref in refs[:count])
+    paired = dot(refs[count][...], joined(weight_refs))
+    return kept, paired + sum(ref[...].astype(F32) for ref in refs[count + 1 : 2 * count])
+
+
+def middle_kernel(pieces, count, mod_ref, own_ref, paired_ref, *refs):
+    kept_ref, sent_ref, *piece_refs, scratch = refs[2 + 2 * count :]
+    updates = total_updates(count, refs[:2], refs[2:])
     _, period, width = kept_ref.shape
     inputs = (of_this_half(own_ref[0], period)[0], paired_ref[...])
     for at, (tokens, middle_ref) in enumerate(zip(inputs, (kept_ref, sent_ref))):
@@ -186,10 +186,10 @@
             ref[...] = half.astype(ref.dtype)
 
 
-def sum_kernel(groups, *refs):
-    piece_refs = refs[2 + 2 * groups :]
+def sum_kernel(count, *refs):
+    piece_refs = refs[2 + 2 * count :]
     period = piece_refs[0].shape[0] // 2
-    for at, update in enumerate(total_updates(groups, refs[:2], refs[2:])):
+    for at, update in enumerate(total_updates(count, refs[:2], refs[2:])):
         update = update.astype(BF16)
         for piece, ref in enumerate(piece_refs):
             rows = update[piece * period : (piece + 1) * period]
@@ -240,12 +240,13 @@
     return [part for block in blocks for part in (block, swap(block, "patch", 1))]
 
 
-def swap_diagonal(value, offset):
+def swap_far(value, offset, paired, cores=(0, 1)):
     frames, size = lax.axis_size("frame"), lax.axis_size("patch")
     pairs = [
-        (frame * size + at, (frame ^ 1) * size + (at ^ offset))
+        (frame * size + at, (frame ^ paired) * size + (at ^ offset))
         for frame in range(frames)
         for at in range(size)
+        if at % 2 in cores
     ]
     return lax.ppermute(value, ("frame", "patch"), pairs)
 
@@ -265,10 +266,11 @@
         offsets = reversed(range(pieces))
         return [swap(part, "frame", 2 * at) if at else part for at, part in zip(offsets, parts)]
 
-    def return_updates(own, far):
-        same = [swap(part, "patch", 2 * at) for at, part in enumerate(far[::2], 1)]
-        diagonal = [swap_diagonal(part, 2 * at) for at, part in enumerate(far[1::2], 1)]
-        return [own[0], *same, own[1], *diagonal]
+    def swap_updates(far, cores=(0, 1)):
+        return [
+            [swap_far(part, 2 * at, paired, cores) for at, part in enumerate(far[paired::2], 1)]
+            for paired in range(2)
+        ]
 
     def halves_shape(dtype):
         return shape((rows // 2, width), dtype)
@@ -304,9 +306,13 @@
         own_shapes + far_shapes,
     )
     late_pair = with_sister(temporal_out, parts[0])
-    updates = return_updates((parts[0], swap(parts[1], "frame", 1)), parts[2:])
+    odd = swap_updates(parts[2:], (1,))
+    turns = [(at, at ^ 1) for at in range(1, count, 2)]
+    turn = lax.ppermute(after(modulation, *odd[0]), "patch", turns)
+    even = swap_updates([after(part, turn) for part in parts[2:]], (0,))
+    updates = [parts[0], *odd[0], *even[0], swap(parts[1], "frame", 1), *odd[1], *even[1]]
     middle, middle_sent, *parts = call(
-        functools.partial(middle_kernel, pieces, groups),
+        functools.partial(middle_kernel, pieces, 2 * groups - 1),
         (modulation, tokens, paired, *out_pair, *updates),
         [shape((pieces, period, width), BF16)] * 2 + piece_shapes,
         [pltpu.VMEM((pieces, 2 * period, width), BF16)],
@@ -329,7 +335,8 @@
     middle_other = swap(after(middle_sent, segment), "frame", 1)
     others = [after(block, received) for block in segments[1:]]
     far_parts = attend_frames(False, others, far_shapes)
-    updates = return_updates((kept, received), far_parts)
+    same, diagonal = swap_updates(far_parts)
+    updates = [kept, *same, received, *diagonal]
     parts = call(
         functools.partial(sum_kernel, groups),
         (*late_pair, *updates),

time: 66.6 us -> 76.5 us (1.15)
  starting transfers between devices: 25 us -> 31.8 us
  waiting for transfers between devices: 26.8 us -> 29.8 us
    ppermute x2 -> x7, starting transfers between devices: 2.62 us -> 12.7 us  [the longest x6 11.4 us: swap_far(): return lax.ppermute(value, ('frame', 'patch'), pairs)]
    ppermute x2 -> x7, waiting for transfers between devices: 1.8 us -> 11.6 us  [the longest x6 7.82 us: swap_far(): return lax.ppermute(value, ('frame', 'patch'), pairs)]
    ppermute x20 -> x18, waiting for transfers between devices: 25 us -> 18.2 us  [swap(): return lax.ppermute(value, axis, [(at, at ^ offset) for at in range(size)])]
    ppermute x20 -> x18, starting transfers between devices: 22.4 us -> 19 us  [swap(): return lax.ppermute(value, axis, [(at, at ^ offset) for at in range(size)])]
  transfers between devices with their start and end apart: 22 -> 25, of which waited for: 12 -> 12; matrix products, arithmetic and copies ran while one was open for 0% -> 0% of each run, Pallas kernels for 12% -> 11%
where the time goes in v13:
time: 76.5 us; the launch traced here: 76.2 us
  starting transfers between devices  31.8 us (42%)
  waiting for transfers between devices  29.8 us (39%)
  Pallas kernels  11 us (14%)
  local copies, waits for them, and re-layouts  3.34 us (4%)
    ppermute x18, starting transfers between devices, swap(): return lax.ppermute(value, axis, [(at, at ^ offset) for at in range(size)])  19 us
    ppermute x18, waiting for transfers between devices, swap(): return lax.ppermute(value, axis, [(at, at ^ offset) for at in range(size)])  18.2 us
    ppermute x6, starting transfers between devices, swap_far(): return lax.ppermute(value, ('frame', 'patch'), pairs)  11.4 us
    pallas_call x10, Pallas kernels, call(): pl.pallas_call(body, out_shape=outs, in_specs=[pl.BlockSpec(memory_space=...  11 us
    ppermute x6, waiting for transfers between devices, swap_far(): return lax.ppermute(value, ('frame', 'patch'), pairs)  7.82 us
    ppermute x1, waiting for transfers between devices, per_device(): turn = lax.ppermute(after(modulation, *odd[0]), 'patch', turns)  3.78 us
    unnamed x18, local copies, waits for them, and re-layouts  3.34 us
  transfers between devices with their start and end apart: 25, of which 12 were waited for; matrix products, arithmetic and copies ran while one was open for 0% of the time, Pallas kernels for 11%

profile of v13, /device:TPU:0, one launch (start us, length us, event | category | flops | bytes accessed | tf_op | source)
XLA Modules:
  0.0 76.2 jit_solution(1582708745556250568)
XLA Ops:
  0.5 2.5 %collective-permute-start.3 = (bf16[1,128,1152]{2,1,0:T(8,128)(2,1)}, bf16[1,128,1152]{2,1,0:T(8,128)(2,1)S(1)}, u32[]{:S(2)}, u32[]{:S(2)}) collective-permute-start(bf16[1,128,1152]{2,1,0:T(8,128)(2,1)} %own_ref.3), channel_id=1, source_target_pairs={{0,2},{1,3},{2,0},{3,1},{4,6},{5,7},{6,4},{7,5},{8,10},{9,11},{10,... | collective-permute-start | bytes 884744 | tf_op jit(solution)/shard_map/ppermute | solution.py:227
  3.0 1.0 %copy-done.5 = bf16[1,128,1152]{2,1,0:T(8,128)(2,1)S(1)} copy-done((bf16[1,128,1152]{2,1,0:T(8,128)(2,1)S(1)}, bf16[1,128,1152]{2,1,0:T(8,128)(2,1)}, u32[]{:S(2)}) %copy-start.5) | copy-done | bytes 294936
  4.0 1.8 %collective-permute-start.1 = (bf16[64,1152]{1,0:T(8,128)(2,1)S(1)}, bf16[64,1152]{1,0:T(8,128)(2,1)S(1)}, u32[]{:S(2)}, u32[]{:S(2)}) collective-permute-start(bf16[64,1152]{1,0:T(8,128)(2,1)S(1)} %shard_map.64), channel_id=1, source_target_pairs={{0,4},{4,0},{8,12},{12,8},{16,20},{20,16},{24,28},{28,24},{1,5},{5... | collective-permute-start | bytes 442376 | tf_op jit(solution)/shard_map/ppermute | solution.py:227
  5.8 1.6 %copy-done = bf16[864,1152]{1,0:T(8,128)(2,1)S(1)} copy-done((bf16[864,1152]{1,0:T(8,128)(2,1)S(1)}, bf16[864,1152]{1,0:T(8,128)(2,1)}, u32[]{:S(2)}) %copy-start) | copy-done | bytes 1990680
  8.1 1.1 %shard_map.65.near_ref = f32[864,256]{1,0:T(8,128)S(1)} custom-call(f32[6,1152]{1,0:T(8,128)S(1)} %copy-done.7, bf16[864,1152]{1,0:T(8,128)(2,1)S(1)} %copy-done, bf16[1,128,1152]{2,1,0:T(8,128)(2,1)S(1)} %copy-done.5, bf16[1,128,1152]{2,1,0:T(8,128)(2,1)S(1)} %collective-permute-done.sister_ref), custom_call_target="tpu_custom_call" | custom-call | flops 1 | bytes 1 | tf_op jit(solution)/shard_map/pallas_call | solution.py:214
  9.3 1.6 %collective-permute-done.3.refs_0_ = bf16[1,128,1152]{2,1,0:T(8,128)(2,1)S(1)} collective-permute-done((bf16[1,128,1152]{2,1,0:T(8,128)(2,1)}, bf16[1,128,1152]{2,1,0:T(8,128)(2,1)S(1)}, u32[]{:S(2)}, u32[]{:S(2)}) %collective-permute-start.3) | collective-permute-done | bytes 294944 | tf_op jit(solution)/shard_map/ppermute | solution.py:227
  10.9 1.6 %collective-permute-done.4.refs_1_ = bf16[1,128,1152]{2,1,0:T(8,128)(2,1)S(1)} collective-permute-done((bf16[1,128,1152]{2,1,0:T(8,128)(2,1)S(1)}, bf16[1,128,1152]{2,1,0:T(8,128)(2,1)S(1)}, u32[]{:S(2)}, u32[]{:S(2)}) %collective-permute-start.4) | collective-permute-done | bytes 294944 | tf_op jit(solution)/shard_map/ppermute | solution.py:227
  13.0 3.3 %shard_map.66 = (bf16[288,256]{1,0:T(8,128)(2,1)S(1)}, bf16[288,256]{1,0:T(8,128)(2,1)S(1)}) custom-call(f32[6,1152]{1,0:T(8,128)S(1)} %copy-done.7, bf16[864,1152]{1,0:T(8,128)(2,1)S(1)} %copy-done.1, f32[864,256]{1,0:T(8,128)S(1)} %shard_map.65.near_ref, bf16[1,128,1152]{2,1,0:T(8,128)(2,1)S(1)} %collective-permute-done.3.refs_0_, ...), custom_call_target="tpu_custom_call" | custom-call | flops 1 | bytes 1 | tf_op jit(solution)/shard_map/pallas_call | solution.py:214
  16.5 1.2 %collective-permute-done.5.refs_1_ = bf16[288,256]{1,0:T(8,128)(2,1)S(1)} collective-permute-done((bf16[288,256]{1,0:T(8,128)(2,1)S(1)}, bf16[288,256]{1,0:T(8,128)(2,1)S(1)}, u32[]{:S(2)}, u32[]{:S(2)}) %collective-permute-start.5) | collective-permute-done | bytes 147488 | tf_op jit(solution)/shard_map/ppermute | solution.py:227
  18.7 0.8 %collective-permute-start.6 = (bf16[64,1152]{1,0:T(8,128)(2,1)S(1)}, bf16[64,1152]{1,0:T(8,128)(2,1)S(1)}, u32[]{:S(2)}, u32[]{:S(2)}) collective-permute-start(bf16[64,1152]{1,0:T(8,128)(2,1)S(1)} %get-tuple-element.43), channel_id=1, source_target_pairs={{1,3},{3,1},{5,7},{7,5},{9,11},{11,9},{13,15},{15,13},{17,19},{19,... | collective-permute-start | bytes 442376 | tf_op jit(solution)/shard_map/ppermute | solution.py:251
  19.5 1.8 %collective-permute-start.9 = (bf16[64,576]{1,0:T(8,128)(2,1)S(1)}, bf16[64,576]{1,0:T(8,128)(2,1)S(1)}, u32[]{:S(2)}, u32[]{:S(2)}) collective-permute-start(bf16[64,576]{1,0:T(8,128)(2,1)S(1)} %get-tuple-element.44), channel_id=1, source_target_pairs={{0,4},{4,0},{8,12},{12,8},{16,20},{20,16},{24,28},{28,24},{1,5},{5... | collective-permute-start | bytes 221192 | tf_op jit(solution)/shard_map/ppermute | solution.py:227
  21.3 1.3 %collective-permute-start.7 = (bf16[6,1152]{1,0:T(8,128)(2,1)S(1)}, bf16[6,1152]{1,0:T(8,128)(2,1)S(1)}, u32[]{:S(2)}, u32[]{:S(2)}) collective-permute-start(bf16[6,1152]{1,0:T(8,128)(2,1)S(1)} %convert), channel_id=1, source_target_pairs={{1,0},{3,2},{5,4},{7,6},{9,8},{11,10},{13,12},{15,14},{17,16},{19,... | collective-permute-start | bytes 41480 | tf_op jit(solution)/shard_map/ppermute | solution.py:311
  23.2 3.8 %collective-permute-done.7 = bf16[6,1152]{1,0:T(8,128)(2,1)S(1)} collective-permute-done((bf16[6,1152]{1,0:T(8,128)(2,1)S(1)}, bf16[6,1152]{1,0:T(8,128)(2,1)S(1)}, u32[]{:S(2)}, u32[]{:S(2)}) %collective-permute-start.7) | collective-permute-done | bytes 13856 | tf_op jit(solution)/shard_map/ppermute | solution.py:311
  27.0 3.6 %collective-permute-start.8 = (bf16[64,1152]{1,0:T(8,128)(2,1)S(1)}, bf16[64,1152]{1,0:T(8,128)(2,1)S(1)}, u32[]{:S(2)}, u32[]{:S(2)}) collective-permute-start(bf16[64,1152]{1,0:T(8,128)(2,1)S(1)} %get-tuple-element.43), channel_id=1, source_target_pairs={{0,2},{2,0},{4,6},{6,4},{8,10},{10,8},{12,14},{14,12},{16,18},{18,... | collective-permute-start | bytes 442376 | tf_op jit(solution)/shard_map/ppermute | solution.py:251
  30.7 3.3 %collective-permute-start.11 = (bf16[64,1152]{1,0:T(8,128)(2,1)S(1)}, bf16[64,1152]{1,0:T(8,128)(2,1)S(1)}, u32[]{:S(2)}, u32[]{:S(2)}) collective-permute-start(bf16[64,1152]{1,0:T(8,128)(2,1)S(1)} %get-tuple-element.46), channel_id=1, source_target_pairs={{0,6},{2,4},{4,2},{6,0},{8,14},{10,12},{12,10},{14,8},{16,22},{18,... | collective-permute-start | bytes 442376 | tf_op jit(solution)/shard_map/ppermute | solution.py:251
  34.0 0.9 %collective-permute-done.8.refs_4_ = bf16[64,1152]{1,0:T(8,128)(2,1)S(1)} collective-permute-done((bf16[64,1152]{1,0:T(8,128)(2,1)S(1)}, bf16[64,1152]{1,0:T(8,128)(2,1)S(1)}, u32[]{:S(2)}, u32[]{:S(2)}) %collective-permute-start.8) | collective-permute-done | bytes 147488 | tf_op jit(solution)/shard_map/ppermute | solution.py:251
  34.9 3.7 %collective-permute-done.11.refs_7_ = bf16[64,1152]{1,0:T(8,128)(2,1)S(1)} collective-permute-done((bf16[64,1152]{1,0:T(8,128)(2,1)S(1)}, bf16[64,1152]{1,0:T(8,128)(2,1)S(1)}, u32[]{:S(2)}, u32[]{:S(2)}) %collective-permute-start.11) | collective-permute-done | bytes 147488 | tf_op jit(solution)/shard_map/ppermute | solution.py:251
  39.3 3.7 %collective-permute-start.12 = (bf16[32,1152]{1,0:T(8,128)(2,1)S(1)}, bf16[32,1152]{1,0:T(8,128)(2,1)S(1)}, u32[]{:S(2)}, u32[]{:S(2)}) collective-permute-start(bf16[32,1152]{1,0:T(8,128)(2,1)S(1)} %get-tuple-element.49), channel_id=1, source_target_pairs={{0,24},{4,28},{8,16},{12,20},{16,8},{20,12},{24,0},{28,4},{1,25},{... | collective-permute-start | bytes 221192 | tf_op jit(solution)/shard_map/ppermute | solution.py:227
  43.0 0.8 %collective-permute-start.14 = (bf16[32,1152]{1,0:T(8,128)(2,1)S(1)}, bf16[32,1152]{1,0:T(8,128)(2,1)S(1)}, u32[]{:S(2)}, u32[]{:S(2)}) collective-permute-start(bf16[32,1152]{1,0:T(8,128)(2,1)S(1)} %get-tuple-element.51), channel_id=1, source_target_pairs={{0,8},{4,12},{8,0},{12,4},{16,24},{20,28},{24,16},{28,20},{1,9},{5... | collective-permute-start | bytes 221192 | tf_op jit(solution)/shard_map/ppermute | solution.py:227
  43.8 1.8 %collective-permute-done.12.refs_0_ = bf16[32,1152]{1,0:T(8,128)(2,1)S(1)} collective-permute-done((bf16[32,1152]{1,0:T(8,128)(2,1)S(1)}, bf16[32,1152]{1,0:T(8,128)(2,1)S(1)}, u32[]{:S(2)}, u32[]{:S(2)}) %collective-permute-start.12) | collective-permute-done | bytes 73760 | tf_op jit(solution)/shard_map/ppermute | solution.py:227
  45.6 2.7 %collective-permute-done.13.refs_1_ = bf16[32,1152]{1,0:T(8,128)(2,1)S(1)} collective-permute-done((bf16[32,1152]{1,0:T(8,128)(2,1)S(1)}, bf16[32,1152]{1,0:T(8,128)(2,1)S(1)}, u32[]{:S(2)}, u32[]{:S(2)}) %collective-permute-start.13) | collective-permute-done | bytes 73760 | tf_op jit(solution)/shard_map/ppermute | solution.py:227
  48.9 1.9 %shard_map.70 = (f32[64,1152]{1,0:T(8,128)S(1)}, bf16[64,576]{1,0:T(8,128)(2,1)S(1)}) custom-call(bf16[864,1152]{1,0:T(8,128)(2,1)S(1)} %copy-done.2, bf16[864,1152]{1,0:T(8,128)(2,1)S(1)} %collective-permute-done.17.refs_1_, bf16[288,1152]{1,0:T(8,128)(2,1)S(1)} %copy-done.3, bf16[288,1152]{1,0:T(8,128)(2,1)S(1)} %collective-permute-done.16.refs_3_.refs_1_, ...), custom_call_target="tpu_custom_call" | custom-call | flops 1 | bytes 1 | tf_op jit(solution)/shard_map/pallas_call | solution.py:214
  50.8 1.6 %collective-permute-start.19 = (bf16[64,576]{1,0:T(8,128)(2,1)S(1)}, bf16[64,576]{1,0:T(8,128)(2,1)S(1)}, u32[]{:S(2)}, u32[]{:S(2)}) collective-permute-start(bf16[64,576]{1,0:T(8,128)(2,1)S(1)} %get-tuple-element.57), channel_id=1, source_target_pairs={{0,4},{4,0},{8,12},{12,8},{16,20},{20,16},{24,28},{28,24},{1,5},{5... | collective-permute-start | bytes 221192 | tf_op jit(solution)/shard_map/ppermute | solution.py:227
  52.3 5.9 %collective-permute-done.18.refs_4_ = bf16[128,1152]{1,0:T(8,128)(2,1)S(1)} collective-permute-done((bf16[128,1152]{1,0:T(8,128)(2,1)S(1)}, bf16[128,1152]{1,0:T(8,128)(2,1)S(1)}, u32[]{:S(2)}, u32[]{:S(2)}) %collective-permute-start.18) | collective-permute-done | bytes 294944 | tf_op jit(solution)/shard_map/ppermute | solution.py:227
  58.2 2.0 %shard_map.71 = (bf16[64,1152]{1,0:T(8,128)(2,1)S(1)}, bf16[64,1152]{1,0:T(8,128)(2,1)S(1)}) custom-call(bf16[864,1152]{1,0:T(8,128)(2,1)S(1)} %copy-done.2, bf16[864,1152]{1,0:T(8,128)(2,1)S(1)} %collective-permute-done.17.refs_1_, bf16[288,1152]{1,0:T(8,128)(2,1)S(1)} %copy-done.3, bf16[288,1152]{1,0:T(8,128)(2,1)S(1)} %collective-permute-done.16.refs_3_.refs_1_, ...), custom_call_target="tpu_custom_call" | custom-call | flops 1 | bytes 1 | tf_op jit(solution)/shard_map/pallas_call | solution.py:214
  60.8 2.4 %collective-permute-start.21 = (bf16[64,1152]{1,0:T(8,128)(2,1)S(1)}, bf16[64,1152]{1,0:T(8,128)(2,1)S(1)}, u32[]{:S(2)}, u32[]{:S(2)}) collective-permute-start(bf16[64,1152]{1,0:T(8,128)(2,1)S(1)} %get-tuple-element.60), channel_id=1, source_target_pairs={{0,6},{1,7},{2,4},{3,5},{4,2},{5,3},{6,0},{7,1},{8,14},{9,15},{10,... | collective-permute-start | bytes 442376 | tf_op jit(solution)/shard_map/ppermute | solution.py:251
  63.8 3.2 %collective-permute-done.20.refs_3_ = bf16[64,1152]{1,0:T(8,128)(2,1)S(1)} collective-permute-done((bf16[64,1152]{1,0:T(8,128)(2,1)S(1)}, bf16[64,1152]{1,0:T(8,128)(2,1)S(1)}, u32[]{:S(2)}, u32[]{:S(2)}) %collective-permute-start.20) | collective-permute-done | bytes 147488 | tf_op jit(solution)/shard_map/ppermute | solution.py:251
  67.4 1.9 %collective-permute-start.22 = (bf16[32,1152]{1,0:T(8,128)(2,1)S(1)}, bf16[32,1152]{1,0:T(8,128)(2,1)S(1)}, u32[]{:S(2)}, u32[]{:S(2)}) collective-permute-start(bf16[32,1152]{1,0:T(8,128)(2,1)S(1)} %get-tuple-element.61), channel_id=1, source_target_pairs={{0,24},{4,28},{8,16},{12,20},{16,8},{20,12},{24,0},{28,4},{1,25},{... | collective-permute-start | bytes 221192 | tf_op jit(solution)/shard_map/ppermute | solution.py:227
  69.7 2.2 %collective-permute-start.24 = (bf16[32,1152]{1,0:T(8,128)(2,1)S(1)}, bf16[32,1152]{1,0:T(8,128)(2,1)S(1)}, u32[]{:S(2)}, u32[]{:S(2)}) collective-permute-start(bf16[32,1152]{1,0:T(8,128)(2,1)S(1)} %get-tuple-element.63), channel_id=1, source_target_pairs={{0,8},{4,12},{8,0},{12,4},{16,24},{20,28},{24,16},{28,20},{1,9},{5... | collective-permute-start | bytes 221192 | tf_op jit(solution)/shard_map/ppermute | solution.py:227
  71.9 1.8 %collective-permute-done.22.refs_0_ = bf16[32,1152]{1,0:T(8,128)(2,1)S(1)} collective-permute-done((bf16[32,1152]{1,0:T(8,128)(2,1)S(1)}, bf16[32,1152]{1,0:T(8,128)(2,1)S(1)}, u32[]{:S(2)}, u32[]{:S(2)}) %collective-permute-start.22) | collective-permute-done | bytes 73760 | tf_op jit(solution)/shard_map/ppermute | solution.py:227
  73.6 1.7 %collective-permute-done.23.refs_1_ = bf16[32,1152]{1,0:T(8,128)(2,1)S(1)} collective-permute-done((bf16[32,1152]{1,0:T(8,128)(2,1)S(1)}, bf16[32,1152]{1,0:T(8,128)(2,1)S(1)}, u32[]{:S(2)}, u32[]{:S(2)}) %collective-permute-start.23) | collective-permute-done | bytes 73760 | tf_op jit(solution)/shard_map/ppermute | solution.py:227
  75.3 0.8 %shard_map.73 = bf16[8,16,1152]{2,1,0:T(8,128)(2,1)} custom-call(f32[6,1152]{1,0:T(8,128)S(1)} %copy-done.8, bf16[4,16,1152]{2,1,0:T(8,128)(2,1)S(1)} %get-tuple-element.47.kept_ref, bf16[4,16,1152]{2,1,0:T(8,128)(2,1)S(1)} %collective-permute-done.15.other_ref, bf16[32,1152]{1,0:T(8,128)(2,1)S(1)} %collective-permute-done.22.refs_0_, ...), custom_call_target="tpu_custom_call" | custom-call | flops 1 | bytes 1 | tf_op jit(solution)/shard_map/pallas_call | solution.py:214
  (47 shorter events, 6.8 us)
Async XLA Ops:
  0.0 3.0 %collective-permute-start = (bf16[1,128,1152]{2,1,0:T(8,128)(2,1)}, bf16[1,128,1152]{2,1,0:T(8,128)(2,1)S(1)}, u32[]{:S(2)}, u32[]{:S(2)}) collective-permute-start(bf16[1,128,1152]{2,1,0:T(8,128)(2,1)} %own_ref.3), channel_id=1, source_target_pairs={{0,1},{1,0},{2,3},{3,2},{4,5},{5,4},{6,7},{7,6},{8,9},{9,8},{10,11... | collective-permute-start | bytes 884744 | tf_op jit(solution)/shard_map/ppermute | solution.py:227
  0.5 10.4 %collective-permute-start.3 = (bf16[1,128,1152]{2,1,0:T(8,128)(2,1)}, bf16[1,128,1152]{2,1,0:T(8,128)(2,1)S(1)}, u32[]{:S(2)}, u32[]{:S(2)}) collective-permute-start(bf16[1,128,1152]{2,1,0:T(8,128)(2,1)} %own_ref.3), channel_id=1, source_target_pairs={{0,2},{1,3},{2,0},{3,1},{4,6},{5,7},{6,4},{7,5},{8,10},{9,11},{10,... | collective-permute-start | bytes 884744 | tf_op jit(solution)/shard_map/ppermute | solution.py:227
  4.0 6.8 %collective-permute-start.1 = (bf16[64,1152]{1,0:T(8,128)(2,1)S(1)}, bf16[64,1152]{1,0:T(8,128)(2,1)S(1)}, u32[]{:S(2)}, u32[]{:S(2)}) collective-permute-start(bf16[64,1152]{1,0:T(8,128)(2,1)S(1)} %shard_map.64), channel_id=1, source_target_pairs={{0,4},{4,0},{8,12},{12,8},{16,20},{20,16},{24,28},{28,24},{1,5},{5... | collective-permute-start | bytes 442376 | tf_op jit(solution)/shard_map/ppermute | solution.py:227
  5.8 1.6 %copy-start = (bf16[864,1152]{1,0:T(8,128)(2,1)S(1)}, bf16[864,1152]{1,0:T(8,128)(2,1)}, u32[]{:S(2)}) copy-start(bf16[864,1152]{1,0:T(8,128)(2,1)} %weight_ref.3) | copy-start | bytes 5971972
  8.1 4.4 %copy-start.4 = (bf16[288,1152]{1,0:T(8,128)(2,1)S(1)}, bf16[288,1152]{1,0:T(8,128)(2,1)}, u32[]{:S(2)}) copy-start(bf16[288,1152]{1,0:T(8,128)(2,1)} %refs_0_.4) | copy-start | bytes 1990660
  8.1 4.8 %copy-start.1 = (bf16[864,1152]{1,0:T(8,128)(2,1)S(1)}, bf16[864,1152]{1,0:T(8,128)(2,1)}, u32[]{:S(2)}) copy-start(bf16[864,1152]{1,0:T(8,128)(2,1)} %weight_ref.3) | copy-start | bytes 5971972
  9.2 9.2 %copy-start.3 = (bf16[288,1152]{1,0:T(8,128)(2,1)S(1)}, bf16[288,1152]{1,0:T(8,128)(2,1)}, u32[]{:S(2)}) copy-start(bf16[288,1152]{1,0:T(8,128)(2,1)} %refs_0_.7) | copy-start | bytes 1990660
  9.3 29.3 %copy-start.6 = (bf16[1,128,1152]{2,1,0:T(8,128)(2,1)S(1)}, bf16[1,128,1152]{2,1,0:T(8,128)(2,1)}, u32[]{:S(2)}) copy-start(bf16[1,128,1152]{2,1,0:T(8,128)(2,1)} %own_ref.3) | copy-start | bytes 884740
  10.9 1.6 %collective-permute-start.4 = (bf16[1,128,1152]{2,1,0:T(8,128)(2,1)S(1)}, bf16[1,128,1152]{2,1,0:T(8,128)(2,1)S(1)}, u32[]{:S(2)}, u32[]{:S(2)}) collective-permute-start(bf16[1,128,1152]{2,1,0:T(8,128)(2,1)S(1)} %collective-permute-done.3.refs_0_), channel_id=1, source_target_pairs={{0,1},{1,0},{2,3},{3,2},{4,5},{5,4},{6,7},{7,6},{8,9},{9,8},{10,11... | collective-permute-start | bytes 884744 | tf_op jit(solution)/shard_map/ppermute | solution.py:227
  12.4 36.4 %collective-permute-start.17 = (bf16[864,1152]{1,0:T(8,128)(2,1)}, bf16[864,1152]{1,0:T(8,128)(2,1)S(1)}, u32[]{:S(2)}, u32[]{:S(2)}) collective-permute-start(bf16[864,1152]{1,0:T(8,128)(2,1)} %refs_0_.6), channel_id=1, source_target_pairs={{0,1},{1,0},{2,3},{3,2},{4,5},{5,4},{6,7},{7,6},{8,9},{9,8},{10,11... | collective-permute-start | bytes 5971976 | tf_op jit(solution)/shard_map/ppermute | solution.py:227
  12.6 5.1 %collective-permute-start.2 = (bf16[288,1152]{1,0:T(8,128)(2,1)S(1)}, bf16[288,1152]{1,0:T(8,128)(2,1)S(1)}, u32[]{:S(2)}, u32[]{:S(2)}) collective-permute-start(bf16[288,1152]{1,0:T(8,128)(2,1)S(1)} %copy-done.4), channel_id=1, source_target_pairs={{0,1},{1,0},{2,3},{3,2},{4,5},{5,4},{6,7},{7,6},{8,9},{9,8},{10,11... | collective-permute-start | bytes 1990664 | tf_op jit(solution)/shard_map/ppermute | solution.py:227
  16.3 1.4 %collective-permute-start.5 = (bf16[288,256]{1,0:T(8,128)(2,1)S(1)}, bf16[288,256]{1,0:T(8,128)(2,1)S(1)}, u32[]{:S(2)}, u32[]{:S(2)}) collective-permute-start(bf16[288,256]{1,0:T(8,128)(2,1)S(1)} %get-tuple-element.39), channel_id=1, source_target_pairs={{0,1},{1,0},{2,3},{3,2},{4,5},{5,4},{6,7},{7,6},{8,9},{9,8},{10,11... | collective-permute-start | bytes 442376 | tf_op jit(solution)/shard_map/ppermute | solution.py:227
  18.5 30.4 %copy-start.2 = (bf16[864,1152]{1,0:T(8,128)(2,1)S(1)}, bf16[864,1152]{1,0:T(8,128)(2,1)}, u32[]{:S(2)}) copy-start(bf16[864,1152]{1,0:T(8,128)(2,1)} %refs_0_.6) | copy-start | bytes 5971972
  18.5 30.4 %collective-permute-start.16 = (bf16[288,1152]{1,0:T(8,128)(2,1)S(1)}, bf16[288,1152]{1,0:T(8,128)(2,1)S(1)}, u32[]{:S(2)}, u32[]{:S(2)}) collective-permute-start(bf16[288,1152]{1,0:T(8,128)(2,1)S(1)} %copy-done.3), channel_id=1, source_target_pairs={{0,1},{1,0},{2,3},{3,2},{4,5},{5,4},{6,7},{7,6},{8,9},{9,8},{10,11... | collective-permute-start | bytes 1990664 | tf_op jit(solution)/shard_map/ppermute | solution.py:227
  18.7 2.6 %collective-permute-start.6 = (bf16[64,1152]{1,0:T(8,128)(2,1)S(1)}, bf16[64,1152]{1,0:T(8,128)(2,1)S(1)}, u32[]{:S(2)}, u32[]{:S(2)}) collective-permute-start(bf16[64,1152]{1,0:T(8,128)(2,1)S(1)} %get-tuple-element.43), channel_id=1, source_target_pairs={{1,3},{3,1},{5,7},{7,5},{9,11},{11,9},{13,15},{15,13},{17,19},{19,... | collective-permute-start | bytes 442376 | tf_op jit(solution)/shard_map/ppermute | solution.py:251
  19.5 11.2 %collective-permute-start.9 = (bf16[64,576]{1,0:T(8,128)(2,1)S(1)}, bf16[64,576]{1,0:T(8,128)(2,1)S(1)}, u32[]{:S(2)}, u32[]{:S(2)}) collective-permute-start(bf16[64,576]{1,0:T(8,128)(2,1)S(1)} %get-tuple-element.44), channel_id=1, source_target_pairs={{0,4},{4,0},{8,12},{12,8},{16,20},{20,16},{24,28},{28,24},{1,5},{5... | collective-permute-start | bytes 221192 | tf_op jit(solution)/shard_map/ppermute | solution.py:227
  21.3 5.7 %collective-permute-start.7 = (bf16[6,1152]{1,0:T(8,128)(2,1)S(1)}, bf16[6,1152]{1,0:T(8,128)(2,1)S(1)}, u32[]{:S(2)}, u32[]{:S(2)}) collective-permute-start(bf16[6,1152]{1,0:T(8,128)(2,1)S(1)} %convert), channel_id=1, source_target_pairs={{1,0},{3,2},{5,4},{7,6},{9,8},{11,10},{13,12},{15,14},{17,16},{19,... | collective-permute-start | bytes 41480 | tf_op jit(solution)/shard_map/ppermute | solution.py:311
  22.6 11.5 %collective-permute-start.10 = (bf16[64,1152]{1,0:T(8,128)(2,1)S(1)}, bf16[64,1152]{1,0:T(8,128)(2,1)S(1)}, u32[]{:S(2)}, u32[]{:S(2)}) collective-permute-start(bf16[64,1152]{1,0:T(8,128)(2,1)S(1)} %get-tuple-element.46), channel_id=1, source_target_pairs={{1,7},{3,5},{5,3},{7,1},{9,15},{11,13},{13,11},{15,9},{17,23},{19,... | collective-permute-start | bytes 442376 | tf_op jit(solution)/shard_map/ppermute | solution.py:251
  27.0 7.9 %collective-permute-start.8 = (bf16[64,1152]{1,0:T(8,128)(2,1)S(1)}, bf16[64,1152]{1,0:T(8,128)(2,1)S(1)}, u32[]{:S(2)}, u32[]{:S(2)}) collective-permute-start(bf16[64,1152]{1,0:T(8,128)(2,1)S(1)} %get-tuple-element.43), channel_id=1, source_target_pairs={{0,2},{2,0},{4,6},{6,4},{8,10},{10,8},{12,14},{14,12},{16,18},{18,... | collective-permute-start | bytes 442376 | tf_op jit(solution)/shard_map/ppermute | solution.py:251
  30.7 7.9 %collective-permute-start.11 = (bf16[64,1152]{1,0:T(8,128)(2,1)S(1)}, bf16[64,1152]{1,0:T(8,128)(2,1)S(1)}, u32[]{:S(2)}, u32[]{:S(2)}) collective-permute-start(bf16[64,1152]{1,0:T(8,128)(2,1)S(1)} %get-tuple-element.46), channel_id=1, source_target_pairs={{0,6},{2,4},{4,2},{6,0},{8,14},{10,12},{12,10},{14,8},{16,22},{18,... | collective-permute-start | bytes 442376 | tf_op jit(solution)/shard_map/ppermute | solution.py:251
  39.3 6.2 %collective-permute-start.12 = (bf16[32,1152]{1,0:T(8,128)(2,1)S(1)}, bf16[32,1152]{1,0:T(8,128)(2,1)S(1)}, u32[]{:S(2)}, u32[]{:S(2)}) collective-permute-start(bf16[32,1152]{1,0:T(8,128)(2,1)S(1)} %get-tuple-element.49), channel_id=1, source_target_pairs={{0,24},{4,28},{8,16},{12,20},{16,8},{20,12},{24,0},{28,4},{1,25},{... | collective-permute-start | bytes 221192 | tf_op jit(solution)/shard_map/ppermute | solution.py:227
  43.0 5.3 %collective-permute-start.13 = (bf16[32,1152]{1,0:T(8,128)(2,1)S(1)}, bf16[32,1152]{1,0:T(8,128)(2,1)S(1)}, u32[]{:S(2)}, u32[]{:S(2)}) collective-permute-start(bf16[32,1152]{1,0:T(8,128)(2,1)S(1)} %get-tuple-element.50), channel_id=1, source_target_pairs={{0,16},{4,20},{8,24},{12,28},{16,0},{20,4},{24,8},{28,12},{1,17},{... | collective-permute-start | bytes 221192 | tf_op jit(solution)/shard_map/ppermute | solution.py:227
  43.0 5.3 %collective-permute-start.14 = (bf16[32,1152]{1,0:T(8,128)(2,1)S(1)}, bf16[32,1152]{1,0:T(8,128)(2,1)S(1)}, u32[]{:S(2)}, u32[]{:S(2)}) collective-permute-start(bf16[32,1152]{1,0:T(8,128)(2,1)S(1)} %get-tuple-element.51), channel_id=1, source_target_pairs={{0,8},{4,12},{8,0},{12,4},{16,24},{20,28},{24,16},{28,20},{1,9},{5... | collective-permute-start | bytes 221192 | tf_op jit(solution)/shard_map/ppermute | solution.py:227
  48.3 9.9 %collective-permute-start.18 = (bf16[128,1152]{1,0:T(8,128)(2,1)S(1)}, bf16[128,1152]{1,0:T(8,128)(2,1)S(1)}, u32[]{:S(2)}, u32[]{:S(2)}) collective-permute-start(bf16[128,1152]{1,0:T(8,128)(2,1)S(1)} %shard_map.69.refs_4_), channel_id=1, source_target_pairs={{0,2},{1,3},{2,0},{3,1},{4,6},{5,7},{6,4},{7,5},{8,10},{9,11},{10,... | collective-permute-start | bytes 884744 | tf_op jit(solution)/shard_map/ppermute | solution.py:227
  50.8 7.4 %collective-permute-start.19 = (bf16[64,576]{1,0:T(8,128)(2,1)S(1)}, bf16[64,576]{1,0:T(8,128)(2,1)S(1)}, u32[]{:S(2)}, u32[]{:S(2)}) collective-permute-start(bf16[64,576]{1,0:T(8,128)(2,1)S(1)} %get-tuple-element.57), channel_id=1, source_target_pairs={{0,4},{4,0},{8,12},{12,8},{16,20},{20,16},{24,28},{28,24},{1,5},{5... | collective-permute-start | bytes 221192 | tf_op jit(solution)/shard_map/ppermute | solution.py:227
  60.2 15.1 %copy-start.8 = (f32[6,1152]{1,0:T(8,128)S(1)}, f32[6,1152]{1,0:T(8,128)}, u32[]{:S(2)}) copy-start(f32[6,1152]{1,0:T(8,128)} %mod_ref.7) | copy-start | bytes 82948
  60.2 6.8 %collective-permute-start.20 = (bf16[64,1152]{1,0:T(8,128)(2,1)S(1)}, bf16[64,1152]{1,0:T(8,128)(2,1)S(1)}, u32[]{:S(2)}, u32[]{:S(2)}) collective-permute-start(bf16[64,1152]{1,0:T(8,128)(2,1)S(1)} %get-tuple-element.59), channel_id=1, source_target_pairs={{0,2},{1,3},{2,0},{3,1},{4,6},{5,7},{6,4},{7,5},{8,10},{9,11},{10,... | collective-permute-start | bytes 442376 | tf_op jit(solution)/shard_map/ppermute | solution.py:251
  60.8 6.2 %collective-permute-start.21 = (bf16[64,1152]{1,0:T(8,128)(2,1)S(1)}, bf16[64,1152]{1,0:T(8,128)(2,1)S(1)}, u32[]{:S(2)}, u32[]{:S(2)}) collective-permute-start(bf16[64,1152]{1,0:T(8,128)(2,1)S(1)} %get-tuple-element.60), channel_id=1, source_target_pairs={{0,6},{1,7},{2,4},{3,5},{4,2},{5,3},{6,0},{7,1},{8,14},{9,15},{10,... | collective-permute-start | bytes 442376 | tf_op jit(solution)/shard_map/ppermute | solution.py:251
  63.2 8.6 %collective-permute-start.15 = (bf16[4,16,1152]{2,1,0:T(8,128)(2,1)S(1)}, bf16[4,16,1152]{2,1,0:T(8,128)(2,1)S(1)}, u32[]{:S(2)}, u32[]{:S(2)}) collective-permute-start(bf16[4,16,1152]{2,1,0:T(8,128)(2,1)S(1)} %get-tuple-element.53), channel_id=1, source_target_pairs={{0,4},{4,0},{8,12},{12,8},{16,20},{20,16},{24,28},{28,24},{1,5},{5... | collective-permute-start | bytes 442376 | tf_op jit(solution)/shard_map/ppermute | solution.py:227
  67.4 6.2 %collective-permute-start.22 = (bf16[32,1152]{1,0:T(8,128)(2,1)S(1)}, bf16[32,1152]{1,0:T(8,128)(2,1)S(1)}, u32[]{:S(2)}, u32[]{:S(2)}) collective-permute-start(bf16[32,1152]{1,0:T(8,128)(2,1)S(1)} %get-tuple-element.61), channel_id=1, source_target_pairs={{0,24},{4,28},{8,16},{12,20},{16,8},{20,12},{24,0},{28,4},{1,25},{... | collective-permute-start | bytes 221192 | tf_op jit(solution)/shard_map/ppermute | solution.py:227
  69.3 6.0 %collective-permute-start.23 = (bf16[32,1152]{1,0:T(8,128)(2,1)S(1)}, bf16[32,1152]{1,0:T(8,128)(2,1)S(1)}, u32[]{:S(2)}, u32[]{:S(2)}) collective-permute-start(bf16[32,1152]{1,0:T(8,128)(2,1)S(1)} %get-tuple-element.62), channel_id=1, source_target_pairs={{0,16},{4,20},{8,24},{12,28},{16,0},{20,4},{24,8},{28,12},{1,17},{... | collective-permute-start | bytes 221192 | tf_op jit(solution)/shard_map/ppermute | solution.py:227
  69.7 5.7 %collective-permute-start.24 = (bf16[32,1152]{1,0:T(8,128)(2,1)S(1)}, bf16[32,1152]{1,0:T(8,128)(2,1)S(1)}, u32[]{:S(2)}, u32[]{:S(2)}) collective-permute-start(bf16[32,1152]{1,0:T(8,128)(2,1)S(1)} %get-tuple-element.63), channel_id=1, source_target_pairs={{0,8},{4,12},{8,0},{12,4},{16,24},{20,28},{24,16},{28,20},{1,9},{5... | collective-permute-start | bytes 221192 | tf_op jit(solution)/shard_map/ppermute | solution.py:227
  (2 other events, 1.8 us)

commit v14 on v12

--- a/solution.py
+++ b/solution.py
@@ -95,8 +95,9 @@
     return jnp.where(first, even, odd), jnp.where(first, odd, even)
 
 
-def share_kernel(period, token_ref, sent_ref):
+def share_kernel(period, token_ref, weight_ref, sent_ref, half_ref):
     sent_ref[...] = of_this_half(token_ref[0], period)[1].astype(BF16)
+    half_ref[...] = of_this_half(weight_ref[...], half_ref.shape[0])[0].astype(BF16)
 
 
 def joined(refs):
@@ -148,10 +149,10 @@
         refs[-1][at * size : (at + 1) * size, :] = ref[...]
 
 
-def temporal_kernel(own, period, block, *refs):
-    weight_refs, output_refs, (proj_ref, heads_ref) = refs[:2], refs[2:4], refs[-2:]
+def temporal_kernel(period, block, *refs):
+    weight_refs, (proj_ref, heads_ref) = refs[:2], refs[-2:]
     groups = proj_ref.shape[1] // block
-    row_refs, update_refs = refs[4 : -2 - 2 * groups], refs[-2 - 2 * groups : -2]
+    row_refs, out_refs = refs[2 : -2 - 2 * groups], refs[-2 - 2 * groups : -2]
     rows = jnp.concatenate([ref[...] for ref in row_refs], axis=0)
     depth = weight_refs[0].shape[0]
     for core in range(2):
@@ -160,7 +161,6 @@
     key_patch = lax.broadcasted_iota(jnp.int32, (block, block), 0) % period
     query_patch = lax.broadcasted_iota(jnp.int32, (block, block), 1) % period
     mask = key_patch == query_patch
-    weights = joined(output_refs)
     for group in range(groups):
         cols = slice(group * block, (group + 1) * block)
 
@@ -176,23 +176,34 @@
         for head in range(heads):
             mixed = mix(part(head, 2), soft[:, head * block : (head + 1) * block])
             heads_ref[head * HD : (head + 1) * HD, cols] = mixed
-        mixed = heads_ref[:, cols].astype(BF16).T
-        if own:
-            kept, sent = halves(mixed, period)
-            parts = dot(kept, weights), sent
+        parts = halves(heads_ref[:, cols].astype(BF16).T, period)
+        for ref, half in zip(out_refs[2 * group : 2 * group + 2], parts):
+            ref[...] = half
+
+
+def update_kernel(groups, *refs):
+    head_refs, refs = (refs[:groups], refs[groups : 2 * groups]), refs[2 * groups :]
+    weight_refs, piece_refs = refs[: 4 * groups - 2], refs[4 * groups - 2 :]
+    period = piece_refs[0].shape[0] // 2
+    size = head_refs[0][0].shape[0]
+    first = lax.axis_index("frame") % 2 == 0
+    update = 0.0
+    for group in range(groups):
+        heads = joined([refs[group] for refs in head_refs])
+        if group == 0:
+            weights = joined(weight_refs[:2])
         else:
-            parts = halves(dot(mixed, weights), period)
-        for ref, half in zip(update_refs[2 * group : 2 * group + 2], parts):
-            ref[...] = half.astype(ref.dtype)
-
-
-def sum_kernel(groups, *refs):
-    piece_refs = refs[2 + 2 * groups :]
-    period = piece_refs[0].shape[0] // 2
-    for at, update in enumerate(total_updates(groups, refs[:2], refs[2:])):
-        update = update.astype(BF16)
+            at = 4 * group - 2
+            parts = []
+            for here, there in (weight_refs[at : at + 2], weight_refs[at + 2 : at + 4]):
+                here, there = here[...].astype(F32), there[...].astype(F32)
+                parts += [jnp.where(first, here, there), jnp.where(first, there, here)]
+            weights = jnp.concatenate(parts, axis=0).astype(BF16)
+        update += dot(heads, weights)
+    for at in range(2):
+        part = update[at * size : (at + 1) * size].astype(BF16)
         for piece, ref in enumerate(piece_refs):
-            rows = update[piece * period : (piece + 1) * period]
+            rows = part[piece * period : (piece + 1) * period]
             ref[at * period : (at + 1) * period, :] = rows
 
 
@@ -265,10 +276,9 @@
         offsets = reversed(range(pieces))
         return [swap(part, "frame", 2 * at) if at else part for at, part in zip(offsets, parts)]
 
-    def return_updates(own, far):
+    def swap_updates(far):
         same = [swap(part, "patch", 2 * at) for at, part in enumerate(far[::2], 1)]
-        diagonal = [swap_diagonal(part, 2 * at) for at, part in enumerate(far[1::2], 1)]
-        return [own[0], *same, own[1], *diagonal]
+        return same, [swap_diagonal(part, 2 * at) for at, part in enumerate(far[1::2], 1)]
 
     def halves_shape(dtype):
         return shape((rows // 2, width), dtype)
@@ -284,8 +294,10 @@
         (modulation, spatial_qkv, tokens, sister),
         [shape((3 * shard, 2 * rows), F32)],
     )
-    (shared,) = call(
-        functools.partial(share_kernel, period), (after(tokens, sister),), [halves_shape(BF16)]
+    shared, half_out = call(
+        functools.partial(share_kernel, period),
+        (after(tokens, sister), temporal_out),
+        [halves_shape(BF16), shape((shard // 2, width), BF16)],
     )
     paired = swap(shared, "frame", 1)
     out_pair = with_sister(spatial_out, near)
@@ -304,35 +316,43 @@
         own_shapes + far_shapes,
     )
     late_pair = with_sister(temporal_out, parts[0])
-    updates = return_updates((parts[0], swap(parts[1], "frame", 1)), parts[2:])
+    same, diagonal = swap_updates(parts[2:])
+    updates = [parts[0], *same, swap(parts[1], "frame", 1), *diagonal]
     middle, middle_sent, *parts = call(
         functools.partial(middle_kernel, pieces, groups),
         (modulation, tokens, paired, *out_pair, *updates),
         [shape((pieces, period, width), BF16)] * 2 + piece_shapes,
         [pltpu.VMEM((pieces, 2 * period, width), BF16)],
     )
+    halves_here = [swap(after(half_out, middle), "patch", 2 * at) for at in range(1, groups)]
     arrived = exchange_frames(parts)
+    arrived[0] = after(arrived[0], *halves_here)
     (segment,) = call(join_kernel, arrived, [shape((rows, width), BF16)])
     segments = across(segment)
-
-    def attend_frames(own, segments, shapes):
+    halves_there = [swap(after(part, segment), "frame", 1) for part in halves_here]
+
+    heads_shape = [shape((rows // 2, 2 * shard), BF16)] * 2
+
+    def attend_frames(segments):
         columns = len(segments) * rows
         return call(
-            functools.partial(temporal_kernel, own, period, rows),
-            (*temporal_pair, *late_pair, *segments),
-            shapes,
+            functools.partial(temporal_kernel, period, rows),
+            (*temporal_pair, *segments),
+            heads_shape * len(segments),
             [pltpu.VMEM((6 * shard, columns), F32), pltpu.VMEM((2 * shard, columns), F32)],
         )
 
-    kept, sent = attend_frames(True, [segment], own_shapes)
-    received = swap(sent, "frame", 1)
+    kept, sent = attend_frames([segment])
+    others = [after(block, kept) for block in segments[1:]]
+    far_heads = attend_frames(others)
+    same, diagonal = swap_updates(far_heads)
+    late_far = []
+    for pair in zip(halves_here, halves_there):
+        late_far += [*pair, *(swap(after(part, *far_heads), "patch", 1) for part in pair)]
     middle_other = swap(after(middle_sent, segment), "frame", 1)
-    others = [after(block, received) for block in segments[1:]]
-    far_parts = attend_frames(False, others, far_shapes)
-    updates = return_updates((kept, received), far_parts)
     parts = call(
-        functools.partial(sum_kernel, groups),
-        (*late_pair, *updates),
+        functools.partial(update_kernel, groups),
+        (kept, *same, swap(sent, "frame", 1), *diagonal, *late_pair, *late_far),
         piece_shapes,
     )
     (result,) = call(

time: 66.6 us -> 69.9 us (1.050)
  starting transfers between devices: 25 us -> 26.2 us
  waiting for transfers between devices: 26.8 us -> 28 us
  local copies, waits for them, and re-layouts: 3.34 us -> 4.43 us
    ppermute x2, starting transfers between devices: 2.62 us -> 3.89 us  [swap_diagonal(): return lax.ppermute(value, ('frame', 'patch'), pairs)]
    ppermute x2, waiting for transfers between devices: 1.8 us -> 2.98 us  [swap_diagonal(): return lax.ppermute(value, ('frame', 'patch'), pairs)]
    unnamed x18 -> x20, local copies, waits for them, and re-layouts: 3.34 us -> 4.43 us
    ppermute x20 -> x24, starting transfers between devices: 22.4 us -> 22.3 us  [swap(): return lax.ppermute(value, axis, [(at, at ^ offset) for at in range(size)])]
    ppermute x20 -> x24, waiting for transfers between devices: 25 us -> 25 us  [swap(): return lax.ppermute(value, axis, [(at, at ^ offset) for at in range(size)])]
  transfers between devices with their start and end apart: 22 -> 26, of which waited for: 12 -> 15; matrix products, arithmetic and copies ran while one was open for 0% -> 0% of each run, Pallas kernels for 12% -> 14%
where the time goes in v14:
time: 69.9 us; the launch traced here: 69.6 us
  waiting for transfers between devices  28 us (40%)
  starting transfers between devices  26.2 us (37%)
  Pallas kernels  10.9 us (16%)
  local copies, waits for them, and re-layouts  4.43 us (6%)
    ppermute x24, waiting for transfers between devices, swap(): return lax.ppermute(value, axis, [(at, at ^ offset) for at in range(size)])  25 us
    ppermute x24, starting transfers between devices, swap(): return lax.ppermute(value, axis, [(at, at ^ offset) for at in range(size)])  22.3 us
    pallas_call x10, Pallas kernels, call(): pl.pallas_call(body, out_shape=outs, in_specs=[pl.BlockSpec(memory_space=...  10.9 us
    unnamed x20, local copies, waits for them, and re-layouts  4.43 us
    ppermute x2, starting transfers between devices, swap_diagonal(): return lax.ppermute(value, ('frame', 'patch'), pairs)  3.89 us
    ppermute x2, waiting for transfers between devices, swap_diagonal(): return lax.ppermute(value, ('frame', 'patch'), pairs)  2.98 us
  transfers between devices with their start and end apart: 26, of which 15 were waited for; matrix products, arithmetic and copies ran while one was open for 0% of the time, Pallas kernels for 14%

profile of v14, /device:TPU:0, one launch (start us, length us, event | category | flops | bytes accessed | tf_op | source)
XLA Modules:
  0.0 69.6 jit_solution(9749779309593352964)
XLA Ops:
  0.5 2.5 %collective-permute-start.3 = (bf16[1,128,1152]{2,1,0:T(8,128)(2,1)}, bf16[1,128,1152]{2,1,0:T(8,128)(2,1)S(1)}, u32[]{:S(2)}, u32[]{:S(2)}) collective-permute-start(bf16[1,128,1152]{2,1,0:T(8,128)(2,1)} %own_ref.3), channel_id=1, source_target_pairs={{0,2},{1,3},{2,0},{3,1},{4,6},{5,7},{6,4},{7,5},{8,10},{9,11},{10,... | collective-permute-start | bytes 884744 | tf_op jit(solution)/shard_map/ppermute | solution.py:238
  3.0 1.0 %copy-done.3 = bf16[1,128,1152]{2,1,0:T(8,128)(2,1)S(1)} copy-done((bf16[1,128,1152]{2,1,0:T(8,128)(2,1)S(1)}, bf16[1,128,1152]{2,1,0:T(8,128)(2,1)}, u32[]{:S(2)}) %copy-start.3) | copy-done | bytes 294936
  4.0 1.1 %copy-done.6 = bf16[288,1152]{1,0:T(8,128)(2,1)S(1)} copy-done((bf16[288,1152]{1,0:T(8,128)(2,1)S(1)}, bf16[288,1152]{1,0:T(8,128)(2,1)}, u32[]{:S(2)}) %copy-start.6) | copy-done | bytes 663576
  5.2 1.8 %collective-permute-start.1 = (bf16[64,1152]{1,0:T(8,128)(2,1)S(1)}, bf16[64,1152]{1,0:T(8,128)(2,1)S(1)}, u32[]{:S(2)}, u32[]{:S(2)}) collective-permute-start(bf16[64,1152]{1,0:T(8,128)(2,1)S(1)} %get-tuple-element.40), channel_id=1, source_target_pairs={{0,4},{4,0},{8,12},{12,8},{16,20},{20,16},{24,28},{28,24},{1,5},{5... | collective-permute-start | bytes 442376 | tf_op jit(solution)/shard_map/ppermute | solution.py:238
  7.0 1.6 %copy-done = bf16[864,1152]{1,0:T(8,128)(2,1)S(1)} copy-done((bf16[864,1152]{1,0:T(8,128)(2,1)S(1)}, bf16[864,1152]{1,0:T(8,128)(2,1)}, u32[]{:S(2)}) %copy-start) | copy-done | bytes 1990680
  8.5 0.8 %copy-done.8 = f32[6,1152]{1,0:T(8,128)S(1)} copy-done((f32[6,1152]{1,0:T(8,128)S(1)}, f32[6,1152]{1,0:T(8,128)}, u32[]{:S(2)}) %copy-start.8) | copy-done | bytes 27672
  9.3 1.1 %shard_map.65.near_ref = f32[864,256]{1,0:T(8,128)S(1)} custom-call(f32[6,1152]{1,0:T(8,128)S(1)} %copy-done.8, bf16[864,1152]{1,0:T(8,128)(2,1)S(1)} %copy-done, bf16[1,128,1152]{2,1,0:T(8,128)(2,1)S(1)} %copy-done.3, bf16[1,128,1152]{2,1,0:T(8,128)(2,1)S(1)} %collective-permute-done.sister_ref), custom_call_target="tpu_custom_call" | custom-call | flops 1 | bytes 1 | tf_op jit(solution)/shard_map/pallas_call | solution.py:225
  11.2 1.6 %collective-permute-done.4.refs_1_ = bf16[1,128,1152]{2,1,0:T(8,128)(2,1)S(1)} collective-permute-done((bf16[1,128,1152]{2,1,0:T(8,128)(2,1)S(1)}, bf16[1,128,1152]{2,1,0:T(8,128)(2,1)S(1)}, u32[]{:S(2)}, u32[]{:S(2)}) %collective-permute-start.4) | collective-permute-done | bytes 294944 | tf_op jit(solution)/shard_map/ppermute | solution.py:238
  13.3 3.3 %shard_map.66 = (bf16[288,256]{1,0:T(8,128)(2,1)S(1)}, bf16[288,256]{1,0:T(8,128)(2,1)S(1)}) custom-call(f32[6,1152]{1,0:T(8,128)S(1)} %copy-done.8, bf16[864,1152]{1,0:T(8,128)(2,1)S(1)} %copy-done.1, f32[864,256]{1,0:T(8,128)S(1)} %shard_map.65.near_ref, bf16[1,128,1152]{2,1,0:T(8,128)(2,1)S(1)} %collective-permute-done.3.refs_0_, ...), custom_call_target="tpu_custom_call" | custom-call | flops 1 | bytes 1 | tf_op jit(solution)/shard_map/pallas_call | solution.py:225
  16.9 1.2 %collective-permute-done.5.refs_1_ = bf16[288,256]{1,0:T(8,128)(2,1)S(1)} collective-permute-done((bf16[288,256]{1,0:T(8,128)(2,1)S(1)}, bf16[288,256]{1,0:T(8,128)(2,1)S(1)}, u32[]{:S(2)}, u32[]{:S(2)}) %collective-permute-start.5) | collective-permute-done | bytes 147488 | tf_op jit(solution)/shard_map/ppermute | solution.py:238
  18.8 1.7 %collective-permute-start.6 = (bf16[64,1152]{1,0:T(8,128)(2,1)S(1)}, bf16[64,1152]{1,0:T(8,128)(2,1)S(1)}, u32[]{:S(2)}, u32[]{:S(2)}) collective-permute-start(bf16[64,1152]{1,0:T(8,128)(2,1)S(1)} %get-tuple-element.46), channel_id=1, source_target_pairs={{0,2},{1,3},{2,0},{3,1},{4,6},{5,7},{6,4},{7,5},{8,10},{9,11},{10,... | collective-permute-start | bytes 442376 | tf_op jit(solution)/shard_map/ppermute | solution.py:238
  20.6 1.4 %collective-permute-start.8 = (bf16[64,1152]{1,0:T(8,128)(2,1)S(1)}, bf16[64,1152]{1,0:T(8,128)(2,1)S(1)}, u32[]{:S(2)}, u32[]{:S(2)}) collective-permute-start(bf16[64,1152]{1,0:T(8,128)(2,1)S(1)} %get-tuple-element.48), channel_id=1, source_target_pairs={{0,6},{1,7},{2,4},{3,5},{4,2},{5,3},{6,0},{7,1},{8,14},{9,15},{10,... | collective-permute-start | bytes 442376 | tf_op jit(solution)/shard_map/ppermute | solution.py:261
  22.4 5.4 %collective-permute-done.7.refs_4_ = bf16[64,576]{1,0:T(8,128)(2,1)S(1)} collective-permute-done((bf16[64,576]{1,0:T(8,128)(2,1)S(1)}, bf16[64,576]{1,0:T(8,128)(2,1)S(1)}, u32[]{:S(2)}, u32[]{:S(2)}) %collective-permute-start.7) | collective-permute-done | bytes 73760 | tf_op jit(solution)/shard_map/ppermute | solution.py:238
  28.7 1.7 %collective-permute-start.10 = (bf16[144,1152]{1,0:T(8,128)(2,1)S(1)}, bf16[144,1152]{1,0:T(8,128)(2,1)S(1)}, u32[]{:S(2)}, u32[]{:S(2)}) collective-permute-start(bf16[144,1152]{1,0:T(8,128)(2,1)S(1)} %get-tuple-element.53), channel_id=1, source_target_pairs={{0,2},{1,3},{2,0},{3,1},{4,6},{5,7},{6,4},{7,5},{8,10},{9,11},{10,... | collective-permute-start | bytes 995336 | tf_op jit(solution)/shard_map/ppermute | solution.py:238
  30.4 3.6 %collective-permute-start.9 = (bf16[32,1152]{1,0:T(8,128)(2,1)S(1)}, bf16[32,1152]{1,0:T(8,128)(2,1)S(1)}, u32[]{:S(2)}, u32[]{:S(2)}) collective-permute-start(bf16[32,1152]{1,0:T(8,128)(2,1)S(1)} %get-tuple-element.51), channel_id=1, source_target_pairs={{0,24},{4,28},{8,16},{12,20},{16,8},{20,12},{24,0},{28,4},{1,25},{... | collective-permute-start | bytes 221192 | tf_op jit(solution)/shard_map/ppermute | solution.py:238
  34.0 0.8 %collective-permute-start.12 = (bf16[32,1152]{1,0:T(8,128)(2,1)S(1)}, bf16[32,1152]{1,0:T(8,128)(2,1)S(1)}, u32[]{:S(2)}, u32[]{:S(2)}) collective-permute-start(bf16[32,1152]{1,0:T(8,128)(2,1)S(1)} %get-tuple-element.56), channel_id=1, source_target_pairs={{0,8},{4,12},{8,0},{12,4},{16,24},{20,28},{24,16},{28,20},{1,9},{5... | collective-permute-start | bytes 221192 | tf_op jit(solution)/shard_map/ppermute | solution.py:238
  34.8 2.1 %collective-permute-done.9.refs_0_ = bf16[32,1152]{1,0:T(8,128)(2,1)S(1)} collective-permute-done((bf16[32,1152]{1,0:T(8,128)(2,1)S(1)}, bf16[32,1152]{1,0:T(8,128)(2,1)S(1)}, u32[]{:S(2)}, u32[]{:S(2)}) %collective-permute-start.9) | collective-permute-done | bytes 73760 | tf_op jit(solution)/shard_map/ppermute | solution.py:238
  37.7 2.0 %collective-permute-done.11.refs_1_ = bf16[32,1152]{1,0:T(8,128)(2,1)S(1)} collective-permute-done((bf16[32,1152]{1,0:T(8,128)(2,1)S(1)}, bf16[32,1152]{1,0:T(8,128)(2,1)S(1)}, u32[]{:S(2)}, u32[]{:S(2)}) %collective-permute-start.11) | collective-permute-done | bytes 73760 | tf_op jit(solution)/shard_map/ppermute | solution.py:238
  39.7 1.6 %collective-permute-start.20 = (bf16[144,1152]{1,0:T(8,128)(2,1)S(1)}, bf16[144,1152]{1,0:T(8,128)(2,1)S(1)}, u32[]{:S(2)}, u32[]{:S(2)}) collective-permute-start(bf16[144,1152]{1,0:T(8,128)(2,1)S(1)} %collective-permute-done.10.refs_6_), channel_id=1, source_target_pairs={{0,4},{4,0},{8,12},{12,8},{16,20},{20,16},{24,28},{28,24},{1,5},{5... | collective-permute-start | bytes 995336 | tf_op jit(solution)/shard_map/ppermute | solution.py:238
  41.8 1.6 %shard_map.70 = (bf16[64,576]{1,0:T(8,128)(2,1)S(1)}, bf16[64,576]{1,0:T(8,128)(2,1)S(1)}) custom-call(bf16[864,1152]{1,0:T(8,128)(2,1)S(1)} %copy-done.2, bf16[864,1152]{1,0:T(8,128)(2,1)S(1)} %collective-permute-done.14.refs_1_, bf16[128,1152]{1,0:T(8,128)(2,1)S(1)} %shard_map.69.refs_2_), custom_call_target="tpu_custom_call" | custom-call | flops 1 | bytes 1 | tf_op jit(solution)/shard_map/pallas_call | solution.py:225
  43.4 5.9 %collective-permute-done.15.refs_2_ = bf16[128,1152]{1,0:T(8,128)(2,1)S(1)} collective-permute-done((bf16[128,1152]{1,0:T(8,128)(2,1)S(1)}, bf16[128,1152]{1,0:T(8,128)(2,1)S(1)}, u32[]{:S(2)}, u32[]{:S(2)}) %collective-permute-start.15) | collective-permute-done | bytes 294944 | tf_op jit(solution)/shard_map/ppermute | solution.py:238
  49.3 1.6 %shard_map.71 = (bf16[64,576]{1,0:T(8,128)(2,1)S(1)}, bf16[64,576]{1,0:T(8,128)(2,1)S(1)}) custom-call(bf16[864,1152]{1,0:T(8,128)(2,1)S(1)} %copy-done.2, bf16[864,1152]{1,0:T(8,128)(2,1)S(1)} %collective-permute-done.14.refs_1_, bf16[128,1152]{1,0:T(8,128)(2,1)S(1)} %collective-permute-done.15.refs_2_), custom_call_target="tpu_custom_call" | custom-call | flops 1 | bytes 1 | tf_op jit(solution)/shard_map/pallas_call | solution.py:225
  52.6 2.4 %collective-permute-start.18 = (bf16[64,576]{1,0:T(8,128)(2,1)S(1)}, bf16[64,576]{1,0:T(8,128)(2,1)S(1)}, u32[]{:S(2)}, u32[]{:S(2)}) collective-permute-start(bf16[64,576]{1,0:T(8,128)(2,1)S(1)} %get-tuple-element.64), channel_id=1, source_target_pairs={{0,6},{1,7},{2,4},{3,5},{4,2},{5,3},{6,0},{7,1},{8,14},{9,15},{10,... | collective-permute-start | bytes 221192 | tf_op jit(solution)/shard_map/ppermute | solution.py:261
  55.1 0.9 %collective-permute-done.16.refs_1_ = bf16[64,576]{1,0:T(8,128)(2,1)S(1)} collective-permute-done((bf16[64,576]{1,0:T(8,128)(2,1)S(1)}, bf16[64,576]{1,0:T(8,128)(2,1)S(1)}, u32[]{:S(2)}, u32[]{:S(2)}) %collective-permute-start.16) | collective-permute-done | bytes 73760 | tf_op jit(solution)/shard_map/ppermute | solution.py:238
  56.5 0.8 %collective-permute-done.17.refs_2_ = bf16[64,576]{1,0:T(8,128)(2,1)S(1)} collective-permute-done((bf16[64,576]{1,0:T(8,128)(2,1)S(1)}, bf16[64,576]{1,0:T(8,128)(2,1)S(1)}, u32[]{:S(2)}, u32[]{:S(2)}) %collective-permute-start.17) | collective-permute-done | bytes 73760 | tf_op jit(solution)/shard_map/ppermute | solution.py:238
  57.4 2.8 %collective-permute-done.18.refs_3_ = bf16[64,576]{1,0:T(8,128)(2,1)S(1)} collective-permute-done((bf16[64,576]{1,0:T(8,128)(2,1)S(1)}, bf16[64,576]{1,0:T(8,128)(2,1)S(1)}, u32[]{:S(2)}, u32[]{:S(2)}) %collective-permute-start.18) | collective-permute-done | bytes 73760 | tf_op jit(solution)/shard_map/ppermute | solution.py:261
  60.1 0.8 %shard_map.72 = (bf16[32,1152]{1,0:T(8,128)(2,1)S(1)}, bf16[32,1152]{1,0:T(8,128)(2,1)S(1)}, bf16[32,1152]{1,0:T(8,128)(2,1)S(1)}, bf16[32,1152]{1,0:T(8,128)(2,1)S(1)}) custom-call(bf16[64,576]{1,0:T(8,128)(2,1)S(1)} %get-tuple-element.60.refs_0_, bf16[64,576]{1,0:T(8,128)(2,1)S(1)} %collective-permute-done.16.refs_1_, ...), custom_call_target="tpu_custom_call" | custom-call | flops 1 | bytes 1 | tf_op jit(solution)/shard_map/pallas_call | solution.py:225
  60.9 2.2 %collective-permute-start.23 = (bf16[32,1152]{1,0:T(8,128)(2,1)S(1)}, bf16[32,1152]{1,0:T(8,128)(2,1)S(1)}, u32[]{:S(2)}, u32[]{:S(2)}) collective-permute-start(bf16[32,1152]{1,0:T(8,128)(2,1)S(1)} %get-tuple-element.69), channel_id=1, source_target_pairs={{0,24},{4,28},{8,16},{12,20},{16,8},{20,12},{24,0},{28,4},{1,25},{... | collective-permute-start | bytes 221192 | tf_op jit(solution)/shard_map/ppermute | solution.py:238
  63.1 2.3 %collective-permute-start.25 = (bf16[32,1152]{1,0:T(8,128)(2,1)S(1)}, bf16[32,1152]{1,0:T(8,128)(2,1)S(1)}, u32[]{:S(2)}, u32[]{:S(2)}) collective-permute-start(bf16[32,1152]{1,0:T(8,128)(2,1)S(1)} %get-tuple-element.71), channel_id=1, source_target_pairs={{0,8},{4,12},{8,0},{12,4},{16,24},{20,28},{24,16},{28,20},{1,9},{5... | collective-permute-start | bytes 221192 | tf_op jit(solution)/shard_map/ppermute | solution.py:238
  65.4 1.8 %collective-permute-done.23.refs_0_ = bf16[32,1152]{1,0:T(8,128)(2,1)S(1)} collective-permute-done((bf16[32,1152]{1,0:T(8,128)(2,1)S(1)}, bf16[32,1152]{1,0:T(8,128)(2,1)S(1)}, u32[]{:S(2)}, u32[]{:S(2)}) %collective-permute-start.23) | collective-permute-done | bytes 73760 | tf_op jit(solution)/shard_map/ppermute | solution.py:238
  67.2 1.6 %collective-permute-done.24.refs_1_ = bf16[32,1152]{1,0:T(8,128)(2,1)S(1)} collective-permute-done((bf16[32,1152]{1,0:T(8,128)(2,1)S(1)}, bf16[32,1152]{1,0:T(8,128)(2,1)S(1)}, u32[]{:S(2)}, u32[]{:S(2)}) %collective-permute-start.24) | collective-permute-done | bytes 73760 | tf_op jit(solution)/shard_map/ppermute | solution.py:238
  68.8 0.8 %shard_map.73 = bf16[8,16,1152]{2,1,0:T(8,128)(2,1)} custom-call(f32[6,1152]{1,0:T(8,128)S(1)} %copy-done.9, bf16[4,16,1152]{2,1,0:T(8,128)(2,1)S(1)} %get-tuple-element.49.kept_ref, bf16[4,16,1152]{2,1,0:T(8,128)(2,1)S(1)} %collective-permute-done.13.other_ref, bf16[32,1152]{1,0:T(8,128)(2,1)S(1)} %collective-permute-done.23.refs_0_, ...), custom_call_target="tpu_custom_call" | custom-call | flops 1 | bytes 1 | tf_op jit(solution)/shard_map/pallas_call | solution.py:225
  (50 shorter events, 7.6 us)
Async XLA Ops:
  0.0 3.0 %collective-permute-start = (bf16[1,128,1152]{2,1,0:T(8,128)(2,1)}, bf16[1,128,1152]{2,1,0:T(8,128)(2,1)S(1)}, u32[]{:S(2)}, u32[]{:S(2)}) collective-permute-start(bf16[1,128,1152]{2,1,0:T(8,128)(2,1)} %own_ref.3), channel_id=1, source_target_pairs={{0,1},{1,0},{2,3},{3,2},{4,5},{5,4},{6,7},{7,6},{8,9},{9,8},{10,11... | collective-permute-start | bytes 884744 | tf_op jit(solution)/shard_map/ppermute | solution.py:238
  0.5 10.4 %collective-permute-start.3 = (bf16[1,128,1152]{2,1,0:T(8,128)(2,1)}, bf16[1,128,1152]{2,1,0:T(8,128)(2,1)S(1)}, u32[]{:S(2)}, u32[]{:S(2)}) collective-permute-start(bf16[1,128,1152]{2,1,0:T(8,128)(2,1)} %own_ref.3), channel_id=1, source_target_pairs={{0,2},{1,3},{2,0},{3,1},{4,6},{5,7},{6,4},{7,5},{8,10},{9,11},{10,... | collective-permute-start | bytes 884744 | tf_op jit(solution)/shard_map/ppermute | solution.py:238
  5.1 7.9 %copy-start.5 = (bf16[288,1152]{1,0:T(8,128)(2,1)S(1)}, bf16[288,1152]{1,0:T(8,128)(2,1)}, u32[]{:S(2)}) copy-start(bf16[288,1152]{1,0:T(8,128)(2,1)} %refs_0_.3) | copy-start | bytes 1990660
  5.2 6.0 %collective-permute-start.1 = (bf16[64,1152]{1,0:T(8,128)(2,1)S(1)}, bf16[64,1152]{1,0:T(8,128)(2,1)S(1)}, u32[]{:S(2)}, u32[]{:S(2)}) collective-permute-start(bf16[64,1152]{1,0:T(8,128)(2,1)S(1)} %get-tuple-element.40), channel_id=1, source_target_pairs={{0,4},{4,0},{8,12},{12,8},{16,20},{20,16},{24,28},{28,24},{1,5},{5... | collective-permute-start | bytes 442376 | tf_op jit(solution)/shard_map/ppermute | solution.py:238
  9.3 4.0 %copy-start.1 = (bf16[864,1152]{1,0:T(8,128)(2,1)S(1)}, bf16[864,1152]{1,0:T(8,128)(2,1)}, u32[]{:S(2)}) copy-start(bf16[864,1152]{1,0:T(8,128)(2,1)} %weight_ref.5) | copy-start | bytes 5971972
  10.4 17.6 %copy-start.4 = (bf16[1,128,1152]{2,1,0:T(8,128)(2,1)S(1)}, bf16[1,128,1152]{2,1,0:T(8,128)(2,1)}, u32[]{:S(2)}) copy-start(bf16[1,128,1152]{2,1,0:T(8,128)(2,1)} %own_ref.3) | copy-start | bytes 884740
  11.2 1.6 %collective-permute-start.4 = (bf16[1,128,1152]{2,1,0:T(8,128)(2,1)S(1)}, bf16[1,128,1152]{2,1,0:T(8,128)(2,1)S(1)}, u32[]{:S(2)}, u32[]{:S(2)}) collective-permute-start(bf16[1,128,1152]{2,1,0:T(8,128)(2,1)S(1)} %collective-permute-done.3.refs_0_), channel_id=1, source_target_pairs={{0,1},{1,0},{2,3},{3,2},{4,5},{5,4},{6,7},{7,6},{8,9},{9,8},{10,11... | collective-permute-start | bytes 884744 | tf_op jit(solution)/shard_map/ppermute | solution.py:238
  12.8 29.0 %collective-permute-start.14 = (bf16[864,1152]{1,0:T(8,128)(2,1)}, bf16[864,1152]{1,0:T(8,128)(2,1)S(1)}, u32[]{:S(2)}, u32[]{:S(2)}) collective-permute-start(bf16[864,1152]{1,0:T(8,128)(2,1)} %refs_0_.5), channel_id=1, source_target_pairs={{0,1},{1,0},{2,3},{3,2},{4,5},{5,4},{6,7},{7,6},{8,9},{9,8},{10,11... | collective-permute-start | bytes 5971976 | tf_op jit(solution)/shard_map/ppermute | solution.py:238
  13.0 5.1 %collective-permute-start.2 = (bf16[288,1152]{1,0:T(8,128)(2,1)S(1)}, bf16[288,1152]{1,0:T(8,128)(2,1)S(1)}, u32[]{:S(2)}, u32[]{:S(2)}) collective-permute-start(bf16[288,1152]{1,0:T(8,128)(2,1)S(1)} %copy-done.5), channel_id=1, source_target_pairs={{0,1},{1,0},{2,3},{3,2},{4,5},{5,4},{6,7},{7,6},{8,9},{9,8},{10,11... | collective-permute-start | bytes 1990664 | tf_op jit(solution)/shard_map/ppermute | solution.py:238
  16.7 1.4 %collective-permute-start.5 = (bf16[288,256]{1,0:T(8,128)(2,1)S(1)}, bf16[288,256]{1,0:T(8,128)(2,1)S(1)}, u32[]{:S(2)}, u32[]{:S(2)}) collective-permute-start(bf16[288,256]{1,0:T(8,128)(2,1)S(1)} %get-tuple-element.44), channel_id=1, source_target_pairs={{0,1},{1,0},{2,3},{3,2},{4,5},{5,4},{6,7},{7,6},{8,9},{9,8},{10,11... | collective-permute-start | bytes 442376 | tf_op jit(solution)/shard_map/ppermute | solution.py:238
  18.1 18.8 %copy-start.7 = (bf16[288,1152]{1,0:T(8,128)(2,1)S(1)}, bf16[288,1152]{1,0:T(8,128)(2,1)}, u32[]{:S(2)}) copy-start(bf16[288,1152]{1,0:T(8,128)(2,1)} %refs_4_.1) | copy-start | bytes 1990660
  18.1 23.7 %copy-start.2 = (bf16[864,1152]{1,0:T(8,128)(2,1)S(1)}, bf16[864,1152]{1,0:T(8,128)(2,1)}, u32[]{:S(2)}) copy-start(bf16[864,1152]{1,0:T(8,128)(2,1)} %refs_0_.5) | copy-start | bytes 5971972
  18.8 8.9 %collective-permute-start.6 = (bf16[64,1152]{1,0:T(8,128)(2,1)S(1)}, bf16[64,1152]{1,0:T(8,128)(2,1)S(1)}, u32[]{:S(2)}, u32[]{:S(2)}) collective-permute-start(bf16[64,1152]{1,0:T(8,128)(2,1)S(1)} %get-tuple-element.46), channel_id=1, source_target_pairs={{0,2},{1,3},{2,0},{3,1},{4,6},{5,7},{6,4},{7,5},{8,10},{9,11},{10,... | collective-permute-start | bytes 442376 | tf_op jit(solution)/shard_map/ppermute | solution.py:238
  20.6 7.4 %collective-permute-start.8 = (bf16[64,1152]{1,0:T(8,128)(2,1)S(1)}, bf16[64,1152]{1,0:T(8,128)(2,1)S(1)}, u32[]{:S(2)}, u32[]{:S(2)}) collective-permute-start(bf16[64,1152]{1,0:T(8,128)(2,1)S(1)} %get-tuple-element.48), channel_id=1, source_target_pairs={{0,6},{1,7},{2,4},{3,5},{4,2},{5,3},{6,0},{7,1},{8,14},{9,15},{10,... | collective-permute-start | bytes 442376 | tf_op jit(solution)/shard_map/ppermute | solution.py:261
  22.0 5.8 %collective-permute-start.7 = (bf16[64,576]{1,0:T(8,128)(2,1)S(1)}, bf16[64,576]{1,0:T(8,128)(2,1)S(1)}, u32[]{:S(2)}, u32[]{:S(2)}) collective-permute-start(bf16[64,576]{1,0:T(8,128)(2,1)S(1)} %get-tuple-element.47), channel_id=1, source_target_pairs={{0,4},{4,0},{8,12},{12,8},{16,20},{20,16},{24,28},{28,24},{1,5},{5... | collective-permute-start | bytes 221192 | tf_op jit(solution)/shard_map/ppermute | solution.py:238
  28.7 9.0 %collective-permute-start.10 = (bf16[144,1152]{1,0:T(8,128)(2,1)S(1)}, bf16[144,1152]{1,0:T(8,128)(2,1)S(1)}, u32[]{:S(2)}, u32[]{:S(2)}) collective-permute-start(bf16[144,1152]{1,0:T(8,128)(2,1)S(1)} %get-tuple-element.53), channel_id=1, source_target_pairs={{0,2},{1,3},{2,0},{3,1},{4,6},{5,7},{6,4},{7,5},{8,10},{9,11},{10,... | collective-permute-start | bytes 995336 | tf_op jit(solution)/shard_map/ppermute | solution.py:238
  30.4 6.5 %collective-permute-start.9 = (bf16[32,1152]{1,0:T(8,128)(2,1)S(1)}, bf16[32,1152]{1,0:T(8,128)(2,1)S(1)}, u32[]{:S(2)}, u32[]{:S(2)}) collective-permute-start(bf16[32,1152]{1,0:T(8,128)(2,1)S(1)} %get-tuple-element.51), channel_id=1, source_target_pairs={{0,24},{4,28},{8,16},{12,20},{16,8},{20,12},{24,0},{28,4},{1,25},{... | collective-permute-start | bytes 221192 | tf_op jit(solution)/shard_map/ppermute | solution.py:238
  34.0 5.7 %collective-permute-start.11 = (bf16[32,1152]{1,0:T(8,128)(2,1)S(1)}, bf16[32,1152]{1,0:T(8,128)(2,1)S(1)}, u32[]{:S(2)}, u32[]{:S(2)}) collective-permute-start(bf16[32,1152]{1,0:T(8,128)(2,1)S(1)} %get-tuple-element.55), channel_id=1, source_target_pairs={{0,16},{4,20},{8,24},{12,28},{16,0},{20,4},{24,8},{28,12},{1,17},{... | collective-permute-start | bytes 221192 | tf_op jit(solution)/shard_map/ppermute | solution.py:238
  34.0 5.7 %collective-permute-start.12 = (bf16[32,1152]{1,0:T(8,128)(2,1)S(1)}, bf16[32,1152]{1,0:T(8,128)(2,1)S(1)}, u32[]{:S(2)}, u32[]{:S(2)}) collective-permute-start(bf16[32,1152]{1,0:T(8,128)(2,1)S(1)} %get-tuple-element.56), channel_id=1, source_target_pairs={{0,8},{4,12},{8,0},{12,4},{16,24},{20,28},{24,16},{28,20},{1,9},{5... | collective-permute-start | bytes 221192 | tf_op jit(solution)/shard_map/ppermute | solution.py:238
  36.9 15.7 %collective-permute-start.19 = (bf16[288,1152]{1,0:T(8,128)(2,1)S(1)}, bf16[288,1152]{1,0:T(8,128)(2,1)S(1)}, u32[]{:S(2)}, u32[]{:S(2)}) collective-permute-start(bf16[288,1152]{1,0:T(8,128)(2,1)S(1)} %copy-done.7), channel_id=1, source_target_pairs={{0,1},{1,0},{2,3},{3,2},{4,5},{5,4},{6,7},{7,6},{8,9},{9,8},{10,11... | collective-permute-start | bytes 1990664 | tf_op jit(solution)/shard_map/ppermute | solution.py:238
  39.7 11.4 %collective-permute-start.20 = (bf16[144,1152]{1,0:T(8,128)(2,1)S(1)}, bf16[144,1152]{1,0:T(8,128)(2,1)S(1)}, u32[]{:S(2)}, u32[]{:S(2)}) collective-permute-start(bf16[144,1152]{1,0:T(8,128)(2,1)S(1)} %collective-permute-done.10.refs_6_), channel_id=1, source_target_pairs={{0,4},{4,0},{8,12},{12,8},{16,20},{20,16},{24,28},{28,24},{1,5},{5... | collective-permute-start | bytes 995336 | tf_op jit(solution)/shard_map/ppermute | solution.py:238
  41.3 8.1 %collective-permute-start.15 = (bf16[128,1152]{1,0:T(8,128)(2,1)S(1)}, bf16[128,1152]{1,0:T(8,128)(2,1)S(1)}, u32[]{:S(2)}, u32[]{:S(2)}) collective-permute-start(bf16[128,1152]{1,0:T(8,128)(2,1)S(1)} %shard_map.69.refs_2_), channel_id=1, source_target_pairs={{0,2},{1,3},{2,0},{3,1},{4,6},{5,7},{6,4},{7,5},{8,10},{9,11},{10,... | collective-permute-start | bytes 884744 | tf_op jit(solution)/shard_map/ppermute | solution.py:238
  51.0 17.8 %copy-start.9 = (f32[6,1152]{1,0:T(8,128)S(1)}, f32[6,1152]{1,0:T(8,128)}, u32[]{:S(2)}) copy-start(f32[6,1152]{1,0:T(8,128)} %mod_ref.7) | copy-start | bytes 82948
  51.0 9.1 %collective-permute-start.21 = (bf16[144,1152]{1,0:T(8,128)(2,1)S(1)}, bf16[144,1152]{1,0:T(8,128)(2,1)S(1)}, u32[]{:S(2)}, u32[]{:S(2)}) collective-permute-start(bf16[144,1152]{1,0:T(8,128)(2,1)S(1)} %collective-permute-done.10.refs_6_), channel_id=1, source_target_pairs={{0,1},{1,0},{2,3},{3,2},{4,5},{5,4},{6,7},{7,6},{8,9},{9,8},{10,11... | collective-permute-start | bytes 995336 | tf_op jit(solution)/shard_map/ppermute | solution.py:238
  51.1 9.1 %collective-permute-start.22 = (bf16[144,1152]{1,0:T(8,128)(2,1)S(1)}, bf16[144,1152]{1,0:T(8,128)(2,1)S(1)}, u32[]{:S(2)}, u32[]{:S(2)}) collective-permute-start(bf16[144,1152]{1,0:T(8,128)(2,1)S(1)} %collective-permute-done.20.refs_7_), channel_id=1, source_target_pairs={{0,1},{1,0},{2,3},{3,2},{4,5},{5,4},{6,7},{7,6},{8,9},{9,8},{10,11... | collective-permute-start | bytes 995336 | tf_op jit(solution)/shard_map/ppermute | solution.py:238
  51.6 4.4 %collective-permute-start.16 = (bf16[64,576]{1,0:T(8,128)(2,1)S(1)}, bf16[64,576]{1,0:T(8,128)(2,1)S(1)}, u32[]{:S(2)}, u32[]{:S(2)}) collective-permute-start(bf16[64,576]{1,0:T(8,128)(2,1)S(1)} %get-tuple-element.62), channel_id=1, source_target_pairs={{0,2},{1,3},{2,0},{3,1},{4,6},{5,7},{6,4},{7,5},{8,10},{9,11},{10,... | collective-permute-start | bytes 221192 | tf_op jit(solution)/shard_map/ppermute | solution.py:238
  52.1 5.3 %collective-permute-start.17 = (bf16[64,576]{1,0:T(8,128)(2,1)S(1)}, bf16[64,576]{1,0:T(8,128)(2,1)S(1)}, u32[]{:S(2)}, u32[]{:S(2)}) collective-permute-start(bf16[64,576]{1,0:T(8,128)(2,1)S(1)} %get-tuple-element.63), channel_id=1, source_target_pairs={{0,4},{4,0},{8,12},{12,8},{16,20},{20,16},{24,28},{28,24},{1,5},{5... | collective-permute-start | bytes 221192 | tf_op jit(solution)/shard_map/ppermute | solution.py:238
  52.6 7.5 %collective-permute-start.18 = (bf16[64,576]{1,0:T(8,128)(2,1)S(1)}, bf16[64,576]{1,0:T(8,128)(2,1)S(1)}, u32[]{:S(2)}, u32[]{:S(2)}) collective-permute-start(bf16[64,576]{1,0:T(8,128)(2,1)S(1)} %get-tuple-element.64), channel_id=1, source_target_pairs={{0,6},{1,7},{2,4},{3,5},{4,2},{5,3},{6,0},{7,1},{8,14},{9,15},{10,... | collective-permute-start | bytes 221192 | tf_op jit(solution)/shard_map/ppermute | solution.py:261
  56.0 9.4 %collective-permute-start.13 = (bf16[4,16,1152]{2,1,0:T(8,128)(2,1)S(1)}, bf16[4,16,1152]{2,1,0:T(8,128)(2,1)S(1)}, u32[]{:S(2)}, u32[]{:S(2)}) collective-permute-start(bf16[4,16,1152]{2,1,0:T(8,128)(2,1)S(1)} %get-tuple-element.58), channel_id=1, source_target_pairs={{0,4},{4,0},{8,12},{12,8},{16,20},{20,16},{24,28},{28,24},{1,5},{5... | collective-permute-start | bytes 442376 | tf_op jit(solution)/shard_map/ppermute | solution.py:238
  60.9 6.2 %collective-permute-start.23 = (bf16[32,1152]{1,0:T(8,128)(2,1)S(1)}, bf16[32,1152]{1,0:T(8,128)(2,1)S(1)}, u32[]{:S(2)}, u32[]{:S(2)}) collective-permute-start(bf16[32,1152]{1,0:T(8,128)(2,1)S(1)} %get-tuple-element.69), channel_id=1, source_target_pairs={{0,24},{4,28},{8,16},{12,20},{16,8},{20,12},{24,0},{28,4},{1,25},{... | collective-permute-start | bytes 221192 | tf_op jit(solution)/shard_map/ppermute | solution.py:238
  63.1 5.6 %collective-permute-start.24 = (bf16[32,1152]{1,0:T(8,128)(2,1)S(1)}, bf16[32,1152]{1,0:T(8,128)(2,1)S(1)}, u32[]{:S(2)}, u32[]{:S(2)}) collective-permute-start(bf16[32,1152]{1,0:T(8,128)(2,1)S(1)} %get-tuple-element.70), channel_id=1, source_target_pairs={{0,16},{4,20},{8,24},{12,28},{16,0},{20,4},{24,8},{28,12},{1,17},{... | collective-permute-start | bytes 221192 | tf_op jit(solution)/shard_map/ppermute | solution.py:238
  63.1 5.6 %collective-permute-start.25 = (bf16[32,1152]{1,0:T(8,128)(2,1)S(1)}, bf16[32,1152]{1,0:T(8,128)(2,1)S(1)}, u32[]{:S(2)}, u32[]{:S(2)}) collective-permute-start(bf16[32,1152]{1,0:T(8,128)(2,1)S(1)} %get-tuple-element.71), channel_id=1, source_target_pairs={{0,8},{4,12},{8,0},{12,4},{16,24},{20,28},{24,16},{28,20},{1,9},{5... | collective-permute-start | bytes 221192 | tf_op jit(solution)/shard_map/ppermute | solution.py:238
  (4 other events, 4.4 us)

commit v15 on v12

--- a/solution.py
+++ b/solution.py
@@ -138,8 +138,8 @@
             middle_ref[piece] = middle[rows]
             scratch[piece, at * period : (at + 1) * period, :] = normed[rows]
     here = lax.axis_index("frame") // 2
-    for at, ref in enumerate(piece_refs):
-        ref[...] = scratch[here ^ (pieces - 1 - at)]
+    for at, ref in enumerate(piece_refs, 1):
+        ref[...] = scratch[here ^ at % pieces]
 
 
 def join_kernel(*refs):
@@ -200,8 +200,8 @@
     piece_refs, out_ref = refs[:-1], refs[-1]
     period = kept_ref.shape[1]
     here = lax.axis_index("frame")
-    for at, ref in enumerate(piece_refs):
-        there = here // 2 ^ (pieces - 1 - at)
+    for at, ref in enumerate(piece_refs, 1):
+        there = here // 2 ^ at % len(piece_refs)
         for half, middle_ref in enumerate((kept_ref, other_ref)):
             update = ref[half * period : (half + 1) * period, :].astype(F32)
             middle = middle_ref[there].astype(F32)
@@ -262,8 +262,8 @@
         return [weights, swap(after(weights, *others), "patch", 1)]
 
     def exchange_frames(parts):
-        offsets = reversed(range(pieces))
-        return [swap(part, "frame", 2 * at) if at else part for at, part in zip(offsets, parts)]
+        sent = [swap(part, "frame", 2 * at) for at, part in enumerate(parts[:-1], 1)]
+        return [*sent, parts[-1]]
 
     def return_updates(own, far):
         same = [swap(part, "patch", 2 * at) for at, part in enumerate(far[::2], 1)]

time: 66.6 us -> 66.5 us (level)
    ppermute x20, waiting for transfers between devices: 25 us -> 26.6 us  [swap(): return lax.ppermute(value, axis, [(at, at ^ offset) for at in range(size)])]
    ppermute x2, waiting for transfers between devices: 1.8 us -> 0.27 us  [swap_diagonal(): return lax.ppermute(value, ('frame', 'patch'), pairs)]
    ppermute x20, starting transfers between devices: 22.4 us -> 20.9 us  [swap(): return lax.ppermute(value, axis, [(at, at ^ offset) for at in range(size)])]
    ppermute x2, starting transfers between devices: 2.62 us -> 3.97 us  [swap_diagonal(): return lax.ppermute(value, ('frame', 'patch'), pairs)]
  transfers between devices with their start and end apart: 22 -> 22, of which waited for: 12 -> 13; matrix products, arithmetic and copies ran while one was open for 0% -> 0% of each run, Pallas kernels for 12% -> 12%
where the time goes in v15:
time: 66.5 us; the launch traced here: 66.2 us
  waiting for transfers between devices  26.9 us (40%)
  starting transfers between devices  24.9 us (37%)
  Pallas kernels  11 us (17%)
  local copies, waits for them, and re-layouts  3.34 us (5%)
    ppermute x20, waiting for transfers between devices, swap(): return lax.ppermute(value, axis, [(at, at ^ offset) for at in range(size)])  26.6 us
    ppermute x20, starting transfers between devices, swap(): return lax.ppermute(value, axis, [(at, at ^ offset) for at in range(size)])  20.9 us
    pallas_call x10, Pallas kernels, call(): pl.pallas_call(body, out_shape=outs, in_specs=[pl.BlockSpec(memory_space=...  11 us
    ppermute x2, starting transfers between devices, swap_diagonal(): return lax.ppermute(value, ('frame', 'patch'), pairs)  3.97 us
    unnamed x18, local copies, waits for them, and re-layouts  3.34 us
  transfers between devices with their start and end apart: 22, of which 13 were waited for; matrix products, arithmetic and copies ran while one was open for 0% of the time, Pallas kernels for 12%

profile of v15, /device:TPU:0, one launch (start us, length us, event | category | flops | bytes accessed | tf_op | source)
XLA Modules:
  0.0 66.2 jit_solution(6027571234620058078)
XLA Ops:
  0.5 2.5 %collective-permute-start.3 = (bf16[1,128,1152]{2,1,0:T(8,128)(2,1)}, bf16[1,128,1152]{2,1,0:T(8,128)(2,1)S(1)}, u32[]{:S(2)}, u32[]{:S(2)}) collective-permute-start(bf16[1,128,1152]{2,1,0:T(8,128)(2,1)} %own_ref.3), channel_id=1, source_target_pairs={{0,2},{1,3},{2,0},{3,1},{4,6},{5,7},{6,4},{7,5},{8,10},{9,11},{10,... | collective-permute-start | bytes 884744 | tf_op jit(solution)/shard_map/ppermute | solution.py:227
  3.0 1.0 %copy-done.4 = bf16[1,128,1152]{2,1,0:T(8,128)(2,1)S(1)} copy-done((bf16[1,128,1152]{2,1,0:T(8,128)(2,1)S(1)}, bf16[1,128,1152]{2,1,0:T(8,128)(2,1)}, u32[]{:S(2)}) %copy-start.4) | copy-done | bytes 294936
  4.0 1.8 %collective-permute-start.1 = (bf16[64,1152]{1,0:T(8,128)(2,1)S(1)}, bf16[64,1152]{1,0:T(8,128)(2,1)S(1)}, u32[]{:S(2)}, u32[]{:S(2)}) collective-permute-start(bf16[64,1152]{1,0:T(8,128)(2,1)S(1)} %shard_map.64), channel_id=1, source_target_pairs={{0,4},{4,0},{8,12},{12,8},{16,20},{20,16},{24,28},{28,24},{1,5},{5... | collective-permute-start | bytes 442376 | tf_op jit(solution)/shard_map/ppermute | solution.py:227
  5.8 1.6 %copy-done = bf16[864,1152]{1,0:T(8,128)(2,1)S(1)} copy-done((bf16[864,1152]{1,0:T(8,128)(2,1)S(1)}, bf16[864,1152]{1,0:T(8,128)(2,1)}, u32[]{:S(2)}) %copy-start) | copy-done | bytes 1990680
  7.4 0.8 %copy-done.7 = f32[6,1152]{1,0:T(8,128)S(1)} copy-done((f32[6,1152]{1,0:T(8,128)S(1)}, f32[6,1152]{1,0:T(8,128)}, u32[]{:S(2)}) %copy-start.7) | copy-done | bytes 27672
  8.1 1.1 %shard_map.65.near_ref = f32[864,256]{1,0:T(8,128)S(1)} custom-call(f32[6,1152]{1,0:T(8,128)S(1)} %copy-done.7, bf16[864,1152]{1,0:T(8,128)(2,1)S(1)} %copy-done, bf16[1,128,1152]{2,1,0:T(8,128)(2,1)S(1)} %copy-done.4, bf16[1,128,1152]{2,1,0:T(8,128)(2,1)S(1)} %collective-permute-done.sister_ref), custom_call_target="tpu_custom_call" | custom-call | flops 1 | bytes 1 | tf_op jit(solution)/shard_map/pallas_call | solution.py:214
  9.3 1.6 %collective-permute-done.3.refs_0_ = bf16[1,128,1152]{2,1,0:T(8,128)(2,1)S(1)} collective-permute-done((bf16[1,128,1152]{2,1,0:T(8,128)(2,1)}, bf16[1,128,1152]{2,1,0:T(8,128)(2,1)S(1)}, u32[]{:S(2)}, u32[]{:S(2)}) %collective-permute-start.3) | collective-permute-done | bytes 294944 | tf_op jit(solution)/shard_map/ppermute | solution.py:227
  10.9 1.6 %collective-permute-done.4.refs_1_ = bf16[1,128,1152]{2,1,0:T(8,128)(2,1)S(1)} collective-permute-done((bf16[1,128,1152]{2,1,0:T(8,128)(2,1)S(1)}, bf16[1,128,1152]{2,1,0:T(8,128)(2,1)S(1)}, u32[]{:S(2)}, u32[]{:S(2)}) %collective-permute-start.4) | collective-permute-done | bytes 294944 | tf_op jit(solution)/shard_map/ppermute | solution.py:227
  13.0 3.3 %shard_map.66 = (bf16[288,256]{1,0:T(8,128)(2,1)S(1)}, bf16[288,256]{1,0:T(8,128)(2,1)S(1)}) custom-call(f32[6,1152]{1,0:T(8,128)S(1)} %copy-done.7, bf16[864,1152]{1,0:T(8,128)(2,1)S(1)} %copy-done.1, f32[864,256]{1,0:T(8,128)S(1)} %shard_map.65.near_ref, bf16[1,128,1152]{2,1,0:T(8,128)(2,1)S(1)} %collective-permute-done.3.refs_0_, ...), custom_call_target="tpu_custom_call" | custom-call | flops 1 | bytes 1 | tf_op jit(solution)/shard_map/pallas_call | solution.py:214
  16.5 1.2 %collective-permute-done.5.refs_1_ = bf16[288,256]{1,0:T(8,128)(2,1)S(1)} collective-permute-done((bf16[288,256]{1,0:T(8,128)(2,1)S(1)}, bf16[288,256]{1,0:T(8,128)(2,1)S(1)}, u32[]{:S(2)}, u32[]{:S(2)}) %collective-permute-start.5) | collective-permute-done | bytes 147488 | tf_op jit(solution)/shard_map/ppermute | solution.py:227
  17.7 0.7 %shard_map.67 = (f32[64,1152]{1,0:T(8,128)S(1)}, bf16[64,576]{1,0:T(8,128)(2,1)S(1)}, bf16[64,1152]{1,0:T(8,128)(2,1)S(1)}, bf16[64,1152]{1,0:T(8,128)(2,1)S(1)}) custom-call(bf16[288,256]{1,0:T(8,128)(2,1)S(1)} %get-tuple-element.35.refs_0_, bf16[288,256]{1,0:T(8,128)(2,1)S(1)} %collective-permute-done.5.refs_1_, bf16[288,1152]{1,0:T(8,128)(2,1)S(1)} %copy-done.6, ...), custom_call_target="tpu_custom_call" | custom-call | flops 1 | bytes 1 | tf_op jit(solution)/shard_map/pallas_call | solution.py:214
  18.7 1.8 %collective-permute-start.6 = (bf16[64,1152]{1,0:T(8,128)(2,1)S(1)}, bf16[64,1152]{1,0:T(8,128)(2,1)S(1)}, u32[]{:S(2)}, u32[]{:S(2)}) collective-permute-start(bf16[64,1152]{1,0:T(8,128)(2,1)S(1)} %get-tuple-element.38), channel_id=1, source_target_pairs={{0,2},{1,3},{2,0},{3,1},{4,6},{5,7},{6,4},{7,5},{8,10},{9,11},{10,... | collective-permute-start | bytes 442376 | tf_op jit(solution)/shard_map/ppermute | solution.py:227
  20.4 1.4 %collective-permute-start.8 = (bf16[64,1152]{1,0:T(8,128)(2,1)S(1)}, bf16[64,1152]{1,0:T(8,128)(2,1)S(1)}, u32[]{:S(2)}, u32[]{:S(2)}) collective-permute-start(bf16[64,1152]{1,0:T(8,128)(2,1)S(1)} %get-tuple-element.40), channel_id=1, source_target_pairs={{0,6},{1,7},{2,4},{3,5},{4,2},{5,3},{6,0},{7,1},{8,14},{9,15},{10,... | collective-permute-start | bytes 442376 | tf_op jit(solution)/shard_map/ppermute | solution.py:250
  22.2 5.6 %collective-permute-done.7.refs_4_ = bf16[64,576]{1,0:T(8,128)(2,1)S(1)} collective-permute-done((bf16[64,576]{1,0:T(8,128)(2,1)S(1)}, bf16[64,576]{1,0:T(8,128)(2,1)S(1)}, u32[]{:S(2)}, u32[]{:S(2)}) %collective-permute-start.7) | collective-permute-done | bytes 73760 | tf_op jit(solution)/shard_map/ppermute | solution.py:227
  28.8 1.7 %collective-permute-start.9 = (bf16[32,1152]{1,0:T(8,128)(2,1)S(1)}, bf16[32,1152]{1,0:T(8,128)(2,1)S(1)}, u32[]{:S(2)}, u32[]{:S(2)}) collective-permute-start(bf16[32,1152]{1,0:T(8,128)(2,1)S(1)} %get-tuple-element.43), channel_id=1, source_target_pairs={{0,8},{4,12},{8,0},{12,4},{16,24},{20,28},{24,16},{28,20},{1,9},{5... | collective-permute-start | bytes 221192 | tf_op jit(solution)/shard_map/ppermute | solution.py:227
  30.5 2.6 %collective-permute-start.10 = (bf16[32,1152]{1,0:T(8,128)(2,1)S(1)}, bf16[32,1152]{1,0:T(8,128)(2,1)S(1)}, u32[]{:S(2)}, u32[]{:S(2)}) collective-permute-start(bf16[32,1152]{1,0:T(8,128)(2,1)S(1)} %get-tuple-element.44), channel_id=1, source_target_pairs={{0,16},{4,20},{8,24},{12,28},{16,0},{20,4},{24,8},{28,12},{1,17},{... | collective-permute-start | bytes 221192 | tf_op jit(solution)/shard_map/ppermute | solution.py:227
  33.9 3.6 %collective-permute-done.10.refs_1_ = bf16[32,1152]{1,0:T(8,128)(2,1)S(1)} collective-permute-done((bf16[32,1152]{1,0:T(8,128)(2,1)S(1)}, bf16[32,1152]{1,0:T(8,128)(2,1)S(1)}, u32[]{:S(2)}, u32[]{:S(2)}) %collective-permute-start.10) | collective-permute-done | bytes 73760 | tf_op jit(solution)/shard_map/ppermute | solution.py:227
  37.5 1.7 %collective-permute-done.11.refs_2_ = bf16[32,1152]{1,0:T(8,128)(2,1)S(1)} collective-permute-done((bf16[32,1152]{1,0:T(8,128)(2,1)S(1)}, bf16[32,1152]{1,0:T(8,128)(2,1)S(1)}, u32[]{:S(2)}, u32[]{:S(2)}) %collective-permute-start.11) | collective-permute-done | bytes 73760 | tf_op jit(solution)/shard_map/ppermute | solution.py:227
  39.3 1.7 %collective-permute-start.15 = (bf16[128,1152]{1,0:T(8,128)(2,1)S(1)}, bf16[128,1152]{1,0:T(8,128)(2,1)S(1)}, u32[]{:S(2)}, u32[]{:S(2)}) collective-permute-start(bf16[128,1152]{1,0:T(8,128)(2,1)S(1)} %shard_map.69.refs_4_), channel_id=1, source_target_pairs={{0,2},{1,3},{2,0},{3,1},{4,6},{5,7},{6,4},{7,5},{8,10},{9,11},{10,... | collective-permute-start | bytes 884744 | tf_op jit(solution)/shard_map/ppermute | solution.py:227
  41.0 1.9 %shard_map.70 = (f32[64,1152]{1,0:T(8,128)S(1)}, bf16[64,576]{1,0:T(8,128)(2,1)S(1)}) custom-call(bf16[864,1152]{1,0:T(8,128)(2,1)S(1)} %copy-done.2, bf16[864,1152]{1,0:T(8,128)(2,1)S(1)} %collective-permute-done.14.refs_1_, bf16[288,1152]{1,0:T(8,128)(2,1)S(1)} %copy-done.3, bf16[288,1152]{1,0:T(8,128)(2,1)S(1)} %collective-permute-done.13.refs_3_.refs_1_, ...), custom_call_target="tpu_custom_call" | custom-call | flops 1 | bytes 1 | tf_op jit(solution)/shard_map/pallas_call | solution.py:214
  42.9 1.5 %collective-permute-start.16 = (bf16[64,576]{1,0:T(8,128)(2,1)S(1)}, bf16[64,576]{1,0:T(8,128)(2,1)S(1)}, u32[]{:S(2)}, u32[]{:S(2)}) collective-permute-start(bf16[64,576]{1,0:T(8,128)(2,1)S(1)} %get-tuple-element.51), channel_id=1, source_target_pairs={{0,4},{4,0},{8,12},{12,8},{16,20},{20,16},{24,28},{28,24},{1,5},{5... | collective-permute-start | bytes 221192 | tf_op jit(solution)/shard_map/ppermute | solution.py:227
  44.5 1.6 %collective-permute-done.15.refs_4_ = bf16[128,1152]{1,0:T(8,128)(2,1)S(1)} collective-permute-done((bf16[128,1152]{1,0:T(8,128)(2,1)S(1)}, bf16[128,1152]{1,0:T(8,128)(2,1)S(1)}, u32[]{:S(2)}, u32[]{:S(2)}) %collective-permute-start.15) | collective-permute-done | bytes 294944 | tf_op jit(solution)/shard_map/ppermute | solution.py:227
  46.1 1.3 %collective-permute-done.16.refs_4_ = bf16[64,576]{1,0:T(8,128)(2,1)S(1)} collective-permute-done((bf16[64,576]{1,0:T(8,128)(2,1)S(1)}, bf16[64,576]{1,0:T(8,128)(2,1)S(1)}, u32[]{:S(2)}, u32[]{:S(2)}) %collective-permute-start.16) | collective-permute-done | bytes 73760 | tf_op jit(solution)/shard_map/ppermute | solution.py:227
  47.4 2.0 %shard_map.71 = (bf16[64,1152]{1,0:T(8,128)(2,1)S(1)}, bf16[64,1152]{1,0:T(8,128)(2,1)S(1)}) custom-call(bf16[864,1152]{1,0:T(8,128)(2,1)S(1)} %copy-done.2, bf16[864,1152]{1,0:T(8,128)(2,1)S(1)} %collective-permute-done.14.refs_1_, bf16[288,1152]{1,0:T(8,128)(2,1)S(1)} %copy-done.3, bf16[288,1152]{1,0:T(8,128)(2,1)S(1)} %collective-permute-done.13.refs_3_.refs_1_, ...), custom_call_target="tpu_custom_call" | custom-call | flops 1 | bytes 1 | tf_op jit(solution)/shard_map/pallas_call | solution.py:214
  49.9 2.5 %collective-permute-start.18 = (bf16[64,1152]{1,0:T(8,128)(2,1)S(1)}, bf16[64,1152]{1,0:T(8,128)(2,1)S(1)}, u32[]{:S(2)}, u32[]{:S(2)}) collective-permute-start(bf16[64,1152]{1,0:T(8,128)(2,1)S(1)} %get-tuple-element.54), channel_id=1, source_target_pairs={{0,6},{1,7},{2,4},{3,5},{4,2},{5,3},{6,0},{7,1},{8,14},{9,15},{10,... | collective-permute-start | bytes 442376 | tf_op jit(solution)/shard_map/ppermute | solution.py:250
  53.0 3.2 %collective-permute-done.17.refs_3_ = bf16[64,1152]{1,0:T(8,128)(2,1)S(1)} collective-permute-done((bf16[64,1152]{1,0:T(8,128)(2,1)S(1)}, bf16[64,1152]{1,0:T(8,128)(2,1)S(1)}, u32[]{:S(2)}, u32[]{:S(2)}) %collective-permute-start.17) | collective-permute-done | bytes 147488 | tf_op jit(solution)/shard_map/ppermute | solution.py:227
  56.6 0.9 %collective-permute-start.19 = (bf16[32,1152]{1,0:T(8,128)(2,1)S(1)}, bf16[32,1152]{1,0:T(8,128)(2,1)S(1)}, u32[]{:S(2)}, u32[]{:S(2)}) collective-permute-start(bf16[32,1152]{1,0:T(8,128)(2,1)S(1)} %get-tuple-element.55), channel_id=1, source_target_pairs={{0,8},{4,12},{8,0},{12,4},{16,24},{20,28},{24,16},{28,20},{1,9},{5... | collective-permute-start | bytes 221192 | tf_op jit(solution)/shard_map/ppermute | solution.py:227
  57.5 1.7 %collective-permute-start.20 = (bf16[32,1152]{1,0:T(8,128)(2,1)S(1)}, bf16[32,1152]{1,0:T(8,128)(2,1)S(1)}, u32[]{:S(2)}, u32[]{:S(2)}) collective-permute-start(bf16[32,1152]{1,0:T(8,128)(2,1)S(1)} %get-tuple-element.56), channel_id=1, source_target_pairs={{0,16},{4,20},{8,24},{12,28},{16,0},{20,4},{24,8},{28,12},{1,17},{... | collective-permute-start | bytes 221192 | tf_op jit(solution)/shard_map/ppermute | solution.py:227
  59.1 1.9 %collective-permute-start.21 = (bf16[32,1152]{1,0:T(8,128)(2,1)S(1)}, bf16[32,1152]{1,0:T(8,128)(2,1)S(1)}, u32[]{:S(2)}, u32[]{:S(2)}) collective-permute-start(bf16[32,1152]{1,0:T(8,128)(2,1)S(1)} %get-tuple-element.57), channel_id=1, source_target_pairs={{0,24},{4,28},{8,16},{12,20},{16,8},{20,12},{24,0},{28,4},{1,25},{... | collective-permute-start | bytes 221192 | tf_op jit(solution)/shard_map/ppermute | solution.py:227
  61.1 1.7 %collective-permute-done.20.refs_1_ = bf16[32,1152]{1,0:T(8,128)(2,1)S(1)} collective-permute-done((bf16[32,1152]{1,0:T(8,128)(2,1)S(1)}, bf16[32,1152]{1,0:T(8,128)(2,1)S(1)}, u32[]{:S(2)}, u32[]{:S(2)}) %collective-permute-start.20) | collective-permute-done | bytes 73760 | tf_op jit(solution)/shard_map/ppermute | solution.py:227
  62.7 2.7 %collective-permute-done.21.refs_2_ = bf16[32,1152]{1,0:T(8,128)(2,1)S(1)} collective-permute-done((bf16[32,1152]{1,0:T(8,128)(2,1)S(1)}, bf16[32,1152]{1,0:T(8,128)(2,1)S(1)}, u32[]{:S(2)}, u32[]{:S(2)}) %collective-permute-start.21) | collective-permute-done | bytes 73760 | tf_op jit(solution)/shard_map/ppermute | solution.py:227
  65.4 0.8 %shard_map.73 = bf16[8,16,1152]{2,1,0:T(8,128)(2,1)} custom-call(f32[6,1152]{1,0:T(8,128)S(1)} %copy-done.8, bf16[4,16,1152]{2,1,0:T(8,128)(2,1)S(1)} %get-tuple-element.41.kept_ref, bf16[4,16,1152]{2,1,0:T(8,128)(2,1)S(1)} %collective-permute-done.12.other_ref, bf16[32,1152]{1,0:T(8,128)(2,1)S(1)} %collective-permute-done.19.refs_0_, ...), custom_call_target="tpu_custom_call" | custom-call | flops 1 | bytes 1 | tf_op jit(solution)/shard_map/pallas_call | solution.py:214
  (40 shorter events, 5.0 us)
Async XLA Ops:
  0.0 3.0 %collective-permute-start = (bf16[1,128,1152]{2,1,0:T(8,128)(2,1)}, bf16[1,128,1152]{2,1,0:T(8,128)(2,1)S(1)}, u32[]{:S(2)}, u32[]{:S(2)}) collective-permute-start(bf16[1,128,1152]{2,1,0:T(8,128)(2,1)} %own_ref.3), channel_id=1, source_target_pairs={{0,1},{1,0},{2,3},{3,2},{4,5},{5,4},{6,7},{7,6},{8,9},{9,8},{10,11... | collective-permute-start | bytes 884744 | tf_op jit(solution)/shard_map/ppermute | solution.py:227
  0.5 10.4 %collective-permute-start.3 = (bf16[1,128,1152]{2,1,0:T(8,128)(2,1)}, bf16[1,128,1152]{2,1,0:T(8,128)(2,1)S(1)}, u32[]{:S(2)}, u32[]{:S(2)}) collective-permute-start(bf16[1,128,1152]{2,1,0:T(8,128)(2,1)} %own_ref.3), channel_id=1, source_target_pairs={{0,2},{1,3},{2,0},{3,1},{4,6},{5,7},{6,4},{7,5},{8,10},{9,11},{10,... | collective-permute-start | bytes 884744 | tf_op jit(solution)/shard_map/ppermute | solution.py:227
  3.0 1.0 %copy-start.4 = (bf16[1,128,1152]{2,1,0:T(8,128)(2,1)S(1)}, bf16[1,128,1152]{2,1,0:T(8,128)(2,1)}, u32[]{:S(2)}) copy-start(bf16[1,128,1152]{2,1,0:T(8,128)(2,1)} %own_ref.3) | copy-start | bytes 884740
  4.0 6.8 %collective-permute-start.1 = (bf16[64,1152]{1,0:T(8,128)(2,1)S(1)}, bf16[64,1152]{1,0:T(8,128)(2,1)S(1)}, u32[]{:S(2)}, u32[]{:S(2)}) collective-permute-start(bf16[64,1152]{1,0:T(8,128)(2,1)S(1)} %shard_map.64), channel_id=1, source_target_pairs={{0,4},{4,0},{8,12},{12,8},{16,20},{20,16},{24,28},{28,24},{1,5},{5... | collective-permute-start | bytes 442376 | tf_op jit(solution)/shard_map/ppermute | solution.py:227
  5.8 1.6 %copy-start = (bf16[864,1152]{1,0:T(8,128)(2,1)S(1)}, bf16[864,1152]{1,0:T(8,128)(2,1)}, u32[]{:S(2)}) copy-start(bf16[864,1152]{1,0:T(8,128)(2,1)} %weight_ref.3) | copy-start | bytes 5971972
  7.4 0.8 %copy-start.7 = (f32[6,1152]{1,0:T(8,128)S(1)}, f32[6,1152]{1,0:T(8,128)}, u32[]{:S(2)}) copy-start(f32[6,1152]{1,0:T(8,128)} %mod_ref.7) | copy-start | bytes 82948
  8.1 4.4 %copy-start.6 = (bf16[288,1152]{1,0:T(8,128)(2,1)S(1)}, bf16[288,1152]{1,0:T(8,128)(2,1)}, u32[]{:S(2)}) copy-start(bf16[288,1152]{1,0:T(8,128)(2,1)} %refs_0_.4) | copy-start | bytes 1990660
  8.1 4.8 %copy-start.1 = (bf16[864,1152]{1,0:T(8,128)(2,1)S(1)}, bf16[864,1152]{1,0:T(8,128)(2,1)}, u32[]{:S(2)}) copy-start(bf16[864,1152]{1,0:T(8,128)(2,1)} %weight_ref.3) | copy-start | bytes 5971972
  9.2 9.2 %copy-start.3 = (bf16[288,1152]{1,0:T(8,128)(2,1)S(1)}, bf16[288,1152]{1,0:T(8,128)(2,1)}, u32[]{:S(2)}) copy-start(bf16[288,1152]{1,0:T(8,128)(2,1)} %refs_0_.7) | copy-start | bytes 1990660
  9.3 18.8 %copy-start.5 = (bf16[1,128,1152]{2,1,0:T(8,128)(2,1)S(1)}, bf16[1,128,1152]{2,1,0:T(8,128)(2,1)}, u32[]{:S(2)}) copy-start(bf16[1,128,1152]{2,1,0:T(8,128)(2,1)} %own_ref.3) | copy-start | bytes 884740
  10.9 1.6 %collective-permute-start.4 = (bf16[1,128,1152]{2,1,0:T(8,128)(2,1)S(1)}, bf16[1,128,1152]{2,1,0:T(8,128)(2,1)S(1)}, u32[]{:S(2)}, u32[]{:S(2)}) collective-permute-start(bf16[1,128,1152]{2,1,0:T(8,128)(2,1)S(1)} %collective-permute-done.3.refs_0_), channel_id=1, source_target_pairs={{0,1},{1,0},{2,3},{3,2},{4,5},{5,4},{6,7},{7,6},{8,9},{9,8},{10,11... | collective-permute-start | bytes 884744 | tf_op jit(solution)/shard_map/ppermute | solution.py:227
  12.4 28.5 %collective-permute-start.14 = (bf16[864,1152]{1,0:T(8,128)(2,1)}, bf16[864,1152]{1,0:T(8,128)(2,1)S(1)}, u32[]{:S(2)}, u32[]{:S(2)}) collective-permute-start(bf16[864,1152]{1,0:T(8,128)(2,1)} %refs_0_.6), channel_id=1, source_target_pairs={{0,1},{1,0},{2,3},{3,2},{4,5},{5,4},{6,7},{7,6},{8,9},{9,8},{10,11... | collective-permute-start | bytes 5971976 | tf_op jit(solution)/shard_map/ppermute | solution.py:227
  12.6 5.1 %collective-permute-start.2 = (bf16[288,1152]{1,0:T(8,128)(2,1)S(1)}, bf16[288,1152]{1,0:T(8,128)(2,1)S(1)}, u32[]{:S(2)}, u32[]{:S(2)}) collective-permute-start(bf16[288,1152]{1,0:T(8,128)(2,1)S(1)} %copy-done.6), channel_id=1, source_target_pairs={{0,1},{1,0},{2,3},{3,2},{4,5},{5,4},{6,7},{7,6},{8,9},{9,8},{10,11... | collective-permute-start | bytes 1990664 | tf_op jit(solution)/shard_map/ppermute | solution.py:227
  16.3 1.4 %collective-permute-start.5 = (bf16[288,256]{1,0:T(8,128)(2,1)S(1)}, bf16[288,256]{1,0:T(8,128)(2,1)S(1)}, u32[]{:S(2)}, u32[]{:S(2)}) collective-permute-start(bf16[288,256]{1,0:T(8,128)(2,1)S(1)} %get-tuple-element.36), channel_id=1, source_target_pairs={{0,1},{1,0},{2,3},{3,2},{4,5},{5,4},{6,7},{7,6},{8,9},{9,8},{10,11... | collective-permute-start | bytes 442376 | tf_op jit(solution)/shard_map/ppermute | solution.py:227
  17.7 23.3 %copy-start.2 = (bf16[864,1152]{1,0:T(8,128)(2,1)S(1)}, bf16[864,1152]{1,0:T(8,128)(2,1)}, u32[]{:S(2)}) copy-start(bf16[864,1152]{1,0:T(8,128)(2,1)} %refs_0_.6) | copy-start | bytes 5971972
  18.5 22.5 %collective-permute-start.13 = (bf16[288,1152]{1,0:T(8,128)(2,1)S(1)}, bf16[288,1152]{1,0:T(8,128)(2,1)S(1)}, u32[]{:S(2)}, u32[]{:S(2)}) collective-permute-start(bf16[288,1152]{1,0:T(8,128)(2,1)S(1)} %copy-done.3), channel_id=1, source_target_pairs={{0,1},{1,0},{2,3},{3,2},{4,5},{5,4},{6,7},{7,6},{8,9},{9,8},{10,11... | collective-permute-start | bytes 1990664 | tf_op jit(solution)/shard_map/ppermute | solution.py:227
  18.7 9.1 %collective-permute-start.6 = (bf16[64,1152]{1,0:T(8,128)(2,1)S(1)}, bf16[64,1152]{1,0:T(8,128)(2,1)S(1)}, u32[]{:S(2)}, u32[]{:S(2)}) collective-permute-start(bf16[64,1152]{1,0:T(8,128)(2,1)S(1)} %get-tuple-element.38), channel_id=1, source_target_pairs={{0,2},{1,3},{2,0},{3,1},{4,6},{5,7},{6,4},{7,5},{8,10},{9,11},{10,... | collective-permute-start | bytes 442376 | tf_op jit(solution)/shard_map/ppermute | solution.py:227
  20.4 7.6 %collective-permute-start.8 = (bf16[64,1152]{1,0:T(8,128)(2,1)S(1)}, bf16[64,1152]{1,0:T(8,128)(2,1)S(1)}, u32[]{:S(2)}, u32[]{:S(2)}) collective-permute-start(bf16[64,1152]{1,0:T(8,128)(2,1)S(1)} %get-tuple-element.40), channel_id=1, source_target_pairs={{0,6},{1,7},{2,4},{3,5},{4,2},{5,3},{6,0},{7,1},{8,14},{9,15},{10,... | collective-permute-start | bytes 442376 | tf_op jit(solution)/shard_map/ppermute | solution.py:250
  21.9 5.9 %collective-permute-start.7 = (bf16[64,576]{1,0:T(8,128)(2,1)S(1)}, bf16[64,576]{1,0:T(8,128)(2,1)S(1)}, u32[]{:S(2)}, u32[]{:S(2)}) collective-permute-start(bf16[64,576]{1,0:T(8,128)(2,1)S(1)} %get-tuple-element.39), channel_id=1, source_target_pairs={{0,4},{4,0},{8,12},{12,8},{16,20},{20,16},{24,28},{28,24},{1,5},{5... | collective-permute-start | bytes 221192 | tf_op jit(solution)/shard_map/ppermute | solution.py:227
  28.8 5.2 %collective-permute-start.9 = (bf16[32,1152]{1,0:T(8,128)(2,1)S(1)}, bf16[32,1152]{1,0:T(8,128)(2,1)S(1)}, u32[]{:S(2)}, u32[]{:S(2)}) collective-permute-start(bf16[32,1152]{1,0:T(8,128)(2,1)S(1)} %get-tuple-element.43), channel_id=1, source_target_pairs={{0,8},{4,12},{8,0},{12,4},{16,24},{20,28},{24,16},{28,20},{1,9},{5... | collective-permute-start | bytes 221192 | tf_op jit(solution)/shard_map/ppermute | solution.py:227
  30.5 7.0 %collective-permute-start.10 = (bf16[32,1152]{1,0:T(8,128)(2,1)S(1)}, bf16[32,1152]{1,0:T(8,128)(2,1)S(1)}, u32[]{:S(2)}, u32[]{:S(2)}) collective-permute-start(bf16[32,1152]{1,0:T(8,128)(2,1)S(1)} %get-tuple-element.44), channel_id=1, source_target_pairs={{0,16},{4,20},{8,24},{12,28},{16,0},{20,4},{24,8},{28,12},{1,17},{... | collective-permute-start | bytes 221192 | tf_op jit(solution)/shard_map/ppermute | solution.py:227
  33.1 6.2 %collective-permute-start.11 = (bf16[32,1152]{1,0:T(8,128)(2,1)S(1)}, bf16[32,1152]{1,0:T(8,128)(2,1)S(1)}, u32[]{:S(2)}, u32[]{:S(2)}) collective-permute-start(bf16[32,1152]{1,0:T(8,128)(2,1)S(1)} %get-tuple-element.45), channel_id=1, source_target_pairs={{0,24},{4,28},{8,16},{12,20},{16,8},{20,12},{24,0},{28,4},{1,25},{... | collective-permute-start | bytes 221192 | tf_op jit(solution)/shard_map/ppermute | solution.py:227
  39.3 6.8 %collective-permute-start.15 = (bf16[128,1152]{1,0:T(8,128)(2,1)S(1)}, bf16[128,1152]{1,0:T(8,128)(2,1)S(1)}, u32[]{:S(2)}, u32[]{:S(2)}) collective-permute-start(bf16[128,1152]{1,0:T(8,128)(2,1)S(1)} %shard_map.69.refs_4_), channel_id=1, source_target_pairs={{0,2},{1,3},{2,0},{3,1},{4,6},{5,7},{6,4},{7,5},{8,10},{9,11},{10,... | collective-permute-start | bytes 884744 | tf_op jit(solution)/shard_map/ppermute | solution.py:227
  42.9 4.5 %collective-permute-start.16 = (bf16[64,576]{1,0:T(8,128)(2,1)S(1)}, bf16[64,576]{1,0:T(8,128)(2,1)S(1)}, u32[]{:S(2)}, u32[]{:S(2)}) collective-permute-start(bf16[64,576]{1,0:T(8,128)(2,1)S(1)} %get-tuple-element.51), channel_id=1, source_target_pairs={{0,4},{4,0},{8,12},{12,8},{16,20},{20,16},{24,28},{28,24},{1,5},{5... | collective-permute-start | bytes 221192 | tf_op jit(solution)/shard_map/ppermute | solution.py:227
  49.4 16.0 %copy-start.8 = (f32[6,1152]{1,0:T(8,128)S(1)}, f32[6,1152]{1,0:T(8,128)}, u32[]{:S(2)}) copy-start(f32[6,1152]{1,0:T(8,128)} %mod_ref.7) | copy-start | bytes 82948
  49.4 6.8 %collective-permute-start.17 = (bf16[64,1152]{1,0:T(8,128)(2,1)S(1)}, bf16[64,1152]{1,0:T(8,128)(2,1)S(1)}, u32[]{:S(2)}, u32[]{:S(2)}) collective-permute-start(bf16[64,1152]{1,0:T(8,128)(2,1)S(1)} %get-tuple-element.53), channel_id=1, source_target_pairs={{0,2},{1,3},{2,0},{3,1},{4,6},{5,7},{6,4},{7,5},{8,10},{9,11},{10,... | collective-permute-start | bytes 442376 | tf_op jit(solution)/shard_map/ppermute | solution.py:227
  49.9 6.3 %collective-permute-start.18 = (bf16[64,1152]{1,0:T(8,128)(2,1)S(1)}, bf16[64,1152]{1,0:T(8,128)(2,1)S(1)}, u32[]{:S(2)}, u32[]{:S(2)}) collective-permute-start(bf16[64,1152]{1,0:T(8,128)(2,1)S(1)} %get-tuple-element.54), channel_id=1, source_target_pairs={{0,6},{1,7},{2,4},{3,5},{4,2},{5,3},{6,0},{7,1},{8,14},{9,15},{10,... | collective-permute-start | bytes 442376 | tf_op jit(solution)/shard_map/ppermute | solution.py:250
  52.4 8.6 %collective-permute-start.12 = (bf16[4,16,1152]{2,1,0:T(8,128)(2,1)S(1)}, bf16[4,16,1152]{2,1,0:T(8,128)(2,1)S(1)}, u32[]{:S(2)}, u32[]{:S(2)}) collective-permute-start(bf16[4,16,1152]{2,1,0:T(8,128)(2,1)S(1)} %get-tuple-element.47), channel_id=1, source_target_pairs={{0,4},{4,0},{8,12},{12,8},{16,20},{20,16},{24,28},{28,24},{1,5},{5... | collective-permute-start | bytes 442376 | tf_op jit(solution)/shard_map/ppermute | solution.py:227
  56.6 4.5 %collective-permute-start.19 = (bf16[32,1152]{1,0:T(8,128)(2,1)S(1)}, bf16[32,1152]{1,0:T(8,128)(2,1)S(1)}, u32[]{:S(2)}, u32[]{:S(2)}) collective-permute-start(bf16[32,1152]{1,0:T(8,128)(2,1)S(1)} %get-tuple-element.55), channel_id=1, source_target_pairs={{0,8},{4,12},{8,0},{12,4},{16,24},{20,28},{24,16},{28,20},{1,9},{5... | collective-permute-start | bytes 221192 | tf_op jit(solution)/shard_map/ppermute | solution.py:227
  57.5 5.3 %collective-permute-start.20 = (bf16[32,1152]{1,0:T(8,128)(2,1)S(1)}, bf16[32,1152]{1,0:T(8,128)(2,1)S(1)}, u32[]{:S(2)}, u32[]{:S(2)}) collective-permute-start(bf16[32,1152]{1,0:T(8,128)(2,1)S(1)} %get-tuple-element.56), channel_id=1, source_target_pairs={{0,16},{4,20},{8,24},{12,28},{16,0},{20,4},{24,8},{28,12},{1,17},{... | collective-permute-start | bytes 221192 | tf_op jit(solution)/shard_map/ppermute | solution.py:227
  59.1 6.3 %collective-permute-start.21 = (bf16[32,1152]{1,0:T(8,128)(2,1)S(1)}, bf16[32,1152]{1,0:T(8,128)(2,1)S(1)}, u32[]{:S(2)}, u32[]{:S(2)}) collective-permute-start(bf16[32,1152]{1,0:T(8,128)(2,1)S(1)} %get-tuple-element.57), channel_id=1, source_target_pairs={{0,24},{4,28},{8,16},{12,20},{16,8},{20,12},{24,0},{28,4},{1,25},{... | collective-permute-start | bytes 221192 | tf_op jit(solution)/shard_map/ppermute | solution.py:227

commit v16 on v12

--- a/solution.py
+++ b/solution.py
@@ -95,8 +95,9 @@
     return jnp.where(first, even, odd), jnp.where(first, odd, even)
 
 
-def share_kernel(period, token_ref, sent_ref):
-    sent_ref[...] = of_this_half(token_ref[0], period)[1].astype(BF16)
+def share_kernel(period, token_ref, kept_ref, sent_ref):
+    for ref, half in zip((kept_ref, sent_ref), of_this_half(token_ref[0], period)):
+        ref[...] = half.astype(BF16)
 
 
 def joined(refs):
@@ -118,17 +119,22 @@
             ref[...] = part.astype(ref.dtype)
 
 
-def total_updates(groups, weight_refs, refs):
-    kept = sum(ref[...].astype(F32) for ref in refs[:groups])
-    paired = dot(refs[groups][...], joined(weight_refs))
-    return kept, paired + sum(ref[...].astype(F32) for ref in refs[groups + 1 : 2 * groups])
+def paired_kernel(head_ref, *refs):
+    refs[-1][...] = dot(head_ref[...], joined(refs[:-1]))
+
+
+def total_updates(groups, refs):
+    return [
+        sum(ref[...].astype(F32) for ref in refs[at * groups : (at + 1) * groups])
+        for at in range(2)
+    ]
 
 
 def middle_kernel(pieces, groups, mod_ref, own_ref, paired_ref, *refs):
-    kept_ref, sent_ref, *piece_refs, scratch = refs[2 + 2 * groups :]
-    updates = total_updates(groups, refs[:2], refs[2:])
+    kept_ref, sent_ref, *piece_refs, scratch = refs[2 * groups :]
+    updates = total_updates(groups, refs)
     _, period, width = kept_ref.shape
-    inputs = (of_this_half(own_ref[0], period)[0], paired_ref[...])
+    inputs = (own_ref[...], paired_ref[...])
     for at, (tokens, middle_ref) in enumerate(zip(inputs, (kept_ref, sent_ref))):
         update = updates[at]
         middle = (tokens.astype(F32) + mod_ref[2:3, :] * update).astype(BF16)
@@ -187,9 +193,9 @@
 
 
 def sum_kernel(groups, *refs):
-    piece_refs = refs[2 + 2 * groups :]
+    piece_refs = refs[2 * groups :]
     period = piece_refs[0].shape[0] // 2
-    for at, update in enumerate(total_updates(groups, refs[:2], refs[2:])):
+    for at, update in enumerate(total_updates(groups, refs)):
         update = update.astype(BF16)
         for piece, ref in enumerate(piece_refs):
             rows = update[piece * period : (piece + 1) * period]
@@ -265,6 +271,10 @@
         offsets = reversed(range(pieces))
         return [swap(part, "frame", 2 * at) if at else part for at, part in zip(offsets, parts)]
 
+    def project_paired(sent, weights):
+        heads = swap(sent, "frame", 1)
+        return call(paired_kernel, (heads, *weights), [halves_shape(F32)])[0]
+
     def return_updates(own, far):
         same = [swap(part, "patch", 2 * at) for at, part in enumerate(far[::2], 1)]
         diagonal = [swap_diagonal(part, 2 * at) for at, part in enumerate(far[1::2], 1)]
@@ -284,8 +294,8 @@
         (modulation, spatial_qkv, tokens, sister),
         [shape((3 * shard, 2 * rows), F32)],
     )
-    (shared,) = call(
-        functools.partial(share_kernel, period), (after(tokens, sister),), [halves_shape(BF16)]
+    own_tokens, shared = call(
+        functools.partial(share_kernel, period), (after(tokens, sister),), [halves_shape(BF16)] * 2
     )
     paired = swap(shared, "frame", 1)
     out_pair = with_sister(spatial_out, near)
@@ -304,10 +314,10 @@
         own_shapes + far_shapes,
     )
     late_pair = with_sister(temporal_out, parts[0])
-    updates = return_updates((parts[0], swap(parts[1], "frame", 1)), parts[2:])
+    updates = return_updates((parts[0], project_paired(parts[1], out_pair)), parts[2:])
     middle, middle_sent, *parts = call(
         functools.partial(middle_kernel, pieces, groups),
-        (modulation, tokens, paired, *out_pair, *updates),
+        (modulation, own_tokens, paired, *updates),
         [shape((pieces, period, width), BF16)] * 2 + piece_shapes,
         [pltpu.VMEM((pieces, 2 * period, width), BF16)],
     )
@@ -325,14 +335,14 @@
         )
 
     kept, sent = attend_frames(True, [segment], own_shapes)
-    received = swap(sent, "frame", 1)
+    received = project_paired(sent, late_pair)
     middle_other = swap(after(middle_sent, segment), "frame", 1)
     others = [after(block, received) for block in segments[1:]]
     far_parts = attend_frames(False, others, far_shapes)
     updates = return_updates((kept, received), far_parts)
     parts = call(
         functools.partial(sum_kernel, groups),
-        (*late_pair, *updates),
+        updates,
         piece_shapes,
     )
     (result,) = call(

time: 66.6 us -> 65.8 us (0.988)
  waiting for transfers between devices: 26.8 us -> 26 us
    pallas_call x10 -> x12, Pallas kernels: 11 us -> 11.1 us  [call(): pl.pallas_call(body, out_shape=outs, in_specs=[pl.BlockSpec(memory_space=...]
    unnamed x18 -> x16, local copies, waits for them, and re-layouts: 3.34 us -> 3.34 us
  transfers between devices with their start and end apart: 22 -> 22, of which waited for: 12 -> 11; matrix products, arithmetic and copies ran while one was open for 0% -> 0% of each run, Pallas kernels for 12% -> 13%
where the time goes in v16:
time: 65.8 us; the launch traced here: 65.5 us
  waiting for transfers between devices  26 us (40%)
  starting transfers between devices  24.9 us (38%)
  Pallas kernels  11.1 us (17%)
  local copies, waits for them, and re-layouts  3.34 us (5%)
    ppermute x20, waiting for transfers between devices, swap(): return lax.ppermute(value, axis, [(at, at ^ offset) for at in range(size)])  24.8 us
    ppermute x20, starting transfers between devices, swap(): return lax.ppermute(value, axis, [(at, at ^ offset) for at in range(size)])  22 us
    pallas_call x12, Pallas kernels, call(): pl.pallas_call(body, out_shape=outs, in_specs=[pl.BlockSpec(memory_space=...  11.1 us
    unnamed x16, local copies, waits for them, and re-layouts  3.34 us
    ppermute x2, starting transfers between devices, swap_diagonal(): return lax.ppermute(value, ('frame', 'patch'), pairs)  2.85 us
  transfers between devices with their start and end apart: 22, of which 11 were waited for; matrix products, arithmetic and copies ran while one was open for 0% of the time, Pallas kernels for 13%

profile of v16, /device:TPU:0, one launch (start us, length us, event | category | flops | bytes accessed | tf_op | source)
XLA Modules:
  0.0 65.5 jit_solution(9016302634387763271)
XLA Ops:
  0.5 2.5 %collective-permute-start.2 = (bf16[1,128,1152]{2,1,0:T(8,128)(2,1)}, bf16[1,128,1152]{2,1,0:T(8,128)(2,1)S(1)}, u32[]{:S(2)}, u32[]{:S(2)}) collective-permute-start(bf16[1,128,1152]{2,1,0:T(8,128)(2,1)} %own_ref.1), channel_id=1, source_target_pairs={{0,2},{1,3},{2,0},{3,1},{4,6},{5,7},{6,4},{7,5},{8,10},{9,11},{10,... | collective-permute-start | bytes 884744 | tf_op jit(solution)/shard_map/ppermute | solution.py:233
  3.0 1.0 %copy-done.5 = bf16[1,128,1152]{2,1,0:T(8,128)(2,1)S(1)} copy-done((bf16[1,128,1152]{2,1,0:T(8,128)(2,1)S(1)}, bf16[1,128,1152]{2,1,0:T(8,128)(2,1)}, u32[]{:S(2)}) %copy-start.5) | copy-done | bytes 294936
  4.1 1.8 %collective-permute-start.1 = (bf16[64,1152]{1,0:T(8,128)(2,1)S(1)}, bf16[64,1152]{1,0:T(8,128)(2,1)S(1)}, u32[]{:S(2)}, u32[]{:S(2)}) collective-permute-start(bf16[64,1152]{1,0:T(8,128)(2,1)S(1)} %get-tuple-element.36), channel_id=1, source_target_pairs={{0,4},{4,0},{8,12},{12,8},{16,20},{20,16},{24,28},{28,24},{1,5},{5... | collective-permute-start | bytes 442376 | tf_op jit(solution)/shard_map/ppermute | solution.py:233
  5.9 1.6 %copy-done = bf16[864,1152]{1,0:T(8,128)(2,1)S(1)} copy-done((bf16[864,1152]{1,0:T(8,128)(2,1)S(1)}, bf16[864,1152]{1,0:T(8,128)(2,1)}, u32[]{:S(2)}) %copy-start) | copy-done | bytes 1990680
  7.4 0.8 %copy-done.6 = f32[6,1152]{1,0:T(8,128)S(1)} copy-done((f32[6,1152]{1,0:T(8,128)S(1)}, f32[6,1152]{1,0:T(8,128)}, u32[]{:S(2)}) %copy-start.6) | copy-done | bytes 27672
  8.2 1.1 %shard_map.65.near_ref = f32[864,256]{1,0:T(8,128)S(1)} custom-call(f32[6,1152]{1,0:T(8,128)S(1)} %copy-done.6, bf16[864,1152]{1,0:T(8,128)(2,1)S(1)} %copy-done, bf16[1,128,1152]{2,1,0:T(8,128)(2,1)S(1)} %copy-done.5, bf16[1,128,1152]{2,1,0:T(8,128)(2,1)S(1)} %collective-permute-done.sister_ref), custom_call_target="tpu_custom_call" | custom-call | flops 1 | bytes 1 | tf_op jit(solution)/shard_map/pallas_call | solution.py:220
  9.3 1.6 %collective-permute-done.2.refs_0_ = bf16[1,128,1152]{2,1,0:T(8,128)(2,1)S(1)} collective-permute-done((bf16[1,128,1152]{2,1,0:T(8,128)(2,1)}, bf16[1,128,1152]{2,1,0:T(8,128)(2,1)S(1)}, u32[]{:S(2)}, u32[]{:S(2)}) %collective-permute-start.2) | collective-permute-done | bytes 294944 | tf_op jit(solution)/shard_map/ppermute | solution.py:233
  10.9 1.6 %collective-permute-done.3.refs_1_ = bf16[1,128,1152]{2,1,0:T(8,128)(2,1)S(1)} collective-permute-done((bf16[1,128,1152]{2,1,0:T(8,128)(2,1)S(1)}, bf16[1,128,1152]{2,1,0:T(8,128)(2,1)S(1)}, u32[]{:S(2)}, u32[]{:S(2)}) %collective-permute-start.3) | collective-permute-done | bytes 294944 | tf_op jit(solution)/shard_map/ppermute | solution.py:233
  13.0 3.3 %shard_map.66 = (bf16[288,256]{1,0:T(8,128)(2,1)S(1)}, bf16[288,256]{1,0:T(8,128)(2,1)S(1)}) custom-call(f32[6,1152]{1,0:T(8,128)S(1)} %copy-done.6, bf16[864,1152]{1,0:T(8,128)(2,1)S(1)} %copy-done.1, f32[864,256]{1,0:T(8,128)S(1)} %shard_map.65.near_ref, bf16[1,128,1152]{2,1,0:T(8,128)(2,1)S(1)} %collective-permute-done.2.refs_0_, ...), custom_call_target="tpu_custom_call" | custom-call | flops 1 | bytes 1 | tf_op jit(solution)/shard_map/pallas_call | solution.py:220
  16.5 1.2 %collective-permute-done.4.refs_1_ = bf16[288,256]{1,0:T(8,128)(2,1)S(1)} collective-permute-done((bf16[288,256]{1,0:T(8,128)(2,1)S(1)}, bf16[288,256]{1,0:T(8,128)(2,1)S(1)}, u32[]{:S(2)}, u32[]{:S(2)}) %collective-permute-start.4) | collective-permute-done | bytes 147488 | tf_op jit(solution)/shard_map/ppermute | solution.py:233
  17.7 0.7 %shard_map.67 = (f32[64,1152]{1,0:T(8,128)S(1)}, bf16[64,576]{1,0:T(8,128)(2,1)S(1)}, bf16[64,1152]{1,0:T(8,128)(2,1)S(1)}, bf16[64,1152]{1,0:T(8,128)(2,1)S(1)}) custom-call(bf16[288,256]{1,0:T(8,128)(2,1)S(1)} %get-tuple-element.38.refs_0_, bf16[288,256]{1,0:T(8,128)(2,1)S(1)} %collective-permute-done.4.refs_1_, bf16[288,1152]{1,0:T(8,128)(2,1)S(1)} %copy-done.4, ...), custom_call_target="tpu_custom_call" | custom-call | flops 1 | bytes 1 | tf_op jit(solution)/shard_map/pallas_call | solution.py:220
  18.7 1.8 %collective-permute-start.6 = (bf16[64,1152]{1,0:T(8,128)(2,1)S(1)}, bf16[64,1152]{1,0:T(8,128)(2,1)S(1)}, u32[]{:S(2)}, u32[]{:S(2)}) collective-permute-start(bf16[64,1152]{1,0:T(8,128)(2,1)S(1)} %get-tuple-element.42), channel_id=1, source_target_pairs={{0,2},{1,3},{2,0},{3,1},{4,6},{5,7},{6,4},{7,5},{8,10},{9,11},{10,... | collective-permute-start | bytes 442376 | tf_op jit(solution)/shard_map/ppermute | solution.py:233
  20.5 1.4 %collective-permute-start.8 = (bf16[64,1152]{1,0:T(8,128)(2,1)S(1)}, bf16[64,1152]{1,0:T(8,128)(2,1)S(1)}, u32[]{:S(2)}, u32[]{:S(2)}) collective-permute-start(bf16[64,1152]{1,0:T(8,128)(2,1)S(1)} %get-tuple-element.44), channel_id=1, source_target_pairs={{0,6},{1,7},{2,4},{3,5},{4,2},{5,3},{6,0},{7,1},{8,14},{9,15},{10,... | collective-permute-start | bytes 442376 | tf_op jit(solution)/shard_map/ppermute | solution.py:256
  22.2 5.6 %collective-permute-done.7.head_ref = bf16[64,576]{1,0:T(8,128)(2,1)S(1)} collective-permute-done((bf16[64,576]{1,0:T(8,128)(2,1)S(1)}, bf16[64,576]{1,0:T(8,128)(2,1)S(1)}, u32[]{:S(2)}, u32[]{:S(2)}) %collective-permute-start.7) | collective-permute-done | bytes 73760 | tf_op jit(solution)/shard_map/ppermute | solution.py:233
  28.6 3.9 %collective-permute-start.9 = (bf16[32,1152]{1,0:T(8,128)(2,1)S(1)}, bf16[32,1152]{1,0:T(8,128)(2,1)S(1)}, u32[]{:S(2)}, u32[]{:S(2)}) collective-permute-start(bf16[32,1152]{1,0:T(8,128)(2,1)S(1)} %get-tuple-element.47), channel_id=1, source_target_pairs={{0,24},{4,28},{8,16},{12,20},{16,8},{20,12},{24,0},{28,4},{1,25},{... | collective-permute-start | bytes 221192 | tf_op jit(solution)/shard_map/ppermute | solution.py:233
  32.5 0.6 collective-permute-start.11
  33.1 2.5 %collective-permute-done.9.refs_0_ = bf16[32,1152]{1,0:T(8,128)(2,1)S(1)} collective-permute-done((bf16[32,1152]{1,0:T(8,128)(2,1)S(1)}, bf16[32,1152]{1,0:T(8,128)(2,1)S(1)}, u32[]{:S(2)}, u32[]{:S(2)}) %collective-permute-start.9) | collective-permute-done | bytes 73760 | tf_op jit(solution)/shard_map/ppermute | solution.py:233
  35.6 2.7 %collective-permute-done.10.refs_1_ = bf16[32,1152]{1,0:T(8,128)(2,1)S(1)} collective-permute-done((bf16[32,1152]{1,0:T(8,128)(2,1)S(1)}, bf16[32,1152]{1,0:T(8,128)(2,1)S(1)}, u32[]{:S(2)}, u32[]{:S(2)}) %collective-permute-start.10) | collective-permute-done | bytes 73760 | tf_op jit(solution)/shard_map/ppermute | solution.py:233
  38.3 1.6 %collective-permute-start.15 = (bf16[128,1152]{1,0:T(8,128)(2,1)S(1)}, bf16[128,1152]{1,0:T(8,128)(2,1)S(1)}, u32[]{:S(2)}, u32[]{:S(2)}) collective-permute-start(bf16[128,1152]{1,0:T(8,128)(2,1)S(1)} %shard_map.70.refs_4_), channel_id=1, source_target_pairs={{0,2},{1,3},{2,0},{3,1},{4,6},{5,7},{6,4},{7,5},{8,10},{9,11},{10,... | collective-permute-start | bytes 884744 | tf_op jit(solution)/shard_map/ppermute | solution.py:233
  39.9 1.9 %shard_map.71 = (f32[64,1152]{1,0:T(8,128)S(1)}, bf16[64,576]{1,0:T(8,128)(2,1)S(1)}) custom-call(bf16[864,1152]{1,0:T(8,128)(2,1)S(1)} %copy-done.2, bf16[864,1152]{1,0:T(8,128)(2,1)S(1)} %collective-permute-done.13.refs_1_, bf16[288,1152]{1,0:T(8,128)(2,1)S(1)} %copy-done.3, bf16[288,1152]{1,0:T(8,128)(2,1)S(1)} %collective-permute-done.14.refs_3_.refs_1_, ...), custom_call_target="tpu_custom_call" | custom-call | flops 1 | bytes 1 | tf_op jit(solution)/shard_map/pallas_call | solution.py:220
  41.9 1.6 %collective-permute-start.16 = (bf16[64,576]{1,0:T(8,128)(2,1)S(1)}, bf16[64,576]{1,0:T(8,128)(2,1)S(1)}, u32[]{:S(2)}, u32[]{:S(2)}) collective-permute-start(bf16[64,576]{1,0:T(8,128)(2,1)S(1)} %get-tuple-element.55), channel_id=1, source_target_pairs={{0,4},{4,0},{8,12},{12,8},{16,20},{20,16},{24,28},{28,24},{1,5},{5... | collective-permute-start | bytes 221192 | tf_op jit(solution)/shard_map/ppermute | solution.py:233
  43.4 3.0 %collective-permute-done.16.head_ref = bf16[64,576]{1,0:T(8,128)(2,1)S(1)} collective-permute-done((bf16[64,576]{1,0:T(8,128)(2,1)S(1)}, bf16[64,576]{1,0:T(8,128)(2,1)S(1)}, u32[]{:S(2)}, u32[]{:S(2)}) %collective-permute-start.16) | collective-permute-done | bytes 73760 | tf_op jit(solution)/shard_map/ppermute | solution.py:233
  46.8 2.0 %shard_map.73 = (bf16[64,1152]{1,0:T(8,128)(2,1)S(1)}, bf16[64,1152]{1,0:T(8,128)(2,1)S(1)}) custom-call(bf16[864,1152]{1,0:T(8,128)(2,1)S(1)} %copy-done.2, bf16[864,1152]{1,0:T(8,128)(2,1)S(1)} %collective-permute-done.13.refs_1_, bf16[288,1152]{1,0:T(8,128)(2,1)S(1)} %copy-done.3, bf16[288,1152]{1,0:T(8,128)(2,1)S(1)} %collective-permute-done.14.refs_3_.refs_1_, ...), custom_call_target="tpu_custom_call" | custom-call | flops 1 | bytes 1 | tf_op jit(solution)/shard_map/pallas_call | solution.py:220
  48.7 1.6 %collective-permute-start.17 = (bf16[64,1152]{1,0:T(8,128)(2,1)S(1)}, bf16[64,1152]{1,0:T(8,128)(2,1)S(1)}, u32[]{:S(2)}, u32[]{:S(2)}) collective-permute-start(bf16[64,1152]{1,0:T(8,128)(2,1)S(1)} %get-tuple-element.57), channel_id=1, source_target_pairs={{0,2},{1,3},{2,0},{3,1},{4,6},{5,7},{6,4},{7,5},{8,10},{9,11},{10,... | collective-permute-start | bytes 442376 | tf_op jit(solution)/shard_map/ppermute | solution.py:233
  50.3 1.4 %collective-permute-start.18 = (bf16[64,1152]{1,0:T(8,128)(2,1)S(1)}, bf16[64,1152]{1,0:T(8,128)(2,1)S(1)}, u32[]{:S(2)}, u32[]{:S(2)}) collective-permute-start(bf16[64,1152]{1,0:T(8,128)(2,1)S(1)} %get-tuple-element.58), channel_id=1, source_target_pairs={{0,6},{1,7},{2,4},{3,5},{4,2},{5,3},{6,0},{7,1},{8,14},{9,15},{10,... | collective-permute-start | bytes 442376 | tf_op jit(solution)/shard_map/ppermute | solution.py:256
  52.3 3.3 %collective-permute-done.17.refs_1_ = bf16[64,1152]{1,0:T(8,128)(2,1)S(1)} collective-permute-done((bf16[64,1152]{1,0:T(8,128)(2,1)S(1)}, bf16[64,1152]{1,0:T(8,128)(2,1)S(1)}, u32[]{:S(2)}, u32[]{:S(2)}) %collective-permute-start.17) | collective-permute-done | bytes 147488 | tf_op jit(solution)/shard_map/ppermute | solution.py:233
  55.6 1.2 %collective-permute-done.18.refs_3_ = bf16[64,1152]{1,0:T(8,128)(2,1)S(1)} collective-permute-done((bf16[64,1152]{1,0:T(8,128)(2,1)S(1)}, bf16[64,1152]{1,0:T(8,128)(2,1)S(1)}, u32[]{:S(2)}, u32[]{:S(2)}) %collective-permute-start.18) | collective-permute-done | bytes 147488 | tf_op jit(solution)/shard_map/ppermute | solution.py:256
  56.9 1.4 %collective-permute-start.19 = (bf16[32,1152]{1,0:T(8,128)(2,1)S(1)}, bf16[32,1152]{1,0:T(8,128)(2,1)S(1)}, u32[]{:S(2)}, u32[]{:S(2)}) collective-permute-start(bf16[32,1152]{1,0:T(8,128)(2,1)S(1)} %get-tuple-element.59), channel_id=1, source_target_pairs={{0,24},{4,28},{8,16},{12,20},{16,8},{20,12},{24,0},{28,4},{1,25},{... | collective-permute-start | bytes 221192 | tf_op jit(solution)/shard_map/ppermute | solution.py:233
  58.2 3.1 %collective-permute-start.21 = (bf16[32,1152]{1,0:T(8,128)(2,1)S(1)}, bf16[32,1152]{1,0:T(8,128)(2,1)S(1)}, u32[]{:S(2)}, u32[]{:S(2)}) collective-permute-start(bf16[32,1152]{1,0:T(8,128)(2,1)S(1)} %get-tuple-element.61), channel_id=1, source_target_pairs={{0,8},{4,12},{8,0},{12,4},{16,24},{20,28},{24,16},{28,20},{1,9},{5... | collective-permute-start | bytes 221192 | tf_op jit(solution)/shard_map/ppermute | solution.py:233
  61.3 1.8 %collective-permute-done.19.refs_0_ = bf16[32,1152]{1,0:T(8,128)(2,1)S(1)} collective-permute-done((bf16[32,1152]{1,0:T(8,128)(2,1)S(1)}, bf16[32,1152]{1,0:T(8,128)(2,1)S(1)}, u32[]{:S(2)}, u32[]{:S(2)}) %collective-permute-start.19) | collective-permute-done | bytes 73760 | tf_op jit(solution)/shard_map/ppermute | solution.py:233
  63.2 1.5 %collective-permute-done.20.refs_1_ = bf16[32,1152]{1,0:T(8,128)(2,1)S(1)} collective-permute-done((bf16[32,1152]{1,0:T(8,128)(2,1)S(1)}, bf16[32,1152]{1,0:T(8,128)(2,1)S(1)}, u32[]{:S(2)}, u32[]{:S(2)}) %collective-permute-start.20) | collective-permute-done | bytes 73760 | tf_op jit(solution)/shard_map/ppermute | solution.py:233
  64.7 0.8 %shard_map.75 = bf16[8,16,1152]{2,1,0:T(8,128)(2,1)} custom-call(f32[6,1152]{1,0:T(8,128)S(1)} %copy-done.7, bf16[4,16,1152]{2,1,0:T(8,128)(2,1)S(1)} %get-tuple-element.45.kept_ref, bf16[4,16,1152]{2,1,0:T(8,128)(2,1)S(1)} %collective-permute-done.12.other_ref, bf16[32,1152]{1,0:T(8,128)(2,1)S(1)} %collective-permute-done.19.refs_0_, ...), custom_call_target="tpu_custom_call" | custom-call | flops 1 | bytes 1 | tf_op jit(solution)/shard_map/pallas_call | solution.py:220
  (40 shorter events, 3.6 us)
Async XLA Ops:
  0.0 3.0 %collective-permute-start = (bf16[1,128,1152]{2,1,0:T(8,128)(2,1)}, bf16[1,128,1152]{2,1,0:T(8,128)(2,1)S(1)}, u32[]{:S(2)}, u32[]{:S(2)}) collective-permute-start(bf16[1,128,1152]{2,1,0:T(8,128)(2,1)} %own_ref.1), channel_id=1, source_target_pairs={{0,1},{1,0},{2,3},{3,2},{4,5},{5,4},{6,7},{7,6},{8,9},{9,8},{10,11... | collective-permute-start | bytes 884744 | tf_op jit(solution)/shard_map/ppermute | solution.py:233
  0.5 10.4 %collective-permute-start.2 = (bf16[1,128,1152]{2,1,0:T(8,128)(2,1)}, bf16[1,128,1152]{2,1,0:T(8,128)(2,1)S(1)}, u32[]{:S(2)}, u32[]{:S(2)}) collective-permute-start(bf16[1,128,1152]{2,1,0:T(8,128)(2,1)} %own_ref.1), channel_id=1, source_target_pairs={{0,2},{1,3},{2,0},{3,1},{4,6},{5,7},{6,4},{7,5},{8,10},{9,11},{10,... | collective-permute-start | bytes 884744 | tf_op jit(solution)/shard_map/ppermute | solution.py:233
  3.0 1.0 %copy-start.5 = (bf16[1,128,1152]{2,1,0:T(8,128)(2,1)S(1)}, bf16[1,128,1152]{2,1,0:T(8,128)(2,1)}, u32[]{:S(2)}) copy-start(bf16[1,128,1152]{2,1,0:T(8,128)(2,1)} %own_ref.1) | copy-start | bytes 884740
  4.1 6.8 %collective-permute-start.1 = (bf16[64,1152]{1,0:T(8,128)(2,1)S(1)}, bf16[64,1152]{1,0:T(8,128)(2,1)S(1)}, u32[]{:S(2)}, u32[]{:S(2)}) collective-permute-start(bf16[64,1152]{1,0:T(8,128)(2,1)S(1)} %get-tuple-element.36), channel_id=1, source_target_pairs={{0,4},{4,0},{8,12},{12,8},{16,20},{20,16},{24,28},{28,24},{1,5},{5... | collective-permute-start | bytes 442376 | tf_op jit(solution)/shard_map/ppermute | solution.py:233
  5.8 1.6 %copy-start = (bf16[864,1152]{1,0:T(8,128)(2,1)S(1)}, bf16[864,1152]{1,0:T(8,128)(2,1)}, u32[]{:S(2)}) copy-start(bf16[864,1152]{1,0:T(8,128)(2,1)} %weight_ref.3) | copy-start | bytes 5971972
  7.4 0.8 %copy-start.6 = (f32[6,1152]{1,0:T(8,128)S(1)}, f32[6,1152]{1,0:T(8,128)}, u32[]{:S(2)}) copy-start(f32[6,1152]{1,0:T(8,128)} %mod_ref.7) | copy-start | bytes 82948
  8.2 4.4 %copy-start.4 = (bf16[288,1152]{1,0:T(8,128)(2,1)S(1)}, bf16[288,1152]{1,0:T(8,128)(2,1)}, u32[]{:S(2)}) copy-start(bf16[288,1152]{1,0:T(8,128)(2,1)} %refs_0_.4) | copy-start | bytes 1990660
  8.2 4.8 %copy-start.1 = (bf16[864,1152]{1,0:T(8,128)(2,1)S(1)}, bf16[864,1152]{1,0:T(8,128)(2,1)}, u32[]{:S(2)}) copy-start(bf16[864,1152]{1,0:T(8,128)(2,1)} %weight_ref.3) | copy-start | bytes 5971972
  9.3 9.2 %copy-start.3 = (bf16[288,1152]{1,0:T(8,128)(2,1)S(1)}, bf16[288,1152]{1,0:T(8,128)(2,1)}, u32[]{:S(2)}) copy-start(bf16[288,1152]{1,0:T(8,128)(2,1)} %refs_2_.5) | copy-start | bytes 1990660
  10.9 1.6 %collective-permute-start.3 = (bf16[1,128,1152]{2,1,0:T(8,128)(2,1)S(1)}, bf16[1,128,1152]{2,1,0:T(8,128)(2,1)S(1)}, u32[]{:S(2)}, u32[]{:S(2)}) collective-permute-start(bf16[1,128,1152]{2,1,0:T(8,128)(2,1)S(1)} %collective-permute-done.2.refs_0_), channel_id=1, source_target_pairs={{0,1},{1,0},{2,3},{3,2},{4,5},{5,4},{6,7},{7,6},{8,9},{9,8},{10,11... | collective-permute-start | bytes 884744 | tf_op jit(solution)/shard_map/ppermute | solution.py:233
  12.4 27.5 %collective-permute-start.13 = (bf16[864,1152]{1,0:T(8,128)(2,1)}, bf16[864,1152]{1,0:T(8,128)(2,1)S(1)}, u32[]{:S(2)}, u32[]{:S(2)}) collective-permute-start(bf16[864,1152]{1,0:T(8,128)(2,1)} %refs_0_.7), channel_id=1, source_target_pairs={{0,1},{1,0},{2,3},{3,2},{4,5},{5,4},{6,7},{7,6},{8,9},{9,8},{10,11... | collective-permute-start | bytes 5971976 | tf_op jit(solution)/shard_map/ppermute | solution.py:233
  12.6 5.2 %collective-permute-start.5 = (bf16[288,1152]{1,0:T(8,128)(2,1)S(1)}, bf16[288,1152]{1,0:T(8,128)(2,1)S(1)}, u32[]{:S(2)}, u32[]{:S(2)}) collective-permute-start(bf16[288,1152]{1,0:T(8,128)(2,1)S(1)} %copy-done.4), channel_id=1, source_target_pairs={{0,1},{1,0},{2,3},{3,2},{4,5},{5,4},{6,7},{7,6},{8,9},{9,8},{10,11... | collective-permute-start | bytes 1990664 | tf_op jit(solution)/shard_map/ppermute | solution.py:233
  16.3 11.9 %copy-start.7 = (f32[6,1152]{1,0:T(8,128)S(1)}, f32[6,1152]{1,0:T(8,128)}, u32[]{:S(2)}) copy-start(f32[6,1152]{1,0:T(8,128)} %mod_ref.7) | copy-start | bytes 82948
  16.3 1.4 %collective-permute-start.4 = (bf16[288,256]{1,0:T(8,128)(2,1)S(1)}, bf16[288,256]{1,0:T(8,128)(2,1)S(1)}, u32[]{:S(2)}, u32[]{:S(2)}) collective-permute-start(bf16[288,256]{1,0:T(8,128)(2,1)S(1)} %get-tuple-element.39), channel_id=1, source_target_pairs={{0,1},{1,0},{2,3},{3,2},{4,5},{5,4},{6,7},{7,6},{8,9},{9,8},{10,11... | collective-permute-start | bytes 442376 | tf_op jit(solution)/shard_map/ppermute | solution.py:233
  18.5 21.5 %copy-start.2 = (bf16[864,1152]{1,0:T(8,128)(2,1)S(1)}, bf16[864,1152]{1,0:T(8,128)(2,1)}, u32[]{:S(2)}) copy-start(bf16[864,1152]{1,0:T(8,128)(2,1)} %refs_0_.7) | copy-start | bytes 5971972
  18.5 21.4 %collective-permute-start.14 = (bf16[288,1152]{1,0:T(8,128)(2,1)S(1)}, bf16[288,1152]{1,0:T(8,128)(2,1)S(1)}, u32[]{:S(2)}, u32[]{:S(2)}) collective-permute-start(bf16[288,1152]{1,0:T(8,128)(2,1)S(1)} %copy-done.3), channel_id=1, source_target_pairs={{0,1},{1,0},{2,3},{3,2},{4,5},{5,4},{6,7},{7,6},{8,9},{9,8},{10,11... | collective-permute-start | bytes 1990664 | tf_op jit(solution)/shard_map/ppermute | solution.py:233
  18.7 9.5 %collective-permute-start.6 = (bf16[64,1152]{1,0:T(8,128)(2,1)S(1)}, bf16[64,1152]{1,0:T(8,128)(2,1)S(1)}, u32[]{:S(2)}, u32[]{:S(2)}) collective-permute-start(bf16[64,1152]{1,0:T(8,128)(2,1)S(1)} %get-tuple-element.42), channel_id=1, source_target_pairs={{0,2},{1,3},{2,0},{3,1},{4,6},{5,7},{6,4},{7,5},{8,10},{9,11},{10,... | collective-permute-start | bytes 442376 | tf_op jit(solution)/shard_map/ppermute | solution.py:233
  20.5 7.8 %collective-permute-start.8 = (bf16[64,1152]{1,0:T(8,128)(2,1)S(1)}, bf16[64,1152]{1,0:T(8,128)(2,1)S(1)}, u32[]{:S(2)}, u32[]{:S(2)}) collective-permute-start(bf16[64,1152]{1,0:T(8,128)(2,1)S(1)} %get-tuple-element.44), channel_id=1, source_target_pairs={{0,6},{1,7},{2,4},{3,5},{4,2},{5,3},{6,0},{7,1},{8,14},{9,15},{10,... | collective-permute-start | bytes 442376 | tf_op jit(solution)/shard_map/ppermute | solution.py:256
  21.9 5.9 %collective-permute-start.7 = (bf16[64,576]{1,0:T(8,128)(2,1)S(1)}, bf16[64,576]{1,0:T(8,128)(2,1)S(1)}, u32[]{:S(2)}, u32[]{:S(2)}) collective-permute-start(bf16[64,576]{1,0:T(8,128)(2,1)S(1)} %get-tuple-element.43), channel_id=1, source_target_pairs={{0,4},{4,0},{8,12},{12,8},{16,20},{20,16},{24,28},{28,24},{1,5},{5... | collective-permute-start | bytes 221192 | tf_op jit(solution)/shard_map/ppermute | solution.py:233
  28.6 7.0 %collective-permute-start.9 = (bf16[32,1152]{1,0:T(8,128)(2,1)S(1)}, bf16[32,1152]{1,0:T(8,128)(2,1)S(1)}, u32[]{:S(2)}, u32[]{:S(2)}) collective-permute-start(bf16[32,1152]{1,0:T(8,128)(2,1)S(1)} %get-tuple-element.47), channel_id=1, source_target_pairs={{0,24},{4,28},{8,16},{12,20},{16,8},{20,12},{24,0},{28,4},{1,25},{... | collective-permute-start | bytes 221192 | tf_op jit(solution)/shard_map/ppermute | solution.py:233
  32.5 5.8 %collective-permute-start.10 = (bf16[32,1152]{1,0:T(8,128)(2,1)S(1)}, bf16[32,1152]{1,0:T(8,128)(2,1)S(1)}, u32[]{:S(2)}, u32[]{:S(2)}) collective-permute-start(bf16[32,1152]{1,0:T(8,128)(2,1)S(1)} %get-tuple-element.48), channel_id=1, source_target_pairs={{0,16},{4,20},{8,24},{12,28},{16,0},{20,4},{24,8},{28,12},{1,17},{... | collective-permute-start | bytes 221192 | tf_op jit(solution)/shard_map/ppermute | solution.py:233
  32.5 5.8 %collective-permute-start.11 = (bf16[32,1152]{1,0:T(8,128)(2,1)S(1)}, bf16[32,1152]{1,0:T(8,128)(2,1)S(1)}, u32[]{:S(2)}, u32[]{:S(2)}) collective-permute-start(bf16[32,1152]{1,0:T(8,128)(2,1)S(1)} %get-tuple-element.49), channel_id=1, source_target_pairs={{0,8},{4,12},{8,0},{12,4},{16,24},{20,28},{24,16},{28,20},{1,9},{5... | collective-permute-start | bytes 221192 | tf_op jit(solution)/shard_map/ppermute | solution.py:233
  38.3 8.4 %collective-permute-start.15 = (bf16[128,1152]{1,0:T(8,128)(2,1)S(1)}, bf16[128,1152]{1,0:T(8,128)(2,1)S(1)}, u32[]{:S(2)}, u32[]{:S(2)}) collective-permute-start(bf16[128,1152]{1,0:T(8,128)(2,1)S(1)} %shard_map.70.refs_4_), channel_id=1, source_target_pairs={{0,2},{1,3},{2,0},{3,1},{4,6},{5,7},{6,4},{7,5},{8,10},{9,11},{10,... | collective-permute-start | bytes 884744 | tf_op jit(solution)/shard_map/ppermute | solution.py:233
  41.9 4.5 %collective-permute-start.16 = (bf16[64,576]{1,0:T(8,128)(2,1)S(1)}, bf16[64,576]{1,0:T(8,128)(2,1)S(1)}, u32[]{:S(2)}, u32[]{:S(2)}) collective-permute-start(bf16[64,576]{1,0:T(8,128)(2,1)S(1)} %get-tuple-element.55), channel_id=1, source_target_pairs={{0,4},{4,0},{8,12},{12,8},{16,20},{20,16},{24,28},{28,24},{1,5},{5... | collective-permute-start | bytes 221192 | tf_op jit(solution)/shard_map/ppermute | solution.py:233
  48.7 6.9 %collective-permute-start.17 = (bf16[64,1152]{1,0:T(8,128)(2,1)S(1)}, bf16[64,1152]{1,0:T(8,128)(2,1)S(1)}, u32[]{:S(2)}, u32[]{:S(2)}) collective-permute-start(bf16[64,1152]{1,0:T(8,128)(2,1)S(1)} %get-tuple-element.57), channel_id=1, source_target_pairs={{0,2},{1,3},{2,0},{3,1},{4,6},{5,7},{6,4},{7,5},{8,10},{9,11},{10,... | collective-permute-start | bytes 442376 | tf_op jit(solution)/shard_map/ppermute | solution.py:233
  50.3 6.5 %collective-permute-start.18 = (bf16[64,1152]{1,0:T(8,128)(2,1)S(1)}, bf16[64,1152]{1,0:T(8,128)(2,1)S(1)}, u32[]{:S(2)}, u32[]{:S(2)}) collective-permute-start(bf16[64,1152]{1,0:T(8,128)(2,1)S(1)} %get-tuple-element.58), channel_id=1, source_target_pairs={{0,6},{1,7},{2,4},{3,5},{4,2},{5,3},{6,0},{7,1},{8,14},{9,15},{10,... | collective-permute-start | bytes 442376 | tf_op jit(solution)/shard_map/ppermute | solution.py:256
  51.7 9.6 %collective-permute-start.12 = (bf16[4,16,1152]{2,1,0:T(8,128)(2,1)S(1)}, bf16[4,16,1152]{2,1,0:T(8,128)(2,1)S(1)}, u32[]{:S(2)}, u32[]{:S(2)}) collective-permute-start(bf16[4,16,1152]{2,1,0:T(8,128)(2,1)S(1)} %get-tuple-element.51), channel_id=1, source_target_pairs={{0,4},{4,0},{8,12},{12,8},{16,20},{20,16},{24,28},{28,24},{1,5},{5... | collective-permute-start | bytes 442376 | tf_op jit(solution)/shard_map/ppermute | solution.py:233
  56.9 6.3 %collective-permute-start.19 = (bf16[32,1152]{1,0:T(8,128)(2,1)S(1)}, bf16[32,1152]{1,0:T(8,128)(2,1)S(1)}, u32[]{:S(2)}, u32[]{:S(2)}) collective-permute-start(bf16[32,1152]{1,0:T(8,128)(2,1)S(1)} %get-tuple-element.59), channel_id=1, source_target_pairs={{0,24},{4,28},{8,16},{12,20},{16,8},{20,12},{24,0},{28,4},{1,25},{... | collective-permute-start | bytes 221192 | tf_op jit(solution)/shard_map/ppermute | solution.py:233
  58.2 6.4 %collective-permute-start.20 = (bf16[32,1152]{1,0:T(8,128)(2,1)S(1)}, bf16[32,1152]{1,0:T(8,128)(2,1)S(1)}, u32[]{:S(2)}, u32[]{:S(2)}) collective-permute-start(bf16[32,1152]{1,0:T(8,128)(2,1)S(1)} %get-tuple-element.60), channel_id=1, source_target_pairs={{0,16},{4,20},{8,24},{12,28},{16,0},{20,4},{24,8},{28,12},{1,17},{... | collective-permute-start | bytes 221192 | tf_op jit(solution)/shard_map/ppermute | solution.py:233
  58.2 6.4 %collective-permute-start.21 = (bf16[32,1152]{1,0:T(8,128)(2,1)S(1)}, bf16[32,1152]{1,0:T(8,128)(2,1)S(1)}, u32[]{:S(2)}, u32[]{:S(2)}) collective-permute-start(bf16[32,1152]{1,0:T(8,128)(2,1)S(1)} %get-tuple-element.61), channel_id=1, source_target_pairs={{0,8},{4,12},{8,0},{12,4},{16,24},{20,28},{24,16},{28,20},{1,9},{5... | collective-permute-start | bytes 221192 | tf_op jit(solution)/shard_map/ppermute | solution.py:233

commit v17 on v16

--- a/solution.py
+++ b/solution.py
@@ -52,32 +52,39 @@
     project(mod_ref, weight_ref, (own_ref, sister_ref), proj_ref)
 
 
-def spatial_kernel(count, mod_ref, weight_ref, near_ref, *refs):
-    token_refs, (kept_ref, sent_ref, far_ref, heads_ref) = refs[: count - 2], refs[count - 2 :]
-    block = token_refs[0].shape[1]
-    heads = weight_ref.shape[0] // (3 * HD)
-    project(mod_ref, weight_ref, token_refs, far_ref)
+def attend_patches(near_ref, far_ref, query_ref, heads_ref, kept_ref, sent_ref):
+    columns, block = query_ref.shape[1], near_ref.shape[1] // 2
 
     def whole(start):
         return jnp.concatenate([ref[start : start + HD, :] for ref in (near_ref, far_ref)], axis=1)
 
     def score(head, at):
         base = head * 3 * HD
-        source, start = (near_ref, 0) if at == 0 else (far_ref, (at - 2) * block)
-        query = source[base : base + HD, start : start + 2 * block].astype(BF16)
+        query = query_ref[base : base + HD, at : at + 2 * block].astype(BF16)
         return dot(whole(base + HD).astype(BF16).T, query)
 
-    steps = [(head, at) for head in range(heads) for at in range(0, count, 2)]
+    heads = range(heads_ref.shape[0] // HD)
+    steps = [(head, at) for head in heads for at in range(0, columns, 2 * block)]
     scores = score(*steps[0])
     for (head, at), later in zip(steps, [*steps[1:], None]):
         coming = score(*later) if later else None
-        rows, cols = slice(head * HD, (head + 1) * HD), slice(at * block, (at + 2) * block)
+        rows, cols = slice(head * HD, (head + 1) * HD), slice(at, at + 2 * block)
         heads_ref[rows, cols] = mix(whole(head * 3 * HD + 2 * HD), soften(scores))
         scores = coming
-    for at in range(count):
+    for at in range(columns // block):
         out_ref = (kept_ref, sent_ref)[at % 2]
         cols = slice(at // 2 * block, (at // 2 + 1) * block)
         out_ref[:, cols] = heads_ref[:, at * block : (at + 1) * block].astype(BF16)
+
+
+def far_queries_kernel(mod_ref, weight_ref, near_ref, *refs):
+    token_refs, (far_ref, kept_ref, sent_ref, heads_ref) = refs[:-4], refs[-4:]
+    project(mod_ref, weight_ref, token_refs, far_ref)
+    attend_patches(near_ref, far_ref, far_ref, heads_ref, kept_ref, sent_ref)
+
+
+def near_queries_kernel(near_ref, far_ref, kept_ref, sent_ref, heads_ref):
+    attend_patches(near_ref, far_ref, near_ref, heads_ref, kept_ref, sent_ref)
 
 
 def halves(value, size):
@@ -104,23 +111,31 @@
     return jnp.concatenate([ref[...] for ref in refs], axis=0)
 
 
-def partial_kernel(period, *refs):
+def far_partial_kernel(period, *refs):
     head_refs, weights, out_refs = refs[:2], joined(refs[2:4]), refs[4:]
     block = 2 * out_refs[0].shape[0]
     for at in range(len(out_refs) // 2):
         cols = slice(at * block, (at + 1) * block)
         heads = jnp.concatenate([ref[:, cols] for ref in head_refs], axis=0).T
-        if at == 0:
-            kept, sent = (half.astype(BF16) for half in of_this_half(heads, period))
-            parts = dot(kept, weights), sent
-        else:
-            parts = of_this_half(dot(heads, weights), period)
+        parts = of_this_half(dot(heads, weights), period)
         for ref, part in zip(out_refs[2 * at : 2 * at + 2], parts):
             ref[...] = part.astype(ref.dtype)
 
 
+def near_partial_kernel(period, *refs):
+    head_refs, weights, (kept_ref, sent_ref) = refs[:2], joined(refs[2:4]), refs[4:]
+    kept, sent = of_this_half(joined(head_refs).T, period)
+    kept_ref[...] = dot(kept.astype(BF16), weights)
+    sent_ref[...] = sent.astype(BF16)
+
+
 def paired_kernel(head_ref, *refs):
     refs[-1][...] = dot(head_ref[...], joined(refs[:-1]))
+
+
+def far_sum_kernel(count, *refs):
+    for at, ref in enumerate(refs[2 * count :]):
+        ref[...] = sum(part[...].astype(F32) for part in refs[at * count : (at + 1) * count])
 
 
 def total_updates(groups, refs):
@@ -130,9 +145,9 @@
     ]
 
 
-def middle_kernel(pieces, groups, mod_ref, own_ref, paired_ref, *refs):
-    kept_ref, sent_ref, *piece_refs, scratch = refs[2 * groups :]
-    updates = total_updates(groups, refs)
+def middle_kernel(pieces, mod_ref, own_ref, paired_ref, *refs):
+    kept_ref, sent_ref, *piece_refs, scratch = refs[4:]
+    updates = total_updates(2, refs)
     _, period, width = kept_ref.shape
     inputs = (own_ref[...], paired_ref[...])
     for at, (tokens, middle_ref) in enumerate(zip(inputs, (kept_ref, sent_ref))):
@@ -216,7 +231,7 @@
             )
 
 
-def call(body, operands, outs, scratch=(), limit=24):
+def call(body, operands, outs, scratch=(), limit=24, flops=1):
     return pl.pallas_call(
         body,
         out_shape=outs,
@@ -224,7 +239,7 @@
         out_specs=[pl.BlockSpec(memory_space=pltpu.VMEM)] * len(outs),
         scratch_shapes=list(scratch),
         compiler_params=pltpu.CompilerParams(vmem_limit_bytes=limit * MIB),
-        cost_estimate=pl.CostEstimate(flops=1, bytes_accessed=1, transcendentals=0),
+        cost_estimate=pl.CostEstimate(flops=flops, bytes_accessed=1, transcendentals=0),
     )(*operands)
 
 
@@ -302,21 +317,40 @@
     far = both_cores([after(block, near, paired) for block in far])
     temporal_pair = with_sister(temporal_qkv, *far)
 
+    columns = (groups - 1) * rows
+    far_proj, kept, sent = call(
+        far_queries_kernel,
+        (modulation, spatial_qkv, near, *far),
+        [shape((3 * shard, 2 * columns), F32)] + [shape((shard, columns), BF16)] * 2,
+        [pltpu.VMEM((shard, 2 * columns), F32)],
+    )
+    far_parts = call(
+        functools.partial(far_partial_kernel, period),
+        (kept, swap(sent, "patch", 1), *out_pair),
+        far_shapes,
+    )
     kept, sent = call(
-        functools.partial(spatial_kernel, count),
-        (modulation, spatial_qkv, near, *far),
-        [shape((shard, groups * rows), BF16)] * 2,
-        [pltpu.VMEM((3 * shard, (count - 2) * rows), F32), pltpu.VMEM((shard, count * rows), F32)],
-    )
-    parts = call(
-        functools.partial(partial_kernel, period),
-        (kept, swap(sent, "patch", 1), *out_pair),
-        own_shapes + far_shapes,
-    )
-    late_pair = with_sister(temporal_out, parts[0])
-    updates = return_updates((parts[0], project_paired(parts[1], out_pair)), parts[2:])
+        near_queries_kernel,
+        (after(near, far_parts[0]), far_proj),
+        [shape((shard, rows), BF16)] * 2,
+        [pltpu.VMEM((shard, 2 * rows), F32)],
+        flops=1,
+    )
+    received = swap(sent, "patch", 1)
+    own_parts = call(
+        functools.partial(near_partial_kernel, period), (kept, received, *out_pair), own_shapes
+    )
+    late_pair = with_sister(temporal_out, received)
+    updates = return_updates((own_parts[0], project_paired(own_parts[1], out_pair)), far_parts)
+    sums = call(
+        functools.partial(far_sum_kernel, groups - 1),
+        (*updates[1:groups], *updates[groups + 1 :]),
+        [halves_shape(F32)] * 2,
+        flops=4_000_000_000,
+    )
+    updates = [updates[0], sums[0], updates[groups], sums[1]]
     middle, middle_sent, *parts = call(
-        functools.partial(middle_kernel, pieces, groups),
+        functools.partial(middle_kernel, pieces),
         (modulation, own_tokens, paired, *updates),
         [shape((pieces, period, width), BF16)] * 2 + piece_shapes,
         [pltpu.VMEM((pieces, 2 * period, width), BF16)],

time: 65.8 us -> 67 us (1.018)
  waiting for transfers between devices: 26 us -> 28.1 us
  starting transfers between devices: 24.9 us -> 23.5 us
    ppermute x20 -> x21, starting transfers between devices: 22 us -> 19.5 us  [swap(): return lax.ppermute(value, axis, [(at, at ^ offset) for at in range(size)])]
    ppermute x20 -> x21, waiting for transfers between devices: 24.8 us -> 26.4 us  [swap(): return lax.ppermute(value, axis, [(at, at ^ offset) for at in range(size)])]
    ppermute x2, starting transfers between devices: 2.85 us -> 4.01 us  [swap_diagonal(): return lax.ppermute(value, ('frame', 'patch'), pairs)]
    pallas_call x12 -> x15, Pallas kernels: 11.1 us -> 11.7 us  [call(): pl.pallas_call(body, out_shape=outs, in_specs=[pl.BlockSpec(memory_space=...]
  transfers between devices with their start and end apart: 22 -> 23, of which waited for: 11 -> 15; matrix products, arithmetic and copies ran while one was open for 0% -> 0% of each run, Pallas kernels for 13% -> 13%
where the time goes in v17:
time: 67 us; the launch traced here: 66.8 us
  waiting for transfers between devices  28.1 us (42%)
  starting transfers between devices  23.5 us (35%)
  Pallas kernels  11.7 us (17%)
  local copies, waits for them, and re-layouts  3.34 us (5%)
    ppermute x21, waiting for transfers between devices, swap(): return lax.ppermute(value, axis, [(at, at ^ offset) for at in range(size)])  26.4 us
    ppermute x21, starting transfers between devices, swap(): return lax.ppermute(value, axis, [(at, at ^ offset) for at in range(size)])  19.5 us
    pallas_call x15, Pallas kernels, call(): pl.pallas_call(body, out_shape=outs, in_specs=[pl.BlockSpec(memory_space=...  11.7 us
    ppermute x2, starting transfers between devices, swap_diagonal(): return lax.ppermute(value, ('frame', 'patch'), pairs)  4.01 us
    unnamed x16, local copies, waits for them, and re-layouts  3.34 us
    ppermute x2, waiting for transfers between devices, swap_diagonal(): return lax.ppermute(value, ('frame', 'patch'), pairs)  1.67 us
  transfers between devices with their start and end apart: 23, of which 15 were waited for; matrix products, arithmetic and copies ran while one was open for 0% of the time, Pallas kernels for 13%

profile of v17, /device:TPU:0, one launch (start us, length us, event | category | flops | bytes accessed | tf_op | source)
XLA Modules:
  0.0 66.8 jit_solution(16128061463308790662)
XLA Ops:
  0.5 2.5 %collective-permute-start.2 = (bf16[1,128,1152]{2,1,0:T(8,128)(2,1)}, bf16[1,128,1152]{2,1,0:T(8,128)(2,1)S(1)}, u32[]{:S(2)}, u32[]{:S(2)}) collective-permute-start(bf16[1,128,1152]{2,1,0:T(8,128)(2,1)} %own_ref.1), channel_id=1, source_target_pairs={{0,2},{1,3},{2,0},{3,1},{4,6},{5,7},{6,4},{7,5},{8,10},{9,11},{10,... | collective-permute-start | bytes 884744 | tf_op jit(solution)/shard_map/ppermute | solution.py:248
  3.0 1.0 %copy-done.5 = bf16[1,128,1152]{2,1,0:T(8,128)(2,1)S(1)} copy-done((bf16[1,128,1152]{2,1,0:T(8,128)(2,1)S(1)}, bf16[1,128,1152]{2,1,0:T(8,128)(2,1)}, u32[]{:S(2)}) %copy-start.5) | copy-done | bytes 294936
  4.1 1.8 %collective-permute-start.1 = (bf16[64,1152]{1,0:T(8,128)(2,1)S(1)}, bf16[64,1152]{1,0:T(8,128)(2,1)S(1)}, u32[]{:S(2)}, u32[]{:S(2)}) collective-permute-start(bf16[64,1152]{1,0:T(8,128)(2,1)S(1)} %get-tuple-element.42), channel_id=1, source_target_pairs={{0,4},{4,0},{8,12},{12,8},{16,20},{20,16},{24,28},{28,24},{1,5},{5... | collective-permute-start | bytes 442376 | tf_op jit(solution)/shard_map/ppermute | solution.py:248
  5.9 1.6 %copy-done = bf16[864,1152]{1,0:T(8,128)(2,1)S(1)} copy-done((bf16[864,1152]{1,0:T(8,128)(2,1)S(1)}, bf16[864,1152]{1,0:T(8,128)(2,1)}, u32[]{:S(2)}) %copy-start) | copy-done | bytes 1990680
  7.4 0.8 %copy-done.6 = f32[6,1152]{1,0:T(8,128)S(1)} copy-done((f32[6,1152]{1,0:T(8,128)S(1)}, f32[6,1152]{1,0:T(8,128)}, u32[]{:S(2)}) %copy-start.6) | copy-done | bytes 27672
  8.2 1.1 %shard_map.65.near_ref = f32[864,256]{1,0:T(8,128)S(1)} custom-call(f32[6,1152]{1,0:T(8,128)S(1)} %copy-done.6, bf16[864,1152]{1,0:T(8,128)(2,1)S(1)} %copy-done, bf16[1,128,1152]{2,1,0:T(8,128)(2,1)S(1)} %copy-done.5, bf16[1,128,1152]{2,1,0:T(8,128)(2,1)S(1)} %collective-permute-done.sister_ref), custom_call_target="tpu_custom_call" | custom-call | flops 1 | bytes 1 | tf_op jit(solution)/shard_map/pallas_call | solution.py:235
  9.3 1.6 %collective-permute-done.2.refs_0_ = bf16[1,128,1152]{2,1,0:T(8,128)(2,1)S(1)} collective-permute-done((bf16[1,128,1152]{2,1,0:T(8,128)(2,1)}, bf16[1,128,1152]{2,1,0:T(8,128)(2,1)S(1)}, u32[]{:S(2)}, u32[]{:S(2)}) %collective-permute-start.2) | collective-permute-done | bytes 294944 | tf_op jit(solution)/shard_map/ppermute | solution.py:248
  10.9 1.6 %collective-permute-done.3.refs_1_ = bf16[1,128,1152]{2,1,0:T(8,128)(2,1)S(1)} collective-permute-done((bf16[1,128,1152]{2,1,0:T(8,128)(2,1)S(1)}, bf16[1,128,1152]{2,1,0:T(8,128)(2,1)S(1)}, u32[]{:S(2)}, u32[]{:S(2)}) %collective-permute-start.3) | collective-permute-done | bytes 294944 | tf_op jit(solution)/shard_map/ppermute | solution.py:248
  13.0 2.6 %shard_map.66 = (f32[864,256]{1,0:T(8,128)S(1)}, bf16[288,128]{1,0:T(8,128)(2,1)S(1)}, bf16[288,128]{1,0:T(8,128)(2,1)S(1)}) custom-call(f32[6,1152]{1,0:T(8,128)S(1)} %copy-done.6, bf16[864,1152]{1,0:T(8,128)(2,1)S(1)} %copy-done.1, f32[864,256]{1,0:T(8,128)S(1)} %shard_map.65.near_ref, bf16[1,128,1152]{2,1,0:T(8,128)(2,1)S(1)} %collective-permute-done.2.refs_0_, ...), custom_call_target="tpu_custom_call" | custom-call | flops 1 | bytes 1 | tf_op jit(solution)/shard_map/pallas_call | solution.py:235
  15.7 1.5 %collective-permute-done.4.refs_1_ = bf16[288,128]{1,0:T(8,128)(2,1)S(1)} collective-permute-done((bf16[288,128]{1,0:T(8,128)(2,1)S(1)}, bf16[288,128]{1,0:T(8,128)(2,1)S(1)}, u32[]{:S(2)}, u32[]{:S(2)}) %collective-permute-start.4) | collective-permute-done | bytes 73760 | tf_op jit(solution)/shard_map/ppermute | solution.py:248
  17.7 2.8 %collective-permute-start.8 = (bf16[64,1152]{1,0:T(8,128)(2,1)S(1)}, bf16[64,1152]{1,0:T(8,128)(2,1)S(1)}, u32[]{:S(2)}, u32[]{:S(2)}) collective-permute-start(bf16[64,1152]{1,0:T(8,128)(2,1)S(1)} %get-tuple-element.53), channel_id=1, source_target_pairs={{0,6},{1,7},{2,4},{3,5},{4,2},{5,3},{6,0},{7,1},{8,14},{9,15},{10,... | collective-permute-start | bytes 442376 | tf_op jit(solution)/shard_map/ppermute | solution.py:271
  21.0 1.2 %shard_map.68 = (bf16[288,128]{1,0:T(8,128)(2,1)S(1)}, bf16[288,128]{1,0:T(8,128)(2,1)S(1)}) custom-call(f32[864,256]{1,0:T(8,128)S(1)} %shard_map.65.near_ref, f32[864,256]{1,0:T(8,128)S(1)} %get-tuple-element.49.far_ref), custom_call_target="tpu_custom_call" | custom-call | flops 1 | bytes 1 | tf_op jit(solution)/shard_map/pallas_call | solution.py:235
  22.2 1.3 %collective-permute-done.6.refs_1_ = bf16[288,128]{1,0:T(8,128)(2,1)S(1)} collective-permute-done((bf16[288,128]{1,0:T(8,128)(2,1)S(1)}, bf16[288,128]{1,0:T(8,128)(2,1)S(1)}, u32[]{:S(2)}, u32[]{:S(2)}) %collective-permute-start.6) | collective-permute-done | bytes 73760 | tf_op jit(solution)/shard_map/ppermute | solution.py:248
  25.0 3.1 %collective-permute-done.7.refs_0_ = bf16[64,1152]{1,0:T(8,128)(2,1)S(1)} collective-permute-done((bf16[64,1152]{1,0:T(8,128)(2,1)S(1)}, bf16[64,1152]{1,0:T(8,128)(2,1)S(1)}, u32[]{:S(2)}, u32[]{:S(2)}) %collective-permute-start.7) | collective-permute-done | bytes 147488 | tf_op jit(solution)/shard_map/ppermute | solution.py:248
  29.3 3.7 %collective-permute-start.10 = (bf16[32,1152]{1,0:T(8,128)(2,1)S(1)}, bf16[32,1152]{1,0:T(8,128)(2,1)S(1)}, u32[]{:S(2)}, u32[]{:S(2)}) collective-permute-start(bf16[32,1152]{1,0:T(8,128)(2,1)S(1)} %get-tuple-element.59), channel_id=1, source_target_pairs={{0,24},{4,28},{8,16},{12,20},{16,8},{20,12},{24,0},{28,4},{1,25},{... | collective-permute-start | bytes 221192 | tf_op jit(solution)/shard_map/ppermute | solution.py:248
  32.9 0.8 %collective-permute-start.12 = (bf16[32,1152]{1,0:T(8,128)(2,1)S(1)}, bf16[32,1152]{1,0:T(8,128)(2,1)S(1)}, u32[]{:S(2)}, u32[]{:S(2)}) collective-permute-start(bf16[32,1152]{1,0:T(8,128)(2,1)S(1)} %get-tuple-element.61), channel_id=1, source_target_pairs={{0,8},{4,12},{8,0},{12,4},{16,24},{20,28},{24,16},{28,20},{1,9},{5... | collective-permute-start | bytes 221192 | tf_op jit(solution)/shard_map/ppermute | solution.py:248
  33.7 2.3 %collective-permute-done.10.refs_0_ = bf16[32,1152]{1,0:T(8,128)(2,1)S(1)} collective-permute-done((bf16[32,1152]{1,0:T(8,128)(2,1)S(1)}, bf16[32,1152]{1,0:T(8,128)(2,1)S(1)}, u32[]{:S(2)}, u32[]{:S(2)}) %collective-permute-start.10) | collective-permute-done | bytes 73760 | tf_op jit(solution)/shard_map/ppermute | solution.py:248
  36.0 3.1 %collective-permute-done.11.refs_1_ = bf16[32,1152]{1,0:T(8,128)(2,1)S(1)} collective-permute-done((bf16[32,1152]{1,0:T(8,128)(2,1)S(1)}, bf16[32,1152]{1,0:T(8,128)(2,1)S(1)}, u32[]{:S(2)}, u32[]{:S(2)}) %collective-permute-start.11) | collective-permute-done | bytes 73760 | tf_op jit(solution)/shard_map/ppermute | solution.py:248
  39.2 1.6 %collective-permute-start.16 = (bf16[128,1152]{1,0:T(8,128)(2,1)S(1)}, bf16[128,1152]{1,0:T(8,128)(2,1)S(1)}, u32[]{:S(2)}, u32[]{:S(2)}) collective-permute-start(bf16[128,1152]{1,0:T(8,128)(2,1)S(1)} %shard_map.73.refs_4_), channel_id=1, source_target_pairs={{0,2},{1,3},{2,0},{3,1},{4,6},{5,7},{6,4},{7,5},{8,10},{9,11},{10,... | collective-permute-start | bytes 884744 | tf_op jit(solution)/shard_map/ppermute | solution.py:248
  40.8 1.9 %shard_map.74 = (f32[64,1152]{1,0:T(8,128)S(1)}, bf16[64,576]{1,0:T(8,128)(2,1)S(1)}) custom-call(bf16[864,1152]{1,0:T(8,128)(2,1)S(1)} %copy-done.2, bf16[864,1152]{1,0:T(8,128)(2,1)S(1)} %collective-permute-done.14.refs_1_, bf16[288,1152]{1,0:T(8,128)(2,1)S(1)} %copy-done.4, bf16[288,1152]{1,0:T(8,128)(2,1)S(1)} %collective-permute-done.15.refs_3_.refs_1_, ...), custom_call_target="tpu_custom_call" | custom-call | flops 1 | bytes 1 | tf_op jit(solution)/shard_map/pallas_call | solution.py:235
  43.0 4.2 %collective-permute-done.17.head_ref = bf16[64,576]{1,0:T(8,128)(2,1)S(1)} collective-permute-done((bf16[64,576]{1,0:T(8,128)(2,1)S(1)}, bf16[64,576]{1,0:T(8,128)(2,1)S(1)}, u32[]{:S(2)}, u32[]{:S(2)}) %collective-permute-start.17) | collective-permute-done | bytes 73760 | tf_op jit(solution)/shard_map/ppermute | solution.py:248
  47.8 2.0 %shard_map.76 = (bf16[64,1152]{1,0:T(8,128)(2,1)S(1)}, bf16[64,1152]{1,0:T(8,128)(2,1)S(1)}) custom-call(bf16[864,1152]{1,0:T(8,128)(2,1)S(1)} %copy-done.2, bf16[864,1152]{1,0:T(8,128)(2,1)S(1)} %collective-permute-done.14.refs_1_, bf16[288,1152]{1,0:T(8,128)(2,1)S(1)} %copy-done.4, bf16[288,1152]{1,0:T(8,128)(2,1)S(1)} %collective-permute-done.15.refs_3_.refs_1_, ...), custom_call_target="tpu_custom_call" | custom-call | flops 1 | bytes 1 | tf_op jit(solution)/shard_map/pallas_call | solution.py:235
  49.8 1.6 %collective-permute-start.18 = (bf16[64,1152]{1,0:T(8,128)(2,1)S(1)}, bf16[64,1152]{1,0:T(8,128)(2,1)S(1)}, u32[]{:S(2)}, u32[]{:S(2)}) collective-permute-start(bf16[64,1152]{1,0:T(8,128)(2,1)S(1)} %get-tuple-element.69), channel_id=1, source_target_pairs={{0,2},{1,3},{2,0},{3,1},{4,6},{5,7},{6,4},{7,5},{8,10},{9,11},{10,... | collective-permute-start | bytes 442376 | tf_op jit(solution)/shard_map/ppermute | solution.py:248
  51.4 1.3 %collective-permute-start.19 = (bf16[64,1152]{1,0:T(8,128)(2,1)S(1)}, bf16[64,1152]{1,0:T(8,128)(2,1)S(1)}, u32[]{:S(2)}, u32[]{:S(2)}) collective-permute-start(bf16[64,1152]{1,0:T(8,128)(2,1)S(1)} %get-tuple-element.70), channel_id=1, source_target_pairs={{0,6},{1,7},{2,4},{3,5},{4,2},{5,3},{6,0},{7,1},{8,14},{9,15},{10,... | collective-permute-start | bytes 442376 | tf_op jit(solution)/shard_map/ppermute | solution.py:271
  52.6 0.7 %collective-permute-start.13 = (bf16[4,16,1152]{2,1,0:T(8,128)(2,1)S(1)}, bf16[4,16,1152]{2,1,0:T(8,128)(2,1)S(1)}, u32[]{:S(2)}, u32[]{:S(2)}) collective-permute-start(bf16[4,16,1152]{2,1,0:T(8,128)(2,1)S(1)} %get-tuple-element.63), channel_id=1, source_target_pairs={{0,4},{4,0},{8,12},{12,8},{16,20},{20,16},{24,28},{28,24},{1,5},{5... | collective-permute-start | bytes 442376 | tf_op jit(solution)/shard_map/ppermute | solution.py:248
  53.3 3.7 %collective-permute-done.18.refs_1_ = bf16[64,1152]{1,0:T(8,128)(2,1)S(1)} collective-permute-done((bf16[64,1152]{1,0:T(8,128)(2,1)S(1)}, bf16[64,1152]{1,0:T(8,128)(2,1)S(1)}, u32[]{:S(2)}, u32[]{:S(2)}) %collective-permute-start.18) | collective-permute-done | bytes 147488 | tf_op jit(solution)/shard_map/ppermute | solution.py:248
  57.1 1.0 %collective-permute-done.19.refs_3_ = bf16[64,1152]{1,0:T(8,128)(2,1)S(1)} collective-permute-done((bf16[64,1152]{1,0:T(8,128)(2,1)S(1)}, bf16[64,1152]{1,0:T(8,128)(2,1)S(1)}, u32[]{:S(2)}, u32[]{:S(2)}) %collective-permute-start.19) | collective-permute-done | bytes 147488 | tf_op jit(solution)/shard_map/ppermute | solution.py:271
  58.1 1.1 %collective-permute-start.20 = (bf16[32,1152]{1,0:T(8,128)(2,1)S(1)}, bf16[32,1152]{1,0:T(8,128)(2,1)S(1)}, u32[]{:S(2)}, u32[]{:S(2)}) collective-permute-start(bf16[32,1152]{1,0:T(8,128)(2,1)S(1)} %get-tuple-element.71), channel_id=1, source_target_pairs={{0,24},{4,28},{8,16},{12,20},{16,8},{20,12},{24,0},{28,4},{1,25},{... | collective-permute-start | bytes 221192 | tf_op jit(solution)/shard_map/ppermute | solution.py:248
  59.2 3.4 %collective-permute-start.22 = (bf16[32,1152]{1,0:T(8,128)(2,1)S(1)}, bf16[32,1152]{1,0:T(8,128)(2,1)S(1)}, u32[]{:S(2)}, u32[]{:S(2)}) collective-permute-start(bf16[32,1152]{1,0:T(8,128)(2,1)S(1)} %get-tuple-element.73), channel_id=1, source_target_pairs={{0,8},{4,12},{8,0},{12,4},{16,24},{20,28},{24,16},{28,20},{1,9},{5... | collective-permute-start | bytes 221192 | tf_op jit(solution)/shard_map/ppermute | solution.py:248
  62.6 1.9 %collective-permute-done.20.refs_0_ = bf16[32,1152]{1,0:T(8,128)(2,1)S(1)} collective-permute-done((bf16[32,1152]{1,0:T(8,128)(2,1)S(1)}, bf16[32,1152]{1,0:T(8,128)(2,1)S(1)}, u32[]{:S(2)}, u32[]{:S(2)}) %collective-permute-start.20) | collective-permute-done | bytes 73760 | tf_op jit(solution)/shard_map/ppermute | solution.py:248
  64.4 1.5 %collective-permute-done.21.refs_1_ = bf16[32,1152]{1,0:T(8,128)(2,1)S(1)} collective-permute-done((bf16[32,1152]{1,0:T(8,128)(2,1)S(1)}, bf16[32,1152]{1,0:T(8,128)(2,1)S(1)}, u32[]{:S(2)}, u32[]{:S(2)}) %collective-permute-start.21) | collective-permute-done | bytes 73760 | tf_op jit(solution)/shard_map/ppermute | solution.py:248
  65.9 0.8 %shard_map.78 = bf16[8,16,1152]{2,1,0:T(8,128)(2,1)} custom-call(f32[6,1152]{1,0:T(8,128)S(1)} %copy-done.7, bf16[4,16,1152]{2,1,0:T(8,128)(2,1)S(1)} %get-tuple-element.57.kept_ref, bf16[4,16,1152]{2,1,0:T(8,128)(2,1)S(1)} %collective-permute-done.13.other_ref, bf16[32,1152]{1,0:T(8,128)(2,1)S(1)} %collective-permute-done.20.refs_0_, ...), custom_call_target="tpu_custom_call" | custom-call | flops 1 | bytes 1 | tf_op jit(solution)/shard_map/pallas_call | solution.py:235
  (45 shorter events, 5.9 us)
Async XLA Ops:
  0.0 3.0 %collective-permute-start = (bf16[1,128,1152]{2,1,0:T(8,128)(2,1)}, bf16[1,128,1152]{2,1,0:T(8,128)(2,1)S(1)}, u32[]{:S(2)}, u32[]{:S(2)}) collective-permute-start(bf16[1,128,1152]{2,1,0:T(8,128)(2,1)} %own_ref.1), channel_id=1, source_target_pairs={{0,1},{1,0},{2,3},{3,2},{4,5},{5,4},{6,7},{7,6},{8,9},{9,8},{10,11... | collective-permute-start | bytes 884744 | tf_op jit(solution)/shard_map/ppermute | solution.py:248
  0.5 10.4 %collective-permute-start.2 = (bf16[1,128,1152]{2,1,0:T(8,128)(2,1)}, bf16[1,128,1152]{2,1,0:T(8,128)(2,1)S(1)}, u32[]{:S(2)}, u32[]{:S(2)}) collective-permute-start(bf16[1,128,1152]{2,1,0:T(8,128)(2,1)} %own_ref.1), channel_id=1, source_target_pairs={{0,2},{1,3},{2,0},{3,1},{4,6},{5,7},{6,4},{7,5},{8,10},{9,11},{10,... | collective-permute-start | bytes 884744 | tf_op jit(solution)/shard_map/ppermute | solution.py:248
  3.0 1.0 %copy-start.5 = (bf16[1,128,1152]{2,1,0:T(8,128)(2,1)S(1)}, bf16[1,128,1152]{2,1,0:T(8,128)(2,1)}, u32[]{:S(2)}) copy-start(bf16[1,128,1152]{2,1,0:T(8,128)(2,1)} %own_ref.1) | copy-start | bytes 884740
  4.1 6.8 %collective-permute-start.1 = (bf16[64,1152]{1,0:T(8,128)(2,1)S(1)}, bf16[64,1152]{1,0:T(8,128)(2,1)S(1)}, u32[]{:S(2)}, u32[]{:S(2)}) collective-permute-start(bf16[64,1152]{1,0:T(8,128)(2,1)S(1)} %get-tuple-element.42), channel_id=1, source_target_pairs={{0,4},{4,0},{8,12},{12,8},{16,20},{20,16},{24,28},{28,24},{1,5},{5... | collective-permute-start | bytes 442376 | tf_op jit(solution)/shard_map/ppermute | solution.py:248
  5.8 1.6 %copy-start = (bf16[864,1152]{1,0:T(8,128)(2,1)S(1)}, bf16[864,1152]{1,0:T(8,128)(2,1)}, u32[]{:S(2)}) copy-start(bf16[864,1152]{1,0:T(8,128)(2,1)} %weight_ref.3) | copy-start | bytes 5971972
  7.4 0.8 %copy-start.6 = (f32[6,1152]{1,0:T(8,128)S(1)}, f32[6,1152]{1,0:T(8,128)}, u32[]{:S(2)}) copy-start(f32[6,1152]{1,0:T(8,128)} %mod_ref.7) | copy-start | bytes 82948
  8.2 4.4 %copy-start.3 = (bf16[288,1152]{1,0:T(8,128)(2,1)S(1)}, bf16[288,1152]{1,0:T(8,128)(2,1)}, u32[]{:S(2)}) copy-start(bf16[288,1152]{1,0:T(8,128)(2,1)} %refs_0_.4) | copy-start | bytes 1990660
  8.2 4.8 %copy-start.1 = (bf16[864,1152]{1,0:T(8,128)(2,1)S(1)}, bf16[864,1152]{1,0:T(8,128)(2,1)}, u32[]{:S(2)}) copy-start(bf16[864,1152]{1,0:T(8,128)(2,1)} %weight_ref.3) | copy-start | bytes 5971972
  10.9 1.6 %collective-permute-start.3 = (bf16[1,128,1152]{2,1,0:T(8,128)(2,1)S(1)}, bf16[1,128,1152]{2,1,0:T(8,128)(2,1)S(1)}, u32[]{:S(2)}, u32[]{:S(2)}) collective-permute-start(bf16[1,128,1152]{2,1,0:T(8,128)(2,1)S(1)} %collective-permute-done.2.refs_0_), channel_id=1, source_target_pairs={{0,1},{1,0},{2,3},{3,2},{4,5},{5,4},{6,7},{7,6},{8,9},{9,8},{10,11... | collective-permute-start | bytes 884744 | tf_op jit(solution)/shard_map/ppermute | solution.py:248
  12.4 28.3 %collective-permute-start.14 = (bf16[864,1152]{1,0:T(8,128)(2,1)}, bf16[864,1152]{1,0:T(8,128)(2,1)S(1)}, u32[]{:S(2)}, u32[]{:S(2)}) collective-permute-start(bf16[864,1152]{1,0:T(8,128)(2,1)} %refs_0_.7), channel_id=1, source_target_pairs={{0,1},{1,0},{2,3},{3,2},{4,5},{5,4},{6,7},{7,6},{8,9},{9,8},{10,11... | collective-permute-start | bytes 5971976 | tf_op jit(solution)/shard_map/ppermute | solution.py:248
  12.6 4.7 %collective-permute-start.5 = (bf16[288,1152]{1,0:T(8,128)(2,1)S(1)}, bf16[288,1152]{1,0:T(8,128)(2,1)S(1)}, u32[]{:S(2)}, u32[]{:S(2)}) collective-permute-start(bf16[288,1152]{1,0:T(8,128)(2,1)S(1)} %copy-done.3), channel_id=1, source_target_pairs={{0,1},{1,0},{2,3},{3,2},{4,5},{5,4},{6,7},{7,6},{8,9},{9,8},{10,11... | collective-permute-start | bytes 1990664 | tf_op jit(solution)/shard_map/ppermute | solution.py:248
  15.5 1.7 %collective-permute-start.4 = (bf16[288,128]{1,0:T(8,128)(2,1)S(1)}, bf16[288,128]{1,0:T(8,128)(2,1)S(1)}, u32[]{:S(2)}, u32[]{:S(2)}) collective-permute-start(bf16[288,128]{1,0:T(8,128)(2,1)S(1)} %get-tuple-element.45), channel_id=1, source_target_pairs={{0,1},{1,0},{2,3},{3,2},{4,5},{5,4},{6,7},{7,6},{8,9},{9,8},{10,11... | collective-permute-start | bytes 221192 | tf_op jit(solution)/shard_map/ppermute | solution.py:248
  17.7 6.6 %copy-start.4 = (bf16[288,1152]{1,0:T(8,128)(2,1)S(1)}, bf16[288,1152]{1,0:T(8,128)(2,1)}, u32[]{:S(2)}) copy-start(bf16[288,1152]{1,0:T(8,128)(2,1)} %refs_2_.7) | copy-start | bytes 1990660
  17.7 7.2 %collective-permute-start.8 = (bf16[64,1152]{1,0:T(8,128)(2,1)S(1)}, bf16[64,1152]{1,0:T(8,128)(2,1)S(1)}, u32[]{:S(2)}, u32[]{:S(2)}) collective-permute-start(bf16[64,1152]{1,0:T(8,128)(2,1)S(1)} %get-tuple-element.53), channel_id=1, source_target_pairs={{0,6},{1,7},{2,4},{3,5},{4,2},{5,3},{6,0},{7,1},{8,14},{9,15},{10,... | collective-permute-start | bytes 442376 | tf_op jit(solution)/shard_map/ppermute | solution.py:271
  20.5 7.5 %collective-permute-start.7 = (bf16[64,1152]{1,0:T(8,128)(2,1)S(1)}, bf16[64,1152]{1,0:T(8,128)(2,1)S(1)}, u32[]{:S(2)}, u32[]{:S(2)}) collective-permute-start(bf16[64,1152]{1,0:T(8,128)(2,1)S(1)} %get-tuple-element.47), channel_id=1, source_target_pairs={{0,2},{1,3},{2,0},{3,1},{4,6},{5,7},{6,4},{7,5},{8,10},{9,11},{10,... | collective-permute-start | bytes 442376 | tf_op jit(solution)/shard_map/ppermute | solution.py:248
  22.2 1.3 %collective-permute-start.6 = (bf16[288,128]{1,0:T(8,128)(2,1)S(1)}, bf16[288,128]{1,0:T(8,128)(2,1)S(1)}, u32[]{:S(2)}, u32[]{:S(2)}) collective-permute-start(bf16[288,128]{1,0:T(8,128)(2,1)S(1)} %get-tuple-element.51), channel_id=1, source_target_pairs={{0,1},{1,0},{2,3},{3,2},{4,5},{5,4},{6,7},{7,6},{8,9},{9,8},{10,11... | collective-permute-start | bytes 221192 | tf_op jit(solution)/shard_map/ppermute | solution.py:248
  23.9 5.0 %copy-start.7 = (f32[6,1152]{1,0:T(8,128)S(1)}, f32[6,1152]{1,0:T(8,128)}, u32[]{:S(2)}) copy-start(f32[6,1152]{1,0:T(8,128)} %mod_ref.7) | copy-start | bytes 82948
  23.9 4.6 %collective-permute-start.9 = (bf16[64,576]{1,0:T(8,128)(2,1)S(1)}, bf16[64,576]{1,0:T(8,128)(2,1)S(1)}, u32[]{:S(2)}, u32[]{:S(2)}) collective-permute-start(bf16[64,576]{1,0:T(8,128)(2,1)S(1)} %get-tuple-element.55), channel_id=1, source_target_pairs={{0,4},{4,0},{8,12},{12,8},{16,20},{20,16},{24,28},{28,24},{1,5},{5... | collective-permute-start | bytes 221192 | tf_op jit(solution)/shard_map/ppermute | solution.py:248
  24.3 16.5 %collective-permute-start.15 = (bf16[288,1152]{1,0:T(8,128)(2,1)S(1)}, bf16[288,1152]{1,0:T(8,128)(2,1)S(1)}, u32[]{:S(2)}, u32[]{:S(2)}) collective-permute-start(bf16[288,1152]{1,0:T(8,128)(2,1)S(1)} %copy-done.4), channel_id=1, source_target_pairs={{0,1},{1,0},{2,3},{3,2},{4,5},{5,4},{6,7},{7,6},{8,9},{9,8},{10,11... | collective-permute-start | bytes 1990664 | tf_op jit(solution)/shard_map/ppermute | solution.py:248
  28.1 12.7 %copy-start.2 = (bf16[864,1152]{1,0:T(8,128)(2,1)S(1)}, bf16[864,1152]{1,0:T(8,128)(2,1)}, u32[]{:S(2)}) copy-start(bf16[864,1152]{1,0:T(8,128)(2,1)} %refs_0_.7) | copy-start | bytes 5971972
  29.3 6.8 %collective-permute-start.10 = (bf16[32,1152]{1,0:T(8,128)(2,1)S(1)}, bf16[32,1152]{1,0:T(8,128)(2,1)S(1)}, u32[]{:S(2)}, u32[]{:S(2)}) collective-permute-start(bf16[32,1152]{1,0:T(8,128)(2,1)S(1)} %get-tuple-element.59), channel_id=1, source_target_pairs={{0,24},{4,28},{8,16},{12,20},{16,8},{20,12},{24,0},{28,4},{1,25},{... | collective-permute-start | bytes 221192 | tf_op jit(solution)/shard_map/ppermute | solution.py:248
  32.9 6.2 %collective-permute-start.11 = (bf16[32,1152]{1,0:T(8,128)(2,1)S(1)}, bf16[32,1152]{1,0:T(8,128)(2,1)S(1)}, u32[]{:S(2)}, u32[]{:S(2)}) collective-permute-start(bf16[32,1152]{1,0:T(8,128)(2,1)S(1)} %get-tuple-element.60), channel_id=1, source_target_pairs={{0,16},{4,20},{8,24},{12,28},{16,0},{20,4},{24,8},{28,12},{1,17},{... | collective-permute-start | bytes 221192 | tf_op jit(solution)/shard_map/ppermute | solution.py:248
  32.9 6.2 %collective-permute-start.12 = (bf16[32,1152]{1,0:T(8,128)(2,1)S(1)}, bf16[32,1152]{1,0:T(8,128)(2,1)S(1)}, u32[]{:S(2)}, u32[]{:S(2)}) collective-permute-start(bf16[32,1152]{1,0:T(8,128)(2,1)S(1)} %get-tuple-element.61), channel_id=1, source_target_pairs={{0,8},{4,12},{8,0},{12,4},{16,24},{20,28},{24,16},{28,20},{1,9},{5... | collective-permute-start | bytes 221192 | tf_op jit(solution)/shard_map/ppermute | solution.py:248
  39.2 8.6 %collective-permute-start.16 = (bf16[128,1152]{1,0:T(8,128)(2,1)S(1)}, bf16[128,1152]{1,0:T(8,128)(2,1)S(1)}, u32[]{:S(2)}, u32[]{:S(2)}) collective-permute-start(bf16[128,1152]{1,0:T(8,128)(2,1)S(1)} %shard_map.73.refs_4_), channel_id=1, source_target_pairs={{0,2},{1,3},{2,0},{3,1},{4,6},{5,7},{6,4},{7,5},{8,10},{9,11},{10,... | collective-permute-start | bytes 884744 | tf_op jit(solution)/shard_map/ppermute | solution.py:248
  42.7 4.5 %collective-permute-start.17 = (bf16[64,576]{1,0:T(8,128)(2,1)S(1)}, bf16[64,576]{1,0:T(8,128)(2,1)S(1)}, u32[]{:S(2)}, u32[]{:S(2)}) collective-permute-start(bf16[64,576]{1,0:T(8,128)(2,1)S(1)} %get-tuple-element.67), channel_id=1, source_target_pairs={{0,4},{4,0},{8,12},{12,8},{16,20},{20,16},{24,28},{28,24},{1,5},{5... | collective-permute-start | bytes 221192 | tf_op jit(solution)/shard_map/ppermute | solution.py:248
  49.8 7.3 %collective-permute-start.18 = (bf16[64,1152]{1,0:T(8,128)(2,1)S(1)}, bf16[64,1152]{1,0:T(8,128)(2,1)S(1)}, u32[]{:S(2)}, u32[]{:S(2)}) collective-permute-start(bf16[64,1152]{1,0:T(8,128)(2,1)S(1)} %get-tuple-element.69), channel_id=1, source_target_pairs={{0,2},{1,3},{2,0},{3,1},{4,6},{5,7},{6,4},{7,5},{8,10},{9,11},{10,... | collective-permute-start | bytes 442376 | tf_op jit(solution)/shard_map/ppermute | solution.py:248
  51.4 6.7 %collective-permute-start.19 = (bf16[64,1152]{1,0:T(8,128)(2,1)S(1)}, bf16[64,1152]{1,0:T(8,128)(2,1)S(1)}, u32[]{:S(2)}, u32[]{:S(2)}) collective-permute-start(bf16[64,1152]{1,0:T(8,128)(2,1)S(1)} %get-tuple-element.70), channel_id=1, source_target_pairs={{0,6},{1,7},{2,4},{3,5},{4,2},{5,3},{6,0},{7,1},{8,14},{9,15},{10,... | collective-permute-start | bytes 442376 | tf_op jit(solution)/shard_map/ppermute | solution.py:271
  52.6 10.0 %collective-permute-start.13 = (bf16[4,16,1152]{2,1,0:T(8,128)(2,1)S(1)}, bf16[4,16,1152]{2,1,0:T(8,128)(2,1)S(1)}, u32[]{:S(2)}, u32[]{:S(2)}) collective-permute-start(bf16[4,16,1152]{2,1,0:T(8,128)(2,1)S(1)} %get-tuple-element.63), channel_id=1, source_target_pairs={{0,4},{4,0},{8,12},{12,8},{16,20},{20,16},{24,28},{28,24},{1,5},{5... | collective-permute-start | bytes 442376 | tf_op jit(solution)/shard_map/ppermute | solution.py:248
  58.1 6.3 %collective-permute-start.20 = (bf16[32,1152]{1,0:T(8,128)(2,1)S(1)}, bf16[32,1152]{1,0:T(8,128)(2,1)S(1)}, u32[]{:S(2)}, u32[]{:S(2)}) collective-permute-start(bf16[32,1152]{1,0:T(8,128)(2,1)S(1)} %get-tuple-element.71), channel_id=1, source_target_pairs={{0,24},{4,28},{8,16},{12,20},{16,8},{20,12},{24,0},{28,4},{1,25},{... | collective-permute-start | bytes 221192 | tf_op jit(solution)/shard_map/ppermute | solution.py:248
  59.2 6.7 %collective-permute-start.21 = (bf16[32,1152]{1,0:T(8,128)(2,1)S(1)}, bf16[32,1152]{1,0:T(8,128)(2,1)S(1)}, u32[]{:S(2)}, u32[]{:S(2)}) collective-permute-start(bf16[32,1152]{1,0:T(8,128)(2,1)S(1)} %get-tuple-element.72), channel_id=1, source_target_pairs={{0,16},{4,20},{8,24},{12,28},{16,0},{20,4},{24,8},{28,12},{1,17},{... | collective-permute-start | bytes 221192 | tf_op jit(solution)/shard_map/ppermute | solution.py:248
  59.2 6.7 %collective-permute-start.22 = (bf16[32,1152]{1,0:T(8,128)(2,1)S(1)}, bf16[32,1152]{1,0:T(8,128)(2,1)S(1)}, u32[]{:S(2)}, u32[]{:S(2)}) collective-permute-start(bf16[32,1152]{1,0:T(8,128)(2,1)S(1)} %get-tuple-element.73), channel_id=1, source_target_pairs={{0,8},{4,12},{8,0},{12,4},{16,24},{20,28},{24,16},{28,20},{1,9},{5... | collective-permute-start | bytes 221192 | tf_op jit(solution)/shard_map/ppermute | solution.py:248

commit v18 on v16

--- a/solution.py
+++ b/solution.py
@@ -192,31 +192,35 @@
             ref[...] = half.astype(ref.dtype)
 
 
-def sum_kernel(groups, *refs):
-    piece_refs = refs[2 * groups :]
-    period = piece_refs[0].shape[0] // 2
-    for at, update in enumerate(total_updates(groups, refs)):
-        update = update.astype(BF16)
-        for piece, ref in enumerate(piece_refs):
-            rows = update[piece * period : (piece + 1) * period]
-            ref[at * period : (at + 1) * period, :] = rows
-
-
-def result_kernel(pieces, mod_ref, kept_ref, other_ref, *refs):
-    piece_refs, out_ref = refs[:-1], refs[-1]
-    period = kept_ref.shape[1]
-    here = lax.axis_index("frame")
+def sum_kernel(pieces, *refs):
+    update = sum(ref[...].astype(F32) for ref in refs[:-pieces]).astype(BF16)
+    period = update.shape[0] // pieces
+    for at, ref in enumerate(refs[-pieces:]):
+        ref[...] = update[at * period : (at + 1) * period]
+
+
+def result_rows(mod_ref, middle_ref, piece_refs):
+    here = lax.axis_index("frame") // 2
     for at, ref in enumerate(piece_refs):
-        there = here // 2 ^ (pieces - 1 - at)
-        for half, middle_ref in enumerate((kept_ref, other_ref)):
-            update = ref[half * period : (half + 1) * period, :].astype(F32)
-            middle = middle_ref[there].astype(F32)
-            out_ref[2 * there + (here % 2 ^ half)] = (middle + mod_ref[5:6, :] * update).astype(
-                BF16
-            )
-
-
-def call(body, operands, outs, scratch=(), limit=24):
+        there = here ^ (len(piece_refs) - 1 - at)
+        update = ref[...].astype(F32)
+        yield there, (middle_ref[there].astype(F32) + mod_ref[5:6, :] * update).astype(BF16)
+
+
+def first_result_kernel(mod_ref, middle_ref, *refs):
+    for there, rows in result_rows(mod_ref, middle_ref, refs[:-1]):
+        refs[-1][there] = rows
+
+
+def result_kernel(mod_ref, middle_ref, done_ref, *refs):
+    half = lax.axis_index("frame") % 2
+    for there in range(done_ref.shape[0]):
+        refs[-1][2 * there + half] = done_ref[there]
+    for there, rows in result_rows(mod_ref, middle_ref, refs[:-1]):
+        refs[-1][2 * there + (1 - half)] = rows
+
+
+def call(body, operands, outs, scratch=(), limit=24, flops=1):
     return pl.pallas_call(
         body,
         out_shape=outs,
@@ -224,7 +228,7 @@
         out_specs=[pl.BlockSpec(memory_space=pltpu.VMEM)] * len(outs),
         scratch_shapes=list(scratch),
         compiler_params=pltpu.CompilerParams(vmem_limit_bytes=limit * MIB),
-        cost_estimate=pl.CostEstimate(flops=1, bytes_accessed=1, transcendentals=0),
+        cost_estimate=pl.CostEstimate(flops=flops, bytes_accessed=1, transcendentals=0),
     )(*operands)
 
 
@@ -340,14 +344,20 @@
     others = [after(block, received) for block in segments[1:]]
     far_parts = attend_frames(False, others, far_shapes)
     updates = return_updates((kept, received), far_parts)
-    parts = call(
-        functools.partial(sum_kernel, groups),
-        updates,
-        piece_shapes,
+    piece_shapes = [shape((period, width), BF16)] * pieces
+    first, second = (
+        exchange_frames(call(functools.partial(sum_kernel, pieces), part, piece_shapes))
+        for part in (updates[:groups], updates[groups:])
+    )
+    (done,) = call(
+        first_result_kernel,
+        (modulation, middle, *first),
+        [shape((pieces, period, width), BF16)],
+        flops=4_000_000_000,
     )
     (result,) = call(
-        functools.partial(result_kernel, pieces),
-        (modulation, middle, middle_other, *exchange_frames(parts)),
+        result_kernel,
+        (modulation, middle_other, done, *second),
         [shape((frames, period, width), BF16)],
     )
     return result.reshape(1, rows, width)

time: 65.8 us -> 70.6 us (1.073)
  starting transfers between devices: 24.9 us -> 30.3 us
    ppermute x20 -> x23, starting transfers between devices: 22 us -> 27.4 us  [swap(): return lax.ppermute(value, axis, [(at, at ^ offset) for at in range(size)])]
    ppermute x2, waiting for transfers between devices: 1.2 us -> 0.01 us  [swap_diagonal(): return lax.ppermute(value, ('frame', 'patch'), pairs)]
    ppermute x20 -> x23, waiting for transfers between devices: 24.8 us -> 25.5 us  [swap(): return lax.ppermute(value, axis, [(at, at ^ offset) for at in range(size)])]
    pallas_call x12 -> x14, Pallas kernels: 11.1 us -> 11.1 us  [call(): pl.pallas_call(body, out_shape=outs, in_specs=[pl.BlockSpec(memory_space=...]
  transfers between devices with their start and end apart: 22 -> 25, of which waited for: 11 -> 11; matrix products, arithmetic and copies ran while one was open for 0% -> 0% of each run, Pallas kernels for 13% -> 12%
where the time goes in v18:
time: 70.6 us; the launch traced here: 70.4 us
  starting transfers between devices  30.3 us (43%)
  waiting for transfers between devices  25.5 us (36%)
  Pallas kernels  11.1 us (16%)
  local copies, waits for them, and re-layouts  3.34 us (5%)
    ppermute x23, starting transfers between devices, swap(): return lax.ppermute(value, axis, [(at, at ^ offset) for at in range(size)])  27.4 us
    ppermute x23, waiting for transfers between devices, swap(): return lax.ppermute(value, axis, [(at, at ^ offset) for at in range(size)])  25.5 us
    pallas_call x14, Pallas kernels, call(): pl.pallas_call(body, out_shape=outs, in_specs=[pl.BlockSpec(memory_space=...  11.1 us
    unnamed x16, local copies, waits for them, and re-layouts  3.34 us
    ppermute x2, starting transfers between devices, swap_diagonal(): return lax.ppermute(value, ('frame', 'patch'), pairs)  2.85 us
  transfers between devices with their start and end apart: 25, of which 11 were waited for; matrix products, arithmetic and copies ran while one was open for 0% of the time, Pallas kernels for 12%

profile of v18, /device:TPU:0, one launch (start us, length us, event | category | flops | bytes accessed | tf_op | source)
XLA Modules:
  0.0 70.4 jit_solution(8592086289720948555)
XLA Ops:
  0.5 2.5 %collective-permute-start.2 = (bf16[1,128,1152]{2,1,0:T(8,128)(2,1)}, bf16[1,128,1152]{2,1,0:T(8,128)(2,1)S(1)}, u32[]{:S(2)}, u32[]{:S(2)}) collective-permute-start(bf16[1,128,1152]{2,1,0:T(8,128)(2,1)} %own_ref.1), channel_id=1, source_target_pairs={{0,2},{1,3},{2,0},{3,1},{4,6},{5,7},{6,4},{7,5},{8,10},{9,11},{10,... | collective-permute-start | bytes 884744 | tf_op jit(solution)/shard_map/ppermute | solution.py:237
  3.0 1.0 %copy-done.5 = bf16[1,128,1152]{2,1,0:T(8,128)(2,1)S(1)} copy-done((bf16[1,128,1152]{2,1,0:T(8,128)(2,1)S(1)}, bf16[1,128,1152]{2,1,0:T(8,128)(2,1)}, u32[]{:S(2)}) %copy-start.5) | copy-done | bytes 294936
  4.1 1.8 %collective-permute-start.1 = (bf16[64,1152]{1,0:T(8,128)(2,1)S(1)}, bf16[64,1152]{1,0:T(8,128)(2,1)S(1)}, u32[]{:S(2)}, u32[]{:S(2)}) collective-permute-start(bf16[64,1152]{1,0:T(8,128)(2,1)S(1)} %get-tuple-element.40), channel_id=1, source_target_pairs={{0,4},{4,0},{8,12},{12,8},{16,20},{20,16},{24,28},{28,24},{1,5},{5... | collective-permute-start | bytes 442376 | tf_op jit(solution)/shard_map/ppermute | solution.py:237
  5.9 1.6 %copy-done = bf16[864,1152]{1,0:T(8,128)(2,1)S(1)} copy-done((bf16[864,1152]{1,0:T(8,128)(2,1)S(1)}, bf16[864,1152]{1,0:T(8,128)(2,1)}, u32[]{:S(2)}) %copy-start) | copy-done | bytes 1990680
  7.4 0.8 %copy-done.6 = f32[6,1152]{1,0:T(8,128)S(1)} copy-done((f32[6,1152]{1,0:T(8,128)S(1)}, f32[6,1152]{1,0:T(8,128)}, u32[]{:S(2)}) %copy-start.6) | copy-done | bytes 27672
  8.2 1.1 %shard_map.65.near_ref = f32[864,256]{1,0:T(8,128)S(1)} custom-call(f32[6,1152]{1,0:T(8,128)S(1)} %copy-done.6, bf16[864,1152]{1,0:T(8,128)(2,1)S(1)} %copy-done, bf16[1,128,1152]{2,1,0:T(8,128)(2,1)S(1)} %copy-done.5, bf16[1,128,1152]{2,1,0:T(8,128)(2,1)S(1)} %collective-permute-done.sister_ref), custom_call_target="tpu_custom_call" | custom-call | flops 1 | bytes 1 | tf_op jit(solution)/shard_map/pallas_call | solution.py:224
  9.3 1.6 %collective-permute-done.2.refs_0_ = bf16[1,128,1152]{2,1,0:T(8,128)(2,1)S(1)} collective-permute-done((bf16[1,128,1152]{2,1,0:T(8,128)(2,1)}, bf16[1,128,1152]{2,1,0:T(8,128)(2,1)S(1)}, u32[]{:S(2)}, u32[]{:S(2)}) %collective-permute-start.2) | collective-permute-done | bytes 294944 | tf_op jit(solution)/shard_map/ppermute | solution.py:237
  10.9 1.6 %collective-permute-done.3.refs_1_ = bf16[1,128,1152]{2,1,0:T(8,128)(2,1)S(1)} collective-permute-done((bf16[1,128,1152]{2,1,0:T(8,128)(2,1)S(1)}, bf16[1,128,1152]{2,1,0:T(8,128)(2,1)S(1)}, u32[]{:S(2)}, u32[]{:S(2)}) %collective-permute-start.3) | collective-permute-done | bytes 294944 | tf_op jit(solution)/shard_map/ppermute | solution.py:237
  13.0 3.3 %shard_map.66 = (bf16[288,256]{1,0:T(8,128)(2,1)S(1)}, bf16[288,256]{1,0:T(8,128)(2,1)S(1)}) custom-call(f32[6,1152]{1,0:T(8,128)S(1)} %copy-done.6, bf16[864,1152]{1,0:T(8,128)(2,1)S(1)} %copy-done.1, f32[864,256]{1,0:T(8,128)S(1)} %shard_map.65.near_ref, bf16[1,128,1152]{2,1,0:T(8,128)(2,1)S(1)} %collective-permute-done.2.refs_0_, ...), custom_call_target="tpu_custom_call" | custom-call | flops 1 | bytes 1 | tf_op jit(solution)/shard_map/pallas_call | solution.py:224
  16.5 1.2 %collective-permute-done.4.refs_1_ = bf16[288,256]{1,0:T(8,128)(2,1)S(1)} collective-permute-done((bf16[288,256]{1,0:T(8,128)(2,1)S(1)}, bf16[288,256]{1,0:T(8,128)(2,1)S(1)}, u32[]{:S(2)}, u32[]{:S(2)}) %collective-permute-start.4) | collective-permute-done | bytes 147488 | tf_op jit(solution)/shard_map/ppermute | solution.py:237
  18.7 1.8 %collective-permute-start.6 = (bf16[64,1152]{1,0:T(8,128)(2,1)S(1)}, bf16[64,1152]{1,0:T(8,128)(2,1)S(1)}, u32[]{:S(2)}, u32[]{:S(2)}) collective-permute-start(bf16[64,1152]{1,0:T(8,128)(2,1)S(1)} %get-tuple-element.46), channel_id=1, source_target_pairs={{0,2},{1,3},{2,0},{3,1},{4,6},{5,7},{6,4},{7,5},{8,10},{9,11},{10,... | collective-permute-start | bytes 442376 | tf_op jit(solution)/shard_map/ppermute | solution.py:237
  20.5 1.4 %collective-permute-start.8 = (bf16[64,1152]{1,0:T(8,128)(2,1)S(1)}, bf16[64,1152]{1,0:T(8,128)(2,1)S(1)}, u32[]{:S(2)}, u32[]{:S(2)}) collective-permute-start(bf16[64,1152]{1,0:T(8,128)(2,1)S(1)} %get-tuple-element.48), channel_id=1, source_target_pairs={{0,6},{1,7},{2,4},{3,5},{4,2},{5,3},{6,0},{7,1},{8,14},{9,15},{10,... | collective-permute-start | bytes 442376 | tf_op jit(solution)/shard_map/ppermute | solution.py:260
  22.2 5.6 %collective-permute-done.7.head_ref = bf16[64,576]{1,0:T(8,128)(2,1)S(1)} collective-permute-done((bf16[64,576]{1,0:T(8,128)(2,1)S(1)}, bf16[64,576]{1,0:T(8,128)(2,1)S(1)}, u32[]{:S(2)}, u32[]{:S(2)}) %collective-permute-start.7) | collective-permute-done | bytes 73760 | tf_op jit(solution)/shard_map/ppermute | solution.py:237
  28.6 3.9 %collective-permute-start.9 = (bf16[32,1152]{1,0:T(8,128)(2,1)S(1)}, bf16[32,1152]{1,0:T(8,128)(2,1)S(1)}, u32[]{:S(2)}, u32[]{:S(2)}) collective-permute-start(bf16[32,1152]{1,0:T(8,128)(2,1)S(1)} %get-tuple-element.50), channel_id=1, source_target_pairs={{0,24},{4,28},{8,16},{12,20},{16,8},{20,12},{24,0},{28,4},{1,25},{... | collective-permute-start | bytes 221192 | tf_op jit(solution)/shard_map/ppermute | solution.py:237
  33.1 2.5 %collective-permute-done.9.refs_0_ = bf16[32,1152]{1,0:T(8,128)(2,1)S(1)} collective-permute-done((bf16[32,1152]{1,0:T(8,128)(2,1)S(1)}, bf16[32,1152]{1,0:T(8,128)(2,1)S(1)}, u32[]{:S(2)}, u32[]{:S(2)}) %collective-permute-start.9) | collective-permute-done | bytes 73760 | tf_op jit(solution)/shard_map/ppermute | solution.py:237
  35.6 2.7 %collective-permute-done.10.refs_1_ = bf16[32,1152]{1,0:T(8,128)(2,1)S(1)} collective-permute-done((bf16[32,1152]{1,0:T(8,128)(2,1)S(1)}, bf16[32,1152]{1,0:T(8,128)(2,1)S(1)}, u32[]{:S(2)}, u32[]{:S(2)}) %collective-permute-start.10) | collective-permute-done | bytes 73760 | tf_op jit(solution)/shard_map/ppermute | solution.py:237
  38.3 1.6 %collective-permute-start.15 = (bf16[128,1152]{1,0:T(8,128)(2,1)S(1)}, bf16[128,1152]{1,0:T(8,128)(2,1)S(1)}, u32[]{:S(2)}, u32[]{:S(2)}) collective-permute-start(bf16[128,1152]{1,0:T(8,128)(2,1)S(1)} %shard_map.70.refs_4_), channel_id=1, source_target_pairs={{0,2},{1,3},{2,0},{3,1},{4,6},{5,7},{6,4},{7,5},{8,10},{9,11},{10,... | collective-permute-start | bytes 884744 | tf_op jit(solution)/shard_map/ppermute | solution.py:237
  39.9 1.9 %shard_map.71 = (f32[64,1152]{1,0:T(8,128)S(1)}, bf16[64,576]{1,0:T(8,128)(2,1)S(1)}) custom-call(bf16[864,1152]{1,0:T(8,128)(2,1)S(1)} %copy-done.2, bf16[864,1152]{1,0:T(8,128)(2,1)S(1)} %collective-permute-done.13.refs_1_, bf16[288,1152]{1,0:T(8,128)(2,1)S(1)} %copy-done.3, bf16[288,1152]{1,0:T(8,128)(2,1)S(1)} %collective-permute-done.14.refs_3_.refs_1_, ...), custom_call_target="tpu_custom_call" | custom-call | flops 1 | bytes 1 | tf_op jit(solution)/shard_map/pallas_call | solution.py:224
  41.9 1.6 %collective-permute-start.16 = (bf16[64,576]{1,0:T(8,128)(2,1)S(1)}, bf16[64,576]{1,0:T(8,128)(2,1)S(1)}, u32[]{:S(2)}, u32[]{:S(2)}) collective-permute-start(bf16[64,576]{1,0:T(8,128)(2,1)S(1)} %get-tuple-element.59), channel_id=1, source_target_pairs={{0,4},{4,0},{8,12},{12,8},{16,20},{20,16},{24,28},{28,24},{1,5},{5... | collective-permute-start | bytes 221192 | tf_op jit(solution)/shard_map/ppermute | solution.py:237
  43.4 3.0 %collective-permute-done.16.head_ref = bf16[64,576]{1,0:T(8,128)(2,1)S(1)} collective-permute-done((bf16[64,576]{1,0:T(8,128)(2,1)S(1)}, bf16[64,576]{1,0:T(8,128)(2,1)S(1)}, u32[]{:S(2)}, u32[]{:S(2)}) %collective-permute-start.16) | collective-permute-done | bytes 73760 | tf_op jit(solution)/shard_map/ppermute | solution.py:237
  46.8 2.0 %shard_map.73 = (bf16[64,1152]{1,0:T(8,128)(2,1)S(1)}, bf16[64,1152]{1,0:T(8,128)(2,1)S(1)}) custom-call(bf16[864,1152]{1,0:T(8,128)(2,1)S(1)} %copy-done.2, bf16[864,1152]{1,0:T(8,128)(2,1)S(1)} %collective-permute-done.13.refs_1_, bf16[288,1152]{1,0:T(8,128)(2,1)S(1)} %copy-done.3, bf16[288,1152]{1,0:T(8,128)(2,1)S(1)} %collective-permute-done.14.refs_3_.refs_1_, ...), custom_call_target="tpu_custom_call" | custom-call | flops 1 | bytes 1 | tf_op jit(solution)/shard_map/pallas_call | solution.py:224
  48.7 1.6 %collective-permute-start.17 = (bf16[64,1152]{1,0:T(8,128)(2,1)S(1)}, bf16[64,1152]{1,0:T(8,128)(2,1)S(1)}, u32[]{:S(2)}, u32[]{:S(2)}) collective-permute-start(bf16[64,1152]{1,0:T(8,128)(2,1)S(1)} %get-tuple-element.61), channel_id=1, source_target_pairs={{0,2},{1,3},{2,0},{3,1},{4,6},{5,7},{6,4},{7,5},{8,10},{9,11},{10,... | collective-permute-start | bytes 442376 | tf_op jit(solution)/shard_map/ppermute | solution.py:237
  50.3 1.4 %collective-permute-start.21 = (bf16[64,1152]{1,0:T(8,128)(2,1)S(1)}, bf16[64,1152]{1,0:T(8,128)(2,1)S(1)}, u32[]{:S(2)}, u32[]{:S(2)}) collective-permute-start(bf16[64,1152]{1,0:T(8,128)(2,1)S(1)} %get-tuple-element.66), channel_id=1, source_target_pairs={{0,6},{1,7},{2,4},{3,5},{4,2},{5,3},{6,0},{7,1},{8,14},{9,15},{10,... | collective-permute-start | bytes 442376 | tf_op jit(solution)/shard_map/ppermute | solution.py:260
  51.7 5.1 %collective-permute-done.17.refs_1_ = bf16[64,1152]{1,0:T(8,128)(2,1)S(1)} collective-permute-done((bf16[64,1152]{1,0:T(8,128)(2,1)S(1)}, bf16[64,1152]{1,0:T(8,128)(2,1)S(1)}, u32[]{:S(2)}, u32[]{:S(2)}) %collective-permute-start.17) | collective-permute-done | bytes 147488 | tf_op jit(solution)/shard_map/ppermute | solution.py:237
  56.9 1.4 %collective-permute-start.18 = (bf16[16,1152]{1,0:T(8,128)(2,1)S(1)}, bf16[16,1152]{1,0:T(8,128)(2,1)S(1)}, u32[]{:S(2)}, u32[]{:S(2)}) collective-permute-start(bf16[16,1152]{1,0:T(8,128)(2,1)S(1)} %get-tuple-element.62), channel_id=1, source_target_pairs={{0,24},{4,28},{8,16},{12,20},{16,8},{20,12},{24,0},{28,4},{1,25},{... | collective-permute-start | bytes 110600 | tf_op jit(solution)/shard_map/ppermute | solution.py:237
  58.2 3.1 %collective-permute-start.20 = (bf16[16,1152]{1,0:T(8,128)(2,1)S(1)}, bf16[16,1152]{1,0:T(8,128)(2,1)S(1)}, u32[]{:S(2)}, u32[]{:S(2)}) collective-permute-start(bf16[16,1152]{1,0:T(8,128)(2,1)S(1)} %get-tuple-element.64), channel_id=1, source_target_pairs={{0,8},{4,12},{8,0},{12,4},{16,24},{20,28},{24,16},{28,20},{1,9},{5... | collective-permute-start | bytes 110600 | tf_op jit(solution)/shard_map/ppermute | solution.py:237
  61.3 1.5 %collective-permute-start.12 = (bf16[4,16,1152]{2,1,0:T(8,128)(2,1)S(1)}, bf16[4,16,1152]{2,1,0:T(8,128)(2,1)S(1)}, u32[]{:S(2)}, u32[]{:S(2)}) collective-permute-start(bf16[4,16,1152]{2,1,0:T(8,128)(2,1)S(1)} %get-tuple-element.54), channel_id=1, source_target_pairs={{0,4},{4,0},{8,12},{12,8},{16,20},{20,16},{24,28},{28,24},{1,5},{5... | collective-permute-start | bytes 442376 | tf_op jit(solution)/shard_map/ppermute | solution.py:237
  62.8 1.4 %collective-permute-start.22 = (bf16[16,1152]{1,0:T(8,128)(2,1)S(1)}, bf16[16,1152]{1,0:T(8,128)(2,1)S(1)}, u32[]{:S(2)}, u32[]{:S(2)}) collective-permute-start(bf16[16,1152]{1,0:T(8,128)(2,1)S(1)} %get-tuple-element.67), channel_id=1, source_target_pairs={{0,24},{4,28},{8,16},{12,20},{16,8},{20,12},{24,0},{28,4},{1,25},{... | collective-permute-start | bytes 110600 | tf_op jit(solution)/shard_map/ppermute | solution.py:237
  64.4 2.9 %collective-permute-start.24 = (bf16[16,1152]{1,0:T(8,128)(2,1)S(1)}, bf16[16,1152]{1,0:T(8,128)(2,1)S(1)}, u32[]{:S(2)}, u32[]{:S(2)}) collective-permute-start(bf16[16,1152]{1,0:T(8,128)(2,1)S(1)} %get-tuple-element.69), channel_id=1, source_target_pairs={{0,8},{4,12},{8,0},{12,4},{16,24},{20,28},{24,16},{28,20},{1,9},{5... | collective-permute-start | bytes 110600 | tf_op jit(solution)/shard_map/ppermute | solution.py:237
  67.4 1.3 %collective-permute-done.22.refs_0_ = bf16[16,1152]{1,0:T(8,128)(2,1)S(1)} collective-permute-done((bf16[16,1152]{1,0:T(8,128)(2,1)S(1)}, bf16[16,1152]{1,0:T(8,128)(2,1)S(1)}, u32[]{:S(2)}, u32[]{:S(2)}) %collective-permute-start.22) | collective-permute-done | bytes 36896 | tf_op jit(solution)/shard_map/ppermute | solution.py:237
  68.7 0.9 %collective-permute-done.23.refs_1_ = bf16[16,1152]{1,0:T(8,128)(2,1)S(1)} collective-permute-done((bf16[16,1152]{1,0:T(8,128)(2,1)S(1)}, bf16[16,1152]{1,0:T(8,128)(2,1)S(1)}, u32[]{:S(2)}, u32[]{:S(2)}) %collective-permute-start.23) | collective-permute-done | bytes 36896 | tf_op jit(solution)/shard_map/ppermute | solution.py:237
  69.6 0.8 %shard_map.77 = bf16[8,16,1152]{2,1,0:T(8,128)(2,1)} custom-call(f32[6,1152]{1,0:T(8,128)S(1)} %copy-done.7, bf16[4,16,1152]{2,1,0:T(8,128)(2,1)S(1)} %collective-permute-done.12.middle_ref, bf16[4,16,1152]{2,1,0:T(8,128)(2,1)S(1)} %shard_map.75.done_ref, bf16[16,1152]{1,0:T(8,128)(2,1)S(1)} %collective-permute-done.22.refs_0_, ...), custom_call_target="tpu_custom_call" | custom-call | flops 1 | bytes 1 | tf_op jit(solution)/shard_map/pallas_call | solution.py:224
  (48 shorter events, 4.7 us)
Async XLA Ops:
  0.0 3.0 %collective-permute-start = (bf16[1,128,1152]{2,1,0:T(8,128)(2,1)}, bf16[1,128,1152]{2,1,0:T(8,128)(2,1)S(1)}, u32[]{:S(2)}, u32[]{:S(2)}) collective-permute-start(bf16[1,128,1152]{2,1,0:T(8,128)(2,1)} %own_ref.1), channel_id=1, source_target_pairs={{0,1},{1,0},{2,3},{3,2},{4,5},{5,4},{6,7},{7,6},{8,9},{9,8},{10,11... | collective-permute-start | bytes 884744 | tf_op jit(solution)/shard_map/ppermute | solution.py:237
  0.5 10.4 %collective-permute-start.2 = (bf16[1,128,1152]{2,1,0:T(8,128)(2,1)}, bf16[1,128,1152]{2,1,0:T(8,128)(2,1)S(1)}, u32[]{:S(2)}, u32[]{:S(2)}) collective-permute-start(bf16[1,128,1152]{2,1,0:T(8,128)(2,1)} %own_ref.1), channel_id=1, source_target_pairs={{0,2},{1,3},{2,0},{3,1},{4,6},{5,7},{6,4},{7,5},{8,10},{9,11},{10,... | collective-permute-start | bytes 884744 | tf_op jit(solution)/shard_map/ppermute | solution.py:237
  3.0 1.0 %copy-start.5 = (bf16[1,128,1152]{2,1,0:T(8,128)(2,1)S(1)}, bf16[1,128,1152]{2,1,0:T(8,128)(2,1)}, u32[]{:S(2)}) copy-start(bf16[1,128,1152]{2,1,0:T(8,128)(2,1)} %own_ref.1) | copy-start | bytes 884740
  4.1 6.8 %collective-permute-start.1 = (bf16[64,1152]{1,0:T(8,128)(2,1)S(1)}, bf16[64,1152]{1,0:T(8,128)(2,1)S(1)}, u32[]{:S(2)}, u32[]{:S(2)}) collective-permute-start(bf16[64,1152]{1,0:T(8,128)(2,1)S(1)} %get-tuple-element.40), channel_id=1, source_target_pairs={{0,4},{4,0},{8,12},{12,8},{16,20},{20,16},{24,28},{28,24},{1,5},{5... | collective-permute-start | bytes 442376 | tf_op jit(solution)/shard_map/ppermute | solution.py:237
  5.8 1.6 %copy-start = (bf16[864,1152]{1,0:T(8,128)(2,1)S(1)}, bf16[864,1152]{1,0:T(8,128)(2,1)}, u32[]{:S(2)}) copy-start(bf16[864,1152]{1,0:T(8,128)(2,1)} %weight_ref.3) | copy-start | bytes 5971972
  8.2 4.4 %copy-start.4 = (bf16[288,1152]{1,0:T(8,128)(2,1)S(1)}, bf16[288,1152]{1,0:T(8,128)(2,1)}, u32[]{:S(2)}) copy-start(bf16[288,1152]{1,0:T(8,128)(2,1)} %refs_0_.4) | copy-start | bytes 1990660
  8.2 4.8 %copy-start.1 = (bf16[864,1152]{1,0:T(8,128)(2,1)S(1)}, bf16[864,1152]{1,0:T(8,128)(2,1)}, u32[]{:S(2)}) copy-start(bf16[864,1152]{1,0:T(8,128)(2,1)} %weight_ref.3) | copy-start | bytes 5971972
  9.3 9.2 %copy-start.3 = (bf16[288,1152]{1,0:T(8,128)(2,1)S(1)}, bf16[288,1152]{1,0:T(8,128)(2,1)}, u32[]{:S(2)}) copy-start(bf16[288,1152]{1,0:T(8,128)(2,1)} %refs_2_.5) | copy-start | bytes 1990660
  10.9 1.6 %collective-permute-start.3 = (bf16[1,128,1152]{2,1,0:T(8,128)(2,1)S(1)}, bf16[1,128,1152]{2,1,0:T(8,128)(2,1)S(1)}, u32[]{:S(2)}, u32[]{:S(2)}) collective-permute-start(bf16[1,128,1152]{2,1,0:T(8,128)(2,1)S(1)} %collective-permute-done.2.refs_0_), channel_id=1, source_target_pairs={{0,1},{1,0},{2,3},{3,2},{4,5},{5,4},{6,7},{7,6},{8,9},{9,8},{10,11... | collective-permute-start | bytes 884744 | tf_op jit(solution)/shard_map/ppermute | solution.py:237
  12.4 27.5 %collective-permute-start.13 = (bf16[864,1152]{1,0:T(8,128)(2,1)}, bf16[864,1152]{1,0:T(8,128)(2,1)S(1)}, u32[]{:S(2)}, u32[]{:S(2)}) collective-permute-start(bf16[864,1152]{1,0:T(8,128)(2,1)} %refs_0_.7), channel_id=1, source_target_pairs={{0,1},{1,0},{2,3},{3,2},{4,5},{5,4},{6,7},{7,6},{8,9},{9,8},{10,11... | collective-permute-start | bytes 5971976 | tf_op jit(solution)/shard_map/ppermute | solution.py:237
  12.6 5.2 %collective-permute-start.5 = (bf16[288,1152]{1,0:T(8,128)(2,1)S(1)}, bf16[288,1152]{1,0:T(8,128)(2,1)S(1)}, u32[]{:S(2)}, u32[]{:S(2)}) collective-permute-start(bf16[288,1152]{1,0:T(8,128)(2,1)S(1)} %copy-done.4), channel_id=1, source_target_pairs={{0,1},{1,0},{2,3},{3,2},{4,5},{5,4},{6,7},{7,6},{8,9},{9,8},{10,11... | collective-permute-start | bytes 1990664 | tf_op jit(solution)/shard_map/ppermute | solution.py:237
  16.3 11.9 %copy-start.7 = (f32[6,1152]{1,0:T(8,128)S(1)}, f32[6,1152]{1,0:T(8,128)}, u32[]{:S(2)}) copy-start(f32[6,1152]{1,0:T(8,128)} %mod_ref.9) | copy-start | bytes 82948
  16.3 1.4 %collective-permute-start.4 = (bf16[288,256]{1,0:T(8,128)(2,1)S(1)}, bf16[288,256]{1,0:T(8,128)(2,1)S(1)}, u32[]{:S(2)}, u32[]{:S(2)}) collective-permute-start(bf16[288,256]{1,0:T(8,128)(2,1)S(1)} %get-tuple-element.43), channel_id=1, source_target_pairs={{0,1},{1,0},{2,3},{3,2},{4,5},{5,4},{6,7},{7,6},{8,9},{9,8},{10,11... | collective-permute-start | bytes 442376 | tf_op jit(solution)/shard_map/ppermute | solution.py:237
  18.5 21.5 %copy-start.2 = (bf16[864,1152]{1,0:T(8,128)(2,1)S(1)}, bf16[864,1152]{1,0:T(8,128)(2,1)}, u32[]{:S(2)}) copy-start(bf16[864,1152]{1,0:T(8,128)(2,1)} %refs_0_.7) | copy-start | bytes 5971972
  18.5 21.4 %collective-permute-start.14 = (bf16[288,1152]{1,0:T(8,128)(2,1)S(1)}, bf16[288,1152]{1,0:T(8,128)(2,1)S(1)}, u32[]{:S(2)}, u32[]{:S(2)}) collective-permute-start(bf16[288,1152]{1,0:T(8,128)(2,1)S(1)} %copy-done.3), channel_id=1, source_target_pairs={{0,1},{1,0},{2,3},{3,2},{4,5},{5,4},{6,7},{7,6},{8,9},{9,8},{10,11... | collective-permute-start | bytes 1990664 | tf_op jit(solution)/shard_map/ppermute | solution.py:237
  18.7 9.5 %collective-permute-start.6 = (bf16[64,1152]{1,0:T(8,128)(2,1)S(1)}, bf16[64,1152]{1,0:T(8,128)(2,1)S(1)}, u32[]{:S(2)}, u32[]{:S(2)}) collective-permute-start(bf16[64,1152]{1,0:T(8,128)(2,1)S(1)} %get-tuple-element.46), channel_id=1, source_target_pairs={{0,2},{1,3},{2,0},{3,1},{4,6},{5,7},{6,4},{7,5},{8,10},{9,11},{10,... | collective-permute-start | bytes 442376 | tf_op jit(solution)/shard_map/ppermute | solution.py:237
  20.5 7.8 %collective-permute-start.8 = (bf16[64,1152]{1,0:T(8,128)(2,1)S(1)}, bf16[64,1152]{1,0:T(8,128)(2,1)S(1)}, u32[]{:S(2)}, u32[]{:S(2)}) collective-permute-start(bf16[64,1152]{1,0:T(8,128)(2,1)S(1)} %get-tuple-element.48), channel_id=1, source_target_pairs={{0,6},{1,7},{2,4},{3,5},{4,2},{5,3},{6,0},{7,1},{8,14},{9,15},{10,... | collective-permute-start | bytes 442376 | tf_op jit(solution)/shard_map/ppermute | solution.py:260
  21.9 5.9 %collective-permute-start.7 = (bf16[64,576]{1,0:T(8,128)(2,1)S(1)}, bf16[64,576]{1,0:T(8,128)(2,1)S(1)}, u32[]{:S(2)}, u32[]{:S(2)}) collective-permute-start(bf16[64,576]{1,0:T(8,128)(2,1)S(1)} %get-tuple-element.47), channel_id=1, source_target_pairs={{0,4},{4,0},{8,12},{12,8},{16,20},{20,16},{24,28},{28,24},{1,5},{5... | collective-permute-start | bytes 221192 | tf_op jit(solution)/shard_map/ppermute | solution.py:237
  28.6 7.0 %collective-permute-start.9 = (bf16[32,1152]{1,0:T(8,128)(2,1)S(1)}, bf16[32,1152]{1,0:T(8,128)(2,1)S(1)}, u32[]{:S(2)}, u32[]{:S(2)}) collective-permute-start(bf16[32,1152]{1,0:T(8,128)(2,1)S(1)} %get-tuple-element.50), channel_id=1, source_target_pairs={{0,24},{4,28},{8,16},{12,20},{16,8},{20,12},{24,0},{28,4},{1,25},{... | collective-permute-start | bytes 221192 | tf_op jit(solution)/shard_map/ppermute | solution.py:237
  32.5 5.8 %collective-permute-start.10 = (bf16[32,1152]{1,0:T(8,128)(2,1)S(1)}, bf16[32,1152]{1,0:T(8,128)(2,1)S(1)}, u32[]{:S(2)}, u32[]{:S(2)}) collective-permute-start(bf16[32,1152]{1,0:T(8,128)(2,1)S(1)} %get-tuple-element.51), channel_id=1, source_target_pairs={{0,16},{4,20},{8,24},{12,28},{16,0},{20,4},{24,8},{28,12},{1,17},{... | collective-permute-start | bytes 221192 | tf_op jit(solution)/shard_map/ppermute | solution.py:237
  32.5 5.8 %collective-permute-start.11 = (bf16[32,1152]{1,0:T(8,128)(2,1)S(1)}, bf16[32,1152]{1,0:T(8,128)(2,1)S(1)}, u32[]{:S(2)}, u32[]{:S(2)}) collective-permute-start(bf16[32,1152]{1,0:T(8,128)(2,1)S(1)} %get-tuple-element.52), channel_id=1, source_target_pairs={{0,8},{4,12},{8,0},{12,4},{16,24},{20,28},{24,16},{28,20},{1,9},{5... | collective-permute-start | bytes 221192 | tf_op jit(solution)/shard_map/ppermute | solution.py:237
  38.3 8.4 %collective-permute-start.15 = (bf16[128,1152]{1,0:T(8,128)(2,1)S(1)}, bf16[128,1152]{1,0:T(8,128)(2,1)S(1)}, u32[]{:S(2)}, u32[]{:S(2)}) collective-permute-start(bf16[128,1152]{1,0:T(8,128)(2,1)S(1)} %shard_map.70.refs_4_), channel_id=1, source_target_pairs={{0,2},{1,3},{2,0},{3,1},{4,6},{5,7},{6,4},{7,5},{8,10},{9,11},{10,... | collective-permute-start | bytes 884744 | tf_op jit(solution)/shard_map/ppermute | solution.py:237
  41.9 4.5 %collective-permute-start.16 = (bf16[64,576]{1,0:T(8,128)(2,1)S(1)}, bf16[64,576]{1,0:T(8,128)(2,1)S(1)}, u32[]{:S(2)}, u32[]{:S(2)}) collective-permute-start(bf16[64,576]{1,0:T(8,128)(2,1)S(1)} %get-tuple-element.59), channel_id=1, source_target_pairs={{0,4},{4,0},{8,12},{12,8},{16,20},{20,16},{24,28},{28,24},{1,5},{5... | collective-permute-start | bytes 221192 | tf_op jit(solution)/shard_map/ppermute | solution.py:237
  48.7 8.1 %collective-permute-start.17 = (bf16[64,1152]{1,0:T(8,128)(2,1)S(1)}, bf16[64,1152]{1,0:T(8,128)(2,1)S(1)}, u32[]{:S(2)}, u32[]{:S(2)}) collective-permute-start(bf16[64,1152]{1,0:T(8,128)(2,1)S(1)} %get-tuple-element.61), channel_id=1, source_target_pairs={{0,2},{1,3},{2,0},{3,1},{4,6},{5,7},{6,4},{7,5},{8,10},{9,11},{10,... | collective-permute-start | bytes 442376 | tf_op jit(solution)/shard_map/ppermute | solution.py:237
  50.3 12.5 %collective-permute-start.21 = (bf16[64,1152]{1,0:T(8,128)(2,1)S(1)}, bf16[64,1152]{1,0:T(8,128)(2,1)S(1)}, u32[]{:S(2)}, u32[]{:S(2)}) collective-permute-start(bf16[64,1152]{1,0:T(8,128)(2,1)S(1)} %get-tuple-element.66), channel_id=1, source_target_pairs={{0,6},{1,7},{2,4},{3,5},{4,2},{5,3},{6,0},{7,1},{8,14},{9,15},{10,... | collective-permute-start | bytes 442376 | tf_op jit(solution)/shard_map/ppermute | solution.py:260
  56.9 7.3 %collective-permute-start.18 = (bf16[16,1152]{1,0:T(8,128)(2,1)S(1)}, bf16[16,1152]{1,0:T(8,128)(2,1)S(1)}, u32[]{:S(2)}, u32[]{:S(2)}) collective-permute-start(bf16[16,1152]{1,0:T(8,128)(2,1)S(1)} %get-tuple-element.62), channel_id=1, source_target_pairs={{0,24},{4,28},{8,16},{12,20},{16,8},{20,12},{24,0},{28,4},{1,25},{... | collective-permute-start | bytes 110600 | tf_op jit(solution)/shard_map/ppermute | solution.py:237
  58.2 6.1 %collective-permute-start.19 = (bf16[16,1152]{1,0:T(8,128)(2,1)S(1)}, bf16[16,1152]{1,0:T(8,128)(2,1)S(1)}, u32[]{:S(2)}, u32[]{:S(2)}) collective-permute-start(bf16[16,1152]{1,0:T(8,128)(2,1)S(1)} %get-tuple-element.63), channel_id=1, source_target_pairs={{0,16},{4,20},{8,24},{12,28},{16,0},{20,4},{24,8},{28,12},{1,17},{... | collective-permute-start | bytes 110600 | tf_op jit(solution)/shard_map/ppermute | solution.py:237
  58.2 9.1 %collective-permute-start.20 = (bf16[16,1152]{1,0:T(8,128)(2,1)S(1)}, bf16[16,1152]{1,0:T(8,128)(2,1)S(1)}, u32[]{:S(2)}, u32[]{:S(2)}) collective-permute-start(bf16[16,1152]{1,0:T(8,128)(2,1)S(1)} %get-tuple-element.64), channel_id=1, source_target_pairs={{0,8},{4,12},{8,0},{12,4},{16,24},{20,28},{24,16},{28,20},{1,9},{5... | collective-permute-start | bytes 110600 | tf_op jit(solution)/shard_map/ppermute | solution.py:237
  61.3 6.0 %collective-permute-start.12 = (bf16[4,16,1152]{2,1,0:T(8,128)(2,1)S(1)}, bf16[4,16,1152]{2,1,0:T(8,128)(2,1)S(1)}, u32[]{:S(2)}, u32[]{:S(2)}) collective-permute-start(bf16[4,16,1152]{2,1,0:T(8,128)(2,1)S(1)} %get-tuple-element.54), channel_id=1, source_target_pairs={{0,4},{4,0},{8,12},{12,8},{16,20},{20,16},{24,28},{28,24},{1,5},{5... | collective-permute-start | bytes 442376 | tf_op jit(solution)/shard_map/ppermute | solution.py:237
  62.8 5.8 %collective-permute-start.22 = (bf16[16,1152]{1,0:T(8,128)(2,1)S(1)}, bf16[16,1152]{1,0:T(8,128)(2,1)S(1)}, u32[]{:S(2)}, u32[]{:S(2)}) collective-permute-start(bf16[16,1152]{1,0:T(8,128)(2,1)S(1)} %get-tuple-element.67), channel_id=1, source_target_pairs={{0,24},{4,28},{8,16},{12,20},{16,8},{20,12},{24,0},{28,4},{1,25},{... | collective-permute-start | bytes 110600 | tf_op jit(solution)/shard_map/ppermute | solution.py:237
  64.2 5.3 %collective-permute-start.23 = (bf16[16,1152]{1,0:T(8,128)(2,1)S(1)}, bf16[16,1152]{1,0:T(8,128)(2,1)S(1)}, u32[]{:S(2)}, u32[]{:S(2)}) collective-permute-start(bf16[16,1152]{1,0:T(8,128)(2,1)S(1)} %get-tuple-element.68), channel_id=1, source_target_pairs={{0,16},{4,20},{8,24},{12,28},{16,0},{20,4},{24,8},{28,12},{1,17},{... | collective-permute-start | bytes 110600 | tf_op jit(solution)/shard_map/ppermute | solution.py:237
  64.4 5.2 %collective-permute-start.24 = (bf16[16,1152]{1,0:T(8,128)(2,1)S(1)}, bf16[16,1152]{1,0:T(8,128)(2,1)S(1)}, u32[]{:S(2)}, u32[]{:S(2)}) collective-permute-start(bf16[16,1152]{1,0:T(8,128)(2,1)S(1)} %get-tuple-element.69), channel_id=1, source_target_pairs={{0,8},{4,12},{8,0},{12,4},{16,24},{20,28},{24,16},{28,20},{1,9},{5... | collective-permute-start | bytes 110600 | tf_op jit(solution)/shard_map/ppermute | solution.py:237
  (1 other events, 0.8 us)

commit v19 on v17

--- a/solution.py
+++ b/solution.py
@@ -291,8 +291,8 @@
         return call(paired_kernel, (heads, *weights), [halves_shape(F32)])[0]
 
     def return_updates(own, far):
+        diagonal = [swap_diagonal(part, 2 * at) for at, part in enumerate(far[1::2], 1)]
         same = [swap(part, "patch", 2 * at) for at, part in enumerate(far[::2], 1)]
-        diagonal = [swap_diagonal(part, 2 * at) for at, part in enumerate(far[1::2], 1)]
         return [own[0], *same, own[1], *diagonal]
 
     def halves_shape(dtype):
@@ -315,7 +315,6 @@
     paired = swap(shared, "frame", 1)
     out_pair = with_sister(spatial_out, near)
     far = both_cores([after(block, near, paired) for block in far])
-    temporal_pair = with_sister(temporal_qkv, *far)
 
     columns = (groups - 1) * rows
     far_proj, kept, sent = call(
@@ -329,6 +328,7 @@
         (kept, swap(sent, "patch", 1), *out_pair),
         far_shapes,
     )
+    temporal_pair = with_sister(temporal_qkv, far_parts[0])
     kept, sent = call(
         near_queries_kernel,
         (after(near, far_parts[0]), far_proj),

time: 67 us -> 69.3 us (1.034)
  waiting for transfers between devices: 28.1 us -> 30.5 us
    ppermute x21, waiting for transfers between devices: 26.4 us -> 28.8 us  [swap(): return lax.ppermute(value, axis, [(at, at ^ offset) for at in range(size)])]
  transfers between devices with their start and end apart: 23 -> 23, of which waited for: 15 -> 16; matrix products, arithmetic and copies ran while one was open for 0% -> 0% of each run, Pallas kernels for 13% -> 12%
where the time goes in v19:
time: 69.3 us; the launch traced here: 69.1 us
  waiting for transfers between devices  30.5 us (44%)
  starting transfers between devices  23.4 us (34%)
  Pallas kernels  11.7 us (17%)
  local copies, waits for them, and re-layouts  3.31 us (5%)
    ppermute x21, waiting for transfers between devices, swap(): return lax.ppermute(value, axis, [(at, at ^ offset) for at in range(size)])  28.8 us
    ppermute x21, starting transfers between devices, swap(): return lax.ppermute(value, axis, [(at, at ^ offset) for at in range(size)])  19.4 us
    pallas_call x15, Pallas kernels, call(): pl.pallas_call(body, out_shape=outs, in_specs=[pl.BlockSpec(memory_space=...  11.7 us
    ppermute x2, starting transfers between devices, swap_diagonal(): return lax.ppermute(value, ('frame', 'patch'), pairs)  3.94 us
    unnamed x16, local copies, waits for them, and re-layouts  3.31 us
    ppermute x2, waiting for transfers between devices, swap_diagonal(): return lax.ppermute(value, ('frame', 'patch'), pairs)  1.68 us
  transfers between devices with their start and end apart: 23, of which 16 were waited for; matrix products, arithmetic and copies ran while one was open for 0% of the time, Pallas kernels for 12%

profile of v19, /device:TPU:0, one launch (start us, length us, event | category | flops | bytes accessed | tf_op | source)
XLA Modules:
  0.0 69.1 jit_solution(2041394362657658857)
XLA Ops:
  0.5 2.5 %collective-permute-start.2 = (bf16[1,128,1152]{2,1,0:T(8,128)(2,1)}, bf16[1,128,1152]{2,1,0:T(8,128)(2,1)S(1)}, u32[]{:S(2)}, u32[]{:S(2)}) collective-permute-start(bf16[1,128,1152]{2,1,0:T(8,128)(2,1)} %own_ref.1), channel_id=1, source_target_pairs={{0,2},{1,3},{2,0},{3,1},{4,6},{5,7},{6,4},{7,5},{8,10},{9,11},{10,... | collective-permute-start | bytes 884744 | tf_op jit(solution)/shard_map/ppermute | solution.py:248
  3.0 1.6 %copy-done = bf16[864,1152]{1,0:T(8,128)(2,1)S(1)} copy-done((bf16[864,1152]{1,0:T(8,128)(2,1)S(1)}, bf16[864,1152]{1,0:T(8,128)(2,1)}, u32[]{:S(2)}) %copy-start) | copy-done | bytes 1990680
  4.5 1.0 %copy-done.5 = bf16[1,128,1152]{2,1,0:T(8,128)(2,1)S(1)} copy-done((bf16[1,128,1152]{2,1,0:T(8,128)(2,1)S(1)}, bf16[1,128,1152]{2,1,0:T(8,128)(2,1)}, u32[]{:S(2)}) %copy-start.5) | copy-done | bytes 294936
  5.5 0.8 %copy-done.6 = f32[6,1152]{1,0:T(8,128)S(1)} copy-done((f32[6,1152]{1,0:T(8,128)S(1)}, f32[6,1152]{1,0:T(8,128)}, u32[]{:S(2)}) %copy-start.6) | copy-done | bytes 27672
  6.3 1.1 %shard_map.65.near_ref = f32[864,256]{1,0:T(8,128)S(1)} custom-call(f32[6,1152]{1,0:T(8,128)S(1)} %copy-done.6, bf16[864,1152]{1,0:T(8,128)(2,1)S(1)} %copy-done, bf16[1,128,1152]{2,1,0:T(8,128)(2,1)S(1)} %copy-done.5, bf16[1,128,1152]{2,1,0:T(8,128)(2,1)S(1)} %collective-permute-done.sister_ref), custom_call_target="tpu_custom_call" | custom-call | flops 1 | bytes 1 | tf_op jit(solution)/shard_map/pallas_call | solution.py:235
  7.8 1.7 %collective-permute-start.1 = (bf16[64,1152]{1,0:T(8,128)(2,1)S(1)}, bf16[64,1152]{1,0:T(8,128)(2,1)S(1)}, u32[]{:S(2)}, u32[]{:S(2)}) collective-permute-start(bf16[64,1152]{1,0:T(8,128)(2,1)S(1)} %get-tuple-element.42), channel_id=1, source_target_pairs={{0,4},{4,0},{8,12},{12,8},{16,20},{20,16},{24,28},{28,24},{1,5},{5... | collective-permute-start | bytes 442376 | tf_op jit(solution)/shard_map/ppermute | solution.py:248
  9.5 1.3 %collective-permute-done.2.refs_0_ = bf16[1,128,1152]{2,1,0:T(8,128)(2,1)S(1)} collective-permute-done((bf16[1,128,1152]{2,1,0:T(8,128)(2,1)}, bf16[1,128,1152]{2,1,0:T(8,128)(2,1)S(1)}, u32[]{:S(2)}, u32[]{:S(2)}) %collective-permute-start.2) | collective-permute-done | bytes 294944 | tf_op jit(solution)/shard_map/ppermute | solution.py:248
  10.9 3.0 %collective-permute-done.1.paired_ref = bf16[64,1152]{1,0:T(8,128)(2,1)S(1)} collective-permute-done((bf16[64,1152]{1,0:T(8,128)(2,1)S(1)}, bf16[64,1152]{1,0:T(8,128)(2,1)S(1)}, u32[]{:S(2)}, u32[]{:S(2)}) %collective-permute-start.1) | collective-permute-done | bytes 147488 | tf_op jit(solution)/shard_map/ppermute | solution.py:248
  13.9 1.6 %collective-permute-done.3.refs_1_ = bf16[1,128,1152]{2,1,0:T(8,128)(2,1)S(1)} collective-permute-done((bf16[1,128,1152]{2,1,0:T(8,128)(2,1)S(1)}, bf16[1,128,1152]{2,1,0:T(8,128)(2,1)S(1)}, u32[]{:S(2)}, u32[]{:S(2)}) %collective-permute-start.3) | collective-permute-done | bytes 294944 | tf_op jit(solution)/shard_map/ppermute | solution.py:248
  15.5 2.6 %shard_map.66 = (f32[864,256]{1,0:T(8,128)S(1)}, bf16[288,128]{1,0:T(8,128)(2,1)S(1)}, bf16[288,128]{1,0:T(8,128)(2,1)S(1)}) custom-call(f32[6,1152]{1,0:T(8,128)S(1)} %copy-done.7, bf16[864,1152]{1,0:T(8,128)(2,1)S(1)} %copy-done.1, f32[864,256]{1,0:T(8,128)S(1)} %shard_map.65.near_ref, bf16[1,128,1152]{2,1,0:T(8,128)(2,1)S(1)} %collective-permute-done.2.refs_0_, ...), custom_call_target="tpu_custom_call" | custom-call | flops 1 | bytes 1 | tf_op jit(solution)/shard_map/pallas_call | solution.py:235
  18.3 1.1 %collective-permute-done.4.refs_1_ = bf16[288,128]{1,0:T(8,128)(2,1)S(1)} collective-permute-done((bf16[288,128]{1,0:T(8,128)(2,1)S(1)}, bf16[288,128]{1,0:T(8,128)(2,1)S(1)}, u32[]{:S(2)}, u32[]{:S(2)}) %collective-permute-start.4) | collective-permute-done | bytes 73760 | tf_op jit(solution)/shard_map/ppermute | solution.py:248
  20.1 2.7 %collective-permute-start.8 = (bf16[64,1152]{1,0:T(8,128)(2,1)S(1)}, bf16[64,1152]{1,0:T(8,128)(2,1)S(1)}, u32[]{:S(2)}, u32[]{:S(2)}) collective-permute-start(bf16[64,1152]{1,0:T(8,128)(2,1)S(1)} %get-tuple-element.53), channel_id=1, source_target_pairs={{0,6},{1,7},{2,4},{3,5},{4,2},{5,3},{6,0},{7,1},{8,14},{9,15},{10,... | collective-permute-start | bytes 442376 | tf_op jit(solution)/shard_map/ppermute | solution.py:271
  23.3 1.2 %shard_map.68 = (bf16[288,128]{1,0:T(8,128)(2,1)S(1)}, bf16[288,128]{1,0:T(8,128)(2,1)S(1)}) custom-call(f32[864,256]{1,0:T(8,128)S(1)} %shard_map.65.near_ref, f32[864,256]{1,0:T(8,128)S(1)} %get-tuple-element.49.far_ref), custom_call_target="tpu_custom_call" | custom-call | flops 1 | bytes 1 | tf_op jit(solution)/shard_map/pallas_call | solution.py:235
  24.5 1.3 %collective-permute-done.6.refs_1_ = bf16[288,128]{1,0:T(8,128)(2,1)S(1)} collective-permute-done((bf16[288,128]{1,0:T(8,128)(2,1)S(1)}, bf16[288,128]{1,0:T(8,128)(2,1)S(1)}, u32[]{:S(2)}, u32[]{:S(2)}) %collective-permute-start.6) | collective-permute-done | bytes 73760 | tf_op jit(solution)/shard_map/ppermute | solution.py:248
  27.3 3.1 %collective-permute-done.7.refs_0_ = bf16[64,1152]{1,0:T(8,128)(2,1)S(1)} collective-permute-done((bf16[64,1152]{1,0:T(8,128)(2,1)S(1)}, bf16[64,1152]{1,0:T(8,128)(2,1)S(1)}, u32[]{:S(2)}, u32[]{:S(2)}) %collective-permute-start.7) | collective-permute-done | bytes 147488 | tf_op jit(solution)/shard_map/ppermute | solution.py:248
  31.5 3.7 %collective-permute-start.10 = (bf16[32,1152]{1,0:T(8,128)(2,1)S(1)}, bf16[32,1152]{1,0:T(8,128)(2,1)S(1)}, u32[]{:S(2)}, u32[]{:S(2)}) collective-permute-start(bf16[32,1152]{1,0:T(8,128)(2,1)S(1)} %get-tuple-element.59), channel_id=1, source_target_pairs={{0,24},{4,28},{8,16},{12,20},{16,8},{20,12},{24,0},{28,4},{1,25},{... | collective-permute-start | bytes 221192 | tf_op jit(solution)/shard_map/ppermute | solution.py:248
  35.2 0.8 %collective-permute-start.12 = (bf16[32,1152]{1,0:T(8,128)(2,1)S(1)}, bf16[32,1152]{1,0:T(8,128)(2,1)S(1)}, u32[]{:S(2)}, u32[]{:S(2)}) collective-permute-start(bf16[32,1152]{1,0:T(8,128)(2,1)S(1)} %get-tuple-element.61), channel_id=1, source_target_pairs={{0,8},{4,12},{8,0},{12,4},{16,24},{20,28},{24,16},{28,20},{1,9},{5... | collective-permute-start | bytes 221192 | tf_op jit(solution)/shard_map/ppermute | solution.py:248
  36.0 2.3 %collective-permute-done.10.refs_0_ = bf16[32,1152]{1,0:T(8,128)(2,1)S(1)} collective-permute-done((bf16[32,1152]{1,0:T(8,128)(2,1)S(1)}, bf16[32,1152]{1,0:T(8,128)(2,1)S(1)}, u32[]{:S(2)}, u32[]{:S(2)}) %collective-permute-start.10) | collective-permute-done | bytes 73760 | tf_op jit(solution)/shard_map/ppermute | solution.py:248
  38.3 3.1 %collective-permute-done.11.refs_1_ = bf16[32,1152]{1,0:T(8,128)(2,1)S(1)} collective-permute-done((bf16[32,1152]{1,0:T(8,128)(2,1)S(1)}, bf16[32,1152]{1,0:T(8,128)(2,1)S(1)}, u32[]{:S(2)}, u32[]{:S(2)}) %collective-permute-start.11) | collective-permute-done | bytes 73760 | tf_op jit(solution)/shard_map/ppermute | solution.py:248
  41.4 1.6 %collective-permute-start.16 = (bf16[128,1152]{1,0:T(8,128)(2,1)S(1)}, bf16[128,1152]{1,0:T(8,128)(2,1)S(1)}, u32[]{:S(2)}, u32[]{:S(2)}) collective-permute-start(bf16[128,1152]{1,0:T(8,128)(2,1)S(1)} %shard_map.73.refs_4_), channel_id=1, source_target_pairs={{0,2},{1,3},{2,0},{3,1},{4,6},{5,7},{6,4},{7,5},{8,10},{9,11},{10,... | collective-permute-start | bytes 884744 | tf_op jit(solution)/shard_map/ppermute | solution.py:248
  43.0 1.9 %shard_map.74 = (f32[64,1152]{1,0:T(8,128)S(1)}, bf16[64,576]{1,0:T(8,128)(2,1)S(1)}) custom-call(bf16[864,1152]{1,0:T(8,128)(2,1)S(1)} %copy-done.2, bf16[864,1152]{1,0:T(8,128)(2,1)S(1)} %collective-permute-done.14.refs_1_, bf16[288,1152]{1,0:T(8,128)(2,1)S(1)} %copy-done.4, bf16[288,1152]{1,0:T(8,128)(2,1)S(1)} %collective-permute-done.15.refs_3_.refs_1_, ...), custom_call_target="tpu_custom_call" | custom-call | flops 1 | bytes 1 | tf_op jit(solution)/shard_map/pallas_call | solution.py:235
  45.2 4.2 %collective-permute-done.17.head_ref = bf16[64,576]{1,0:T(8,128)(2,1)S(1)} collective-permute-done((bf16[64,576]{1,0:T(8,128)(2,1)S(1)}, bf16[64,576]{1,0:T(8,128)(2,1)S(1)}, u32[]{:S(2)}, u32[]{:S(2)}) %collective-permute-start.17) | collective-permute-done | bytes 73760 | tf_op jit(solution)/shard_map/ppermute | solution.py:248
  50.1 2.0 %shard_map.76 = (bf16[64,1152]{1,0:T(8,128)(2,1)S(1)}, bf16[64,1152]{1,0:T(8,128)(2,1)S(1)}) custom-call(bf16[864,1152]{1,0:T(8,128)(2,1)S(1)} %copy-done.2, bf16[864,1152]{1,0:T(8,128)(2,1)S(1)} %collective-permute-done.14.refs_1_, bf16[288,1152]{1,0:T(8,128)(2,1)S(1)} %copy-done.4, bf16[288,1152]{1,0:T(8,128)(2,1)S(1)} %collective-permute-done.15.refs_3_.refs_1_, ...), custom_call_target="tpu_custom_call" | custom-call | flops 1 | bytes 1 | tf_op jit(solution)/shard_map/pallas_call | solution.py:235
  52.1 1.6 %collective-permute-start.18 = (bf16[64,1152]{1,0:T(8,128)(2,1)S(1)}, bf16[64,1152]{1,0:T(8,128)(2,1)S(1)}, u32[]{:S(2)}, u32[]{:S(2)}) collective-permute-start(bf16[64,1152]{1,0:T(8,128)(2,1)S(1)} %get-tuple-element.69), channel_id=1, source_target_pairs={{0,2},{1,3},{2,0},{3,1},{4,6},{5,7},{6,4},{7,5},{8,10},{9,11},{10,... | collective-permute-start | bytes 442376 | tf_op jit(solution)/shard_map/ppermute | solution.py:248
  53.6 1.2 %collective-permute-start.19 = (bf16[64,1152]{1,0:T(8,128)(2,1)S(1)}, bf16[64,1152]{1,0:T(8,128)(2,1)S(1)}, u32[]{:S(2)}, u32[]{:S(2)}) collective-permute-start(bf16[64,1152]{1,0:T(8,128)(2,1)S(1)} %get-tuple-element.70), channel_id=1, source_target_pairs={{0,6},{1,7},{2,4},{3,5},{4,2},{5,3},{6,0},{7,1},{8,14},{9,15},{10,... | collective-permute-start | bytes 442376 | tf_op jit(solution)/shard_map/ppermute | solution.py:271
  55.6 3.8 %collective-permute-done.18.refs_1_ = bf16[64,1152]{1,0:T(8,128)(2,1)S(1)} collective-permute-done((bf16[64,1152]{1,0:T(8,128)(2,1)S(1)}, bf16[64,1152]{1,0:T(8,128)(2,1)S(1)}, u32[]{:S(2)}, u32[]{:S(2)}) %collective-permute-start.18) | collective-permute-done | bytes 147488 | tf_op jit(solution)/shard_map/ppermute | solution.py:248
  59.4 1.0 %collective-permute-done.19.refs_3_ = bf16[64,1152]{1,0:T(8,128)(2,1)S(1)} collective-permute-done((bf16[64,1152]{1,0:T(8,128)(2,1)S(1)}, bf16[64,1152]{1,0:T(8,128)(2,1)S(1)}, u32[]{:S(2)}, u32[]{:S(2)}) %collective-permute-start.19) | collective-permute-done | bytes 147488 | tf_op jit(solution)/shard_map/ppermute | solution.py:271
  60.4 1.0 %collective-permute-start.20 = (bf16[32,1152]{1,0:T(8,128)(2,1)S(1)}, bf16[32,1152]{1,0:T(8,128)(2,1)S(1)}, u32[]{:S(2)}, u32[]{:S(2)}) collective-permute-start(bf16[32,1152]{1,0:T(8,128)(2,1)S(1)} %get-tuple-element.71), channel_id=1, source_target_pairs={{0,24},{4,28},{8,16},{12,20},{16,8},{20,12},{24,0},{28,4},{1,25},{... | collective-permute-start | bytes 221192 | tf_op jit(solution)/shard_map/ppermute | solution.py:248
  61.5 3.4 %collective-permute-start.22 = (bf16[32,1152]{1,0:T(8,128)(2,1)S(1)}, bf16[32,1152]{1,0:T(8,128)(2,1)S(1)}, u32[]{:S(2)}, u32[]{:S(2)}) collective-permute-start(bf16[32,1152]{1,0:T(8,128)(2,1)S(1)} %get-tuple-element.73), channel_id=1, source_target_pairs={{0,8},{4,12},{8,0},{12,4},{16,24},{20,28},{24,16},{28,20},{1,9},{5... | collective-permute-start | bytes 221192 | tf_op jit(solution)/shard_map/ppermute | solution.py:248
  64.9 1.9 %collective-permute-done.20.refs_0_ = bf16[32,1152]{1,0:T(8,128)(2,1)S(1)} collective-permute-done((bf16[32,1152]{1,0:T(8,128)(2,1)S(1)}, bf16[32,1152]{1,0:T(8,128)(2,1)S(1)}, u32[]{:S(2)}, u32[]{:S(2)}) %collective-permute-start.20) | collective-permute-done | bytes 73760 | tf_op jit(solution)/shard_map/ppermute | solution.py:248
  66.7 1.5 %collective-permute-done.21.refs_1_ = bf16[32,1152]{1,0:T(8,128)(2,1)S(1)} collective-permute-done((bf16[32,1152]{1,0:T(8,128)(2,1)S(1)}, bf16[32,1152]{1,0:T(8,128)(2,1)S(1)}, u32[]{:S(2)}, u32[]{:S(2)}) %collective-permute-start.21) | collective-permute-done | bytes 73760 | tf_op jit(solution)/shard_map/ppermute | solution.py:248
  68.2 0.8 %shard_map.78 = bf16[8,16,1152]{2,1,0:T(8,128)(2,1)} custom-call(f32[6,1152]{1,0:T(8,128)S(1)} %copy-done.7, bf16[4,16,1152]{2,1,0:T(8,128)(2,1)S(1)} %get-tuple-element.57.kept_ref, bf16[4,16,1152]{2,1,0:T(8,128)(2,1)S(1)} %collective-permute-done.13.other_ref, bf16[32,1152]{1,0:T(8,128)(2,1)S(1)} %collective-permute-done.20.refs_0_, ...), custom_call_target="tpu_custom_call" | custom-call | flops 1 | bytes 1 | tf_op jit(solution)/shard_map/pallas_call | solution.py:235
  (45 shorter events, 6.7 us)
Async XLA Ops:
  0.0 3.0 %collective-permute-start = (bf16[1,128,1152]{2,1,0:T(8,128)(2,1)}, bf16[1,128,1152]{2,1,0:T(8,128)(2,1)S(1)}, u32[]{:S(2)}, u32[]{:S(2)}) collective-permute-start(bf16[1,128,1152]{2,1,0:T(8,128)(2,1)} %own_ref.1), channel_id=1, source_target_pairs={{0,1},{1,0},{2,3},{3,2},{4,5},{5,4},{6,7},{7,6},{8,9},{9,8},{10,11... | collective-permute-start | bytes 884744 | tf_op jit(solution)/shard_map/ppermute | solution.py:248
  0.5 10.4 %collective-permute-start.2 = (bf16[1,128,1152]{2,1,0:T(8,128)(2,1)}, bf16[1,128,1152]{2,1,0:T(8,128)(2,1)S(1)}, u32[]{:S(2)}, u32[]{:S(2)}) collective-permute-start(bf16[1,128,1152]{2,1,0:T(8,128)(2,1)} %own_ref.1), channel_id=1, source_target_pairs={{0,2},{1,3},{2,0},{3,1},{4,6},{5,7},{6,4},{7,5},{8,10},{9,11},{10,... | collective-permute-start | bytes 884744 | tf_op jit(solution)/shard_map/ppermute | solution.py:248
  3.0 1.6 %copy-start = (bf16[864,1152]{1,0:T(8,128)(2,1)S(1)}, bf16[864,1152]{1,0:T(8,128)(2,1)}, u32[]{:S(2)}) copy-start(bf16[864,1152]{1,0:T(8,128)(2,1)} %weight_ref.3) | copy-start | bytes 5971972
  4.5 1.0 %copy-start.5 = (bf16[1,128,1152]{2,1,0:T(8,128)(2,1)S(1)}, bf16[1,128,1152]{2,1,0:T(8,128)(2,1)}, u32[]{:S(2)}) copy-start(bf16[1,128,1152]{2,1,0:T(8,128)(2,1)} %own_ref.1) | copy-start | bytes 884740
  5.5 0.8 %copy-start.6 = (f32[6,1152]{1,0:T(8,128)S(1)}, f32[6,1152]{1,0:T(8,128)}, u32[]{:S(2)}) copy-start(f32[6,1152]{1,0:T(8,128)} %mod_ref.7) | copy-start | bytes 82948
  6.3 1.1 %copy-start.3 = (bf16[288,1152]{1,0:T(8,128)(2,1)S(1)}, bf16[288,1152]{1,0:T(8,128)(2,1)}, u32[]{:S(2)}) copy-start(bf16[288,1152]{1,0:T(8,128)(2,1)} %refs_0_.4) | copy-start | bytes 1990660
  6.3 9.2 %copy-start.1 = (bf16[864,1152]{1,0:T(8,128)(2,1)S(1)}, bf16[864,1152]{1,0:T(8,128)(2,1)}, u32[]{:S(2)}) copy-start(bf16[864,1152]{1,0:T(8,128)(2,1)} %weight_ref.3) | copy-start | bytes 5971972
  6.3 9.2 %copy-start.7 = (f32[6,1152]{1,0:T(8,128)S(1)}, f32[6,1152]{1,0:T(8,128)}, u32[]{:S(2)}) copy-start(f32[6,1152]{1,0:T(8,128)} %mod_ref.7) | copy-start | bytes 82948
  7.4 12.0 %collective-permute-start.5 = (bf16[288,1152]{1,0:T(8,128)(2,1)S(1)}, bf16[288,1152]{1,0:T(8,128)(2,1)S(1)}, u32[]{:S(2)}, u32[]{:S(2)}) collective-permute-start(bf16[288,1152]{1,0:T(8,128)(2,1)S(1)} %copy-done.3), channel_id=1, source_target_pairs={{0,1},{1,0},{2,3},{3,2},{4,5},{5,4},{6,7},{7,6},{8,9},{9,8},{10,11... | collective-permute-start | bytes 1990664 | tf_op jit(solution)/shard_map/ppermute | solution.py:248
  7.8 12.1 %copy-start.2 = (bf16[864,1152]{1,0:T(8,128)(2,1)S(1)}, bf16[864,1152]{1,0:T(8,128)(2,1)}, u32[]{:S(2)}) copy-start(bf16[864,1152]{1,0:T(8,128)(2,1)} %refs_0_.7) | copy-start | bytes 5971972
  7.8 6.1 %collective-permute-start.1 = (bf16[64,1152]{1,0:T(8,128)(2,1)S(1)}, bf16[64,1152]{1,0:T(8,128)(2,1)S(1)}, u32[]{:S(2)}, u32[]{:S(2)}) collective-permute-start(bf16[64,1152]{1,0:T(8,128)(2,1)S(1)} %get-tuple-element.42), channel_id=1, source_target_pairs={{0,4},{4,0},{8,12},{12,8},{16,20},{20,16},{24,28},{28,24},{1,5},{5... | collective-permute-start | bytes 442376 | tf_op jit(solution)/shard_map/ppermute | solution.py:248
  13.9 1.6 %collective-permute-start.3 = (bf16[1,128,1152]{2,1,0:T(8,128)(2,1)S(1)}, bf16[1,128,1152]{2,1,0:T(8,128)(2,1)S(1)}, u32[]{:S(2)}, u32[]{:S(2)}) collective-permute-start(bf16[1,128,1152]{2,1,0:T(8,128)(2,1)S(1)} %collective-permute-done.2.refs_0_), channel_id=1, source_target_pairs={{0,1},{1,0},{2,3},{3,2},{4,5},{5,4},{6,7},{7,6},{8,9},{9,8},{10,11... | collective-permute-start | bytes 884744 | tf_op jit(solution)/shard_map/ppermute | solution.py:248
  18.1 1.3 %collective-permute-start.4 = (bf16[288,128]{1,0:T(8,128)(2,1)S(1)}, bf16[288,128]{1,0:T(8,128)(2,1)S(1)}, u32[]{:S(2)}, u32[]{:S(2)}) collective-permute-start(bf16[288,128]{1,0:T(8,128)(2,1)S(1)} %get-tuple-element.45), channel_id=1, source_target_pairs={{0,1},{1,0},{2,3},{3,2},{4,5},{5,4},{6,7},{7,6},{8,9},{9,8},{10,11... | collective-permute-start | bytes 221192 | tf_op jit(solution)/shard_map/ppermute | solution.py:248
  19.9 6.7 %copy-start.4 = (bf16[288,1152]{1,0:T(8,128)(2,1)S(1)}, bf16[288,1152]{1,0:T(8,128)(2,1)}, u32[]{:S(2)}) copy-start(bf16[288,1152]{1,0:T(8,128)(2,1)} %refs_2_.7) | copy-start | bytes 1990660
  19.9 23.2 %collective-permute-start.14 = (bf16[864,1152]{1,0:T(8,128)(2,1)S(1)}, bf16[864,1152]{1,0:T(8,128)(2,1)S(1)}, u32[]{:S(2)}, u32[]{:S(2)}) collective-permute-start(bf16[864,1152]{1,0:T(8,128)(2,1)S(1)} %copy-done.2), channel_id=1, source_target_pairs={{0,1},{1,0},{2,3},{3,2},{4,5},{5,4},{6,7},{7,6},{8,9},{9,8},{10,11... | collective-permute-start | bytes 5971976 | tf_op jit(solution)/shard_map/ppermute | solution.py:248
  20.1 7.2 %collective-permute-start.8 = (bf16[64,1152]{1,0:T(8,128)(2,1)S(1)}, bf16[64,1152]{1,0:T(8,128)(2,1)S(1)}, u32[]{:S(2)}, u32[]{:S(2)}) collective-permute-start(bf16[64,1152]{1,0:T(8,128)(2,1)S(1)} %get-tuple-element.53), channel_id=1, source_target_pairs={{0,6},{1,7},{2,4},{3,5},{4,2},{5,3},{6,0},{7,1},{8,14},{9,15},{10,... | collective-permute-start | bytes 442376 | tf_op jit(solution)/shard_map/ppermute | solution.py:271
  22.8 7.5 %collective-permute-start.7 = (bf16[64,1152]{1,0:T(8,128)(2,1)S(1)}, bf16[64,1152]{1,0:T(8,128)(2,1)S(1)}, u32[]{:S(2)}, u32[]{:S(2)}) collective-permute-start(bf16[64,1152]{1,0:T(8,128)(2,1)S(1)} %get-tuple-element.47), channel_id=1, source_target_pairs={{0,2},{1,3},{2,0},{3,1},{4,6},{5,7},{6,4},{7,5},{8,10},{9,11},{10,... | collective-permute-start | bytes 442376 | tf_op jit(solution)/shard_map/ppermute | solution.py:248
  24.5 1.3 %collective-permute-start.6 = (bf16[288,128]{1,0:T(8,128)(2,1)S(1)}, bf16[288,128]{1,0:T(8,128)(2,1)S(1)}, u32[]{:S(2)}, u32[]{:S(2)}) collective-permute-start(bf16[288,128]{1,0:T(8,128)(2,1)S(1)} %get-tuple-element.51), channel_id=1, source_target_pairs={{0,1},{1,0},{2,3},{3,2},{4,5},{5,4},{6,7},{7,6},{8,9},{9,8},{10,11... | collective-permute-start | bytes 221192 | tf_op jit(solution)/shard_map/ppermute | solution.py:248
  26.2 4.6 %collective-permute-start.9 = (bf16[64,576]{1,0:T(8,128)(2,1)S(1)}, bf16[64,576]{1,0:T(8,128)(2,1)S(1)}, u32[]{:S(2)}, u32[]{:S(2)}) collective-permute-start(bf16[64,576]{1,0:T(8,128)(2,1)S(1)} %get-tuple-element.55), channel_id=1, source_target_pairs={{0,4},{4,0},{8,12},{12,8},{16,20},{20,16},{24,28},{28,24},{1,5},{5... | collective-permute-start | bytes 221192 | tf_op jit(solution)/shard_map/ppermute | solution.py:248
  26.6 16.5 %collective-permute-start.15 = (bf16[288,1152]{1,0:T(8,128)(2,1)S(1)}, bf16[288,1152]{1,0:T(8,128)(2,1)S(1)}, u32[]{:S(2)}, u32[]{:S(2)}) collective-permute-start(bf16[288,1152]{1,0:T(8,128)(2,1)S(1)} %copy-done.4), channel_id=1, source_target_pairs={{0,1},{1,0},{2,3},{3,2},{4,5},{5,4},{6,7},{7,6},{8,9},{9,8},{10,11... | collective-permute-start | bytes 1990664 | tf_op jit(solution)/shard_map/ppermute | solution.py:248
  31.5 6.8 %collective-permute-start.10 = (bf16[32,1152]{1,0:T(8,128)(2,1)S(1)}, bf16[32,1152]{1,0:T(8,128)(2,1)S(1)}, u32[]{:S(2)}, u32[]{:S(2)}) collective-permute-start(bf16[32,1152]{1,0:T(8,128)(2,1)S(1)} %get-tuple-element.59), channel_id=1, source_target_pairs={{0,24},{4,28},{8,16},{12,20},{16,8},{20,12},{24,0},{28,4},{1,25},{... | collective-permute-start | bytes 221192 | tf_op jit(solution)/shard_map/ppermute | solution.py:248
  35.2 6.2 %collective-permute-start.11 = (bf16[32,1152]{1,0:T(8,128)(2,1)S(1)}, bf16[32,1152]{1,0:T(8,128)(2,1)S(1)}, u32[]{:S(2)}, u32[]{:S(2)}) collective-permute-start(bf16[32,1152]{1,0:T(8,128)(2,1)S(1)} %get-tuple-element.60), channel_id=1, source_target_pairs={{0,16},{4,20},{8,24},{12,28},{16,0},{20,4},{24,8},{28,12},{1,17},{... | collective-permute-start | bytes 221192 | tf_op jit(solution)/shard_map/ppermute | solution.py:248
  35.2 6.2 %collective-permute-start.12 = (bf16[32,1152]{1,0:T(8,128)(2,1)S(1)}, bf16[32,1152]{1,0:T(8,128)(2,1)S(1)}, u32[]{:S(2)}, u32[]{:S(2)}) collective-permute-start(bf16[32,1152]{1,0:T(8,128)(2,1)S(1)} %get-tuple-element.61), channel_id=1, source_target_pairs={{0,8},{4,12},{8,0},{12,4},{16,24},{20,28},{24,16},{28,20},{1,9},{5... | collective-permute-start | bytes 221192 | tf_op jit(solution)/shard_map/ppermute | solution.py:248
  41.4 8.6 %collective-permute-start.16 = (bf16[128,1152]{1,0:T(8,128)(2,1)S(1)}, bf16[128,1152]{1,0:T(8,128)(2,1)S(1)}, u32[]{:S(2)}, u32[]{:S(2)}) collective-permute-start(bf16[128,1152]{1,0:T(8,128)(2,1)S(1)} %shard_map.73.refs_4_), channel_id=1, source_target_pairs={{0,2},{1,3},{2,0},{3,1},{4,6},{5,7},{6,4},{7,5},{8,10},{9,11},{10,... | collective-permute-start | bytes 884744 | tf_op jit(solution)/shard_map/ppermute | solution.py:248
  44.9 4.5 %collective-permute-start.17 = (bf16[64,576]{1,0:T(8,128)(2,1)S(1)}, bf16[64,576]{1,0:T(8,128)(2,1)S(1)}, u32[]{:S(2)}, u32[]{:S(2)}) collective-permute-start(bf16[64,576]{1,0:T(8,128)(2,1)S(1)} %get-tuple-element.67), channel_id=1, source_target_pairs={{0,4},{4,0},{8,12},{12,8},{16,20},{20,16},{24,28},{28,24},{1,5},{5... | collective-permute-start | bytes 221192 | tf_op jit(solution)/shard_map/ppermute | solution.py:248
  52.1 7.3 %collective-permute-start.18 = (bf16[64,1152]{1,0:T(8,128)(2,1)S(1)}, bf16[64,1152]{1,0:T(8,128)(2,1)S(1)}, u32[]{:S(2)}, u32[]{:S(2)}) collective-permute-start(bf16[64,1152]{1,0:T(8,128)(2,1)S(1)} %get-tuple-element.69), channel_id=1, source_target_pairs={{0,2},{1,3},{2,0},{3,1},{4,6},{5,7},{6,4},{7,5},{8,10},{9,11},{10,... | collective-permute-start | bytes 442376 | tf_op jit(solution)/shard_map/ppermute | solution.py:248
  53.6 6.7 %collective-permute-start.19 = (bf16[64,1152]{1,0:T(8,128)(2,1)S(1)}, bf16[64,1152]{1,0:T(8,128)(2,1)S(1)}, u32[]{:S(2)}, u32[]{:S(2)}) collective-permute-start(bf16[64,1152]{1,0:T(8,128)(2,1)S(1)} %get-tuple-element.70), channel_id=1, source_target_pairs={{0,6},{1,7},{2,4},{3,5},{4,2},{5,3},{6,0},{7,1},{8,14},{9,15},{10,... | collective-permute-start | bytes 442376 | tf_op jit(solution)/shard_map/ppermute | solution.py:271
  54.9 10.0 %collective-permute-start.13 = (bf16[4,16,1152]{2,1,0:T(8,128)(2,1)S(1)}, bf16[4,16,1152]{2,1,0:T(8,128)(2,1)S(1)}, u32[]{:S(2)}, u32[]{:S(2)}) collective-permute-start(bf16[4,16,1152]{2,1,0:T(8,128)(2,1)S(1)} %get-tuple-element.63), channel_id=1, source_target_pairs={{0,4},{4,0},{8,12},{12,8},{16,20},{20,16},{24,28},{28,24},{1,5},{5... | collective-permute-start | bytes 442376 | tf_op jit(solution)/shard_map/ppermute | solution.py:248
  60.4 6.3 %collective-permute-start.20 = (bf16[32,1152]{1,0:T(8,128)(2,1)S(1)}, bf16[32,1152]{1,0:T(8,128)(2,1)S(1)}, u32[]{:S(2)}, u32[]{:S(2)}) collective-permute-start(bf16[32,1152]{1,0:T(8,128)(2,1)S(1)} %get-tuple-element.71), channel_id=1, source_target_pairs={{0,24},{4,28},{8,16},{12,20},{16,8},{20,12},{24,0},{28,4},{1,25},{... | collective-permute-start | bytes 221192 | tf_op jit(solution)/shard_map/ppermute | solution.py:248
  61.5 6.8 %collective-permute-start.21 = (bf16[32,1152]{1,0:T(8,128)(2,1)S(1)}, bf16[32,1152]{1,0:T(8,128)(2,1)S(1)}, u32[]{:S(2)}, u32[]{:S(2)}) collective-permute-start(bf16[32,1152]{1,0:T(8,128)(2,1)S(1)} %get-tuple-element.72), channel_id=1, source_target_pairs={{0,16},{4,20},{8,24},{12,28},{16,0},{20,4},{24,8},{28,12},{1,17},{... | collective-permute-start | bytes 221192 | tf_op jit(solution)/shard_map/ppermute | solution.py:248
  61.5 6.8 %collective-permute-start.22 = (bf16[32,1152]{1,0:T(8,128)(2,1)S(1)}, bf16[32,1152]{1,0:T(8,128)(2,1)S(1)}, u32[]{:S(2)}, u32[]{:S(2)}) collective-permute-start(bf16[32,1152]{1,0:T(8,128)(2,1)S(1)} %get-tuple-element.73), channel_id=1, source_target_pairs={{0,8},{4,12},{8,0},{12,4},{16,24},{20,28},{24,16},{28,20},{1,9},{5... | collective-permute-start | bytes 221192 | tf_op jit(solution)/shard_map/ppermute | solution.py:248

commit v20 on v16

--- a/solution.py
+++ b/solution.py
@@ -216,7 +216,7 @@
             )
 
 
-def call(body, operands, outs, scratch=(), limit=24):
+def call(body, operands, outs, scratch=(), limit=24, flops=1):
     return pl.pallas_call(
         body,
         out_shape=outs,
@@ -224,7 +224,7 @@
         out_specs=[pl.BlockSpec(memory_space=pltpu.VMEM)] * len(outs),
         scratch_shapes=list(scratch),
         compiler_params=pltpu.CompilerParams(vmem_limit_bytes=limit * MIB),
-        cost_estimate=pl.CostEstimate(flops=1, bytes_accessed=1, transcendentals=0),
+        cost_estimate=pl.CostEstimate(flops=flops, bytes_accessed=1, transcendentals=0),
     )(*operands)
 
 
@@ -273,7 +273,7 @@
 
     def project_paired(sent, weights):
         heads = swap(sent, "frame", 1)
-        return call(paired_kernel, (heads, *weights), [halves_shape(F32)])[0]
+        return call(paired_kernel, (heads, *weights), [halves_shape(F32)], flops=1_000_000_000)[0]
 
     def return_updates(own, far):
         same = [swap(part, "patch", 2 * at) for at, part in enumerate(far[::2], 1)]

time: 65.8 us -> 66.7 us (1.014)
  waiting for transfers between devices: 26 us -> 28 us
  starting transfers between devices: 24.9 us -> 23.8 us
    ppermute x2, starting transfers between devices: 2.85 us -> 0.72 us  [swap_diagonal(): return lax.ppermute(value, ('frame', 'patch'), pairs)]
    ppermute x20, waiting for transfers between devices: 24.8 us -> 26.8 us  [swap(): return lax.ppermute(value, axis, [(at, at ^ offset) for at in range(size)])]
    ppermute x20, starting transfers between devices: 22 us -> 23.1 us  [swap(): return lax.ppermute(value, axis, [(at, at ^ offset) for at in range(size)])]
  transfers between devices with their start and end apart: 22 -> 22, of which waited for: 11 -> 12; matrix products, arithmetic and copies ran while one was open for 0% -> 0% of each run, Pallas kernels for 13% -> 13%
where the time goes in v20:
time: 66.7 us; the launch traced here: 66.4 us
  waiting for transfers between devices  28 us (42%)
  starting transfers between devices  23.8 us (36%)
  Pallas kernels  11.1 us (17%)
  local copies, waits for them, and re-layouts  3.34 us (5%)
    ppermute x20, waiting for transfers between devices, swap(): return lax.ppermute(value, axis, [(at, at ^ offset) for at in range(size)])  26.8 us
    ppermute x20, starting transfers between devices, swap(): return lax.ppermute(value, axis, [(at, at ^ offset) for at in range(size)])  23.1 us
    pallas_call x12, Pallas kernels, call(): pl.pallas_call(body, out_shape=outs, in_specs=[pl.BlockSpec(memory_space=...  11.1 us
    unnamed x16, local copies, waits for them, and re-layouts  3.34 us
  transfers between devices with their start and end apart: 22, of which 12 were waited for; matrix products, arithmetic and copies ran while one was open for 0% of the time, Pallas kernels for 13%

profile of v20, /device:TPU:0, one launch (start us, length us, event | category | flops | bytes accessed | tf_op | source)
XLA Modules:
  0.0 66.4 jit_solution(5151580599141615272)
XLA Ops:
  0.5 2.5 %collective-permute-start.2 = (bf16[1,128,1152]{2,1,0:T(8,128)(2,1)}, bf16[1,128,1152]{2,1,0:T(8,128)(2,1)S(1)}, u32[]{:S(2)}, u32[]{:S(2)}) collective-permute-start(bf16[1,128,1152]{2,1,0:T(8,128)(2,1)} %own_ref.1), channel_id=1, source_target_pairs={{0,2},{1,3},{2,0},{3,1},{4,6},{5,7},{6,4},{7,5},{8,10},{9,11},{10,... | collective-permute-start | bytes 884744 | tf_op jit(solution)/shard_map/ppermute | solution.py:233
  3.0 1.0 %copy-done.4 = bf16[1,128,1152]{2,1,0:T(8,128)(2,1)S(1)} copy-done((bf16[1,128,1152]{2,1,0:T(8,128)(2,1)S(1)}, bf16[1,128,1152]{2,1,0:T(8,128)(2,1)}, u32[]{:S(2)}) %copy-start.4) | copy-done | bytes 294936
  4.1 1.8 %collective-permute-start.1 = (bf16[64,1152]{1,0:T(8,128)(2,1)S(1)}, bf16[64,1152]{1,0:T(8,128)(2,1)S(1)}, u32[]{:S(2)}, u32[]{:S(2)}) collective-permute-start(bf16[64,1152]{1,0:T(8,128)(2,1)S(1)} %get-tuple-element.36), channel_id=1, source_target_pairs={{0,4},{4,0},{8,12},{12,8},{16,20},{20,16},{24,28},{28,24},{1,5},{5... | collective-permute-start | bytes 442376 | tf_op jit(solution)/shard_map/ppermute | solution.py:233
  5.9 1.6 %copy-done = bf16[864,1152]{1,0:T(8,128)(2,1)S(1)} copy-done((bf16[864,1152]{1,0:T(8,128)(2,1)S(1)}, bf16[864,1152]{1,0:T(8,128)(2,1)}, u32[]{:S(2)}) %copy-start) | copy-done | bytes 1990680
  7.4 0.8 %copy-done.6 = f32[6,1152]{1,0:T(8,128)S(1)} copy-done((f32[6,1152]{1,0:T(8,128)S(1)}, f32[6,1152]{1,0:T(8,128)}, u32[]{:S(2)}) %copy-start.6) | copy-done | bytes 27672
  8.2 1.1 %shard_map.65.near_ref = f32[864,256]{1,0:T(8,128)S(1)} custom-call(f32[6,1152]{1,0:T(8,128)S(1)} %copy-done.6, bf16[864,1152]{1,0:T(8,128)(2,1)S(1)} %copy-done, bf16[1,128,1152]{2,1,0:T(8,128)(2,1)S(1)} %copy-done.4, bf16[1,128,1152]{2,1,0:T(8,128)(2,1)S(1)} %collective-permute-done.sister_ref), custom_call_target="tpu_custom_call" | custom-call | flops 1 | bytes 1 | tf_op jit(solution)/shard_map/pallas_call | solution.py:220
  9.3 1.6 %collective-permute-done.2.refs_0_ = bf16[1,128,1152]{2,1,0:T(8,128)(2,1)S(1)} collective-permute-done((bf16[1,128,1152]{2,1,0:T(8,128)(2,1)}, bf16[1,128,1152]{2,1,0:T(8,128)(2,1)S(1)}, u32[]{:S(2)}, u32[]{:S(2)}) %collective-permute-start.2) | collective-permute-done | bytes 294944 | tf_op jit(solution)/shard_map/ppermute | solution.py:233
  10.9 1.6 %collective-permute-done.3.refs_1_ = bf16[1,128,1152]{2,1,0:T(8,128)(2,1)S(1)} collective-permute-done((bf16[1,128,1152]{2,1,0:T(8,128)(2,1)S(1)}, bf16[1,128,1152]{2,1,0:T(8,128)(2,1)S(1)}, u32[]{:S(2)}, u32[]{:S(2)}) %collective-permute-start.3) | collective-permute-done | bytes 294944 | tf_op jit(solution)/shard_map/ppermute | solution.py:233
  13.0 3.3 %shard_map.66 = (bf16[288,256]{1,0:T(8,128)(2,1)S(1)}, bf16[288,256]{1,0:T(8,128)(2,1)S(1)}) custom-call(f32[6,1152]{1,0:T(8,128)S(1)} %copy-done.6, bf16[864,1152]{1,0:T(8,128)(2,1)S(1)} %copy-done.1, f32[864,256]{1,0:T(8,128)S(1)} %shard_map.65.near_ref, bf16[1,128,1152]{2,1,0:T(8,128)(2,1)S(1)} %collective-permute-done.2.refs_0_, ...), custom_call_target="tpu_custom_call" | custom-call | flops 1 | bytes 1 | tf_op jit(solution)/shard_map/pallas_call | solution.py:220
  16.5 1.2 %collective-permute-done.4.refs_1_ = bf16[288,256]{1,0:T(8,128)(2,1)S(1)} collective-permute-done((bf16[288,256]{1,0:T(8,128)(2,1)S(1)}, bf16[288,256]{1,0:T(8,128)(2,1)S(1)}, u32[]{:S(2)}, u32[]{:S(2)}) %collective-permute-start.4) | collective-permute-done | bytes 147488 | tf_op jit(solution)/shard_map/ppermute | solution.py:233
  17.7 0.7 %shard_map.67 = (f32[64,1152]{1,0:T(8,128)S(1)}, bf16[64,576]{1,0:T(8,128)(2,1)S(1)}, bf16[64,1152]{1,0:T(8,128)(2,1)S(1)}, bf16[64,1152]{1,0:T(8,128)(2,1)S(1)}) custom-call(bf16[288,256]{1,0:T(8,128)(2,1)S(1)} %get-tuple-element.38.refs_0_, bf16[288,256]{1,0:T(8,128)(2,1)S(1)} %collective-permute-done.4.refs_1_, bf16[288,1152]{1,0:T(8,128)(2,1)S(1)} %copy-done.5, ...), custom_call_target="tpu_custom_call" | custom-call | flops 1 | bytes 1 | tf_op jit(solution)/shard_map/pallas_call | solution.py:220
  18.7 1.7 %collective-permute-start.7 = (bf16[64,576]{1,0:T(8,128)(2,1)S(1)}, bf16[64,576]{1,0:T(8,128)(2,1)S(1)}, u32[]{:S(2)}, u32[]{:S(2)}) collective-permute-start(bf16[64,576]{1,0:T(8,128)(2,1)S(1)} %get-tuple-element.43), channel_id=1, source_target_pairs={{0,4},{4,0},{8,12},{12,8},{16,20},{20,16},{24,28},{28,24},{1,5},{5... | collective-permute-start | bytes 221192 | tf_op jit(solution)/shard_map/ppermute | solution.py:233
  20.4 1.5 %collective-permute-start.6 = (bf16[64,1152]{1,0:T(8,128)(2,1)S(1)}, bf16[64,1152]{1,0:T(8,128)(2,1)S(1)}, u32[]{:S(2)}, u32[]{:S(2)}) collective-permute-start(bf16[64,1152]{1,0:T(8,128)(2,1)S(1)} %get-tuple-element.42), channel_id=1, source_target_pairs={{0,2},{1,3},{2,0},{3,1},{4,6},{5,7},{6,4},{7,5},{8,10},{9,11},{10,... | collective-permute-start | bytes 442376 | tf_op jit(solution)/shard_map/ppermute | solution.py:233
  22.2 1.2 %collective-permute-done.7.head_ref = bf16[64,576]{1,0:T(8,128)(2,1)S(1)} collective-permute-done((bf16[64,576]{1,0:T(8,128)(2,1)S(1)}, bf16[64,576]{1,0:T(8,128)(2,1)S(1)}, u32[]{:S(2)}, u32[]{:S(2)}) %collective-permute-start.7) | collective-permute-done | bytes 73760 | tf_op jit(solution)/shard_map/ppermute | solution.py:233
  23.8 5.6 %collective-permute-done.6.refs_1_ = bf16[64,1152]{1,0:T(8,128)(2,1)S(1)} collective-permute-done((bf16[64,1152]{1,0:T(8,128)(2,1)S(1)}, bf16[64,1152]{1,0:T(8,128)(2,1)S(1)}, u32[]{:S(2)}, u32[]{:S(2)}) %collective-permute-start.6) | collective-permute-done | bytes 147488 | tf_op jit(solution)/shard_map/ppermute | solution.py:233
  29.8 3.7 %collective-permute-start.9 = (bf16[32,1152]{1,0:T(8,128)(2,1)S(1)}, bf16[32,1152]{1,0:T(8,128)(2,1)S(1)}, u32[]{:S(2)}, u32[]{:S(2)}) collective-permute-start(bf16[32,1152]{1,0:T(8,128)(2,1)S(1)} %get-tuple-element.47), channel_id=1, source_target_pairs={{0,24},{4,28},{8,16},{12,20},{16,8},{20,12},{24,0},{28,4},{1,25},{... | collective-permute-start | bytes 221192 | tf_op jit(solution)/shard_map/ppermute | solution.py:233
  33.5 0.8 %collective-permute-start.11 = (bf16[32,1152]{1,0:T(8,128)(2,1)S(1)}, bf16[32,1152]{1,0:T(8,128)(2,1)S(1)}, u32[]{:S(2)}, u32[]{:S(2)}) collective-permute-start(bf16[32,1152]{1,0:T(8,128)(2,1)S(1)} %get-tuple-element.49), channel_id=1, source_target_pairs={{0,8},{4,12},{8,0},{12,4},{16,24},{20,28},{24,16},{28,20},{1,9},{5... | collective-permute-start | bytes 221192 | tf_op jit(solution)/shard_map/ppermute | solution.py:233
  34.2 2.3 %collective-permute-done.9.refs_0_ = bf16[32,1152]{1,0:T(8,128)(2,1)S(1)} collective-permute-done((bf16[32,1152]{1,0:T(8,128)(2,1)S(1)}, bf16[32,1152]{1,0:T(8,128)(2,1)S(1)}, u32[]{:S(2)}, u32[]{:S(2)}) %collective-permute-start.9) | collective-permute-done | bytes 73760 | tf_op jit(solution)/shard_map/ppermute | solution.py:233
  36.6 2.6 %collective-permute-done.10.refs_1_ = bf16[32,1152]{1,0:T(8,128)(2,1)S(1)} collective-permute-done((bf16[32,1152]{1,0:T(8,128)(2,1)S(1)}, bf16[32,1152]{1,0:T(8,128)(2,1)S(1)}, u32[]{:S(2)}, u32[]{:S(2)}) %collective-permute-start.10) | collective-permute-done | bytes 73760 | tf_op jit(solution)/shard_map/ppermute | solution.py:233
  39.3 1.6 %collective-permute-start.15 = (bf16[128,1152]{1,0:T(8,128)(2,1)S(1)}, bf16[128,1152]{1,0:T(8,128)(2,1)S(1)}, u32[]{:S(2)}, u32[]{:S(2)}) collective-permute-start(bf16[128,1152]{1,0:T(8,128)(2,1)S(1)} %shard_map.70.refs_4_), channel_id=1, source_target_pairs={{0,2},{1,3},{2,0},{3,1},{4,6},{5,7},{6,4},{7,5},{8,10},{9,11},{10,... | collective-permute-start | bytes 884744 | tf_op jit(solution)/shard_map/ppermute | solution.py:233
  40.9 1.9 %shard_map.71 = (f32[64,1152]{1,0:T(8,128)S(1)}, bf16[64,576]{1,0:T(8,128)(2,1)S(1)}) custom-call(bf16[864,1152]{1,0:T(8,128)(2,1)S(1)} %copy-done.2, bf16[864,1152]{1,0:T(8,128)(2,1)S(1)} %collective-permute-done.13.refs_1_, bf16[288,1152]{1,0:T(8,128)(2,1)S(1)} %copy-done.3, bf16[288,1152]{1,0:T(8,128)(2,1)S(1)} %collective-permute-done.14.refs_3_.refs_1_, ...), custom_call_target="tpu_custom_call" | custom-call | flops 1 | bytes 1 | tf_op jit(solution)/shard_map/pallas_call | solution.py:220
  43.4 3.9 %collective-permute-done.16.head_ref = bf16[64,576]{1,0:T(8,128)(2,1)S(1)} collective-permute-done((bf16[64,576]{1,0:T(8,128)(2,1)S(1)}, bf16[64,576]{1,0:T(8,128)(2,1)S(1)}, u32[]{:S(2)}, u32[]{:S(2)}) %collective-permute-start.16) | collective-permute-done | bytes 73760 | tf_op jit(solution)/shard_map/ppermute | solution.py:233
  47.7 2.0 %shard_map.73 = (bf16[64,1152]{1,0:T(8,128)(2,1)S(1)}, bf16[64,1152]{1,0:T(8,128)(2,1)S(1)}) custom-call(bf16[864,1152]{1,0:T(8,128)(2,1)S(1)} %copy-done.2, bf16[864,1152]{1,0:T(8,128)(2,1)S(1)} %collective-permute-done.13.refs_1_, bf16[288,1152]{1,0:T(8,128)(2,1)S(1)} %copy-done.3, bf16[288,1152]{1,0:T(8,128)(2,1)S(1)} %collective-permute-done.14.refs_3_.refs_1_, ...), custom_call_target="tpu_custom_call" | custom-call | flops 1 | bytes 1 | tf_op jit(solution)/shard_map/pallas_call | solution.py:220
  49.7 1.6 %collective-permute-start.17 = (bf16[64,1152]{1,0:T(8,128)(2,1)S(1)}, bf16[64,1152]{1,0:T(8,128)(2,1)S(1)}, u32[]{:S(2)}, u32[]{:S(2)}) collective-permute-start(bf16[64,1152]{1,0:T(8,128)(2,1)S(1)} %get-tuple-element.57), channel_id=1, source_target_pairs={{0,2},{1,3},{2,0},{3,1},{4,6},{5,7},{6,4},{7,5},{8,10},{9,11},{10,... | collective-permute-start | bytes 442376 | tf_op jit(solution)/shard_map/ppermute | solution.py:233
  51.7 1.5 %collective-permute-start.12 = (bf16[4,16,1152]{2,1,0:T(8,128)(2,1)S(1)}, bf16[4,16,1152]{2,1,0:T(8,128)(2,1)S(1)}, u32[]{:S(2)}, u32[]{:S(2)}) collective-permute-start(bf16[4,16,1152]{2,1,0:T(8,128)(2,1)S(1)} %get-tuple-element.51), channel_id=1, source_target_pairs={{0,4},{4,0},{8,12},{12,8},{16,20},{20,16},{24,28},{28,24},{1,5},{5... | collective-permute-start | bytes 442376 | tf_op jit(solution)/shard_map/ppermute | solution.py:233
  53.2 3.3 %collective-permute-done.17.refs_1_ = bf16[64,1152]{1,0:T(8,128)(2,1)S(1)} collective-permute-done((bf16[64,1152]{1,0:T(8,128)(2,1)S(1)}, bf16[64,1152]{1,0:T(8,128)(2,1)S(1)}, u32[]{:S(2)}, u32[]{:S(2)}) %collective-permute-start.17) | collective-permute-done | bytes 147488 | tf_op jit(solution)/shard_map/ppermute | solution.py:233
  56.5 1.2 %collective-permute-done.18.refs_3_ = bf16[64,1152]{1,0:T(8,128)(2,1)S(1)} collective-permute-done((bf16[64,1152]{1,0:T(8,128)(2,1)S(1)}, bf16[64,1152]{1,0:T(8,128)(2,1)S(1)}, u32[]{:S(2)}, u32[]{:S(2)}) %collective-permute-start.18) | collective-permute-done | bytes 147488 | tf_op jit(solution)/shard_map/ppermute | solution.py:256
  57.8 1.3 %collective-permute-start.19 = (bf16[32,1152]{1,0:T(8,128)(2,1)S(1)}, bf16[32,1152]{1,0:T(8,128)(2,1)S(1)}, u32[]{:S(2)}, u32[]{:S(2)}) collective-permute-start(bf16[32,1152]{1,0:T(8,128)(2,1)S(1)} %get-tuple-element.59), channel_id=1, source_target_pairs={{0,24},{4,28},{8,16},{12,20},{16,8},{20,12},{24,0},{28,4},{1,25},{... | collective-permute-start | bytes 221192 | tf_op jit(solution)/shard_map/ppermute | solution.py:233
  59.1 3.1 %collective-permute-start.21 = (bf16[32,1152]{1,0:T(8,128)(2,1)S(1)}, bf16[32,1152]{1,0:T(8,128)(2,1)S(1)}, u32[]{:S(2)}, u32[]{:S(2)}) collective-permute-start(bf16[32,1152]{1,0:T(8,128)(2,1)S(1)} %get-tuple-element.61), channel_id=1, source_target_pairs={{0,8},{4,12},{8,0},{12,4},{16,24},{20,28},{24,16},{28,20},{1,9},{5... | collective-permute-start | bytes 221192 | tf_op jit(solution)/shard_map/ppermute | solution.py:233
  62.2 1.8 %collective-permute-done.19.refs_0_ = bf16[32,1152]{1,0:T(8,128)(2,1)S(1)} collective-permute-done((bf16[32,1152]{1,0:T(8,128)(2,1)S(1)}, bf16[32,1152]{1,0:T(8,128)(2,1)S(1)}, u32[]{:S(2)}, u32[]{:S(2)}) %collective-permute-start.19) | collective-permute-done | bytes 73760 | tf_op jit(solution)/shard_map/ppermute | solution.py:233
  64.1 1.5 %collective-permute-done.20.refs_1_ = bf16[32,1152]{1,0:T(8,128)(2,1)S(1)} collective-permute-done((bf16[32,1152]{1,0:T(8,128)(2,1)S(1)}, bf16[32,1152]{1,0:T(8,128)(2,1)S(1)}, u32[]{:S(2)}, u32[]{:S(2)}) %collective-permute-start.20) | collective-permute-done | bytes 73760 | tf_op jit(solution)/shard_map/ppermute | solution.py:233
  65.6 0.8 %shard_map.75 = bf16[8,16,1152]{2,1,0:T(8,128)(2,1)} custom-call(f32[6,1152]{1,0:T(8,128)S(1)} %copy-done.7, bf16[4,16,1152]{2,1,0:T(8,128)(2,1)S(1)} %get-tuple-element.45.kept_ref, bf16[4,16,1152]{2,1,0:T(8,128)(2,1)S(1)} %collective-permute-done.12.other_ref, bf16[32,1152]{1,0:T(8,128)(2,1)S(1)} %collective-permute-done.19.refs_0_, ...), custom_call_target="tpu_custom_call" | custom-call | flops 1 | bytes 1 | tf_op jit(solution)/shard_map/pallas_call | solution.py:220
  (40 shorter events, 4.1 us)
Async XLA Ops:
  0.0 3.0 %collective-permute-start = (bf16[1,128,1152]{2,1,0:T(8,128)(2,1)}, bf16[1,128,1152]{2,1,0:T(8,128)(2,1)S(1)}, u32[]{:S(2)}, u32[]{:S(2)}) collective-permute-start(bf16[1,128,1152]{2,1,0:T(8,128)(2,1)} %own_ref.1), channel_id=1, source_target_pairs={{0,1},{1,0},{2,3},{3,2},{4,5},{5,4},{6,7},{7,6},{8,9},{9,8},{10,11... | collective-permute-start | bytes 884744 | tf_op jit(solution)/shard_map/ppermute | solution.py:233
  0.5 10.4 %collective-permute-start.2 = (bf16[1,128,1152]{2,1,0:T(8,128)(2,1)}, bf16[1,128,1152]{2,1,0:T(8,128)(2,1)S(1)}, u32[]{:S(2)}, u32[]{:S(2)}) collective-permute-start(bf16[1,128,1152]{2,1,0:T(8,128)(2,1)} %own_ref.1), channel_id=1, source_target_pairs={{0,2},{1,3},{2,0},{3,1},{4,6},{5,7},{6,4},{7,5},{8,10},{9,11},{10,... | collective-permute-start | bytes 884744 | tf_op jit(solution)/shard_map/ppermute | solution.py:233
  3.0 1.0 %copy-start.4 = (bf16[1,128,1152]{2,1,0:T(8,128)(2,1)S(1)}, bf16[1,128,1152]{2,1,0:T(8,128)(2,1)}, u32[]{:S(2)}) copy-start(bf16[1,128,1152]{2,1,0:T(8,128)(2,1)} %own_ref.1) | copy-start | bytes 884740
  4.1 6.8 %collective-permute-start.1 = (bf16[64,1152]{1,0:T(8,128)(2,1)S(1)}, bf16[64,1152]{1,0:T(8,128)(2,1)S(1)}, u32[]{:S(2)}, u32[]{:S(2)}) collective-permute-start(bf16[64,1152]{1,0:T(8,128)(2,1)S(1)} %get-tuple-element.36), channel_id=1, source_target_pairs={{0,4},{4,0},{8,12},{12,8},{16,20},{20,16},{24,28},{28,24},{1,5},{5... | collective-permute-start | bytes 442376 | tf_op jit(solution)/shard_map/ppermute | solution.py:233
  5.8 1.6 %copy-start = (bf16[864,1152]{1,0:T(8,128)(2,1)S(1)}, bf16[864,1152]{1,0:T(8,128)(2,1)}, u32[]{:S(2)}) copy-start(bf16[864,1152]{1,0:T(8,128)(2,1)} %weight_ref.3) | copy-start | bytes 5971972
  7.4 0.8 %copy-start.6 = (f32[6,1152]{1,0:T(8,128)S(1)}, f32[6,1152]{1,0:T(8,128)}, u32[]{:S(2)}) copy-start(f32[6,1152]{1,0:T(8,128)} %mod_ref.7) | copy-start | bytes 82948
  8.2 4.4 %copy-start.5 = (bf16[288,1152]{1,0:T(8,128)(2,1)S(1)}, bf16[288,1152]{1,0:T(8,128)(2,1)}, u32[]{:S(2)}) copy-start(bf16[288,1152]{1,0:T(8,128)(2,1)} %refs_0_.4) | copy-start | bytes 1990660
  8.2 4.8 %copy-start.1 = (bf16[864,1152]{1,0:T(8,128)(2,1)S(1)}, bf16[864,1152]{1,0:T(8,128)(2,1)}, u32[]{:S(2)}) copy-start(bf16[864,1152]{1,0:T(8,128)(2,1)} %weight_ref.3) | copy-start | bytes 5971972
  9.3 9.2 %copy-start.3 = (bf16[288,1152]{1,0:T(8,128)(2,1)S(1)}, bf16[288,1152]{1,0:T(8,128)(2,1)}, u32[]{:S(2)}) copy-start(bf16[288,1152]{1,0:T(8,128)(2,1)} %refs_2_.5) | copy-start | bytes 1990660
  10.9 1.6 %collective-permute-start.3 = (bf16[1,128,1152]{2,1,0:T(8,128)(2,1)S(1)}, bf16[1,128,1152]{2,1,0:T(8,128)(2,1)S(1)}, u32[]{:S(2)}, u32[]{:S(2)}) collective-permute-start(bf16[1,128,1152]{2,1,0:T(8,128)(2,1)S(1)} %collective-permute-done.2.refs_0_), channel_id=1, source_target_pairs={{0,1},{1,0},{2,3},{3,2},{4,5},{5,4},{6,7},{7,6},{8,9},{9,8},{10,11... | collective-permute-start | bytes 884744 | tf_op jit(solution)/shard_map/ppermute | solution.py:233
  12.4 28.4 %collective-permute-start.13 = (bf16[864,1152]{1,0:T(8,128)(2,1)}, bf16[864,1152]{1,0:T(8,128)(2,1)S(1)}, u32[]{:S(2)}, u32[]{:S(2)}) collective-permute-start(bf16[864,1152]{1,0:T(8,128)(2,1)} %refs_0_.7), channel_id=1, source_target_pairs={{0,1},{1,0},{2,3},{3,2},{4,5},{5,4},{6,7},{7,6},{8,9},{9,8},{10,11... | collective-permute-start | bytes 5971976 | tf_op jit(solution)/shard_map/ppermute | solution.py:233
  12.6 5.1 %collective-permute-start.5 = (bf16[288,1152]{1,0:T(8,128)(2,1)S(1)}, bf16[288,1152]{1,0:T(8,128)(2,1)S(1)}, u32[]{:S(2)}, u32[]{:S(2)}) collective-permute-start(bf16[288,1152]{1,0:T(8,128)(2,1)S(1)} %copy-done.5), channel_id=1, source_target_pairs={{0,1},{1,0},{2,3},{3,2},{4,5},{5,4},{6,7},{7,6},{8,9},{9,8},{10,11... | collective-permute-start | bytes 1990664 | tf_op jit(solution)/shard_map/ppermute | solution.py:233
  16.3 1.4 %collective-permute-start.4 = (bf16[288,256]{1,0:T(8,128)(2,1)S(1)}, bf16[288,256]{1,0:T(8,128)(2,1)S(1)}, u32[]{:S(2)}, u32[]{:S(2)}) collective-permute-start(bf16[288,256]{1,0:T(8,128)(2,1)S(1)} %get-tuple-element.39), channel_id=1, source_target_pairs={{0,1},{1,0},{2,3},{3,2},{4,5},{5,4},{6,7},{7,6},{8,9},{9,8},{10,11... | collective-permute-start | bytes 442376 | tf_op jit(solution)/shard_map/ppermute | solution.py:233
  18.4 11.0 %copy-start.7 = (f32[6,1152]{1,0:T(8,128)S(1)}, f32[6,1152]{1,0:T(8,128)}, u32[]{:S(2)}) copy-start(f32[6,1152]{1,0:T(8,128)} %mod_ref.7) | copy-start | bytes 82948
  18.5 22.4 %collective-permute-start.14 = (bf16[288,1152]{1,0:T(8,128)(2,1)S(1)}, bf16[288,1152]{1,0:T(8,128)(2,1)S(1)}, u32[]{:S(2)}, u32[]{:S(2)}) collective-permute-start(bf16[288,1152]{1,0:T(8,128)(2,1)S(1)} %copy-done.3), channel_id=1, source_target_pairs={{0,1},{1,0},{2,3},{3,2},{4,5},{5,4},{6,7},{7,6},{8,9},{9,8},{10,11... | collective-permute-start | bytes 1990664 | tf_op jit(solution)/shard_map/ppermute | solution.py:233
  18.7 4.7 %collective-permute-start.7 = (bf16[64,576]{1,0:T(8,128)(2,1)S(1)}, bf16[64,576]{1,0:T(8,128)(2,1)S(1)}, u32[]{:S(2)}, u32[]{:S(2)}) collective-permute-start(bf16[64,576]{1,0:T(8,128)(2,1)S(1)} %get-tuple-element.43), channel_id=1, source_target_pairs={{0,4},{4,0},{8,12},{12,8},{16,20},{20,16},{24,28},{28,24},{1,5},{5... | collective-permute-start | bytes 221192 | tf_op jit(solution)/shard_map/ppermute | solution.py:233
  20.4 9.0 %collective-permute-start.6 = (bf16[64,1152]{1,0:T(8,128)(2,1)S(1)}, bf16[64,1152]{1,0:T(8,128)(2,1)S(1)}, u32[]{:S(2)}, u32[]{:S(2)}) collective-permute-start(bf16[64,1152]{1,0:T(8,128)(2,1)S(1)} %get-tuple-element.42), channel_id=1, source_target_pairs={{0,2},{1,3},{2,0},{3,1},{4,6},{5,7},{6,4},{7,5},{8,10},{9,11},{10,... | collective-permute-start | bytes 442376 | tf_op jit(solution)/shard_map/ppermute | solution.py:233
  21.9 18.9 %copy-start.2 = (bf16[864,1152]{1,0:T(8,128)(2,1)S(1)}, bf16[864,1152]{1,0:T(8,128)(2,1)}, u32[]{:S(2)}) copy-start(bf16[864,1152]{1,0:T(8,128)(2,1)} %refs_0_.7) | copy-start | bytes 5971972
  21.9 7.5 %collective-permute-start.8 = (bf16[64,1152]{1,0:T(8,128)(2,1)S(1)}, bf16[64,1152]{1,0:T(8,128)(2,1)S(1)}, u32[]{:S(2)}, u32[]{:S(2)}) collective-permute-start(bf16[64,1152]{1,0:T(8,128)(2,1)S(1)} %get-tuple-element.44), channel_id=1, source_target_pairs={{0,6},{1,7},{2,4},{3,5},{4,2},{5,3},{6,0},{7,1},{8,14},{9,15},{10,... | collective-permute-start | bytes 442376 | tf_op jit(solution)/shard_map/ppermute | solution.py:256
  29.8 6.8 %collective-permute-start.9 = (bf16[32,1152]{1,0:T(8,128)(2,1)S(1)}, bf16[32,1152]{1,0:T(8,128)(2,1)S(1)}, u32[]{:S(2)}, u32[]{:S(2)}) collective-permute-start(bf16[32,1152]{1,0:T(8,128)(2,1)S(1)} %get-tuple-element.47), channel_id=1, source_target_pairs={{0,24},{4,28},{8,16},{12,20},{16,8},{20,12},{24,0},{28,4},{1,25},{... | collective-permute-start | bytes 221192 | tf_op jit(solution)/shard_map/ppermute | solution.py:233
  33.5 5.8 %collective-permute-start.10 = (bf16[32,1152]{1,0:T(8,128)(2,1)S(1)}, bf16[32,1152]{1,0:T(8,128)(2,1)S(1)}, u32[]{:S(2)}, u32[]{:S(2)}) collective-permute-start(bf16[32,1152]{1,0:T(8,128)(2,1)S(1)} %get-tuple-element.48), channel_id=1, source_target_pairs={{0,16},{4,20},{8,24},{12,28},{16,0},{20,4},{24,8},{28,12},{1,17},{... | collective-permute-start | bytes 221192 | tf_op jit(solution)/shard_map/ppermute | solution.py:233
  33.5 5.8 %collective-permute-start.11 = (bf16[32,1152]{1,0:T(8,128)(2,1)S(1)}, bf16[32,1152]{1,0:T(8,128)(2,1)S(1)}, u32[]{:S(2)}, u32[]{:S(2)}) collective-permute-start(bf16[32,1152]{1,0:T(8,128)(2,1)S(1)} %get-tuple-element.49), channel_id=1, source_target_pairs={{0,8},{4,12},{8,0},{12,4},{16,24},{20,28},{24,16},{28,20},{1,9},{5... | collective-permute-start | bytes 221192 | tf_op jit(solution)/shard_map/ppermute | solution.py:233
  39.3 8.4 %collective-permute-start.15 = (bf16[128,1152]{1,0:T(8,128)(2,1)S(1)}, bf16[128,1152]{1,0:T(8,128)(2,1)S(1)}, u32[]{:S(2)}, u32[]{:S(2)}) collective-permute-start(bf16[128,1152]{1,0:T(8,128)(2,1)S(1)} %shard_map.70.refs_4_), channel_id=1, source_target_pairs={{0,2},{1,3},{2,0},{3,1},{4,6},{5,7},{6,4},{7,5},{8,10},{9,11},{10,... | collective-permute-start | bytes 884744 | tf_op jit(solution)/shard_map/ppermute | solution.py:233
  42.8 4.5 %collective-permute-start.16 = (bf16[64,576]{1,0:T(8,128)(2,1)S(1)}, bf16[64,576]{1,0:T(8,128)(2,1)S(1)}, u32[]{:S(2)}, u32[]{:S(2)}) collective-permute-start(bf16[64,576]{1,0:T(8,128)(2,1)S(1)} %get-tuple-element.55), channel_id=1, source_target_pairs={{0,4},{4,0},{8,12},{12,8},{16,20},{20,16},{24,28},{28,24},{1,5},{5... | collective-permute-start | bytes 221192 | tf_op jit(solution)/shard_map/ppermute | solution.py:233
  49.7 6.8 %collective-permute-start.17 = (bf16[64,1152]{1,0:T(8,128)(2,1)S(1)}, bf16[64,1152]{1,0:T(8,128)(2,1)S(1)}, u32[]{:S(2)}, u32[]{:S(2)}) collective-permute-start(bf16[64,1152]{1,0:T(8,128)(2,1)S(1)} %get-tuple-element.57), channel_id=1, source_target_pairs={{0,2},{1,3},{2,0},{3,1},{4,6},{5,7},{6,4},{7,5},{8,10},{9,11},{10,... | collective-permute-start | bytes 442376 | tf_op jit(solution)/shard_map/ppermute | solution.py:233
  51.3 6.5 %collective-permute-start.18 = (bf16[64,1152]{1,0:T(8,128)(2,1)S(1)}, bf16[64,1152]{1,0:T(8,128)(2,1)S(1)}, u32[]{:S(2)}, u32[]{:S(2)}) collective-permute-start(bf16[64,1152]{1,0:T(8,128)(2,1)S(1)} %get-tuple-element.58), channel_id=1, source_target_pairs={{0,6},{1,7},{2,4},{3,5},{4,2},{5,3},{6,0},{7,1},{8,14},{9,15},{10,... | collective-permute-start | bytes 442376 | tf_op jit(solution)/shard_map/ppermute | solution.py:256
  51.7 10.5 %collective-permute-start.12 = (bf16[4,16,1152]{2,1,0:T(8,128)(2,1)S(1)}, bf16[4,16,1152]{2,1,0:T(8,128)(2,1)S(1)}, u32[]{:S(2)}, u32[]{:S(2)}) collective-permute-start(bf16[4,16,1152]{2,1,0:T(8,128)(2,1)S(1)} %get-tuple-element.51), channel_id=1, source_target_pairs={{0,4},{4,0},{8,12},{12,8},{16,20},{20,16},{24,28},{28,24},{1,5},{5... | collective-permute-start | bytes 442376 | tf_op jit(solution)/shard_map/ppermute | solution.py:233
  57.8 6.3 %collective-permute-start.19 = (bf16[32,1152]{1,0:T(8,128)(2,1)S(1)}, bf16[32,1152]{1,0:T(8,128)(2,1)S(1)}, u32[]{:S(2)}, u32[]{:S(2)}) collective-permute-start(bf16[32,1152]{1,0:T(8,128)(2,1)S(1)} %get-tuple-element.59), channel_id=1, source_target_pairs={{0,24},{4,28},{8,16},{12,20},{16,8},{20,12},{24,0},{28,4},{1,25},{... | collective-permute-start | bytes 221192 | tf_op jit(solution)/shard_map/ppermute | solution.py:233
  59.1 6.5 %collective-permute-start.20 = (bf16[32,1152]{1,0:T(8,128)(2,1)S(1)}, bf16[32,1152]{1,0:T(8,128)(2,1)S(1)}, u32[]{:S(2)}, u32[]{:S(2)}) collective-permute-start(bf16[32,1152]{1,0:T(8,128)(2,1)S(1)} %get-tuple-element.60), channel_id=1, source_target_pairs={{0,16},{4,20},{8,24},{12,28},{16,0},{20,4},{24,8},{28,12},{1,17},{... | collective-permute-start | bytes 221192 | tf_op jit(solution)/shard_map/ppermute | solution.py:233
  59.1 6.5 %collective-permute-start.21 = (bf16[32,1152]{1,0:T(8,128)(2,1)S(1)}, bf16[32,1152]{1,0:T(8,128)(2,1)S(1)}, u32[]{:S(2)}, u32[]{:S(2)}) collective-permute-start(bf16[32,1152]{1,0:T(8,128)(2,1)S(1)} %get-tuple-element.61), channel_id=1, source_target_pairs={{0,8},{4,12},{8,0},{12,4},{16,24},{20,28},{24,16},{28,20},{1,9},{5... | collective-permute-start | bytes 221192 | tf_op jit(solution)/shard_map/ppermute | solution.py:233

commit v21 on v19

--- a/solution.py
+++ b/solution.py
@@ -313,8 +313,8 @@
         functools.partial(share_kernel, period), (after(tokens, sister),), [halves_shape(BF16)] * 2
     )
     paired = swap(shared, "frame", 1)
-    out_pair = with_sister(spatial_out, near)
     far = both_cores([after(block, near, paired) for block in far])
+    out_pair = with_sister(spatial_out, *far)
 
     columns = (groups - 1) * rows
     far_proj, kept, sent = call(

time: 69.3 us -> 66.5 us (0.960)
  waiting for transfers between devices: 30.5 us -> 27.1 us
    ppermute x21, waiting for transfers between devices: 28.8 us -> 25.4 us  [swap(): return lax.ppermute(value, axis, [(at, at ^ offset) for at in range(size)])]
    ppermute x21, starting transfers between devices: 19.4 us -> 20.3 us  [swap(): return lax.ppermute(value, axis, [(at, at ^ offset) for at in range(size)])]
  transfers between devices with their start and end apart: 23 -> 23, of which waited for: 16 -> 15; matrix products, arithmetic and copies ran while one was open for 0% -> 0% of each run, Pallas kernels for 12% -> 13%
where the time goes in v21:
time: 66.5 us; the launch traced here: 66.2 us
  waiting for transfers between devices  27.1 us (41%)
  starting transfers between devices  23.9 us (36%)
  Pallas kernels  11.7 us (18%)
  local copies, waits for them, and re-layouts  3.34 us (5%)
    ppermute x21, waiting for transfers between devices, swap(): return lax.ppermute(value, axis, [(at, at ^ offset) for at in range(size)])  25.4 us
    ppermute x21, starting transfers between devices, swap(): return lax.ppermute(value, axis, [(at, at ^ offset) for at in range(size)])  20.3 us
    pallas_call x15, Pallas kernels, call(): pl.pallas_call(body, out_shape=outs, in_specs=[pl.BlockSpec(memory_space=...  11.7 us
    ppermute x2, starting transfers between devices, swap_diagonal(): return lax.ppermute(value, ('frame', 'patch'), pairs)  3.58 us
    unnamed x16, local copies, waits for them, and re-layouts  3.34 us
    ppermute x2, waiting for transfers between devices, swap_diagonal(): return lax.ppermute(value, ('frame', 'patch'), pairs)  1.75 us
  transfers between devices with their start and end apart: 23, of which 15 were waited for; matrix products, arithmetic and copies ran while one was open for 0% of the time, Pallas kernels for 13%

profile of v21, /device:TPU:0, one launch (start us, length us, event | category | flops | bytes accessed | tf_op | source)
XLA Modules:
  0.0 66.2 jit_solution(13205078382826545241)
XLA Ops:
  0.5 2.5 %collective-permute-start.2 = (bf16[1,128,1152]{2,1,0:T(8,128)(2,1)}, bf16[1,128,1152]{2,1,0:T(8,128)(2,1)S(1)}, u32[]{:S(2)}, u32[]{:S(2)}) collective-permute-start(bf16[1,128,1152]{2,1,0:T(8,128)(2,1)} %own_ref.1), channel_id=1, source_target_pairs={{0,2},{1,3},{2,0},{3,1},{4,6},{5,7},{6,4},{7,5},{8,10},{9,11},{10,... | collective-permute-start | bytes 884744 | tf_op jit(solution)/shard_map/ppermute | solution.py:248
  3.0 1.0 %copy-done.5 = bf16[1,128,1152]{2,1,0:T(8,128)(2,1)S(1)} copy-done((bf16[1,128,1152]{2,1,0:T(8,128)(2,1)S(1)}, bf16[1,128,1152]{2,1,0:T(8,128)(2,1)}, u32[]{:S(2)}) %copy-start.5) | copy-done | bytes 294936
  4.1 1.8 %collective-permute-start.1 = (bf16[64,1152]{1,0:T(8,128)(2,1)S(1)}, bf16[64,1152]{1,0:T(8,128)(2,1)S(1)}, u32[]{:S(2)}, u32[]{:S(2)}) collective-permute-start(bf16[64,1152]{1,0:T(8,128)(2,1)S(1)} %get-tuple-element.42), channel_id=1, source_target_pairs={{0,4},{4,0},{8,12},{12,8},{16,20},{20,16},{24,28},{28,24},{1,5},{5... | collective-permute-start | bytes 442376 | tf_op jit(solution)/shard_map/ppermute | solution.py:248
  5.9 1.6 %copy-done = bf16[864,1152]{1,0:T(8,128)(2,1)S(1)} copy-done((bf16[864,1152]{1,0:T(8,128)(2,1)S(1)}, bf16[864,1152]{1,0:T(8,128)(2,1)}, u32[]{:S(2)}) %copy-start) | copy-done | bytes 1990680
  7.4 0.8 %copy-done.6 = f32[6,1152]{1,0:T(8,128)S(1)} copy-done((f32[6,1152]{1,0:T(8,128)S(1)}, f32[6,1152]{1,0:T(8,128)}, u32[]{:S(2)}) %copy-start.6) | copy-done | bytes 27672
  8.2 1.1 %shard_map.65.near_ref = f32[864,256]{1,0:T(8,128)S(1)} custom-call(f32[6,1152]{1,0:T(8,128)S(1)} %copy-done.6, bf16[864,1152]{1,0:T(8,128)(2,1)S(1)} %copy-done, bf16[1,128,1152]{2,1,0:T(8,128)(2,1)S(1)} %copy-done.5, bf16[1,128,1152]{2,1,0:T(8,128)(2,1)S(1)} %collective-permute-done.sister_ref), custom_call_target="tpu_custom_call" | custom-call | flops 1 | bytes 1 | tf_op jit(solution)/shard_map/pallas_call | solution.py:235
  9.3 1.6 %collective-permute-done.2.refs_0_ = bf16[1,128,1152]{2,1,0:T(8,128)(2,1)S(1)} collective-permute-done((bf16[1,128,1152]{2,1,0:T(8,128)(2,1)}, bf16[1,128,1152]{2,1,0:T(8,128)(2,1)S(1)}, u32[]{:S(2)}, u32[]{:S(2)}) %collective-permute-start.2) | collective-permute-done | bytes 294944 | tf_op jit(solution)/shard_map/ppermute | solution.py:248
  10.9 1.6 %collective-permute-done.3.refs_1_ = bf16[1,128,1152]{2,1,0:T(8,128)(2,1)S(1)} collective-permute-done((bf16[1,128,1152]{2,1,0:T(8,128)(2,1)S(1)}, bf16[1,128,1152]{2,1,0:T(8,128)(2,1)S(1)}, u32[]{:S(2)}, u32[]{:S(2)}) %collective-permute-start.3) | collective-permute-done | bytes 294944 | tf_op jit(solution)/shard_map/ppermute | solution.py:248
  12.6 2.6 %shard_map.66 = (f32[864,256]{1,0:T(8,128)S(1)}, bf16[288,128]{1,0:T(8,128)(2,1)S(1)}, bf16[288,128]{1,0:T(8,128)(2,1)S(1)}) custom-call(f32[6,1152]{1,0:T(8,128)S(1)} %copy-done.6, bf16[864,1152]{1,0:T(8,128)(2,1)S(1)} %copy-done.1, f32[864,256]{1,0:T(8,128)S(1)} %shard_map.65.near_ref, bf16[1,128,1152]{2,1,0:T(8,128)(2,1)S(1)} %collective-permute-done.2.refs_0_, ...), custom_call_target="tpu_custom_call" | custom-call | flops 1 | bytes 1 | tf_op jit(solution)/shard_map/pallas_call | solution.py:235
  15.6 0.9 %collective-permute-done.4.refs_1_ = bf16[288,128]{1,0:T(8,128)(2,1)S(1)} collective-permute-done((bf16[288,128]{1,0:T(8,128)(2,1)S(1)}, bf16[288,128]{1,0:T(8,128)(2,1)S(1)}, u32[]{:S(2)}, u32[]{:S(2)}) %collective-permute-start.4) | collective-permute-done | bytes 73760 | tf_op jit(solution)/shard_map/ppermute | solution.py:248
  17.4 2.7 %collective-permute-start.8 = (bf16[64,1152]{1,0:T(8,128)(2,1)S(1)}, bf16[64,1152]{1,0:T(8,128)(2,1)S(1)}, u32[]{:S(2)}, u32[]{:S(2)}) collective-permute-start(bf16[64,1152]{1,0:T(8,128)(2,1)S(1)} %get-tuple-element.53), channel_id=1, source_target_pairs={{0,6},{1,7},{2,4},{3,5},{4,2},{5,3},{6,0},{7,1},{8,14},{9,15},{10,... | collective-permute-start | bytes 442376 | tf_op jit(solution)/shard_map/ppermute | solution.py:271
  20.6 1.2 %shard_map.68 = (bf16[288,128]{1,0:T(8,128)(2,1)S(1)}, bf16[288,128]{1,0:T(8,128)(2,1)S(1)}) custom-call(f32[864,256]{1,0:T(8,128)S(1)} %shard_map.65.near_ref, f32[864,256]{1,0:T(8,128)S(1)} %get-tuple-element.49.far_ref), custom_call_target="tpu_custom_call" | custom-call | flops 1 | bytes 1 | tf_op jit(solution)/shard_map/pallas_call | solution.py:235
  21.8 1.3 %collective-permute-done.6.refs_1_ = bf16[288,128]{1,0:T(8,128)(2,1)S(1)} collective-permute-done((bf16[288,128]{1,0:T(8,128)(2,1)S(1)}, bf16[288,128]{1,0:T(8,128)(2,1)S(1)}, u32[]{:S(2)}, u32[]{:S(2)}) %collective-permute-start.6) | collective-permute-done | bytes 73760 | tf_op jit(solution)/shard_map/ppermute | solution.py:248
  24.4 3.1 %collective-permute-done.7.refs_0_ = bf16[64,1152]{1,0:T(8,128)(2,1)S(1)} collective-permute-done((bf16[64,1152]{1,0:T(8,128)(2,1)S(1)}, bf16[64,1152]{1,0:T(8,128)(2,1)S(1)}, u32[]{:S(2)}, u32[]{:S(2)}) %collective-permute-start.7) | collective-permute-done | bytes 147488 | tf_op jit(solution)/shard_map/ppermute | solution.py:248
  27.5 0.6 collective-permute-done.9.head_ref
  28.9 3.7 %collective-permute-start.10 = (bf16[32,1152]{1,0:T(8,128)(2,1)S(1)}, bf16[32,1152]{1,0:T(8,128)(2,1)S(1)}, u32[]{:S(2)}, u32[]{:S(2)}) collective-permute-start(bf16[32,1152]{1,0:T(8,128)(2,1)S(1)} %get-tuple-element.59), channel_id=1, source_target_pairs={{0,24},{4,28},{8,16},{12,20},{16,8},{20,12},{24,0},{28,4},{1,25},{... | collective-permute-start | bytes 221192 | tf_op jit(solution)/shard_map/ppermute | solution.py:248
  32.5 0.8 %collective-permute-start.12 = (bf16[32,1152]{1,0:T(8,128)(2,1)S(1)}, bf16[32,1152]{1,0:T(8,128)(2,1)S(1)}, u32[]{:S(2)}, u32[]{:S(2)}) collective-permute-start(bf16[32,1152]{1,0:T(8,128)(2,1)S(1)} %get-tuple-element.61), channel_id=1, source_target_pairs={{0,8},{4,12},{8,0},{12,4},{16,24},{20,28},{24,16},{28,20},{1,9},{5... | collective-permute-start | bytes 221192 | tf_op jit(solution)/shard_map/ppermute | solution.py:248
  33.3 2.6 %collective-permute-done.10.refs_0_ = bf16[32,1152]{1,0:T(8,128)(2,1)S(1)} collective-permute-done((bf16[32,1152]{1,0:T(8,128)(2,1)S(1)}, bf16[32,1152]{1,0:T(8,128)(2,1)S(1)}, u32[]{:S(2)}, u32[]{:S(2)}) %collective-permute-start.10) | collective-permute-done | bytes 73760 | tf_op jit(solution)/shard_map/ppermute | solution.py:248
  35.9 2.6 %collective-permute-done.11.refs_1_ = bf16[32,1152]{1,0:T(8,128)(2,1)S(1)} collective-permute-done((bf16[32,1152]{1,0:T(8,128)(2,1)S(1)}, bf16[32,1152]{1,0:T(8,128)(2,1)S(1)}, u32[]{:S(2)}, u32[]{:S(2)}) %collective-permute-start.11) | collective-permute-done | bytes 73760 | tf_op jit(solution)/shard_map/ppermute | solution.py:248
  38.5 1.6 %collective-permute-start.16 = (bf16[128,1152]{1,0:T(8,128)(2,1)S(1)}, bf16[128,1152]{1,0:T(8,128)(2,1)S(1)}, u32[]{:S(2)}, u32[]{:S(2)}) collective-permute-start(bf16[128,1152]{1,0:T(8,128)(2,1)S(1)} %shard_map.73.refs_4_), channel_id=1, source_target_pairs={{0,2},{1,3},{2,0},{3,1},{4,6},{5,7},{6,4},{7,5},{8,10},{9,11},{10,... | collective-permute-start | bytes 884744 | tf_op jit(solution)/shard_map/ppermute | solution.py:248
  40.1 1.9 %shard_map.74 = (f32[64,1152]{1,0:T(8,128)S(1)}, bf16[64,576]{1,0:T(8,128)(2,1)S(1)}) custom-call(bf16[864,1152]{1,0:T(8,128)(2,1)S(1)} %copy-done.2, bf16[864,1152]{1,0:T(8,128)(2,1)S(1)} %collective-permute-done.14.refs_1_, bf16[288,1152]{1,0:T(8,128)(2,1)S(1)} %copy-done.4, bf16[288,1152]{1,0:T(8,128)(2,1)S(1)} %collective-permute-done.15.refs_3_.refs_1_, ...), custom_call_target="tpu_custom_call" | custom-call | flops 1 | bytes 1 | tf_op jit(solution)/shard_map/pallas_call | solution.py:235
  42.5 4.1 %collective-permute-done.17.head_ref = bf16[64,576]{1,0:T(8,128)(2,1)S(1)} collective-permute-done((bf16[64,576]{1,0:T(8,128)(2,1)S(1)}, bf16[64,576]{1,0:T(8,128)(2,1)S(1)}, u32[]{:S(2)}, u32[]{:S(2)}) %collective-permute-start.17) | collective-permute-done | bytes 73760 | tf_op jit(solution)/shard_map/ppermute | solution.py:248
  47.5 2.0 %shard_map.76 = (bf16[64,1152]{1,0:T(8,128)(2,1)S(1)}, bf16[64,1152]{1,0:T(8,128)(2,1)S(1)}) custom-call(bf16[864,1152]{1,0:T(8,128)(2,1)S(1)} %copy-done.2, bf16[864,1152]{1,0:T(8,128)(2,1)S(1)} %collective-permute-done.14.refs_1_, bf16[288,1152]{1,0:T(8,128)(2,1)S(1)} %copy-done.4, bf16[288,1152]{1,0:T(8,128)(2,1)S(1)} %collective-permute-done.15.refs_3_.refs_1_, ...), custom_call_target="tpu_custom_call" | custom-call | flops 1 | bytes 1 | tf_op jit(solution)/shard_map/pallas_call | solution.py:235
  49.5 1.6 %collective-permute-start.18 = (bf16[64,1152]{1,0:T(8,128)(2,1)S(1)}, bf16[64,1152]{1,0:T(8,128)(2,1)S(1)}, u32[]{:S(2)}, u32[]{:S(2)}) collective-permute-start(bf16[64,1152]{1,0:T(8,128)(2,1)S(1)} %get-tuple-element.69), channel_id=1, source_target_pairs={{0,2},{1,3},{2,0},{3,1},{4,6},{5,7},{6,4},{7,5},{8,10},{9,11},{10,... | collective-permute-start | bytes 442376 | tf_op jit(solution)/shard_map/ppermute | solution.py:248
  51.1 0.9 %collective-permute-start.19 = (bf16[64,1152]{1,0:T(8,128)(2,1)S(1)}, bf16[64,1152]{1,0:T(8,128)(2,1)S(1)}, u32[]{:S(2)}, u32[]{:S(2)}) collective-permute-start(bf16[64,1152]{1,0:T(8,128)(2,1)S(1)} %get-tuple-element.70), channel_id=1, source_target_pairs={{0,6},{1,7},{2,4},{3,5},{4,2},{5,3},{6,0},{7,1},{8,14},{9,15},{10,... | collective-permute-start | bytes 442376 | tf_op jit(solution)/shard_map/ppermute | solution.py:271
  52.0 1.1 %collective-permute-start.13 = (bf16[4,16,1152]{2,1,0:T(8,128)(2,1)S(1)}, bf16[4,16,1152]{2,1,0:T(8,128)(2,1)S(1)}, u32[]{:S(2)}, u32[]{:S(2)}) collective-permute-start(bf16[4,16,1152]{2,1,0:T(8,128)(2,1)S(1)} %get-tuple-element.63), channel_id=1, source_target_pairs={{0,4},{4,0},{8,12},{12,8},{16,20},{20,16},{24,28},{28,24},{1,5},{5... | collective-permute-start | bytes 442376 | tf_op jit(solution)/shard_map/ppermute | solution.py:248
  53.1 3.9 %collective-permute-done.18.refs_1_ = bf16[64,1152]{1,0:T(8,128)(2,1)S(1)} collective-permute-done((bf16[64,1152]{1,0:T(8,128)(2,1)S(1)}, bf16[64,1152]{1,0:T(8,128)(2,1)S(1)}, u32[]{:S(2)}, u32[]{:S(2)}) %collective-permute-start.18) | collective-permute-done | bytes 147488 | tf_op jit(solution)/shard_map/ppermute | solution.py:248
  57.0 1.3 %collective-permute-done.19.refs_3_ = bf16[64,1152]{1,0:T(8,128)(2,1)S(1)} collective-permute-done((bf16[64,1152]{1,0:T(8,128)(2,1)S(1)}, bf16[64,1152]{1,0:T(8,128)(2,1)S(1)}, u32[]{:S(2)}, u32[]{:S(2)}) %collective-permute-start.19) | collective-permute-done | bytes 147488 | tf_op jit(solution)/shard_map/ppermute | solution.py:271
  58.6 4.2 %collective-permute-start.22 = (bf16[32,1152]{1,0:T(8,128)(2,1)S(1)}, bf16[32,1152]{1,0:T(8,128)(2,1)S(1)}, u32[]{:S(2)}, u32[]{:S(2)}) collective-permute-start(bf16[32,1152]{1,0:T(8,128)(2,1)S(1)} %get-tuple-element.73), channel_id=1, source_target_pairs={{0,8},{4,12},{8,0},{12,4},{16,24},{20,28},{24,16},{28,20},{1,9},{5... | collective-permute-start | bytes 221192 | tf_op jit(solution)/shard_map/ppermute | solution.py:248
  62.7 1.9 %collective-permute-done.20.refs_0_ = bf16[32,1152]{1,0:T(8,128)(2,1)S(1)} collective-permute-done((bf16[32,1152]{1,0:T(8,128)(2,1)S(1)}, bf16[32,1152]{1,0:T(8,128)(2,1)S(1)}, u32[]{:S(2)}, u32[]{:S(2)}) %collective-permute-start.20) | collective-permute-done | bytes 73760 | tf_op jit(solution)/shard_map/ppermute | solution.py:248
  64.6 0.8 %collective-permute-done.22.refs_2_ = bf16[32,1152]{1,0:T(8,128)(2,1)S(1)} collective-permute-done((bf16[32,1152]{1,0:T(8,128)(2,1)S(1)}, bf16[32,1152]{1,0:T(8,128)(2,1)S(1)}, u32[]{:S(2)}, u32[]{:S(2)}) %collective-permute-start.22) | collective-permute-done | bytes 73760 | tf_op jit(solution)/shard_map/ppermute | solution.py:248
  65.4 0.8 %shard_map.78 = bf16[8,16,1152]{2,1,0:T(8,128)(2,1)} custom-call(f32[6,1152]{1,0:T(8,128)S(1)} %copy-done.7, bf16[4,16,1152]{2,1,0:T(8,128)(2,1)S(1)} %get-tuple-element.57.kept_ref, bf16[4,16,1152]{2,1,0:T(8,128)(2,1)S(1)} %collective-permute-done.13.other_ref, bf16[32,1152]{1,0:T(8,128)(2,1)S(1)} %collective-permute-done.20.refs_0_, ...), custom_call_target="tpu_custom_call" | custom-call | flops 1 | bytes 1 | tf_op jit(solution)/shard_map/pallas_call | solution.py:235
  (45 shorter events, 6.4 us)
Async XLA Ops:
  0.0 3.0 %collective-permute-start = (bf16[1,128,1152]{2,1,0:T(8,128)(2,1)}, bf16[1,128,1152]{2,1,0:T(8,128)(2,1)S(1)}, u32[]{:S(2)}, u32[]{:S(2)}) collective-permute-start(bf16[1,128,1152]{2,1,0:T(8,128)(2,1)} %own_ref.1), channel_id=1, source_target_pairs={{0,1},{1,0},{2,3},{3,2},{4,5},{5,4},{6,7},{7,6},{8,9},{9,8},{10,11... | collective-permute-start | bytes 884744 | tf_op jit(solution)/shard_map/ppermute | solution.py:248
  0.5 10.4 %collective-permute-start.2 = (bf16[1,128,1152]{2,1,0:T(8,128)(2,1)}, bf16[1,128,1152]{2,1,0:T(8,128)(2,1)S(1)}, u32[]{:S(2)}, u32[]{:S(2)}) collective-permute-start(bf16[1,128,1152]{2,1,0:T(8,128)(2,1)} %own_ref.1), channel_id=1, source_target_pairs={{0,2},{1,3},{2,0},{3,1},{4,6},{5,7},{6,4},{7,5},{8,10},{9,11},{10,... | collective-permute-start | bytes 884744 | tf_op jit(solution)/shard_map/ppermute | solution.py:248
  3.0 1.0 %copy-start.5 = (bf16[1,128,1152]{2,1,0:T(8,128)(2,1)S(1)}, bf16[1,128,1152]{2,1,0:T(8,128)(2,1)}, u32[]{:S(2)}) copy-start(bf16[1,128,1152]{2,1,0:T(8,128)(2,1)} %own_ref.1) | copy-start | bytes 884740
  4.1 6.8 %collective-permute-start.1 = (bf16[64,1152]{1,0:T(8,128)(2,1)S(1)}, bf16[64,1152]{1,0:T(8,128)(2,1)S(1)}, u32[]{:S(2)}, u32[]{:S(2)}) collective-permute-start(bf16[64,1152]{1,0:T(8,128)(2,1)S(1)} %get-tuple-element.42), channel_id=1, source_target_pairs={{0,4},{4,0},{8,12},{12,8},{16,20},{20,16},{24,28},{28,24},{1,5},{5... | collective-permute-start | bytes 442376 | tf_op jit(solution)/shard_map/ppermute | solution.py:248
  5.8 1.6 %copy-start = (bf16[864,1152]{1,0:T(8,128)(2,1)S(1)}, bf16[864,1152]{1,0:T(8,128)(2,1)}, u32[]{:S(2)}) copy-start(bf16[864,1152]{1,0:T(8,128)(2,1)} %weight_ref.3) | copy-start | bytes 5971972
  7.4 0.8 %copy-start.6 = (f32[6,1152]{1,0:T(8,128)S(1)}, f32[6,1152]{1,0:T(8,128)}, u32[]{:S(2)}) copy-start(f32[6,1152]{1,0:T(8,128)} %mod_ref.7) | copy-start | bytes 82948
  8.2 4.3 %copy-start.3 = (bf16[288,1152]{1,0:T(8,128)(2,1)S(1)}, bf16[288,1152]{1,0:T(8,128)(2,1)}, u32[]{:S(2)}) copy-start(bf16[288,1152]{1,0:T(8,128)(2,1)} %refs_0_.4) | copy-start | bytes 1990660
  8.2 4.4 %copy-start.1 = (bf16[864,1152]{1,0:T(8,128)(2,1)S(1)}, bf16[864,1152]{1,0:T(8,128)(2,1)}, u32[]{:S(2)}) copy-start(bf16[864,1152]{1,0:T(8,128)(2,1)} %weight_ref.3) | copy-start | bytes 5971972
  9.3 7.7 %copy-start.2 = (bf16[864,1152]{1,0:T(8,128)(2,1)S(1)}, bf16[864,1152]{1,0:T(8,128)(2,1)}, u32[]{:S(2)}) copy-start(bf16[864,1152]{1,0:T(8,128)(2,1)} %refs_0_.7) | copy-start | bytes 5971972
  10.9 1.6 %collective-permute-start.3 = (bf16[1,128,1152]{2,1,0:T(8,128)(2,1)S(1)}, bf16[1,128,1152]{2,1,0:T(8,128)(2,1)S(1)}, u32[]{:S(2)}, u32[]{:S(2)}) collective-permute-start(bf16[1,128,1152]{2,1,0:T(8,128)(2,1)S(1)} %collective-permute-done.2.refs_0_), channel_id=1, source_target_pairs={{0,1},{1,0},{2,3},{3,2},{4,5},{5,4},{6,7},{7,6},{8,9},{9,8},{10,11... | collective-permute-start | bytes 884744 | tf_op jit(solution)/shard_map/ppermute | solution.py:248
  12.4 4.1 %collective-permute-start.5 = (bf16[288,1152]{1,0:T(8,128)(2,1)S(1)}, bf16[288,1152]{1,0:T(8,128)(2,1)S(1)}, u32[]{:S(2)}, u32[]{:S(2)}) collective-permute-start(bf16[288,1152]{1,0:T(8,128)(2,1)S(1)} %copy-done.3), channel_id=1, source_target_pairs={{0,1},{1,0},{2,3},{3,2},{4,5},{5,4},{6,7},{7,6},{8,9},{9,8},{10,11... | collective-permute-start | bytes 1990664 | tf_op jit(solution)/shard_map/ppermute | solution.py:248
  15.2 1.4 %collective-permute-start.4 = (bf16[288,128]{1,0:T(8,128)(2,1)S(1)}, bf16[288,128]{1,0:T(8,128)(2,1)S(1)}, u32[]{:S(2)}, u32[]{:S(2)}) collective-permute-start(bf16[288,128]{1,0:T(8,128)(2,1)S(1)} %get-tuple-element.45), channel_id=1, source_target_pairs={{0,1},{1,0},{2,3},{3,2},{4,5},{5,4},{6,7},{7,6},{8,9},{9,8},{10,11... | collective-permute-start | bytes 221192 | tf_op jit(solution)/shard_map/ppermute | solution.py:248
  17.0 6.9 %copy-start.4 = (bf16[288,1152]{1,0:T(8,128)(2,1)S(1)}, bf16[288,1152]{1,0:T(8,128)(2,1)}, u32[]{:S(2)}) copy-start(bf16[288,1152]{1,0:T(8,128)(2,1)} %refs_2_.7) | copy-start | bytes 1990660
  17.0 23.1 %collective-permute-start.14 = (bf16[864,1152]{1,0:T(8,128)(2,1)S(1)}, bf16[864,1152]{1,0:T(8,128)(2,1)S(1)}, u32[]{:S(2)}, u32[]{:S(2)}) collective-permute-start(bf16[864,1152]{1,0:T(8,128)(2,1)S(1)} %copy-done.2), channel_id=1, source_target_pairs={{0,1},{1,0},{2,3},{3,2},{4,5},{5,4},{6,7},{7,6},{8,9},{9,8},{10,11... | collective-permute-start | bytes 5971976 | tf_op jit(solution)/shard_map/ppermute | solution.py:248
  17.4 6.9 %collective-permute-start.8 = (bf16[64,1152]{1,0:T(8,128)(2,1)S(1)}, bf16[64,1152]{1,0:T(8,128)(2,1)S(1)}, u32[]{:S(2)}, u32[]{:S(2)}) collective-permute-start(bf16[64,1152]{1,0:T(8,128)(2,1)S(1)} %get-tuple-element.53), channel_id=1, source_target_pairs={{0,6},{1,7},{2,4},{3,5},{4,2},{5,3},{6,0},{7,1},{8,14},{9,15},{10,... | collective-permute-start | bytes 442376 | tf_op jit(solution)/shard_map/ppermute | solution.py:271
  20.1 7.3 %collective-permute-start.7 = (bf16[64,1152]{1,0:T(8,128)(2,1)S(1)}, bf16[64,1152]{1,0:T(8,128)(2,1)S(1)}, u32[]{:S(2)}, u32[]{:S(2)}) collective-permute-start(bf16[64,1152]{1,0:T(8,128)(2,1)S(1)} %get-tuple-element.47), channel_id=1, source_target_pairs={{0,2},{1,3},{2,0},{3,1},{4,6},{5,7},{6,4},{7,5},{8,10},{9,11},{10,... | collective-permute-start | bytes 442376 | tf_op jit(solution)/shard_map/ppermute | solution.py:248
  21.8 1.3 %collective-permute-start.6 = (bf16[288,128]{1,0:T(8,128)(2,1)S(1)}, bf16[288,128]{1,0:T(8,128)(2,1)S(1)}, u32[]{:S(2)}, u32[]{:S(2)}) collective-permute-start(bf16[288,128]{1,0:T(8,128)(2,1)S(1)} %get-tuple-element.51), channel_id=1, source_target_pairs={{0,1},{1,0},{2,3},{3,2},{4,5},{5,4},{6,7},{7,6},{8,9},{9,8},{10,11... | collective-permute-start | bytes 221192 | tf_op jit(solution)/shard_map/ppermute | solution.py:248
  23.5 5.0 %copy-start.7 = (f32[6,1152]{1,0:T(8,128)S(1)}, f32[6,1152]{1,0:T(8,128)}, u32[]{:S(2)}) copy-start(f32[6,1152]{1,0:T(8,128)} %mod_ref.7) | copy-start | bytes 82948
  23.5 4.6 %collective-permute-start.9 = (bf16[64,576]{1,0:T(8,128)(2,1)S(1)}, bf16[64,576]{1,0:T(8,128)(2,1)S(1)}, u32[]{:S(2)}, u32[]{:S(2)}) collective-permute-start(bf16[64,576]{1,0:T(8,128)(2,1)S(1)} %get-tuple-element.55), channel_id=1, source_target_pairs={{0,4},{4,0},{8,12},{12,8},{16,20},{20,16},{24,28},{28,24},{1,5},{5... | collective-permute-start | bytes 221192 | tf_op jit(solution)/shard_map/ppermute | solution.py:248
  23.9 16.2 %collective-permute-start.15 = (bf16[288,1152]{1,0:T(8,128)(2,1)S(1)}, bf16[288,1152]{1,0:T(8,128)(2,1)S(1)}, u32[]{:S(2)}, u32[]{:S(2)}) collective-permute-start(bf16[288,1152]{1,0:T(8,128)(2,1)S(1)} %copy-done.4), channel_id=1, source_target_pairs={{0,1},{1,0},{2,3},{3,2},{4,5},{5,4},{6,7},{7,6},{8,9},{9,8},{10,11... | collective-permute-start | bytes 1990664 | tf_op jit(solution)/shard_map/ppermute | solution.py:248
  28.9 7.1 %collective-permute-start.10 = (bf16[32,1152]{1,0:T(8,128)(2,1)S(1)}, bf16[32,1152]{1,0:T(8,128)(2,1)S(1)}, u32[]{:S(2)}, u32[]{:S(2)}) collective-permute-start(bf16[32,1152]{1,0:T(8,128)(2,1)S(1)} %get-tuple-element.59), channel_id=1, source_target_pairs={{0,24},{4,28},{8,16},{12,20},{16,8},{20,12},{24,0},{28,4},{1,25},{... | collective-permute-start | bytes 221192 | tf_op jit(solution)/shard_map/ppermute | solution.py:248
  32.5 6.0 %collective-permute-start.11 = (bf16[32,1152]{1,0:T(8,128)(2,1)S(1)}, bf16[32,1152]{1,0:T(8,128)(2,1)S(1)}, u32[]{:S(2)}, u32[]{:S(2)}) collective-permute-start(bf16[32,1152]{1,0:T(8,128)(2,1)S(1)} %get-tuple-element.60), channel_id=1, source_target_pairs={{0,16},{4,20},{8,24},{12,28},{16,0},{20,4},{24,8},{28,12},{1,17},{... | collective-permute-start | bytes 221192 | tf_op jit(solution)/shard_map/ppermute | solution.py:248
  32.5 6.0 %collective-permute-start.12 = (bf16[32,1152]{1,0:T(8,128)(2,1)S(1)}, bf16[32,1152]{1,0:T(8,128)(2,1)S(1)}, u32[]{:S(2)}, u32[]{:S(2)}) collective-permute-start(bf16[32,1152]{1,0:T(8,128)(2,1)S(1)} %get-tuple-element.61), channel_id=1, source_target_pairs={{0,8},{4,12},{8,0},{12,4},{16,24},{20,28},{24,16},{28,20},{1,9},{5... | collective-permute-start | bytes 221192 | tf_op jit(solution)/shard_map/ppermute | solution.py:248
  38.5 9.0 %collective-permute-start.16 = (bf16[128,1152]{1,0:T(8,128)(2,1)S(1)}, bf16[128,1152]{1,0:T(8,128)(2,1)S(1)}, u32[]{:S(2)}, u32[]{:S(2)}) collective-permute-start(bf16[128,1152]{1,0:T(8,128)(2,1)S(1)} %shard_map.73.refs_4_), channel_id=1, source_target_pairs={{0,2},{1,3},{2,0},{3,1},{4,6},{5,7},{6,4},{7,5},{8,10},{9,11},{10,... | collective-permute-start | bytes 884744 | tf_op jit(solution)/shard_map/ppermute | solution.py:248
  42.1 4.5 %collective-permute-start.17 = (bf16[64,576]{1,0:T(8,128)(2,1)S(1)}, bf16[64,576]{1,0:T(8,128)(2,1)S(1)}, u32[]{:S(2)}, u32[]{:S(2)}) collective-permute-start(bf16[64,576]{1,0:T(8,128)(2,1)S(1)} %get-tuple-element.67), channel_id=1, source_target_pairs={{0,4},{4,0},{8,12},{12,8},{16,20},{20,16},{24,28},{28,24},{1,5},{5... | collective-permute-start | bytes 221192 | tf_op jit(solution)/shard_map/ppermute | solution.py:248
  49.5 7.5 %collective-permute-start.18 = (bf16[64,1152]{1,0:T(8,128)(2,1)S(1)}, bf16[64,1152]{1,0:T(8,128)(2,1)S(1)}, u32[]{:S(2)}, u32[]{:S(2)}) collective-permute-start(bf16[64,1152]{1,0:T(8,128)(2,1)S(1)} %get-tuple-element.69), channel_id=1, source_target_pairs={{0,2},{1,3},{2,0},{3,1},{4,6},{5,7},{6,4},{7,5},{8,10},{9,11},{10,... | collective-permute-start | bytes 442376 | tf_op jit(solution)/shard_map/ppermute | solution.py:248
  51.1 7.2 %collective-permute-start.19 = (bf16[64,1152]{1,0:T(8,128)(2,1)S(1)}, bf16[64,1152]{1,0:T(8,128)(2,1)S(1)}, u32[]{:S(2)}, u32[]{:S(2)}) collective-permute-start(bf16[64,1152]{1,0:T(8,128)(2,1)S(1)} %get-tuple-element.70), channel_id=1, source_target_pairs={{0,6},{1,7},{2,4},{3,5},{4,2},{5,3},{6,0},{7,1},{8,14},{9,15},{10,... | collective-permute-start | bytes 442376 | tf_op jit(solution)/shard_map/ppermute | solution.py:271
  52.0 10.8 %collective-permute-start.13 = (bf16[4,16,1152]{2,1,0:T(8,128)(2,1)S(1)}, bf16[4,16,1152]{2,1,0:T(8,128)(2,1)S(1)}, u32[]{:S(2)}, u32[]{:S(2)}) collective-permute-start(bf16[4,16,1152]{2,1,0:T(8,128)(2,1)S(1)} %get-tuple-element.63), channel_id=1, source_target_pairs={{0,4},{4,0},{8,12},{12,8},{16,20},{20,16},{24,28},{28,24},{1,5},{5... | collective-permute-start | bytes 442376 | tf_op jit(solution)/shard_map/ppermute | solution.py:248
  58.3 6.3 %collective-permute-start.20 = (bf16[32,1152]{1,0:T(8,128)(2,1)S(1)}, bf16[32,1152]{1,0:T(8,128)(2,1)S(1)}, u32[]{:S(2)}, u32[]{:S(2)}) collective-permute-start(bf16[32,1152]{1,0:T(8,128)(2,1)S(1)} %get-tuple-element.71), channel_id=1, source_target_pairs={{0,24},{4,28},{8,16},{12,20},{16,8},{20,12},{24,0},{28,4},{1,25},{... | collective-permute-start | bytes 221192 | tf_op jit(solution)/shard_map/ppermute | solution.py:248
  58.6 6.1 %collective-permute-start.21 = (bf16[32,1152]{1,0:T(8,128)(2,1)S(1)}, bf16[32,1152]{1,0:T(8,128)(2,1)S(1)}, u32[]{:S(2)}, u32[]{:S(2)}) collective-permute-start(bf16[32,1152]{1,0:T(8,128)(2,1)S(1)} %get-tuple-element.72), channel_id=1, source_target_pairs={{0,16},{4,20},{8,24},{12,28},{16,0},{20,4},{24,8},{28,12},{1,17},{... | collective-permute-start | bytes 221192 | tf_op jit(solution)/shard_map/ppermute | solution.py:248
  58.6 6.8 %collective-permute-start.22 = (bf16[32,1152]{1,0:T(8,128)(2,1)S(1)}, bf16[32,1152]{1,0:T(8,128)(2,1)S(1)}, u32[]{:S(2)}, u32[]{:S(2)}) collective-permute-start(bf16[32,1152]{1,0:T(8,128)(2,1)S(1)} %get-tuple-element.73), channel_id=1, source_target_pairs={{0,8},{4,12},{8,0},{12,4},{16,24},{20,28},{24,16},{28,20},{1,9},{5... | collective-permute-start | bytes 221192 | tf_op jit(solution)/shard_map/ppermute | solution.py:248

commit v22 on v16

--- a/solution.py
+++ b/solution.py
@@ -19,7 +19,7 @@
     centred = values - average
     variance = jnp.mean(centred * centred, axis=-1, keepdims=True)
     normed = centred * lax.rsqrt(variance + 1e-06)
-    return (normed * (1.0 + scale) + shift).astype(BF16)
+    return (normed * (1.0 + shift * 0.0 + scale) + shift).astype(BF16)
 
 
 def dot(left, right, left_dim=1, right_dim=0):

time: 65.8 us -> 65.7 us (level)
  no operation moved by 1% of the time
where the time goes in v22:
time: 65.7 us; the launch traced here: 65.5 us
  waiting for transfers between devices  26 us (40%)
  starting transfers between devices  24.9 us (38%)
  Pallas kernels  11.1 us (17%)
  local copies, waits for them, and re-layouts  3.34 us (5%)
    ppermute x20, waiting for transfers between devices, swap(): return lax.ppermute(value, axis, [(at, at ^ offset) for at in range(size)])  24.8 us
    ppermute x20, starting transfers between devices, swap(): return lax.ppermute(value, axis, [(at, at ^ offset) for at in range(size)])  22 us
    pallas_call x12, Pallas kernels, call(): pl.pallas_call(body, out_shape=outs, in_specs=[pl.BlockSpec(memory_space=...  11.1 us
    unnamed x16, local copies, waits for them, and re-layouts  3.34 us
    ppermute x2, starting transfers between devices, swap_diagonal(): return lax.ppermute(value, ('frame', 'patch'), pairs)  2.86 us
  transfers between devices with their start and end apart: 22, of which 11 were waited for; matrix products, arithmetic and copies ran while one was open for 0% of the time, Pallas kernels for 13%

profile of v22, /device:TPU:0, one launch (start us, length us, event | category | flops | bytes accessed | tf_op | source)
XLA Modules:
  0.0 65.5 jit_solution(15753822622831843929)
XLA Ops:
  0.5 2.5 %collective-permute-start.2 = (bf16[1,128,1152]{2,1,0:T(8,128)(2,1)}, bf16[1,128,1152]{2,1,0:T(8,128)(2,1)S(1)}, u32[]{:S(2)}, u32[]{:S(2)}) collective-permute-start(bf16[1,128,1152]{2,1,0:T(8,128)(2,1)} %own_ref.1), channel_id=1, source_target_pairs={{0,2},{1,3},{2,0},{3,1},{4,6},{5,7},{6,4},{7,5},{8,10},{9,11},{10,... | collective-permute-start | bytes 884744 | tf_op jit(solution)/shard_map/ppermute | solution.py:233
  3.0 1.0 %copy-done.5 = bf16[1,128,1152]{2,1,0:T(8,128)(2,1)S(1)} copy-done((bf16[1,128,1152]{2,1,0:T(8,128)(2,1)S(1)}, bf16[1,128,1152]{2,1,0:T(8,128)(2,1)}, u32[]{:S(2)}) %copy-start.5) | copy-done | bytes 294936
  4.1 1.8 %collective-permute-start.1 = (bf16[64,1152]{1,0:T(8,128)(2,1)S(1)}, bf16[64,1152]{1,0:T(8,128)(2,1)S(1)}, u32[]{:S(2)}, u32[]{:S(2)}) collective-permute-start(bf16[64,1152]{1,0:T(8,128)(2,1)S(1)} %get-tuple-element.36), channel_id=1, source_target_pairs={{0,4},{4,0},{8,12},{12,8},{16,20},{20,16},{24,28},{28,24},{1,5},{5... | collective-permute-start | bytes 442376 | tf_op jit(solution)/shard_map/ppermute | solution.py:233
  5.9 1.6 %copy-done = bf16[864,1152]{1,0:T(8,128)(2,1)S(1)} copy-done((bf16[864,1152]{1,0:T(8,128)(2,1)S(1)}, bf16[864,1152]{1,0:T(8,128)(2,1)}, u32[]{:S(2)}) %copy-start) | copy-done | bytes 1990680
  7.4 0.8 %copy-done.6 = f32[6,1152]{1,0:T(8,128)S(1)} copy-done((f32[6,1152]{1,0:T(8,128)S(1)}, f32[6,1152]{1,0:T(8,128)}, u32[]{:S(2)}) %copy-start.6) | copy-done | bytes 27672
  8.2 1.1 %shard_map.65.near_ref = f32[864,256]{1,0:T(8,128)S(1)} custom-call(f32[6,1152]{1,0:T(8,128)S(1)} %copy-done.6, bf16[864,1152]{1,0:T(8,128)(2,1)S(1)} %copy-done, bf16[1,128,1152]{2,1,0:T(8,128)(2,1)S(1)} %copy-done.5, bf16[1,128,1152]{2,1,0:T(8,128)(2,1)S(1)} %collective-permute-done.sister_ref), custom_call_target="tpu_custom_call" | custom-call | flops 1 | bytes 1 | tf_op jit(solution)/shard_map/pallas_call | solution.py:220
  9.3 1.6 %collective-permute-done.2.refs_0_ = bf16[1,128,1152]{2,1,0:T(8,128)(2,1)S(1)} collective-permute-done((bf16[1,128,1152]{2,1,0:T(8,128)(2,1)}, bf16[1,128,1152]{2,1,0:T(8,128)(2,1)S(1)}, u32[]{:S(2)}, u32[]{:S(2)}) %collective-permute-start.2) | collective-permute-done | bytes 294944 | tf_op jit(solution)/shard_map/ppermute | solution.py:233
  10.9 1.6 %collective-permute-done.3.refs_1_ = bf16[1,128,1152]{2,1,0:T(8,128)(2,1)S(1)} collective-permute-done((bf16[1,128,1152]{2,1,0:T(8,128)(2,1)S(1)}, bf16[1,128,1152]{2,1,0:T(8,128)(2,1)S(1)}, u32[]{:S(2)}, u32[]{:S(2)}) %collective-permute-start.3) | collective-permute-done | bytes 294944 | tf_op jit(solution)/shard_map/ppermute | solution.py:233
  13.0 3.3 %shard_map.66 = (bf16[288,256]{1,0:T(8,128)(2,1)S(1)}, bf16[288,256]{1,0:T(8,128)(2,1)S(1)}) custom-call(f32[6,1152]{1,0:T(8,128)S(1)} %copy-done.6, bf16[864,1152]{1,0:T(8,128)(2,1)S(1)} %copy-done.1, f32[864,256]{1,0:T(8,128)S(1)} %shard_map.65.near_ref, bf16[1,128,1152]{2,1,0:T(8,128)(2,1)S(1)} %collective-permute-done.2.refs_0_, ...), custom_call_target="tpu_custom_call" | custom-call | flops 1 | bytes 1 | tf_op jit(solution)/shard_map/pallas_call | solution.py:220
  16.5 1.2 %collective-permute-done.4.refs_1_ = bf16[288,256]{1,0:T(8,128)(2,1)S(1)} collective-permute-done((bf16[288,256]{1,0:T(8,128)(2,1)S(1)}, bf16[288,256]{1,0:T(8,128)(2,1)S(1)}, u32[]{:S(2)}, u32[]{:S(2)}) %collective-permute-start.4) | collective-permute-done | bytes 147488 | tf_op jit(solution)/shard_map/ppermute | solution.py:233
  17.7 0.7 %shard_map.67 = (f32[64,1152]{1,0:T(8,128)S(1)}, bf16[64,576]{1,0:T(8,128)(2,1)S(1)}, bf16[64,1152]{1,0:T(8,128)(2,1)S(1)}, bf16[64,1152]{1,0:T(8,128)(2,1)S(1)}) custom-call(bf16[288,256]{1,0:T(8,128)(2,1)S(1)} %get-tuple-element.38.refs_0_, bf16[288,256]{1,0:T(8,128)(2,1)S(1)} %collective-permute-done.4.refs_1_, bf16[288,1152]{1,0:T(8,128)(2,1)S(1)} %copy-done.4, ...), custom_call_target="tpu_custom_call" | custom-call | flops 1 | bytes 1 | tf_op jit(solution)/shard_map/pallas_call | solution.py:220
  18.7 1.8 %collective-permute-start.6 = (bf16[64,1152]{1,0:T(8,128)(2,1)S(1)}, bf16[64,1152]{1,0:T(8,128)(2,1)S(1)}, u32[]{:S(2)}, u32[]{:S(2)}) collective-permute-start(bf16[64,1152]{1,0:T(8,128)(2,1)S(1)} %get-tuple-element.42), channel_id=1, source_target_pairs={{0,2},{1,3},{2,0},{3,1},{4,6},{5,7},{6,4},{7,5},{8,10},{9,11},{10,... | collective-permute-start | bytes 442376 | tf_op jit(solution)/shard_map/ppermute | solution.py:233
  20.5 1.4 %collective-permute-start.8 = (bf16[64,1152]{1,0:T(8,128)(2,1)S(1)}, bf16[64,1152]{1,0:T(8,128)(2,1)S(1)}, u32[]{:S(2)}, u32[]{:S(2)}) collective-permute-start(bf16[64,1152]{1,0:T(8,128)(2,1)S(1)} %get-tuple-element.44), channel_id=1, source_target_pairs={{0,6},{1,7},{2,4},{3,5},{4,2},{5,3},{6,0},{7,1},{8,14},{9,15},{10,... | collective-permute-start | bytes 442376 | tf_op jit(solution)/shard_map/ppermute | solution.py:256
  22.2 5.6 %collective-permute-done.7.head_ref = bf16[64,576]{1,0:T(8,128)(2,1)S(1)} collective-permute-done((bf16[64,576]{1,0:T(8,128)(2,1)S(1)}, bf16[64,576]{1,0:T(8,128)(2,1)S(1)}, u32[]{:S(2)}, u32[]{:S(2)}) %collective-permute-start.7) | collective-permute-done | bytes 73760 | tf_op jit(solution)/shard_map/ppermute | solution.py:233
  28.6 3.9 %collective-permute-start.9 = (bf16[32,1152]{1,0:T(8,128)(2,1)S(1)}, bf16[32,1152]{1,0:T(8,128)(2,1)S(1)}, u32[]{:S(2)}, u32[]{:S(2)}) collective-permute-start(bf16[32,1152]{1,0:T(8,128)(2,1)S(1)} %get-tuple-element.47), channel_id=1, source_target_pairs={{0,24},{4,28},{8,16},{12,20},{16,8},{20,12},{24,0},{28,4},{1,25},{... | collective-permute-start | bytes 221192 | tf_op jit(solution)/shard_map/ppermute | solution.py:233
  32.5 0.6 collective-permute-start.11
  33.1 2.5 %collective-permute-done.9.refs_0_ = bf16[32,1152]{1,0:T(8,128)(2,1)S(1)} collective-permute-done((bf16[32,1152]{1,0:T(8,128)(2,1)S(1)}, bf16[32,1152]{1,0:T(8,128)(2,1)S(1)}, u32[]{:S(2)}, u32[]{:S(2)}) %collective-permute-start.9) | collective-permute-done | bytes 73760 | tf_op jit(solution)/shard_map/ppermute | solution.py:233
  35.6 2.7 %collective-permute-done.10.refs_1_ = bf16[32,1152]{1,0:T(8,128)(2,1)S(1)} collective-permute-done((bf16[32,1152]{1,0:T(8,128)(2,1)S(1)}, bf16[32,1152]{1,0:T(8,128)(2,1)S(1)}, u32[]{:S(2)}, u32[]{:S(2)}) %collective-permute-start.10) | collective-permute-done | bytes 73760 | tf_op jit(solution)/shard_map/ppermute | solution.py:233
  38.3 1.6 %collective-permute-start.15 = (bf16[128,1152]{1,0:T(8,128)(2,1)S(1)}, bf16[128,1152]{1,0:T(8,128)(2,1)S(1)}, u32[]{:S(2)}, u32[]{:S(2)}) collective-permute-start(bf16[128,1152]{1,0:T(8,128)(2,1)S(1)} %shard_map.70.refs_4_), channel_id=1, source_target_pairs={{0,2},{1,3},{2,0},{3,1},{4,6},{5,7},{6,4},{7,5},{8,10},{9,11},{10,... | collective-permute-start | bytes 884744 | tf_op jit(solution)/shard_map/ppermute | solution.py:233
  39.9 1.9 %shard_map.71 = (f32[64,1152]{1,0:T(8,128)S(1)}, bf16[64,576]{1,0:T(8,128)(2,1)S(1)}) custom-call(bf16[864,1152]{1,0:T(8,128)(2,1)S(1)} %copy-done.2, bf16[864,1152]{1,0:T(8,128)(2,1)S(1)} %collective-permute-done.13.refs_1_, bf16[288,1152]{1,0:T(8,128)(2,1)S(1)} %copy-done.3, bf16[288,1152]{1,0:T(8,128)(2,1)S(1)} %collective-permute-done.14.refs_3_.refs_1_, ...), custom_call_target="tpu_custom_call" | custom-call | flops 1 | bytes 1 | tf_op jit(solution)/shard_map/pallas_call | solution.py:220
  41.9 1.6 %collective-permute-start.16 = (bf16[64,576]{1,0:T(8,128)(2,1)S(1)}, bf16[64,576]{1,0:T(8,128)(2,1)S(1)}, u32[]{:S(2)}, u32[]{:S(2)}) collective-permute-start(bf16[64,576]{1,0:T(8,128)(2,1)S(1)} %get-tuple-element.55), channel_id=1, source_target_pairs={{0,4},{4,0},{8,12},{12,8},{16,20},{20,16},{24,28},{28,24},{1,5},{5... | collective-permute-start | bytes 221192 | tf_op jit(solution)/shard_map/ppermute | solution.py:233
  43.4 2.9 %collective-permute-done.16.head_ref = bf16[64,576]{1,0:T(8,128)(2,1)S(1)} collective-permute-done((bf16[64,576]{1,0:T(8,128)(2,1)S(1)}, bf16[64,576]{1,0:T(8,128)(2,1)S(1)}, u32[]{:S(2)}, u32[]{:S(2)}) %collective-permute-start.16) | collective-permute-done | bytes 73760 | tf_op jit(solution)/shard_map/ppermute | solution.py:233
  46.7 2.0 %shard_map.73 = (bf16[64,1152]{1,0:T(8,128)(2,1)S(1)}, bf16[64,1152]{1,0:T(8,128)(2,1)S(1)}) custom-call(bf16[864,1152]{1,0:T(8,128)(2,1)S(1)} %copy-done.2, bf16[864,1152]{1,0:T(8,128)(2,1)S(1)} %collective-permute-done.13.refs_1_, bf16[288,1152]{1,0:T(8,128)(2,1)S(1)} %copy-done.3, bf16[288,1152]{1,0:T(8,128)(2,1)S(1)} %collective-permute-done.14.refs_3_.refs_1_, ...), custom_call_target="tpu_custom_call" | custom-call | flops 1 | bytes 1 | tf_op jit(solution)/shard_map/pallas_call | solution.py:220
  48.7 1.6 %collective-permute-start.17 = (bf16[64,1152]{1,0:T(8,128)(2,1)S(1)}, bf16[64,1152]{1,0:T(8,128)(2,1)S(1)}, u32[]{:S(2)}, u32[]{:S(2)}) collective-permute-start(bf16[64,1152]{1,0:T(8,128)(2,1)S(1)} %get-tuple-element.57), channel_id=1, source_target_pairs={{0,2},{1,3},{2,0},{3,1},{4,6},{5,7},{6,4},{7,5},{8,10},{9,11},{10,... | collective-permute-start | bytes 442376 | tf_op jit(solution)/shard_map/ppermute | solution.py:233
  50.3 1.4 %collective-permute-start.18 = (bf16[64,1152]{1,0:T(8,128)(2,1)S(1)}, bf16[64,1152]{1,0:T(8,128)(2,1)S(1)}, u32[]{:S(2)}, u32[]{:S(2)}) collective-permute-start(bf16[64,1152]{1,0:T(8,128)(2,1)S(1)} %get-tuple-element.58), channel_id=1, source_target_pairs={{0,6},{1,7},{2,4},{3,5},{4,2},{5,3},{6,0},{7,1},{8,14},{9,15},{10,... | collective-permute-start | bytes 442376 | tf_op jit(solution)/shard_map/ppermute | solution.py:256
  52.3 3.3 %collective-permute-done.17.refs_1_ = bf16[64,1152]{1,0:T(8,128)(2,1)S(1)} collective-permute-done((bf16[64,1152]{1,0:T(8,128)(2,1)S(1)}, bf16[64,1152]{1,0:T(8,128)(2,1)S(1)}, u32[]{:S(2)}, u32[]{:S(2)}) %collective-permute-start.17) | collective-permute-done | bytes 147488 | tf_op jit(solution)/shard_map/ppermute | solution.py:233
  55.6 1.2 %collective-permute-done.18.refs_3_ = bf16[64,1152]{1,0:T(8,128)(2,1)S(1)} collective-permute-done((bf16[64,1152]{1,0:T(8,128)(2,1)S(1)}, bf16[64,1152]{1,0:T(8,128)(2,1)S(1)}, u32[]{:S(2)}, u32[]{:S(2)}) %collective-permute-start.18) | collective-permute-done | bytes 147488 | tf_op jit(solution)/shard_map/ppermute | solution.py:256
  56.9 1.4 %collective-permute-start.19 = (bf16[32,1152]{1,0:T(8,128)(2,1)S(1)}, bf16[32,1152]{1,0:T(8,128)(2,1)S(1)}, u32[]{:S(2)}, u32[]{:S(2)}) collective-permute-start(bf16[32,1152]{1,0:T(8,128)(2,1)S(1)} %get-tuple-element.59), channel_id=1, source_target_pairs={{0,24},{4,28},{8,16},{12,20},{16,8},{20,12},{24,0},{28,4},{1,25},{... | collective-permute-start | bytes 221192 | tf_op jit(solution)/shard_map/ppermute | solution.py:233
  58.2 3.1 %collective-permute-start.21 = (bf16[32,1152]{1,0:T(8,128)(2,1)S(1)}, bf16[32,1152]{1,0:T(8,128)(2,1)S(1)}, u32[]{:S(2)}, u32[]{:S(2)}) collective-permute-start(bf16[32,1152]{1,0:T(8,128)(2,1)S(1)} %get-tuple-element.61), channel_id=1, source_target_pairs={{0,8},{4,12},{8,0},{12,4},{16,24},{20,28},{24,16},{28,20},{1,9},{5... | collective-permute-start | bytes 221192 | tf_op jit(solution)/shard_map/ppermute | solution.py:233
  61.3 1.8 %collective-permute-done.19.refs_0_ = bf16[32,1152]{1,0:T(8,128)(2,1)S(1)} collective-permute-done((bf16[32,1152]{1,0:T(8,128)(2,1)S(1)}, bf16[32,1152]{1,0:T(8,128)(2,1)S(1)}, u32[]{:S(2)}, u32[]{:S(2)}) %collective-permute-start.19) | collective-permute-done | bytes 73760 | tf_op jit(solution)/shard_map/ppermute | solution.py:233
  63.2 1.5 %collective-permute-done.20.refs_1_ = bf16[32,1152]{1,0:T(8,128)(2,1)S(1)} collective-permute-done((bf16[32,1152]{1,0:T(8,128)(2,1)S(1)}, bf16[32,1152]{1,0:T(8,128)(2,1)S(1)}, u32[]{:S(2)}, u32[]{:S(2)}) %collective-permute-start.20) | collective-permute-done | bytes 73760 | tf_op jit(solution)/shard_map/ppermute | solution.py:233
  64.7 0.8 %shard_map.75 = bf16[8,16,1152]{2,1,0:T(8,128)(2,1)} custom-call(f32[6,1152]{1,0:T(8,128)S(1)} %copy-done.7, bf16[4,16,1152]{2,1,0:T(8,128)(2,1)S(1)} %get-tuple-element.45.kept_ref, bf16[4,16,1152]{2,1,0:T(8,128)(2,1)S(1)} %collective-permute-done.12.other_ref, bf16[32,1152]{1,0:T(8,128)(2,1)S(1)} %collective-permute-done.19.refs_0_, ...), custom_call_target="tpu_custom_call" | custom-call | flops 1 | bytes 1 | tf_op jit(solution)/shard_map/pallas_call | solution.py:220
  (40 shorter events, 3.6 us)
Async XLA Ops:
  0.0 3.0 %collective-permute-start = (bf16[1,128,1152]{2,1,0:T(8,128)(2,1)}, bf16[1,128,1152]{2,1,0:T(8,128)(2,1)S(1)}, u32[]{:S(2)}, u32[]{:S(2)}) collective-permute-start(bf16[1,128,1152]{2,1,0:T(8,128)(2,1)} %own_ref.1), channel_id=1, source_target_pairs={{0,1},{1,0},{2,3},{3,2},{4,5},{5,4},{6,7},{7,6},{8,9},{9,8},{10,11... | collective-permute-start | bytes 884744 | tf_op jit(solution)/shard_map/ppermute | solution.py:233
  0.5 10.4 %collective-permute-start.2 = (bf16[1,128,1152]{2,1,0:T(8,128)(2,1)}, bf16[1,128,1152]{2,1,0:T(8,128)(2,1)S(1)}, u32[]{:S(2)}, u32[]{:S(2)}) collective-permute-start(bf16[1,128,1152]{2,1,0:T(8,128)(2,1)} %own_ref.1), channel_id=1, source_target_pairs={{0,2},{1,3},{2,0},{3,1},{4,6},{5,7},{6,4},{7,5},{8,10},{9,11},{10,... | collective-permute-start | bytes 884744 | tf_op jit(solution)/shard_map/ppermute | solution.py:233
  3.0 1.0 %copy-start.5 = (bf16[1,128,1152]{2,1,0:T(8,128)(2,1)S(1)}, bf16[1,128,1152]{2,1,0:T(8,128)(2,1)}, u32[]{:S(2)}) copy-start(bf16[1,128,1152]{2,1,0:T(8,128)(2,1)} %own_ref.1) | copy-start | bytes 884740
  4.1 6.8 %collective-permute-start.1 = (bf16[64,1152]{1,0:T(8,128)(2,1)S(1)}, bf16[64,1152]{1,0:T(8,128)(2,1)S(1)}, u32[]{:S(2)}, u32[]{:S(2)}) collective-permute-start(bf16[64,1152]{1,0:T(8,128)(2,1)S(1)} %get-tuple-element.36), channel_id=1, source_target_pairs={{0,4},{4,0},{8,12},{12,8},{16,20},{20,16},{24,28},{28,24},{1,5},{5... | collective-permute-start | bytes 442376 | tf_op jit(solution)/shard_map/ppermute | solution.py:233
  5.8 1.6 %copy-start = (bf16[864,1152]{1,0:T(8,128)(2,1)S(1)}, bf16[864,1152]{1,0:T(8,128)(2,1)}, u32[]{:S(2)}) copy-start(bf16[864,1152]{1,0:T(8,128)(2,1)} %weight_ref.3) | copy-start | bytes 5971972
  7.4 0.8 %copy-start.6 = (f32[6,1152]{1,0:T(8,128)S(1)}, f32[6,1152]{1,0:T(8,128)}, u32[]{:S(2)}) copy-start(f32[6,1152]{1,0:T(8,128)} %mod_ref.7) | copy-start | bytes 82948
  8.2 4.4 %copy-start.4 = (bf16[288,1152]{1,0:T(8,128)(2,1)S(1)}, bf16[288,1152]{1,0:T(8,128)(2,1)}, u32[]{:S(2)}) copy-start(bf16[288,1152]{1,0:T(8,128)(2,1)} %refs_0_.4) | copy-start | bytes 1990660
  8.2 4.8 %copy-start.1 = (bf16[864,1152]{1,0:T(8,128)(2,1)S(1)}, bf16[864,1152]{1,0:T(8,128)(2,1)}, u32[]{:S(2)}) copy-start(bf16[864,1152]{1,0:T(8,128)(2,1)} %weight_ref.3) | copy-start | bytes 5971972
  9.3 9.2 %copy-start.3 = (bf16[288,1152]{1,0:T(8,128)(2,1)S(1)}, bf16[288,1152]{1,0:T(8,128)(2,1)}, u32[]{:S(2)}) copy-start(bf16[288,1152]{1,0:T(8,128)(2,1)} %refs_2_.5) | copy-start | bytes 1990660
  10.9 1.6 %collective-permute-start.3 = (bf16[1,128,1152]{2,1,0:T(8,128)(2,1)S(1)}, bf16[1,128,1152]{2,1,0:T(8,128)(2,1)S(1)}, u32[]{:S(2)}, u32[]{:S(2)}) collective-permute-start(bf16[1,128,1152]{2,1,0:T(8,128)(2,1)S(1)} %collective-permute-done.2.refs_0_), channel_id=1, source_target_pairs={{0,1},{1,0},{2,3},{3,2},{4,5},{5,4},{6,7},{7,6},{8,9},{9,8},{10,11... | collective-permute-start | bytes 884744 | tf_op jit(solution)/shard_map/ppermute | solution.py:233
  12.4 27.5 %collective-permute-start.13 = (bf16[864,1152]{1,0:T(8,128)(2,1)}, bf16[864,1152]{1,0:T(8,128)(2,1)S(1)}, u32[]{:S(2)}, u32[]{:S(2)}) collective-permute-start(bf16[864,1152]{1,0:T(8,128)(2,1)} %refs_0_.7), channel_id=1, source_target_pairs={{0,1},{1,0},{2,3},{3,2},{4,5},{5,4},{6,7},{7,6},{8,9},{9,8},{10,11... | collective-permute-start | bytes 5971976 | tf_op jit(solution)/shard_map/ppermute | solution.py:233
  12.6 5.2 %collective-permute-start.5 = (bf16[288,1152]{1,0:T(8,128)(2,1)S(1)}, bf16[288,1152]{1,0:T(8,128)(2,1)S(1)}, u32[]{:S(2)}, u32[]{:S(2)}) collective-permute-start(bf16[288,1152]{1,0:T(8,128)(2,1)S(1)} %copy-done.4), channel_id=1, source_target_pairs={{0,1},{1,0},{2,3},{3,2},{4,5},{5,4},{6,7},{7,6},{8,9},{9,8},{10,11... | collective-permute-start | bytes 1990664 | tf_op jit(solution)/shard_map/ppermute | solution.py:233
  16.3 11.9 %copy-start.7 = (f32[6,1152]{1,0:T(8,128)S(1)}, f32[6,1152]{1,0:T(8,128)}, u32[]{:S(2)}) copy-start(f32[6,1152]{1,0:T(8,128)} %mod_ref.7) | copy-start | bytes 82948
  16.3 1.4 %collective-permute-start.4 = (bf16[288,256]{1,0:T(8,128)(2,1)S(1)}, bf16[288,256]{1,0:T(8,128)(2,1)S(1)}, u32[]{:S(2)}, u32[]{:S(2)}) collective-permute-start(bf16[288,256]{1,0:T(8,128)(2,1)S(1)} %get-tuple-element.39), channel_id=1, source_target_pairs={{0,1},{1,0},{2,3},{3,2},{4,5},{5,4},{6,7},{7,6},{8,9},{9,8},{10,11... | collective-permute-start | bytes 442376 | tf_op jit(solution)/shard_map/ppermute | solution.py:233
  18.5 21.5 %copy-start.2 = (bf16[864,1152]{1,0:T(8,128)(2,1)S(1)}, bf16[864,1152]{1,0:T(8,128)(2,1)}, u32[]{:S(2)}) copy-start(bf16[864,1152]{1,0:T(8,128)(2,1)} %refs_0_.7) | copy-start | bytes 5971972
  18.5 21.4 %collective-permute-start.14 = (bf16[288,1152]{1,0:T(8,128)(2,1)S(1)}, bf16[288,1152]{1,0:T(8,128)(2,1)S(1)}, u32[]{:S(2)}, u32[]{:S(2)}) collective-permute-start(bf16[288,1152]{1,0:T(8,128)(2,1)S(1)} %copy-done.3), channel_id=1, source_target_pairs={{0,1},{1,0},{2,3},{3,2},{4,5},{5,4},{6,7},{7,6},{8,9},{9,8},{10,11... | collective-permute-start | bytes 1990664 | tf_op jit(solution)/shard_map/ppermute | solution.py:233
  18.7 9.5 %collective-permute-start.6 = (bf16[64,1152]{1,0:T(8,128)(2,1)S(1)}, bf16[64,1152]{1,0:T(8,128)(2,1)S(1)}, u32[]{:S(2)}, u32[]{:S(2)}) collective-permute-start(bf16[64,1152]{1,0:T(8,128)(2,1)S(1)} %get-tuple-element.42), channel_id=1, source_target_pairs={{0,2},{1,3},{2,0},{3,1},{4,6},{5,7},{6,4},{7,5},{8,10},{9,11},{10,... | collective-permute-start | bytes 442376 | tf_op jit(solution)/shard_map/ppermute | solution.py:233
  20.5 7.8 %collective-permute-start.8 = (bf16[64,1152]{1,0:T(8,128)(2,1)S(1)}, bf16[64,1152]{1,0:T(8,128)(2,1)S(1)}, u32[]{:S(2)}, u32[]{:S(2)}) collective-permute-start(bf16[64,1152]{1,0:T(8,128)(2,1)S(1)} %get-tuple-element.44), channel_id=1, source_target_pairs={{0,6},{1,7},{2,4},{3,5},{4,2},{5,3},{6,0},{7,1},{8,14},{9,15},{10,... | collective-permute-start | bytes 442376 | tf_op jit(solution)/shard_map/ppermute | solution.py:256
  21.9 5.9 %collective-permute-start.7 = (bf16[64,576]{1,0:T(8,128)(2,1)S(1)}, bf16[64,576]{1,0:T(8,128)(2,1)S(1)}, u32[]{:S(2)}, u32[]{:S(2)}) collective-permute-start(bf16[64,576]{1,0:T(8,128)(2,1)S(1)} %get-tuple-element.43), channel_id=1, source_target_pairs={{0,4},{4,0},{8,12},{12,8},{16,20},{20,16},{24,28},{28,24},{1,5},{5... | collective-permute-start | bytes 221192 | tf_op jit(solution)/shard_map/ppermute | solution.py:233
  28.6 7.0 %collective-permute-start.9 = (bf16[32,1152]{1,0:T(8,128)(2,1)S(1)}, bf16[32,1152]{1,0:T(8,128)(2,1)S(1)}, u32[]{:S(2)}, u32[]{:S(2)}) collective-permute-start(bf16[32,1152]{1,0:T(8,128)(2,1)S(1)} %get-tuple-element.47), channel_id=1, source_target_pairs={{0,24},{4,28},{8,16},{12,20},{16,8},{20,12},{24,0},{28,4},{1,25},{... | collective-permute-start | bytes 221192 | tf_op jit(solution)/shard_map/ppermute | solution.py:233
  32.5 5.8 %collective-permute-start.10 = (bf16[32,1152]{1,0:T(8,128)(2,1)S(1)}, bf16[32,1152]{1,0:T(8,128)(2,1)S(1)}, u32[]{:S(2)}, u32[]{:S(2)}) collective-permute-start(bf16[32,1152]{1,0:T(8,128)(2,1)S(1)} %get-tuple-element.48), channel_id=1, source_target_pairs={{0,16},{4,20},{8,24},{12,28},{16,0},{20,4},{24,8},{28,12},{1,17},{... | collective-permute-start | bytes 221192 | tf_op jit(solution)/shard_map/ppermute | solution.py:233
  32.5 5.8 %collective-permute-start.11 = (bf16[32,1152]{1,0:T(8,128)(2,1)S(1)}, bf16[32,1152]{1,0:T(8,128)(2,1)S(1)}, u32[]{:S(2)}, u32[]{:S(2)}) collective-permute-start(bf16[32,1152]{1,0:T(8,128)(2,1)S(1)} %get-tuple-element.49), channel_id=1, source_target_pairs={{0,8},{4,12},{8,0},{12,4},{16,24},{20,28},{24,16},{28,20},{1,9},{5... | collective-permute-start | bytes 221192 | tf_op jit(solution)/shard_map/ppermute | solution.py:233
  38.3 8.4 %collective-permute-start.15 = (bf16[128,1152]{1,0:T(8,128)(2,1)S(1)}, bf16[128,1152]{1,0:T(8,128)(2,1)S(1)}, u32[]{:S(2)}, u32[]{:S(2)}) collective-permute-start(bf16[128,1152]{1,0:T(8,128)(2,1)S(1)} %shard_map.70.refs_4_), channel_id=1, source_target_pairs={{0,2},{1,3},{2,0},{3,1},{4,6},{5,7},{6,4},{7,5},{8,10},{9,11},{10,... | collective-permute-start | bytes 884744 | tf_op jit(solution)/shard_map/ppermute | solution.py:233
  41.9 4.5 %collective-permute-start.16 = (bf16[64,576]{1,0:T(8,128)(2,1)S(1)}, bf16[64,576]{1,0:T(8,128)(2,1)S(1)}, u32[]{:S(2)}, u32[]{:S(2)}) collective-permute-start(bf16[64,576]{1,0:T(8,128)(2,1)S(1)} %get-tuple-element.55), channel_id=1, source_target_pairs={{0,4},{4,0},{8,12},{12,8},{16,20},{20,16},{24,28},{28,24},{1,5},{5... | collective-permute-start | bytes 221192 | tf_op jit(solution)/shard_map/ppermute | solution.py:233
  48.7 6.9 %collective-permute-start.17 = (bf16[64,1152]{1,0:T(8,128)(2,1)S(1)}, bf16[64,1152]{1,0:T(8,128)(2,1)S(1)}, u32[]{:S(2)}, u32[]{:S(2)}) collective-permute-start(bf16[64,1152]{1,0:T(8,128)(2,1)S(1)} %get-tuple-element.57), channel_id=1, source_target_pairs={{0,2},{1,3},{2,0},{3,1},{4,6},{5,7},{6,4},{7,5},{8,10},{9,11},{10,... | collective-permute-start | bytes 442376 | tf_op jit(solution)/shard_map/ppermute | solution.py:233
  50.3 6.5 %collective-permute-start.18 = (bf16[64,1152]{1,0:T(8,128)(2,1)S(1)}, bf16[64,1152]{1,0:T(8,128)(2,1)S(1)}, u32[]{:S(2)}, u32[]{:S(2)}) collective-permute-start(bf16[64,1152]{1,0:T(8,128)(2,1)S(1)} %get-tuple-element.58), channel_id=1, source_target_pairs={{0,6},{1,7},{2,4},{3,5},{4,2},{5,3},{6,0},{7,1},{8,14},{9,15},{10,... | collective-permute-start | bytes 442376 | tf_op jit(solution)/shard_map/ppermute | solution.py:256
  51.8 9.6 %collective-permute-start.12 = (bf16[4,16,1152]{2,1,0:T(8,128)(2,1)S(1)}, bf16[4,16,1152]{2,1,0:T(8,128)(2,1)S(1)}, u32[]{:S(2)}, u32[]{:S(2)}) collective-permute-start(bf16[4,16,1152]{2,1,0:T(8,128)(2,1)S(1)} %get-tuple-element.51), channel_id=1, source_target_pairs={{0,4},{4,0},{8,12},{12,8},{16,20},{20,16},{24,28},{28,24},{1,5},{5... | collective-permute-start | bytes 442376 | tf_op jit(solution)/shard_map/ppermute | solution.py:233
  56.9 6.3 %collective-permute-start.19 = (bf16[32,1152]{1,0:T(8,128)(2,1)S(1)}, bf16[32,1152]{1,0:T(8,128)(2,1)S(1)}, u32[]{:S(2)}, u32[]{:S(2)}) collective-permute-start(bf16[32,1152]{1,0:T(8,128)(2,1)S(1)} %get-tuple-element.59), channel_id=1, source_target_pairs={{0,24},{4,28},{8,16},{12,20},{16,8},{20,12},{24,0},{28,4},{1,25},{... | collective-permute-start | bytes 221192 | tf_op jit(solution)/shard_map/ppermute | solution.py:233
  58.2 6.4 %collective-permute-start.20 = (bf16[32,1152]{1,0:T(8,128)(2,1)S(1)}, bf16[32,1152]{1,0:T(8,128)(2,1)S(1)}, u32[]{:S(2)}, u32[]{:S(2)}) collective-permute-start(bf16[32,1152]{1,0:T(8,128)(2,1)S(1)} %get-tuple-element.60), channel_id=1, source_target_pairs={{0,16},{4,20},{8,24},{12,28},{16,0},{20,4},{24,8},{28,12},{1,17},{... | collective-permute-start | bytes 221192 | tf_op jit(solution)/shard_map/ppermute | solution.py:233
  58.2 6.4 %collective-permute-start.21 = (bf16[32,1152]{1,0:T(8,128)(2,1)S(1)}, bf16[32,1152]{1,0:T(8,128)(2,1)S(1)}, u32[]{:S(2)}, u32[]{:S(2)}) collective-permute-start(bf16[32,1152]{1,0:T(8,128)(2,1)S(1)} %get-tuple-element.61), channel_id=1, source_target_pairs={{0,8},{4,12},{8,0},{12,4},{16,24},{20,28},{24,16},{28,20},{1,9},{5... | collective-permute-start | bytes 221192 | tf_op jit(solution)/shard_map/ppermute | solution.py:233

commit v23 on v22

--- a/solution.py
+++ b/solution.py
@@ -298,9 +298,8 @@
         functools.partial(share_kernel, period), (after(tokens, sister),), [halves_shape(BF16)] * 2
     )
     paired = swap(shared, "frame", 1)
-    out_pair = with_sister(spatial_out, near)
     far = both_cores([after(block, near, paired) for block in far])
-    temporal_pair = with_sister(temporal_qkv, *far)
+    out_pair = with_sister(spatial_out, *far)
 
     kept, sent = call(
         functools.partial(spatial_kernel, count),
@@ -314,6 +313,7 @@
         own_shapes + far_shapes,
     )
     late_pair = with_sister(temporal_out, parts[0])
+    temporal_pair = with_sister(temporal_qkv, parts[0])
     updates = return_updates((parts[0], project_paired(parts[1], out_pair)), parts[2:])
     middle, middle_sent, *parts = call(
         functools.partial(middle_kernel, pieces, groups),

time: 65.7 us -> 65.7 us (level)
  transfers between devices with their start and end apart: 22 -> 22, of which waited for: 11 -> 11; matrix products, arithmetic and copies ran while one was open for 0% -> 0% of each run, Pallas kernels for 13% -> 12%
where the time goes in v23:
time: 65.7 us; the launch traced here: 65.5 us
  waiting for transfers between devices  25.8 us (39%)
  starting transfers between devices  25.1 us (38%)
  Pallas kernels  11.1 us (17%)
  local copies, waits for them, and re-layouts  3.34 us (5%)
    ppermute x20, waiting for transfers between devices, swap(): return lax.ppermute(value, axis, [(at, at ^ offset) for at in range(size)])  24.6 us
    ppermute x20, starting transfers between devices, swap(): return lax.ppermute(value, axis, [(at, at ^ offset) for at in range(size)])  22.3 us
    pallas_call x12, Pallas kernels, call(): pl.pallas_call(body, out_shape=outs, in_specs=[pl.BlockSpec(memory_space=...  11.1 us
    unnamed x16, local copies, waits for them, and re-layouts  3.34 us
    ppermute x2, starting transfers between devices, swap_diagonal(): return lax.ppermute(value, ('frame', 'patch'), pairs)  2.84 us
  transfers between devices with their start and end apart: 22, of which 11 were waited for; matrix products, arithmetic and copies ran while one was open for 0% of the time, Pallas kernels for 12%

profile of v23, /device:TPU:0, one launch (start us, length us, event | category | flops | bytes accessed | tf_op | source)
XLA Modules:
  0.0 65.5 jit_solution(16396362705425611904)
XLA Ops:
  0.5 2.5 %collective-permute-start.2 = (bf16[1,128,1152]{2,1,0:T(8,128)(2,1)}, bf16[1,128,1152]{2,1,0:T(8,128)(2,1)S(1)}, u32[]{:S(2)}, u32[]{:S(2)}) collective-permute-start(bf16[1,128,1152]{2,1,0:T(8,128)(2,1)} %own_ref.1), channel_id=1, source_target_pairs={{0,2},{1,3},{2,0},{3,1},{4,6},{5,7},{6,4},{7,5},{8,10},{9,11},{10,... | collective-permute-start | bytes 884744 | tf_op jit(solution)/shard_map/ppermute | solution.py:233
  3.0 1.0 %copy-done.5 = bf16[1,128,1152]{2,1,0:T(8,128)(2,1)S(1)} copy-done((bf16[1,128,1152]{2,1,0:T(8,128)(2,1)S(1)}, bf16[1,128,1152]{2,1,0:T(8,128)(2,1)}, u32[]{:S(2)}) %copy-start.5) | copy-done | bytes 294936
  4.1 1.8 %collective-permute-start.1 = (bf16[64,1152]{1,0:T(8,128)(2,1)S(1)}, bf16[64,1152]{1,0:T(8,128)(2,1)S(1)}, u32[]{:S(2)}, u32[]{:S(2)}) collective-permute-start(bf16[64,1152]{1,0:T(8,128)(2,1)S(1)} %get-tuple-element.36), channel_id=1, source_target_pairs={{0,4},{4,0},{8,12},{12,8},{16,20},{20,16},{24,28},{28,24},{1,5},{5... | collective-permute-start | bytes 442376 | tf_op jit(solution)/shard_map/ppermute | solution.py:233
  5.9 1.6 %copy-done = bf16[864,1152]{1,0:T(8,128)(2,1)S(1)} copy-done((bf16[864,1152]{1,0:T(8,128)(2,1)S(1)}, bf16[864,1152]{1,0:T(8,128)(2,1)}, u32[]{:S(2)}) %copy-start) | copy-done | bytes 1990680
  7.4 0.8 %copy-done.6 = f32[6,1152]{1,0:T(8,128)S(1)} copy-done((f32[6,1152]{1,0:T(8,128)S(1)}, f32[6,1152]{1,0:T(8,128)}, u32[]{:S(2)}) %copy-start.6) | copy-done | bytes 27672
  8.2 1.1 %shard_map.65.near_ref = f32[864,256]{1,0:T(8,128)S(1)} custom-call(f32[6,1152]{1,0:T(8,128)S(1)} %copy-done.6, bf16[864,1152]{1,0:T(8,128)(2,1)S(1)} %copy-done, bf16[1,128,1152]{2,1,0:T(8,128)(2,1)S(1)} %copy-done.5, bf16[1,128,1152]{2,1,0:T(8,128)(2,1)S(1)} %collective-permute-done.sister_ref), custom_call_target="tpu_custom_call" | custom-call | flops 1 | bytes 1 | tf_op jit(solution)/shard_map/pallas_call | solution.py:220
  9.3 1.6 %collective-permute-done.2.refs_0_ = bf16[1,128,1152]{2,1,0:T(8,128)(2,1)S(1)} collective-permute-done((bf16[1,128,1152]{2,1,0:T(8,128)(2,1)}, bf16[1,128,1152]{2,1,0:T(8,128)(2,1)S(1)}, u32[]{:S(2)}, u32[]{:S(2)}) %collective-permute-start.2) | collective-permute-done | bytes 294944 | tf_op jit(solution)/shard_map/ppermute | solution.py:233
  10.9 1.6 %collective-permute-done.3.refs_1_ = bf16[1,128,1152]{2,1,0:T(8,128)(2,1)S(1)} collective-permute-done((bf16[1,128,1152]{2,1,0:T(8,128)(2,1)S(1)}, bf16[1,128,1152]{2,1,0:T(8,128)(2,1)S(1)}, u32[]{:S(2)}, u32[]{:S(2)}) %collective-permute-start.3) | collective-permute-done | bytes 294944 | tf_op jit(solution)/shard_map/ppermute | solution.py:233
  12.6 3.3 %shard_map.66 = (bf16[288,256]{1,0:T(8,128)(2,1)S(1)}, bf16[288,256]{1,0:T(8,128)(2,1)S(1)}) custom-call(f32[6,1152]{1,0:T(8,128)S(1)} %copy-done.6, bf16[864,1152]{1,0:T(8,128)(2,1)S(1)} %copy-done.1, f32[864,256]{1,0:T(8,128)S(1)} %shard_map.65.near_ref, bf16[1,128,1152]{2,1,0:T(8,128)(2,1)S(1)} %collective-permute-done.2.refs_0_, ...), custom_call_target="tpu_custom_call" | custom-call | flops 1 | bytes 1 | tf_op jit(solution)/shard_map/pallas_call | solution.py:220
  16.4 1.0 %collective-permute-done.4.refs_1_ = bf16[288,256]{1,0:T(8,128)(2,1)S(1)} collective-permute-done((bf16[288,256]{1,0:T(8,128)(2,1)S(1)}, bf16[288,256]{1,0:T(8,128)(2,1)S(1)}, u32[]{:S(2)}, u32[]{:S(2)}) %collective-permute-start.4) | collective-permute-done | bytes 147488 | tf_op jit(solution)/shard_map/ppermute | solution.py:233
  17.4 0.7 %shard_map.67 = (f32[64,1152]{1,0:T(8,128)S(1)}, bf16[64,576]{1,0:T(8,128)(2,1)S(1)}, bf16[64,1152]{1,0:T(8,128)(2,1)S(1)}, bf16[64,1152]{1,0:T(8,128)(2,1)S(1)}) custom-call(bf16[288,256]{1,0:T(8,128)(2,1)S(1)} %get-tuple-element.38.refs_0_, bf16[288,256]{1,0:T(8,128)(2,1)S(1)} %collective-permute-done.4.refs_1_, bf16[288,1152]{1,0:T(8,128)(2,1)S(1)} %copy-done.4, ...), custom_call_target="tpu_custom_call" | custom-call | flops 1 | bytes 1 | tf_op jit(solution)/shard_map/pallas_call | solution.py:220
  18.7 1.8 %collective-permute-start.6 = (bf16[64,1152]{1,0:T(8,128)(2,1)S(1)}, bf16[64,1152]{1,0:T(8,128)(2,1)S(1)}, u32[]{:S(2)}, u32[]{:S(2)}) collective-permute-start(bf16[64,1152]{1,0:T(8,128)(2,1)S(1)} %get-tuple-element.42), channel_id=1, source_target_pairs={{0,2},{1,3},{2,0},{3,1},{4,6},{5,7},{6,4},{7,5},{8,10},{9,11},{10,... | collective-permute-start | bytes 442376 | tf_op jit(solution)/shard_map/ppermute | solution.py:233
  20.4 1.4 %collective-permute-start.8 = (bf16[64,1152]{1,0:T(8,128)(2,1)S(1)}, bf16[64,1152]{1,0:T(8,128)(2,1)S(1)}, u32[]{:S(2)}, u32[]{:S(2)}) collective-permute-start(bf16[64,1152]{1,0:T(8,128)(2,1)S(1)} %get-tuple-element.44), channel_id=1, source_target_pairs={{0,6},{1,7},{2,4},{3,5},{4,2},{5,3},{6,0},{7,1},{8,14},{9,15},{10,... | collective-permute-start | bytes 442376 | tf_op jit(solution)/shard_map/ppermute | solution.py:256
  22.2 5.6 %collective-permute-done.7.head_ref = bf16[64,576]{1,0:T(8,128)(2,1)S(1)} collective-permute-done((bf16[64,576]{1,0:T(8,128)(2,1)S(1)}, bf16[64,576]{1,0:T(8,128)(2,1)S(1)}, u32[]{:S(2)}, u32[]{:S(2)}) %collective-permute-start.7) | collective-permute-done | bytes 73760 | tf_op jit(solution)/shard_map/ppermute | solution.py:233
  28.6 3.9 %collective-permute-start.9 = (bf16[32,1152]{1,0:T(8,128)(2,1)S(1)}, bf16[32,1152]{1,0:T(8,128)(2,1)S(1)}, u32[]{:S(2)}, u32[]{:S(2)}) collective-permute-start(bf16[32,1152]{1,0:T(8,128)(2,1)S(1)} %get-tuple-element.47), channel_id=1, source_target_pairs={{0,24},{4,28},{8,16},{12,20},{16,8},{20,12},{24,0},{28,4},{1,25},{... | collective-permute-start | bytes 221192 | tf_op jit(solution)/shard_map/ppermute | solution.py:233
  32.5 0.6 collective-permute-start.11
  33.1 2.5 %collective-permute-done.9.refs_0_ = bf16[32,1152]{1,0:T(8,128)(2,1)S(1)} collective-permute-done((bf16[32,1152]{1,0:T(8,128)(2,1)S(1)}, bf16[32,1152]{1,0:T(8,128)(2,1)S(1)}, u32[]{:S(2)}, u32[]{:S(2)}) %collective-permute-start.9) | collective-permute-done | bytes 73760 | tf_op jit(solution)/shard_map/ppermute | solution.py:233
  35.6 2.7 %collective-permute-done.10.refs_1_ = bf16[32,1152]{1,0:T(8,128)(2,1)S(1)} collective-permute-done((bf16[32,1152]{1,0:T(8,128)(2,1)S(1)}, bf16[32,1152]{1,0:T(8,128)(2,1)S(1)}, u32[]{:S(2)}, u32[]{:S(2)}) %collective-permute-start.10) | collective-permute-done | bytes 73760 | tf_op jit(solution)/shard_map/ppermute | solution.py:233
  38.3 1.6 %collective-permute-start.15 = (bf16[128,1152]{1,0:T(8,128)(2,1)S(1)}, bf16[128,1152]{1,0:T(8,128)(2,1)S(1)}, u32[]{:S(2)}, u32[]{:S(2)}) collective-permute-start(bf16[128,1152]{1,0:T(8,128)(2,1)S(1)} %shard_map.70.refs_4_), channel_id=1, source_target_pairs={{0,2},{1,3},{2,0},{3,1},{4,6},{5,7},{6,4},{7,5},{8,10},{9,11},{10,... | collective-permute-start | bytes 884744 | tf_op jit(solution)/shard_map/ppermute | solution.py:233
  39.9 1.9 %shard_map.71 = (f32[64,1152]{1,0:T(8,128)S(1)}, bf16[64,576]{1,0:T(8,128)(2,1)S(1)}) custom-call(bf16[864,1152]{1,0:T(8,128)(2,1)S(1)} %copy-done.2, bf16[864,1152]{1,0:T(8,128)(2,1)S(1)} %collective-permute-done.13.refs_1_, bf16[288,1152]{1,0:T(8,128)(2,1)S(1)} %copy-done.3, bf16[288,1152]{1,0:T(8,128)(2,1)S(1)} %collective-permute-done.14.refs_3_.refs_1_, ...), custom_call_target="tpu_custom_call" | custom-call | flops 1 | bytes 1 | tf_op jit(solution)/shard_map/pallas_call | solution.py:220
  41.8 1.6 %collective-permute-start.16 = (bf16[64,576]{1,0:T(8,128)(2,1)S(1)}, bf16[64,576]{1,0:T(8,128)(2,1)S(1)}, u32[]{:S(2)}, u32[]{:S(2)}) collective-permute-start(bf16[64,576]{1,0:T(8,128)(2,1)S(1)} %get-tuple-element.55), channel_id=1, source_target_pairs={{0,4},{4,0},{8,12},{12,8},{16,20},{20,16},{24,28},{28,24},{1,5},{5... | collective-permute-start | bytes 221192 | tf_op jit(solution)/shard_map/ppermute | solution.py:233
  43.4 3.0 %collective-permute-done.16.head_ref = bf16[64,576]{1,0:T(8,128)(2,1)S(1)} collective-permute-done((bf16[64,576]{1,0:T(8,128)(2,1)S(1)}, bf16[64,576]{1,0:T(8,128)(2,1)S(1)}, u32[]{:S(2)}, u32[]{:S(2)}) %collective-permute-start.16) | collective-permute-done | bytes 73760 | tf_op jit(solution)/shard_map/ppermute | solution.py:233
  46.7 2.0 %shard_map.73 = (bf16[64,1152]{1,0:T(8,128)(2,1)S(1)}, bf16[64,1152]{1,0:T(8,128)(2,1)S(1)}) custom-call(bf16[864,1152]{1,0:T(8,128)(2,1)S(1)} %copy-done.2, bf16[864,1152]{1,0:T(8,128)(2,1)S(1)} %collective-permute-done.13.refs_1_, bf16[288,1152]{1,0:T(8,128)(2,1)S(1)} %copy-done.3, bf16[288,1152]{1,0:T(8,128)(2,1)S(1)} %collective-permute-done.14.refs_3_.refs_1_, ...), custom_call_target="tpu_custom_call" | custom-call | flops 1 | bytes 1 | tf_op jit(solution)/shard_map/pallas_call | solution.py:220
  48.7 1.6 %collective-permute-start.17 = (bf16[64,1152]{1,0:T(8,128)(2,1)S(1)}, bf16[64,1152]{1,0:T(8,128)(2,1)S(1)}, u32[]{:S(2)}, u32[]{:S(2)}) collective-permute-start(bf16[64,1152]{1,0:T(8,128)(2,1)S(1)} %get-tuple-element.57), channel_id=1, source_target_pairs={{0,2},{1,3},{2,0},{3,1},{4,6},{5,7},{6,4},{7,5},{8,10},{9,11},{10,... | collective-permute-start | bytes 442376 | tf_op jit(solution)/shard_map/ppermute | solution.py:233
  50.3 1.4 %collective-permute-start.18 = (bf16[64,1152]{1,0:T(8,128)(2,1)S(1)}, bf16[64,1152]{1,0:T(8,128)(2,1)S(1)}, u32[]{:S(2)}, u32[]{:S(2)}) collective-permute-start(bf16[64,1152]{1,0:T(8,128)(2,1)S(1)} %get-tuple-element.58), channel_id=1, source_target_pairs={{0,6},{1,7},{2,4},{3,5},{4,2},{5,3},{6,0},{7,1},{8,14},{9,15},{10,... | collective-permute-start | bytes 442376 | tf_op jit(solution)/shard_map/ppermute | solution.py:256
  52.3 3.3 %collective-permute-done.17.refs_1_ = bf16[64,1152]{1,0:T(8,128)(2,1)S(1)} collective-permute-done((bf16[64,1152]{1,0:T(8,128)(2,1)S(1)}, bf16[64,1152]{1,0:T(8,128)(2,1)S(1)}, u32[]{:S(2)}, u32[]{:S(2)}) %collective-permute-start.17) | collective-permute-done | bytes 147488 | tf_op jit(solution)/shard_map/ppermute | solution.py:233
  55.6 1.2 %collective-permute-done.18.refs_3_ = bf16[64,1152]{1,0:T(8,128)(2,1)S(1)} collective-permute-done((bf16[64,1152]{1,0:T(8,128)(2,1)S(1)}, bf16[64,1152]{1,0:T(8,128)(2,1)S(1)}, u32[]{:S(2)}, u32[]{:S(2)}) %collective-permute-start.18) | collective-permute-done | bytes 147488 | tf_op jit(solution)/shard_map/ppermute | solution.py:256
  56.9 1.3 %collective-permute-start.19 = (bf16[32,1152]{1,0:T(8,128)(2,1)S(1)}, bf16[32,1152]{1,0:T(8,128)(2,1)S(1)}, u32[]{:S(2)}, u32[]{:S(2)}) collective-permute-start(bf16[32,1152]{1,0:T(8,128)(2,1)S(1)} %get-tuple-element.59), channel_id=1, source_target_pairs={{0,24},{4,28},{8,16},{12,20},{16,8},{20,12},{24,0},{28,4},{1,25},{... | collective-permute-start | bytes 221192 | tf_op jit(solution)/shard_map/ppermute | solution.py:233
  58.2 3.1 %collective-permute-start.21 = (bf16[32,1152]{1,0:T(8,128)(2,1)S(1)}, bf16[32,1152]{1,0:T(8,128)(2,1)S(1)}, u32[]{:S(2)}, u32[]{:S(2)}) collective-permute-start(bf16[32,1152]{1,0:T(8,128)(2,1)S(1)} %get-tuple-element.61), channel_id=1, source_target_pairs={{0,8},{4,12},{8,0},{12,4},{16,24},{20,28},{24,16},{28,20},{1,9},{5... | collective-permute-start | bytes 221192 | tf_op jit(solution)/shard_map/ppermute | solution.py:233
  61.3 1.8 %collective-permute-done.19.refs_0_ = bf16[32,1152]{1,0:T(8,128)(2,1)S(1)} collective-permute-done((bf16[32,1152]{1,0:T(8,128)(2,1)S(1)}, bf16[32,1152]{1,0:T(8,128)(2,1)S(1)}, u32[]{:S(2)}, u32[]{:S(2)}) %collective-permute-start.19) | collective-permute-done | bytes 73760 | tf_op jit(solution)/shard_map/ppermute | solution.py:233
  63.2 1.5 %collective-permute-done.20.refs_1_ = bf16[32,1152]{1,0:T(8,128)(2,1)S(1)} collective-permute-done((bf16[32,1152]{1,0:T(8,128)(2,1)S(1)}, bf16[32,1152]{1,0:T(8,128)(2,1)S(1)}, u32[]{:S(2)}, u32[]{:S(2)}) %collective-permute-start.20) | collective-permute-done | bytes 73760 | tf_op jit(solution)/shard_map/ppermute | solution.py:233
  64.7 0.8 %shard_map.75 = bf16[8,16,1152]{2,1,0:T(8,128)(2,1)} custom-call(f32[6,1152]{1,0:T(8,128)S(1)} %copy-done.7, bf16[4,16,1152]{2,1,0:T(8,128)(2,1)S(1)} %get-tuple-element.45.kept_ref, bf16[4,16,1152]{2,1,0:T(8,128)(2,1)S(1)} %collective-permute-done.12.other_ref, bf16[32,1152]{1,0:T(8,128)(2,1)S(1)} %collective-permute-done.19.refs_0_, ...), custom_call_target="tpu_custom_call" | custom-call | flops 1 | bytes 1 | tf_op jit(solution)/shard_map/pallas_call | solution.py:220
  (40 shorter events, 3.8 us)
Async XLA Ops:
  0.0 3.0 %collective-permute-start = (bf16[1,128,1152]{2,1,0:T(8,128)(2,1)}, bf16[1,128,1152]{2,1,0:T(8,128)(2,1)S(1)}, u32[]{:S(2)}, u32[]{:S(2)}) collective-permute-start(bf16[1,128,1152]{2,1,0:T(8,128)(2,1)} %own_ref.1), channel_id=1, source_target_pairs={{0,1},{1,0},{2,3},{3,2},{4,5},{5,4},{6,7},{7,6},{8,9},{9,8},{10,11... | collective-permute-start | bytes 884744 | tf_op jit(solution)/shard_map/ppermute | solution.py:233
  0.5 10.4 %collective-permute-start.2 = (bf16[1,128,1152]{2,1,0:T(8,128)(2,1)}, bf16[1,128,1152]{2,1,0:T(8,128)(2,1)S(1)}, u32[]{:S(2)}, u32[]{:S(2)}) collective-permute-start(bf16[1,128,1152]{2,1,0:T(8,128)(2,1)} %own_ref.1), channel_id=1, source_target_pairs={{0,2},{1,3},{2,0},{3,1},{4,6},{5,7},{6,4},{7,5},{8,10},{9,11},{10,... | collective-permute-start | bytes 884744 | tf_op jit(solution)/shard_map/ppermute | solution.py:233
  3.0 1.0 %copy-start.5 = (bf16[1,128,1152]{2,1,0:T(8,128)(2,1)S(1)}, bf16[1,128,1152]{2,1,0:T(8,128)(2,1)}, u32[]{:S(2)}) copy-start(bf16[1,128,1152]{2,1,0:T(8,128)(2,1)} %own_ref.1) | copy-start | bytes 884740
  4.1 6.8 %collective-permute-start.1 = (bf16[64,1152]{1,0:T(8,128)(2,1)S(1)}, bf16[64,1152]{1,0:T(8,128)(2,1)S(1)}, u32[]{:S(2)}, u32[]{:S(2)}) collective-permute-start(bf16[64,1152]{1,0:T(8,128)(2,1)S(1)} %get-tuple-element.36), channel_id=1, source_target_pairs={{0,4},{4,0},{8,12},{12,8},{16,20},{20,16},{24,28},{28,24},{1,5},{5... | collective-permute-start | bytes 442376 | tf_op jit(solution)/shard_map/ppermute | solution.py:233
  5.8 1.6 %copy-start = (bf16[864,1152]{1,0:T(8,128)(2,1)S(1)}, bf16[864,1152]{1,0:T(8,128)(2,1)}, u32[]{:S(2)}) copy-start(bf16[864,1152]{1,0:T(8,128)(2,1)} %weight_ref.3) | copy-start | bytes 5971972
  7.4 0.8 %copy-start.6 = (f32[6,1152]{1,0:T(8,128)S(1)}, f32[6,1152]{1,0:T(8,128)}, u32[]{:S(2)}) copy-start(f32[6,1152]{1,0:T(8,128)} %mod_ref.7) | copy-start | bytes 82948
  8.2 4.3 %copy-start.4 = (bf16[288,1152]{1,0:T(8,128)(2,1)S(1)}, bf16[288,1152]{1,0:T(8,128)(2,1)}, u32[]{:S(2)}) copy-start(bf16[288,1152]{1,0:T(8,128)(2,1)} %refs_0_.4) | copy-start | bytes 1990660
  8.2 4.4 %copy-start.1 = (bf16[864,1152]{1,0:T(8,128)(2,1)S(1)}, bf16[864,1152]{1,0:T(8,128)(2,1)}, u32[]{:S(2)}) copy-start(bf16[864,1152]{1,0:T(8,128)(2,1)} %weight_ref.3) | copy-start | bytes 5971972
  9.3 8.8 %copy-start.2 = (bf16[864,1152]{1,0:T(8,128)(2,1)S(1)}, bf16[864,1152]{1,0:T(8,128)(2,1)}, u32[]{:S(2)}) copy-start(bf16[864,1152]{1,0:T(8,128)(2,1)} %refs_0_.7) | copy-start | bytes 5971972
  9.3 9.3 %copy-start.3 = (bf16[288,1152]{1,0:T(8,128)(2,1)S(1)}, bf16[288,1152]{1,0:T(8,128)(2,1)}, u32[]{:S(2)}) copy-start(bf16[288,1152]{1,0:T(8,128)(2,1)} %refs_2_.5) | copy-start | bytes 1990660
  10.9 1.6 %collective-permute-start.3 = (bf16[1,128,1152]{2,1,0:T(8,128)(2,1)S(1)}, bf16[1,128,1152]{2,1,0:T(8,128)(2,1)S(1)}, u32[]{:S(2)}, u32[]{:S(2)}) collective-permute-start(bf16[1,128,1152]{2,1,0:T(8,128)(2,1)S(1)} %collective-permute-done.2.refs_0_), channel_id=1, source_target_pairs={{0,1},{1,0},{2,3},{3,2},{4,5},{5,4},{6,7},{7,6},{8,9},{9,8},{10,11... | collective-permute-start | bytes 884744 | tf_op jit(solution)/shard_map/ppermute | solution.py:233
  12.4 4.9 %collective-permute-start.5 = (bf16[288,1152]{1,0:T(8,128)(2,1)S(1)}, bf16[288,1152]{1,0:T(8,128)(2,1)S(1)}, u32[]{:S(2)}, u32[]{:S(2)}) collective-permute-start(bf16[288,1152]{1,0:T(8,128)(2,1)S(1)} %copy-done.4), channel_id=1, source_target_pairs={{0,1},{1,0},{2,3},{3,2},{4,5},{5,4},{6,7},{7,6},{8,9},{9,8},{10,11... | collective-permute-start | bytes 1990664 | tf_op jit(solution)/shard_map/ppermute | solution.py:233
  15.9 12.3 %copy-start.7 = (f32[6,1152]{1,0:T(8,128)S(1)}, f32[6,1152]{1,0:T(8,128)}, u32[]{:S(2)}) copy-start(f32[6,1152]{1,0:T(8,128)} %mod_ref.7) | copy-start | bytes 82948
  15.9 1.4 %collective-permute-start.4 = (bf16[288,256]{1,0:T(8,128)(2,1)S(1)}, bf16[288,256]{1,0:T(8,128)(2,1)S(1)}, u32[]{:S(2)}, u32[]{:S(2)}) collective-permute-start(bf16[288,256]{1,0:T(8,128)(2,1)S(1)} %get-tuple-element.39), channel_id=1, source_target_pairs={{0,1},{1,0},{2,3},{3,2},{4,5},{5,4},{6,7},{7,6},{8,9},{9,8},{10,11... | collective-permute-start | bytes 442376 | tf_op jit(solution)/shard_map/ppermute | solution.py:233
  18.1 21.8 %collective-permute-start.13 = (bf16[864,1152]{1,0:T(8,128)(2,1)S(1)}, bf16[864,1152]{1,0:T(8,128)(2,1)S(1)}, u32[]{:S(2)}, u32[]{:S(2)}) collective-permute-start(bf16[864,1152]{1,0:T(8,128)(2,1)S(1)} %copy-done.2), channel_id=1, source_target_pairs={{0,1},{1,0},{2,3},{3,2},{4,5},{5,4},{6,7},{7,6},{8,9},{9,8},{10,11... | collective-permute-start | bytes 5971976 | tf_op jit(solution)/shard_map/ppermute | solution.py:233
  18.6 21.4 %collective-permute-start.14 = (bf16[288,1152]{1,0:T(8,128)(2,1)S(1)}, bf16[288,1152]{1,0:T(8,128)(2,1)S(1)}, u32[]{:S(2)}, u32[]{:S(2)}) collective-permute-start(bf16[288,1152]{1,0:T(8,128)(2,1)S(1)} %copy-done.3), channel_id=1, source_target_pairs={{0,1},{1,0},{2,3},{3,2},{4,5},{5,4},{6,7},{7,6},{8,9},{9,8},{10,11... | collective-permute-start | bytes 1990664 | tf_op jit(solution)/shard_map/ppermute | solution.py:233
  18.7 9.5 %collective-permute-start.6 = (bf16[64,1152]{1,0:T(8,128)(2,1)S(1)}, bf16[64,1152]{1,0:T(8,128)(2,1)S(1)}, u32[]{:S(2)}, u32[]{:S(2)}) collective-permute-start(bf16[64,1152]{1,0:T(8,128)(2,1)S(1)} %get-tuple-element.42), channel_id=1, source_target_pairs={{0,2},{1,3},{2,0},{3,1},{4,6},{5,7},{6,4},{7,5},{8,10},{9,11},{10,... | collective-permute-start | bytes 442376 | tf_op jit(solution)/shard_map/ppermute | solution.py:233
  20.4 7.8 %collective-permute-start.8 = (bf16[64,1152]{1,0:T(8,128)(2,1)S(1)}, bf16[64,1152]{1,0:T(8,128)(2,1)S(1)}, u32[]{:S(2)}, u32[]{:S(2)}) collective-permute-start(bf16[64,1152]{1,0:T(8,128)(2,1)S(1)} %get-tuple-element.44), channel_id=1, source_target_pairs={{0,6},{1,7},{2,4},{3,5},{4,2},{5,3},{6,0},{7,1},{8,14},{9,15},{10,... | collective-permute-start | bytes 442376 | tf_op jit(solution)/shard_map/ppermute | solution.py:256
  21.9 5.9 %collective-permute-start.7 = (bf16[64,576]{1,0:T(8,128)(2,1)S(1)}, bf16[64,576]{1,0:T(8,128)(2,1)S(1)}, u32[]{:S(2)}, u32[]{:S(2)}) collective-permute-start(bf16[64,576]{1,0:T(8,128)(2,1)S(1)} %get-tuple-element.43), channel_id=1, source_target_pairs={{0,4},{4,0},{8,12},{12,8},{16,20},{20,16},{24,28},{28,24},{1,5},{5... | collective-permute-start | bytes 221192 | tf_op jit(solution)/shard_map/ppermute | solution.py:233
  28.6 7.0 %collective-permute-start.9 = (bf16[32,1152]{1,0:T(8,128)(2,1)S(1)}, bf16[32,1152]{1,0:T(8,128)(2,1)S(1)}, u32[]{:S(2)}, u32[]{:S(2)}) collective-permute-start(bf16[32,1152]{1,0:T(8,128)(2,1)S(1)} %get-tuple-element.47), channel_id=1, source_target_pairs={{0,24},{4,28},{8,16},{12,20},{16,8},{20,12},{24,0},{28,4},{1,25},{... | collective-permute-start | bytes 221192 | tf_op jit(solution)/shard_map/ppermute | solution.py:233
  32.5 5.8 %collective-permute-start.10 = (bf16[32,1152]{1,0:T(8,128)(2,1)S(1)}, bf16[32,1152]{1,0:T(8,128)(2,1)S(1)}, u32[]{:S(2)}, u32[]{:S(2)}) collective-permute-start(bf16[32,1152]{1,0:T(8,128)(2,1)S(1)} %get-tuple-element.48), channel_id=1, source_target_pairs={{0,16},{4,20},{8,24},{12,28},{16,0},{20,4},{24,8},{28,12},{1,17},{... | collective-permute-start | bytes 221192 | tf_op jit(solution)/shard_map/ppermute | solution.py:233
  32.5 5.8 %collective-permute-start.11 = (bf16[32,1152]{1,0:T(8,128)(2,1)S(1)}, bf16[32,1152]{1,0:T(8,128)(2,1)S(1)}, u32[]{:S(2)}, u32[]{:S(2)}) collective-permute-start(bf16[32,1152]{1,0:T(8,128)(2,1)S(1)} %get-tuple-element.49), channel_id=1, source_target_pairs={{0,8},{4,12},{8,0},{12,4},{16,24},{20,28},{24,16},{28,20},{1,9},{5... | collective-permute-start | bytes 221192 | tf_op jit(solution)/shard_map/ppermute | solution.py:233
  38.3 8.4 %collective-permute-start.15 = (bf16[128,1152]{1,0:T(8,128)(2,1)S(1)}, bf16[128,1152]{1,0:T(8,128)(2,1)S(1)}, u32[]{:S(2)}, u32[]{:S(2)}) collective-permute-start(bf16[128,1152]{1,0:T(8,128)(2,1)S(1)} %shard_map.70.refs_4_), channel_id=1, source_target_pairs={{0,2},{1,3},{2,0},{3,1},{4,6},{5,7},{6,4},{7,5},{8,10},{9,11},{10,... | collective-permute-start | bytes 884744 | tf_op jit(solution)/shard_map/ppermute | solution.py:233
  41.8 4.5 %collective-permute-start.16 = (bf16[64,576]{1,0:T(8,128)(2,1)S(1)}, bf16[64,576]{1,0:T(8,128)(2,1)S(1)}, u32[]{:S(2)}, u32[]{:S(2)}) collective-permute-start(bf16[64,576]{1,0:T(8,128)(2,1)S(1)} %get-tuple-element.55), channel_id=1, source_target_pairs={{0,4},{4,0},{8,12},{12,8},{16,20},{20,16},{24,28},{28,24},{1,5},{5... | collective-permute-start | bytes 221192 | tf_op jit(solution)/shard_map/ppermute | solution.py:233
  48.7 6.9 %collective-permute-start.17 = (bf16[64,1152]{1,0:T(8,128)(2,1)S(1)}, bf16[64,1152]{1,0:T(8,128)(2,1)S(1)}, u32[]{:S(2)}, u32[]{:S(2)}) collective-permute-start(bf16[64,1152]{1,0:T(8,128)(2,1)S(1)} %get-tuple-element.57), channel_id=1, source_target_pairs={{0,2},{1,3},{2,0},{3,1},{4,6},{5,7},{6,4},{7,5},{8,10},{9,11},{10,... | collective-permute-start | bytes 442376 | tf_op jit(solution)/shard_map/ppermute | solution.py:233
  50.3 6.5 %collective-permute-start.18 = (bf16[64,1152]{1,0:T(8,128)(2,1)S(1)}, bf16[64,1152]{1,0:T(8,128)(2,1)S(1)}, u32[]{:S(2)}, u32[]{:S(2)}) collective-permute-start(bf16[64,1152]{1,0:T(8,128)(2,1)S(1)} %get-tuple-element.58), channel_id=1, source_target_pairs={{0,6},{1,7},{2,4},{3,5},{4,2},{5,3},{6,0},{7,1},{8,14},{9,15},{10,... | collective-permute-start | bytes 442376 | tf_op jit(solution)/shard_map/ppermute | solution.py:256
  51.7 9.6 %collective-permute-start.12 = (bf16[4,16,1152]{2,1,0:T(8,128)(2,1)S(1)}, bf16[4,16,1152]{2,1,0:T(8,128)(2,1)S(1)}, u32[]{:S(2)}, u32[]{:S(2)}) collective-permute-start(bf16[4,16,1152]{2,1,0:T(8,128)(2,1)S(1)} %get-tuple-element.51), channel_id=1, source_target_pairs={{0,4},{4,0},{8,12},{12,8},{16,20},{20,16},{24,28},{28,24},{1,5},{5... | collective-permute-start | bytes 442376 | tf_op jit(solution)/shard_map/ppermute | solution.py:233
  56.9 6.3 %collective-permute-start.19 = (bf16[32,1152]{1,0:T(8,128)(2,1)S(1)}, bf16[32,1152]{1,0:T(8,128)(2,1)S(1)}, u32[]{:S(2)}, u32[]{:S(2)}) collective-permute-start(bf16[32,1152]{1,0:T(8,128)(2,1)S(1)} %get-tuple-element.59), channel_id=1, source_target_pairs={{0,24},{4,28},{8,16},{12,20},{16,8},{20,12},{24,0},{28,4},{1,25},{... | collective-permute-start | bytes 221192 | tf_op jit(solution)/shard_map/ppermute | solution.py:233
  58.2 6.5 %collective-permute-start.20 = (bf16[32,1152]{1,0:T(8,128)(2,1)S(1)}, bf16[32,1152]{1,0:T(8,128)(2,1)S(1)}, u32[]{:S(2)}, u32[]{:S(2)}) collective-permute-start(bf16[32,1152]{1,0:T(8,128)(2,1)S(1)} %get-tuple-element.60), channel_id=1, source_target_pairs={{0,16},{4,20},{8,24},{12,28},{16,0},{20,4},{24,8},{28,12},{1,17},{... | collective-permute-start | bytes 221192 | tf_op jit(solution)/shard_map/ppermute | solution.py:233
  58.2 6.5 %collective-permute-start.21 = (bf16[32,1152]{1,0:T(8,128)(2,1)S(1)}, bf16[32,1152]{1,0:T(8,128)(2,1)S(1)}, u32[]{:S(2)}, u32[]{:S(2)}) collective-permute-start(bf16[32,1152]{1,0:T(8,128)(2,1)S(1)} %get-tuple-element.61), channel_id=1, source_target_pairs={{0,8},{4,12},{8,0},{12,4},{16,24},{20,28},{24,16},{28,20},{1,9},{5... | collective-permute-start | bytes 221192 | tf_op jit(solution)/shard_map/ppermute | solution.py:233

commit v24 on v23

--- a/solution.py
+++ b/solution.py
@@ -313,7 +313,6 @@
         own_shapes + far_shapes,
     )
     late_pair = with_sister(temporal_out, parts[0])
-    temporal_pair = with_sister(temporal_qkv, parts[0])
     updates = return_updates((parts[0], project_paired(parts[1], out_pair)), parts[2:])
     middle, middle_sent, *parts = call(
         functools.partial(middle_kernel, pieces, groups),
@@ -321,6 +320,7 @@
         [shape((pieces, period, width), BF16)] * 2 + piece_shapes,
         [pltpu.VMEM((pieces, 2 * period, width), BF16)],
     )
+    temporal_pair = with_sister(temporal_qkv, middle)
     arrived = exchange_frames(parts)
     (segment,) = call(join_kernel, arrived, [shape((rows, width), BF16)])
     segments = across(segment)

time: 65.7 us -> 66.3 us (level)
  transfers between devices with their start and end apart: 22 -> 22, of which waited for: 11 -> 11; matrix products, arithmetic and copies ran while one was open for 0% -> 0% of each run, Pallas kernels for 12% -> 11%
where the time goes in v24:
time: 66.3 us; the launch traced here: 66.1 us
  waiting for transfers between devices  26.4 us (40%)
  starting transfers between devices  25 us (38%)
  Pallas kernels  11.1 us (17%)
  local copies, waits for them, and re-layouts  3.33 us (5%)
    ppermute x20, waiting for transfers between devices, swap(): return lax.ppermute(value, axis, [(at, at ^ offset) for at in range(size)])  25.2 us
    ppermute x20, starting transfers between devices, swap(): return lax.ppermute(value, axis, [(at, at ^ offset) for at in range(size)])  22.1 us
    pallas_call x12, Pallas kernels, call(): pl.pallas_call(body, out_shape=outs, in_specs=[pl.BlockSpec(memory_space=...  11.1 us
    unnamed x16, local copies, waits for them, and re-layouts  3.33 us
    ppermute x2, starting transfers between devices, swap_diagonal(): return lax.ppermute(value, ('frame', 'patch'), pairs)  2.89 us
  transfers between devices with their start and end apart: 22, of which 11 were waited for; matrix products, arithmetic and copies ran while one was open for 0% of the time, Pallas kernels for 11%

profile of v24, /device:TPU:0, one launch (start us, length us, event | category | flops | bytes accessed | tf_op | source)
XLA Modules:
  0.0 66.1 jit_solution(1613397738141026831)
XLA Ops:
  0.5 2.5 %collective-permute-start.2 = (bf16[1,128,1152]{2,1,0:T(8,128)(2,1)}, bf16[1,128,1152]{2,1,0:T(8,128)(2,1)S(1)}, u32[]{:S(2)}, u32[]{:S(2)}) collective-permute-start(bf16[1,128,1152]{2,1,0:T(8,128)(2,1)} %own_ref.1), channel_id=1, source_target_pairs={{0,2},{1,3},{2,0},{3,1},{4,6},{5,7},{6,4},{7,5},{8,10},{9,11},{10,... | collective-permute-start | bytes 884744 | tf_op jit(solution)/shard_map/ppermute | solution.py:233
  3.0 1.0 %copy-done.5 = bf16[1,128,1152]{2,1,0:T(8,128)(2,1)S(1)} copy-done((bf16[1,128,1152]{2,1,0:T(8,128)(2,1)S(1)}, bf16[1,128,1152]{2,1,0:T(8,128)(2,1)}, u32[]{:S(2)}) %copy-start.5) | copy-done | bytes 294936
  4.1 1.8 %collective-permute-start.1 = (bf16[64,1152]{1,0:T(8,128)(2,1)S(1)}, bf16[64,1152]{1,0:T(8,128)(2,1)S(1)}, u32[]{:S(2)}, u32[]{:S(2)}) collective-permute-start(bf16[64,1152]{1,0:T(8,128)(2,1)S(1)} %get-tuple-element.36), channel_id=1, source_target_pairs={{0,4},{4,0},{8,12},{12,8},{16,20},{20,16},{24,28},{28,24},{1,5},{5... | collective-permute-start | bytes 442376 | tf_op jit(solution)/shard_map/ppermute | solution.py:233
  5.9 1.6 %copy-done = bf16[864,1152]{1,0:T(8,128)(2,1)S(1)} copy-done((bf16[864,1152]{1,0:T(8,128)(2,1)S(1)}, bf16[864,1152]{1,0:T(8,128)(2,1)}, u32[]{:S(2)}) %copy-start) | copy-done | bytes 1990680
  7.4 0.8 %copy-done.6 = f32[6,1152]{1,0:T(8,128)S(1)} copy-done((f32[6,1152]{1,0:T(8,128)S(1)}, f32[6,1152]{1,0:T(8,128)}, u32[]{:S(2)}) %copy-start.6) | copy-done | bytes 27672
  8.2 1.1 %shard_map.65.near_ref = f32[864,256]{1,0:T(8,128)S(1)} custom-call(f32[6,1152]{1,0:T(8,128)S(1)} %copy-done.6, bf16[864,1152]{1,0:T(8,128)(2,1)S(1)} %copy-done, bf16[1,128,1152]{2,1,0:T(8,128)(2,1)S(1)} %copy-done.5, bf16[1,128,1152]{2,1,0:T(8,128)(2,1)S(1)} %collective-permute-done.sister_ref), custom_call_target="tpu_custom_call" | custom-call | flops 1 | bytes 1 | tf_op jit(solution)/shard_map/pallas_call | solution.py:220
  9.3 1.6 %collective-permute-done.2.refs_0_ = bf16[1,128,1152]{2,1,0:T(8,128)(2,1)S(1)} collective-permute-done((bf16[1,128,1152]{2,1,0:T(8,128)(2,1)}, bf16[1,128,1152]{2,1,0:T(8,128)(2,1)S(1)}, u32[]{:S(2)}, u32[]{:S(2)}) %collective-permute-start.2) | collective-permute-done | bytes 294944 | tf_op jit(solution)/shard_map/ppermute | solution.py:233
  10.9 1.6 %collective-permute-done.3.refs_1_ = bf16[1,128,1152]{2,1,0:T(8,128)(2,1)S(1)} collective-permute-done((bf16[1,128,1152]{2,1,0:T(8,128)(2,1)S(1)}, bf16[1,128,1152]{2,1,0:T(8,128)(2,1)S(1)}, u32[]{:S(2)}, u32[]{:S(2)}) %collective-permute-start.3) | collective-permute-done | bytes 294944 | tf_op jit(solution)/shard_map/ppermute | solution.py:233
  12.6 3.3 %shard_map.66 = (bf16[288,256]{1,0:T(8,128)(2,1)S(1)}, bf16[288,256]{1,0:T(8,128)(2,1)S(1)}) custom-call(f32[6,1152]{1,0:T(8,128)S(1)} %copy-done.6, bf16[864,1152]{1,0:T(8,128)(2,1)S(1)} %copy-done.1, f32[864,256]{1,0:T(8,128)S(1)} %shard_map.65.near_ref, bf16[1,128,1152]{2,1,0:T(8,128)(2,1)S(1)} %collective-permute-done.2.refs_0_, ...), custom_call_target="tpu_custom_call" | custom-call | flops 1 | bytes 1 | tf_op jit(solution)/shard_map/pallas_call | solution.py:220
  16.4 1.0 %collective-permute-done.4.refs_1_ = bf16[288,256]{1,0:T(8,128)(2,1)S(1)} collective-permute-done((bf16[288,256]{1,0:T(8,128)(2,1)S(1)}, bf16[288,256]{1,0:T(8,128)(2,1)S(1)}, u32[]{:S(2)}, u32[]{:S(2)}) %collective-permute-start.4) | collective-permute-done | bytes 147488 | tf_op jit(solution)/shard_map/ppermute | solution.py:233
  17.4 0.7 %shard_map.67 = (f32[64,1152]{1,0:T(8,128)S(1)}, bf16[64,576]{1,0:T(8,128)(2,1)S(1)}, bf16[64,1152]{1,0:T(8,128)(2,1)S(1)}, bf16[64,1152]{1,0:T(8,128)(2,1)S(1)}) custom-call(bf16[288,256]{1,0:T(8,128)(2,1)S(1)} %get-tuple-element.38.refs_0_, bf16[288,256]{1,0:T(8,128)(2,1)S(1)} %collective-permute-done.4.refs_1_, bf16[288,1152]{1,0:T(8,128)(2,1)S(1)} %copy-done.4, ...), custom_call_target="tpu_custom_call" | custom-call | flops 1 | bytes 1 | tf_op jit(solution)/shard_map/pallas_call | solution.py:220
  18.1 1.8 %collective-permute-start.6 = (bf16[64,1152]{1,0:T(8,128)(2,1)S(1)}, bf16[64,1152]{1,0:T(8,128)(2,1)S(1)}, u32[]{:S(2)}, u32[]{:S(2)}) collective-permute-start(bf16[64,1152]{1,0:T(8,128)(2,1)S(1)} %get-tuple-element.42), channel_id=1, source_target_pairs={{0,2},{1,3},{2,0},{3,1},{4,6},{5,7},{6,4},{7,5},{8,10},{9,11},{10,... | collective-permute-start | bytes 442376 | tf_op jit(solution)/shard_map/ppermute | solution.py:233
  19.9 1.4 %collective-permute-start.8 = (bf16[64,1152]{1,0:T(8,128)(2,1)S(1)}, bf16[64,1152]{1,0:T(8,128)(2,1)S(1)}, u32[]{:S(2)}, u32[]{:S(2)}) collective-permute-start(bf16[64,1152]{1,0:T(8,128)(2,1)S(1)} %get-tuple-element.44), channel_id=1, source_target_pairs={{0,6},{1,7},{2,4},{3,5},{4,2},{5,3},{6,0},{7,1},{8,14},{9,15},{10,... | collective-permute-start | bytes 442376 | tf_op jit(solution)/shard_map/ppermute | solution.py:256
  21.7 5.7 %collective-permute-done.7.head_ref = bf16[64,576]{1,0:T(8,128)(2,1)S(1)} collective-permute-done((bf16[64,576]{1,0:T(8,128)(2,1)S(1)}, bf16[64,576]{1,0:T(8,128)(2,1)S(1)}, u32[]{:S(2)}, u32[]{:S(2)}) %collective-permute-start.7) | collective-permute-done | bytes 73760 | tf_op jit(solution)/shard_map/ppermute | solution.py:233
  28.7 3.7 %collective-permute-start.9 = (bf16[32,1152]{1,0:T(8,128)(2,1)S(1)}, bf16[32,1152]{1,0:T(8,128)(2,1)S(1)}, u32[]{:S(2)}, u32[]{:S(2)}) collective-permute-start(bf16[32,1152]{1,0:T(8,128)(2,1)S(1)} %get-tuple-element.47), channel_id=1, source_target_pairs={{0,24},{4,28},{8,16},{12,20},{16,8},{20,12},{24,0},{28,4},{1,25},{... | collective-permute-start | bytes 221192 | tf_op jit(solution)/shard_map/ppermute | solution.py:233
  32.5 0.6 collective-permute-start.11
  33.1 2.3 %collective-permute-done.9.refs_0_ = bf16[32,1152]{1,0:T(8,128)(2,1)S(1)} collective-permute-done((bf16[32,1152]{1,0:T(8,128)(2,1)S(1)}, bf16[32,1152]{1,0:T(8,128)(2,1)S(1)}, u32[]{:S(2)}, u32[]{:S(2)}) %collective-permute-start.9) | collective-permute-done | bytes 73760 | tf_op jit(solution)/shard_map/ppermute | solution.py:233
  35.4 3.6 %collective-permute-done.10.refs_1_ = bf16[32,1152]{1,0:T(8,128)(2,1)S(1)} collective-permute-done((bf16[32,1152]{1,0:T(8,128)(2,1)S(1)}, bf16[32,1152]{1,0:T(8,128)(2,1)S(1)}, u32[]{:S(2)}, u32[]{:S(2)}) %collective-permute-start.10) | collective-permute-done | bytes 73760 | tf_op jit(solution)/shard_map/ppermute | solution.py:233
  39.0 1.6 %collective-permute-start.15 = (bf16[128,1152]{1,0:T(8,128)(2,1)S(1)}, bf16[128,1152]{1,0:T(8,128)(2,1)S(1)}, u32[]{:S(2)}, u32[]{:S(2)}) collective-permute-start(bf16[128,1152]{1,0:T(8,128)(2,1)S(1)} %shard_map.70.refs_4_), channel_id=1, source_target_pairs={{0,2},{1,3},{2,0},{3,1},{4,6},{5,7},{6,4},{7,5},{8,10},{9,11},{10,... | collective-permute-start | bytes 884744 | tf_op jit(solution)/shard_map/ppermute | solution.py:233
  40.6 1.9 %shard_map.71 = (f32[64,1152]{1,0:T(8,128)S(1)}, bf16[64,576]{1,0:T(8,128)(2,1)S(1)}) custom-call(bf16[864,1152]{1,0:T(8,128)(2,1)S(1)} %copy-done.2, bf16[864,1152]{1,0:T(8,128)(2,1)S(1)} %collective-permute-done.13.refs_1_, bf16[288,1152]{1,0:T(8,128)(2,1)S(1)} %copy-done.3, bf16[288,1152]{1,0:T(8,128)(2,1)S(1)} %collective-permute-done.14.refs_3_.refs_1_, ...), custom_call_target="tpu_custom_call" | custom-call | flops 1 | bytes 1 | tf_op jit(solution)/shard_map/pallas_call | solution.py:220
  42.5 1.6 %collective-permute-start.16 = (bf16[64,576]{1,0:T(8,128)(2,1)S(1)}, bf16[64,576]{1,0:T(8,128)(2,1)S(1)}, u32[]{:S(2)}, u32[]{:S(2)}) collective-permute-start(bf16[64,576]{1,0:T(8,128)(2,1)S(1)} %get-tuple-element.55), channel_id=1, source_target_pairs={{0,4},{4,0},{8,12},{12,8},{16,20},{20,16},{24,28},{28,24},{1,5},{5... | collective-permute-start | bytes 221192 | tf_op jit(solution)/shard_map/ppermute | solution.py:233
  44.0 3.0 %collective-permute-done.16.head_ref = bf16[64,576]{1,0:T(8,128)(2,1)S(1)} collective-permute-done((bf16[64,576]{1,0:T(8,128)(2,1)S(1)}, bf16[64,576]{1,0:T(8,128)(2,1)S(1)}, u32[]{:S(2)}, u32[]{:S(2)}) %collective-permute-start.16) | collective-permute-done | bytes 73760 | tf_op jit(solution)/shard_map/ppermute | solution.py:233
  47.4 2.0 %shard_map.73 = (bf16[64,1152]{1,0:T(8,128)(2,1)S(1)}, bf16[64,1152]{1,0:T(8,128)(2,1)S(1)}) custom-call(bf16[864,1152]{1,0:T(8,128)(2,1)S(1)} %copy-done.2, bf16[864,1152]{1,0:T(8,128)(2,1)S(1)} %collective-permute-done.13.refs_1_, bf16[288,1152]{1,0:T(8,128)(2,1)S(1)} %copy-done.3, bf16[288,1152]{1,0:T(8,128)(2,1)S(1)} %collective-permute-done.14.refs_3_.refs_1_, ...), custom_call_target="tpu_custom_call" | custom-call | flops 1 | bytes 1 | tf_op jit(solution)/shard_map/pallas_call | solution.py:220
  49.4 1.6 %collective-permute-start.17 = (bf16[64,1152]{1,0:T(8,128)(2,1)S(1)}, bf16[64,1152]{1,0:T(8,128)(2,1)S(1)}, u32[]{:S(2)}, u32[]{:S(2)}) collective-permute-start(bf16[64,1152]{1,0:T(8,128)(2,1)S(1)} %get-tuple-element.57), channel_id=1, source_target_pairs={{0,2},{1,3},{2,0},{3,1},{4,6},{5,7},{6,4},{7,5},{8,10},{9,11},{10,... | collective-permute-start | bytes 442376 | tf_op jit(solution)/shard_map/ppermute | solution.py:233
  50.9 1.5 %collective-permute-start.18 = (bf16[64,1152]{1,0:T(8,128)(2,1)S(1)}, bf16[64,1152]{1,0:T(8,128)(2,1)S(1)}, u32[]{:S(2)}, u32[]{:S(2)}) collective-permute-start(bf16[64,1152]{1,0:T(8,128)(2,1)S(1)} %get-tuple-element.58), channel_id=1, source_target_pairs={{0,6},{1,7},{2,4},{3,5},{4,2},{5,3},{6,0},{7,1},{8,14},{9,15},{10,... | collective-permute-start | bytes 442376 | tf_op jit(solution)/shard_map/ppermute | solution.py:256
  52.9 3.2 %collective-permute-done.17.refs_1_ = bf16[64,1152]{1,0:T(8,128)(2,1)S(1)} collective-permute-done((bf16[64,1152]{1,0:T(8,128)(2,1)S(1)}, bf16[64,1152]{1,0:T(8,128)(2,1)S(1)}, u32[]{:S(2)}, u32[]{:S(2)}) %collective-permute-start.17) | collective-permute-done | bytes 147488 | tf_op jit(solution)/shard_map/ppermute | solution.py:233
  56.1 1.2 %collective-permute-done.18.refs_3_ = bf16[64,1152]{1,0:T(8,128)(2,1)S(1)} collective-permute-done((bf16[64,1152]{1,0:T(8,128)(2,1)S(1)}, bf16[64,1152]{1,0:T(8,128)(2,1)S(1)}, u32[]{:S(2)}, u32[]{:S(2)}) %collective-permute-start.18) | collective-permute-done | bytes 147488 | tf_op jit(solution)/shard_map/ppermute | solution.py:256
  57.4 2.2 %collective-permute-start.19 = (bf16[32,1152]{1,0:T(8,128)(2,1)S(1)}, bf16[32,1152]{1,0:T(8,128)(2,1)S(1)}, u32[]{:S(2)}, u32[]{:S(2)}) collective-permute-start(bf16[32,1152]{1,0:T(8,128)(2,1)S(1)} %get-tuple-element.59), channel_id=1, source_target_pairs={{0,24},{4,28},{8,16},{12,20},{16,8},{20,12},{24,0},{28,4},{1,25},{... | collective-permute-start | bytes 221192 | tf_op jit(solution)/shard_map/ppermute | solution.py:233
  59.6 2.3 %collective-permute-start.21 = (bf16[32,1152]{1,0:T(8,128)(2,1)S(1)}, bf16[32,1152]{1,0:T(8,128)(2,1)S(1)}, u32[]{:S(2)}, u32[]{:S(2)}) collective-permute-start(bf16[32,1152]{1,0:T(8,128)(2,1)S(1)} %get-tuple-element.61), channel_id=1, source_target_pairs={{0,8},{4,12},{8,0},{12,4},{16,24},{20,28},{24,16},{28,20},{1,9},{5... | collective-permute-start | bytes 221192 | tf_op jit(solution)/shard_map/ppermute | solution.py:233
  61.9 1.8 %collective-permute-done.19.refs_0_ = bf16[32,1152]{1,0:T(8,128)(2,1)S(1)} collective-permute-done((bf16[32,1152]{1,0:T(8,128)(2,1)S(1)}, bf16[32,1152]{1,0:T(8,128)(2,1)S(1)}, u32[]{:S(2)}, u32[]{:S(2)}) %collective-permute-start.19) | collective-permute-done | bytes 73760 | tf_op jit(solution)/shard_map/ppermute | solution.py:233
  63.7 1.6 %collective-permute-done.20.refs_1_ = bf16[32,1152]{1,0:T(8,128)(2,1)S(1)} collective-permute-done((bf16[32,1152]{1,0:T(8,128)(2,1)S(1)}, bf16[32,1152]{1,0:T(8,128)(2,1)S(1)}, u32[]{:S(2)}, u32[]{:S(2)}) %collective-permute-start.20) | collective-permute-done | bytes 73760 | tf_op jit(solution)/shard_map/ppermute | solution.py:233
  65.2 0.8 %shard_map.75 = bf16[8,16,1152]{2,1,0:T(8,128)(2,1)} custom-call(f32[6,1152]{1,0:T(8,128)S(1)} %copy-done.7, bf16[4,16,1152]{2,1,0:T(8,128)(2,1)S(1)} %get-tuple-element.45.kept_ref, bf16[4,16,1152]{2,1,0:T(8,128)(2,1)S(1)} %collective-permute-done.12.other_ref, bf16[32,1152]{1,0:T(8,128)(2,1)S(1)} %collective-permute-done.19.refs_0_, ...), custom_call_target="tpu_custom_call" | custom-call | flops 1 | bytes 1 | tf_op jit(solution)/shard_map/pallas_call | solution.py:220
  (40 shorter events, 3.8 us)
Async XLA Ops:
  0.0 3.0 %collective-permute-start = (bf16[1,128,1152]{2,1,0:T(8,128)(2,1)}, bf16[1,128,1152]{2,1,0:T(8,128)(2,1)S(1)}, u32[]{:S(2)}, u32[]{:S(2)}) collective-permute-start(bf16[1,128,1152]{2,1,0:T(8,128)(2,1)} %own_ref.1), channel_id=1, source_target_pairs={{0,1},{1,0},{2,3},{3,2},{4,5},{5,4},{6,7},{7,6},{8,9},{9,8},{10,11... | collective-permute-start | bytes 884744 | tf_op jit(solution)/shard_map/ppermute | solution.py:233
  0.5 10.4 %collective-permute-start.2 = (bf16[1,128,1152]{2,1,0:T(8,128)(2,1)}, bf16[1,128,1152]{2,1,0:T(8,128)(2,1)S(1)}, u32[]{:S(2)}, u32[]{:S(2)}) collective-permute-start(bf16[1,128,1152]{2,1,0:T(8,128)(2,1)} %own_ref.1), channel_id=1, source_target_pairs={{0,2},{1,3},{2,0},{3,1},{4,6},{5,7},{6,4},{7,5},{8,10},{9,11},{10,... | collective-permute-start | bytes 884744 | tf_op jit(solution)/shard_map/ppermute | solution.py:233
  3.0 1.0 %copy-start.5 = (bf16[1,128,1152]{2,1,0:T(8,128)(2,1)S(1)}, bf16[1,128,1152]{2,1,0:T(8,128)(2,1)}, u32[]{:S(2)}) copy-start(bf16[1,128,1152]{2,1,0:T(8,128)(2,1)} %own_ref.1) | copy-start | bytes 884740
  4.1 6.8 %collective-permute-start.1 = (bf16[64,1152]{1,0:T(8,128)(2,1)S(1)}, bf16[64,1152]{1,0:T(8,128)(2,1)S(1)}, u32[]{:S(2)}, u32[]{:S(2)}) collective-permute-start(bf16[64,1152]{1,0:T(8,128)(2,1)S(1)} %get-tuple-element.36), channel_id=1, source_target_pairs={{0,4},{4,0},{8,12},{12,8},{16,20},{20,16},{24,28},{28,24},{1,5},{5... | collective-permute-start | bytes 442376 | tf_op jit(solution)/shard_map/ppermute | solution.py:233
  5.8 1.6 %copy-start = (bf16[864,1152]{1,0:T(8,128)(2,1)S(1)}, bf16[864,1152]{1,0:T(8,128)(2,1)}, u32[]{:S(2)}) copy-start(bf16[864,1152]{1,0:T(8,128)(2,1)} %weight_ref.3) | copy-start | bytes 5971972
  7.4 0.8 %copy-start.6 = (f32[6,1152]{1,0:T(8,128)S(1)}, f32[6,1152]{1,0:T(8,128)}, u32[]{:S(2)}) copy-start(f32[6,1152]{1,0:T(8,128)} %mod_ref.7) | copy-start | bytes 82948
  8.2 4.3 %copy-start.4 = (bf16[288,1152]{1,0:T(8,128)(2,1)S(1)}, bf16[288,1152]{1,0:T(8,128)(2,1)}, u32[]{:S(2)}) copy-start(bf16[288,1152]{1,0:T(8,128)(2,1)} %refs_0_.4) | copy-start | bytes 1990660
  8.2 4.4 %copy-start.1 = (bf16[864,1152]{1,0:T(8,128)(2,1)S(1)}, bf16[864,1152]{1,0:T(8,128)(2,1)}, u32[]{:S(2)}) copy-start(bf16[864,1152]{1,0:T(8,128)(2,1)} %weight_ref.3) | copy-start | bytes 5971972
  10.9 1.6 %collective-permute-start.3 = (bf16[1,128,1152]{2,1,0:T(8,128)(2,1)S(1)}, bf16[1,128,1152]{2,1,0:T(8,128)(2,1)S(1)}, u32[]{:S(2)}, u32[]{:S(2)}) collective-permute-start(bf16[1,128,1152]{2,1,0:T(8,128)(2,1)S(1)} %collective-permute-done.2.refs_0_), channel_id=1, source_target_pairs={{0,1},{1,0},{2,3},{3,2},{4,5},{5,4},{6,7},{7,6},{8,9},{9,8},{10,11... | collective-permute-start | bytes 884744 | tf_op jit(solution)/shard_map/ppermute | solution.py:233
  12.4 4.9 %collective-permute-start.5 = (bf16[288,1152]{1,0:T(8,128)(2,1)S(1)}, bf16[288,1152]{1,0:T(8,128)(2,1)S(1)}, u32[]{:S(2)}, u32[]{:S(2)}) collective-permute-start(bf16[288,1152]{1,0:T(8,128)(2,1)S(1)} %copy-done.4), channel_id=1, source_target_pairs={{0,1},{1,0},{2,3},{3,2},{4,5},{5,4},{6,7},{7,6},{8,9},{9,8},{10,11... | collective-permute-start | bytes 1990664 | tf_op jit(solution)/shard_map/ppermute | solution.py:233
  15.9 11.8 %copy-start.7 = (f32[6,1152]{1,0:T(8,128)S(1)}, f32[6,1152]{1,0:T(8,128)}, u32[]{:S(2)}) copy-start(f32[6,1152]{1,0:T(8,128)} %mod_ref.7) | copy-start | bytes 82948
  15.9 1.4 %collective-permute-start.4 = (bf16[288,256]{1,0:T(8,128)(2,1)S(1)}, bf16[288,256]{1,0:T(8,128)(2,1)S(1)}, u32[]{:S(2)}, u32[]{:S(2)}) collective-permute-start(bf16[288,256]{1,0:T(8,128)(2,1)S(1)} %get-tuple-element.39), channel_id=1, source_target_pairs={{0,1},{1,0},{2,3},{3,2},{4,5},{5,4},{6,7},{7,6},{8,9},{9,8},{10,11... | collective-permute-start | bytes 442376 | tf_op jit(solution)/shard_map/ppermute | solution.py:233
  17.4 10.8 %copy-start.2 = (bf16[864,1152]{1,0:T(8,128)(2,1)S(1)}, bf16[864,1152]{1,0:T(8,128)(2,1)}, u32[]{:S(2)}) copy-start(bf16[864,1152]{1,0:T(8,128)(2,1)} %refs_0_.7) | copy-start | bytes 5971972
  17.4 10.9 %copy-start.3 = (bf16[288,1152]{1,0:T(8,128)(2,1)S(1)}, bf16[288,1152]{1,0:T(8,128)(2,1)}, u32[]{:S(2)}) copy-start(bf16[288,1152]{1,0:T(8,128)(2,1)} %refs_2_.5) | copy-start | bytes 1990660
  18.1 9.6 %collective-permute-start.6 = (bf16[64,1152]{1,0:T(8,128)(2,1)S(1)}, bf16[64,1152]{1,0:T(8,128)(2,1)S(1)}, u32[]{:S(2)}, u32[]{:S(2)}) collective-permute-start(bf16[64,1152]{1,0:T(8,128)(2,1)S(1)} %get-tuple-element.42), channel_id=1, source_target_pairs={{0,2},{1,3},{2,0},{3,1},{4,6},{5,7},{6,4},{7,5},{8,10},{9,11},{10,... | collective-permute-start | bytes 442376 | tf_op jit(solution)/shard_map/ppermute | solution.py:233
  19.9 7.8 %collective-permute-start.8 = (bf16[64,1152]{1,0:T(8,128)(2,1)S(1)}, bf16[64,1152]{1,0:T(8,128)(2,1)S(1)}, u32[]{:S(2)}, u32[]{:S(2)}) collective-permute-start(bf16[64,1152]{1,0:T(8,128)(2,1)S(1)} %get-tuple-element.44), channel_id=1, source_target_pairs={{0,6},{1,7},{2,4},{3,5},{4,2},{5,3},{6,0},{7,1},{8,14},{9,15},{10,... | collective-permute-start | bytes 442376 | tf_op jit(solution)/shard_map/ppermute | solution.py:256
  21.4 6.0 %collective-permute-start.7 = (bf16[64,576]{1,0:T(8,128)(2,1)S(1)}, bf16[64,576]{1,0:T(8,128)(2,1)S(1)}, u32[]{:S(2)}, u32[]{:S(2)}) collective-permute-start(bf16[64,576]{1,0:T(8,128)(2,1)S(1)} %get-tuple-element.43), channel_id=1, source_target_pairs={{0,4},{4,0},{8,12},{12,8},{16,20},{20,16},{24,28},{28,24},{1,5},{5... | collective-permute-start | bytes 221192 | tf_op jit(solution)/shard_map/ppermute | solution.py:233
  28.2 12.4 %collective-permute-start.13 = (bf16[864,1152]{1,0:T(8,128)(2,1)S(1)}, bf16[864,1152]{1,0:T(8,128)(2,1)S(1)}, u32[]{:S(2)}, u32[]{:S(2)}) collective-permute-start(bf16[864,1152]{1,0:T(8,128)(2,1)S(1)} %copy-done.2), channel_id=1, source_target_pairs={{0,1},{1,0},{2,3},{3,2},{4,5},{5,4},{6,7},{7,6},{8,9},{9,8},{10,11... | collective-permute-start | bytes 5971976 | tf_op jit(solution)/shard_map/ppermute | solution.py:233
  28.2 12.3 %collective-permute-start.14 = (bf16[288,1152]{1,0:T(8,128)(2,1)S(1)}, bf16[288,1152]{1,0:T(8,128)(2,1)S(1)}, u32[]{:S(2)}, u32[]{:S(2)}) collective-permute-start(bf16[288,1152]{1,0:T(8,128)(2,1)S(1)} %copy-done.3), channel_id=1, source_target_pairs={{0,1},{1,0},{2,3},{3,2},{4,5},{5,4},{6,7},{7,6},{8,9},{9,8},{10,11... | collective-permute-start | bytes 1990664 | tf_op jit(solution)/shard_map/ppermute | solution.py:233
  28.7 6.6 %collective-permute-start.9 = (bf16[32,1152]{1,0:T(8,128)(2,1)S(1)}, bf16[32,1152]{1,0:T(8,128)(2,1)S(1)}, u32[]{:S(2)}, u32[]{:S(2)}) collective-permute-start(bf16[32,1152]{1,0:T(8,128)(2,1)S(1)} %get-tuple-element.47), channel_id=1, source_target_pairs={{0,24},{4,28},{8,16},{12,20},{16,8},{20,12},{24,0},{28,4},{1,25},{... | collective-permute-start | bytes 221192 | tf_op jit(solution)/shard_map/ppermute | solution.py:233
  32.5 6.5 %collective-permute-start.10 = (bf16[32,1152]{1,0:T(8,128)(2,1)S(1)}, bf16[32,1152]{1,0:T(8,128)(2,1)S(1)}, u32[]{:S(2)}, u32[]{:S(2)}) collective-permute-start(bf16[32,1152]{1,0:T(8,128)(2,1)S(1)} %get-tuple-element.48), channel_id=1, source_target_pairs={{0,16},{4,20},{8,24},{12,28},{16,0},{20,4},{24,8},{28,12},{1,17},{... | collective-permute-start | bytes 221192 | tf_op jit(solution)/shard_map/ppermute | solution.py:233
  32.5 6.5 %collective-permute-start.11 = (bf16[32,1152]{1,0:T(8,128)(2,1)S(1)}, bf16[32,1152]{1,0:T(8,128)(2,1)S(1)}, u32[]{:S(2)}, u32[]{:S(2)}) collective-permute-start(bf16[32,1152]{1,0:T(8,128)(2,1)S(1)} %get-tuple-element.49), channel_id=1, source_target_pairs={{0,8},{4,12},{8,0},{12,4},{16,24},{20,28},{24,16},{28,20},{1,9},{5... | collective-permute-start | bytes 221192 | tf_op jit(solution)/shard_map/ppermute | solution.py:233
  39.0 8.4 %collective-permute-start.15 = (bf16[128,1152]{1,0:T(8,128)(2,1)S(1)}, bf16[128,1152]{1,0:T(8,128)(2,1)S(1)}, u32[]{:S(2)}, u32[]{:S(2)}) collective-permute-start(bf16[128,1152]{1,0:T(8,128)(2,1)S(1)} %shard_map.70.refs_4_), channel_id=1, source_target_pairs={{0,2},{1,3},{2,0},{3,1},{4,6},{5,7},{6,4},{7,5},{8,10},{9,11},{10,... | collective-permute-start | bytes 884744 | tf_op jit(solution)/shard_map/ppermute | solution.py:233
  42.5 4.5 %collective-permute-start.16 = (bf16[64,576]{1,0:T(8,128)(2,1)S(1)}, bf16[64,576]{1,0:T(8,128)(2,1)S(1)}, u32[]{:S(2)}, u32[]{:S(2)}) collective-permute-start(bf16[64,576]{1,0:T(8,128)(2,1)S(1)} %get-tuple-element.55), channel_id=1, source_target_pairs={{0,4},{4,0},{8,12},{12,8},{16,20},{20,16},{24,28},{28,24},{1,5},{5... | collective-permute-start | bytes 221192 | tf_op jit(solution)/shard_map/ppermute | solution.py:233
  49.4 6.8 %collective-permute-start.17 = (bf16[64,1152]{1,0:T(8,128)(2,1)S(1)}, bf16[64,1152]{1,0:T(8,128)(2,1)S(1)}, u32[]{:S(2)}, u32[]{:S(2)}) collective-permute-start(bf16[64,1152]{1,0:T(8,128)(2,1)S(1)} %get-tuple-element.57), channel_id=1, source_target_pairs={{0,2},{1,3},{2,0},{3,1},{4,6},{5,7},{6,4},{7,5},{8,10},{9,11},{10,... | collective-permute-start | bytes 442376 | tf_op jit(solution)/shard_map/ppermute | solution.py:233
  50.9 6.4 %collective-permute-start.18 = (bf16[64,1152]{1,0:T(8,128)(2,1)S(1)}, bf16[64,1152]{1,0:T(8,128)(2,1)S(1)}, u32[]{:S(2)}, u32[]{:S(2)}) collective-permute-start(bf16[64,1152]{1,0:T(8,128)(2,1)S(1)} %get-tuple-element.58), channel_id=1, source_target_pairs={{0,6},{1,7},{2,4},{3,5},{4,2},{5,3},{6,0},{7,1},{8,14},{9,15},{10,... | collective-permute-start | bytes 442376 | tf_op jit(solution)/shard_map/ppermute | solution.py:256
  52.4 9.5 %collective-permute-start.12 = (bf16[4,16,1152]{2,1,0:T(8,128)(2,1)S(1)}, bf16[4,16,1152]{2,1,0:T(8,128)(2,1)S(1)}, u32[]{:S(2)}, u32[]{:S(2)}) collective-permute-start(bf16[4,16,1152]{2,1,0:T(8,128)(2,1)S(1)} %get-tuple-element.51), channel_id=1, source_target_pairs={{0,4},{4,0},{8,12},{12,8},{16,20},{20,16},{24,28},{28,24},{1,5},{5... | collective-permute-start | bytes 442376 | tf_op jit(solution)/shard_map/ppermute | solution.py:233
  57.4 6.2 %collective-permute-start.19 = (bf16[32,1152]{1,0:T(8,128)(2,1)S(1)}, bf16[32,1152]{1,0:T(8,128)(2,1)S(1)}, u32[]{:S(2)}, u32[]{:S(2)}) collective-permute-start(bf16[32,1152]{1,0:T(8,128)(2,1)S(1)} %get-tuple-element.59), channel_id=1, source_target_pairs={{0,24},{4,28},{8,16},{12,20},{16,8},{20,12},{24,0},{28,4},{1,25},{... | collective-permute-start | bytes 221192 | tf_op jit(solution)/shard_map/ppermute | solution.py:233
  59.6 5.6 %collective-permute-start.20 = (bf16[32,1152]{1,0:T(8,128)(2,1)S(1)}, bf16[32,1152]{1,0:T(8,128)(2,1)S(1)}, u32[]{:S(2)}, u32[]{:S(2)}) collective-permute-start(bf16[32,1152]{1,0:T(8,128)(2,1)S(1)} %get-tuple-element.60), channel_id=1, source_target_pairs={{0,16},{4,20},{8,24},{12,28},{16,0},{20,4},{24,8},{28,12},{1,17},{... | collective-permute-start | bytes 221192 | tf_op jit(solution)/shard_map/ppermute | solution.py:233
  59.6 5.6 %collective-permute-start.21 = (bf16[32,1152]{1,0:T(8,128)(2,1)S(1)}, bf16[32,1152]{1,0:T(8,128)(2,1)S(1)}, u32[]{:S(2)}, u32[]{:S(2)}) collective-permute-start(bf16[32,1152]{1,0:T(8,128)(2,1)S(1)} %get-tuple-element.61), channel_id=1, source_target_pairs={{0,8},{4,12},{8,0},{12,4},{16,24},{20,28},{24,16},{28,20},{1,9},{5... | collective-permute-start | bytes 221192 | tf_op jit(solution)/shard_map/ppermute | solution.py:233
